TPU v7x, 32 devices: a whole 2x2x4 slice. The times are simulated.
32 devices in a mesh: groups: 2 (over y), req: 16 (over z, x, core), tp: 1.
Axes of the slice: x: 2, y: 2, z: 4, core: 2. Of those that a mesh axis runs over, the one named last changes fastest.
Arguments:
- tokens: bfloat16 [16384, 8192], P(('groups', 'req'), 'tp'), parts along dimension 0, may hold values from -6 to 6
- row_adapter_index: int32 [16384, 1], P(('groups', 'req')), parts along dimension 0, may hold values from 0 to 63; in each aligned block of 512 rows (0 to 511, 512 to 1023, ...) at most 10 rows name the same one
- adapter_storage_slot: int32 [64], replicated, may hold values from 0 to 63, each once
- base_value_weight: bfloat16 [8192, 1024], P('tp'), may hold values from -0.0625 to 0.0625
- adapter_down_weight: bfloat16 [64, 16, 8192], P('req', None, 'tp'), may hold values from -0.0625 to 0.0625
- adapter_up_weight: bfloat16 [64, 16, 1024], P('req', None, 'tp'), may hold values from -1.5 to 1.5
Outputs:
- values_out: bfloat16 [16384, 1024], P(('groups', 'req'), 'tp'), parts along dimension 0
There are 2 independent parts, one for each index of `groups`. A program takes and returns all parts, laid end to end along the dimension named above; an argument that names none is the same for every part. Nothing has to cross between parts.
Inputs may be any that keep to these rules, and one draw needn't show every extreme that they name: `row_adapter_index`: within each device's aligned block of 512 rows no adapter is named by more than 10 rows. `adapter_storage_slot`: each slot appears once.
All inputs are finite; a program needn't handle non-finite values.
Results may differ from a plain program's by a relative error of at most 0.001.
Values may be sent and summed in bfloat16 or wider, within the bound.
No kernel may reach another device: no remote copies, remote signals or barrier semaphores. Data moves between devices by JAX's collectives and lax.ppermute only.
A program may use at most 128 MiB of HBM per device.

v0:
```python
import jax
import jax.numpy as jnp
from jax import lax
from jax.sharding import PartitionSpec as P


def per_device(
    tokens,
    row_adapter_index,
    adapter_storage_slot,
    base_value_weight,
    adapter_down_weight,
    adapter_up_weight,
):
    row_count = tokens.shape[0]
    half_width = tokens.shape[1]
    slot_owners = lax.axis_size("req")
    rows_per_owner = adapter_down_weight.shape[0]
    adapter_count = adapter_storage_slot.shape[0]
    slot_capacity = max(2, (5 * row_count + 4 * adapter_count - 1) // (4 * adapter_count))
    adapter_rows = row_adapter_index[:, 0]
    catalog = jnp.arange(adapter_count, dtype=jnp.int32)
    slot_of = jnp.sum(
        jnp.where(adapter_rows[:, None] == catalog[None, :], adapter_storage_slot[None, :], 0),
        axis=1,
    )
    positions = jnp.arange(row_count, dtype=jnp.int32)
    same_adapter = adapter_rows[:, None] == adapter_rows[None, :]
    earlier = positions[None, :] < positions[:, None]
    row_rank = jnp.sum(jnp.logical_and(same_adapter, earlier).astype(jnp.int32), axis=1)
    storage_slot_index = slot_of * slot_capacity + row_rank
    source_row = (
        jnp.full((adapter_count * slot_capacity,), row_count, jnp.int32)
        .at[storage_slot_index]
        .set(positions)
    )
    padded = jnp.concatenate([tokens, jnp.zeros((1, half_width), tokens.dtype)], axis=0)
    outgoing = jnp.take(padded, source_row, axis=0).reshape(
        slot_owners, rows_per_owner * slot_capacity, half_width
    )
    incoming_rows = lax.all_to_all(outgoing, "req", split_axis=0, concat_axis=0, tiled=True)
    incoming_rows = incoming_rows.reshape(slot_owners, rows_per_owner, slot_capacity, half_width)
    partial_shrink = jnp.einsum(
        "bygl,yel->byge", incoming_rows, adapter_down_weight, preferred_element_type=jnp.float32
    )
    base_partial = jnp.dot(tokens, base_value_weight, preferred_element_type=jnp.float32)
    down_projected = lax.psum(partial_shrink, "tp")
    adapter_slot_count = jnp.einsum(
        "xnwe,nev->xnwv",
        down_projected,
        adapter_up_weight.astype(jnp.float32),
        precision=lax.Precision.HIGHEST,
    )
    adapter_slot_count = adapter_slot_count.reshape(
        slot_owners, rows_per_owner * slot_capacity, adapter_up_weight.shape[2]
    )
    returned_rows = lax.all_to_all(
        adapter_slot_count, "req", split_axis=0, concat_axis=0, tiled=True
    )
    adapter_output_rows = jnp.take(
        returned_rows.reshape(adapter_count * slot_capacity, adapter_up_weight.shape[2]),
        storage_slot_index,
        axis=0,
    )
    base_output_half = lax.psum_scatter(base_partial, "tp", scatter_dimension=1, tiled=True)
    return (base_output_half + adapter_output_rows).astype(jnp.bfloat16)


def solution(mesh):
    placed = (
        P(("groups", "req"), "tp"),
        P(("groups", "req"), None),
        P(),
        P("tp", None),
        P("req", None, "tp"),
        P("req", None, "tp"),
    )
    return jax.shard_map(
        per_device,
        mesh=mesh,
        in_specs=placed,
        out_specs=P(("groups", "req"), "tp"),
        check_vma=False,
    )
```

profile of v0, /device:TPU:15, one launch (start us, length us, event | category | flops | bytes accessed | tf_op | source)
XLA Modules:
  0.0 386.0 jit_solution(17288430217489478795)
XLA Ops:
  0.0 0.0 copy-start
  0.0 1.0 convert_reduce_fusion
  1.0 0.8 select_reduce_fusion
  1.9 2.4 scatter_custom_fusion
  4.4 0.1 broadcast_in_dim.49
  4.5 8.0 %concatenate.3 = bf16[513,8192]{1,0:T(8,128)(2,1)} pad(bf16[512,8192]{1,0:T(8,128)(2,1)} %param.6, bf16[]{:T(256)} %constant.36.clone.1), padding=0_1x0_0 | pad | bytes 16793602 | tf_op jit(solution)/shard_map/concatenate | solution.py:37
  12.5 25.9 %gather_fusion = bf16[640,8192]{1,0:T(8,128)(2,1)} fusion(bf16[513,8192]{1,0:T(8,128)(2,1)} %concatenate.3, s32[1024]{0:T(1024)S(1)} %pad_clamp_fusion.1), kind=kCustom, calls=%fused_computation | custom fusion | bytes 20974080 | tf_op jit(solution)/shard_map/jit(_take)/gather | solution.py:38
  38.4 5.8 %broadcast_select_fusion = bf16[16,40,8192]{2,1,0:T(8,128)(2,1)S(1)} fusion(bf16[16,40,8192]{2,1,0:T(8,128)(2,1)} %bitcast.25, pred[16,40]{1,0:T(8,128)(4,1)S(1)} %broadcast_in_dim.49), kind=kLoop, calls=%fused_computation.3 | loop fusion | flops 5242880 | bytes 20972160 | tf_op jit(solution)/shard_map/jit(_take)/select_n | solution.py:38
  44.2 233.5 %all_to_all.10 = bf16[16,40,8192]{2,1,0:T(8,128)(2,1)} all-to-all(bf16[16,40,8192]{2,1,0:T(8,128)(2,1)S(1)} %broadcast_select_fusion), channel_id=1, replica_groups=mesh['groups'=2,'req'=16,'tp'=1] {'req'}, dimensions={0} | all-to-all | bytes 20971520 | tf_op jit(solution)/shard_map/all_to_all | solution.py:41
  277.7 13.5 %copy.15 = bf16[16,40,8192]{2,0,1:T(8,128)(2,1)} copy(bf16[16,40,8192]{2,1,0:T(8,128)(2,1)} %all_to_all.10) | data formatting | bytes 20971520 | tf_op jit(solution)/shard_map/all_to_all | solution.py:41
  291.2 0.0 copy-start.1
  291.2 0.0 copy-done
  291.2 5.6 %convolution_bitcast_fusion = f32[16,4,10,16]{3,0,2,1:T(8,128)S(1)} fusion(bf16[16,4,10,8192]{3,0,2,1:T(8,128)(2,1)} %bitcast.26, bf16[4,16,8192]{2,1,0:T(8,128)(2,1)S(1)} %copy-done), kind=kOutput, calls=%fused_computation.5 | convolution fusion | flops 167772160 | bytes 11575296 | tf_op jit(solution)/shard_map/bygl,yel->byge/dot_general | solution.py:43
  296.9 0.0 copy-done.1
  296.9 1.2 fusion.2
  298.0 3.1 copy.16
  301.1 5.9 %all-to-all-start.1 = ((f32[16,40,1024]{2,1,0:T(8,128)}), f32[16,40,1024]{2,1,0:T(8,128)}, u32[]{:S(2)}, u32[]{:S(2)}) async-start(f32[16,40,1024]{2,1,0:T(8,128)} %copy.16), calls=%async_computation.1 | async-start | bytes 5242880 | tf_op jit(solution)/shard_map/all_to_all | solution.py:57
  307.0 58.8 %all-to-all-done.1 = f32[16,40,1024]{2,1,0:T(8,128)} async-done(((f32[16,40,1024]{2,1,0:T(8,128)}), f32[16,40,1024]{2,1,0:T(8,128)}, u32[]{:S(2)}, u32[]{:S(2)}) %all-to-all-start.1) | async-done | bytes 2621472 | tf_op jit(solution)/shard_map/all_to_all | solution.py:57
  365.8 4.6 %gather_fusion.1 = f32[512,1024]{1,0:T(8,128)S(1)} fusion(f32[640,1024]{1,0:T(8,128)} %bitcast.12, s32[1024]{0:T(1024)S(1)} %pad_clamp_fusion), kind=kCustom, calls=%fused_computation.1 | custom fusion | bytes 4196352 | tf_op jit(solution)/shard_map/jit(_take)/gather | solution.py:60
  370.3 15.7 %add_convert_fusion = bf16[512,1024]{1,0:T(8,128)(2,1)} fusion(f32[512,1024]{1,0:T(8,128)S(1)} %gather_fusion.1, bf16[512,8192]{1,0:T(8,128)(2,1)} %param.6, bf16[8192,1024]{1,0:T(8,128)(2,1)} %param.9, pred[512]{0:T(512)(128)(4,1)S(1)} %get-tuple-element.5), kind=kOutput, calls=%fused_computation.4 | convolution fusion | flops 8591507456 | bytes 28312064 | tf_op jit(solution)/shard_map/dot_general | solution.py:46
  (7 shorter events, 0.0 us)
Async XLA Ops:
  0.0 291.2 %copy-start = (bf16[4,16,8192]{2,1,0:T(8,128)(2,1)S(1)}, bf16[4,16,8192]{2,1,0:T(8,128)(2,1)}, u32[]{:S(2)}) copy-start(bf16[4,16,8192]{2,1,0:T(8,128)(2,1)} %param.10) | copy-start | bytes 3145732
  291.2 5.6 %copy-start.1 = (bf16[4,16,1024]{2,1,0:T(8,128)(2,1)S(1)}, bf16[4,16,1024]{2,1,0:T(8,128)(2,1)}, u32[]{:S(2)}) copy-start(bf16[4,16,1024]{2,1,0:T(8,128)(2,1)} %param.11) | copy-start | bytes 393220
  301.1 64.7 %all-to-all-start.1 = ((f32[16,40,1024]{2,1,0:T(8,128)}), f32[16,40,1024]{2,1,0:T(8,128)}, u32[]{:S(2)}, u32[]{:S(2)}) async-start(f32[16,40,1024]{2,1,0:T(8,128)} %copy.16), calls=%async_computation.1 | async-start | bytes 5242880 | tf_op jit(solution)/shard_map/all_to_all | solution.py:57
where the time goes:
time: 386 us
  blocking collectives  234 us (61%)
  waiting for transfers between devices  58.8 us (15%)
  local copies, waits for them, and re-layouts  57.6 us (15%)
  matrix products  22.5 us (6%)
  other arithmetic  7.66 us (2%)
  starting transfers between devices  5.92 us (2%)
    all_to_all x1, blocking collectives, per_device(): lax.all_to_all(outgoing, 'req', split_axis=0, concat_axis=0, tiled=True)  234 us
    all_to_all x1, waiting for transfers between devices, per_device(): lax.all_to_all(adapter_slot_count, 'req', split_axis=0, concat_axis=0, ti...  58.8 us
    gather x1, local copies, waits for them, and re-layouts, per_device(): jnp.take(padded, source_row, axis=0)  25.9 us
    dot_general x1, matrix products, per_device(): jnp.dot(tokens, base_value_weight, preferred_element_type=jnp.float32)  15.7 us
    all_to_all x1, local copies, waits for them, and re-layouts, per_device(): lax.all_to_all(outgoing, 'req', split_axis=0, concat_axis=0, tiled=True)  13.5 us
    concatenate x1, local copies, waits for them, and re-layouts, per_device(): jnp.concatenate([tokens, jnp.zeros((1, half_width), tokens.dtype)], axis=0)  8 us
  transfers between devices with their start and end apart: 1, of which 1 were waited for; matrix products, arithmetic and copies ran while one was open for 0% of the time, Pallas kernels for 0%

commit v1 on v0

v1 whole, which is shorter than its diff:
```python
import jax
import jax.numpy as jnp
from jax import lax
from jax.sharding import PartitionSpec as P


def per_device(
    tokens,
    row_adapter_index,
    adapter_storage_slot,
    base_value_weight,
    adapter_down_weight,
    adapter_up_weight,
):
    adapter_count = adapter_storage_slot.shape[0]
    rank = adapter_down_weight.shape[1]
    adapter_rows = row_adapter_index[:, 0]
    catalog = jnp.arange(adapter_count, dtype=jnp.int32)
    slot_of = jnp.sum(
        jnp.where(adapter_rows[:, None] == catalog[None, :], adapter_storage_slot[None, :], 0),
        axis=1,
    )
    down_all = lax.all_gather(
        adapter_down_weight.reshape(-1, adapter_down_weight.shape[2]), "req", axis=0, tiled=True
    )
    up_all = lax.all_gather(
        adapter_up_weight.reshape(-1, adapter_up_weight.shape[2]), "req", axis=0, tiled=True
    )
    base_partial = jnp.dot(tokens, base_value_weight, preferred_element_type=jnp.float32)
    base_output = lax.psum_scatter(base_partial, "tp", scatter_dimension=1, tiled=True)
    shrink = lax.dot_general(
        tokens, down_all, (((1,), (1,)), ((), ())), preferred_element_type=jnp.float32
    )
    column_slot = jnp.arange(adapter_count * rank, dtype=jnp.int32) // rank
    shrink = jnp.where(slot_of[:, None] == column_slot[None, :], shrink, 0.0)
    shrink = lax.psum(shrink, "tp")
    high = lax.reduce_precision(shrink, 8, 7)
    rest = shrink - high
    middle = lax.reduce_precision(rest, 8, 7)
    low = rest - middle
    lora = sum(
        jnp.dot(piece.astype(jnp.bfloat16), up_all, preferred_element_type=jnp.float32)
        for piece in (low, middle, high)
    )
    return (base_output + lora).astype(jnp.bfloat16)


def solution(mesh):
    placed = (
        P(("groups", "req"), "tp"),
        P(("groups", "req"), None),
        P(),
        P("tp", None),
        P("req", None, "tp"),
        P("req", None, "tp"),
    )
    return jax.shard_map(
        per_device,
        mesh=mesh,
        in_specs=placed,
        out_specs=P(("groups", "req"), "tp"),
        check_vma=False,
    )
```

time: 386 us -> 209 us (0.54)
  the two profiles are of different devices: /device:TPU:15 before, /device:TPU:0 now
where the time goes in v1:
time: 209 us
  waiting for transfers between devices  159 us (76%)
  matrix products  35.1 us (17%)
  between operations  13.5 us (6%)
    all_gather x1, waiting for transfers between devices, per_device(): lax.all_gather(adapter_down_weight.reshape(-1, adapter_down_weight.shape[...  130 us
    all_gather x1, waiting for transfers between devices, per_device(): lax.all_gather(adapter_up_weight.reshape(-1, adapter_up_weight.shape[2]),...  27.4 us
    dot_general x1, matrix products, per_device(): lax.dot_general(tokens, down_all, (((1,), (1,)), ((), ())), preferred_ele...  14.4 us
    dot_general x1, matrix products, per_device(): jnp.dot(tokens, base_value_weight, preferred_element_type=jnp.float32)  13.7 us
    dot_general x3, matrix products, per_device(): jnp.dot(piece.astype(jnp.bfloat16), up_all, preferred_element_type=jnp.fl...  7.06 us
  transfers between devices with their start and end apart: 2, of which 2 were waited for; matrix products, arithmetic and copies ran while one was open for 7% of the time, Pallas kernels for 0%

profile of v1, /device:TPU:0, one launch (start us, length us, event | category | flops | bytes accessed | tf_op | source)
XLA Modules:
  0.0 208.6 jit_solution(16199065453007428824)
XLA Ops:
  6.5 0.0 all-gather.3.cloned.1.call-start
  6.5 0.7 all-gather.3.cloned.1.call-update
  7.3 0.0 all-gather.5.cloned.1.call-start
  7.3 0.7 all-gather.5.cloned.1.call-update
  8.0 0.8 select_reduce_fusion
  8.8 130.3 %all-gather.3.cloned.1.call-done = bf16[1024,8192]{1,0:T(8,128)(2,1)} async-done(((bf16[64,8192]{1,0:T(8,128)(2,1)}), bf16[1024,8192]{1,0:T(8,128)(2,1)}) %all-gather.3.cloned.1.call-update) | async-done | bytes 16777232 | tf_op jit(solution)/shard_map/all_gather | solution.py:23
  139.1 14.4 %fusion.20 = f32[512,1024]{1,0:T(8,128)S(1)} fusion(bf16[512,8192]{1,0:T(8,128)(2,1)} %param.6, bf16[1024,8192]{1,0:T(8,128)(2,1)} %all-gather.3.cloned.1.call-done), kind=kOutput, calls=%fused_computation.31 | convolution fusion | flops 8589934592 | bytes 27262976 | tf_op jit(solution)/shard_map/dot_general | solution.py:31
  153.5 27.4 %all-gather.5.cloned.1.call-done = bf16[1024,1024]{1,0:T(8,128)(2,1)} async-done(((bf16[64,1024]{1,0:T(8,128)(2,1)}), bf16[1024,1024]{1,0:T(8,128)(2,1)}) %all-gather.5.cloned.1.call-update) | async-done | bytes 2097168 | tf_op jit(solution)/shard_map/all_gather | solution.py:26
  180.9 0.0 copy-start
  180.9 0.0 slice-start
  180.9 3.1 %fusion.4 = f32[512,1024]{1,0:T(8,128)S(1)} fusion(bf16[1024,1024]{1,0:T(8,128)(2,1)} %all-gather.5.cloned.1.call-done, f32[512,1024]{1,0:T(8,128)S(1)} %fusion.20, s32[1024]{0:T(1024)S(1)} %add_select_fusion, s32[512]{0:T(512)S(1)} %select_reduce_fusion), kind=kOutput, calls=%fused_computation.9 | convolution fusion | flops 1076887552 | bytes 6297600 | tf_op jit(solution)/shard_map/dot_general | solution.py:42
  184.0 0.0 copy-done
  184.0 0.0 slice-start.1
  184.0 2.7 %fusion.1 = f32[512,1024]{1,0:T(8,128)} fusion(bf16[1024,1024]{1,0:T(8,128)(2,1)S(1)} %copy-done, f32[512,1024]{1,0:T(8,128)S(1)} %fusion.20, s32[1024]{0:T(1024)S(1)} %add_select_fusion, s32[512]{0:T(512)S(1)} %select_reduce_fusion), kind=kOutput, calls=%fused_computation.7 | convolution fusion | flops 1077411840 | bytes 6297600 | tf_op jit(solution)/shard_map/dot_general | solution.py:42
  186.7 1.3 fusion.3
  188.0 0.0 slice-done
  188.0 0.0 slice-done.1
  188.0 13.7 %add_convert_fusion = bf16[512,1024]{1,0:T(8,128)(2,1)} fusion(f32[512,1024]{1,0:T(8,128)S(1)} %fusion.3, f32[512,1024]{1,0:T(8,128)} %fusion.1, f32[512,1024]{1,0:T(8,128)S(1)} %fusion.4, bf16[512,8192]{1,0:T(8,128)(2,1)S(1)} %bitcast.14, bf16[8192,1024]{1,0:T(8,128)(2,1)} %param.9), kind=kOutput, calls=%fused_computation.5 | convolution fusion | flops 8592031744 | bytes 32505856 | tf_op jit(solution)/shard_map/dot_general | solution.py:29
  (2 shorter events, 0.0 us)
Async XLA Ops:
  6.5 132.6 %all-gather.3.cloned.1.call-start = ((), (), s32[]{:S(2)}) async-start(), calls=%async_computation | async-start | bytes 17825792 | tf_op jit(solution)/shard_map/all_gather | solution.py:23
  7.3 173.7 %all-gather.5.cloned.1.call-start = ((), (), s32[]{:S(2)}) async-start(), calls=%async_computation.1 | async-start | bytes 2228224 | tf_op jit(solution)/shard_map/all_gather | solution.py:26
  180.9 3.1 %copy-start = (bf16[1024,1024]{1,0:T(8,128)(2,1)S(1)}, bf16[1024,1024]{1,0:T(8,128)(2,1)}, u32[]{:S(2)}) copy-start(bf16[1024,1024]{1,0:T(8,128)(2,1)} %all-gather.5.cloned.1.call-done) | copy-start | bytes 6291460
  180.9 7.1 %slice-start = ((s8[8388608]{0:T(1024)(128)(4,1)}), s8[4194304]{0:T(1024)(128)(4,1)S(1)}, s32[]{:S(2)}) async-start(s8[8388608]{0:T(1024)(128)(4,1)} %bitcast.13), calls=%async_computation.2 | async-start | bytes 8388608
  184.0 4.0 %slice-start.1 = ((s8[8388608]{0:T(1024)(128)(4,1)}), s8[4194304]{0:T(1024)(128)(4,1)S(1)}, s32[]{:S(2)}) async-start(s8[8388608]{0:T(1024)(128)(4,1)} %bitcast.13), calls=%async_computation.3 | async-start | bytes 8388608
Sparse Core Ops, SparseCore 0:
  9.5 129.5 all-gather.2
  141.3 39.5 all-gather.4

commit v2 on v1

v2 whole, which is shorter than its diff:
```python
import functools

import jax
import jax.numpy as jnp
from jax import lax
from jax.experimental import pallas as pl
from jax.experimental.pallas import tpu as pltpu
from jax.sharding import PartitionSpec as P

RING = (0, 1, 3, 2)
PLACE_IN_RING = (0, 1, 3, 2)
DEPTH_TILE = 2048


def slots_of_rows(row_adapter_index, adapter_storage_slot):
    catalog = jnp.arange(adapter_storage_slot.shape[0], dtype=jnp.int32)
    return jnp.sum(
        jnp.where(row_adapter_index == catalog[None, :], adapter_storage_slot[None, :], 0),
        axis=1,
        keepdims=True,
    )


def gathered(
    tokens,
    row_adapter_index,
    adapter_storage_slot,
    base_value_weight,
    adapter_down_weight,
    adapter_up_weight,
):
    adapter_count = adapter_storage_slot.shape[0]
    rank = adapter_down_weight.shape[1]
    slot_of = slots_of_rows(row_adapter_index, adapter_storage_slot)
    down_all = lax.all_gather(
        adapter_down_weight.reshape(-1, adapter_down_weight.shape[2]), "req", axis=0, tiled=True
    )
    up_all = lax.all_gather(
        adapter_up_weight.reshape(-1, adapter_up_weight.shape[2]), "req", axis=0, tiled=True
    )
    base_partial = jnp.dot(tokens, base_value_weight, preferred_element_type=jnp.float32)
    base_output = lax.psum_scatter(base_partial, "tp", scatter_dimension=1, tiled=True)
    shrink = lax.dot_general(
        tokens, down_all, (((1,), (1,)), ((), ())), preferred_element_type=jnp.float32
    )
    column_slot = jnp.arange(adapter_count * rank, dtype=jnp.int32) // rank
    shrink = jnp.where(slot_of == column_slot[None, :], shrink, 0.0)
    shrink = lax.psum(shrink, "tp")
    high = lax.reduce_precision(shrink, 8, 7)
    rest = shrink - high
    middle = lax.reduce_precision(rest, 8, 7)
    low = rest - middle
    lora = sum(
        jnp.dot(piece.astype(jnp.bfloat16), up_all, preferred_element_type=jnp.float32)
        for piece in (low, middle, high)
    )
    return (base_output + lora).astype(jnp.bfloat16)


def absorb_kernel(count, steps, *refs):
    tokens_ref, row_slot_ref, column_slot_ref, total_ref = refs[:4]
    downs = refs[4 : 4 + count]
    ups = refs[4 + count : 4 + 2 * count]
    out_ref, shrink_ref = refs[4 + 2 * count :]
    step = pl.program_id(0)
    part = lax.dot_general(
        tokens_ref[...],
        jnp.concatenate([down[...] for down in downs], axis=0),
        (((1,), (1,)), ((), ())),
        preferred_element_type=jnp.float32,
    )

    @pl.when(step == 0)
    def _():
        shrink_ref[...] = part

    @pl.when(step > 0)
    def _():
        shrink_ref[...] += part

    @pl.when(step == steps - 1)
    def _():
        kept = jnp.where(row_slot_ref[...] == column_slot_ref[...], shrink_ref[...], 0.0)
        high = kept.astype(jnp.bfloat16)
        low = (kept - high.astype(jnp.float32)).astype(jnp.bfloat16)
        up = jnp.concatenate([up[...] for up in ups], axis=0)
        lora = jnp.dot(low, up, preferred_element_type=jnp.float32)
        lora += jnp.dot(high, up, preferred_element_type=jnp.float32)
        out_ref[...] = (total_ref[...] + lora).astype(out_ref.dtype)


def absorb(tokens, row_slot, total, pieces, slots, out_dtype):
    rows, depth = tokens.shape
    width = total.shape[1]
    columns = sum(piece.shape[0] for piece in pieces)
    rank = columns // len(slots)
    column_slot = jnp.repeat(jnp.stack(slots).astype(jnp.int32), rank)[None, :]
    tile = min(DEPTH_TILE, depth)
    steps = depth // tile
    whole = lambda *shape: pl.BlockSpec(shape, lambda k: (0, 0))
    return pl.pallas_call(
        functools.partial(absorb_kernel, len(pieces), steps),
        out_shape=jax.ShapeDtypeStruct(total.shape, out_dtype),
        grid=(steps,),
        in_specs=[
            pl.BlockSpec((rows, tile), lambda k: (0, k)),
            whole(rows, 1),
            whole(1, columns),
            whole(rows, width),
        ]
        + [pl.BlockSpec((piece.shape[0], tile), lambda k: (0, k)) for piece in pieces]
        + [pl.BlockSpec((piece.shape[0], width), lambda k: (0, depth // width)) for piece in pieces],
        out_specs=whole(rows, width),
        scratch_shapes=[pltpu.VMEM((rows, columns), jnp.float32)],
        cost_estimate=pl.CostEstimate(
            flops=2 * rows * columns * (depth + 2 * width),
            bytes_accessed=2 * (rows + columns) * depth + 8 * rows * width,
            transcendentals=0,
        ),
        compiler_params=pltpu.CompilerParams(vmem_limit_bytes=48 * 1024 * 1024),
    )(tokens, row_slot, column_slot, total, *pieces, *pieces)


def passed_round(
    tokens,
    row_adapter_index,
    adapter_storage_slot,
    base_value_weight,
    adapter_down_weight,
    adapter_up_weight,
):
    held, rank, depth = adapter_down_weight.shape
    axes = ("groups", "req")
    planes, owners = lax.axis_size("groups"), lax.axis_size("req")
    y, at = lax.axis_index("groups"), lax.axis_index("req")
    z, x, core = at // 4, (at // 2) % 2, at % 2
    ring = jnp.array(RING, jnp.int32)
    place = jnp.array(PLACE_IN_RING, jnp.int32)[z]

    def permuted(array, target):
        pairs = [
            (g * owners + r, target(g, r)) for g in range(planes) for r in range(owners)
        ]
        return lax.ppermute(array, axes, pairs)

    def next_z(g, r):
        to = RING[(PLACE_IN_RING[r // 4] + 1) % 4]
        return g * owners + to * 4 + r % 4

    z_ring = lambda array: permuted(array, next_z)
    x_swap = lambda array: permuted(array, lambda g, r: g * owners + (r ^ 2))
    y_swap = lambda array: permuted(array, lambda g, r: (1 - g) * owners + r)
    core_swap = lambda array: permuted(array, lambda g, r: g * owners + (r ^ 1))

    own = jnp.concatenate(
        [adapter_down_weight, adapter_up_weight], axis=2
    )
    own = jnp.where(y == 0, own, own[::-1])
    front = own[:2].reshape(2 * rank, -1)
    third = own[2]
    back = own[2:].reshape(2 * rank, -1)

    def slots(step, other_x, other_y, other_core, units):
        from_z = ring[(place - step) % 4]
        from_x = 1 - x if other_x else x
        from_y = 1 - y if other_y else y
        from_core = 1 - core if other_core else core
        first = held * ((from_z * 2 + from_x) * 2 + from_core)
        return [first + jnp.where(from_y == 0, unit, held - 1 - unit) for unit in units]

    row_slot = slots_of_rows(row_adapter_index, adapter_storage_slot)
    base = jnp.dot(tokens, base_value_weight, preferred_element_type=jnp.float32)

    z1 = z_ring(front)
    x0 = x_swap(front)
    z2 = z_ring(z1)
    x1 = x_swap(z1)
    m1 = y_swap(z1[:rank])
    z3 = z_ring(z2)
    x2 = x_swap(z2)
    m2 = y_swap(z2[:rank])
    y1 = y_swap(x1)
    third, _ = lax.optimization_barrier((third, z2))
    t1 = z_ring(third)
    x3 = x_swap(z3)
    y2 = y_swap(x2)
    m3 = y_swap(z3[:rank])
    t2 = z_ring(t1)
    y3 = y_swap(x3)
    back_late, _ = lax.optimization_barrier((back, z3))
    xr = x_swap(back_late)
    t3 = z_ring(t2)

    pair = (0, 1)
    groups = [
        [
            (front, slots, (0, False, False), pair),
            (back, slots, (0, False, False), (2, 3)),
            (x0, slots, (0, True, False), pair),
            (z1, slots, (1, False, False), pair),
        ],
        [
            (z2, slots, (2, False, False), pair),
            (x1, slots, (1, True, False), pair),
            (m1, slots, (1, False, True), (0,)),
            (m2, slots, (2, False, True), (0,)),
            (x2, slots, (2, True, False), pair),
        ],
        [
            (z3, slots, (3, False, False), pair),
            (m3, slots, (3, False, True), (0,)),
            (t1, slots, (1, False, False), (2,)),
            (x3, slots, (3, True, False), pair),
            (y1, slots, (1, True, True), pair),
        ],
        [
            (t2, slots, (2, False, False), (2,)),
            (t3, slots, (3, False, False), (2,)),
            (y2, slots, (2, True, True), pair),
            (xr, slots, (0, True, False), (2, 3)),
            (y3, slots, (3, True, True), pair),
        ],
    ]
    total = base
    for number, group in enumerate(groups):
        pieces, held_slots = [], []
        for array, lookup, (step, other_x, other_y), units in group:
            for other_core in (False, True):
                pieces.append(core_swap(array) if other_core else array)
                held_slots += lookup(step, other_x, other_y, other_core, units)
        last = number == len(groups) - 1
        total = absorb(
            tokens, row_slot, total, pieces, held_slots, jnp.bfloat16 if last else jnp.float32
        )
    return total


def solution(mesh):
    placed = (
        P(("groups", "req"), "tp"),
        P(("groups", "req"), None),
        P(),
        P("tp", None),
        P("req", None, "tp"),
        P("req", None, "tp"),
    )
    sizes = mesh.shape
    small = sizes["groups"] == 2 and sizes["req"] == 16 and sizes["tp"] == 1
    return jax.shard_map(
        passed_round if small else gathered,
        mesh=mesh,
        in_specs=placed,
        out_specs=P(("groups", "req"), "tp"),
        check_vma=False,
    )
```

time: 209 us -> 157 us (0.75)
  waiting for transfers between devices: 159 us -> 48.8 us
  Pallas kernels: 0 us -> 36.9 us
  starting transfers between devices: 0.04 us -> 26.7 us
  local copies, waits for them, and re-layouts: 0.02 us -> 20.2 us
  matrix products: 35.1 us -> 15.9 us
  between operations: 13.5 us -> 7.25 us
    all_gather x2 -> x0, waiting for transfers between devices: 158 us -> none  [the longest x1 130 us: per_device(): lax.all_gather(adapter_down_weight.reshape(-1, adapter_down_weight.shape[...]
    ppermute x0 -> x36, waiting for transfers between devices: none -> 48.8 us  [permuted(): return lax.ppermute(array, axes, pairs)]
    pallas_call x0 -> x4, Pallas kernels: none -> 36.9 us  [absorb(): pl.pallas_call(functools.partial(absorb_kernel, len(pieces), steps), out_...]
    ppermute x0 -> x36, starting transfers between devices: none -> 26.7 us  [permuted(): return lax.ppermute(array, axes, pairs)]
    dot_general x5 -> x1, matrix products: 35.1 us -> 15.9 us  [passed_round(): jnp.dot(tokens, base_value_weight, preferred_element_type=jnp.float32)]
    unnamed x6 -> x85, local copies, waits for them, and re-layouts: 0.02 us -> 17.6 us
  transfers between devices with their start and end apart: 2 -> 36, of which waited for: 2 -> 9; matrix products, arithmetic and copies ran while one was open for 7% -> 12% of each run, Pallas kernels for 0% -> 18%
where the time goes in v2:
time: 157 us; the launch traced here: 156 us
  waiting for transfers between devices  48.8 us (31%)
  Pallas kernels  36.9 us (24%)
  starting transfers between devices  26.7 us (17%)
  local copies, waits for them, and re-layouts  20.2 us (13%)
  matrix products  15.9 us (10%)
  between operations  7.25 us (5%)
    ppermute x36, waiting for transfers between devices, permuted(): return lax.ppermute(array, axes, pairs)  48.8 us
    pallas_call x4, Pallas kernels, absorb(): pl.pallas_call(functools.partial(absorb_kernel, len(pieces), steps), out_...  36.9 us
    ppermute x36, starting transfers between devices, permuted(): return lax.ppermute(array, axes, pairs)  26.7 us
    unnamed x85, local copies, waits for them, and re-layouts  17.6 us
    dot_general x1, matrix products, passed_round(): jnp.dot(tokens, base_value_weight, preferred_element_type=jnp.float32)  15.9 us
  transfers between devices with their start and end apart: 36, of which 9 were waited for; matrix products, arithmetic and copies ran while one was open for 12% of the time, Pallas kernels for 18%

profile of v2, /device:TPU:0, one launch (start us, length us, event | category | flops | bytes accessed | tf_op | source)
XLA Modules:
  0.0 156.0 jit_solution(7250910001261397663)
XLA Ops:
  0.0 1.3 constant_dynamic-update-slice_fusion.1
  1.4 0.2 reverse_select_fusion
  1.7 3.1 %collective-permute-start.4 = (bf16[32,9216]{1,0:T(8,128)(2,1)S(1)}, bf16[32,9216]{1,0:T(8,128)(2,1)S(1)}, u32[]{:S(2)}, u32[]{:S(2)}) collective-permute-start(bf16[32,9216]{1,0:T(8,128)(2,1)S(1)} %bitcast.81), channel_id=1, source_target_pairs={{0,4},{1,5},{2,6},{3,7},{4,12},{5,13},{6,14},{7,15},{8,0},{9,1},{1... | collective-permute-start | bytes 1769480 | tf_op jit(solution)/shard_map/ppermute | solution.py:144
  4.7 1.5 collective-permute-start.2
  6.2 12.8 %collective-permute-done.4.refs_10_.refs_18_ = bf16[32,9216]{1,0:T(8,128)(2,1)S(1)} collective-permute-done((bf16[32,9216]{1,0:T(8,128)(2,1)S(1)}, bf16[32,9216]{1,0:T(8,128)(2,1)S(1)}, u32[]{:S(2)}, u32[]{:S(2)}) %collective-permute-start.4) | collective-permute-done | bytes 589856 | tf_op jit(solution)/shard_map/ppermute | solution.py:144
  19.1 0.8 collective-permute-start.6
  19.9 1.6 %collective-permute-start.10 = (bf16[16,9216]{1,0:T(8,128)(2,1)S(1)}, bf16[16,9216]{1,0:T(8,128)(2,1)S(1)}, u32[]{:S(2)}, u32[]{:S(2)}) collective-permute-start(bf16[16,9216]{1,0:T(8,128)(2,1)S(1)} %slice.26), channel_id=1, source_target_pairs={{0,16},{1,17},{2,18},{3,19},{4,20},{5,21},{6,22},{7,23},{8,24},{9,... | collective-permute-start | bytes 884744 | tf_op jit(solution)/shard_map/ppermute | solution.py:144
  21.5 0.2 collective-permute-start.5
  21.8 1.5 collective-permute-start.8
  23.3 11.2 %collective-permute-done.6.refs_4_.refs_14_ = bf16[32,9216]{1,0:T(8,128)(2,1)S(1)} collective-permute-done((bf16[32,9216]{1,0:T(8,128)(2,1)S(1)}, bf16[32,9216]{1,0:T(8,128)(2,1)S(1)}, u32[]{:S(2)}, u32[]{:S(2)}) %collective-permute-start.6) | collective-permute-done | bytes 589856 | tf_op jit(solution)/shard_map/ppermute | solution.py:144
  34.5 0.6 collective-permute-start.11
  35.1 0.8 copy-done.6
  36.0 0.5 collective-permute-done.3.refs_9_.refs_17_
  36.5 0.8 copy-done.12
  37.3 1.3 collective-permute-start.12
  38.6 0.8 copy-done.8
  39.4 2.1 %collective-permute-start.20 = (bf16[16,9216]{1,0:T(8,128)(2,1)S(1)}, bf16[16,9216]{1,0:T(8,128)(2,1)S(1)}, u32[]{:S(2)}, u32[]{:S(2)}) collective-permute-start(bf16[16,9216]{1,0:T(8,128)(2,1)S(1)} %slice_bitcast_fusion), channel_id=1, source_target_pairs={{0,4},{1,5},{2,6},{3,7},{4,12},{5,13},{6,14},{7,15},{8,0},{9,1},{1... | collective-permute-start | bytes 884744 | tf_op jit(solution)/shard_map/ppermute | solution.py:144
  41.5 0.7 copy-done.20
  42.3 2.1 %collective-permute-start.16 = (bf16[32,9216]{1,0:T(8,128)(2,1)S(1)}, bf16[32,9216]{1,0:T(8,128)(2,1)S(1)}, u32[]{:S(2)}, u32[]{:S(2)}) collective-permute-start(bf16[32,9216]{1,0:T(8,128)(2,1)S(1)} %collective-permute-done.6.refs_4_.refs_14_), channel_id=1, source_target_pairs={{0,4},{1,5},{2,6},{3,7},{4,12},{5,13},{6,14},{7,15},{8,0},{9,1},{1... | collective-permute-start | bytes 1769480 | tf_op jit(solution)/shard_map/ppermute | solution.py:144
  44.3 2.0 %collective-permute-done.12.refs_10_.refs_20_ = bf16[16,9216]{1,0:T(8,128)(2,1)S(1)} collective-permute-done((bf16[16,9216]{1,0:T(8,128)(2,1)S(1)}, bf16[16,9216]{1,0:T(8,128)(2,1)S(1)}, u32[]{:S(2)}, u32[]{:S(2)}) %collective-permute-start.12) | collective-permute-done | bytes 294944 | tf_op jit(solution)/shard_map/ppermute | solution.py:144
  46.4 1.2 collective-permute-start.14
  47.6 2.6 %collective-permute-done.20.refs_8_.refs_18_ = bf16[16,9216]{1,0:T(8,128)(2,1)S(1)} collective-permute-done((bf16[16,9216]{1,0:T(8,128)(2,1)S(1)}, bf16[16,9216]{1,0:T(8,128)(2,1)S(1)}, u32[]{:S(2)}, u32[]{:S(2)}) %collective-permute-start.20) | collective-permute-done | bytes 294944 | tf_op jit(solution)/shard_map/ppermute | solution.py:144
  50.1 0.8 collective-permute-start.24
  50.9 0.8 copy-done.10
  51.7 0.7 copy-done.22
  52.5 0.8 copy-done.14
  53.3 0.5 collective-permute-start.21
  53.8 8.5 %collective-permute-done.16.refs_4_.refs_14_ = bf16[32,9216]{1,0:T(8,128)(2,1)S(1)} collective-permute-done((bf16[32,9216]{1,0:T(8,128)(2,1)S(1)}, bf16[32,9216]{1,0:T(8,128)(2,1)S(1)}, u32[]{:S(2)}, u32[]{:S(2)}) %collective-permute-start.16) | collective-permute-done | bytes 589856 | tf_op jit(solution)/shard_map/ppermute | solution.py:144
  62.4 1.2 collective-permute-start.26
  63.6 0.7 copy-done.24
  64.3 0.7 copy-done.30
  65.1 0.5 collective-permute-start.18
  65.6 0.7 copy-done.28
  66.3 1.5 collective-permute-start.22
  67.8 0.2 collective-permute-start.17
  68.0 3.8 %collective-permute-done.26.refs_4_.refs_14_ = bf16[16,9216]{1,0:T(8,128)(2,1)S(1)} collective-permute-done((bf16[16,9216]{1,0:T(8,128)(2,1)S(1)}, bf16[16,9216]{1,0:T(8,128)(2,1)S(1)}, u32[]{:S(2)}, u32[]{:S(2)}) %collective-permute-start.26) | collective-permute-done | bytes 294944 | tf_op jit(solution)/shard_map/ppermute | solution.py:144
  71.9 0.8 collective-permute-start.28
  72.6 0.8 collective-permute-done.18.refs_6_.refs_16_
  73.5 0.7 copy-done.32
  74.2 6.3 %collective-permute-done.28.refs_6_.refs_16_ = bf16[16,9216]{1,0:T(8,128)(2,1)S(1)} collective-permute-done((bf16[16,9216]{1,0:T(8,128)(2,1)S(1)}, bf16[16,9216]{1,0:T(8,128)(2,1)S(1)}, u32[]{:S(2)}, u32[]{:S(2)}) %collective-permute-start.28) | collective-permute-done | bytes 294944 | tf_op jit(solution)/shard_map/ppermute | solution.py:144
  80.5 1.5 collective-permute-start.32
  82.0 0.7 copy-done.36
  82.7 0.5 collective-permute-start.30
  83.2 0.8 copy-done.16
  84.0 0.5 collective-permute-start.23
  84.6 0.8 copy-done.18
  85.5 1.5 collective-permute-start.34
  87.0 15.9 %fusion.2.refs_3_ = f32[512,1024]{1,0:T(8,128)} fusion(bf16[512,8192]{1,0:T(8,128)(2,1)} %refs_0_.7, bf16[8192,1024]{1,0:T(8,128)(2,1)} %param.11), kind=kOutput, calls=%fused_computation.8 | convolution fusion | flops 8589934592 | bytes 27262976 | tf_op jit(solution)/shard_map/dot_general | solution.py:172
  102.9 0.6 dynamic_slice.10
  107.7 0.7 fusion.1
  111.1 0.1 copy.16.refs_1_
  111.3 0.1 stack.220
  111.6 0.1 stack.237
  112.4 0.5 collective-permute-start.33
  113.0 1.1 copy-done.1
  114.1 1.1 copy-done.3
  115.1 1.1 copy-done.7
  116.2 1.1 copy-done.9
  117.3 1.1 copy-done.13
  118.4 9.4 %shard_map.82.refs_3_ = f32[512,1024]{1,0:T(8,128)} custom-call(bf16[512,8192]{1,0:T(8,128)(2,1)} %refs_0_.7, s32[512,1]{1,0:T(8,128)S(1)} %copy.16.refs_1_, s32[1,256]{1,0:T(1,128)S(1)} %broadcast_in_dim_reshape.15.refs_2_, f32[512,1024]{1,0:T(8,128)} %fusion.2.refs_3_, bf16[32,9216]{1,0:T(8,128)(2,1)S(1)} %bitcast.84, bf16[32,9216]{1,0:T(8,128)(2,1)S(1)} %copy-done.1, ...), custom_call_target="tpu_custom_call" | custom-call | flops 2684354560 | bytes 16777216 | tf_op jit(solution)/shard_map/pallas_call | solution.py:101
  127.8 0.5 collective-permute-start.27
  128.4 9.3 %shard_map.83.refs_3_ = f32[512,1024]{1,0:T(8,128)} custom-call(bf16[512,8192]{1,0:T(8,128)(2,1)} %refs_0_.7, s32[512,1]{1,0:T(8,128)S(1)} %copy.16.refs_1_, s32[1,256]{1,0:T(1,128)S(1)} %broadcast_in_dim_reshape.14.refs_2_, f32[512,1024]{1,0:T(8,128)} %shard_map.82.refs_3_, bf16[32,9216]{1,0:T(8,128)(2,1)S(1)} %collective-permute-done.6.refs_4_.refs_14_, ...), custom_call_target="tpu_custom_call" | custom-call | flops 2684354560 | bytes 16777216 | tf_op jit(solution)/shard_map/pallas_call | solution.py:101
  137.8 9.3 %shard_map.84.refs_3_ = f32[512,1024]{1,0:T(8,128)} custom-call(bf16[512,8192]{1,0:T(8,128)(2,1)} %refs_0_.7, s32[512,1]{1,0:T(8,128)S(1)} %copy.16.refs_1_, s32[1,256]{1,0:T(1,128)S(1)} %broadcast_in_dim_reshape.13.refs_2_, f32[512,1024]{1,0:T(8,128)} %shard_map.83.refs_3_, bf16[32,9216]{1,0:T(8,128)(2,1)S(1)} %collective-permute-done.16.refs_4_.refs_14_, ...), custom_call_target="tpu_custom_call" | custom-call | flops 2684354560 | bytes 16777216 | tf_op jit(solution)/shard_map/pallas_call | solution.py:101
  147.1 8.9 %shard_map.85 = bf16[512,1024]{1,0:T(8,128)(2,1)} custom-call(bf16[512,8192]{1,0:T(8,128)(2,1)} %refs_0_.7, s32[512,1]{1,0:T(8,128)S(1)} %copy.16.refs_1_, s32[1,256]{1,0:T(1,128)S(1)} %broadcast_in_dim_reshape.12.refs_2_, f32[512,1024]{1,0:T(8,128)} %shard_map.84.refs_3_, bf16[16,9216]{1,0:T(8,128)(2,1)S(1)} %copy-done.27, ...), custom_call_target="tpu_custom_call" | custom-call | flops 2684354560 | bytes 16777216 | tf_op jit(solution)/shard_map/pallas_call | solution.py:101
  (121 shorter events, 1.6 us)
Async XLA Ops:
  0.0 1.3 copy-start.38
  1.7 17.4 %collective-permute-start.4 = (bf16[32,9216]{1,0:T(8,128)(2,1)S(1)}, bf16[32,9216]{1,0:T(8,128)(2,1)S(1)}, u32[]{:S(2)}, u32[]{:S(2)}) collective-permute-start(bf16[32,9216]{1,0:T(8,128)(2,1)S(1)} %bitcast.81), channel_id=1, source_target_pairs={{0,4},{1,5},{2,6},{3,7},{4,12},{5,13},{6,14},{7,15},{8,0},{9,1},{1... | collective-permute-start | bytes 1769480 | tf_op jit(solution)/shard_map/ppermute | solution.py:144
  4.7 16.8 %collective-permute-start = (bf16[32,9216]{1,0:T(8,128)(2,1)S(1)}, bf16[32,9216]{1,0:T(8,128)(2,1)S(1)}, u32[]{:S(2)}, u32[]{:S(2)}) collective-permute-start(bf16[32,9216]{1,0:T(8,128)(2,1)S(1)} %bitcast.82), channel_id=1, source_target_pairs={{0,1},{1,0},{2,3},{3,2},{4,5},{5,4},{6,7},{7,6},{8,9},{9,8},{10,11... | collective-permute-start | bytes 1769480 | tf_op jit(solution)/shard_map/ppermute | solution.py:144
  4.7 17.0 %collective-permute-start.2 = (bf16[32,9216]{1,0:T(8,128)(2,1)S(1)}, bf16[32,9216]{1,0:T(8,128)(2,1)S(1)}, u32[]{:S(2)}, u32[]{:S(2)}) collective-permute-start(bf16[32,9216]{1,0:T(8,128)(2,1)S(1)} %bitcast.83), channel_id=1, source_target_pairs={{0,2},{1,3},{2,0},{3,1},{4,6},{5,7},{6,4},{7,5},{8,10},{9,11},{10,... | collective-permute-start | bytes 1769480 | tf_op jit(solution)/shard_map/ppermute | solution.py:144
  19.1 15.4 %collective-permute-start.6 = (bf16[32,9216]{1,0:T(8,128)(2,1)S(1)}, bf16[32,9216]{1,0:T(8,128)(2,1)S(1)}, u32[]{:S(2)}, u32[]{:S(2)}) collective-permute-start(bf16[32,9216]{1,0:T(8,128)(2,1)S(1)} %collective-permute-done.4.refs_10_.refs_18_), channel_id=1, source_target_pairs={{0,4},{1,5},{2,6},{3,7},{4,12},{5,13},{6,14},{7,15},{8,0},{9,1},{1... | collective-permute-start | bytes 1769480 | tf_op jit(solution)/shard_map/ppermute | solution.py:144
  19.9 15.2 %collective-permute-start.1 = (bf16[32,9216]{1,0:T(8,128)(2,1)S(1)}, bf16[32,9216]{1,0:T(8,128)(2,1)S(1)}, u32[]{:S(2)}, u32[]{:S(2)}) collective-permute-start(bf16[32,9216]{1,0:T(8,128)(2,1)S(1)} %bitcast.77), channel_id=1, source_target_pairs={{0,1},{1,0},{2,3},{3,2},{4,5},{5,4},{6,7},{7,6},{8,9},{9,8},{10,11... | collective-permute-start | bytes 1769480 | tf_op jit(solution)/shard_map/ppermute | solution.py:144
  19.9 14.6 %collective-permute-start.10 = (bf16[16,9216]{1,0:T(8,128)(2,1)S(1)}, bf16[16,9216]{1,0:T(8,128)(2,1)S(1)}, u32[]{:S(2)}, u32[]{:S(2)}) collective-permute-start(bf16[16,9216]{1,0:T(8,128)(2,1)S(1)} %slice.26), channel_id=1, source_target_pairs={{0,16},{1,17},{2,18},{3,19},{4,20},{5,21},{6,22},{7,23},{8,24},{9,... | collective-permute-start | bytes 884744 | tf_op jit(solution)/shard_map/ppermute | solution.py:144
  21.5 63.0 %copy-start = (bf16[32,9216]{1,0:T(8,128)(2,1)}, bf16[32,9216]{1,0:T(8,128)(2,1)S(1)}, u32[]{:S(2)}) copy-start(bf16[32,9216]{1,0:T(8,128)(2,1)S(1)} %collective-permute-done.refs_5_.refs_13_) | copy-start | bytes 1769476
  21.5 17.0 %collective-permute-start.5 = (bf16[32,9216]{1,0:T(8,128)(2,1)S(1)}, bf16[32,9216]{1,0:T(8,128)(2,1)S(1)}, u32[]{:S(2)}, u32[]{:S(2)}) collective-permute-start(bf16[32,9216]{1,0:T(8,128)(2,1)S(1)} %collective-permute-done.4.refs_10_.refs_18_), channel_id=1, source_target_pairs={{0,1},{1,0},{2,3},{3,2},{4,5},{5,4},{6,7},{7,6},{8,9},{9,8},{10,11... | collective-permute-start | bytes 1769480 | tf_op jit(solution)/shard_map/ppermute | solution.py:144
  21.8 62.8 %copy-start.2 = (bf16[32,9216]{1,0:T(8,128)(2,1)}, bf16[32,9216]{1,0:T(8,128)(2,1)S(1)}, u32[]{:S(2)}) copy-start(bf16[32,9216]{1,0:T(8,128)(2,1)S(1)} %collective-permute-done.2.refs_8_.refs_16_) | copy-start | bytes 1769476
  21.8 16.8 %collective-permute-start.8 = (bf16[32,9216]{1,0:T(8,128)(2,1)S(1)}, bf16[32,9216]{1,0:T(8,128)(2,1)S(1)}, u32[]{:S(2)}, u32[]{:S(2)}) collective-permute-start(bf16[32,9216]{1,0:T(8,128)(2,1)S(1)} %collective-permute-done.4.refs_10_.refs_18_), channel_id=1, source_target_pairs={{0,2},{1,3},{2,0},{3,1},{4,6},{5,7},{6,4},{7,5},{8,10},{9,11},{10,... | collective-permute-start | bytes 1769480 | tf_op jit(solution)/shard_map/ppermute | solution.py:144
  34.5 2.0 %collective-permute-start.3 = (bf16[32,9216]{1,0:T(8,128)(2,1)S(1)}, bf16[32,9216]{1,0:T(8,128)(2,1)S(1)}, u32[]{:S(2)}, u32[]{:S(2)}) collective-permute-start(bf16[32,9216]{1,0:T(8,128)(2,1)S(1)} %collective-permute-done.2.refs_8_.refs_16_), channel_id=1, source_target_pairs={{0,1},{1,0},{2,3},{3,2},{4,5},{5,4},{6,7},{7,6},{8,9},{9,8},{10,11... | collective-permute-start | bytes 1769480 | tf_op jit(solution)/shard_map/ppermute | solution.py:144
  34.5 7.0 %collective-permute-start.11 = (bf16[16,9216]{1,0:T(8,128)(2,1)S(1)}, bf16[16,9216]{1,0:T(8,128)(2,1)S(1)}, u32[]{:S(2)}, u32[]{:S(2)}) collective-permute-start(bf16[16,9216]{1,0:T(8,128)(2,1)S(1)} %collective-permute-done.10.refs_8_.refs_18_), channel_id=1, source_target_pairs={{0,1},{1,0},{2,3},{3,2},{4,5},{5,4},{6,7},{7,6},{8,9},{9,8},{10,11... | collective-permute-start | bytes 884744 | tf_op jit(solution)/shard_map/ppermute | solution.py:144
  35.9 15.0 %collective-permute-start.7 = (bf16[32,9216]{1,0:T(8,128)(2,1)S(1)}, bf16[32,9216]{1,0:T(8,128)(2,1)S(1)}, u32[]{:S(2)}, u32[]{:S(2)}) collective-permute-start(bf16[32,9216]{1,0:T(8,128)(2,1)S(1)} %collective-permute-done.6.refs_4_.refs_14_), channel_id=1, source_target_pairs={{0,1},{1,0},{2,3},{3,2},{4,5},{5,4},{6,7},{7,6},{8,9},{9,8},{10,11... | collective-permute-start | bytes 1769480 | tf_op jit(solution)/shard_map/ppermute | solution.py:144
  37.3 9.0 %collective-permute-start.12 = (bf16[16,9216]{1,0:T(8,128)(2,1)S(1)}, bf16[16,9216]{1,0:T(8,128)(2,1)S(1)}, u32[]{:S(2)}, u32[]{:S(2)}) collective-permute-start(bf16[16,9216]{1,0:T(8,128)(2,1)S(1)} %slice.27), channel_id=1, source_target_pairs={{0,16},{1,17},{2,18},{3,19},{4,20},{5,21},{6,22},{7,23},{8,24},{9,... | collective-permute-start | bytes 884744 | tf_op jit(solution)/shard_map/ppermute | solution.py:144
  38.6 46.0 %copy-start.4 = (bf16[32,9216]{1,0:T(8,128)(2,1)}, bf16[32,9216]{1,0:T(8,128)(2,1)S(1)}, u32[]{:S(2)}) copy-start(bf16[32,9216]{1,0:T(8,128)(2,1)S(1)} %collective-permute-done.8.refs_6_.refs_16_) | copy-start | bytes 1769476
  38.6 13.9 %collective-permute-start.9 = (bf16[32,9216]{1,0:T(8,128)(2,1)S(1)}, bf16[32,9216]{1,0:T(8,128)(2,1)S(1)}, u32[]{:S(2)}, u32[]{:S(2)}) collective-permute-start(bf16[32,9216]{1,0:T(8,128)(2,1)S(1)} %collective-permute-done.8.refs_6_.refs_16_), channel_id=1, source_target_pairs={{0,1},{1,0},{2,3},{3,2},{4,5},{5,4},{6,7},{7,6},{8,9},{9,8},{10,11... | collective-permute-start | bytes 1769480 | tf_op jit(solution)/shard_map/ppermute | solution.py:144
  39.4 10.7 %collective-permute-start.20 = (bf16[16,9216]{1,0:T(8,128)(2,1)S(1)}, bf16[16,9216]{1,0:T(8,128)(2,1)S(1)}, u32[]{:S(2)}, u32[]{:S(2)}) collective-permute-start(bf16[16,9216]{1,0:T(8,128)(2,1)S(1)} %slice_bitcast_fusion), channel_id=1, source_target_pairs={{0,4},{1,5},{2,6},{3,7},{4,12},{5,13},{6,14},{7,15},{8,0},{9,1},{1... | collective-permute-start | bytes 884744 | tf_op jit(solution)/shard_map/ppermute | solution.py:144
  42.3 20.1 %collective-permute-start.16 = (bf16[32,9216]{1,0:T(8,128)(2,1)S(1)}, bf16[32,9216]{1,0:T(8,128)(2,1)S(1)}, u32[]{:S(2)}, u32[]{:S(2)}) collective-permute-start(bf16[32,9216]{1,0:T(8,128)(2,1)S(1)} %collective-permute-done.6.refs_4_.refs_14_), channel_id=1, source_target_pairs={{0,4},{1,5},{2,6},{3,7},{4,12},{5,13},{6,14},{7,15},{8,0},{9,1},{1... | collective-permute-start | bytes 1769480 | tf_op jit(solution)/shard_map/ppermute | solution.py:144
  46.4 19.2 %collective-permute-start.14 = (bf16[32,9216]{1,0:T(8,128)(2,1)S(1)}, bf16[32,9216]{1,0:T(8,128)(2,1)}, u32[]{:S(2)}, u32[]{:S(2)}) collective-permute-start(bf16[32,9216]{1,0:T(8,128)(2,1)S(1)} %collective-permute-done.6.refs_4_.refs_14_), channel_id=1, source_target_pairs={{0,2},{1,3},{2,0},{3,1},{4,6},{5,7},{6,4},{7,5},{8,10},{9,11},{10,... | collective-permute-start | bytes 1769480 | tf_op jit(solution)/shard_map/ppermute | solution.py:144
  50.1 17.6 %collective-permute-start.24 = (bf16[32,9216]{1,0:T(8,128)(2,1)S(1)}, bf16[32,9216]{1,0:T(8,128)(2,1)}, u32[]{:S(2)}, u32[]{:S(2)}) collective-permute-start(bf16[32,9216]{1,0:T(8,128)(2,1)S(1)} %collective-permute-done.8.refs_6_.refs_16_), channel_id=1, source_target_pairs={{0,16},{1,17},{2,18},{3,19},{4,20},{5,21},{6,22},{7,23},{8,24},{9,... | collective-permute-start | bytes 1769480 | tf_op jit(solution)/shard_map/ppermute | solution.py:144
  51.7 12.6 %collective-permute-start.13 = (bf16[16,9216]{1,0:T(8,128)(2,1)S(1)}, bf16[16,9216]{1,0:T(8,128)(2,1)S(1)}, u32[]{:S(2)}, u32[]{:S(2)}) collective-permute-start(bf16[16,9216]{1,0:T(8,128)(2,1)S(1)} %collective-permute-done.12.refs_10_.refs_20_), channel_id=1, source_target_pairs={{0,1},{1,0},{2,3},{3,2},{4,5},{5,4},{6,7},{7,6},{8,9},{9,8},{10,11... | collective-permute-start | bytes 884744 | tf_op jit(solution)/shard_map/ppermute | solution.py:144
  53.3 12.3 %collective-permute-start.21 = (bf16[16,9216]{1,0:T(8,128)(2,1)S(1)}, bf16[16,9216]{1,0:T(8,128)(2,1)S(1)}, u32[]{:S(2)}, u32[]{:S(2)}) collective-permute-start(bf16[16,9216]{1,0:T(8,128)(2,1)S(1)} %collective-permute-done.20.refs_8_.refs_18_), channel_id=1, source_target_pairs={{0,1},{1,0},{2,3},{3,2},{4,5},{5,4},{6,7},{7,6},{8,9},{9,8},{10,11... | collective-permute-start | bytes 884744 | tf_op jit(solution)/shard_map/ppermute | solution.py:144
  62.4 9.5 %collective-permute-start.26 = (bf16[16,9216]{1,0:T(8,128)(2,1)S(1)}, bf16[16,9216]{1,0:T(8,128)(2,1)S(1)}, u32[]{:S(2)}, u32[]{:S(2)}) collective-permute-start(bf16[16,9216]{1,0:T(8,128)(2,1)S(1)} %collective-permute-done.20.refs_8_.refs_18_), channel_id=1, source_target_pairs={{0,4},{1,5},{2,6},{3,7},{4,12},{5,13},{6,14},{7,15},{8,0},{9,1},{1... | collective-permute-start | bytes 884744 | tf_op jit(solution)/shard_map/ppermute | solution.py:144
  64.3 38.6 %copy-start.39 = (s32[4]{0:T(128)S(1)}, s32[4]{0:T(128)}, u32[]{:S(2)}) copy-start(s32[4]{0:T(128)} %constant.150.clone) | copy-start | bytes 52
  64.3 46.7 %copy-start.40 = (s32[512,1]{0,1:T(1,128)S(1)}, s32[512,1]{0,1:T(1,128)}, u32[]{:S(2)}) copy-start(s32[512,1]{0,1:T(1,128)} %param.9) | copy-start | bytes 6148
  64.3 46.7 %copy-start.41 = (s32[64]{0:T(128)S(1)}, s32[64]{0:T(128)}, u32[]{:S(2)}) copy-start(s32[64]{0:T(128)} %param.10) | copy-start | bytes 772
  65.1 8.4 %collective-permute-start.18 = (bf16[16,9216]{1,0:T(8,128)(2,1)S(1)}, bf16[16,9216]{1,0:T(8,128)(2,1)S(1)}, u32[]{:S(2)}, u32[]{:S(2)}) collective-permute-start(bf16[16,9216]{1,0:T(8,128)(2,1)S(1)} %slice.28), channel_id=1, source_target_pairs={{0,16},{1,17},{2,18},{3,19},{4,20},{5,21},{6,22},{7,23},{8,24},{9,... | collective-permute-start | bytes 884744 | tf_op jit(solution)/shard_map/ppermute | solution.py:144
  65.6 17.6 %collective-permute-start.15 = (bf16[32,9216]{1,0:T(8,128)(2,1)}, bf16[32,9216]{1,0:T(8,128)(2,1)S(1)}, u32[]{:S(2)}, u32[]{:S(2)}) collective-permute-start(bf16[32,9216]{1,0:T(8,128)(2,1)} %collective-permute-done.14.refs_12_.refs_22_), channel_id=1, source_target_pairs={{0,1},{1,0},{2,3},{3,2},{4,5},{5,4},{6,7},{7,6},{8,9},{9,8},{10,11... | collective-permute-start | bytes 1769480 | tf_op jit(solution)/shard_map/ppermute | solution.py:144
  66.3 17.8 %collective-permute-start.22 = (bf16[32,9216]{1,0:T(8,128)(2,1)S(1)}, bf16[32,9216]{1,0:T(8,128)(2,1)}, u32[]{:S(2)}, u32[]{:S(2)}) collective-permute-start(bf16[32,9216]{1,0:T(8,128)(2,1)S(1)} %collective-permute-done.16.refs_4_.refs_14_), channel_id=1, source_target_pairs={{0,2},{1,3},{2,0},{3,1},{4,6},{5,7},{6,4},{7,5},{8,10},{9,11},{10,... | collective-permute-start | bytes 1769480 | tf_op jit(solution)/shard_map/ppermute | solution.py:144
  67.8 16.8 %collective-permute-start.17 = (bf16[32,9216]{1,0:T(8,128)(2,1)S(1)}, bf16[32,9216]{1,0:T(8,128)(2,1)S(1)}, u32[]{:S(2)}, u32[]{:S(2)}) collective-permute-start(bf16[32,9216]{1,0:T(8,128)(2,1)S(1)} %collective-permute-done.16.refs_4_.refs_14_), channel_id=1, source_target_pairs={{0,1},{1,0},{2,3},{3,2},{4,5},{5,4},{6,7},{7,6},{8,9},{9,8},{10,11... | collective-permute-start | bytes 1769480 | tf_op jit(solution)/shard_map/ppermute | solution.py:144
  71.9 12.7 %copy-start.26 = (bf16[16,9216]{1,0:T(8,128)(2,1)}, bf16[16,9216]{1,0:T(8,128)(2,1)S(1)}, u32[]{:S(2)}) copy-start(bf16[16,9216]{1,0:T(8,128)(2,1)S(1)} %collective-permute-done.26.refs_4_.refs_14_) | copy-start | bytes 884740
  71.9 8.6 %collective-permute-start.28 = (bf16[16,9216]{1,0:T(8,128)(2,1)S(1)}, bf16[16,9216]{1,0:T(8,128)(2,1)S(1)}, u32[]{:S(2)}, u32[]{:S(2)}) collective-permute-start(bf16[16,9216]{1,0:T(8,128)(2,1)S(1)} %collective-permute-done.26.refs_4_.refs_14_), channel_id=1, source_target_pairs={{0,4},{1,5},{2,6},{3,7},{4,12},{5,13},{6,14},{7,15},{8,0},{9,1},{1... | collective-permute-start | bytes 884744 | tf_op jit(solution)/shard_map/ppermute | solution.py:144
  73.5 8.5 %collective-permute-start.19 = (bf16[16,9216]{1,0:T(8,128)(2,1)S(1)}, bf16[16,9216]{1,0:T(8,128)(2,1)S(1)}, u32[]{:S(2)}, u32[]{:S(2)}) collective-permute-start(bf16[16,9216]{1,0:T(8,128)(2,1)S(1)} %collective-permute-done.18.refs_6_.refs_16_), channel_id=1, source_target_pairs={{0,1},{1,0},{2,3},{3,2},{4,5},{5,4},{6,7},{7,6},{8,9},{9,8},{10,11... | collective-permute-start | bytes 884744 | tf_op jit(solution)/shard_map/ppermute | solution.py:144
  80.5 4.1 %copy-start.34 = (bf16[16,9216]{1,0:T(8,128)(2,1)}, bf16[16,9216]{1,0:T(8,128)(2,1)S(1)}, u32[]{:S(2)}) copy-start(bf16[16,9216]{1,0:T(8,128)(2,1)S(1)} %collective-permute-done.28.refs_6_.refs_16_) | copy-start | bytes 884740
  80.5 32.0 %collective-permute-start.32 = (bf16[32,9216]{1,0:T(8,128)(2,1)S(1)}, bf16[32,9216]{1,0:T(8,128)(2,1)}, u32[]{:S(2)}, u32[]{:S(2)}) collective-permute-start(bf16[32,9216]{1,0:T(8,128)(2,1)S(1)} %bitcast.78), channel_id=1, source_target_pairs={{0,2},{1,3},{2,0},{3,1},{4,6},{5,7},{6,4},{7,5},{8,10},{9,11},{10,... | collective-permute-start | bytes 1769480 | tf_op jit(solution)/shard_map/ppermute | solution.py:144
  82.7 29.7 %collective-permute-start.30 = (bf16[32,9216]{1,0:T(8,128)(2,1)}, bf16[32,9216]{1,0:T(8,128)(2,1)}, u32[]{:S(2)}, u32[]{:S(2)}) collective-permute-start(bf16[32,9216]{1,0:T(8,128)(2,1)} %collective-permute-done.14.refs_12_.refs_22_), channel_id=1, source_target_pairs={{0,16},{1,17},{2,18},{3,19},{4,20},{5,21},{6,22},{7,23},{8,24},{9,... | collective-permute-start | bytes 1769480 | tf_op jit(solution)/shard_map/ppermute | solution.py:144
  84.0 43.8 %collective-permute-start.25 = (bf16[32,9216]{1,0:T(8,128)(2,1)}, bf16[32,9216]{1,0:T(8,128)(2,1)}, u32[]{:S(2)}, u32[]{:S(2)}) collective-permute-start(bf16[32,9216]{1,0:T(8,128)(2,1)} %collective-permute-done.24.refs_12_.refs_22_), channel_id=1, source_target_pairs={{0,1},{1,0},{2,3},{3,2},{4,5},{5,4},{6,7},{7,6},{8,9},{9,8},{10,11... | collective-permute-start | bytes 1769480 | tf_op jit(solution)/shard_map/ppermute | solution.py:144
  84.0 44.3 %collective-permute-start.23 = (bf16[32,9216]{1,0:T(8,128)(2,1)}, bf16[32,9216]{1,0:T(8,128)(2,1)}, u32[]{:S(2)}, u32[]{:S(2)}) collective-permute-start(bf16[32,9216]{1,0:T(8,128)(2,1)} %collective-permute-done.22.refs_10_.refs_20_), channel_id=1, source_target_pairs={{0,1},{1,0},{2,3},{3,2},{4,5},{5,4},{6,7},{7,6},{8,9},{9,8},{10,11... | collective-permute-start | bytes 1769480 | tf_op jit(solution)/shard_map/ppermute | solution.py:144
  85.5 27.5 %collective-permute-start.34 = (bf16[32,9216]{1,0:T(8,128)(2,1)}, bf16[32,9216]{1,0:T(8,128)(2,1)}, u32[]{:S(2)}, u32[]{:S(2)}) collective-permute-start(bf16[32,9216]{1,0:T(8,128)(2,1)} %collective-permute-done.22.refs_10_.refs_20_), channel_id=1, source_target_pairs={{0,16},{1,17},{2,18},{3,19},{4,20},{5,21},{6,22},{7,23},{8,24},{9,... | collective-permute-start | bytes 1769480 | tf_op jit(solution)/shard_map/ppermute | solution.py:144
  112.3 34.7 %collective-permute-start.31 = (bf16[32,9216]{1,0:T(8,128)(2,1)}, bf16[32,9216]{1,0:T(8,128)(2,1)S(1)}, u32[]{:S(2)}, u32[]{:S(2)}) collective-permute-start(bf16[32,9216]{1,0:T(8,128)(2,1)} %collective-permute-done.30.refs_8_.refs_18_), channel_id=1, source_target_pairs={{0,1},{1,0},{2,3},{3,2},{4,5},{5,4},{6,7},{7,6},{8,9},{9,8},{10,11... | collective-permute-start | bytes 1769480 | tf_op jit(solution)/shard_map/ppermute | solution.py:144
  112.4 34.7 %collective-permute-start.33 = (bf16[32,9216]{1,0:T(8,128)(2,1)}, bf16[32,9216]{1,0:T(8,128)(2,1)S(1)}, u32[]{:S(2)}, u32[]{:S(2)}) collective-permute-start(bf16[32,9216]{1,0:T(8,128)(2,1)} %collective-permute-done.32.refs_10_.refs_20_), channel_id=1, source_target_pairs={{0,1},{1,0},{2,3},{3,2},{4,5},{5,4},{6,7},{7,6},{8,9},{9,8},{10,11... | collective-permute-start | bytes 1769480 | tf_op jit(solution)/shard_map/ppermute | solution.py:144
  112.9 34.2 %collective-permute-start.35 = (bf16[32,9216]{1,0:T(8,128)(2,1)}, bf16[32,9216]{1,0:T(8,128)(2,1)S(1)}, u32[]{:S(2)}, u32[]{:S(2)}) collective-permute-start(bf16[32,9216]{1,0:T(8,128)(2,1)} %collective-permute-done.34.refs_12_.refs_22_), channel_id=1, source_target_pairs={{0,1},{1,0},{2,3},{3,2},{4,5},{5,4},{6,7},{7,6},{8,9},{9,8},{10,11... | collective-permute-start | bytes 1769480 | tf_op jit(solution)/shard_map/ppermute | solution.py:144
  113.0 1.1 copy-start.1
  114.1 1.1 copy-start.3
  115.1 1.1 copy-start.7
  116.2 1.1 copy-start.9
  117.3 1.1 copy-start.13
  118.3 9.5 %copy-start.27 = (bf16[16,9216]{1,0:T(8,128)(2,1)S(1)}, bf16[16,9216]{1,0:T(8,128)(2,1)}, u32[]{:S(2)}) copy-start(bf16[16,9216]{1,0:T(8,128)(2,1)} %copy-done.26) | copy-start | bytes 884740
  118.3 10.0 %copy-start.35 = (bf16[16,9216]{1,0:T(8,128)(2,1)S(1)}, bf16[16,9216]{1,0:T(8,128)(2,1)}, u32[]{:S(2)}) copy-start(bf16[16,9216]{1,0:T(8,128)(2,1)} %copy-done.34) | copy-start | bytes 884740
  118.3 10.1 %copy-start.5 = (bf16[32,9216]{1,0:T(8,128)(2,1)S(1)}, bf16[32,9216]{1,0:T(8,128)(2,1)}, u32[]{:S(2)}) copy-start(bf16[32,9216]{1,0:T(8,128)(2,1)} %copy-done.4) | copy-start | bytes 1769476
  118.3 10.1 %copy-start.11 = (bf16[32,9216]{1,0:T(8,128)(2,1)S(1)}, bf16[32,9216]{1,0:T(8,128)(2,1)}, u32[]{:S(2)}) copy-start(bf16[32,9216]{1,0:T(8,128)(2,1)} %copy-done.10) | copy-start | bytes 1769476
  118.3 10.1 %copy-start.15 = (bf16[32,9216]{1,0:T(8,128)(2,1)S(1)}, bf16[32,9216]{1,0:T(8,128)(2,1)}, u32[]{:S(2)}) copy-start(bf16[32,9216]{1,0:T(8,128)(2,1)} %copy-done.14) | copy-start | bytes 1769476
  118.4 10.1 %copy-start.17 = (bf16[32,9216]{1,0:T(8,128)(2,1)S(1)}, bf16[32,9216]{1,0:T(8,128)(2,1)}, u32[]{:S(2)}) copy-start(bf16[32,9216]{1,0:T(8,128)(2,1)} %copy-done.16) | copy-start | bytes 1769476
  118.4 10.1 %copy-start.21 = (bf16[16,9216]{1,0:T(8,128)(2,1)S(1)}, bf16[16,9216]{1,0:T(8,128)(2,1)}, u32[]{:S(2)}) copy-start(bf16[16,9216]{1,0:T(8,128)(2,1)} %copy-done.20) | copy-start | bytes 884740
  118.4 10.1 %copy-start.23 = (bf16[16,9216]{1,0:T(8,128)(2,1)S(1)}, bf16[16,9216]{1,0:T(8,128)(2,1)}, u32[]{:S(2)}) copy-start(bf16[16,9216]{1,0:T(8,128)(2,1)} %copy-done.22) | copy-start | bytes 884740
  118.4 10.1 %copy-start.31 = (bf16[16,9216]{1,0:T(8,128)(2,1)S(1)}, bf16[16,9216]{1,0:T(8,128)(2,1)}, u32[]{:S(2)}) copy-start(bf16[16,9216]{1,0:T(8,128)(2,1)} %copy-done.30) | copy-start | bytes 884740
  127.8 10.0 %copy-start.19 = (bf16[32,9216]{1,0:T(8,128)(2,1)S(1)}, bf16[32,9216]{1,0:T(8,128)(2,1)}, u32[]{:S(2)}) copy-start(bf16[32,9216]{1,0:T(8,128)(2,1)} %copy-done.18) | copy-start | bytes 1769476
  127.8 10.0 %copy-start.25 = (bf16[16,9216]{1,0:T(8,128)(2,1)S(1)}, bf16[16,9216]{1,0:T(8,128)(2,1)}, u32[]{:S(2)}) copy-start(bf16[16,9216]{1,0:T(8,128)(2,1)} %copy-done.24) | copy-start | bytes 884740
  127.8 10.0 %copy-start.29 = (bf16[16,9216]{1,0:T(8,128)(2,1)S(1)}, bf16[16,9216]{1,0:T(8,128)(2,1)}, u32[]{:S(2)}) copy-start(bf16[16,9216]{1,0:T(8,128)(2,1)} %copy-done.28) | copy-start | bytes 884740
  127.8 10.0 %copy-start.33 = (bf16[16,9216]{1,0:T(8,128)(2,1)S(1)}, bf16[16,9216]{1,0:T(8,128)(2,1)}, u32[]{:S(2)}) copy-start(bf16[16,9216]{1,0:T(8,128)(2,1)} %copy-done.32) | copy-start | bytes 884740
  127.8 10.0 %copy-start.37 = (bf16[16,9216]{1,0:T(8,128)(2,1)S(1)}, bf16[16,9216]{1,0:T(8,128)(2,1)}, u32[]{:S(2)}) copy-start(bf16[16,9216]{1,0:T(8,128)(2,1)} %copy-done.36) | copy-start | bytes 884740
  127.8 19.3 %collective-permute-start.27 = (bf16[16,9216]{1,0:T(8,128)(2,1)S(1)}, bf16[16,9216]{1,0:T(8,128)(2,1)S(1)}, u32[]{:S(2)}, u32[]{:S(2)}) collective-permute-start(bf16[16,9216]{1,0:T(8,128)(2,1)S(1)} %copy-done.27), channel_id=1, source_target_pairs={{0,1},{1,0},{2,3},{3,2},{4,5},{5,4},{6,7},{7,6},{8,9},{9,8},{10,11... | collective-permute-start | bytes 884744 | tf_op jit(solution)/shard_map/ppermute | solution.py:144
  128.3 18.8 %collective-permute-start.29 = (bf16[16,9216]{1,0:T(8,128)(2,1)S(1)}, bf16[16,9216]{1,0:T(8,128)(2,1)S(1)}, u32[]{:S(2)}, u32[]{:S(2)}) collective-permute-start(bf16[16,9216]{1,0:T(8,128)(2,1)S(1)} %copy-done.35), channel_id=1, source_target_pairs={{0,1},{1,0},{2,3},{3,2},{4,5},{5,4},{6,7},{7,6},{8,9},{9,8},{10,11... | collective-permute-start | bytes 884744 | tf_op jit(solution)/shard_map/ppermute | solution.py:144
  (14 other events, 10.9 us)

commit v3 on v2

v3 whole, which is shorter than its diff:
```python
import functools

import jax
import jax.numpy as jnp
from jax import lax
from jax.experimental import pallas as pl
from jax.experimental.pallas import tpu as pltpu
from jax.sharding import PartitionSpec as P

RING = (0, 1, 3, 2)
PLACE_IN_RING = (0, 1, 3, 2)
DEPTH_TILE = 2048


def slots_of_rows(row_adapter_index, adapter_storage_slot):
    catalog = jnp.arange(adapter_storage_slot.shape[0], dtype=jnp.int32)
    return jnp.sum(
        jnp.where(row_adapter_index == catalog[None, :], adapter_storage_slot[None, :], 0),
        axis=1,
        keepdims=True,
    )


def gathered(
    tokens,
    row_adapter_index,
    adapter_storage_slot,
    base_value_weight,
    adapter_down_weight,
    adapter_up_weight,
):
    adapter_count = adapter_storage_slot.shape[0]
    rank = adapter_down_weight.shape[1]
    slot_of = slots_of_rows(row_adapter_index, adapter_storage_slot)
    down_all = lax.all_gather(
        adapter_down_weight.reshape(-1, adapter_down_weight.shape[2]), "req", axis=0, tiled=True
    )
    up_all = lax.all_gather(
        adapter_up_weight.reshape(-1, adapter_up_weight.shape[2]), "req", axis=0, tiled=True
    )
    base_partial = jnp.dot(tokens, base_value_weight, preferred_element_type=jnp.float32)
    base_output = lax.psum_scatter(base_partial, "tp", scatter_dimension=1, tiled=True)
    shrink = lax.dot_general(
        tokens, down_all, (((1,), (1,)), ((), ())), preferred_element_type=jnp.float32
    )
    column_slot = jnp.arange(adapter_count * rank, dtype=jnp.int32) // rank
    shrink = jnp.where(slot_of == column_slot[None, :], shrink, 0.0)
    shrink = lax.psum(shrink, "tp")
    high = lax.reduce_precision(shrink, 8, 7)
    rest = shrink - high
    middle = lax.reduce_precision(rest, 8, 7)
    low = rest - middle
    lora = sum(
        jnp.dot(piece.astype(jnp.bfloat16), up_all, preferred_element_type=jnp.float32)
        for piece in (low, middle, high)
    )
    return (base_output + lora).astype(jnp.bfloat16)


def absorb_kernel(totals, count, steps, *refs):
    tokens_ref, row_slot_ref, column_slot_ref = refs[:3]
    total_refs, refs = refs[3 : 3 + totals], refs[3 + totals :]
    downs, ups, (out_ref, shrink_ref) = refs[:count], refs[count : 2 * count], refs[2 * count :]
    step = pl.program_id(0)
    part = lax.dot_general(
        tokens_ref[...],
        jnp.concatenate([down[...] for down in downs], axis=0),
        (((1,), (1,)), ((), ())),
        preferred_element_type=jnp.float32,
    )

    @pl.when(step == 0)
    def _():
        shrink_ref[...] = part

    @pl.when(step > 0)
    def _():
        shrink_ref[...] += part

    @pl.when(step == steps - 1)
    def _():
        kept = jnp.where(row_slot_ref[...] == column_slot_ref[...], shrink_ref[...], 0.0)
        high = kept.astype(jnp.bfloat16)
        low = (kept - high.astype(jnp.float32)).astype(jnp.bfloat16)
        up = jnp.concatenate([up[...] for up in ups], axis=0)
        lora = jnp.dot(low, up, preferred_element_type=jnp.float32)
        lora += jnp.dot(high, up, preferred_element_type=jnp.float32)
        total = jnp.concatenate([total[...] for total in total_refs], axis=1)
        out_ref[...] = (total + lora).astype(out_ref.dtype)


def absorb(tokens, row_slot, totals, pieces, out_dtype):
    rows, depth = tokens.shape
    width = sum(total.shape[1] for total in totals)
    block = pieces[0][2]
    columns = block * len(pieces)
    slots = [slot for piece in pieces for slot in piece[3]]
    column_slot = jnp.repeat(jnp.stack(slots).astype(jnp.int32), columns // len(slots))[None, :]
    tile = min(DEPTH_TILE, depth)
    steps = depth // tile
    whole = lambda *shape: pl.BlockSpec(shape, lambda k: (0, 0))

    def down_spec(piece):
        return pl.BlockSpec((block, tile), lambda k: (piece[1], k))

    def up_spec(piece):
        return pl.BlockSpec((block, width), lambda k: (piece[1], depth // width))

    return pl.pallas_call(
        functools.partial(absorb_kernel, len(totals), len(pieces), steps),
        out_shape=jax.ShapeDtypeStruct((rows, width), out_dtype),
        grid=(steps,),
        in_specs=[
            pl.BlockSpec((rows, tile), lambda k: (0, k)),
            whole(rows, 1),
            whole(1, columns),
        ]
        + [whole(*total.shape) for total in totals]
        + [down_spec(piece) for piece in pieces]
        + [up_spec(piece) for piece in pieces],
        out_specs=whole(rows, width),
        scratch_shapes=[pltpu.VMEM((rows, columns), jnp.float32)],
        cost_estimate=pl.CostEstimate(
            flops=2 * rows * columns * (depth + 2 * width),
            bytes_accessed=2 * (rows + columns) * depth + 8 * rows * width,
            transcendentals=0,
        ),
        compiler_params=pltpu.CompilerParams(vmem_limit_bytes=20 * 1024 * 1024),
    )(tokens, row_slot, column_slot, *totals, *[piece[0] for piece in pieces * 2])


def passed_round(
    tokens,
    row_adapter_index,
    adapter_storage_slot,
    base_value_weight,
    adapter_down_weight,
    adapter_up_weight,
):
    held, rank, depth = adapter_down_weight.shape
    axes = ("groups", "req")
    planes, owners = lax.axis_size("groups"), lax.axis_size("req")
    y, at = lax.axis_index("groups"), lax.axis_index("req")
    z, x, core = at // 4, (at // 2) % 2, at % 2
    ring = jnp.array(RING, jnp.int32)
    ring_place = jnp.array(PLACE_IN_RING, jnp.int32)[z]

    def permuted(array, target):
        pairs = [
            (g * owners + r, target(g, r)) for g in range(planes) for r in range(owners)
        ]
        return lax.ppermute(array, axes, pairs)

    def along_z(g, r, by):
        to = RING[(PLACE_IN_RING[r // 4] + by) % 4]
        return g * owners + to * 4 + r % 4

    z_ring = lambda array: permuted(array, lambda g, r: along_z(g, r, 1))
    z_back = lambda array: permuted(array, lambda g, r: along_z(g, r, -1))
    x_swap = lambda array: permuted(array, lambda g, r: g * owners + (r ^ 2))
    y_swap = lambda array: permuted(array, lambda g, r: (1 - g) * owners + r)
    core_swap = lambda array: permuted(array, lambda g, r: g * owners + (r ^ 1))

    own = jnp.concatenate(
        [adapter_down_weight, adapter_up_weight], axis=2
    )
    own = jnp.where(y == 0, own, own[::-1])
    front = own[:2].reshape(2 * rank, -1)
    back = own[2:].reshape(2 * rank, -1)

    def slots(step, other_x, other_y, other_core, units):
        from_z = ring[(ring_place - step) % 4]
        from_x = 1 - x if other_x else x
        from_y = 1 - y if other_y else y
        from_core = 1 - core if other_core else core
        first = held * ((from_z * 2 + from_x) * 2 + from_core)
        return [first + jnp.where(from_y == 0, unit, held - 1 - unit) for unit in units]

    block = 2 * rank
    pair, rest = (0, 1), (2, 3)

    def pieces_of(arrived, batch):
        here = [(array, 0, block, slots(*place[:3], 0, place[3])) for array, place in arrived]
        batch = core_swap(batch)
        there = [
            (batch, number, block, slots(*place[:3], 1, place[3]))
            for number, (_, place) in enumerate(arrived)
        ]
        return here, there

    def joined(*arrived):
        return pieces_of(arrived, jnp.concatenate([array for array, _ in arrived], axis=0))

    row_slot = slots_of_rows(row_adapter_index, adapter_storage_slot)
    half = base_value_weight.shape[1] // 2
    update = functools.partial(absorb, tokens, row_slot)

    z1, x0 = z_ring(front), x_swap(front)
    here_0, there_0 = pieces_of(
        [(front, (0, 0, 0, pair)), (back, (0, 0, 0, rest))], own.reshape(held * rank, -1)
    )
    base_left = jnp.dot(
        tokens, base_value_weight[:, :half], preferred_element_type=jnp.float32
    )
    z1, x0, base_left = lax.optimization_barrier((z1, x0, base_left))

    z2, x1, yx0 = z_ring(z1), x_swap(z1), y_swap(x0)
    here_1, there_1 = joined((z1, (1, 0, 0, pair)), (x0, (0, 1, 0, pair)))
    tokens_late, base_left = lax.optimization_barrier((tokens, base_left))
    base_right = jnp.dot(
        tokens_late, base_value_weight[:, half:], preferred_element_type=jnp.float32
    )
    z2, x1, yx0, front, base_right = lax.optimization_barrier((z2, x1, yx0, front, base_right))

    z3, x2, yz2 = z_back(front), x_swap(z2), y_swap(z2)
    here_2, there_2 = joined((z2, (2, 0, 0, pair)), (x1, (1, 1, 0, pair)), (yx0, (0, 1, 1, pair)))
    total = update([base_left, base_right], here_0 + there_0 + here_1 + there_1, jnp.float32)
    z3, x2, yz2, x1, back, total = lax.optimization_barrier((z3, x2, yz2, x1, back, total))

    zb1, x3, yx1 = z_ring(back), x_swap(z3), y_swap(x1)
    here_3, there_3 = joined((z3, (3, 0, 0, pair)), (x2, (2, 1, 0, pair)), (yz2, (2, 0, 1, pair)))
    total = update([total], here_2 + there_2 + here_3[:1] + there_3[:1], jnp.float32)
    zb1, x3, yx1, yz2, back, total = lax.optimization_barrier((zb1, x3, yx1, yz2, back, total))

    zb3, xyz2, yx3 = z_back(back), x_swap(yz2), y_swap(x3)
    here_4, there_4 = joined((zb1, (1, 0, 0, rest)), (x3, (3, 1, 0, pair)), (yx1, (1, 1, 1, pair)))
    total = update(
        [total], here_3[1:] + there_3[1:] + here_4[:2] + there_4[:2], jnp.float32
    )
    zb3, xyz2, yx3, total = lax.optimization_barrier((zb3, xyz2, yx3, total))

    pieces = here_4[2:] + there_4[2:]
    for array, place in (
        (zb3, (3, 0, 0, rest)),
        (xyz2, (2, 1, 1, pair)),
        (yx3, (3, 1, 1, pair)),
    ):
        here, there = pieces_of([(array, place)], array)
        pieces += here + there
    return update([total], pieces, jnp.bfloat16)


def solution(mesh):
    placed = (
        P(("groups", "req"), "tp"),
        P(("groups", "req"), None),
        P(),
        P("tp", None),
        P("req", None, "tp"),
        P("req", None, "tp"),
    )
    sizes = mesh.shape
    small = sizes["groups"] == 2 and sizes["req"] == 16 and sizes["tp"] == 1
    return jax.shard_map(
        passed_round if small else gathered,
        mesh=mesh,
        in_specs=placed,
        out_specs=P(("groups", "req"), "tp"),
        check_vma=False,
    )
```

time: 157 us -> 128 us (0.82)
  waiting for transfers between devices: 48.8 us -> 9.18 us
  local copies, waits for them, and re-layouts: 20.2 us -> 31.9 us
  Pallas kernels: 36.9 us -> 27.4 us
  other arithmetic: 0.29 us -> 9.19 us
  starting transfers between devices: 26.7 us -> 20.3 us
  matrix products: 15.9 us -> 21.9 us
    ppermute x36 -> x22, waiting for transfers between devices: 48.8 us -> 9.18 us  [permuted(): return lax.ppermute(array, axes, pairs)]
    unnamed x85 -> x61, local copies, waits for them, and re-layouts: 17.6 us -> 27.1 us
    pallas_call x4, Pallas kernels: 36.9 us -> 27.4 us  [absorb(): pl.pallas_call(functools.partial(absorb_kernel, len(totals), len(pieces),...]
    concatenate x0 -> x4, other arithmetic: none -> 7.83 us  [joined(): jnp.concatenate([array for array, _ in arrived], axis=0)]
    ppermute x36 -> x22, starting transfers between devices: 26.7 us -> 20.3 us  [permuted(): return lax.ppermute(array, axes, pairs)]
    dot_general x1 -> x2, matrix products: 15.9 us -> 21.9 us  [the longest x1 11.4 us: passed_round(): jnp.dot(tokens, base_value_weight[:, :half], preferred_element_type=jnp.f...]
    slice x1, local copies, waits for them, and re-layouts: 0.08 us -> 2.34 us  [passed_round(): back = own[2:].reshape(2 * rank, -1)]
  transfers between devices with their start and end apart: 36 -> 22, of which waited for: 9 -> 9; matrix products, arithmetic and copies ran while one was open for 12% -> 23% of each run, Pallas kernels for 18% -> 16%
where the time goes in v3:
time: 128 us; the launch traced here: 127 us
  local copies, waits for them, and re-layouts  31.9 us (25%)
  Pallas kernels  27.4 us (21%)
  matrix products  21.9 us (17%)
  starting transfers between devices  20.3 us (16%)
  other arithmetic  9.19 us (7%)
  waiting for transfers between devices  9.18 us (7%)
  between operations  7.24 us (6%)
    pallas_call x4, Pallas kernels, absorb(): pl.pallas_call(functools.partial(absorb_kernel, len(totals), len(pieces),...  27.4 us
    unnamed x61, local copies, waits for them, and re-layouts  27.1 us
    ppermute x22, starting transfers between devices, permuted(): return lax.ppermute(array, axes, pairs)  20.3 us
    dot_general x1, matrix products, passed_round(): jnp.dot(tokens, base_value_weight[:, :half], preferred_element_type=jnp.f...  11.4 us
    dot_general x1, matrix products, passed_round(): jnp.dot(tokens_late, base_value_weight[:, half:], preferred_element_type=...  10.5 us
    ppermute x22, waiting for transfers between devices, permuted(): return lax.ppermute(array, axes, pairs)  9.18 us
    concatenate x4, other arithmetic, joined(): jnp.concatenate([array for array, _ in arrived], axis=0)  7.83 us
  transfers between devices with their start and end apart: 22, of which 9 were waited for; matrix products, arithmetic and copies ran while one was open for 23% of the time, Pallas kernels for 16%

profile of v3, /device:TPU:0, one launch (start us, length us, event | category | flops | bytes accessed | tf_op | source)
XLA Modules:
  0.0 127.1 jit_solution(117209322163441389)
XLA Ops:
  0.0 1.3 %constant_dynamic-update-slice_fusion.1 = bf16[4,16,9216]{2,1,0:T(8,128)(2,1)S(1)} fusion(bf16[4,16,8192]{2,1,0:T(8,128)(2,1)} %param.12), kind=kLoop, calls=%fused_computation.12 | loop fusion | bytes 2097152
  1.4 1.3 reverse_select_fusion
  2.6 2.3 %fusion.4 = (bf16[2,16,9216]{2,1,0:T(8,128)(2,1)}, bf16[2,16,9216]{2,1,0:T(8,128)(2,1)}) fusion(bf16[4,16,9216]{2,1,0:T(8,128)(2,1)} %reverse_select_fusion), kind=kLoop, calls=%fused_computation.13 | loop fusion | bytes 2359296 | tf_op jit(solution)/shard_map/slice | solution.py:169
  5.0 3.0 %collective-permute-start = (bf16[32,9216]{1,0:T(8,128)(2,1)}, bf16[32,9216]{1,0:T(8,128)(2,1)S(1)}, u32[]{:S(2)}, u32[]{:S(2)}) collective-permute-start(bf16[32,9216]{1,0:T(8,128)(2,1)} %bitcast.22.refs_5_.refs_13_), channel_id=1, source_target_pairs={{0,4},{1,5},{2,6},{3,7},{4,12},{5,13},{6,14},{7,15},{8,0},{9,1},{1... | collective-permute-start | bytes 1769480 | tf_op jit(solution)/shard_map/ppermute | solution.py:152
  8.0 1.5 %collective-permute-start.1 = (bf16[32,9216]{1,0:T(8,128)(2,1)}, bf16[32,9216]{1,0:T(8,128)(2,1)S(1)}, u32[]{:S(2)}, u32[]{:S(2)}) collective-permute-start(bf16[32,9216]{1,0:T(8,128)(2,1)} %bitcast.22.refs_5_.refs_13_), channel_id=1, source_target_pairs={{0,2},{1,3},{2,0},{3,1},{4,6},{5,7},{6,4},{7,5},{8,10},{9,11},{10,... | collective-permute-start | bytes 1769480 | tf_op jit(solution)/shard_map/ppermute | solution.py:152
  9.5 11.4 %fusion.2.refs_3_ = f32[512,512]{1,0:T(8,128)} fusion(bf16[512,8192]{1,0:T(8,128)(2,1)} %refs_0_.7, bf16[8192,1024]{1,0:T(8,128)(2,1)} %param.11), kind=kOutput, calls=%fused_computation.2 | convolution fusion | flops 4294967296 | bytes 17825792 | tf_op jit(solution)/shard_map/dot_general | solution.py:202
  20.9 0.7 dynamic_slice.10
  25.8 0.7 fusion.5
  27.8 0.1 stack.237
  27.9 0.1 broadcast_in_dim_reshape.13.refs_2_
  28.0 0.1 select_reduce_fusion
  28.1 0.1 copy.16.refs_1_
  28.3 2.6 %collective-permute-start.2 = (bf16[32,9216]{1,0:T(8,128)(2,1)S(1)}, bf16[32,9216]{1,0:T(8,128)(2,1)S(1)}, u32[]{:S(2)}, u32[]{:S(2)}) collective-permute-start(bf16[32,9216]{1,0:T(8,128)(2,1)S(1)} %collective-permute-done.refs_9_.refs_17_), channel_id=1, source_target_pairs={{0,4},{1,5},{2,6},{3,7},{4,12},{5,13},{6,14},{7,15},{8,0},{9,1},{1... | collective-permute-start | bytes 1769480 | tf_op jit(solution)/shard_map/ppermute | solution.py:152
  31.0 0.5 collective-permute-start.3
  31.5 1.5 %collective-permute-start.4 = (bf16[32,9216]{1,0:T(8,128)(2,1)S(1)}, bf16[32,9216]{1,0:T(8,128)(2,1)S(1)}, u32[]{:S(2)}, u32[]{:S(2)}) collective-permute-start(bf16[32,9216]{1,0:T(8,128)(2,1)S(1)} %collective-permute-done.1.refs_10_.refs_18_), channel_id=1, source_target_pairs={{0,16},{1,17},{2,18},{3,19},{4,20},{5,21},{6,22},{7,23},{8,24},{9,... | collective-permute-start | bytes 1769480 | tf_op jit(solution)/shard_map/ppermute | solution.py:152
  33.2 10.5 %fusion.refs_4_ = f32[512,512]{1,0:T(8,128)S(1)} fusion(bf16[512,8192]{1,0:T(8,128)(2,1)} %refs_0_.7, bf16[8192,1024]{1,0:T(8,128)(2,1)} %param.11), kind=kOutput, calls=%fused_computation | convolution fusion | flops 4294967296 | bytes 17825792 | tf_op jit(solution)/shard_map/dot_general | solution.py:210
  43.7 1.3 %collective-permute-done.2.refs_4_.refs_12_ = bf16[32,9216]{1,0:T(8,128)(2,1)S(1)} collective-permute-done((bf16[32,9216]{1,0:T(8,128)(2,1)S(1)}, bf16[32,9216]{1,0:T(8,128)(2,1)S(1)}, u32[]{:S(2)}, u32[]{:S(2)}) %collective-permute-start.2) | collective-permute-done | bytes 589856 | tf_op jit(solution)/shard_map/ppermute | solution.py:152
  45.0 1.5 %collective-permute-done.3.refs_5_.refs_13_ = bf16[32,9216]{1,0:T(8,128)(2,1)} collective-permute-done((bf16[32,9216]{1,0:T(8,128)(2,1)S(1)}, bf16[32,9216]{1,0:T(8,128)(2,1)}, u32[]{:S(2)}, u32[]{:S(2)}) %collective-permute-start.3) | collective-permute-done | bytes 589856 | tf_op jit(solution)/shard_map/ppermute | solution.py:152
  46.5 0.1 collective-permute-done.4.refs_6_.refs_14_
  46.7 1.5 %collective-permute-start.6 = (bf16[32,9216]{1,0:T(8,128)(2,1)S(1)}, bf16[32,9216]{1,0:T(8,128)(2,1)S(1)}, u32[]{:S(2)}, u32[]{:S(2)}) collective-permute-start(bf16[32,9216]{1,0:T(8,128)(2,1)S(1)} %collective-permute-done.2.refs_4_.refs_12_), channel_id=1, source_target_pairs={{0,2},{1,3},{2,0},{3,1},{4,6},{5,7},{6,4},{7,5},{8,10},{9,11},{10,... | collective-permute-start | bytes 1769480 | tf_op jit(solution)/shard_map/ppermute | solution.py:152
  48.2 1.5 %collective-permute-start.7 = (bf16[32,9216]{1,0:T(8,128)(2,1)S(1)}, bf16[32,9216]{1,0:T(8,128)(2,1)}, u32[]{:S(2)}, u32[]{:S(2)}) collective-permute-start(bf16[32,9216]{1,0:T(8,128)(2,1)S(1)} %collective-permute-done.2.refs_4_.refs_12_), channel_id=1, source_target_pairs={{0,16},{1,17},{2,18},{3,19},{4,20},{5,21},{6,22},{7,23},{8,24},{9,... | collective-permute-start | bytes 1769480 | tf_op jit(solution)/shard_map/ppermute | solution.py:152
  49.7 0.3 collective-permute-start.5
  50.0 2.4 %pad_maximum_fusion = bf16[96,9216]{1,0:T(8,128)(2,1)} fusion(bf16[32,9216]{1,0:T(8,128)(2,1)S(1)} %collective-permute-done.4.refs_6_.refs_14_, bf16[32,9216]{1,0:T(8,128)(2,1)} %collective-permute-done.3.refs_5_.refs_13_, bf16[32,9216]{1,0:T(8,128)(2,1)S(1)} %collective-permute-done.2.refs_4_.refs_12_), kind=kLoop, calls=%fused_computation.4 | loop fusion | flops 5308416 | bytes 3538944 | tf_op jit(solution)/shard_map/concatenate | solution.py:192
  52.5 6.7 %shard_map.82.refs_3_ = f32[512,1024]{1,0:T(8,128)S(1)} custom-call(bf16[512,8192]{1,0:T(8,128)(2,1)S(1)} %bitcast.77, s32[512,1]{1,0:T(8,128)S(1)} %copy.16.refs_1_, s32[1,256]{1,0:T(1,128)S(1)} %broadcast_in_dim_reshape.13.refs_2_, f32[512,512]{1,0:T(8,128)S(1)} %copy-done.23, f32[512,512]{1,0:T(8,128)S(1)} %fusion.refs_4_, ...), custom_call_target="tpu_custom_call" | custom-call | flops 2684354560 | bytes 16777216 | tf_op jit(solution)/shard_map/pallas_call | solution.py:109
  59.3 1.3 %copy-done.7 = f32[512,1024]{1,0:T(8,128)} copy-done((f32[512,1024]{1,0:T(8,128)}, f32[512,1024]{1,0:T(8,128)S(1)}, u32[]{:S(2)}) %copy-start.7) | copy-done | bytes 2097176
  60.6 0.6 collective-permute-done.6.refs_4_.refs_12_
  61.2 1.1 collective-permute-done.7.refs_5_.refs_13_
  62.3 1.4 %collective-permute-done.5.refs_10_.refs_18_ = bf16[32,9216]{1,0:T(8,128)(2,1)} collective-permute-done((bf16[32,9216]{1,0:T(8,128)(2,1)}, bf16[32,9216]{1,0:T(8,128)(2,1)}, u32[]{:S(2)}, u32[]{:S(2)}) %collective-permute-start.5) | collective-permute-done | bytes 589856 | tf_op jit(solution)/shard_map/ppermute | solution.py:152
  63.8 2.6 %pad_maximum_fusion.1 = bf16[96,9216]{1,0:T(8,128)(2,1)} fusion(bf16[32,9216]{1,0:T(8,128)(2,1)} %collective-permute-done.7.refs_5_.refs_13_, bf16[32,9216]{1,0:T(8,128)(2,1)S(1)} %collective-permute-done.6.refs_4_.refs_12_, bf16[32,9216]{1,0:T(8,128)(2,1)} %collective-permute-done.5.refs_10_.refs_18_), kind=kLoop, calls=%fused_computation.5 | loop fusion | flops 5308416 | bytes 3538944 | tf_op jit(solution)/shard_map/concatenate | solution.py:192
  66.4 0.8 copy-done.13
  67.2 0.7 collective-permute-start.11
  67.9 1.6 %collective-permute-start.10 = (bf16[32,9216]{1,0:T(8,128)(2,1)}, bf16[32,9216]{1,0:T(8,128)(2,1)}, u32[]{:S(2)}, u32[]{:S(2)}) collective-permute-start(bf16[32,9216]{1,0:T(8,128)(2,1)} %bitcast.23.refs_6_.refs_14_), channel_id=1, source_target_pairs={{0,4},{1,5},{2,6},{3,7},{4,12},{5,13},{6,14},{7,15},{8,0},{9,1},{1... | collective-permute-start | bytes 1769480 | tf_op jit(solution)/shard_map/ppermute | solution.py:152
  69.5 0.5 collective-permute-start.12
  71.3 0.1 stack.254
  71.5 0.1 broadcast_in_dim_reshape.14.refs_2_
  71.6 3.4 %copy-done = bf16[512,8192]{1,0:T(8,128)(2,1)S(1)} copy-done((bf16[512,8192]{1,0:T(8,128)(2,1)S(1)}, bf16[512,8192]{1,0:T(8,128)(2,1)}, u32[]{:S(2)}) %copy-start) | copy-done | bytes 8388632
  75.0 1.6 %copy-done.8 = f32[512,1024]{1,0:T(8,128)S(1)} copy-done((f32[512,1024]{1,0:T(8,128)S(1)}, f32[512,1024]{1,0:T(8,128)}, u32[]{:S(2)}) %copy-start.8) | copy-done | bytes 2097176
  76.6 0.9 copy-done.10
  77.5 1.1 copy-done.16
  78.6 1.1 copy-done.18
  79.7 6.7 %shard_map.83.refs_3_ = f32[512,1024]{1,0:T(8,128)S(1)} custom-call(bf16[512,8192]{1,0:T(8,128)(2,1)S(1)} %copy-done, s32[512,1]{1,0:T(8,128)S(1)} %copy-done.10, s32[1,256]{1,0:T(1,128)S(1)} %broadcast_in_dim_reshape.14.refs_2_, f32[512,1024]{1,0:T(8,128)S(1)} %copy-done.8, bf16[32,9216]{1,0:T(8,128)(2,1)S(1)} %copy-done.16, ...), custom_call_target="tpu_custom_call" | custom-call | flops 2684354560 | bytes 16777216 | tf_op jit(solution)/shard_map/pallas_call | solution.py:109
  86.4 1.3 %copy-done.3 = f32[512,1024]{1,0:T(8,128)} copy-done((f32[512,1024]{1,0:T(8,128)}, f32[512,1024]{1,0:T(8,128)S(1)}, u32[]{:S(2)}) %copy-start.3) | copy-done | bytes 2097176
  87.7 2.8 %pad_maximum_fusion.2 = bf16[96,9216]{1,0:T(8,128)(2,1)} fusion(bf16[32,9216]{1,0:T(8,128)(2,1)} %collective-permute-done.12.refs_4_.refs_12_, bf16[32,9216]{1,0:T(8,128)(2,1)} %collective-permute-done.11.refs_9_.refs_17_, bf16[32,9216]{1,0:T(8,128)(2,1)} %collective-permute-done.10.refs_8_.refs_16_), kind=kLoop, calls=%fused_computation.6 | loop fusion | flops 5308416 | bytes 3538944 | tf_op jit(solution)/shard_map/concatenate | solution.py:192
  90.5 1.3 %collective-permute-start.15 = (bf16[32,9216]{1,0:T(8,128)(2,1)}, bf16[32,9216]{1,0:T(8,128)(2,1)}, u32[]{:S(2)}, u32[]{:S(2)}) collective-permute-start(bf16[32,9216]{1,0:T(8,128)(2,1)} %bitcast.23.refs_6_.refs_14_), channel_id=1, source_target_pairs={{0,8},{1,9},{2,10},{3,11},{4,0},{5,1},{6,2},{7,3},{8,12},{9,13},{1... | collective-permute-start | bytes 1769480 | tf_op jit(solution)/shard_map/ppermute | solution.py:152
  91.8 1.3 %collective-permute-start.16 = (bf16[32,9216]{1,0:T(8,128)(2,1)}, bf16[32,9216]{1,0:T(8,128)(2,1)}, u32[]{:S(2)}, u32[]{:S(2)}) collective-permute-start(bf16[32,9216]{1,0:T(8,128)(2,1)} %collective-permute-done.7.refs_5_.refs_13_), channel_id=1, source_target_pairs={{0,2},{1,3},{2,0},{3,1},{4,6},{5,7},{6,4},{7,5},{8,10},{9,11},{10,... | collective-permute-start | bytes 1769480 | tf_op jit(solution)/shard_map/ppermute | solution.py:152
  93.2 1.5 %collective-permute-start.17 = (bf16[32,9216]{1,0:T(8,128)(2,1)}, bf16[32,9216]{1,0:T(8,128)(2,1)}, u32[]{:S(2)}, u32[]{:S(2)}) collective-permute-start(bf16[32,9216]{1,0:T(8,128)(2,1)} %collective-permute-done.11.refs_9_.refs_17_), channel_id=1, source_target_pairs={{0,16},{1,17},{2,18},{3,19},{4,20},{5,21},{6,22},{7,23},{8,24},{9,... | collective-permute-start | bytes 1769480 | tf_op jit(solution)/shard_map/ppermute | solution.py:152
  94.7 0.1 stack.271
  94.8 0.1 broadcast_in_dim_reshape.15.refs_2_
  94.9 3.4 %copy-done.1 = bf16[512,8192]{1,0:T(8,128)(2,1)S(1)} copy-done((bf16[512,8192]{1,0:T(8,128)(2,1)S(1)}, bf16[512,8192]{1,0:T(8,128)(2,1)}, u32[]{:S(2)}) %copy-start.1) | copy-done | bytes 8388632
  98.3 1.6 %copy-done.4 = f32[512,1024]{1,0:T(8,128)S(1)} copy-done((f32[512,1024]{1,0:T(8,128)S(1)}, f32[512,1024]{1,0:T(8,128)}, u32[]{:S(2)}) %copy-start.4) | copy-done | bytes 2097176
  99.9 0.9 copy-done.11
  100.9 1.1 copy-done.14
  101.9 6.6 %shard_map.84.refs_3_ = f32[512,1024]{1,0:T(8,128)S(1)} custom-call(bf16[512,8192]{1,0:T(8,128)(2,1)S(1)} %copy-done.1, s32[512,1]{1,0:T(8,128)S(1)} %copy-done.11, s32[1,256]{1,0:T(1,128)S(1)} %broadcast_in_dim_reshape.15.refs_2_, f32[512,1024]{1,0:T(8,128)S(1)} %copy-done.4, bf16[32,9216]{1,0:T(8,128)(2,1)S(1)} %copy-done.14, ...), custom_call_target="tpu_custom_call" | custom-call | flops 2684354560 | bytes 16777216 | tf_op jit(solution)/shard_map/pallas_call | solution.py:109
  108.5 1.3 %copy-done.5 = f32[512,1024]{1,0:T(8,128)} copy-done((f32[512,1024]{1,0:T(8,128)}, f32[512,1024]{1,0:T(8,128)S(1)}, u32[]{:S(2)}) %copy-start.5) | copy-done | bytes 2097176
  109.9 0.5 collective-permute-start.20
  110.5 0.1 stack.220
  110.7 0.1 broadcast_in_dim_reshape.12.refs_2_
  110.8 1.4 %collective-permute-done.19.refs_7_.refs_15_ = bf16[32,9216]{1,0:T(8,128)(2,1)S(1)} collective-permute-done((bf16[32,9216]{1,0:T(8,128)(2,1)}, bf16[32,9216]{1,0:T(8,128)(2,1)S(1)}, u32[]{:S(2)}, u32[]{:S(2)}) %collective-permute-start.19) | collective-permute-done | bytes 589856 | tf_op jit(solution)/shard_map/ppermute | solution.py:152
  112.1 0.8 collective-permute-done.20.refs_9_.refs_17_
  113.0 0.8 collective-permute-done.21.refs_11_.refs_19_
  113.8 3.4 %copy-done.2 = bf16[512,8192]{1,0:T(8,128)(2,1)S(1)} copy-done((bf16[512,8192]{1,0:T(8,128)(2,1)S(1)}, bf16[512,8192]{1,0:T(8,128)(2,1)}, u32[]{:S(2)}) %copy-start.2) | copy-done | bytes 8388632
  117.2 1.6 %copy-done.6 = f32[512,1024]{1,0:T(8,128)S(1)} copy-done((f32[512,1024]{1,0:T(8,128)S(1)}, f32[512,1024]{1,0:T(8,128)}, u32[]{:S(2)}) %copy-start.6) | copy-done | bytes 2097176
  118.8 0.9 copy-done.12
  119.7 7.4 %shard_map.85 = bf16[512,1024]{1,0:T(8,128)(2,1)} custom-call(bf16[512,8192]{1,0:T(8,128)(2,1)S(1)} %copy-done.2, s32[512,1]{1,0:T(8,128)S(1)} %copy-done.12, s32[1,256]{1,0:T(1,128)S(1)} %broadcast_in_dim_reshape.12.refs_2_, f32[512,1024]{1,0:T(8,128)S(1)} %copy-done.6, bf16[32,9216]{1,0:T(8,128)(2,1)} %collective-permute-done.12.refs_4_.refs_12_, ...), custom_call_target="tpu_custom_call" | custom-call | flops 2684354560 | bytes 16777216 | tf_op jit(solution)/shard_map/pallas_call | solution.py:109
  (71 shorter events, 0.7 us)
Async XLA Ops:
  0.0 1.3 %copy-start.24 = (bf16[4,16,1024]{2,1,0:T(8,128)(2,1)S(1)}, bf16[4,16,1024]{2,1,0:T(8,128)(2,1)}, u32[]{:S(2)}) copy-start(bf16[4,16,1024]{2,1,0:T(8,128)(2,1)} %param.13) | copy-start | bytes 393220
  5.0 23.3 %collective-permute-start = (bf16[32,9216]{1,0:T(8,128)(2,1)}, bf16[32,9216]{1,0:T(8,128)(2,1)S(1)}, u32[]{:S(2)}, u32[]{:S(2)}) collective-permute-start(bf16[32,9216]{1,0:T(8,128)(2,1)} %bitcast.22.refs_5_.refs_13_), channel_id=1, source_target_pairs={{0,4},{1,5},{2,6},{3,7},{4,12},{5,13},{6,14},{7,15},{8,0},{9,1},{1... | collective-permute-start | bytes 1769480 | tf_op jit(solution)/shard_map/ppermute | solution.py:152
  8.0 20.3 %collective-permute-start.1 = (bf16[32,9216]{1,0:T(8,128)(2,1)}, bf16[32,9216]{1,0:T(8,128)(2,1)S(1)}, u32[]{:S(2)}, u32[]{:S(2)}) collective-permute-start(bf16[32,9216]{1,0:T(8,128)(2,1)} %bitcast.22.refs_5_.refs_13_), channel_id=1, source_target_pairs={{0,2},{1,3},{2,0},{3,1},{4,6},{5,7},{6,4},{7,5},{8,10},{9,11},{10,... | collective-permute-start | bytes 1769480 | tf_op jit(solution)/shard_map/ppermute | solution.py:152
  9.5 11.4 %copy-start.25 = (s32[4]{0:T(128)S(1)}, s32[4]{0:T(128)}, u32[]{:S(2)}) copy-start(s32[4]{0:T(128)} %constant.138.clone) | copy-start | bytes 52
  9.5 18.5 %copy-start.26 = (s32[512,1]{0,1:T(1,128)S(1)}, s32[512,1]{0,1:T(1,128)}, u32[]{:S(2)}) copy-start(s32[512,1]{0,1:T(1,128)} %param.9) | copy-start | bytes 6148
  9.5 18.5 %copy-start.27 = (s32[64]{0:T(128)S(1)}, s32[64]{0:T(128)}, u32[]{:S(2)}) copy-start(s32[64]{0:T(128)} %param.10) | copy-start | bytes 772
  9.5 42.9 %collective-permute-start.8 = (bf16[64,9216]{1,0:T(8,128)(2,1)}, bf16[64,9216]{1,0:T(8,128)(2,1)S(1)}, u32[]{:S(2)}, u32[]{:S(2)}) collective-permute-start(bf16[64,9216]{1,0:T(8,128)(2,1)} %bitcast.41), channel_id=1, source_target_pairs={{0,1},{1,0},{2,3},{3,2},{4,5},{5,4},{6,7},{7,6},{8,9},{9,8},{10,11... | collective-permute-start | bytes 3538952 | tf_op jit(solution)/shard_map/ppermute | solution.py:152
  28.3 24.2 %copy-start.9 = (s32[512,1]{1,0:T(8,128)}, s32[512,1]{1,0:T(8,128)S(1)}, u32[]{:S(2)}) copy-start(s32[512,1]{1,0:T(8,128)S(1)} %copy.16.refs_1_) | copy-start | bytes 6148
  28.3 15.4 %copy-start.19 = (bf16[32,9216]{1,0:T(8,128)(2,1)}, bf16[32,9216]{1,0:T(8,128)(2,1)S(1)}, u32[]{:S(2)}) copy-start(bf16[32,9216]{1,0:T(8,128)(2,1)S(1)} %collective-permute-done.refs_9_.refs_17_) | copy-start | bytes 1769476
  28.3 15.4 %copy-start.21 = (bf16[32,9216]{1,0:T(8,128)(2,1)}, bf16[32,9216]{1,0:T(8,128)(2,1)S(1)}, u32[]{:S(2)}) copy-start(bf16[32,9216]{1,0:T(8,128)(2,1)S(1)} %collective-permute-done.1.refs_10_.refs_18_) | copy-start | bytes 1769476
  28.3 16.7 %collective-permute-start.2 = (bf16[32,9216]{1,0:T(8,128)(2,1)S(1)}, bf16[32,9216]{1,0:T(8,128)(2,1)S(1)}, u32[]{:S(2)}, u32[]{:S(2)}) collective-permute-start(bf16[32,9216]{1,0:T(8,128)(2,1)S(1)} %collective-permute-done.refs_9_.refs_17_), channel_id=1, source_target_pairs={{0,4},{1,5},{2,6},{3,7},{4,12},{5,13},{6,14},{7,15},{8,0},{9,1},{1... | collective-permute-start | bytes 1769480 | tf_op jit(solution)/shard_map/ppermute | solution.py:152
  31.0 15.6 %collective-permute-start.3 = (bf16[32,9216]{1,0:T(8,128)(2,1)S(1)}, bf16[32,9216]{1,0:T(8,128)(2,1)}, u32[]{:S(2)}, u32[]{:S(2)}) collective-permute-start(bf16[32,9216]{1,0:T(8,128)(2,1)S(1)} %collective-permute-done.refs_9_.refs_17_), channel_id=1, source_target_pairs={{0,2},{1,3},{2,0},{3,1},{4,6},{5,7},{6,4},{7,5},{8,10},{9,11},{10,... | collective-permute-start | bytes 1769480 | tf_op jit(solution)/shard_map/ppermute | solution.py:152
  31.5 15.2 %collective-permute-start.4 = (bf16[32,9216]{1,0:T(8,128)(2,1)S(1)}, bf16[32,9216]{1,0:T(8,128)(2,1)S(1)}, u32[]{:S(2)}, u32[]{:S(2)}) collective-permute-start(bf16[32,9216]{1,0:T(8,128)(2,1)S(1)} %collective-permute-done.1.refs_10_.refs_18_), channel_id=1, source_target_pairs={{0,16},{1,17},{2,18},{3,19},{4,20},{5,21},{6,22},{7,23},{8,24},{9,... | collective-permute-start | bytes 1769480 | tf_op jit(solution)/shard_map/ppermute | solution.py:152
  33.0 19.4 %slice-start = ((s8[8388608]{0:T(1024)(128)(4,1)}), s8[4194304]{0:T(1024)(128)(4,1)S(1)}, s32[]{:S(2)}) async-start(s8[8388608]{0:T(1024)(128)(4,1)} %bitcast.76), calls=%async_computation | async-start | bytes 8388608
  33.1 19.4 %slice-start.1 = ((s8[8388608]{0:T(1024)(128)(4,1)}), s8[4194304]{0:T(1024)(128)(4,1)S(1)}, s32[]{:S(2)}) async-start(s8[8388608]{0:T(1024)(128)(4,1)} %bitcast.76), calls=%async_computation.1 | async-start | bytes 8388608
  33.1 19.3 %collective-permute-start.9 = (bf16[64,9216]{1,0:T(8,128)(2,1)S(1)}, bf16[64,9216]{1,0:T(8,128)(2,1)S(1)}, u32[]{:S(2)}, u32[]{:S(2)}) collective-permute-start(bf16[64,9216]{1,0:T(8,128)(2,1)S(1)} %pad_maximum_fusion.3), channel_id=1, source_target_pairs={{0,1},{1,0},{2,3},{3,2},{4,5},{5,4},{6,7},{7,6},{8,9},{9,8},{10,11... | collective-permute-start | bytes 3538952 | tf_op jit(solution)/shard_map/ppermute | solution.py:152
  43.7 8.8 %copy-start.23 = (f32[512,512]{1,0:T(8,128)S(1)}, f32[512,512]{1,0:T(8,128)}, u32[]{:S(2)}) copy-start(f32[512,512]{1,0:T(8,128)} %fusion.2.refs_3_) | copy-start | bytes 3145732
  45.0 14.3 %copy-start.15 = (bf16[32,9216]{1,0:T(8,128)(2,1)}, bf16[32,9216]{1,0:T(8,128)(2,1)S(1)}, u32[]{:S(2)}) copy-start(bf16[32,9216]{1,0:T(8,128)(2,1)S(1)} %collective-permute-done.2.refs_4_.refs_12_) | copy-start | bytes 1769476
  45.0 7.5 %copy-start.20 = (bf16[32,9216]{1,0:T(8,128)(2,1)S(1)}, bf16[32,9216]{1,0:T(8,128)(2,1)}, u32[]{:S(2)}) copy-start(bf16[32,9216]{1,0:T(8,128)(2,1)} %copy-done.19) | copy-start | bytes 1769476
  45.0 7.5 %copy-start.22 = (bf16[32,9216]{1,0:T(8,128)(2,1)S(1)}, bf16[32,9216]{1,0:T(8,128)(2,1)}, u32[]{:S(2)}) copy-start(bf16[32,9216]{1,0:T(8,128)(2,1)} %copy-done.21) | copy-start | bytes 1769476
  46.7 12.6 %copy-start.17 = (bf16[32,9216]{1,0:T(8,128)(2,1)}, bf16[32,9216]{1,0:T(8,128)(2,1)S(1)}, u32[]{:S(2)}) copy-start(bf16[32,9216]{1,0:T(8,128)(2,1)S(1)} %collective-permute-done.4.refs_6_.refs_14_) | copy-start | bytes 1769476
  46.7 14.5 %collective-permute-start.6 = (bf16[32,9216]{1,0:T(8,128)(2,1)S(1)}, bf16[32,9216]{1,0:T(8,128)(2,1)S(1)}, u32[]{:S(2)}, u32[]{:S(2)}) collective-permute-start(bf16[32,9216]{1,0:T(8,128)(2,1)S(1)} %collective-permute-done.2.refs_4_.refs_12_), channel_id=1, source_target_pairs={{0,2},{1,3},{2,0},{3,1},{4,6},{5,7},{6,4},{7,5},{8,10},{9,11},{10,... | collective-permute-start | bytes 1769480 | tf_op jit(solution)/shard_map/ppermute | solution.py:152
  48.2 14.1 %collective-permute-start.7 = (bf16[32,9216]{1,0:T(8,128)(2,1)S(1)}, bf16[32,9216]{1,0:T(8,128)(2,1)}, u32[]{:S(2)}, u32[]{:S(2)}) collective-permute-start(bf16[32,9216]{1,0:T(8,128)(2,1)S(1)} %collective-permute-done.2.refs_4_.refs_12_), channel_id=1, source_target_pairs={{0,16},{1,17},{2,18},{3,19},{4,20},{5,21},{6,22},{7,23},{8,24},{9,... | collective-permute-start | bytes 1769480 | tf_op jit(solution)/shard_map/ppermute | solution.py:152
  49.7 14.1 %collective-permute-start.5 = (bf16[32,9216]{1,0:T(8,128)(2,1)}, bf16[32,9216]{1,0:T(8,128)(2,1)}, u32[]{:S(2)}, u32[]{:S(2)}) collective-permute-start(bf16[32,9216]{1,0:T(8,128)(2,1)} %bitcast.22.refs_5_.refs_13_), channel_id=1, source_target_pairs={{0,8},{1,9},{2,10},{3,11},{4,0},{5,1},{6,2},{7,3},{8,12},{9,13},{1... | collective-permute-start | bytes 1769480 | tf_op jit(solution)/shard_map/ppermute | solution.py:152
  52.4 19.1 %collective-permute-start.13 = (bf16[96,9216]{1,0:T(8,128)(2,1)}, bf16[96,9216]{1,0:T(8,128)(2,1)S(1)}, u32[]{:S(2)}, u32[]{:S(2)}) collective-permute-start(bf16[96,9216]{1,0:T(8,128)(2,1)} %pad_maximum_fusion), channel_id=1, source_target_pairs={{0,1},{1,0},{2,3},{3,2},{4,5},{5,4},{6,7},{7,6},{8,9},{9,8},{10,11... | collective-permute-start | bytes 5308424 | tf_op jit(solution)/shard_map/ppermute | solution.py:152
  59.3 1.3 %copy-start.7 = (f32[512,1024]{1,0:T(8,128)}, f32[512,1024]{1,0:T(8,128)S(1)}, u32[]{:S(2)}) copy-start(f32[512,1024]{1,0:T(8,128)S(1)} %shard_map.82.refs_3_) | copy-start | bytes 6291460
  66.4 0.8 copy-start.13
  67.2 4.4 %collective-permute-start.14 = (bf16[96,9216]{1,0:T(8,128)(2,1)}, bf16[96,9216]{1,0:T(8,128)(2,1)S(1)}, u32[]{:S(2)}, u32[]{:S(2)}) collective-permute-start(bf16[96,9216]{1,0:T(8,128)(2,1)} %pad_maximum_fusion.1), channel_id=1, source_target_pairs={{0,1},{1,0},{2,3},{3,2},{4,5},{5,4},{6,7},{7,6},{8,9},{9,8},{10,11... | collective-permute-start | bytes 5308424 | tf_op jit(solution)/shard_map/ppermute | solution.py:152
  67.2 20.6 %collective-permute-start.11 = (bf16[32,9216]{1,0:T(8,128)(2,1)}, bf16[32,9216]{1,0:T(8,128)(2,1)}, u32[]{:S(2)}, u32[]{:S(2)}) collective-permute-start(bf16[32,9216]{1,0:T(8,128)(2,1)} %collective-permute-done.5.refs_10_.refs_18_), channel_id=1, source_target_pairs={{0,2},{1,3},{2,0},{3,1},{4,6},{5,7},{6,4},{7,5},{8,10},{9,11},{10,... | collective-permute-start | bytes 1769480 | tf_op jit(solution)/shard_map/ppermute | solution.py:152
  67.9 19.8 %collective-permute-start.10 = (bf16[32,9216]{1,0:T(8,128)(2,1)}, bf16[32,9216]{1,0:T(8,128)(2,1)}, u32[]{:S(2)}, u32[]{:S(2)}) collective-permute-start(bf16[32,9216]{1,0:T(8,128)(2,1)} %bitcast.23.refs_6_.refs_14_), channel_id=1, source_target_pairs={{0,4},{1,5},{2,6},{3,7},{4,12},{5,13},{6,14},{7,15},{8,0},{9,1},{1... | collective-permute-start | bytes 1769480 | tf_op jit(solution)/shard_map/ppermute | solution.py:152
  69.5 18.3 %collective-permute-start.12 = (bf16[32,9216]{1,0:T(8,128)(2,1)}, bf16[32,9216]{1,0:T(8,128)(2,1)}, u32[]{:S(2)}, u32[]{:S(2)}) collective-permute-start(bf16[32,9216]{1,0:T(8,128)(2,1)} %collective-permute-done.3.refs_5_.refs_13_), channel_id=1, source_target_pairs={{0,16},{1,17},{2,18},{3,19},{4,20},{5,21},{6,22},{7,23},{8,24},{9,... | collective-permute-start | bytes 1769480 | tf_op jit(solution)/shard_map/ppermute | solution.py:152
  71.6 3.4 %copy-start = (bf16[512,8192]{1,0:T(8,128)(2,1)S(1)}, bf16[512,8192]{1,0:T(8,128)(2,1)}, u32[]{:S(2)}) copy-start(bf16[512,8192]{1,0:T(8,128)(2,1)} %refs_0_.7) | copy-start | bytes 25165828
  75.0 1.6 %copy-start.8 = (f32[512,1024]{1,0:T(8,128)S(1)}, f32[512,1024]{1,0:T(8,128)}, u32[]{:S(2)}) copy-start(f32[512,1024]{1,0:T(8,128)} %copy-done.7) | copy-start | bytes 6291460
  76.6 0.9 copy-start.10
  77.5 1.1 copy-start.16
  78.6 1.1 copy-start.18
  86.4 1.3 %copy-start.3 = (f32[512,1024]{1,0:T(8,128)}, f32[512,1024]{1,0:T(8,128)S(1)}, u32[]{:S(2)}) copy-start(f32[512,1024]{1,0:T(8,128)S(1)} %shard_map.83.refs_3_) | copy-start | bytes 6291460
  90.5 4.4 %collective-permute-start.18 = (bf16[96,9216]{1,0:T(8,128)(2,1)}, bf16[96,9216]{1,0:T(8,128)(2,1)S(1)}, u32[]{:S(2)}, u32[]{:S(2)}) collective-permute-start(bf16[96,9216]{1,0:T(8,128)(2,1)} %pad_maximum_fusion.2), channel_id=1, source_target_pairs={{0,1},{1,0},{2,3},{3,2},{4,5},{5,4},{6,7},{7,6},{8,9},{9,8},{10,11... | collective-permute-start | bytes 5308424 | tf_op jit(solution)/shard_map/ppermute | solution.py:152
  90.5 19.4 %collective-permute-start.15 = (bf16[32,9216]{1,0:T(8,128)(2,1)}, bf16[32,9216]{1,0:T(8,128)(2,1)}, u32[]{:S(2)}, u32[]{:S(2)}) collective-permute-start(bf16[32,9216]{1,0:T(8,128)(2,1)} %bitcast.23.refs_6_.refs_14_), channel_id=1, source_target_pairs={{0,8},{1,9},{2,10},{3,11},{4,0},{5,1},{6,2},{7,3},{8,12},{9,13},{1... | collective-permute-start | bytes 1769480 | tf_op jit(solution)/shard_map/ppermute | solution.py:152
  91.8 18.0 %collective-permute-start.16 = (bf16[32,9216]{1,0:T(8,128)(2,1)}, bf16[32,9216]{1,0:T(8,128)(2,1)}, u32[]{:S(2)}, u32[]{:S(2)}) collective-permute-start(bf16[32,9216]{1,0:T(8,128)(2,1)} %collective-permute-done.7.refs_5_.refs_13_), channel_id=1, source_target_pairs={{0,2},{1,3},{2,0},{3,1},{4,6},{5,7},{6,4},{7,5},{8,10},{9,11},{10,... | collective-permute-start | bytes 1769480 | tf_op jit(solution)/shard_map/ppermute | solution.py:152
  93.2 16.7 %collective-permute-start.17 = (bf16[32,9216]{1,0:T(8,128)(2,1)}, bf16[32,9216]{1,0:T(8,128)(2,1)}, u32[]{:S(2)}, u32[]{:S(2)}) collective-permute-start(bf16[32,9216]{1,0:T(8,128)(2,1)} %collective-permute-done.11.refs_9_.refs_17_), channel_id=1, source_target_pairs={{0,16},{1,17},{2,18},{3,19},{4,20},{5,21},{6,22},{7,23},{8,24},{9,... | collective-permute-start | bytes 1769480 | tf_op jit(solution)/shard_map/ppermute | solution.py:152
  94.9 3.4 %copy-start.1 = (bf16[512,8192]{1,0:T(8,128)(2,1)S(1)}, bf16[512,8192]{1,0:T(8,128)(2,1)}, u32[]{:S(2)}) copy-start(bf16[512,8192]{1,0:T(8,128)(2,1)} %refs_0_.7) | copy-start | bytes 25165828
  98.3 1.6 %copy-start.4 = (f32[512,1024]{1,0:T(8,128)S(1)}, f32[512,1024]{1,0:T(8,128)}, u32[]{:S(2)}) copy-start(f32[512,1024]{1,0:T(8,128)} %copy-done.3) | copy-start | bytes 6291460
  99.9 0.9 copy-start.11
  100.8 1.1 copy-start.14
  108.5 1.3 %copy-start.5 = (f32[512,1024]{1,0:T(8,128)}, f32[512,1024]{1,0:T(8,128)S(1)}, u32[]{:S(2)}) copy-start(f32[512,1024]{1,0:T(8,128)S(1)} %shard_map.84.refs_3_) | copy-start | bytes 6291460
  109.9 2.3 %collective-permute-start.19 = (bf16[32,9216]{1,0:T(8,128)(2,1)}, bf16[32,9216]{1,0:T(8,128)(2,1)S(1)}, u32[]{:S(2)}, u32[]{:S(2)}) collective-permute-start(bf16[32,9216]{1,0:T(8,128)(2,1)} %collective-permute-done.15.refs_6_.refs_14_), channel_id=1, source_target_pairs={{0,1},{1,0},{2,3},{3,2},{4,5},{5,4},{6,7},{7,6},{8,9},{9,8},{10,11... | collective-permute-start | bytes 1769480 | tf_op jit(solution)/shard_map/ppermute | solution.py:152
  109.9 3.0 %collective-permute-start.20 = (bf16[32,9216]{1,0:T(8,128)(2,1)}, bf16[32,9216]{1,0:T(8,128)(2,1)S(1)}, u32[]{:S(2)}, u32[]{:S(2)}) collective-permute-start(bf16[32,9216]{1,0:T(8,128)(2,1)} %collective-permute-done.16.refs_8_.refs_16_), channel_id=1, source_target_pairs={{0,1},{1,0},{2,3},{3,2},{4,5},{5,4},{6,7},{7,6},{8,9},{9,8},{10,11... | collective-permute-start | bytes 1769480 | tf_op jit(solution)/shard_map/ppermute | solution.py:152
  110.4 3.4 %collective-permute-start.21 = (bf16[32,9216]{1,0:T(8,128)(2,1)}, bf16[32,9216]{1,0:T(8,128)(2,1)S(1)}, u32[]{:S(2)}, u32[]{:S(2)}) collective-permute-start(bf16[32,9216]{1,0:T(8,128)(2,1)} %collective-permute-done.17.refs_10_.refs_18_), channel_id=1, source_target_pairs={{0,1},{1,0},{2,3},{3,2},{4,5},{5,4},{6,7},{7,6},{8,9},{9,8},{10,11... | collective-permute-start | bytes 1769480 | tf_op jit(solution)/shard_map/ppermute | solution.py:152
  113.8 3.4 %copy-start.2 = (bf16[512,8192]{1,0:T(8,128)(2,1)S(1)}, bf16[512,8192]{1,0:T(8,128)(2,1)}, u32[]{:S(2)}) copy-start(bf16[512,8192]{1,0:T(8,128)(2,1)} %refs_0_.7) | copy-start | bytes 25165828
  117.2 1.6 %copy-start.6 = (f32[512,1024]{1,0:T(8,128)S(1)}, f32[512,1024]{1,0:T(8,128)}, u32[]{:S(2)}) copy-start(f32[512,1024]{1,0:T(8,128)} %copy-done.5) | copy-start | bytes 6291460
  118.8 0.9 copy-start.12

commit v4 on v1

v4 whole, which is shorter than its diff:
```python
import functools

import jax
import jax.numpy as jnp
import numpy as np
from jax import lax
from jax.experimental import pallas as pl
from jax.experimental.pallas import tpu as pltpu
from jax.sharding import PartitionSpec as P

RING = (0, 1, 3, 2)
PLACE_IN_RING = (0, 1, 3, 2)
DEPTH_TILE = 1024
VMEM_BYTES = 64 * 1024 * 1024 - 512 * 1024


def slots_of_rows(row_adapter_index, adapter_storage_slot):
    catalog = jnp.arange(adapter_storage_slot.shape[0], dtype=jnp.int32)
    return jnp.sum(
        jnp.where(row_adapter_index == catalog[None, :], adapter_storage_slot[None, :], 0),
        axis=1,
        keepdims=True,
    )


def gathered(
    tokens,
    row_adapter_index,
    adapter_storage_slot,
    base_value_weight,
    adapter_down_weight,
    adapter_up_weight,
):
    adapter_count = adapter_storage_slot.shape[0]
    rank = adapter_down_weight.shape[1]
    slot_of = slots_of_rows(row_adapter_index, adapter_storage_slot)
    down_all = lax.all_gather(
        adapter_down_weight.reshape(-1, adapter_down_weight.shape[2]), "req", axis=0, tiled=True
    )
    up_all = lax.all_gather(
        adapter_up_weight.reshape(-1, adapter_up_weight.shape[2]), "req", axis=0, tiled=True
    )
    base_partial = jnp.dot(tokens, base_value_weight, preferred_element_type=jnp.float32)
    base_output = lax.psum_scatter(base_partial, "tp", scatter_dimension=1, tiled=True)
    shrink = lax.dot_general(
        tokens, down_all, (((1,), (1,)), ((), ())), preferred_element_type=jnp.float32
    )
    column_slot = jnp.arange(adapter_count * rank, dtype=jnp.int32) // rank
    shrink = jnp.where(slot_of == column_slot[None, :], shrink, 0.0)
    shrink = lax.psum(shrink, "tp")
    high = lax.reduce_precision(shrink, 8, 7)
    rest = shrink - high
    middle = lax.reduce_precision(rest, 8, 7)
    low = rest - middle
    lora = sum(
        jnp.dot(piece.astype(jnp.bfloat16), up_all, preferred_element_type=jnp.float32)
        for piece in (low, middle, high)
    )
    return (base_output + lora).astype(jnp.bfloat16)


def params():
    return pltpu.CompilerParams(vmem_limit_bytes=VMEM_BYTES)


def started(copies):
    for copy in copies:
        copy.start()


def awaited(copies):
    for copy in copies:
        copy.wait()


def own_kernel(y_ref, down_ref, up_ref, front_ref, back_ref):
    depth = down_ref.shape[2]
    count = down_ref.shape[0] // 2
    for out_ref, first in ((front_ref, y_ref[0] * count), (back_ref, (1 - y_ref[0]) * count)):
        rows = out_ref.shape[0]
        out_ref[:, :depth] = down_ref[pl.ds(first, count)].reshape(rows, depth)
        out_ref[:, depth:] = up_ref[pl.ds(first, count)].reshape(rows, up_ref.shape[2])


def own_pieces(y, down, up):
    held, rank, depth = down.shape
    piece = jax.ShapeDtypeStruct((held // 2 * rank, depth + up.shape[2]), down.dtype)
    vmem = pl.BlockSpec(memory_space=pltpu.VMEM)
    return pl.pallas_call(
        own_kernel,
        out_shape=(piece, piece),
        in_specs=[pl.BlockSpec(memory_space=pltpu.SMEM), vmem, vmem],
        out_specs=(vmem, vmem),
        compiler_params=params(),
    )(y[None], down, up)


def join_kernel(count, *refs):
    sources, out_ref, sems = refs[:count], refs[count], refs[count + 1]
    rows = sources[0].shape[0]
    copies = [
        pltpu.make_async_copy(source, out_ref.at[pl.ds(n * rows, rows)], sems.at[n])
        for n, source in enumerate(sources)
    ]
    started(copies)
    awaited(copies)


def join(*arrays):
    rows, width = arrays[0].shape
    count = len(arrays)
    anywhere = pl.BlockSpec(memory_space=pl.ANY)
    return pl.pallas_call(
        functools.partial(join_kernel, count),
        out_shape=jax.ShapeDtypeStruct((count * rows, width), arrays[0].dtype),
        in_specs=[anywhere] * count,
        out_specs=anywhere,
        scratch_shapes=[pltpu.SemaphoreType.DMA((count,))],
        cost_estimate=pl.CostEstimate(
            flops=0, bytes_accessed=4 * count * rows * width, transcendentals=0
        ),
        compiler_params=params(),
    )(*arrays)


def base_kernel(steps, tokens_ref, weight_ref, *refs):
    step = pl.program_id(0)
    more = len(refs) > 1
    out_ref = refs[1] if more else refs[0]
    copies = [pltpu.make_async_copy(refs[0], refs[2], refs[3].at[0])] if more else []
    part = jnp.dot(tokens_ref[...], weight_ref[...], preferred_element_type=jnp.float32)

    @pl.when(step == 0)
    def _():
        started(copies)
        out_ref[...] = part

    @pl.when(step > 0)
    def _():
        out_ref[...] += part

    if more:

        @pl.when(step == steps - 1)
        def _():
            awaited(copies)
            out_ref[...] += refs[2][...]


def base_part(tokens, weight, begin, end, total=None):
    rows, depth = tokens.shape
    width = weight.shape[1]
    steps, first = (end - begin) // DEPTH_TILE, begin // DEPTH_TILE
    result = jax.ShapeDtypeStruct((rows, width), jnp.float32)
    more = total is not None
    return pl.pallas_call(
        functools.partial(base_kernel, steps),
        out_shape=result,
        grid=(steps,),
        in_specs=[
            pl.BlockSpec((rows, DEPTH_TILE), lambda k: (0, first + k)),
            pl.BlockSpec((DEPTH_TILE, width), lambda k: (first + k, 0)),
        ]
        + [pl.BlockSpec(memory_space=pl.ANY)] * more,
        out_specs=pl.BlockSpec((rows, width), lambda k: (0, 0)),
        scratch_shapes=[pltpu.VMEM((rows, width), jnp.float32), pltpu.SemaphoreType.DMA((1,))]
        if more
        else [],
        cost_estimate=pl.CostEstimate(
            flops=2 * rows * width * (end - begin),
            bytes_accessed=2 * (rows + width) * (end - begin) + 4 * rows * width,
            transcendentals=0,
        ),
        compiler_params=params(),
    )(tokens, weight, *([total] if more else []))


def absorb_kernel(places, steps, tokens_ref, row_slot_ref, column_slot_ref, total_ref, *refs):
    count = len(places)
    downs, sources = refs[:count], refs[count : 2 * count]
    out_ref, shrink_ref, total, up, sems = refs[2 * count :]
    step = pl.program_id(0)
    block = downs[0].shape[0]
    width = up.shape[1]
    depth = sources[0].shape[1] - width
    copies = [pltpu.make_async_copy(total_ref, total, sems.at[count])] + [
        pltpu.make_async_copy(
            source.at[pl.ds(place * block, block), pl.ds(depth, width)],
            up.at[pl.ds(n * block, block)],
            sems.at[n],
        )
        for n, (source, place) in enumerate(zip(sources, places))
    ]

    @pl.when(step == 0)
    def _():
        started(copies)

    part = lax.dot_general(
        tokens_ref[...],
        jnp.concatenate([down[...] for down in downs], axis=0),
        (((1,), (1,)), ((), ())),
        preferred_element_type=jnp.float32,
    )

    @pl.when(step == 0)
    def _():
        shrink_ref[...] = part

    @pl.when(step > 0)
    def _():
        shrink_ref[...] += part

    @pl.when(step == steps - 1)
    def _():
        kept = jnp.where(row_slot_ref[...] == column_slot_ref[...], shrink_ref[...], 0.0)
        high = kept.astype(jnp.bfloat16)
        low = (kept - high.astype(jnp.float32)).astype(jnp.bfloat16)
        awaited(copies)
        lora = jnp.dot(low, up[...], preferred_element_type=jnp.float32)
        lora += jnp.dot(high, up[...], preferred_element_type=jnp.float32)
        out_ref[...] = (total[...] + lora).astype(out_ref.dtype)


def absorb(tokens, row_slot, column_slot, total, pieces, out_dtype):
    rows, depth = tokens.shape
    width = total.shape[1]
    columns = column_slot.shape[1]
    block = columns // len(pieces)
    places = [place for _, place in pieces]
    steps = depth // DEPTH_TILE
    whole = lambda *shape: pl.BlockSpec(shape, lambda k: (0, 0))
    anywhere = pl.BlockSpec(memory_space=pl.ANY)

    def down_spec(place):
        return pl.BlockSpec((block, DEPTH_TILE), lambda k: (place, k))

    return pl.pallas_call(
        functools.partial(absorb_kernel, places, steps),
        out_shape=jax.ShapeDtypeStruct((rows, width), out_dtype),
        grid=(steps,),
        in_specs=[
            pl.BlockSpec((rows, DEPTH_TILE), lambda k: (0, k)),
            whole(rows, 1),
            whole(1, columns),
            anywhere,
        ]
        + [down_spec(place) for place in places]
        + [anywhere] * len(pieces),
        out_specs=whole(rows, width),
        scratch_shapes=[
            pltpu.VMEM((rows, columns), jnp.float32),
            pltpu.VMEM((rows, width), jnp.float32),
            pltpu.VMEM((columns, width), jnp.bfloat16),
            pltpu.SemaphoreType.DMA((len(pieces) + 1,)),
        ],
        cost_estimate=pl.CostEstimate(
            flops=2 * rows * columns * (depth + 2 * width),
            bytes_accessed=2 * (rows + columns) * depth + 8 * rows * width,
            transcendentals=0,
        ),
        compiler_params=params(),
    )(tokens, row_slot, column_slot, total, *[array for array, _ in pieces * 2])


def passed_round(
    tokens,
    row_adapter_index,
    adapter_storage_slot,
    base_value_weight,
    adapter_down_weight,
    adapter_up_weight,
):
    held, rank, depth = adapter_down_weight.shape
    axes = ("groups", "req")
    planes, owners = lax.axis_size("groups"), lax.axis_size("req")
    y, at = lax.axis_index("groups"), lax.axis_index("req")

    def permuted(array, target):
        pairs = [
            (g * owners + r, target(g, r)) for g in range(planes) for r in range(owners)
        ]
        return lax.ppermute(array, axes, pairs)

    def along_z(r, by):
        return RING[(PLACE_IN_RING[r // 4] + by) % 4] * 4 + r % 4

    z_ring = lambda array: permuted(array, lambda g, r: g * owners + along_z(r, 1))
    z_back = lambda array: permuted(array, lambda g, r: g * owners + along_z(r, -1))
    x_swap = lambda array: permuted(array, lambda g, r: g * owners + (r ^ 2))
    y_swap = lambda array: permuted(array, lambda g, r: (1 - g) * owners + r)
    core_swap = lambda array: permuted(array, lambda g, r: g * owners + (r ^ 1))

    def slots(g, r, step, other_x, other_core, back):
        owner = along_z(r, -step) ^ (2 * other_x) ^ other_core
        return [owner * held + (g ^ back) * (held // 2) + unit for unit in range(held // 2)]

    groups = (
        ((0, 0, 0), (0, 0, 1), (1, 0, 0), (0, 1, 0)),
        ((2, 0, 0), (1, 1, 0), (0, 1, 1), (3, 0, 0)),
        ((2, 1, 0), (2, 0, 1), (1, 0, 1), (3, 1, 0)),
        ((1, 1, 1), (3, 0, 1), (2, 1, 1), (3, 1, 1)),
    )
    table = np.array(
        [
            [
                [
                    np.repeat(
                        [
                            slot
                            for step, other_x, back in group
                            for other_core in (0, 1)
                            for slot in slots(g, r, step, other_x, other_core, back)
                        ],
                        rank,
                    )
                ]
                for group in groups
            ]
            for g in range(planes)
            for r in range(owners)
        ],
        np.int32,
    )
    column_slots = lax.dynamic_index_in_dim(jnp.array(table), y * owners + at, 0, keepdims=False)
    row_slot = slots_of_rows(row_adapter_index, adapter_storage_slot)
    front, back = own_pieces(y, adapter_down_weight, adapter_up_weight)

    def update(number, total, pieces, out_dtype=jnp.float32):
        return absorb(tokens, row_slot, column_slots[number], total, pieces, out_dtype)

    def interleaved(here, there):
        return [piece for both in zip(here, there) for piece in both]

    def shared(*arrays):
        batch = core_swap(join(*arrays))
        return interleaved(
            [(array, 0) for array in arrays], [(batch, n) for n in range(len(arrays))]
        )

    def shared_singly(*arrays):
        there = [core_swap(array) for array in arrays]
        return interleaved([(array, 0) for array in arrays], [(array, 0) for array in there])

    def together(*values):
        leaves, tree = jax.tree.flatten(values)
        arrays = {id(leaf): leaf for leaf in leaves if not isinstance(leaf, int)}
        arrays = dict(zip(arrays, lax.optimization_barrier(tuple(arrays.values()))))
        return tree.unflatten([arrays.get(id(leaf), leaf) for leaf in leaves])

    z1, x0 = z_ring(front), x_swap(front)
    own = shared_singly(front, back)
    total = base_part(tokens, base_value_weight, 0, depth // 2)
    z1, x0, own, front, back, total, row_slot, column_slots = together(
        z1, x0, own, front, back, total, row_slot, column_slots
    )

    z2, x1, yx0 = z_ring(z1), x_swap(z1), y_swap(x0)
    first = shared(z1, x0)
    total = base_part(tokens, base_value_weight, depth // 2, depth, total)
    z2, x1, yx0, first, front, total = together(z2, x1, yx0, first, front, total)

    z3, x2, yz2 = z_back(front), x_swap(z2), y_swap(z2)
    second = shared(z2, x1, yx0)
    total = update(0, total, own + first)
    z3, x2, yz2, x1, second, back, total = together(z3, x2, yz2, x1, second, back, total)

    zb1, x3, yx1 = z_ring(back), x_swap(z3), y_swap(x1)
    third = shared(z3, x2, yz2)
    total = update(1, total, second + third[:2])
    zb1, x3, yx1, yz2, third, back, total = together(zb1, x3, yx1, yz2, third, back, total)

    zb3, xyz2, yx3 = z_back(back), x_swap(yz2), y_swap(x3)
    fourth = shared(zb1, x3, yx1)
    total = update(2, total, third[2:] + fourth[:4])
    zb3, xyz2, yx3, fourth, total = together(zb3, xyz2, yx3, fourth, total)

    return update(3, total, fourth[4:] + shared_singly(zb3, xyz2, yx3), jnp.bfloat16)


def solution(mesh):
    placed = (
        P(("groups", "req"), "tp"),
        P(("groups", "req"), None),
        P(),
        P("tp", None),
        P("req", None, "tp"),
        P("req", None, "tp"),
    )
    sizes = mesh.shape
    small = sizes["groups"] == 2 and sizes["req"] == 16 and sizes["tp"] == 1
    return jax.shard_map(
        passed_round if small else gathered,
        mesh=mesh,
        in_specs=placed,
        out_specs=P(("groups", "req"), "tp"),
        check_vma=False,
    )
```

time: 209 us -> 310 us (1.48)
  Pallas kernels: 0 us -> 267 us
  waiting for transfers between devices: 159 us -> 19.3 us
  matrix products: 35.1 us -> 0 us
  starting transfers between devices: 0.04 us -> 20 us
  between operations: 13.5 us -> 0.12 us
    pallas_call x0 -> x11, Pallas kernels: none -> 267 us  [the longest x4 201 us: join(): pl.pallas_call(functools.partial(join_kernel, count), out_shape=jax.Shape...]
    all_gather x2 -> x0, waiting for transfers between devices: 158 us -> none  [the longest x1 130 us: per_device(): lax.all_gather(adapter_down_weight.reshape(-1, adapter_down_weight.shape[...]
    dot_general x5 -> x0, matrix products: 35.1 us -> none  [the longest x1 14.4 us: per_device(): lax.dot_general(tokens, down_all, (((1,), (1,)), ((), ())), preferred_ele...]
    ppermute x0 -> x23, starting transfers between devices: none -> 20 us  [permuted(): return lax.ppermute(array, axes, pairs)]
    ppermute x0 -> x23, waiting for transfers between devices: none -> 19.3 us  [permuted(): return lax.ppermute(array, axes, pairs)]
  transfers between devices with their start and end apart: 2 -> 23, of which waited for: 2 -> 18; matrix products, arithmetic and copies ran while one was open for 7% -> 1% of each run, Pallas kernels for 0% -> 17%
where the time goes in v4:
time: 310 us
  Pallas kernels  267 us (86%)
  starting transfers between devices  20 us (6%)
  waiting for transfers between devices  19.3 us (6%)
    pallas_call x4, Pallas kernels, join(): pl.pallas_call(functools.partial(join_kernel, count), out_shape=jax.Shape...  201 us
    pallas_call x4, Pallas kernels, absorb(): pl.pallas_call(functools.partial(absorb_kernel, places, steps), out_shape...  44.4 us
    ppermute x23, starting transfers between devices, permuted(): return lax.ppermute(array, axes, pairs)  20 us
    pallas_call x2, Pallas kernels, base_part(): pl.pallas_call(functools.partial(base_kernel, steps), out_shape=result, g...  19.4 us
    ppermute x23, waiting for transfers between devices, permuted(): return lax.ppermute(array, axes, pairs)  19.3 us
  transfers between devices with their start and end apart: 23, of which 18 were waited for; matrix products, arithmetic and copies ran while one was open for 1% of the time, Pallas kernels for 17%

profile of v4, /device:TPU:0, one launch (start us, length us, event | category | flops | bytes accessed | tf_op | source)
XLA Modules:
  0.0 309.6 jit_solution(17867258870432928971)
XLA Ops:
  0.0 2.3 shard_map.73
  2.3 3.0 collective-permute-start
  5.3 1.5 collective-permute-start.1
  6.8 0.0 collective-permute-start.2
  6.8 0.5 collective-permute-start.3
  7.3 0.7 dynamic-slice_bitcast_fusion
  8.0 0.8 select_reduce_fusion
  8.8 9.6 %shard_map.74.refs_0_ = f32[512,1024]{1,0:T(8,128)} custom-call(bf16[512,8192]{1,0:T(8,128)(2,1)} %tokens_ref.11, bf16[8192,1024]{1,0:T(8,128)(2,1)} %weight_ref.3), custom_call_target="tpu_custom_call" | custom-call | flops 4294967296 | bytes 14680064 | tf_op jit(solution)/shard_map/pallas_call | solution.py:156
  18.4 1.6 collective-permute-done.refs_0_.refs_4_.refs_12_
  20.0 0.5 collective-permute-done.1.refs_1_.refs_6_.refs_14_
  20.4 0.0 collective-permute-done.2.refs_1_.refs_9_
  20.4 0.0 collective-permute-done.3.refs_3_.refs_11_
  20.4 36.9 %shard_map.75 = bf16[64,9216]{1,0:T(8,128)(2,1)} custom-call(bf16[32,9216]{1,0:T(8,128)(2,1)} %collective-permute-done.refs_0_.refs_4_.refs_12_, bf16[32,9216]{1,0:T(8,128)(2,1)} %collective-permute-done.1.refs_1_.refs_6_.refs_14_), custom_call_target="tpu_custom_call" | custom-call | bytes 2359296 | tf_op jit(solution)/shard_map/pallas_call | solution.py:113
  57.3 0.1 collective-permute-start.7
  57.4 2.6 collective-permute-start.4
  60.0 1.5 collective-permute-start.5
  61.5 1.5 collective-permute-start.6
  63.0 9.8 %shard_map.76.total_ref = f32[512,1024]{1,0:T(8,128)} custom-call(bf16[512,8192]{1,0:T(8,128)(2,1)} %tokens_ref.11, bf16[8192,1024]{1,0:T(8,128)(2,1)} %weight_ref.3, f32[512,1024]{1,0:T(8,128)} %shard_map.74.refs_0_), custom_call_target="tpu_custom_call" | custom-call | flops 4294967296 | bytes 14680064 | tf_op jit(solution)/shard_map/pallas_call | solution.py:156
  72.9 1.5 collective-permute-done.4.refs_0_.refs_8_
  74.3 1.4 collective-permute-done.5.refs_1_.refs_2_.refs_10_
  75.7 1.2 collective-permute-done.6.refs_2_.refs_4_.refs_12_
  77.0 0.0 collective-permute-done.7.refs_5_.refs_7_.refs_13_.refs_15_
  77.0 54.7 %shard_map.77 = bf16[96,9216]{1,0:T(8,128)(2,1)} custom-call(bf16[32,9216]{1,0:T(8,128)(2,1)} %collective-permute-done.4.refs_0_.refs_8_, bf16[32,9216]{1,0:T(8,128)(2,1)} %collective-permute-done.5.refs_1_.refs_2_.refs_10_, bf16[32,9216]{1,0:T(8,128)(2,1)} %collective-permute-done.6.refs_2_.refs_4_.refs_12_), custom_call_target="tpu_custom_call" | custom-call | bytes 3538944 | tf_op jit(solution)/shard_map/pallas_call | solution.py:113
  131.7 0.1 collective-permute-start.11
  131.8 1.6 collective-permute-start.10
  133.4 0.3 collective-permute-start.8
  133.7 0.5 collective-permute-start.9
  134.2 0.9 copy.15.row_slot_ref
  135.1 0.6 slice_bitcast_fusion
  135.7 11.2 %shard_map.78.total_ref = f32[512,1024]{1,0:T(8,128)} custom-call(bf16[512,8192]{1,0:T(8,128)(2,1)} %tokens_ref.11, s32[512,1]{1,0:T(8,128)} %copy.15.row_slot_ref, s32[1,256]{1,0:T(1,128)} %get-tuple-element.91.column_slot_ref, f32[512,1024]{1,0:T(8,128)} %shard_map.76.total_ref, bf16[32,9216]{1,0:T(8,128)(2,1)} %get-tuple-element.55.refs_0_.refs_8_, ...), custom_call_target="tpu_custom_call" | custom-call | flops 2684354560 | bytes 16777216 | tf_op jit(solution)/shard_map/pallas_call | solution.py:238
  146.9 0.9 collective-permute-done.10.refs_2_.refs_10_
  147.8 1.2 collective-permute-done.8.refs_0_.refs_6_.refs_14_
  149.1 0.1 collective-permute-done.9.refs_1_.refs_0_.refs_8_
  149.1 0.0 collective-permute-done.11.refs_1_.refs_3_.refs_5_.refs_9_.refs_11_.refs_13_
  149.1 54.7 %shard_map.79 = bf16[96,9216]{1,0:T(8,128)(2,1)} custom-call(bf16[32,9216]{1,0:T(8,128)(2,1)} %collective-permute-done.8.refs_0_.refs_6_.refs_14_, bf16[32,9216]{1,0:T(8,128)(2,1)} %collective-permute-done.9.refs_1_.refs_0_.refs_8_, bf16[32,9216]{1,0:T(8,128)(2,1)} %collective-permute-done.10.refs_2_.refs_10_), custom_call_target="tpu_custom_call" | custom-call | bytes 3538944 | tf_op jit(solution)/shard_map/pallas_call | solution.py:113
  203.9 0.1 collective-permute-start.15
  204.0 0.6 collective-permute-start.13
  204.6 2.0 collective-permute-start.12
  206.6 0.5 collective-permute-start.14
  207.1 0.9 collective-permute-done.15.refs_7_.refs_15_.refs_1_.refs_3_.refs_9_.refs_11_
  208.0 11.2 %shard_map.80.total_ref = f32[512,1024]{1,0:T(8,128)} custom-call(bf16[512,8192]{1,0:T(8,128)(2,1)} %tokens_ref.11, s32[512,1]{1,0:T(8,128)} %copy.15.row_slot_ref, s32[1,256]{1,0:T(1,128)} %get-tuple-element.90.column_slot_ref, f32[512,1024]{1,0:T(8,128)} %shard_map.78.total_ref, bf16[32,9216]{1,0:T(8,128)(2,1)} %collective-permute-done.4.refs_0_.refs_8_, ...), custom_call_target="tpu_custom_call" | custom-call | flops 2684354560 | bytes 16777216 | tf_op jit(solution)/shard_map/pallas_call | solution.py:238
  219.2 2.0 collective-permute-done.12.refs_0_.refs_4_.refs_12_
  221.2 0.0 collective-permute-done.13.refs_1_.refs_6_.refs_14_
  221.2 0.8 collective-permute-done.14.refs_2_.refs_0_.refs_8_
  222.0 54.7 %shard_map.81 = bf16[96,9216]{1,0:T(8,128)(2,1)} custom-call(bf16[32,9216]{1,0:T(8,128)(2,1)} %collective-permute-done.12.refs_0_.refs_4_.refs_12_, bf16[32,9216]{1,0:T(8,128)(2,1)} %collective-permute-done.13.refs_1_.refs_6_.refs_14_, bf16[32,9216]{1,0:T(8,128)(2,1)} %collective-permute-done.14.refs_2_.refs_0_.refs_8_), custom_call_target="tpu_custom_call" | custom-call | bytes 3538944 | tf_op jit(solution)/shard_map/pallas_call | solution.py:113
  276.8 0.1 collective-permute-start.19
  276.8 0.9 collective-permute-start.16
  277.8 1.5 collective-permute-start.17
  279.3 0.5 collective-permute-start.18
  279.8 1.1 collective-permute-done.19.refs_5_.refs_7_.refs_13_.refs_15_.refs_1_.refs_9_
  280.9 11.2 %shard_map.82.total_ref = f32[512,1024]{1,0:T(8,128)} custom-call(bf16[512,8192]{1,0:T(8,128)(2,1)} %tokens_ref.11, s32[512,1]{1,0:T(8,128)} %copy.15.row_slot_ref, s32[1,256]{1,0:T(1,128)} %get-tuple-element.89.column_slot_ref, f32[512,1024]{1,0:T(8,128)} %shard_map.80.total_ref, bf16[32,9216]{1,0:T(8,128)(2,1)} %collective-permute-done.9.refs_1_.refs_0_.refs_8_, ...), custom_call_target="tpu_custom_call" | custom-call | flops 2684354560 | bytes 16777216 | tf_op jit(solution)/shard_map/pallas_call | solution.py:238
  292.0 0.8 collective-permute-done.16.refs_2_.refs_10_
  292.9 0.6 collective-permute-done.17.refs_4_.refs_12_
  293.5 1.2 collective-permute-done.18.refs_6_.refs_14_
  294.7 0.0 collective-permute-start.20
  294.7 0.5 collective-permute-start.21
  295.2 0.0 collective-permute-start.22
  295.2 1.8 collective-permute-done.20.refs_3_.refs_11_
  297.1 0.8 collective-permute-done.21.refs_5_.refs_13_
  297.9 0.8 collective-permute-done.22.refs_7_.refs_15_
  298.7 10.8 %shard_map.83 = bf16[512,1024]{1,0:T(8,128)(2,1)} custom-call(bf16[512,8192]{1,0:T(8,128)(2,1)} %tokens_ref.11, s32[512,1]{1,0:T(8,128)} %copy.15.row_slot_ref, s32[1,256]{1,0:T(1,128)} %get-tuple-element.92.column_slot_ref, f32[512,1024]{1,0:T(8,128)} %shard_map.82.total_ref, bf16[32,9216]{1,0:T(8,128)(2,1)} %collective-permute-done.14.refs_2_.refs_0_.refs_8_, ...), custom_call_target="tpu_custom_call" | custom-call | flops 2684354560 | bytes 16777216 | tf_op jit(solution)/shard_map/pallas_call | solution.py:238
Async XLA Ops:
  2.3 17.7 %collective-permute-start = (bf16[32,9216]{1,0:T(8,128)(2,1)}, bf16[32,9216]{1,0:T(8,128)(2,1)}, u32[]{:S(2)}, u32[]{:S(2)}) collective-permute-start(bf16[32,9216]{1,0:T(8,128)(2,1)} %get-tuple-element.55.refs_0_.refs_8_), channel_id=1, source_target_pairs={{0,4},{1,5},{2,6},{3,7},{4,12},{5,13},{6,14},{7,15},{8,0},{9,1},{1... | collective-permute-start | bytes 1769480 | tf_op jit(solution)/shard_map/ppermute | solution.py:283
  5.3 15.1 %collective-permute-start.1 = (bf16[32,9216]{1,0:T(8,128)(2,1)}, bf16[32,9216]{1,0:T(8,128)(2,1)}, u32[]{:S(2)}, u32[]{:S(2)}) collective-permute-start(bf16[32,9216]{1,0:T(8,128)(2,1)} %get-tuple-element.55.refs_0_.refs_8_), channel_id=1, source_target_pairs={{0,2},{1,3},{2,0},{3,1},{4,6},{5,7},{6,4},{7,5},{8,10},{9,11},{10,... | collective-permute-start | bytes 1769480 | tf_op jit(solution)/shard_map/ppermute | solution.py:283
  6.8 13.6 %collective-permute-start.2 = (bf16[32,9216]{1,0:T(8,128)(2,1)}, bf16[32,9216]{1,0:T(8,128)(2,1)}, u32[]{:S(2)}, u32[]{:S(2)}) collective-permute-start(bf16[32,9216]{1,0:T(8,128)(2,1)} %get-tuple-element.55.refs_0_.refs_8_), channel_id=1, source_target_pairs={{0,1},{1,0},{2,3},{3,2},{4,5},{5,4},{6,7},{7,6},{8,9},{9,8},{10,11... | collective-permute-start | bytes 1769480 | tf_op jit(solution)/shard_map/ppermute | solution.py:283
  6.8 13.6 %collective-permute-start.3 = (bf16[32,9216]{1,0:T(8,128)(2,1)}, bf16[32,9216]{1,0:T(8,128)(2,1)}, u32[]{:S(2)}, u32[]{:S(2)}) collective-permute-start(bf16[32,9216]{1,0:T(8,128)(2,1)} %get-tuple-element.75.refs_2_.refs_10_), channel_id=1, source_target_pairs={{0,1},{1,0},{2,3},{3,2},{4,5},{5,4},{6,7},{7,6},{8,9},{9,8},{10,11... | collective-permute-start | bytes 1769480 | tf_op jit(solution)/shard_map/ppermute | solution.py:283
  57.3 19.6 %collective-permute-start.7 = (bf16[64,9216]{1,0:T(8,128)(2,1)}, bf16[64,9216]{1,0:T(8,128)(2,1)}, u32[]{:S(2)}, u32[]{:S(2)}) collective-permute-start(bf16[64,9216]{1,0:T(8,128)(2,1)} %shard_map.75), channel_id=1, source_target_pairs={{0,1},{1,0},{2,3},{3,2},{4,5},{5,4},{6,7},{7,6},{8,9},{9,8},{10,11... | collective-permute-start | bytes 3538952 | tf_op jit(solution)/shard_map/ppermute | solution.py:283
  57.4 16.9 %collective-permute-start.4 = (bf16[32,9216]{1,0:T(8,128)(2,1)}, bf16[32,9216]{1,0:T(8,128)(2,1)}, u32[]{:S(2)}, u32[]{:S(2)}) collective-permute-start(bf16[32,9216]{1,0:T(8,128)(2,1)} %collective-permute-done.refs_0_.refs_4_.refs_12_), channel_id=1, source_target_pairs={{0,4},{1,5},{2,6},{3,7},{4,12},{5,13},{6,14},{7,15},{8,0},{9,1},{1... | collective-permute-start | bytes 1769480 | tf_op jit(solution)/shard_map/ppermute | solution.py:283
  60.0 15.7 %collective-permute-start.5 = (bf16[32,9216]{1,0:T(8,128)(2,1)}, bf16[32,9216]{1,0:T(8,128)(2,1)}, u32[]{:S(2)}, u32[]{:S(2)}) collective-permute-start(bf16[32,9216]{1,0:T(8,128)(2,1)} %collective-permute-done.refs_0_.refs_4_.refs_12_), channel_id=1, source_target_pairs={{0,2},{1,3},{2,0},{3,1},{4,6},{5,7},{6,4},{7,5},{8,10},{9,11},{10,... | collective-permute-start | bytes 1769480 | tf_op jit(solution)/shard_map/ppermute | solution.py:283
  61.5 15.4 %collective-permute-start.6 = (bf16[32,9216]{1,0:T(8,128)(2,1)}, bf16[32,9216]{1,0:T(8,128)(2,1)}, u32[]{:S(2)}, u32[]{:S(2)}) collective-permute-start(bf16[32,9216]{1,0:T(8,128)(2,1)} %collective-permute-done.1.refs_1_.refs_6_.refs_14_), channel_id=1, source_target_pairs={{0,16},{1,17},{2,18},{3,19},{4,20},{5,21},{6,22},{7,23},{8,24},{9,... | collective-permute-start | bytes 1769480 | tf_op jit(solution)/shard_map/ppermute | solution.py:283
  131.7 17.4 %collective-permute-start.11 = (bf16[96,9216]{1,0:T(8,128)(2,1)}, bf16[96,9216]{1,0:T(8,128)(2,1)}, u32[]{:S(2)}, u32[]{:S(2)}) collective-permute-start(bf16[96,9216]{1,0:T(8,128)(2,1)} %shard_map.77), channel_id=1, source_target_pairs={{0,1},{1,0},{2,3},{3,2},{4,5},{5,4},{6,7},{7,6},{8,9},{9,8},{10,11... | collective-permute-start | bytes 5308424 | tf_op jit(solution)/shard_map/ppermute | solution.py:283
  131.8 16.1 %collective-permute-start.10 = (bf16[32,9216]{1,0:T(8,128)(2,1)}, bf16[32,9216]{1,0:T(8,128)(2,1)}, u32[]{:S(2)}, u32[]{:S(2)}) collective-permute-start(bf16[32,9216]{1,0:T(8,128)(2,1)} %collective-permute-done.4.refs_0_.refs_8_), channel_id=1, source_target_pairs={{0,16},{1,17},{2,18},{3,19},{4,20},{5,21},{6,22},{7,23},{8,24},{9,... | collective-permute-start | bytes 1769480 | tf_op jit(solution)/shard_map/ppermute | solution.py:283
  133.4 15.7 %collective-permute-start.8 = (bf16[32,9216]{1,0:T(8,128)(2,1)}, bf16[32,9216]{1,0:T(8,128)(2,1)}, u32[]{:S(2)}, u32[]{:S(2)}) collective-permute-start(bf16[32,9216]{1,0:T(8,128)(2,1)} %get-tuple-element.55.refs_0_.refs_8_), channel_id=1, source_target_pairs={{0,8},{1,9},{2,10},{3,11},{4,0},{5,1},{6,2},{7,3},{8,12},{9,13},{1... | collective-permute-start | bytes 1769480 | tf_op jit(solution)/shard_map/ppermute | solution.py:283
  133.7 15.4 %collective-permute-start.9 = (bf16[32,9216]{1,0:T(8,128)(2,1)}, bf16[32,9216]{1,0:T(8,128)(2,1)}, u32[]{:S(2)}, u32[]{:S(2)}) collective-permute-start(bf16[32,9216]{1,0:T(8,128)(2,1)} %collective-permute-done.4.refs_0_.refs_8_), channel_id=1, source_target_pairs={{0,2},{1,3},{2,0},{3,1},{4,6},{5,7},{6,4},{7,5},{8,10},{9,11},{10,... | collective-permute-start | bytes 1769480 | tf_op jit(solution)/shard_map/ppermute | solution.py:283
  203.9 4.1 %collective-permute-start.15 = (bf16[96,9216]{1,0:T(8,128)(2,1)}, bf16[96,9216]{1,0:T(8,128)(2,1)}, u32[]{:S(2)}, u32[]{:S(2)}) collective-permute-start(bf16[96,9216]{1,0:T(8,128)(2,1)} %shard_map.79), channel_id=1, source_target_pairs={{0,1},{1,0},{2,3},{3,2},{4,5},{5,4},{6,7},{7,6},{8,9},{9,8},{10,11... | collective-permute-start | bytes 5308424 | tf_op jit(solution)/shard_map/ppermute | solution.py:283
  204.0 17.2 %collective-permute-start.13 = (bf16[32,9216]{1,0:T(8,128)(2,1)}, bf16[32,9216]{1,0:T(8,128)(2,1)}, u32[]{:S(2)}, u32[]{:S(2)}) collective-permute-start(bf16[32,9216]{1,0:T(8,128)(2,1)} %collective-permute-done.8.refs_0_.refs_6_.refs_14_), channel_id=1, source_target_pairs={{0,2},{1,3},{2,0},{3,1},{4,6},{5,7},{6,4},{7,5},{8,10},{9,11},{10,... | collective-permute-start | bytes 1769480 | tf_op jit(solution)/shard_map/ppermute | solution.py:283
  204.6 16.6 %collective-permute-start.12 = (bf16[32,9216]{1,0:T(8,128)(2,1)}, bf16[32,9216]{1,0:T(8,128)(2,1)}, u32[]{:S(2)}, u32[]{:S(2)}) collective-permute-start(bf16[32,9216]{1,0:T(8,128)(2,1)} %get-tuple-element.75.refs_2_.refs_10_), channel_id=1, source_target_pairs={{0,4},{1,5},{2,6},{3,7},{4,12},{5,13},{6,14},{7,15},{8,0},{9,1},{1... | collective-permute-start | bytes 1769480 | tf_op jit(solution)/shard_map/ppermute | solution.py:283
  206.6 15.4 %collective-permute-start.14 = (bf16[32,9216]{1,0:T(8,128)(2,1)}, bf16[32,9216]{1,0:T(8,128)(2,1)}, u32[]{:S(2)}, u32[]{:S(2)}) collective-permute-start(bf16[32,9216]{1,0:T(8,128)(2,1)} %collective-permute-done.5.refs_1_.refs_2_.refs_10_), channel_id=1, source_target_pairs={{0,16},{1,17},{2,18},{3,19},{4,20},{5,21},{6,22},{7,23},{8,24},{9,... | collective-permute-start | bytes 1769480 | tf_op jit(solution)/shard_map/ppermute | solution.py:283
  276.8 4.1 %collective-permute-start.19 = (bf16[96,9216]{1,0:T(8,128)(2,1)}, bf16[96,9216]{1,0:T(8,128)(2,1)}, u32[]{:S(2)}, u32[]{:S(2)}) collective-permute-start(bf16[96,9216]{1,0:T(8,128)(2,1)} %shard_map.81), channel_id=1, source_target_pairs={{0,1},{1,0},{2,3},{3,2},{4,5},{5,4},{6,7},{7,6},{8,9},{9,8},{10,11... | collective-permute-start | bytes 5308424 | tf_op jit(solution)/shard_map/ppermute | solution.py:283
  276.8 16.0 %collective-permute-start.16 = (bf16[32,9216]{1,0:T(8,128)(2,1)}, bf16[32,9216]{1,0:T(8,128)(2,1)}, u32[]{:S(2)}, u32[]{:S(2)}) collective-permute-start(bf16[32,9216]{1,0:T(8,128)(2,1)} %get-tuple-element.75.refs_2_.refs_10_), channel_id=1, source_target_pairs={{0,8},{1,9},{2,10},{3,11},{4,0},{5,1},{6,2},{7,3},{8,12},{9,13},{1... | collective-permute-start | bytes 1769480 | tf_op jit(solution)/shard_map/ppermute | solution.py:283
  277.8 15.7 %collective-permute-start.17 = (bf16[32,9216]{1,0:T(8,128)(2,1)}, bf16[32,9216]{1,0:T(8,128)(2,1)}, u32[]{:S(2)}, u32[]{:S(2)}) collective-permute-start(bf16[32,9216]{1,0:T(8,128)(2,1)} %collective-permute-done.10.refs_2_.refs_10_), channel_id=1, source_target_pairs={{0,2},{1,3},{2,0},{3,1},{4,6},{5,7},{6,4},{7,5},{8,10},{9,11},{10,... | collective-permute-start | bytes 1769480 | tf_op jit(solution)/shard_map/ppermute | solution.py:283
  279.3 15.4 %collective-permute-start.18 = (bf16[32,9216]{1,0:T(8,128)(2,1)}, bf16[32,9216]{1,0:T(8,128)(2,1)}, u32[]{:S(2)}, u32[]{:S(2)}) collective-permute-start(bf16[32,9216]{1,0:T(8,128)(2,1)} %collective-permute-done.13.refs_1_.refs_6_.refs_14_), channel_id=1, source_target_pairs={{0,16},{1,17},{2,18},{3,19},{4,20},{5,21},{6,22},{7,23},{8,24},{9,... | collective-permute-start | bytes 1769480 | tf_op jit(solution)/shard_map/ppermute | solution.py:283
  294.7 2.3 collective-permute-start.20
  294.7 3.2 %collective-permute-start.21 = (bf16[32,9216]{1,0:T(8,128)(2,1)}, bf16[32,9216]{1,0:T(8,128)(2,1)}, u32[]{:S(2)}, u32[]{:S(2)}) collective-permute-start(bf16[32,9216]{1,0:T(8,128)(2,1)} %collective-permute-done.17.refs_4_.refs_12_), channel_id=1, source_target_pairs={{0,1},{1,0},{2,3},{3,2},{4,5},{5,4},{6,7},{7,6},{8,9},{9,8},{10,11... | collective-permute-start | bytes 1769480 | tf_op jit(solution)/shard_map/ppermute | solution.py:283
  295.2 3.5 %collective-permute-start.22 = (bf16[32,9216]{1,0:T(8,128)(2,1)}, bf16[32,9216]{1,0:T(8,128)(2,1)}, u32[]{:S(2)}, u32[]{:S(2)}) collective-permute-start(bf16[32,9216]{1,0:T(8,128)(2,1)} %collective-permute-done.18.refs_6_.refs_14_), channel_id=1, source_target_pairs={{0,1},{1,0},{2,3},{3,2},{4,5},{5,4},{6,7},{7,6},{8,9},{9,8},{10,11... | collective-permute-start | bytes 1769480 | tf_op jit(solution)/shard_map/ppermute | solution.py:283

commit v5 on v1

v5 whole, which is shorter than its diff:
```python
import functools

import jax
import jax.numpy as jnp
import numpy as np
from jax import lax
from jax.experimental import pallas as pl
from jax.experimental.pallas import tpu as pltpu
from jax.sharding import PartitionSpec as P

RING = (0, 1, 3, 2)
PLACE_IN_RING = (0, 1, 3, 2)
DEPTH_TILE = 1024
LANES = 128
RANK = 16
VMEM_BYTES = 64 * 1024 * 1024 - 512 * 1024


def slots_of_rows(row_adapter_index, adapter_storage_slot):
    catalog = jnp.arange(adapter_storage_slot.shape[0], dtype=jnp.int32)
    return jnp.sum(
        jnp.where(row_adapter_index == catalog[None, :], adapter_storage_slot[None, :], 0),
        axis=1,
        keepdims=True,
    )


def gathered(
    tokens,
    row_adapter_index,
    adapter_storage_slot,
    base_value_weight,
    adapter_down_weight,
    adapter_up_weight,
):
    adapter_count = adapter_storage_slot.shape[0]
    rank = adapter_down_weight.shape[1]
    slot_of = slots_of_rows(row_adapter_index, adapter_storage_slot)
    down_all = lax.all_gather(
        adapter_down_weight.reshape(-1, adapter_down_weight.shape[2]), "req", axis=0, tiled=True
    )
    up_all = lax.all_gather(
        adapter_up_weight.reshape(-1, adapter_up_weight.shape[2]), "req", axis=0, tiled=True
    )
    base_partial = jnp.dot(tokens, base_value_weight, preferred_element_type=jnp.float32)
    base_output = lax.psum_scatter(base_partial, "tp", scatter_dimension=1, tiled=True)
    shrink = lax.dot_general(
        tokens, down_all, (((1,), (1,)), ((), ())), preferred_element_type=jnp.float32
    )
    column_slot = jnp.arange(adapter_count * rank, dtype=jnp.int32) // rank
    shrink = jnp.where(slot_of == column_slot[None, :], shrink, 0.0)
    shrink = lax.psum(shrink, "tp")
    high = lax.reduce_precision(shrink, 8, 7)
    rest = shrink - high
    middle = lax.reduce_precision(rest, 8, 7)
    low = rest - middle
    lora = sum(
        jnp.dot(piece.astype(jnp.bfloat16), up_all, preferred_element_type=jnp.float32)
        for piece in (low, middle, high)
    )
    return (base_output + lora).astype(jnp.bfloat16)


def params():
    return pltpu.CompilerParams(vmem_limit_bytes=VMEM_BYTES)


def started(copies):
    for copy in copies:
        copy.start()


def awaited(copies):
    for copy in copies:
        copy.wait()


def assemble_kernel(at_ref, here_ref, there_ref, front_ref, back_ref, sems):
    y, core = at_ref[0], at_ref[1]
    count, _, half = front_ref.shape
    count //= 2
    columns = pl.ds(pl.multiple_of(core * half, half), half)
    copies = []
    for back, out_ref in ((0, front_ref), (1, back_ref)):
        first = count * (y + back - 2 * y * back)
        for source, of_core in ((here_ref, core), (there_ref, 1 - core)):
            copies.append(
                pltpu.make_async_copy(
                    source.at[pl.ds(first, count), :, columns],
                    out_ref.at[pl.ds(of_core * count, count)],
                    sems.at[len(copies)],
                )
            )
    started(copies)
    awaited(copies)


def assemble(y, core, here, there):
    held, rank, depth = here.shape
    piece = jax.ShapeDtypeStruct((held, rank, depth // 2), here.dtype)
    anywhere = pl.BlockSpec(memory_space=pl.ANY)
    vmem = pl.BlockSpec(memory_space=pltpu.VMEM)
    return pl.pallas_call(
        assemble_kernel,
        out_shape=(piece, piece),
        in_specs=[pl.BlockSpec(memory_space=pltpu.SMEM), anywhere, anywhere],
        out_specs=(vmem, vmem),
        scratch_shapes=[pltpu.SemaphoreType.DMA((4,))],
        compiler_params=params(),
    )(jnp.stack([y, core]), here, there)


def base_kernel(steps, tokens_ref, weight_ref, *refs):
    step = pl.program_id(0)
    more = len(refs) > 1
    out_ref = refs[1] if more else refs[0]
    copies = [pltpu.make_async_copy(refs[0], refs[2], refs[3].at[0])] if more else []
    part = jnp.dot(tokens_ref[...], weight_ref[...], preferred_element_type=jnp.float32)

    @pl.when(step == 0)
    def _():
        started(copies)
        out_ref[...] = part

    @pl.when(step > 0)
    def _():
        out_ref[...] += part

    if more:

        @pl.when(step == steps - 1)
        def _():
            awaited(copies)
            out_ref[...] += refs[2][...]


def base_part(tokens, weight, begin, end, total=None):
    rows, depth = tokens.shape
    width = weight.shape[1]
    steps, first = (end - begin) // DEPTH_TILE, begin // DEPTH_TILE
    result = jax.ShapeDtypeStruct((rows, width), jnp.float32)
    more = total is not None
    return pl.pallas_call(
        functools.partial(base_kernel, steps),
        out_shape=result,
        grid=(steps,),
        in_specs=[
            pl.BlockSpec((rows, DEPTH_TILE), lambda k: (0, first + k)),
            pl.BlockSpec((DEPTH_TILE, width), lambda k: (first + k, 0)),
        ]
        + [pl.BlockSpec(memory_space=pl.ANY)] * more,
        out_specs=pl.BlockSpec((rows, width), lambda k: (0, 0)),
        scratch_shapes=[pltpu.VMEM((rows, width), jnp.float32), pltpu.SemaphoreType.DMA((1,))]
        if more
        else [],
        cost_estimate=pl.CostEstimate(
            flops=2 * rows * width * (end - begin),
            bytes_accessed=2 * (rows + width) * (end - begin) + 4 * rows * width,
            transcendentals=0,
        ),
        compiler_params=params(),
    )(tokens, weight, *([total] if more else []))


def absorb_kernel(
    count, more, at_ref, row_slot_ref, column_slot_ref, tokens_ref, other_ref, *refs
):
    sources, refs = refs[:count], refs[count:]
    before, refs = refs[: 2 * more], refs[2 * more :]
    outs, (rows_ref, down_ref, sems) = refs[:2], refs[2:]
    rows = tokens_ref.shape[0]
    block, half = sources[0].shape
    core = at_ref[1]
    downs = [
        pltpu.make_async_copy(source, down_ref.at[pl.ds(n * block, block)], sems.at[n])
        for n, source in enumerate(sources)
    ]
    started(downs)
    tiles = []
    for k in range(half // DEPTH_TILE):
        source_columns = pl.ds(
            pl.multiple_of(core * half + k * DEPTH_TILE, DEPTH_TILE), DEPTH_TILE
        )
        columns = pl.ds(k * DEPTH_TILE, DEPTH_TILE)
        pair = [
            pltpu.make_async_copy(
                source.at[:, source_columns],
                rows_ref.at[pl.ds(n * rows, rows), columns],
                sems.at[count + 2 * k + n],
            )
            for n, source in enumerate((tokens_ref, other_ref))
        ]
        started(pair)
        tiles.append((pair, columns))
    awaited(downs)
    shrink = None
    for pair, columns in tiles:
        awaited(pair)
        part = lax.dot_general(
            rows_ref[:, columns],
            down_ref[:, columns],
            (((1,), (1,)), ((), ())),
            preferred_element_type=jnp.float32,
        )
        shrink = part if shrink is None else shrink + part
    kept = jnp.where(row_slot_ref[...] == column_slot_ref[...], shrink, 0.0)
    folded = sum(kept[:, n : n + LANES] for n in range(0, kept.shape[1], LANES))
    shift = LANES // 2
    while shift >= RANK:
        folded += pltpu.roll(folded, shift, 1)
        shift //= 2
    for n, out_ref in enumerate(outs):
        own = folded[n * rows : (n + 1) * rows]
        out_ref[...] = own + before[n][...] if more else own


def absorb(at, row_slots, column_slot, tokens, other, pieces, before=None):
    rows, depth = tokens.shape
    block, half = pieces[0].shape
    columns = block * len(pieces)
    anywhere = pl.BlockSpec(memory_space=pl.ANY)
    vmem = pl.BlockSpec(memory_space=pltpu.VMEM)
    more = before is not None
    state = jax.ShapeDtypeStruct((rows, LANES), jnp.float32)
    return pl.pallas_call(
        functools.partial(absorb_kernel, len(pieces), more),
        out_shape=(state, state),
        in_specs=[pl.BlockSpec(memory_space=pltpu.SMEM), vmem, vmem]
        + [anywhere] * (2 + len(pieces))
        + [vmem] * (2 * more),
        out_specs=(vmem, vmem),
        scratch_shapes=[
            pltpu.VMEM((2 * rows, half), jnp.bfloat16),
            pltpu.VMEM((columns, half), jnp.bfloat16),
            pltpu.SemaphoreType.DMA((len(pieces) + 2 * (half // DEPTH_TILE),)),
        ],
        cost_estimate=pl.CostEstimate(
            flops=4 * rows * columns * half,
            bytes_accessed=2 * (2 * rows + columns) * half,
            transcendentals=0,
        ),
        compiler_params=params(),
    )(at, row_slots, column_slot, tokens, other, *pieces, *(before or ()))


def finish_kernel(row_slot_ref, mine_ref, theirs_ref, total_ref, up_ref, out_ref, total, up, sems):
    rows = out_ref.shape[0]
    copies = [
        pltpu.make_async_copy(up_ref, up, sems.at[0]),
        pltpu.make_async_copy(total_ref, total, sems.at[1]),
    ]
    started(copies)
    shrink = mine_ref[...] + theirs_ref[...]
    lane_slot = lax.broadcasted_iota(jnp.int32, (rows, LANES), 1) // RANK
    high, low = [], []
    for n in range(up.shape[0] // LANES):
        kept = jnp.where(row_slot_ref[...] == lane_slot + n * (LANES // RANK), shrink, 0.0)
        high.append(kept.astype(jnp.bfloat16))
        low.append((kept - high[-1].astype(jnp.float32)).astype(jnp.bfloat16))
    awaited(copies)
    lora = jnp.dot(jnp.concatenate(low, axis=1), up[...], preferred_element_type=jnp.float32)
    lora += jnp.dot(jnp.concatenate(high, axis=1), up[...], preferred_element_type=jnp.float32)
    out_ref[...] = (total[...] + lora).astype(out_ref.dtype)


def finish(row_slot, mine, theirs, total, up):
    rows, width = total.shape
    anywhere = pl.BlockSpec(memory_space=pl.ANY)
    vmem = pl.BlockSpec(memory_space=pltpu.VMEM)
    return pl.pallas_call(
        finish_kernel,
        out_shape=jax.ShapeDtypeStruct((rows, width), jnp.bfloat16),
        in_specs=[vmem, vmem, vmem, anywhere, anywhere],
        out_specs=vmem,
        scratch_shapes=[
            pltpu.VMEM((rows, width), jnp.float32),
            pltpu.VMEM(up.shape, up.dtype),
            pltpu.SemaphoreType.DMA((2,)),
        ],
        cost_estimate=pl.CostEstimate(
            flops=4 * rows * width * up.shape[0],
            bytes_accessed=6 * rows * width + 2 * up.size,
            transcendentals=0,
        ),
        compiler_params=params(),
    )(row_slot, mine, theirs, total, up)


def passed_round(
    tokens,
    row_adapter_index,
    adapter_storage_slot,
    base_value_weight,
    adapter_down_weight,
    adapter_up_weight,
):
    rows, depth = tokens.shape
    held, rank, _ = adapter_down_weight.shape
    axes = ("groups", "req")
    planes, owners = lax.axis_size("groups"), lax.axis_size("req")
    y, owner = lax.axis_index("groups"), lax.axis_index("req")
    at = jnp.stack([y, owner % 2])

    def permuted(array, target):
        pairs = [
            (g * owners + r, target(g, r)) for g in range(planes) for r in range(owners)
        ]
        return lax.ppermute(array, axes, pairs)

    def along_z(r, by):
        return RING[(PLACE_IN_RING[r // 4] + by) % 4] * 4 + r % 4

    z_ring = lambda array: permuted(array, lambda g, r: g * owners + along_z(r, 1))
    z_back = lambda array: permuted(array, lambda g, r: g * owners + along_z(r, -1))
    x_swap = lambda array: permuted(array, lambda g, r: g * owners + (r ^ 2))
    y_swap = lambda array: permuted(array, lambda g, r: (1 - g) * owners + r)
    core_swap = lambda array: permuted(array, lambda g, r: g * owners + (r ^ 1))

    def slots(g, r, step, other_x, back):
        chip = (along_z(r, -step) ^ (2 * other_x)) & ~1
        half = held // 2
        return [
            (chip + core) * held + (g ^ back) * half + unit
            for core in (0, 1)
            for unit in range(half)
        ]

    groups = (
        ((0, 0, 0), (0, 0, 1), (1, 0, 0), (0, 1, 0)),
        ((2, 0, 0), (1, 1, 0), (0, 1, 1), (3, 0, 0)),
        ((2, 1, 0), (2, 0, 1), (1, 0, 1), (3, 1, 0)),
        ((1, 1, 1), (3, 0, 1), (2, 1, 1), (3, 1, 1)),
    )
    table = np.array(
        [
            [
                [np.repeat([slot for piece in group for slot in slots(g, r, *piece)], rank)]
                for group in groups
            ]
            for g in range(planes)
            for r in range(owners)
        ],
        np.int32,
    )

    def together(*values):
        return lax.optimization_barrier(values)

    there = core_swap(adapter_down_weight)
    up = lax.all_gather(
        adapter_up_weight.reshape(held * rank, -1), "req", axis=0, tiled=True
    )
    column_slots = lax.dynamic_index_in_dim(jnp.array(table), y * owners + owner, 0, keepdims=False)
    row_slot = slots_of_rows(row_adapter_index, adapter_storage_slot)
    there, tokens_late = together(there, tokens)
    other = core_swap(tokens_late)
    other_slot = core_swap(row_slot[:, 0])
    front, back = [
        piece.reshape(held * rank, -1)
        for piece in assemble(y, owner % 2, adapter_down_weight, there)
    ]

    z1, x0 = z_ring(front), x_swap(front)
    total = base_part(tokens, base_value_weight, 0, depth // 2)
    row_slots = jnp.concatenate([row_slot, other_slot[:, None]], axis=0)
    z1, x0, front, back, total, row_slots, column_slots = together(
        z1, x0, front, back, total, row_slots, column_slots
    )

    z2, x1, yx0 = z_ring(z1), x_swap(z1), y_swap(x0)
    total = base_part(tokens, base_value_weight, depth // 2, depth, total)
    z2, x1, yx0, front, other, total = together(z2, x1, yx0, front, other, total)
    update = lambda number, pieces, before=None: absorb(
        at, row_slots, column_slots[number], tokens, other, pieces, before
    )

    z3, x2, yz2 = z_back(front), x_swap(z2), y_swap(z2)
    state = update(0, [front, back, z1, x0])
    z3, x2, yz2, x1, back, state = together(z3, x2, yz2, x1, back, state)

    zb1, x3, yx1 = z_ring(back), x_swap(z3), y_swap(x1)
    state = update(1, [z2, x1, yx0, z3], state)
    zb1, x3, yx1, yz2, back, state, up = together(zb1, x3, yx1, yz2, back, state, up)

    zb3, xyz2, yx3 = z_back(back), x_swap(yz2), y_swap(x3)
    state = update(2, [x2, yz2, zb1, x3], state)
    zb3, xyz2, yx3, state = together(zb3, xyz2, yx3, state)

    state = update(3, [yx1, zb3, xyz2, yx3], state)
    mine, others = state
    return finish(row_slot, mine, core_swap(others), total, up)


def solution(mesh):
    placed = (
        P(("groups", "req"), "tp"),
        P(("groups", "req"), None),
        P(),
        P("tp", None),
        P("req", None, "tp"),
        P("req", None, "tp"),
    )
    sizes = mesh.shape
    small = sizes["groups"] == 2 and sizes["req"] == 16 and sizes["tp"] == 1
    return jax.shard_map(
        passed_round if small else gathered,
        mesh=mesh,
        in_specs=placed,
        out_specs=P(("groups", "req"), "tp"),
        check_vma=False,
    )
```

time: 209 us -> 139 us (0.67)
  waiting for transfers between devices: 159 us -> 17.6 us
  Pallas kernels: 0 us -> 68.5 us
  matrix products: 35.1 us -> 0 us
  starting transfers between devices: 0.04 us -> 34 us
  local copies, waits for them, and re-layouts: 0.02 us -> 3.88 us
    all_gather x2 -> x1, waiting for transfers between devices: 158 us -> 0.02 us  [passed_round(): lax.all_gather(adapter_up_weight.reshape(held * rank, -1), 'req', axis=0,...]
    pallas_call x0 -> x8, Pallas kernels: none -> 68.5 us  [the longest x4 39.3 us: absorb(): pl.pallas_call(functools.partial(absorb_kernel, len(pieces), more), out_s...]
    dot_general x5 -> x0, matrix products: 35.1 us -> none  [the longest x1 14.4 us: per_device(): lax.dot_general(tokens, down_all, (((1,), (1,)), ((), ())), preferred_ele...]
    ppermute x0 -> x18, starting transfers between devices: none -> 34 us  [permuted(): return lax.ppermute(array, axes, pairs)]
    ppermute x0 -> x18, waiting for transfers between devices: none -> 17.6 us  [permuted(): return lax.ppermute(array, axes, pairs)]
  transfers between devices with their start and end apart: 2 -> 19, of which waited for: 2 -> 6; matrix products, arithmetic and copies ran while one was open for 7% -> 3% of each run, Pallas kernels for 0% -> 37%
where the time goes in v5:
time: 139 us
  Pallas kernels  68.5 us (49%)
  starting transfers between devices  34 us (24%)
  waiting for transfers between devices  17.6 us (13%)
  between operations  13.5 us (10%)
  local copies, waits for them, and re-layouts  3.88 us (3%)
    pallas_call x4, Pallas kernels, absorb(): pl.pallas_call(functools.partial(absorb_kernel, len(pieces), more), out_s...  39.3 us
    ppermute x18, starting transfers between devices, permuted(): return lax.ppermute(array, axes, pairs)  34 us
    pallas_call x2, Pallas kernels, base_part(): pl.pallas_call(functools.partial(base_kernel, steps), out_shape=result, g...  19.7 us
    ppermute x18, waiting for transfers between devices, permuted(): return lax.ppermute(array, axes, pairs)  17.6 us
    pallas_call x1, Pallas kernels, finish(): pl.pallas_call(finish_kernel, out_shape=jax.ShapeDtypeStruct((rows, width...  6.65 us
    pallas_call x1, Pallas kernels, assemble(): pl.pallas_call(assemble_kernel, out_shape=(piece, piece), in_specs=[pl.Bl...  2.83 us
  transfers between devices with their start and end apart: 19, of which 6 were waited for; matrix products, arithmetic and copies ran while one was open for 3% of the time, Pallas kernels for 37%

profile of v5, /device:TPU:0, one launch (start us, length us, event | category | flops | bytes accessed | tf_op | source)
XLA Modules:
  0.0 139.0 jit_solution(17762505318930368948)
XLA Ops:
  6.5 0.0 all-gather.2.cloned.1.call-start
  6.5 0.5 collective-permute-start
  7.0 2.6 %collective-permute-done.there_ref = bf16[4,16,8192]{2,1,0:T(8,128)(2,1)} collective-permute-done((bf16[4,16,8192]{2,1,0:T(8,128)(2,1)}, bf16[4,16,8192]{2,1,0:T(8,128)(2,1)}, u32[]{:S(2)}, u32[]{:S(2)}) %collective-permute-start) | collective-permute-done | bytes 1048608 | tf_op jit(solution)/shard_map/ppermute | solution.py:308
  9.6 0.4 collective-permute-start.7
  10.0 0.0 all-gather.2.cloned.1.call-update
  10.0 0.8 select_reduce_fusion
  10.8 0.2 collective-permute-start.3
  11.0 0.6 pad_add_fusion.1.at_ref
  11.6 2.8 %shard_map.73 = (bf16[4,16,4096]{2,1,0:T(8,128)(2,1)}, bf16[4,16,4096]{2,1,0:T(8,128)(2,1)}) custom-call(s32[2]{0:T(128)} %pad_add_fusion.1.at_ref, bf16[4,16,8192]{2,1,0:T(8,128)(2,1)} %here_ref.1, bf16[4,16,8192]{2,1,0:T(8,128)(2,1)} %collective-permute-done.there_ref), custom_call_target="tpu_custom_call" | custom-call | tf_op jit(solution)/shard_map/pallas_call | solution.py:103
  14.4 3.0 %collective-permute-start.1 = (bf16[64,4096]{1,0:T(8,128)(2,1)}, bf16[64,4096]{1,0:T(8,128)(2,1)}, u32[]{:S(2)}, u32[]{:S(2)}) collective-permute-start(bf16[64,4096]{1,0:T(8,128)(2,1)} %bitcast.21), channel_id=1, source_target_pairs={{0,4},{1,5},{2,6},{3,7},{4,12},{5,13},{6,14},{7,15},{8,0},{9,1},{1... | collective-permute-start | bytes 1572872 | tf_op jit(solution)/shard_map/ppermute | solution.py:308
  17.4 1.5 %collective-permute-start.2 = (bf16[64,4096]{1,0:T(8,128)(2,1)}, bf16[64,4096]{1,0:T(8,128)(2,1)}, u32[]{:S(2)}, u32[]{:S(2)}) collective-permute-start(bf16[64,4096]{1,0:T(8,128)(2,1)} %bitcast.22), channel_id=1, source_target_pairs={{0,2},{1,3},{2,0},{3,1},{4,6},{5,7},{6,4},{7,5},{8,10},{9,11},{10,... | collective-permute-start | bytes 1572872 | tf_op jit(solution)/shard_map/ppermute | solution.py:308
  18.9 9.6 %shard_map.74.refs_0_ = f32[512,1024]{1,0:T(8,128)} custom-call(bf16[512,8192]{1,0:T(8,128)(2,1)} %tokens_ref.11, bf16[8192,1024]{1,0:T(8,128)(2,1)} %weight_ref.3), custom_call_target="tpu_custom_call" | custom-call | flops 4294967296 | bytes 14680064 | tf_op jit(solution)/shard_map/pallas_call | solution.py:143
  28.6 0.7 dynamic-slice_bitcast_fusion
  29.3 0.0 collective-permute-done.3
  29.3 5.7 %collective-permute-done.1.refs_2_ = bf16[64,4096]{1,0:T(8,128)(2,1)} collective-permute-done((bf16[64,4096]{1,0:T(8,128)(2,1)}, bf16[64,4096]{1,0:T(8,128)(2,1)}, u32[]{:S(2)}, u32[]{:S(2)}) %collective-permute-start.1) | collective-permute-done | bytes 524320 | tf_op jit(solution)/shard_map/ppermute | solution.py:308
  35.0 0.0 collective-permute-done.2.refs_3_
  35.0 1.0 collective-permute-start.4
  36.0 1.5 %collective-permute-start.5 = (bf16[64,4096]{1,0:T(8,128)(2,1)}, bf16[64,4096]{1,0:T(8,128)(2,1)}, u32[]{:S(2)}, u32[]{:S(2)}) collective-permute-start(bf16[64,4096]{1,0:T(8,128)(2,1)} %collective-permute-done.1.refs_2_), channel_id=1, source_target_pairs={{0,2},{1,3},{2,0},{3,1},{4,6},{5,7},{6,4},{7,5},{8,10},{9,11},{10,... | collective-permute-start | bytes 1572872 | tf_op jit(solution)/shard_map/ppermute | solution.py:308
  37.5 1.5 %collective-permute-start.6 = (bf16[64,4096]{1,0:T(8,128)(2,1)}, bf16[64,4096]{1,0:T(8,128)(2,1)}, u32[]{:S(2)}, u32[]{:S(2)}) collective-permute-start(bf16[64,4096]{1,0:T(8,128)(2,1)} %collective-permute-done.2.refs_3_), channel_id=1, source_target_pairs={{0,16},{1,17},{2,18},{3,19},{4,20},{5,21},{6,22},{7,23},{8,24},{9,... | collective-permute-start | bytes 1572872 | tf_op jit(solution)/shard_map/ppermute | solution.py:308
  39.1 10.1 %shard_map.75.total_ref = f32[512,1024]{1,0:T(8,128)} custom-call(bf16[512,8192]{1,0:T(8,128)(2,1)} %tokens_ref.11, bf16[8192,1024]{1,0:T(8,128)(2,1)} %weight_ref.3, f32[512,1024]{1,0:T(8,128)} %shard_map.74.refs_0_), custom_call_target="tpu_custom_call" | custom-call | flops 4294967296 | bytes 14680064 | tf_op jit(solution)/shard_map/pallas_call | solution.py:143
  49.2 5.2 %collective-permute-done.4.refs_0_ = bf16[64,4096]{1,0:T(8,128)(2,1)} collective-permute-done((bf16[64,4096]{1,0:T(8,128)(2,1)}, bf16[64,4096]{1,0:T(8,128)(2,1)}, u32[]{:S(2)}, u32[]{:S(2)}) %collective-permute-start.4) | collective-permute-done | bytes 524320 | tf_op jit(solution)/shard_map/ppermute | solution.py:308
  54.4 0.2 collective-permute-done.5.refs_1_
  54.7 0.0 collective-permute-done.6.refs_2_
  54.7 0.0 collective-permute-done.7.other_ref
  54.7 1.5 %collective-permute-start.10 = (bf16[64,4096]{1,0:T(8,128)(2,1)}, bf16[64,4096]{1,0:T(8,128)(2,1)}, u32[]{:S(2)}, u32[]{:S(2)}) collective-permute-start(bf16[64,4096]{1,0:T(8,128)(2,1)} %collective-permute-done.4.refs_0_), channel_id=1, source_target_pairs={{0,16},{1,17},{2,18},{3,19},{4,20},{5,21},{6,22},{7,23},{8,24},{9,... | collective-permute-start | bytes 1572872 | tf_op jit(solution)/shard_map/ppermute | solution.py:308
  56.1 1.6 %collective-permute-start.8 = (bf16[64,4096]{1,0:T(8,128)(2,1)}, bf16[64,4096]{1,0:T(8,128)(2,1)}, u32[]{:S(2)}, u32[]{:S(2)}) collective-permute-start(bf16[64,4096]{1,0:T(8,128)(2,1)} %bitcast.23), channel_id=1, source_target_pairs={{0,8},{1,9},{2,10},{3,11},{4,0},{5,1},{6,2},{7,3},{8,12},{9,13},{1... | collective-permute-start | bytes 1572872 | tf_op jit(solution)/shard_map/ppermute | solution.py:308
  57.8 2.0 %collective-permute-start.9 = (bf16[64,4096]{1,0:T(8,128)(2,1)}, bf16[64,4096]{1,0:T(8,128)(2,1)}, u32[]{:S(2)}, u32[]{:S(2)}) collective-permute-start(bf16[64,4096]{1,0:T(8,128)(2,1)} %collective-permute-done.4.refs_0_), channel_id=1, source_target_pairs={{0,2},{1,3},{2,0},{3,1},{4,6},{5,7},{6,4},{7,5},{8,10},{9,11},{10,... | collective-permute-start | bytes 1572872 | tf_op jit(solution)/shard_map/ppermute | solution.py:308
  59.8 1.0 copy.19.row_slot_ref
  60.9 0.6 slice_bitcast_fusion
  61.5 9.7 %shard_map.76 = (f32[512,128]{1,0:T(8,128)}, f32[512,128]{1,0:T(8,128)}) custom-call(s32[2]{0:T(128)} %pad_add_fusion.1.at_ref, s32[1024,1]{1,0:T(8,128)} %copy.19.row_slot_ref, s32[1,256]{1,0:T(1,128)} %get-tuple-element.97.column_slot_ref, bf16[512,8192]{1,0:T(8,128)(2,1)} %tokens_ref.11, bf16[512,8192]{1,0:T(8,128)(2,1)} %collective-permute-done.7.other_ref, ...), custom_call_target="tpu_custom_call" | custom-call | flops 2147483648 | bytes 10485760 | tf_op jit(solution)/shard_map/pallas_call | solution.py:225
  71.2 0.0 collective-permute-done.10.refs_1_
  71.2 0.0 collective-permute-done.8.refs_3_
  71.2 0.0 collective-permute-done.9.refs_0_
  71.2 14.2 %collective-permute-start.11 = (bf16[64,4096]{1,0:T(8,128)(2,1)}, bf16[64,4096]{1,0:T(8,128)(2,1)}, u32[]{:S(2)}, u32[]{:S(2)}) collective-permute-start(bf16[64,4096]{1,0:T(8,128)(2,1)} %bitcast.19), channel_id=1, source_target_pairs={{0,4},{1,5},{2,6},{3,7},{4,12},{5,13},{6,14},{7,15},{8,0},{9,1},{1... | collective-permute-start | bytes 1572872 | tf_op jit(solution)/shard_map/ppermute | solution.py:308
  85.5 1.9 %collective-permute-start.12 = (bf16[64,4096]{1,0:T(8,128)(2,1)}, bf16[64,4096]{1,0:T(8,128)(2,1)}, u32[]{:S(2)}, u32[]{:S(2)}) collective-permute-start(bf16[64,4096]{1,0:T(8,128)(2,1)} %collective-permute-done.8.refs_3_), channel_id=1, source_target_pairs={{0,2},{1,3},{2,0},{3,1},{4,6},{5,7},{6,4},{7,5},{8,10},{9,11},{10,... | collective-permute-start | bytes 1572872 | tf_op jit(solution)/shard_map/ppermute | solution.py:308
  87.4 0.5 collective-permute-start.13
  87.9 9.9 %shard_map.77 = (f32[512,128]{1,0:T(8,128)}, f32[512,128]{1,0:T(8,128)}) custom-call(s32[2]{0:T(128)} %pad_add_fusion.1.at_ref, s32[1024,1]{1,0:T(8,128)} %copy.19.row_slot_ref, s32[1,256]{1,0:T(1,128)} %get-tuple-element.96.column_slot_ref, bf16[512,8192]{1,0:T(8,128)(2,1)} %tokens_ref.11, bf16[512,8192]{1,0:T(8,128)(2,1)} %collective-permute-done.7.other_ref, ...), custom_call_target="tpu_custom_call" | custom-call | flops 2147483648 | bytes 10485760 | tf_op jit(solution)/shard_map/pallas_call | solution.py:225
  97.7 0.0 all-gather.2.cloned.1.call-done.up_ref
  97.7 2.8 %collective-permute-done.11.refs_2_ = bf16[64,4096]{1,0:T(8,128)(2,1)} collective-permute-done((bf16[64,4096]{1,0:T(8,128)(2,1)}, bf16[64,4096]{1,0:T(8,128)(2,1)}, u32[]{:S(2)}, u32[]{:S(2)}) %collective-permute-start.11) | collective-permute-done | bytes 524320 | tf_op jit(solution)/shard_map/ppermute | solution.py:308
  100.6 0.0 collective-permute-done.12.refs_3_
  100.6 0.0 collective-permute-done.13.refs_0_
  100.6 1.4 %collective-permute-start.14 = (bf16[64,4096]{1,0:T(8,128)(2,1)}, bf16[64,4096]{1,0:T(8,128)(2,1)}, u32[]{:S(2)}, u32[]{:S(2)}) collective-permute-start(bf16[64,4096]{1,0:T(8,128)(2,1)} %bitcast.20), channel_id=1, source_target_pairs={{0,8},{1,9},{2,10},{3,11},{4,0},{5,1},{6,2},{7,3},{8,12},{9,13},{1... | collective-permute-start | bytes 1572872 | tf_op jit(solution)/shard_map/ppermute | solution.py:308
  102.0 0.3 collective-permute-start.15
  102.3 0.8 collective-permute-start.16
  103.1 9.9 %shard_map.78 = (f32[512,128]{1,0:T(8,128)}, f32[512,128]{1,0:T(8,128)}) custom-call(s32[2]{0:T(128)} %pad_add_fusion.1.at_ref, s32[1024,1]{1,0:T(8,128)} %copy.19.row_slot_ref, s32[1,256]{1,0:T(1,128)} %get-tuple-element.95.column_slot_ref, bf16[512,8192]{1,0:T(8,128)(2,1)} %tokens_ref.11, bf16[512,8192]{1,0:T(8,128)(2,1)} %collective-permute-done.7.other_ref, ...), custom_call_target="tpu_custom_call" | custom-call | flops 2147483648 | bytes 10485760 | tf_op jit(solution)/shard_map/pallas_call | solution.py:225
  113.0 0.0 collective-permute-done.14.refs_1_
  113.0 0.0 collective-permute-done.15.refs_2_
  113.0 0.0 collective-permute-done.16.refs_3_
  113.0 9.9 %shard_map.79 = (f32[512,128]{1,0:T(8,128)}, f32[512,128]{1,0:T(8,128)}) custom-call(s32[2]{0:T(128)} %pad_add_fusion.1.at_ref, s32[1024,1]{1,0:T(8,128)} %copy.19.row_slot_ref, s32[1,256]{1,0:T(1,128)} %get-tuple-element.98.column_slot_ref, bf16[512,8192]{1,0:T(8,128)(2,1)} %tokens_ref.11, bf16[512,8192]{1,0:T(8,128)(2,1)} %collective-permute-done.7.other_ref, ...), custom_call_target="tpu_custom_call" | custom-call | flops 2147483648 | bytes 10485760 | tf_op jit(solution)/shard_map/pallas_call | solution.py:225
  122.9 0.1 collective-permute-start.17
  123.0 0.9 copy.20.row_slot_ref
  123.9 0.9 collective-permute-done.17.theirs_ref
  124.7 0.0 copy-start
  124.7 0.7 copy-done
  125.5 6.6 %shard_map.80 = bf16[512,1024]{1,0:T(8,128)(2,1)} custom-call(s32[512,1]{1,0:T(8,128)} %copy.20.row_slot_ref, f32[512,128]{1,0:T(8,128)} %get-tuple-element.91.mine_ref, f32[512,128]{1,0:T(8,128)} %copy-done, f32[512,1024]{1,0:T(8,128)} %shard_map.75.total_ref, bf16[1024,1024]{1,0:T(8,128)(2,1)} %all-gather.2.cloned.1.call-done.up_ref), custom_call_target="tpu_custom_call" | custom-call | flops 2147483648 | bytes 5242880 | tf_op jit(solution)/shard_map/pallas_call | solution.py:270
  (1 shorter events, 0.0 us)
Async XLA Ops:
  6.5 91.2 %all-gather.2.cloned.1.call-start = ((), (), s32[]{:S(2)}) async-start(), calls=%async_computation | async-start | bytes 2228224 | tf_op jit(solution)/shard_map/all_gather | solution.py:350
  6.5 3.1 %collective-permute-start = (bf16[4,16,8192]{2,1,0:T(8,128)(2,1)}, bf16[4,16,8192]{2,1,0:T(8,128)(2,1)}, u32[]{:S(2)}, u32[]{:S(2)}) collective-permute-start(bf16[4,16,8192]{2,1,0:T(8,128)(2,1)} %here_ref.1), channel_id=1, source_target_pairs={{0,1},{1,0},{2,3},{3,2},{4,5},{5,4},{6,7},{7,6},{8,9},{9,8},{10,11... | collective-permute-start | bytes 3145736 | tf_op jit(solution)/shard_map/ppermute | solution.py:308
  9.6 45.0 %collective-permute-start.7 = (bf16[512,8192]{1,0:T(8,128)(2,1)}, bf16[512,8192]{1,0:T(8,128)(2,1)}, u32[]{:S(2)}, u32[]{:S(2)}) collective-permute-start(bf16[512,8192]{1,0:T(8,128)(2,1)} %tokens_ref.11), channel_id=1, source_target_pairs={{0,1},{1,0},{2,3},{3,2},{4,5},{5,4},{6,7},{7,6},{8,9},{9,8},{10,11... | collective-permute-start | bytes 25165832 | tf_op jit(solution)/shard_map/ppermute | solution.py:308
  10.8 18.4 %collective-permute-start.3 = (s32[512]{0:T(512)S(1)}, s32[512]{0:T(512)S(1)}, u32[]{:S(2)}, u32[]{:S(2)}) collective-permute-start(s32[512]{0:T(512)S(1)} %select_reduce_fusion), channel_id=1, source_target_pairs={{0,1},{1,0},{2,3},{3,2},{4,5},{5,4},{6,7},{7,6},{8,9},{9,8},{10,11... | collective-permute-start | bytes 6152 | tf_op jit(solution)/shard_map/ppermute | solution.py:308
  14.4 20.6 %collective-permute-start.1 = (bf16[64,4096]{1,0:T(8,128)(2,1)}, bf16[64,4096]{1,0:T(8,128)(2,1)}, u32[]{:S(2)}, u32[]{:S(2)}) collective-permute-start(bf16[64,4096]{1,0:T(8,128)(2,1)} %bitcast.21), channel_id=1, source_target_pairs={{0,4},{1,5},{2,6},{3,7},{4,12},{5,13},{6,14},{7,15},{8,0},{9,1},{1... | collective-permute-start | bytes 1572872 | tf_op jit(solution)/shard_map/ppermute | solution.py:308
  17.4 17.6 %collective-permute-start.2 = (bf16[64,4096]{1,0:T(8,128)(2,1)}, bf16[64,4096]{1,0:T(8,128)(2,1)}, u32[]{:S(2)}, u32[]{:S(2)}) collective-permute-start(bf16[64,4096]{1,0:T(8,128)(2,1)} %bitcast.22), channel_id=1, source_target_pairs={{0,2},{1,3},{2,0},{3,1},{4,6},{5,7},{6,4},{7,5},{8,10},{9,11},{10,... | collective-permute-start | bytes 1572872 | tf_op jit(solution)/shard_map/ppermute | solution.py:308
  35.0 19.4 %collective-permute-start.4 = (bf16[64,4096]{1,0:T(8,128)(2,1)}, bf16[64,4096]{1,0:T(8,128)(2,1)}, u32[]{:S(2)}, u32[]{:S(2)}) collective-permute-start(bf16[64,4096]{1,0:T(8,128)(2,1)} %collective-permute-done.1.refs_2_), channel_id=1, source_target_pairs={{0,4},{1,5},{2,6},{3,7},{4,12},{5,13},{6,14},{7,15},{8,0},{9,1},{1... | collective-permute-start | bytes 1572872 | tf_op jit(solution)/shard_map/ppermute | solution.py:308
  36.0 18.6 %collective-permute-start.5 = (bf16[64,4096]{1,0:T(8,128)(2,1)}, bf16[64,4096]{1,0:T(8,128)(2,1)}, u32[]{:S(2)}, u32[]{:S(2)}) collective-permute-start(bf16[64,4096]{1,0:T(8,128)(2,1)} %collective-permute-done.1.refs_2_), channel_id=1, source_target_pairs={{0,2},{1,3},{2,0},{3,1},{4,6},{5,7},{6,4},{7,5},{8,10},{9,11},{10,... | collective-permute-start | bytes 1572872 | tf_op jit(solution)/shard_map/ppermute | solution.py:308
  37.5 17.1 %collective-permute-start.6 = (bf16[64,4096]{1,0:T(8,128)(2,1)}, bf16[64,4096]{1,0:T(8,128)(2,1)}, u32[]{:S(2)}, u32[]{:S(2)}) collective-permute-start(bf16[64,4096]{1,0:T(8,128)(2,1)} %collective-permute-done.2.refs_3_), channel_id=1, source_target_pairs={{0,16},{1,17},{2,18},{3,19},{4,20},{5,21},{6,22},{7,23},{8,24},{9,... | collective-permute-start | bytes 1572872 | tf_op jit(solution)/shard_map/ppermute | solution.py:308
  54.7 16.5 %collective-permute-start.10 = (bf16[64,4096]{1,0:T(8,128)(2,1)}, bf16[64,4096]{1,0:T(8,128)(2,1)}, u32[]{:S(2)}, u32[]{:S(2)}) collective-permute-start(bf16[64,4096]{1,0:T(8,128)(2,1)} %collective-permute-done.4.refs_0_), channel_id=1, source_target_pairs={{0,16},{1,17},{2,18},{3,19},{4,20},{5,21},{6,22},{7,23},{8,24},{9,... | collective-permute-start | bytes 1572872 | tf_op jit(solution)/shard_map/ppermute | solution.py:308
  56.1 15.1 %collective-permute-start.8 = (bf16[64,4096]{1,0:T(8,128)(2,1)}, bf16[64,4096]{1,0:T(8,128)(2,1)}, u32[]{:S(2)}, u32[]{:S(2)}) collective-permute-start(bf16[64,4096]{1,0:T(8,128)(2,1)} %bitcast.23), channel_id=1, source_target_pairs={{0,8},{1,9},{2,10},{3,11},{4,0},{5,1},{6,2},{7,3},{8,12},{9,13},{1... | collective-permute-start | bytes 1572872 | tf_op jit(solution)/shard_map/ppermute | solution.py:308
  57.8 13.4 %collective-permute-start.9 = (bf16[64,4096]{1,0:T(8,128)(2,1)}, bf16[64,4096]{1,0:T(8,128)(2,1)}, u32[]{:S(2)}, u32[]{:S(2)}) collective-permute-start(bf16[64,4096]{1,0:T(8,128)(2,1)} %collective-permute-done.4.refs_0_), channel_id=1, source_target_pairs={{0,2},{1,3},{2,0},{3,1},{4,6},{5,7},{6,4},{7,5},{8,10},{9,11},{10,... | collective-permute-start | bytes 1572872 | tf_op jit(solution)/shard_map/ppermute | solution.py:308
  71.2 29.4 %collective-permute-start.11 = (bf16[64,4096]{1,0:T(8,128)(2,1)}, bf16[64,4096]{1,0:T(8,128)(2,1)}, u32[]{:S(2)}, u32[]{:S(2)}) collective-permute-start(bf16[64,4096]{1,0:T(8,128)(2,1)} %bitcast.19), channel_id=1, source_target_pairs={{0,4},{1,5},{2,6},{3,7},{4,12},{5,13},{6,14},{7,15},{8,0},{9,1},{1... | collective-permute-start | bytes 1572872 | tf_op jit(solution)/shard_map/ppermute | solution.py:308
  85.5 15.1 %collective-permute-start.12 = (bf16[64,4096]{1,0:T(8,128)(2,1)}, bf16[64,4096]{1,0:T(8,128)(2,1)}, u32[]{:S(2)}, u32[]{:S(2)}) collective-permute-start(bf16[64,4096]{1,0:T(8,128)(2,1)} %collective-permute-done.8.refs_3_), channel_id=1, source_target_pairs={{0,2},{1,3},{2,0},{3,1},{4,6},{5,7},{6,4},{7,5},{8,10},{9,11},{10,... | collective-permute-start | bytes 1572872 | tf_op jit(solution)/shard_map/ppermute | solution.py:308
  87.4 13.2 %collective-permute-start.13 = (bf16[64,4096]{1,0:T(8,128)(2,1)}, bf16[64,4096]{1,0:T(8,128)(2,1)}, u32[]{:S(2)}, u32[]{:S(2)}) collective-permute-start(bf16[64,4096]{1,0:T(8,128)(2,1)} %collective-permute-done.5.refs_1_), channel_id=1, source_target_pairs={{0,16},{1,17},{2,18},{3,19},{4,20},{5,21},{6,22},{7,23},{8,24},{9,... | collective-permute-start | bytes 1572872 | tf_op jit(solution)/shard_map/ppermute | solution.py:308
  100.6 12.4 %collective-permute-start.14 = (bf16[64,4096]{1,0:T(8,128)(2,1)}, bf16[64,4096]{1,0:T(8,128)(2,1)}, u32[]{:S(2)}, u32[]{:S(2)}) collective-permute-start(bf16[64,4096]{1,0:T(8,128)(2,1)} %bitcast.20), channel_id=1, source_target_pairs={{0,8},{1,9},{2,10},{3,11},{4,0},{5,1},{6,2},{7,3},{8,12},{9,13},{1... | collective-permute-start | bytes 1572872 | tf_op jit(solution)/shard_map/ppermute | solution.py:308
  102.0 11.0 %collective-permute-start.15 = (bf16[64,4096]{1,0:T(8,128)(2,1)}, bf16[64,4096]{1,0:T(8,128)(2,1)}, u32[]{:S(2)}, u32[]{:S(2)}) collective-permute-start(bf16[64,4096]{1,0:T(8,128)(2,1)} %collective-permute-done.10.refs_1_), channel_id=1, source_target_pairs={{0,2},{1,3},{2,0},{3,1},{4,6},{5,7},{6,4},{7,5},{8,10},{9,11},{10,... | collective-permute-start | bytes 1572872 | tf_op jit(solution)/shard_map/ppermute | solution.py:308
  102.3 10.7 %collective-permute-start.16 = (bf16[64,4096]{1,0:T(8,128)(2,1)}, bf16[64,4096]{1,0:T(8,128)(2,1)}, u32[]{:S(2)}, u32[]{:S(2)}) collective-permute-start(bf16[64,4096]{1,0:T(8,128)(2,1)} %collective-permute-done.12.refs_3_), channel_id=1, source_target_pairs={{0,16},{1,17},{2,18},{3,19},{4,20},{5,21},{6,22},{7,23},{8,24},{9,... | collective-permute-start | bytes 1572872 | tf_op jit(solution)/shard_map/ppermute | solution.py:308
  122.9 1.8 %collective-permute-start.17 = (f32[512,128]{1,0:T(8,128)}, f32[512,128]{1,0:T(8,128)S(1)}, u32[]{:S(2)}, u32[]{:S(2)}) collective-permute-start(f32[512,128]{1,0:T(8,128)} %get-tuple-element.92), channel_id=1, source_target_pairs={{0,1},{1,0},{2,3},{3,2},{4,5},{5,4},{6,7},{7,6},{8,9},{9,8},{10,11... | collective-permute-start | bytes 786440 | tf_op jit(solution)/shard_map/ppermute | solution.py:308
  124.7 0.7 copy-start
Sparse Core Ops, SparseCore 0:
  10.1 51.0 all-gather.1

commit v6 on v5

v6 whole, which is shorter than its diff:
```python
import functools

import jax
import jax.numpy as jnp
import numpy as np
from jax import lax
from jax.experimental import pallas as pl
from jax.experimental.pallas import tpu as pltpu
from jax.sharding import PartitionSpec as P

RING = (0, 1, 3, 2)
PLACE_IN_RING = (0, 1, 3, 2)
DEPTH_TILE = 1024
LANES = 128
RANK = 16

PIECES = (
    *((0, 0, 0), (1, 0, 0), (0, 0, 1), (0, 1, 1)),
    *((0, 1, 0), (2, 0, 0), (1, 1, 0), (3, 0, 0)),
    *((2, 1, 0), (3, 1, 0), (2, 0, 1), (1, 0, 1)),
    *((1, 1, 1), (3, 0, 1), (2, 1, 1), (3, 1, 1)),
)
VMEM_BYTES = 64 * 1024 * 1024 - 512 * 1024


def slots_of_rows(row_adapter_index, adapter_storage_slot):
    catalog = jnp.arange(adapter_storage_slot.shape[0], dtype=jnp.int32)
    return jnp.sum(
        jnp.where(row_adapter_index == catalog[None, :], adapter_storage_slot[None, :], 0),
        axis=1,
        keepdims=True,
    )


def gathered(
    tokens,
    row_adapter_index,
    adapter_storage_slot,
    base_value_weight,
    adapter_down_weight,
    adapter_up_weight,
):
    adapter_count = adapter_storage_slot.shape[0]
    rank = adapter_down_weight.shape[1]
    slot_of = slots_of_rows(row_adapter_index, adapter_storage_slot)
    down_all = lax.all_gather(
        adapter_down_weight.reshape(-1, adapter_down_weight.shape[2]), "req", axis=0, tiled=True
    )
    up_all = lax.all_gather(
        adapter_up_weight.reshape(-1, adapter_up_weight.shape[2]), "req", axis=0, tiled=True
    )
    base_partial = jnp.dot(tokens, base_value_weight, preferred_element_type=jnp.float32)
    base_output = lax.psum_scatter(base_partial, "tp", scatter_dimension=1, tiled=True)
    shrink = lax.dot_general(
        tokens, down_all, (((1,), (1,)), ((), ())), preferred_element_type=jnp.float32
    )
    column_slot = jnp.arange(adapter_count * rank, dtype=jnp.int32) // rank
    shrink = jnp.where(slot_of == column_slot[None, :], shrink, 0.0)
    shrink = lax.psum(shrink, "tp")
    high = lax.reduce_precision(shrink, 8, 7)
    rest = shrink - high
    middle = lax.reduce_precision(rest, 8, 7)
    low = rest - middle
    lora = sum(
        jnp.dot(piece.astype(jnp.bfloat16), up_all, preferred_element_type=jnp.float32)
        for piece in (low, middle, high)
    )
    return (base_output + lora).astype(jnp.bfloat16)


def params():
    return pltpu.CompilerParams(vmem_limit_bytes=VMEM_BYTES)


def started(copies):
    for copy in copies:
        copy.start()


def awaited(copies):
    for copy in copies:
        copy.wait()


def assemble_kernel(
    info_ref, here_ref, there_ref, up_ref, front_ref, back_ref, down_ref, sems
):
    y, core = info_ref[0], info_ref[1]
    held, rank, half = down_ref.shape
    held //= 2
    columns = pl.ds(pl.multiple_of(core * half, half), half)
    copies = [
        pltpu.make_async_copy(
            source.at[:, :, columns], down_ref.at[pl.ds(of_core * held, held)], sems.at[n]
        )
        for n, (source, of_core) in enumerate(((here_ref, core), (there_ref, 1 - core)))
    ]
    started(copies)
    awaited(copies)
    quarter = half // 2
    for out_ref, place in ((front_ref, y), (back_ref, 1 - y)):
        for n in range(0, quarter, LANES):
            columns = pl.ds(pl.multiple_of(place * quarter + n, LANES), LANES)
            block = down_ref[:, :, columns].reshape(2 * held * rank, LANES)
            out_ref[n : n + LANES] = block.T
        up = up_ref[pl.ds(place * (held // 2), held // 2)].reshape(held // 2 * rank, -1)
        rows = up.shape[0]
        for n in range(up.shape[1] // LANES):
            first = quarter + n * rows
            out_ref[first : first + rows] = up[:, n * LANES : (n + 1) * LANES]


def assemble(info, here, there, up):
    held, rank, depth = here.shape
    width = up.shape[2]
    rows = depth // 4 + held // 2 * rank * width // LANES
    piece = jax.ShapeDtypeStruct((rows, LANES), here.dtype)
    anywhere = pl.BlockSpec(memory_space=pl.ANY)
    vmem = pl.BlockSpec(memory_space=pltpu.VMEM)
    return pl.pallas_call(
        assemble_kernel,
        out_shape=(piece, piece),
        in_specs=[pl.BlockSpec(memory_space=pltpu.SMEM), anywhere, anywhere, vmem],
        out_specs=(vmem, vmem),
        scratch_shapes=[
            pltpu.VMEM((2 * held, rank, depth // 2), here.dtype),
            pltpu.SemaphoreType.DMA((2,)),
        ],
        compiler_params=params(),
    )(info, here, there, up)


def base_kernel(steps, tokens_ref, weight_ref, *refs):
    step = pl.program_id(0)
    more = len(refs) > 1
    out_ref = refs[1] if more else refs[0]
    copies = [pltpu.make_async_copy(refs[0], refs[2], refs[3].at[0])] if more else []
    part = jnp.dot(tokens_ref[...], weight_ref[...], preferred_element_type=jnp.float32)

    @pl.when(step == 0)
    def _():
        started(copies)
        out_ref[...] = part

    @pl.when(step > 0)
    def _():
        out_ref[...] += part

    if more:

        @pl.when(step == steps - 1)
        def _():
            awaited(copies)
            out_ref[...] += refs[2][...]


def base_part(tokens, weight, begin, end, total=None):
    rows, depth = tokens.shape
    width = weight.shape[1]
    steps, first = (end - begin) // DEPTH_TILE, begin // DEPTH_TILE
    result = jax.ShapeDtypeStruct((rows, width), jnp.float32)
    more = total is not None
    return pl.pallas_call(
        functools.partial(base_kernel, steps),
        out_shape=result,
        grid=(steps,),
        in_specs=[
            pl.BlockSpec((rows, DEPTH_TILE), lambda k: (0, first + k)),
            pl.BlockSpec((DEPTH_TILE, width), lambda k: (first + k, 0)),
        ]
        + [pl.BlockSpec(memory_space=pl.ANY)] * more,
        out_specs=pl.BlockSpec((rows, width), lambda k: (0, 0)),
        scratch_shapes=[pltpu.VMEM((rows, width), jnp.float32), pltpu.SemaphoreType.DMA((1,))]
        if more
        else [],
        cost_estimate=pl.CostEstimate(
            flops=2 * rows * width * (end - begin),
            bytes_accessed=2 * (rows + width) * (end - begin) + 4 * rows * width,
            transcendentals=0,
        ),
        compiler_params=params(),
    )(tokens, weight, *([total] if more else []))


def absorb_kernel(
    backs, more, info_ref, row_slot_ref, column_slot_ref, tokens_ref, other_ref, *refs
):
    count = 2 * len(backs)
    sources, refs = refs[:count], refs[count:]
    before, refs = refs[: 2 * more], refs[2 * more :]
    outs, up_ref, (rows_ref, down_ref, sems) = refs[:2], refs[2], refs[3:]
    rows = tokens_ref.shape[0]
    quarter = rows_ref.shape[2]
    y, core = info_ref[0], info_ref[1]
    copies = 0
    downs, tiles = [], {}

    def begin(source, target):
        nonlocal copies
        copy = pltpu.make_async_copy(source, target, sems.at[copies])
        copies += 1
        copy.start()
        return copy

    for n, back in enumerate(backs):
        downs.append(
            [
                begin(sources[2 * n + i], down_ref.at[n, :, pl.ds(i * LANES, LANES)])
                for i in range(2)
            ]
        )
        if back in tiles:
            continue
        place = len(tiles)
        tiles[back] = []
        first = core * 2 * quarter + (1 - y if back else y) * quarter
        for k in range(0, quarter, DEPTH_TILE):
            columns = pl.ds(pl.multiple_of(first + k, DEPTH_TILE), DEPTH_TILE)
            pair = [
                begin(
                    source.at[:, columns],
                    rows_ref.at[place, pl.ds(i * rows, rows), pl.ds(k, DEPTH_TILE)],
                )
                for i, source in enumerate((tokens_ref, other_ref))
            ]
            tiles[back].append([place, k, pair])
    state = None
    for n, back in enumerate(backs):
        awaited(downs[n])
        shrink = None
        for tile in tiles[back]:
            place, k, pair = tile
            awaited(pair)
            tile[2] = []
            part = jnp.dot(
                rows_ref[place, :, k : k + DEPTH_TILE],
                down_ref[n, k : k + DEPTH_TILE, :],
                preferred_element_type=jnp.float32,
            )
            shrink = part if shrink is None else shrink + part
        for i in range(2):
            lanes = slice(i * LANES, (i + 1) * LANES)
            wanted = column_slot_ref[:, 2 * n * LANES + i * LANES : 2 * n * LANES + (i + 1) * LANES]
            kept = jnp.where(row_slot_ref[...] == wanted, shrink[:, lanes], 0.0)
            state = kept if state is None else state + kept
            height = up_ref.shape[0] // count
            for j in range(up_ref.shape[1] // LANES):
                first = quarter + j * height
                up_ref[
                    (2 * n + i) * height : (2 * n + i + 1) * height,
                    j * LANES : (j + 1) * LANES,
                ] = down_ref[n, first : first + height, lanes]
    for i, out_ref in enumerate(outs):
        own = state[i * rows : (i + 1) * rows]
        out_ref[...] = own + before[i][...] if more else own


def absorb(info, row_slots, column_slot, tokens, other, width, pairs, before=None):
    rows, depth = tokens.shape
    pieces = [piece for pair, _ in pairs for piece in pair]
    backs = [back for _, back in pairs]
    quarter = depth // 4
    height = pieces[0].shape[0]
    anywhere = pl.BlockSpec(memory_space=pl.ANY)
    vmem = pl.BlockSpec(memory_space=pltpu.VMEM)
    more = before is not None
    state = jax.ShapeDtypeStruct((rows, LANES), jnp.float32)
    up_rows = len(pieces) * (height - quarter) * LANES // width
    quarters = len(set(backs))
    copies = len(pieces) + 2 * quarters * (quarter // DEPTH_TILE)
    return pl.pallas_call(
        functools.partial(absorb_kernel, backs, more),
        out_shape=(state, state, jax.ShapeDtypeStruct((up_rows, width), tokens.dtype)),
        in_specs=[pl.BlockSpec(memory_space=pltpu.SMEM), vmem, vmem]
        + [anywhere] * (2 + len(pieces))
        + [vmem] * (2 * more),
        out_specs=(vmem, vmem, vmem),
        scratch_shapes=[
            pltpu.VMEM((quarters, 2 * rows, quarter), tokens.dtype),
            pltpu.VMEM((len(pairs), height, 2 * LANES), tokens.dtype),
            pltpu.SemaphoreType.DMA((copies,)),
        ],
        cost_estimate=pl.CostEstimate(
            flops=4 * rows * len(pieces) * LANES * quarter,
            bytes_accessed=4 * rows * quarters * quarter + 2 * len(pieces) * LANES * height,
            transcendentals=0,
        ),
        compiler_params=params(),
    )(info, row_slots, column_slot, tokens, other, *pieces, *(before or ()))


def finish_kernel(
    count, info_ref, row_slot_ref, mine_ref, theirs_ref, total_ref, *refs
):
    sources, (out_ref, total, up, sems) = refs[:count], refs[count:]
    rows = out_ref.shape[0]
    height = up.shape[0] // (len(PIECES) * 2)
    per = sources[0].shape[0] // height
    copies = [pltpu.make_async_copy(total_ref, total, sems.at[0])]
    for n in range(count * per):
        first = pl.multiple_of(info_ref[2 + n], height)
        copies.append(
            pltpu.make_async_copy(
                sources[n // per].at[pl.ds(n % per * height, height)],
                up.at[pl.ds(first, height)],
                sems.at[1 + n],
            )
        )
    started(copies)
    shrink = mine_ref[...] + theirs_ref[...]
    lane_slot = lax.broadcasted_iota(jnp.int32, (rows, LANES), 1) // RANK
    high, low = [], []
    for n in range(up.shape[0] // LANES):
        kept = jnp.where(row_slot_ref[...] == lane_slot + n * (LANES // RANK), shrink, 0.0)
        high.append(kept.astype(jnp.bfloat16))
        low.append((kept - high[-1].astype(jnp.float32)).astype(jnp.bfloat16))
    awaited(copies)
    lora = jnp.dot(jnp.concatenate(low, axis=1), up[...], preferred_element_type=jnp.float32)
    lora += jnp.dot(jnp.concatenate(high, axis=1), up[...], preferred_element_type=jnp.float32)
    out_ref[...] = (total[...] + lora).astype(out_ref.dtype)


def finish(info, row_slot, mine, theirs, total, ups):
    rows, width = total.shape
    anywhere = pl.BlockSpec(memory_space=pl.ANY)
    vmem = pl.BlockSpec(memory_space=pltpu.VMEM)
    up_rows = sum(up.shape[0] for up in ups)
    return pl.pallas_call(
        functools.partial(finish_kernel, len(ups)),
        out_shape=jax.ShapeDtypeStruct((rows, width), jnp.bfloat16),
        in_specs=[pl.BlockSpec(memory_space=pltpu.SMEM), vmem, vmem, vmem]
        + [anywhere] * (1 + len(ups)),
        out_specs=vmem,
        scratch_shapes=[
            pltpu.VMEM((rows, width), jnp.float32),
            pltpu.VMEM((up_rows, width), ups[0].dtype),
            pltpu.SemaphoreType.DMA((1 + 2 * len(PIECES),)),
        ],
        cost_estimate=pl.CostEstimate(
            flops=4 * rows * width * up_rows,
            bytes_accessed=6 * rows * width + 2 * up_rows * width,
            transcendentals=0,
        ),
        compiler_params=params(),
    )(info, row_slot, mine, theirs, total, *ups)


def passed_round(
    tokens,
    row_adapter_index,
    adapter_storage_slot,
    base_value_weight,
    adapter_down_weight,
    adapter_up_weight,
):
    rows, depth = tokens.shape
    held, rank, _ = adapter_down_weight.shape
    width = adapter_up_weight.shape[2]
    axes = ("groups", "req")
    planes, owners = lax.axis_size("groups"), lax.axis_size("req")
    device = lax.axis_index("groups") * owners + lax.axis_index("req")

    def permuted(array, target):
        pairs = [
            (g * owners + r, target(g, r)) for g in range(planes) for r in range(owners)
        ]
        return lax.ppermute(array, axes, pairs)

    def along_z(r, by):
        return RING[(PLACE_IN_RING[r // 4] + by) % 4] * 4 + r % 4

    z_ring = lambda array: permuted(array, lambda g, r: g * owners + along_z(r, 1))
    z_back = lambda array: permuted(array, lambda g, r: g * owners + along_z(r, -1))
    x_swap = lambda array: permuted(array, lambda g, r: g * owners + (r ^ 2))
    y_swap = lambda array: permuted(array, lambda g, r: (1 - g) * owners + r)
    core_swap = lambda array: permuted(array, lambda g, r: g * owners + (r ^ 1))

    def chip(r, piece):
        return (along_z(r, -piece[0]) ^ (2 * piece[1])) // 2

    per_chip = LANES // rank
    column_table, info_table = [], []
    for g in range(planes):
        for r in range(owners):
            column_table.append(
                [
                    [
                        np.repeat(
                            [chip(r, p) * per_chip + n for p in PIECES[k : k + 4] for n in range(per_chip)],
                            rank,
                        )
                    ]
                    for k in range(0, len(PIECES), 4)
                ]
            )
            info = [g, r % 2]
            for k in range(0, len(PIECES), 4):
                for core in (r % 2, 1 - r % 2):
                    for p in PIECES[k : k + 4]:
                        info.append(
                            chip(r, p) * LANES
                            + core * held * rank
                            + (g ^ p[2]) * (held // 2 * rank)
                        )
            info_table.append(info)
    here_of = lambda table: lax.dynamic_index_in_dim(
        jnp.array(np.array(table, np.int32)), device, 0, keepdims=False
    )
    info, column_slots = here_of(info_table), here_of(column_table)

    def together(*values):
        return lax.optimization_barrier(values)

    there = core_swap(adapter_down_weight)
    row_slot = slots_of_rows(row_adapter_index, adapter_storage_slot)
    there, tokens_late = together(there, tokens)
    other = core_swap(tokens_late)
    other_slot = core_swap(row_slot[:, 0])
    front, back = assemble(info, adapter_down_weight, there, adapter_up_weight)

    z1, x0 = z_ring(front), x_swap(front)
    total = base_part(tokens, base_value_weight, 0, depth // 2)
    row_slots = jnp.concatenate([row_slot, other_slot[:, None]], axis=0)
    z1, x0, front, back, total, row_slots, column_slots = together(
        z1, x0, front, back, total, row_slots, column_slots
    )

    z2, x1, yx0 = z_ring(z1), x_swap(z1), y_swap(x0)
    total = base_part(tokens, base_value_weight, depth // 2, depth, total)
    z2, x1, yx0, front, other, total = together(z2, x1, yx0, front, other, total)
    ups = []

    def update(number, pairs, before=None):
        mine, others, up = absorb(
            info, row_slots, column_slots[number], tokens, other, width, pairs, before
        )
        ups.extend([up, core_swap(up)])
        return mine, others

    z3, x2, yz2 = z_back(front), x_swap(z2), y_swap(z2)
    state = update(0, [((front, z1), 0), ((back, yx0), 1)])
    z3, x2, yz2, x1, back, state = together(z3, x2, yz2, x1, back, state)

    zb1, x3, yx1 = z_ring(back), x_swap(z3), y_swap(x1)
    state = update(1, [((x0, z2), 0), ((x1, z3), 0)], state)
    zb1, x3, yx1, yz2, back, state = together(zb1, x3, yx1, yz2, back, state)

    zb3, xyz2, yx3 = z_back(back), x_swap(yz2), y_swap(x3)
    state = update(2, [((x2, x3), 0), ((yz2, zb1), 1)], state)
    zb3, xyz2, yx3, state = together(zb3, xyz2, yx3, state)

    mine, others = update(3, [((yx1, zb3), 1), ((xyz2, yx3), 1)], state)
    return finish(info, row_slot, mine, core_swap(others), total, ups)


def solution(mesh):
    placed = (
        P(("groups", "req"), "tp"),
        P(("groups", "req"), None),
        P(),
        P("tp", None),
        P("req", None, "tp"),
        P("req", None, "tp"),
    )
    sizes = mesh.shape
    small = sizes["groups"] == 2 and sizes["req"] == 16 and sizes["tp"] == 1
    return jax.shard_map(
        passed_round if small else gathered,
        mesh=mesh,
        in_specs=placed,
        out_specs=P(("groups", "req"), "tp"),
        check_vma=False,
    )
```

time: 139 us -> 117 us (0.84)
  the two profiles are of different devices: /device:TPU:0 before, /device:TPU:17 now
where the time goes in v6:
time: 117 us
  Pallas kernels  67.2 us (57%)
  starting transfers between devices  33.2 us (28%)
  waiting for transfers between devices  10.7 us (9%)
  local copies, waits for them, and re-layouts  4.39 us (4%)
    pallas_call x4, Pallas kernels, absorb(): pl.pallas_call(functools.partial(absorb_kernel, backs, more), out_shape=(...  37.5 us
    ppermute x22, starting transfers between devices, permuted(): return lax.ppermute(array, axes, pairs)  33.2 us
    pallas_call x2, Pallas kernels, base_part(): pl.pallas_call(functools.partial(base_kernel, steps), out_shape=result, g...  19.5 us
    ppermute x22, waiting for transfers between devices, permuted(): return lax.ppermute(array, axes, pairs)  10.7 us
    pallas_call x1, Pallas kernels, finish(): pl.pallas_call(functools.partial(finish_kernel, len(ups)), out_shape=jax....  6.79 us
    pallas_call x1, Pallas kernels, assemble(): pl.pallas_call(assemble_kernel, out_shape=(piece, piece), in_specs=[pl.Bl...  3.43 us
  transfers between devices with their start and end apart: 22, of which 8 were waited for; matrix products, arithmetic and copies ran while one was open for 4% of the time, Pallas kernels for 52%

profile of v6, /device:TPU:17, one launch (start us, length us, event | category | flops | bytes accessed | tf_op | source)
XLA Modules:
  0.0 116.6 jit_solution(18207149917881915315)
XLA Ops:
  0.0 0.7 collective-permute-start
  0.7 2.6 %collective-permute-done.there_ref = bf16[4,16,8192]{2,1,0:T(8,128)(2,1)} collective-permute-done((bf16[4,16,8192]{2,1,0:T(8,128)(2,1)}, bf16[4,16,8192]{2,1,0:T(8,128)(2,1)}, u32[]{:S(2)}, u32[]{:S(2)}) %collective-permute-start) | collective-permute-done | bytes 1048608 | tf_op jit(solution)/shard_map/ppermute | solution.py:367
  3.3 0.4 collective-permute-start.7
  3.7 0.8 select_reduce_fusion
  4.5 0.2 collective-permute-start.3
  4.7 1.2 %dynamic-slice_bitcast_fusion.1.info_ref = s32[34]{0:T(128)} fusion(s32[32,34]{1,0:T(8,128)} %constant.26.clone, s32[]{:T(128)S(6)} %select_n.10), kind=kLoop, calls=%fused_computation.8 | loop fusion | bytes 276 | tf_op jit(solution)/shard_map/jit(dynamic_index_in_dim)/squeeze | solution.py:406
  5.9 3.4 %shard_map.82 = (bf16[2304,128]{1,0:T(8,128)(2,1)}, bf16[2304,128]{1,0:T(8,128)(2,1)}) custom-call(s32[34]{0:T(128)} %dynamic-slice_bitcast_fusion.1.info_ref, bf16[4,16,8192]{2,1,0:T(8,128)(2,1)} %here_ref.1, bf16[4,16,8192]{2,1,0:T(8,128)(2,1)} %collective-permute-done.there_ref, bf16[4,16,1024]{2,1,0:T(8,128)(2,1)} %up_ref.1), custom_call_target="tpu_custom_call" | custom-call | tf_op jit(solution)/shard_map/pallas_call | solution.py:120
  9.3 0.1 collective-permute-start.1
  9.4 1.3 %collective-permute-start.2 = (bf16[2304,128]{1,0:T(8,128)(2,1)}, bf16[2304,128]{1,0:T(8,128)(2,1)}, u32[]{:S(2)}, u32[]{:S(2)}) collective-permute-start(bf16[2304,128]{1,0:T(8,128)(2,1)} %get-tuple-element.64.refs_0_), channel_id=1, source_target_pairs={{0,2},{1,3},{2,0},{3,1},{4,6},{5,7},{6,4},{7,5},{8,10},{9,11},{10,... | collective-permute-start | bytes 1769480 | tf_op jit(solution)/shard_map/ppermute | solution.py:367
  10.7 9.7 %shard_map.83.refs_0_ = f32[512,1024]{1,0:T(8,128)} custom-call(bf16[512,8192]{1,0:T(8,128)(2,1)} %tokens_ref.11, bf16[8192,1024]{1,0:T(8,128)(2,1)} %weight_ref.3), custom_call_target="tpu_custom_call" | custom-call | flops 4294967296 | bytes 14680064 | tf_op jit(solution)/shard_map/pallas_call | solution.py:163
  20.3 0.7 dynamic-slice_bitcast_fusion
  21.0 0.0 collective-permute-done.3
  21.0 3.2 %collective-permute-done.1.refs_1_ = bf16[2304,128]{1,0:T(8,128)(2,1)} collective-permute-done((bf16[2304,128]{1,0:T(8,128)(2,1)}, bf16[2304,128]{1,0:T(8,128)(2,1)}, u32[]{:S(2)}, u32[]{:S(2)}) %collective-permute-start.1) | collective-permute-done | bytes 589856 | tf_op jit(solution)/shard_map/ppermute | solution.py:367
  24.2 0.1 collective-permute-done.2.refs_0_
  24.3 1.1 collective-permute-start.4
  25.5 1.0 collective-permute-start.5
  26.5 1.2 %collective-permute-start.6 = (bf16[2304,128]{1,0:T(8,128)(2,1)}, bf16[2304,128]{1,0:T(8,128)(2,1)}, u32[]{:S(2)}, u32[]{:S(2)}) collective-permute-start(bf16[2304,128]{1,0:T(8,128)(2,1)} %collective-permute-done.2.refs_0_), channel_id=1, source_target_pairs={{0,16},{1,17},{2,18},{3,19},{4,20},{5,21},{6,22},{7,23},{8,24},{9,... | collective-permute-start | bytes 1769480 | tf_op jit(solution)/shard_map/ppermute | solution.py:367
  27.7 9.8 %shard_map.84.total_ref = f32[512,1024]{1,0:T(8,128)} custom-call(bf16[512,8192]{1,0:T(8,128)(2,1)} %tokens_ref.11, bf16[8192,1024]{1,0:T(8,128)(2,1)} %weight_ref.3, f32[512,1024]{1,0:T(8,128)} %shard_map.83.refs_0_), custom_call_target="tpu_custom_call" | custom-call | flops 4294967296 | bytes 14680064 | tf_op jit(solution)/shard_map/pallas_call | solution.py:163
  37.6 1.6 %collective-permute-done.4.refs_1_ = bf16[2304,128]{1,0:T(8,128)(2,1)} collective-permute-done((bf16[2304,128]{1,0:T(8,128)(2,1)}, bf16[2304,128]{1,0:T(8,128)(2,1)}, u32[]{:S(2)}, u32[]{:S(2)}) %collective-permute-start.4) | collective-permute-done | bytes 589856 | tf_op jit(solution)/shard_map/ppermute | solution.py:367
  39.2 0.0 collective-permute-done.5.refs_2_
  39.2 0.3 collective-permute-done.6.refs_3_
  39.5 0.0 collective-permute-done.7.other_ref
  39.5 1.2 %collective-permute-start.10 = (bf16[2304,128]{1,0:T(8,128)(2,1)}, bf16[2304,128]{1,0:T(8,128)(2,1)}, u32[]{:S(2)}, u32[]{:S(2)}) collective-permute-start(bf16[2304,128]{1,0:T(8,128)(2,1)} %collective-permute-done.4.refs_1_), channel_id=1, source_target_pairs={{0,16},{1,17},{2,18},{3,19},{4,20},{5,21},{6,22},{7,23},{8,24},{9,... | collective-permute-start | bytes 1769480 | tf_op jit(solution)/shard_map/ppermute | solution.py:367
  40.8 1.8 %collective-permute-start.8 = (bf16[2304,128]{1,0:T(8,128)(2,1)}, bf16[2304,128]{1,0:T(8,128)(2,1)}, u32[]{:S(2)}, u32[]{:S(2)}) collective-permute-start(bf16[2304,128]{1,0:T(8,128)(2,1)} %get-tuple-element.64.refs_0_), channel_id=1, source_target_pairs={{0,8},{1,9},{2,10},{3,11},{4,0},{5,1},{6,2},{7,3},{8,12},{9,13},{1... | collective-permute-start | bytes 1769480 | tf_op jit(solution)/shard_map/ppermute | solution.py:367
  42.6 1.2 %collective-permute-start.9 = (bf16[2304,128]{1,0:T(8,128)(2,1)}, bf16[2304,128]{1,0:T(8,128)(2,1)}, u32[]{:S(2)}, u32[]{:S(2)}) collective-permute-start(bf16[2304,128]{1,0:T(8,128)(2,1)} %collective-permute-done.4.refs_1_), channel_id=1, source_target_pairs={{0,2},{1,3},{2,0},{3,1},{4,6},{5,7},{6,4},{7,5},{8,10},{9,11},{10,... | collective-permute-start | bytes 1769480 | tf_op jit(solution)/shard_map/ppermute | solution.py:367
  43.8 1.0 copy.20.row_slot_ref
  44.8 0.6 slice_bitcast_fusion
  45.4 9.4 %shard_map.85 = (f32[512,128]{1,0:T(8,128)}, f32[512,128]{1,0:T(8,128)}, bf16[128,1024]{1,0:T(8,128)(2,1)}) custom-call(s32[34]{0:T(128)} %dynamic-slice_bitcast_fusion.1.info_ref, s32[1024,1]{1,0:T(8,128)} %copy.20.row_slot_ref, s32[1,512]{1,0:T(1,128)} %get-tuple-element.103.column_slot_ref, bf16[512,8192]{1,0:T(8,128)(2,1)} %tokens_ref.11, ...), custom_call_target="tpu_custom_call" | custom-call | flops 2147483648 | bytes 10747904 | tf_op jit(solution)/shard_map/pallas_call | solution.py:271
  54.8 0.0 collective-permute-done.10.refs_2_
  54.8 0.0 collective-permute-done.8.refs_3_
  54.9 0.0 collective-permute-done.9.refs_0_
  54.9 0.4 collective-permute-start.11
  55.2 1.1 collective-permute-start.12
  56.4 0.1 collective-permute-start.13
  56.5 0.0 copy-start
  56.5 9.3 %shard_map.86 = (f32[512,128]{1,0:T(8,128)}, f32[512,128]{1,0:T(8,128)}, bf16[128,1024]{1,0:T(8,128)(2,1)}) custom-call(s32[34]{0:T(128)} %dynamic-slice_bitcast_fusion.1.info_ref, s32[1024,1]{1,0:T(8,128)} %copy.20.row_slot_ref, s32[1,512]{1,0:T(1,128)} %get-tuple-element.102.column_slot_ref, bf16[512,8192]{1,0:T(8,128)(2,1)} %tokens_ref.11, ...), custom_call_target="tpu_custom_call" | custom-call | flops 2147483648 | bytes 6553600 | tf_op jit(solution)/shard_map/pallas_call | solution.py:271
  65.8 1.9 %collective-permute-done.11.refs_3_ = bf16[2304,128]{1,0:T(8,128)(2,1)} collective-permute-done((bf16[2304,128]{1,0:T(8,128)(2,1)}, bf16[2304,128]{1,0:T(8,128)(2,1)}, u32[]{:S(2)}, u32[]{:S(2)}) %collective-permute-start.11) | collective-permute-done | bytes 589856 | tf_op jit(solution)/shard_map/ppermute | solution.py:367
  67.7 0.0 collective-permute-done.12.refs_1_
  67.7 0.0 collective-permute-done.13.refs_0_
  67.7 1.0 collective-permute-start.14
  68.7 0.8 collective-permute-start.15
  69.5 0.2 collective-permute-start.16
  69.8 0.0 copy-done
  69.8 18.1 %collective-permute-start.18 = (bf16[128,1024]{1,0:T(8,128)(2,1)S(1)}, bf16[128,1024]{1,0:T(8,128)(2,1)}, u32[]{:S(2)}, u32[]{:S(2)}) collective-permute-start(bf16[128,1024]{1,0:T(8,128)(2,1)S(1)} %copy-done), channel_id=1, source_target_pairs={{0,1},{1,0},{2,3},{3,2},{4,5},{5,4},{6,7},{7,6},{8,9},{9,8},{10,11... | collective-permute-start | bytes 786440 | tf_op jit(solution)/shard_map/ppermute | solution.py:367
  87.9 0.0 collective-permute-start.19
  87.9 9.6 %shard_map.87 = (f32[512,128]{1,0:T(8,128)}, f32[512,128]{1,0:T(8,128)}, bf16[128,1024]{1,0:T(8,128)(2,1)}) custom-call(s32[34]{0:T(128)} %dynamic-slice_bitcast_fusion.1.info_ref, s32[1024,1]{1,0:T(8,128)} %copy.20.row_slot_ref, s32[1,512]{1,0:T(1,128)} %get-tuple-element.101.column_slot_ref, bf16[512,8192]{1,0:T(8,128)(2,1)} %tokens_ref.11, ...), custom_call_target="tpu_custom_call" | custom-call | flops 2147483648 | bytes 10747904 | tf_op jit(solution)/shard_map/pallas_call | solution.py:271
  97.5 0.0 collective-permute-done.14.refs_1_
  97.5 0.6 collective-permute-start.20
  98.1 0.0 collective-permute-done.15.refs_2_
  98.1 0.0 collective-permute-done.16.refs_3_
  98.1 9.3 %shard_map.88 = (f32[512,128]{1,0:T(8,128)}, f32[512,128]{1,0:T(8,128)}, bf16[128,1024]{1,0:T(8,128)(2,1)}) custom-call(s32[34]{0:T(128)} %dynamic-slice_bitcast_fusion.1.info_ref, s32[1024,1]{1,0:T(8,128)} %copy.20.row_slot_ref, s32[1,512]{1,0:T(1,128)} %get-tuple-element.104.column_slot_ref, bf16[512,8192]{1,0:T(8,128)(2,1)} %tokens_ref.11, ...), custom_call_target="tpu_custom_call" | custom-call | flops 2147483648 | bytes 6553600 | tf_op jit(solution)/shard_map/pallas_call | solution.py:271
  107.3 0.1 collective-permute-start.17
  107.4 0.5 collective-permute-start.21
  107.9 0.8 copy.21.row_slot_ref
  108.8 0.0 collective-permute-done.18.refs_1_
  108.8 0.0 collective-permute-done.19.refs_3_
  108.8 0.0 collective-permute-done.20.refs_5_
  108.8 0.5 collective-permute-done.17.theirs_ref
  109.3 0.4 collective-permute-done.21.refs_7_
  109.6 6.8 %shard_map.89 = bf16[512,1024]{1,0:T(8,128)(2,1)} custom-call(s32[34]{0:T(128)} %dynamic-slice_bitcast_fusion.1.info_ref, s32[512,1]{1,0:T(8,128)} %copy.21.row_slot_ref, f32[512,128]{1,0:T(8,128)} %get-tuple-element.94.mine_ref, f32[512,128]{1,0:T(8,128)} %collective-permute-done.17.theirs_ref, f32[512,1024]{1,0:T(8,128)} %shard_map.84.total_ref, ...), custom_call_target="tpu_custom_call" | custom-call | flops 2147483648 | bytes 5242880 | tf_op jit(solution)/shard_map/pallas_call | solution.py:328
  (1 shorter events, 0.0 us)
Async XLA Ops:
  0.0 3.3 %collective-permute-start = (bf16[4,16,8192]{2,1,0:T(8,128)(2,1)}, bf16[4,16,8192]{2,1,0:T(8,128)(2,1)}, u32[]{:S(2)}, u32[]{:S(2)}) collective-permute-start(bf16[4,16,8192]{2,1,0:T(8,128)(2,1)} %here_ref.1), channel_id=1, source_target_pairs={{0,1},{1,0},{2,3},{3,2},{4,5},{5,4},{6,7},{7,6},{8,9},{9,8},{10,11... | collective-permute-start | bytes 3145736 | tf_op jit(solution)/shard_map/ppermute | solution.py:367
  3.3 36.2 %collective-permute-start.7 = (bf16[512,8192]{1,0:T(8,128)(2,1)}, bf16[512,8192]{1,0:T(8,128)(2,1)}, u32[]{:S(2)}, u32[]{:S(2)}) collective-permute-start(bf16[512,8192]{1,0:T(8,128)(2,1)} %tokens_ref.11), channel_id=1, source_target_pairs={{0,1},{1,0},{2,3},{3,2},{4,5},{5,4},{6,7},{7,6},{8,9},{9,8},{10,11... | collective-permute-start | bytes 25165832 | tf_op jit(solution)/shard_map/ppermute | solution.py:367
  4.5 16.6 %collective-permute-start.3 = (s32[512]{0:T(512)S(1)}, s32[512]{0:T(512)S(1)}, u32[]{:S(2)}, u32[]{:S(2)}) collective-permute-start(s32[512]{0:T(512)S(1)} %select_reduce_fusion), channel_id=1, source_target_pairs={{0,1},{1,0},{2,3},{3,2},{4,5},{5,4},{6,7},{7,6},{8,9},{9,8},{10,11... | collective-permute-start | bytes 6152 | tf_op jit(solution)/shard_map/ppermute | solution.py:367
  9.3 14.9 %collective-permute-start.1 = (bf16[2304,128]{1,0:T(8,128)(2,1)}, bf16[2304,128]{1,0:T(8,128)(2,1)}, u32[]{:S(2)}, u32[]{:S(2)}) collective-permute-start(bf16[2304,128]{1,0:T(8,128)(2,1)} %get-tuple-element.64.refs_0_), channel_id=1, source_target_pairs={{0,4},{1,5},{2,6},{3,7},{4,12},{5,13},{6,14},{7,15},{8,0},{9,1},{1... | collective-permute-start | bytes 1769480 | tf_op jit(solution)/shard_map/ppermute | solution.py:367
  9.4 14.9 %collective-permute-start.2 = (bf16[2304,128]{1,0:T(8,128)(2,1)}, bf16[2304,128]{1,0:T(8,128)(2,1)}, u32[]{:S(2)}, u32[]{:S(2)}) collective-permute-start(bf16[2304,128]{1,0:T(8,128)(2,1)} %get-tuple-element.64.refs_0_), channel_id=1, source_target_pairs={{0,2},{1,3},{2,0},{3,1},{4,6},{5,7},{6,4},{7,5},{8,10},{9,11},{10,... | collective-permute-start | bytes 1769480 | tf_op jit(solution)/shard_map/ppermute | solution.py:367
  24.3 14.9 %collective-permute-start.4 = (bf16[2304,128]{1,0:T(8,128)(2,1)}, bf16[2304,128]{1,0:T(8,128)(2,1)}, u32[]{:S(2)}, u32[]{:S(2)}) collective-permute-start(bf16[2304,128]{1,0:T(8,128)(2,1)} %collective-permute-done.1.refs_1_), channel_id=1, source_target_pairs={{0,4},{1,5},{2,6},{3,7},{4,12},{5,13},{6,14},{7,15},{8,0},{9,1},{1... | collective-permute-start | bytes 1769480 | tf_op jit(solution)/shard_map/ppermute | solution.py:367
  25.5 13.7 %collective-permute-start.5 = (bf16[2304,128]{1,0:T(8,128)(2,1)}, bf16[2304,128]{1,0:T(8,128)(2,1)}, u32[]{:S(2)}, u32[]{:S(2)}) collective-permute-start(bf16[2304,128]{1,0:T(8,128)(2,1)} %collective-permute-done.1.refs_1_), channel_id=1, source_target_pairs={{0,2},{1,3},{2,0},{3,1},{4,6},{5,7},{6,4},{7,5},{8,10},{9,11},{10,... | collective-permute-start | bytes 1769480 | tf_op jit(solution)/shard_map/ppermute | solution.py:367
  26.5 13.1 %collective-permute-start.6 = (bf16[2304,128]{1,0:T(8,128)(2,1)}, bf16[2304,128]{1,0:T(8,128)(2,1)}, u32[]{:S(2)}, u32[]{:S(2)}) collective-permute-start(bf16[2304,128]{1,0:T(8,128)(2,1)} %collective-permute-done.2.refs_0_), channel_id=1, source_target_pairs={{0,16},{1,17},{2,18},{3,19},{4,20},{5,21},{6,22},{7,23},{8,24},{9,... | collective-permute-start | bytes 1769480 | tf_op jit(solution)/shard_map/ppermute | solution.py:367
  39.5 15.3 %collective-permute-start.10 = (bf16[2304,128]{1,0:T(8,128)(2,1)}, bf16[2304,128]{1,0:T(8,128)(2,1)}, u32[]{:S(2)}, u32[]{:S(2)}) collective-permute-start(bf16[2304,128]{1,0:T(8,128)(2,1)} %collective-permute-done.4.refs_1_), channel_id=1, source_target_pairs={{0,16},{1,17},{2,18},{3,19},{4,20},{5,21},{6,22},{7,23},{8,24},{9,... | collective-permute-start | bytes 1769480 | tf_op jit(solution)/shard_map/ppermute | solution.py:367
  40.8 14.1 %collective-permute-start.8 = (bf16[2304,128]{1,0:T(8,128)(2,1)}, bf16[2304,128]{1,0:T(8,128)(2,1)}, u32[]{:S(2)}, u32[]{:S(2)}) collective-permute-start(bf16[2304,128]{1,0:T(8,128)(2,1)} %get-tuple-element.64.refs_0_), channel_id=1, source_target_pairs={{0,8},{1,9},{2,10},{3,11},{4,0},{5,1},{6,2},{7,3},{8,12},{9,13},{1... | collective-permute-start | bytes 1769480 | tf_op jit(solution)/shard_map/ppermute | solution.py:367
  42.6 12.3 %collective-permute-start.9 = (bf16[2304,128]{1,0:T(8,128)(2,1)}, bf16[2304,128]{1,0:T(8,128)(2,1)}, u32[]{:S(2)}, u32[]{:S(2)}) collective-permute-start(bf16[2304,128]{1,0:T(8,128)(2,1)} %collective-permute-done.4.refs_1_), channel_id=1, source_target_pairs={{0,2},{1,3},{2,0},{3,1},{4,6},{5,7},{6,4},{7,5},{8,10},{9,11},{10,... | collective-permute-start | bytes 1769480 | tf_op jit(solution)/shard_map/ppermute | solution.py:367
  54.9 12.8 %collective-permute-start.11 = (bf16[2304,128]{1,0:T(8,128)(2,1)}, bf16[2304,128]{1,0:T(8,128)(2,1)}, u32[]{:S(2)}, u32[]{:S(2)}) collective-permute-start(bf16[2304,128]{1,0:T(8,128)(2,1)} %get-tuple-element.80.refs_2_), channel_id=1, source_target_pairs={{0,4},{1,5},{2,6},{3,7},{4,12},{5,13},{6,14},{7,15},{8,0},{9,1},{1... | collective-permute-start | bytes 1769480 | tf_op jit(solution)/shard_map/ppermute | solution.py:367
  55.2 12.5 %collective-permute-start.12 = (bf16[2304,128]{1,0:T(8,128)(2,1)}, bf16[2304,128]{1,0:T(8,128)(2,1)}, u32[]{:S(2)}, u32[]{:S(2)}) collective-permute-start(bf16[2304,128]{1,0:T(8,128)(2,1)} %collective-permute-done.8.refs_3_), channel_id=1, source_target_pairs={{0,2},{1,3},{2,0},{3,1},{4,6},{5,7},{6,4},{7,5},{8,10},{9,11},{10,... | collective-permute-start | bytes 1769480 | tf_op jit(solution)/shard_map/ppermute | solution.py:367
  56.4 11.3 %collective-permute-start.13 = (bf16[2304,128]{1,0:T(8,128)(2,1)}, bf16[2304,128]{1,0:T(8,128)(2,1)}, u32[]{:S(2)}, u32[]{:S(2)}) collective-permute-start(bf16[2304,128]{1,0:T(8,128)(2,1)} %collective-permute-done.5.refs_2_), channel_id=1, source_target_pairs={{0,16},{1,17},{2,18},{3,19},{4,20},{5,21},{6,22},{7,23},{8,24},{9,... | collective-permute-start | bytes 1769480 | tf_op jit(solution)/shard_map/ppermute | solution.py:367
  56.5 13.3 %copy-start = (bf16[128,1024]{1,0:T(8,128)(2,1)S(1)}, bf16[128,1024]{1,0:T(8,128)(2,1)}, u32[]{:S(2)}) copy-start(bf16[128,1024]{1,0:T(8,128)(2,1)} %get-tuple-element.97.refs_0_) | copy-start | bytes 786436
  67.7 29.8 %collective-permute-start.14 = (bf16[2304,128]{1,0:T(8,128)(2,1)}, bf16[2304,128]{1,0:T(8,128)(2,1)}, u32[]{:S(2)}, u32[]{:S(2)}) collective-permute-start(bf16[2304,128]{1,0:T(8,128)(2,1)} %get-tuple-element.80.refs_2_), channel_id=1, source_target_pairs={{0,8},{1,9},{2,10},{3,11},{4,0},{5,1},{6,2},{7,3},{8,12},{9,13},{1... | collective-permute-start | bytes 1769480 | tf_op jit(solution)/shard_map/ppermute | solution.py:367
  68.7 29.4 %collective-permute-start.15 = (bf16[2304,128]{1,0:T(8,128)(2,1)}, bf16[2304,128]{1,0:T(8,128)(2,1)}, u32[]{:S(2)}, u32[]{:S(2)}) collective-permute-start(bf16[2304,128]{1,0:T(8,128)(2,1)} %collective-permute-done.10.refs_2_), channel_id=1, source_target_pairs={{0,2},{1,3},{2,0},{3,1},{4,6},{5,7},{6,4},{7,5},{8,10},{9,11},{10,... | collective-permute-start | bytes 1769480 | tf_op jit(solution)/shard_map/ppermute | solution.py:367
  69.5 28.5 %collective-permute-start.16 = (bf16[2304,128]{1,0:T(8,128)(2,1)}, bf16[2304,128]{1,0:T(8,128)(2,1)}, u32[]{:S(2)}, u32[]{:S(2)}) collective-permute-start(bf16[2304,128]{1,0:T(8,128)(2,1)} %collective-permute-done.12.refs_1_), channel_id=1, source_target_pairs={{0,16},{1,17},{2,18},{3,19},{4,20},{5,21},{6,22},{7,23},{8,24},{9,... | collective-permute-start | bytes 1769480 | tf_op jit(solution)/shard_map/ppermute | solution.py:367
  69.8 39.0 %collective-permute-start.18 = (bf16[128,1024]{1,0:T(8,128)(2,1)S(1)}, bf16[128,1024]{1,0:T(8,128)(2,1)}, u32[]{:S(2)}, u32[]{:S(2)}) collective-permute-start(bf16[128,1024]{1,0:T(8,128)(2,1)S(1)} %copy-done), channel_id=1, source_target_pairs={{0,1},{1,0},{2,3},{3,2},{4,5},{5,4},{6,7},{7,6},{8,9},{9,8},{10,11... | collective-permute-start | bytes 786440 | tf_op jit(solution)/shard_map/ppermute | solution.py:367
  87.9 20.9 %collective-permute-start.19 = (bf16[128,1024]{1,0:T(8,128)(2,1)}, bf16[128,1024]{1,0:T(8,128)(2,1)}, u32[]{:S(2)}, u32[]{:S(2)}) collective-permute-start(bf16[128,1024]{1,0:T(8,128)(2,1)} %get-tuple-element.98.refs_2_), channel_id=1, source_target_pairs={{0,1},{1,0},{2,3},{3,2},{4,5},{5,4},{6,7},{7,6},{8,9},{9,8},{10,11... | collective-permute-start | bytes 786440 | tf_op jit(solution)/shard_map/ppermute | solution.py:367
  97.5 11.3 %collective-permute-start.20 = (bf16[128,1024]{1,0:T(8,128)(2,1)}, bf16[128,1024]{1,0:T(8,128)(2,1)}, u32[]{:S(2)}, u32[]{:S(2)}) collective-permute-start(bf16[128,1024]{1,0:T(8,128)(2,1)} %get-tuple-element.99.refs_4_), channel_id=1, source_target_pairs={{0,1},{1,0},{2,3},{3,2},{4,5},{5,4},{6,7},{7,6},{8,9},{9,8},{10,11... | collective-permute-start | bytes 786440 | tf_op jit(solution)/shard_map/ppermute | solution.py:367
  107.3 1.9 %collective-permute-start.17 = (f32[512,128]{1,0:T(8,128)}, f32[512,128]{1,0:T(8,128)}, u32[]{:S(2)}, u32[]{:S(2)}) collective-permute-start(f32[512,128]{1,0:T(8,128)} %get-tuple-element.95), channel_id=1, source_target_pairs={{0,1},{1,0},{2,3},{3,2},{4,5},{5,4},{6,7},{7,6},{8,9},{9,8},{10,11... | collective-permute-start | bytes 786440 | tf_op jit(solution)/shard_map/ppermute | solution.py:367
  107.4 2.2 %collective-permute-start.21 = (bf16[128,1024]{1,0:T(8,128)(2,1)}, bf16[128,1024]{1,0:T(8,128)(2,1)}, u32[]{:S(2)}, u32[]{:S(2)}) collective-permute-start(bf16[128,1024]{1,0:T(8,128)(2,1)} %get-tuple-element.100.refs_6_), channel_id=1, source_target_pairs={{0,1},{1,0},{2,3},{3,2},{4,5},{5,4},{6,7},{7,6},{8,9},{9,8},{10,11... | collective-permute-start | bytes 786440 | tf_op jit(solution)/shard_map/ppermute | solution.py:367

commit v7 on v6

--- a/solution.py
+++ b/solution.py
@@ -15,11 +15,12 @@
 RANK = 16
 
 PIECES = (
-    *((0, 0, 0), (1, 0, 0), (0, 0, 1), (0, 1, 1)),
-    *((0, 1, 0), (2, 0, 0), (1, 1, 0), (3, 0, 0)),
-    *((2, 1, 0), (3, 1, 0), (2, 0, 1), (1, 0, 1)),
+    *((0, 0, 0), (1, 0, 0), (0, 1, 0), (2, 0, 0)),
+    *((1, 1, 0), (3, 0, 0), (2, 1, 0), (3, 1, 0)),
+    *((0, 0, 1), (0, 1, 1), (2, 0, 1), (1, 0, 1)),
     *((1, 1, 1), (3, 0, 1), (2, 1, 1), (3, 1, 1)),
 )
+TOGETHER = 4
 VMEM_BYTES = 64 * 1024 * 1024 - 512 * 1024
 
 
@@ -82,13 +83,12 @@
         copy.wait()
 
 
-def assemble_kernel(
-    info_ref, here_ref, there_ref, up_ref, front_ref, back_ref, down_ref, sems
-):
+def assemble_kernel(back, info_ref, here_ref, there_ref, up_ref, out_ref, down_ref, sems):
     y, core = info_ref[0], info_ref[1]
-    held, rank, half = down_ref.shape
+    place = 1 - y if back else y
+    held, rank, quarter = down_ref.shape
     held //= 2
-    columns = pl.ds(pl.multiple_of(core * half, half), half)
+    columns = pl.ds(pl.multiple_of((2 * core + place) * quarter, quarter), quarter)
     copies = [
         pltpu.make_async_copy(
             source.at[:, :, columns], down_ref.at[pl.ds(of_core * held, held)], sems.at[n]
@@ -96,34 +96,30 @@
         for n, (source, of_core) in enumerate(((here_ref, core), (there_ref, 1 - core)))
     ]
     started(copies)
+    up = up_ref[pl.ds(place * (held // 2), held // 2)].reshape(held // 2 * rank, -1)
+    rows = up.shape[0]
+    for n in range(up.shape[1] // LANES):
+        first = quarter + n * rows
+        out_ref[first : first + rows] = up[:, n * LANES : (n + 1) * LANES]
     awaited(copies)
-    quarter = half // 2
-    for out_ref, place in ((front_ref, y), (back_ref, 1 - y)):
-        for n in range(0, quarter, LANES):
-            columns = pl.ds(pl.multiple_of(place * quarter + n, LANES), LANES)
-            block = down_ref[:, :, columns].reshape(2 * held * rank, LANES)
-            out_ref[n : n + LANES] = block.T
-        up = up_ref[pl.ds(place * (held // 2), held // 2)].reshape(held // 2 * rank, -1)
-        rows = up.shape[0]
-        for n in range(up.shape[1] // LANES):
-            first = quarter + n * rows
-            out_ref[first : first + rows] = up[:, n * LANES : (n + 1) * LANES]
-
-
-def assemble(info, here, there, up):
+    for n in range(0, quarter, LANES):
+        block = down_ref[:, :, n : n + LANES].reshape(2 * held * rank, LANES)
+        out_ref[n : n + LANES] = block.T
+
+
+def assemble(back, info, here, there, up):
     held, rank, depth = here.shape
     width = up.shape[2]
     rows = depth // 4 + held // 2 * rank * width // LANES
-    piece = jax.ShapeDtypeStruct((rows, LANES), here.dtype)
     anywhere = pl.BlockSpec(memory_space=pl.ANY)
     vmem = pl.BlockSpec(memory_space=pltpu.VMEM)
     return pl.pallas_call(
-        assemble_kernel,
-        out_shape=(piece, piece),
+        functools.partial(assemble_kernel, back),
+        out_shape=jax.ShapeDtypeStruct((rows, LANES), here.dtype),
         in_specs=[pl.BlockSpec(memory_space=pltpu.SMEM), anywhere, anywhere, vmem],
-        out_specs=(vmem, vmem),
+        out_specs=vmem,
         scratch_shapes=[
-            pltpu.VMEM((2 * held, rank, depth // 2), here.dtype),
+            pltpu.VMEM((2 * held, rank, depth // 4), here.dtype),
             pltpu.SemaphoreType.DMA((2,)),
         ],
         compiler_params=params(),
@@ -185,7 +181,7 @@
 def absorb_kernel(
     backs, more, info_ref, row_slot_ref, column_slot_ref, tokens_ref, other_ref, *refs
 ):
-    count = 2 * len(backs)
+    count = TOGETHER * len(backs)
     sources, refs = refs[:count], refs[count:]
     before, refs = refs[: 2 * more], refs[2 * more :]
     outs, up_ref, (rows_ref, down_ref, sems) = refs[:2], refs[2], refs[3:]
@@ -205,8 +201,8 @@
     for n, back in enumerate(backs):
         downs.append(
             [
-                begin(sources[2 * n + i], down_ref.at[n, :, pl.ds(i * LANES, LANES)])
-                for i in range(2)
+                begin(sources[TOGETHER * n + i], down_ref.at[n, :, pl.ds(i * LANES, LANES)])
+                for i in range(TOGETHER)
             ]
         )
         if back in tiles:
@@ -238,27 +234,26 @@
                 preferred_element_type=jnp.float32,
             )
             shrink = part if shrink is None else shrink + part
-        for i in range(2):
-            lanes = slice(i * LANES, (i + 1) * LANES)
-            wanted = column_slot_ref[:, 2 * n * LANES + i * LANES : 2 * n * LANES + (i + 1) * LANES]
+        height = up_ref.shape[0] // count
+        for i in range(TOGETHER):
+            lanes, which = slice(i * LANES, (i + 1) * LANES), TOGETHER * n + i
+            wanted = column_slot_ref[:, which * LANES : (which + 1) * LANES]
             kept = jnp.where(row_slot_ref[...] == wanted, shrink[:, lanes], 0.0)
             state = kept if state is None else state + kept
-            height = up_ref.shape[0] // count
             for j in range(up_ref.shape[1] // LANES):
                 first = quarter + j * height
                 up_ref[
-                    (2 * n + i) * height : (2 * n + i + 1) * height,
-                    j * LANES : (j + 1) * LANES,
+                    which * height : (which + 1) * height, j * LANES : (j + 1) * LANES
                 ] = down_ref[n, first : first + height, lanes]
     for i, out_ref in enumerate(outs):
         own = state[i * rows : (i + 1) * rows]
         out_ref[...] = own + before[i][...] if more else own
 
 
-def absorb(info, row_slots, column_slot, tokens, other, width, pairs, before=None):
+def absorb(info, row_slots, column_slot, tokens, other, width, fours, before=None):
     rows, depth = tokens.shape
-    pieces = [piece for pair, _ in pairs for piece in pair]
-    backs = [back for _, back in pairs]
+    pieces = [piece for four, _ in fours for piece in four]
+    backs = [back for _, back in fours]
     quarter = depth // 4
     height = pieces[0].shape[0]
     anywhere = pl.BlockSpec(memory_space=pl.ANY)
@@ -277,7 +272,7 @@
         out_specs=(vmem, vmem, vmem),
         scratch_shapes=[
             pltpu.VMEM((quarters, 2 * rows, quarter), tokens.dtype),
-            pltpu.VMEM((len(pairs), height, 2 * LANES), tokens.dtype),
+            pltpu.VMEM((len(fours), height, TOGETHER * LANES), tokens.dtype),
             pltpu.SemaphoreType.DMA((copies,)),
         ],
         cost_estimate=pl.CostEstimate(
@@ -295,17 +290,15 @@
     sources, (out_ref, total, up, sems) = refs[:count], refs[count:]
     rows = out_ref.shape[0]
     height = up.shape[0] // (len(PIECES) * 2)
-    per = sources[0].shape[0] // height
     copies = [pltpu.make_async_copy(total_ref, total, sems.at[0])]
-    for n in range(count * per):
-        first = pl.multiple_of(info_ref[2 + n], height)
-        copies.append(
-            pltpu.make_async_copy(
-                sources[n // per].at[pl.ds(n % per * height, height)],
-                up.at[pl.ds(first, height)],
-                sems.at[1 + n],
+    for source in sources:
+        for n in range(0, source.shape[0], height):
+            first = pl.multiple_of(info_ref[1 + len(copies)], height)
+            copies.append(
+                pltpu.make_async_copy(
+                    source.at[pl.ds(n, height)], up.at[pl.ds(first, height)], sems.at[len(copies)]
+                )
             )
-        )
     started(copies)
     shrink = mine_ref[...] + theirs_ref[...]
     lane_slot = lax.broadcasted_iota(jnp.int32, (rows, LANES), 1) // RANK
@@ -315,9 +308,9 @@
         high.append(kept.astype(jnp.bfloat16))
         low.append((kept - high[-1].astype(jnp.float32)).astype(jnp.bfloat16))
     awaited(copies)
-    lora = jnp.dot(jnp.concatenate(low, axis=1), up[...], preferred_element_type=jnp.float32)
-    lora += jnp.dot(jnp.concatenate(high, axis=1), up[...], preferred_element_type=jnp.float32)
-    out_ref[...] = (total[...] + lora).astype(out_ref.dtype)
+    both = jnp.concatenate([jnp.concatenate(part, axis=1) for part in (low, high)], axis=0)
+    lora = jnp.dot(both, up[...], preferred_element_type=jnp.float32)
+    out_ref[...] = (total[...] + (lora[:rows] + lora[rows:])).astype(out_ref.dtype)
 
 
 def finish(info, row_slot, mine, theirs, total, ups):
@@ -379,77 +372,73 @@
         return (along_z(r, -piece[0]) ^ (2 * piece[1])) // 2
 
     per_chip = LANES // rank
+    kernels = (PIECES[:4], PIECES[4:12], PIECES[12:])
     column_table, info_table = [], []
     for g in range(planes):
         for r in range(owners):
             column_table.append(
-                [
-                    [
-                        np.repeat(
-                            [chip(r, p) * per_chip + n for p in PIECES[k : k + 4] for n in range(per_chip)],
-                            rank,
-                        )
-                    ]
-                    for k in range(0, len(PIECES), 4)
+                [chip(r, p) * per_chip + n // rank for p in PIECES for n in range(LANES)]
+            )
+            info_table.append(
+                [g, r % 2]
+                + [
+                    chip(r, p) * LANES + core * held * rank + (g ^ p[2]) * (held // 2 * rank)
+                    for pieces in kernels
+                    for core in (r % 2, 1 - r % 2)
+                    for p in pieces
                 ]
             )
-            info = [g, r % 2]
-            for k in range(0, len(PIECES), 4):
-                for core in (r % 2, 1 - r % 2):
-                    for p in PIECES[k : k + 4]:
-                        info.append(
-                            chip(r, p) * LANES
-                            + core * held * rank
-                            + (g ^ p[2]) * (held // 2 * rank)
-                        )
-            info_table.append(info)
     here_of = lambda table: lax.dynamic_index_in_dim(
         jnp.array(np.array(table, np.int32)), device, 0, keepdims=False
     )
-    info, column_slots = here_of(info_table), here_of(column_table)
+    info, column_slots = here_of(info_table), here_of(column_table)[None, :]
 
     def together(*values):
         return lax.optimization_barrier(values)
 
     there = core_swap(adapter_down_weight)
     row_slot = slots_of_rows(row_adapter_index, adapter_storage_slot)
-    there, tokens_late = together(there, tokens)
+    there, tokens_late, info, row_slot, column_slots = together(
+        there, tokens, info, row_slot, column_slots
+    )
+    piece = lambda back: assemble(back, info, adapter_down_weight, there, adapter_up_weight)
+    front = piece(0)
+
+    z1, x0 = z_ring(front), x_swap(front)
     other = core_swap(tokens_late)
     other_slot = core_swap(row_slot[:, 0])
-    front, back = assemble(info, adapter_down_weight, there, adapter_up_weight)
-
-    z1, x0 = z_ring(front), x_swap(front)
-    total = base_part(tokens, base_value_weight, 0, depth // 2)
+    back = piece(1)
+    third = 3 * DEPTH_TILE
+    total = base_part(tokens, base_value_weight, 0, third)
     row_slots = jnp.concatenate([row_slot, other_slot[:, None]], axis=0)
-    z1, x0, front, back, total, row_slots, column_slots = together(
-        z1, x0, front, back, total, row_slots, column_slots
-    )
+    z1, x0, front, back, total, row_slots = together(z1, x0, front, back, total, row_slots)
 
     z2, x1, yx0 = z_ring(z1), x_swap(z1), y_swap(x0)
-    total = base_part(tokens, base_value_weight, depth // 2, depth, total)
+    total = base_part(tokens, base_value_weight, third, 2 * third, total)
     z2, x1, yx0, front, other, total = together(z2, x1, yx0, front, other, total)
     ups = []
 
-    def update(number, pairs, before=None):
+    def update(first, fours, before=None):
+        lanes = slice(first * LANES, (first + TOGETHER * len(fours)) * LANES)
         mine, others, up = absorb(
-            info, row_slots, column_slots[number], tokens, other, width, pairs, before
+            info, row_slots, column_slots[:, lanes], tokens, other, width, fours, before
         )
         ups.extend([up, core_swap(up)])
         return mine, others
 
     z3, x2, yz2 = z_back(front), x_swap(z2), y_swap(z2)
-    state = update(0, [((front, z1), 0), ((back, yx0), 1)])
-    z3, x2, yz2, x1, back, state = together(z3, x2, yz2, x1, back, state)
+    state = update(0, [((front, z1, x0, z2), 0)])
+    z3, x2, yz2, x1, back, state, total = together(z3, x2, yz2, x1, back, state, total)
 
     zb1, x3, yx1 = z_ring(back), x_swap(z3), y_swap(x1)
-    state = update(1, [((x0, z2), 0), ((x1, z3), 0)], state)
-    zb1, x3, yx1, yz2, back, state = together(zb1, x3, yx1, yz2, back, state)
+    total = base_part(tokens, base_value_weight, 2 * third, depth, total)
+    zb1, x3, yx1, yz2, back, state, total = together(zb1, x3, yx1, yz2, back, state, total)
 
     zb3, xyz2, yx3 = z_back(back), x_swap(yz2), y_swap(x3)
-    state = update(2, [((x2, x3), 0), ((yz2, zb1), 1)], state)
+    state = update(4, [((x1, z3, x2, x3), 0), ((back, yx0, yz2, zb1), 1)], state)
     zb3, xyz2, yx3, state = together(zb3, xyz2, yx3, state)
 
-    mine, others = update(3, [((yx1, zb3), 1), ((xyz2, yx3), 1)], state)
+    mine, others = update(12, [((yx1, zb3, xyz2, yx3), 1)], state)
     return finish(info, row_slot, mine, core_swap(others), total, ups)
 
 

time: 117 us -> 103 us (0.88)
  the two profiles are of different devices: /device:TPU:17 before, /device:TPU:0 now
where the time goes in v7:
time: 103 us; the launch traced here: 102 us
  Pallas kernels  60.2 us (58%)
  starting transfers between devices  20 us (19%)
  waiting for transfers between devices  15.7 us (15%)
  local copies, waits for them, and re-layouts  5.2 us (5%)
    pallas_call x3, Pallas kernels, absorb(): pl.pallas_call(functools.partial(absorb_kernel, backs, more), out_shape=(...  24.7 us
    pallas_call x3, Pallas kernels, base_part(): pl.pallas_call(functools.partial(base_kernel, steps), out_shape=result, g...  22.8 us
    ppermute x21, starting transfers between devices, permuted(): return lax.ppermute(array, axes, pairs)  20 us
    ppermute x21, waiting for transfers between devices, permuted(): return lax.ppermute(array, axes, pairs)  15.7 us
    pallas_call x1, Pallas kernels, finish(): pl.pallas_call(functools.partial(finish_kernel, len(ups)), out_shape=jax....  6.78 us
    pallas_call x2, Pallas kernels, assemble(): pl.pallas_call(functools.partial(assemble_kernel, back), out_shape=jax.Sh...  5.99 us
  transfers between devices with their start and end apart: 21, of which 10 were waited for; matrix products, arithmetic and copies ran while one was open for 6% of the time, Pallas kernels for 52%

profile of v7, /device:TPU:0, one launch (start us, length us, event | category | flops | bytes accessed | tf_op | source)
XLA Modules:
  0.0 102.2 jit_solution(4240170893645849328)
XLA Ops:
  0.0 0.5 collective-permute-start
  0.5 1.3 %dynamic-slice_bitcast_fusion.info_ref = s32[34]{0:T(128)} fusion(s32[32,34]{1,0:T(8,128)} %constant.26.clone, s32[]{:T(128)S(6)} %select_n.10), kind=kLoop, calls=%fused_computation.3 | loop fusion | bytes 276 | tf_op jit(solution)/shard_map/jit(dynamic_index_in_dim)/squeeze | solution.py:391
  1.7 0.8 select_reduce_fusion
  2.5 0.9 constant_dynamic-slice_fusion
  3.4 0.0 collective-permute-done.there_ref
  3.4 0.1 collective-permute-start.7
  3.5 3.0 %shard_map.82.refs_0_ = bf16[2304,128]{1,0:T(8,128)(2,1)} custom-call(s32[34]{0:T(128)} %dynamic-slice_bitcast_fusion.info_ref, bf16[4,16,8192]{2,1,0:T(8,128)(2,1)} %here_ref.3, bf16[4,16,8192]{2,1,0:T(8,128)(2,1)} %collective-permute-done.there_ref, bf16[4,16,1024]{2,1,0:T(8,128)(2,1)} %up_ref.3), custom_call_target="tpu_custom_call" | custom-call | tf_op jit(solution)/shard_map/pallas_call | solution.py:116
  6.5 3.1 %collective-permute-start.1 = (bf16[2304,128]{1,0:T(8,128)(2,1)}, bf16[2304,128]{1,0:T(8,128)(2,1)}, u32[]{:S(2)}, u32[]{:S(2)}) collective-permute-start(bf16[2304,128]{1,0:T(8,128)(2,1)} %shard_map.82.refs_0_), channel_id=1, source_target_pairs={{0,4},{1,5},{2,6},{3,7},{4,12},{5,13},{6,14},{7,15},{8,0},{9,1},{1... | collective-permute-start | bytes 1769480 | tf_op jit(solution)/shard_map/ppermute | solution.py:360
  9.6 1.5 %collective-permute-start.2 = (bf16[2304,128]{1,0:T(8,128)(2,1)}, bf16[2304,128]{1,0:T(8,128)(2,1)}, u32[]{:S(2)}, u32[]{:S(2)}) collective-permute-start(bf16[2304,128]{1,0:T(8,128)(2,1)} %shard_map.82.refs_0_), channel_id=1, source_target_pairs={{0,2},{1,3},{2,0},{3,1},{4,6},{5,7},{6,4},{7,5},{8,10},{9,11},{10,... | collective-permute-start | bytes 1769480 | tf_op jit(solution)/shard_map/ppermute | solution.py:360
  11.0 0.0 collective-permute-start.3
  11.0 8.1 %shard_map.84.refs_0_ = f32[512,1024]{1,0:T(8,128)} custom-call(bf16[512,8192]{1,0:T(8,128)(2,1)} %tokens_ref.11, bf16[8192,1024]{1,0:T(8,128)(2,1)} %weight_ref.5), custom_call_target="tpu_custom_call" | custom-call | flops 3221225472 | bytes 11534336 | tf_op jit(solution)/shard_map/pallas_call | solution.py:159
  19.1 3.0 %shard_map.83.refs_4_ = bf16[2304,128]{1,0:T(8,128)(2,1)} custom-call(s32[34]{0:T(128)} %dynamic-slice_bitcast_fusion.info_ref, bf16[4,16,8192]{2,1,0:T(8,128)(2,1)} %here_ref.3, bf16[4,16,8192]{2,1,0:T(8,128)(2,1)} %collective-permute-done.there_ref, bf16[4,16,1024]{2,1,0:T(8,128)(2,1)} %up_ref.3), custom_call_target="tpu_custom_call" | custom-call | tf_op jit(solution)/shard_map/pallas_call | solution.py:116
  22.2 0.0 collective-permute-done.3
  22.2 2.2 %collective-permute-done.1.refs_1_ = bf16[2304,128]{1,0:T(8,128)(2,1)} collective-permute-done((bf16[2304,128]{1,0:T(8,128)(2,1)}, bf16[2304,128]{1,0:T(8,128)(2,1)}, u32[]{:S(2)}, u32[]{:S(2)}) %collective-permute-start.1) | collective-permute-done | bytes 589856 | tf_op jit(solution)/shard_map/ppermute | solution.py:360
  24.4 0.4 collective-permute-done.2.refs_2_
  24.8 2.6 %collective-permute-start.4 = (bf16[2304,128]{1,0:T(8,128)(2,1)}, bf16[2304,128]{1,0:T(8,128)(2,1)}, u32[]{:S(2)}, u32[]{:S(2)}) collective-permute-start(bf16[2304,128]{1,0:T(8,128)(2,1)} %collective-permute-done.1.refs_1_), channel_id=1, source_target_pairs={{0,4},{1,5},{2,6},{3,7},{4,12},{5,13},{6,14},{7,15},{8,0},{9,1},{1... | collective-permute-start | bytes 1769480 | tf_op jit(solution)/shard_map/ppermute | solution.py:360
  27.4 1.5 %collective-permute-start.5 = (bf16[2304,128]{1,0:T(8,128)(2,1)}, bf16[2304,128]{1,0:T(8,128)(2,1)}, u32[]{:S(2)}, u32[]{:S(2)}) collective-permute-start(bf16[2304,128]{1,0:T(8,128)(2,1)} %collective-permute-done.1.refs_1_), channel_id=1, source_target_pairs={{0,2},{1,3},{2,0},{3,1},{4,6},{5,7},{6,4},{7,5},{8,10},{9,11},{10,... | collective-permute-start | bytes 1769480 | tf_op jit(solution)/shard_map/ppermute | solution.py:360
  28.9 1.5 %collective-permute-start.6 = (bf16[2304,128]{1,0:T(8,128)(2,1)}, bf16[2304,128]{1,0:T(8,128)(2,1)}, u32[]{:S(2)}, u32[]{:S(2)}) collective-permute-start(bf16[2304,128]{1,0:T(8,128)(2,1)} %collective-permute-done.2.refs_2_), channel_id=1, source_target_pairs={{0,16},{1,17},{2,18},{3,19},{4,20},{5,21},{6,22},{7,23},{8,24},{9,... | collective-permute-start | bytes 1769480 | tf_op jit(solution)/shard_map/ppermute | solution.py:360
  30.4 8.3 %shard_map.85.refs_0_ = f32[512,1024]{1,0:T(8,128)} custom-call(bf16[512,8192]{1,0:T(8,128)(2,1)} %tokens_ref.11, bf16[8192,1024]{1,0:T(8,128)(2,1)} %weight_ref.5, f32[512,1024]{1,0:T(8,128)} %shard_map.84.refs_0_), custom_call_target="tpu_custom_call" | custom-call | flops 3221225472 | bytes 11534336 | tf_op jit(solution)/shard_map/pallas_call | solution.py:159
  38.8 1.5 %collective-permute-done.4.refs_3_ = bf16[2304,128]{1,0:T(8,128)(2,1)} collective-permute-done((bf16[2304,128]{1,0:T(8,128)(2,1)}, bf16[2304,128]{1,0:T(8,128)(2,1)}, u32[]{:S(2)}, u32[]{:S(2)}) %collective-permute-start.4) | collective-permute-done | bytes 589856 | tf_op jit(solution)/shard_map/ppermute | solution.py:360
  40.3 1.2 %collective-permute-done.5.refs_0_ = bf16[2304,128]{1,0:T(8,128)(2,1)} collective-permute-done((bf16[2304,128]{1,0:T(8,128)(2,1)}, bf16[2304,128]{1,0:T(8,128)(2,1)}, u32[]{:S(2)}, u32[]{:S(2)}) %collective-permute-start.5) | collective-permute-done | bytes 589856 | tf_op jit(solution)/shard_map/ppermute | solution.py:360
  41.6 1.2 %collective-permute-done.6.refs_5_ = bf16[2304,128]{1,0:T(8,128)(2,1)} collective-permute-done((bf16[2304,128]{1,0:T(8,128)(2,1)}, bf16[2304,128]{1,0:T(8,128)(2,1)}, u32[]{:S(2)}, u32[]{:S(2)}) %collective-permute-start.6) | collective-permute-done | bytes 589856 | tf_op jit(solution)/shard_map/ppermute | solution.py:360
  42.8 0.0 collective-permute-done.7.other_ref
  42.8 1.5 %collective-permute-start.10 = (bf16[2304,128]{1,0:T(8,128)(2,1)}, bf16[2304,128]{1,0:T(8,128)(2,1)}, u32[]{:S(2)}, u32[]{:S(2)}) collective-permute-start(bf16[2304,128]{1,0:T(8,128)(2,1)} %collective-permute-done.4.refs_3_), channel_id=1, source_target_pairs={{0,16},{1,17},{2,18},{3,19},{4,20},{5,21},{6,22},{7,23},{8,24},{9,... | collective-permute-start | bytes 1769480 | tf_op jit(solution)/shard_map/ppermute | solution.py:360
  44.3 0.3 collective-permute-start.8
  44.6 0.5 collective-permute-start.9
  45.2 0.6 fusion
  45.8 1.0 %copy.18.row_slot_ref = s32[1024,1]{1,0:T(8,128)} copy(s32[1024,1]{0,1:T(1,128)S(1)} %pad_add_fusion) | data formatting | bytes 8192 | tf_op jit(solution)/shard_map/optimization_barrier | solution.py:397
  46.8 7.1 %shard_map.86 = (f32[512,128]{1,0:T(8,128)}, f32[512,128]{1,0:T(8,128)}, bf16[128,1024]{1,0:T(8,128)(2,1)}) custom-call(s32[34]{0:T(128)} %dynamic-slice_bitcast_fusion.info_ref, s32[1024,1]{1,0:T(8,128)} %copy.18.row_slot_ref, s32[1,512]{1,0:T(1,128)} %get-tuple-element.99.column_slot_ref, bf16[512,8192]{1,0:T(8,128)(2,1)} %tokens_ref.11, ...), custom_call_target="tpu_custom_call" | custom-call | flops 2147483648 | bytes 6553600 | tf_op jit(solution)/shard_map/pallas_call | solution.py:266
  54.0 1.7 %collective-permute-done.10.refs_6_ = bf16[2304,128]{1,0:T(8,128)(2,1)} collective-permute-done((bf16[2304,128]{1,0:T(8,128)(2,1)}, bf16[2304,128]{1,0:T(8,128)(2,1)}, u32[]{:S(2)}, u32[]{:S(2)}) %collective-permute-start.10) | collective-permute-done | bytes 589856 | tf_op jit(solution)/shard_map/ppermute | solution.py:360
  55.7 1.3 %collective-permute-done.8.refs_1_ = bf16[2304,128]{1,0:T(8,128)(2,1)} collective-permute-done((bf16[2304,128]{1,0:T(8,128)(2,1)}, bf16[2304,128]{1,0:T(8,128)(2,1)}, u32[]{:S(2)}, u32[]{:S(2)}) %collective-permute-start.8) | collective-permute-done | bytes 589856 | tf_op jit(solution)/shard_map/ppermute | solution.py:360
  57.0 0.0 collective-permute-done.9.refs_2_
  57.0 3.4 %collective-permute-start.11 = (bf16[2304,128]{1,0:T(8,128)(2,1)}, bf16[2304,128]{1,0:T(8,128)(2,1)}, u32[]{:S(2)}, u32[]{:S(2)}) collective-permute-start(bf16[2304,128]{1,0:T(8,128)(2,1)} %shard_map.83.refs_4_), channel_id=1, source_target_pairs={{0,4},{1,5},{2,6},{3,7},{4,12},{5,13},{6,14},{7,15},{8,0},{9,1},{1... | collective-permute-start | bytes 1769480 | tf_op jit(solution)/shard_map/ppermute | solution.py:360
  60.5 0.0 collective-permute-start.12
  60.5 0.5 collective-permute-start.13
  61.0 6.4 %shard_map.87.total_ref = f32[512,1024]{1,0:T(8,128)} custom-call(bf16[512,8192]{1,0:T(8,128)(2,1)} %tokens_ref.11, bf16[8192,1024]{1,0:T(8,128)(2,1)} %weight_ref.5, f32[512,1024]{1,0:T(8,128)} %shard_map.85.refs_0_), custom_call_target="tpu_custom_call" | custom-call | flops 2147483648 | bytes 8388608 | tf_op jit(solution)/shard_map/pallas_call | solution.py:159
  67.4 5.1 %collective-permute-done.11.refs_7_ = bf16[2304,128]{1,0:T(8,128)(2,1)} collective-permute-done((bf16[2304,128]{1,0:T(8,128)(2,1)}, bf16[2304,128]{1,0:T(8,128)(2,1)}, u32[]{:S(2)}, u32[]{:S(2)}) %collective-permute-start.11) | collective-permute-done | bytes 589856 | tf_op jit(solution)/shard_map/ppermute | solution.py:360
  72.4 0.0 collective-permute-done.12.refs_3_
  72.4 0.0 collective-permute-done.13.refs_0_
  72.5 0.6 collective-permute-start.14
  73.0 0.7 collective-permute-start.15
  73.7 0.6 collective-permute-start.16
  74.2 0.6 slice.11.column_slot_ref
  74.8 0.0 copy-start
  74.8 10.2 %shard_map.88 = (f32[512,128]{1,0:T(8,128)}, f32[512,128]{1,0:T(8,128)}, bf16[256,1024]{1,0:T(8,128)(2,1)}) custom-call(s32[34]{0:T(128)} %dynamic-slice_bitcast_fusion.info_ref, s32[1024,1]{1,0:T(8,128)} %copy.18.row_slot_ref, s32[1,1024]{1,0:T(1,128)} %slice.11.column_slot_ref, bf16[512,8192]{1,0:T(8,128)(2,1)} %tokens_ref.11, ...), custom_call_target="tpu_custom_call" | custom-call | flops 4294967296 | bytes 13107200 | tf_op jit(solution)/shard_map/pallas_call | solution.py:266
  85.0 0.1 collective-permute-start.19
  85.1 0.0 copy-done
  85.1 0.5 collective-permute-start.18
  85.6 0.0 collective-permute-done.14.refs_1_
  85.6 0.0 collective-permute-done.15.refs_2_
  85.6 0.0 collective-permute-done.16.refs_3_
  85.6 7.3 %shard_map.89 = (f32[512,128]{1,0:T(8,128)}, f32[512,128]{1,0:T(8,128)}, bf16[128,1024]{1,0:T(8,128)(2,1)}) custom-call(s32[34]{0:T(128)} %dynamic-slice_bitcast_fusion.info_ref, s32[1024,1]{1,0:T(8,128)} %copy.18.row_slot_ref, s32[1,512]{1,0:T(1,128)} %get-tuple-element.100.column_slot_ref, bf16[512,8192]{1,0:T(8,128)(2,1)} %tokens_ref.11, ...), custom_call_target="tpu_custom_call" | custom-call | flops 2147483648 | bytes 6553600 | tf_op jit(solution)/shard_map/pallas_call | solution.py:266
  93.0 0.2 collective-permute-start.17
  93.1 0.4 collective-permute-start.20
  93.5 0.8 copy.19.row_slot_ref
  94.4 0.0 collective-permute-done.18.refs_1_
  94.4 0.0 collective-permute-done.19.refs_3_
  94.4 0.5 collective-permute-done.17.theirs_ref
  94.9 0.4 collective-permute-done.20.refs_5_
  95.3 6.8 %shard_map.90 = bf16[512,1024]{1,0:T(8,128)(2,1)} custom-call(s32[34]{0:T(128)} %dynamic-slice_bitcast_fusion.info_ref, s32[512,1]{1,0:T(8,128)} %copy.19.row_slot_ref, f32[512,128]{1,0:T(8,128)} %get-tuple-element.93.mine_ref, f32[512,128]{1,0:T(8,128)} %collective-permute-done.17.theirs_ref, f32[512,1024]{1,0:T(8,128)} %shard_map.87.total_ref, ...), custom_call_target="tpu_custom_call" | custom-call | flops 2147483648 | bytes 5242880 | tf_op jit(solution)/shard_map/pallas_call | solution.py:321
  (1 shorter events, 0.0 us)
Async XLA Ops:
  0.0 3.4 %collective-permute-start = (bf16[4,16,8192]{2,1,0:T(8,128)(2,1)}, bf16[4,16,8192]{2,1,0:T(8,128)(2,1)}, u32[]{:S(2)}, u32[]{:S(2)}) collective-permute-start(bf16[4,16,8192]{2,1,0:T(8,128)(2,1)} %here_ref.3), channel_id=1, source_target_pairs={{0,1},{1,0},{2,3},{3,2},{4,5},{5,4},{6,7},{7,6},{8,9},{9,8},{10,11... | collective-permute-start | bytes 3145736 | tf_op jit(solution)/shard_map/ppermute | solution.py:360
  3.4 39.4 %collective-permute-start.7 = (bf16[512,8192]{1,0:T(8,128)(2,1)}, bf16[512,8192]{1,0:T(8,128)(2,1)}, u32[]{:S(2)}, u32[]{:S(2)}) collective-permute-start(bf16[512,8192]{1,0:T(8,128)(2,1)} %tokens_ref.11), channel_id=1, source_target_pairs={{0,1},{1,0},{2,3},{3,2},{4,5},{5,4},{6,7},{7,6},{8,9},{9,8},{10,11... | collective-permute-start | bytes 25165832 | tf_op jit(solution)/shard_map/ppermute | solution.py:360
  6.5 17.9 %collective-permute-start.1 = (bf16[2304,128]{1,0:T(8,128)(2,1)}, bf16[2304,128]{1,0:T(8,128)(2,1)}, u32[]{:S(2)}, u32[]{:S(2)}) collective-permute-start(bf16[2304,128]{1,0:T(8,128)(2,1)} %shard_map.82.refs_0_), channel_id=1, source_target_pairs={{0,4},{1,5},{2,6},{3,7},{4,12},{5,13},{6,14},{7,15},{8,0},{9,1},{1... | collective-permute-start | bytes 1769480 | tf_op jit(solution)/shard_map/ppermute | solution.py:360
  9.6 15.3 %collective-permute-start.2 = (bf16[2304,128]{1,0:T(8,128)(2,1)}, bf16[2304,128]{1,0:T(8,128)(2,1)}, u32[]{:S(2)}, u32[]{:S(2)}) collective-permute-start(bf16[2304,128]{1,0:T(8,128)(2,1)} %shard_map.82.refs_0_), channel_id=1, source_target_pairs={{0,2},{1,3},{2,0},{3,1},{4,6},{5,7},{6,4},{7,5},{8,10},{9,11},{10,... | collective-permute-start | bytes 1769480 | tf_op jit(solution)/shard_map/ppermute | solution.py:360
  11.0 11.1 %collective-permute-start.3 = (s32[512]{0:T(512)S(1)}, s32[512]{0:T(512)S(1)}, u32[]{:S(2)}, u32[]{:S(2)}) collective-permute-start(s32[512]{0:T(512)S(1)} %select_reduce_fusion), channel_id=1, source_target_pairs={{0,1},{1,0},{2,3},{3,2},{4,5},{5,4},{6,7},{7,6},{8,9},{9,8},{10,11... | collective-permute-start | bytes 6152 | tf_op jit(solution)/shard_map/ppermute | solution.py:360
  24.8 15.5 %collective-permute-start.4 = (bf16[2304,128]{1,0:T(8,128)(2,1)}, bf16[2304,128]{1,0:T(8,128)(2,1)}, u32[]{:S(2)}, u32[]{:S(2)}) collective-permute-start(bf16[2304,128]{1,0:T(8,128)(2,1)} %collective-permute-done.1.refs_1_), channel_id=1, source_target_pairs={{0,4},{1,5},{2,6},{3,7},{4,12},{5,13},{6,14},{7,15},{8,0},{9,1},{1... | collective-permute-start | bytes 1769480 | tf_op jit(solution)/shard_map/ppermute | solution.py:360
  27.4 14.1 %collective-permute-start.5 = (bf16[2304,128]{1,0:T(8,128)(2,1)}, bf16[2304,128]{1,0:T(8,128)(2,1)}, u32[]{:S(2)}, u32[]{:S(2)}) collective-permute-start(bf16[2304,128]{1,0:T(8,128)(2,1)} %collective-permute-done.1.refs_1_), channel_id=1, source_target_pairs={{0,2},{1,3},{2,0},{3,1},{4,6},{5,7},{6,4},{7,5},{8,10},{9,11},{10,... | collective-permute-start | bytes 1769480 | tf_op jit(solution)/shard_map/ppermute | solution.py:360
  28.9 13.8 %collective-permute-start.6 = (bf16[2304,128]{1,0:T(8,128)(2,1)}, bf16[2304,128]{1,0:T(8,128)(2,1)}, u32[]{:S(2)}, u32[]{:S(2)}) collective-permute-start(bf16[2304,128]{1,0:T(8,128)(2,1)} %collective-permute-done.2.refs_2_), channel_id=1, source_target_pairs={{0,16},{1,17},{2,18},{3,19},{4,20},{5,21},{6,22},{7,23},{8,24},{9,... | collective-permute-start | bytes 1769480 | tf_op jit(solution)/shard_map/ppermute | solution.py:360
  42.8 12.9 %collective-permute-start.10 = (bf16[2304,128]{1,0:T(8,128)(2,1)}, bf16[2304,128]{1,0:T(8,128)(2,1)}, u32[]{:S(2)}, u32[]{:S(2)}) collective-permute-start(bf16[2304,128]{1,0:T(8,128)(2,1)} %collective-permute-done.4.refs_3_), channel_id=1, source_target_pairs={{0,16},{1,17},{2,18},{3,19},{4,20},{5,21},{6,22},{7,23},{8,24},{9,... | collective-permute-start | bytes 1769480 | tf_op jit(solution)/shard_map/ppermute | solution.py:360
  44.3 12.7 %collective-permute-start.8 = (bf16[2304,128]{1,0:T(8,128)(2,1)}, bf16[2304,128]{1,0:T(8,128)(2,1)}, u32[]{:S(2)}, u32[]{:S(2)}) collective-permute-start(bf16[2304,128]{1,0:T(8,128)(2,1)} %shard_map.82.refs_0_), channel_id=1, source_target_pairs={{0,8},{1,9},{2,10},{3,11},{4,0},{5,1},{6,2},{7,3},{8,12},{9,13},{1... | collective-permute-start | bytes 1769480 | tf_op jit(solution)/shard_map/ppermute | solution.py:360
  44.6 12.4 %collective-permute-start.9 = (bf16[2304,128]{1,0:T(8,128)(2,1)}, bf16[2304,128]{1,0:T(8,128)(2,1)}, u32[]{:S(2)}, u32[]{:S(2)}) collective-permute-start(bf16[2304,128]{1,0:T(8,128)(2,1)} %collective-permute-done.4.refs_3_), channel_id=1, source_target_pairs={{0,2},{1,3},{2,0},{3,1},{4,6},{5,7},{6,4},{7,5},{8,10},{9,11},{10,... | collective-permute-start | bytes 1769480 | tf_op jit(solution)/shard_map/ppermute | solution.py:360
  57.0 15.4 %collective-permute-start.11 = (bf16[2304,128]{1,0:T(8,128)(2,1)}, bf16[2304,128]{1,0:T(8,128)(2,1)}, u32[]{:S(2)}, u32[]{:S(2)}) collective-permute-start(bf16[2304,128]{1,0:T(8,128)(2,1)} %shard_map.83.refs_4_), channel_id=1, source_target_pairs={{0,4},{1,5},{2,6},{3,7},{4,12},{5,13},{6,14},{7,15},{8,0},{9,1},{1... | collective-permute-start | bytes 1769480 | tf_op jit(solution)/shard_map/ppermute | solution.py:360
  60.5 12.0 %collective-permute-start.12 = (bf16[2304,128]{1,0:T(8,128)(2,1)}, bf16[2304,128]{1,0:T(8,128)(2,1)}, u32[]{:S(2)}, u32[]{:S(2)}) collective-permute-start(bf16[2304,128]{1,0:T(8,128)(2,1)} %collective-permute-done.8.refs_1_), channel_id=1, source_target_pairs={{0,2},{1,3},{2,0},{3,1},{4,6},{5,7},{6,4},{7,5},{8,10},{9,11},{10,... | collective-permute-start | bytes 1769480 | tf_op jit(solution)/shard_map/ppermute | solution.py:360
  60.5 12.0 %collective-permute-start.13 = (bf16[2304,128]{1,0:T(8,128)(2,1)}, bf16[2304,128]{1,0:T(8,128)(2,1)}, u32[]{:S(2)}, u32[]{:S(2)}) collective-permute-start(bf16[2304,128]{1,0:T(8,128)(2,1)} %collective-permute-done.5.refs_0_), channel_id=1, source_target_pairs={{0,16},{1,17},{2,18},{3,19},{4,20},{5,21},{6,22},{7,23},{8,24},{9,... | collective-permute-start | bytes 1769480 | tf_op jit(solution)/shard_map/ppermute | solution.py:360
  72.5 13.1 %collective-permute-start.14 = (bf16[2304,128]{1,0:T(8,128)(2,1)}, bf16[2304,128]{1,0:T(8,128)(2,1)}, u32[]{:S(2)}, u32[]{:S(2)}) collective-permute-start(bf16[2304,128]{1,0:T(8,128)(2,1)} %shard_map.83.refs_4_), channel_id=1, source_target_pairs={{0,8},{1,9},{2,10},{3,11},{4,0},{5,1},{6,2},{7,3},{8,12},{9,13},{1... | collective-permute-start | bytes 1769480 | tf_op jit(solution)/shard_map/ppermute | solution.py:360
  73.0 12.6 %collective-permute-start.15 = (bf16[2304,128]{1,0:T(8,128)(2,1)}, bf16[2304,128]{1,0:T(8,128)(2,1)}, u32[]{:S(2)}, u32[]{:S(2)}) collective-permute-start(bf16[2304,128]{1,0:T(8,128)(2,1)} %collective-permute-done.10.refs_6_), channel_id=1, source_target_pairs={{0,2},{1,3},{2,0},{3,1},{4,6},{5,7},{6,4},{7,5},{8,10},{9,11},{10,... | collective-permute-start | bytes 1769480 | tf_op jit(solution)/shard_map/ppermute | solution.py:360
  73.7 11.9 %collective-permute-start.16 = (bf16[2304,128]{1,0:T(8,128)(2,1)}, bf16[2304,128]{1,0:T(8,128)(2,1)}, u32[]{:S(2)}, u32[]{:S(2)}) collective-permute-start(bf16[2304,128]{1,0:T(8,128)(2,1)} %collective-permute-done.12.refs_3_), channel_id=1, source_target_pairs={{0,16},{1,17},{2,18},{3,19},{4,20},{5,21},{6,22},{7,23},{8,24},{9,... | collective-permute-start | bytes 1769480 | tf_op jit(solution)/shard_map/ppermute | solution.py:360
  74.8 10.3 %copy-start = (bf16[128,1024]{1,0:T(8,128)(2,1)S(1)}, bf16[128,1024]{1,0:T(8,128)(2,1)}, u32[]{:S(2)}) copy-start(bf16[128,1024]{1,0:T(8,128)(2,1)} %get-tuple-element.96.refs_0_) | copy-start | bytes 786436
  85.0 9.4 %collective-permute-start.19 = (bf16[256,1024]{1,0:T(8,128)(2,1)}, bf16[256,1024]{1,0:T(8,128)(2,1)}, u32[]{:S(2)}, u32[]{:S(2)}) collective-permute-start(bf16[256,1024]{1,0:T(8,128)(2,1)} %get-tuple-element.97.refs_2_), channel_id=1, source_target_pairs={{0,1},{1,0},{2,3},{3,2},{4,5},{5,4},{6,7},{7,6},{8,9},{9,8},{10,11... | collective-permute-start | bytes 1572872 | tf_op jit(solution)/shard_map/ppermute | solution.py:360
  85.1 9.3 %collective-permute-start.18 = (bf16[128,1024]{1,0:T(8,128)(2,1)S(1)}, bf16[128,1024]{1,0:T(8,128)(2,1)}, u32[]{:S(2)}, u32[]{:S(2)}) collective-permute-start(bf16[128,1024]{1,0:T(8,128)(2,1)S(1)} %copy-done), channel_id=1, source_target_pairs={{0,1},{1,0},{2,3},{3,2},{4,5},{5,4},{6,7},{7,6},{8,9},{9,8},{10,11... | collective-permute-start | bytes 786440 | tf_op jit(solution)/shard_map/ppermute | solution.py:360
  93.0 1.9 %collective-permute-start.17 = (f32[512,128]{1,0:T(8,128)}, f32[512,128]{1,0:T(8,128)}, u32[]{:S(2)}, u32[]{:S(2)}) collective-permute-start(f32[512,128]{1,0:T(8,128)} %get-tuple-element.94), channel_id=1, source_target_pairs={{0,1},{1,0},{2,3},{3,2},{4,5},{5,4},{6,7},{7,6},{8,9},{9,8},{10,11... | collective-permute-start | bytes 786440 | tf_op jit(solution)/shard_map/ppermute | solution.py:360
  93.1 2.2 %collective-permute-start.20 = (bf16[128,1024]{1,0:T(8,128)(2,1)}, bf16[128,1024]{1,0:T(8,128)(2,1)}, u32[]{:S(2)}, u32[]{:S(2)}) collective-permute-start(bf16[128,1024]{1,0:T(8,128)(2,1)} %get-tuple-element.98.refs_4_), channel_id=1, source_target_pairs={{0,1},{1,0},{2,3},{3,2},{4,5},{5,4},{6,7},{7,6},{8,9},{9,8},{10,11... | collective-permute-start | bytes 786440 | tf_op jit(solution)/shard_map/ppermute | solution.py:360

commit v8 on v7

--- a/solution.py
+++ b/solution.py
@@ -15,12 +15,13 @@
 RANK = 16
 
 PIECES = (
-    *((0, 0, 0), (1, 0, 0), (0, 1, 0), (2, 0, 0)),
-    *((1, 1, 0), (3, 0, 0), (2, 1, 0), (3, 1, 0)),
-    *((0, 0, 1), (0, 1, 1), (2, 0, 1), (1, 0, 1)),
+    *((0, 0, 0), (1, 0, 0), (0, 1, 0)),
+    *((2, 0, 0), (1, 1, 0), (3, 0, 0), (2, 1, 0)),
+    *((0, 0, 1), (0, 1, 1), (2, 0, 1), (1, 0, 1), (3, 1, 0)),
     *((1, 1, 1), (3, 0, 1), (2, 1, 1), (3, 1, 1)),
 )
-TOGETHER = 4
+KERNEL_BOUNDS = (0, 3, 7, 12, 16)
+QUARTER_CUTS = (0, 512, 1024, 2048)
 VMEM_BYTES = 64 * 1024 * 1024 - 512 * 1024
 
 
@@ -126,134 +127,118 @@
     )(info, here, there, up)
 
 
-def base_kernel(steps, tokens_ref, weight_ref, *refs):
+def base_kernel(tokens_ref, weight_ref, out_ref):
     step = pl.program_id(0)
-    more = len(refs) > 1
-    out_ref = refs[1] if more else refs[0]
-    copies = [pltpu.make_async_copy(refs[0], refs[2], refs[3].at[0])] if more else []
     part = jnp.dot(tokens_ref[...], weight_ref[...], preferred_element_type=jnp.float32)
 
     @pl.when(step == 0)
     def _():
-        started(copies)
         out_ref[...] = part
 
     @pl.when(step > 0)
     def _():
         out_ref[...] += part
 
-    if more:
-
-        @pl.when(step == steps - 1)
-        def _():
-            awaited(copies)
-            out_ref[...] += refs[2][...]
-
-
-def base_part(tokens, weight, begin, end, total=None):
+
+def base_half(tokens, weight, half):
     rows, depth = tokens.shape
-    width = weight.shape[1]
-    steps, first = (end - begin) // DEPTH_TILE, begin // DEPTH_TILE
-    result = jax.ShapeDtypeStruct((rows, width), jnp.float32)
-    more = total is not None
+    width = weight.shape[1] // 2
     return pl.pallas_call(
-        functools.partial(base_kernel, steps),
-        out_shape=result,
-        grid=(steps,),
+        base_kernel,
+        out_shape=jax.ShapeDtypeStruct((rows, width), jnp.float32),
+        grid=(depth // DEPTH_TILE,),
         in_specs=[
-            pl.BlockSpec((rows, DEPTH_TILE), lambda k: (0, first + k)),
-            pl.BlockSpec((DEPTH_TILE, width), lambda k: (first + k, 0)),
-        ]
-        + [pl.BlockSpec(memory_space=pl.ANY)] * more,
+            pl.BlockSpec((rows, DEPTH_TILE), lambda k: (0, k)),
+            pl.BlockSpec((DEPTH_TILE, width), lambda k: (k, half)),
+        ],
         out_specs=pl.BlockSpec((rows, width), lambda k: (0, 0)),
-        scratch_shapes=[pltpu.VMEM((rows, width), jnp.float32), pltpu.SemaphoreType.DMA((1,))]
-        if more
-        else [],
         cost_estimate=pl.CostEstimate(
-            flops=2 * rows * width * (end - begin),
-            bytes_accessed=2 * (rows + width) * (end - begin) + 4 * rows * width,
+            flops=2 * rows * width * depth,
+            bytes_accessed=2 * (rows + width) * depth + 4 * rows * width,
             transcendentals=0,
         ),
         compiler_params=params(),
-    )(tokens, weight, *([total] if more else []))
+    )(tokens, weight)
 
 
 def absorb_kernel(
-    backs, more, info_ref, row_slot_ref, column_slot_ref, tokens_ref, other_ref, *refs
+    groups, start, more, info_ref, row_slot_ref, column_slot_ref, tokens_ref, other_ref, *refs
 ):
-    count = TOGETHER * len(backs)
+    count = sum(size for size, _ in groups)
     sources, refs = refs[:count], refs[count:]
     before, refs = refs[: 2 * more], refs[2 * more :]
-    outs, up_ref, (rows_ref, down_ref, sems) = refs[:2], refs[2], refs[3:]
+    outs, up_ref, rows_ref, refs = refs[:2], refs[2], refs[3], refs[4:]
+    down_refs, sems = refs[: len(groups)], refs[len(groups)]
     rows = tokens_ref.shape[0]
     quarter = rows_ref.shape[2]
     y, core = info_ref[0], info_ref[1]
-    copies = 0
-    downs, tiles = [], {}
-
-    def begin(source, target):
-        nonlocal copies
-        copy = pltpu.make_async_copy(source, target, sems.at[copies])
-        copies += 1
+    cuts = list(zip(QUARTER_CUTS, QUARTER_CUTS[1:]))
+    copies, waits = [], {}
+
+    def begin(key, source, target):
+        copy = pltpu.make_async_copy(source, target, sems.at[len(copies)])
+        copies.append(copy)
+        waits.setdefault(key, []).append(copy)
         copy.start()
-        return copy
-
-    for n, back in enumerate(backs):
-        downs.append(
-            [
-                begin(sources[TOGETHER * n + i], down_ref.at[n, :, pl.ds(i * LANES, LANES)])
-                for i in range(TOGETHER)
-            ]
-        )
-        if back in tiles:
-            continue
-        place = len(tiles)
-        tiles[back] = []
-        first = core * 2 * quarter + (1 - y if back else y) * quarter
-        for k in range(0, quarter, DEPTH_TILE):
-            columns = pl.ds(pl.multiple_of(first + k, DEPTH_TILE), DEPTH_TILE)
-            pair = [
+
+    places = {}
+    first = 0
+    for n, ((size, back), down_ref) in enumerate(zip(groups, down_refs)):
+        load = back not in places
+        place = places.setdefault(back, len(places))
+        column = (2 * core + (1 - y if back else y)) * quarter
+        ends = cuts + [(quarter, sources[0].shape[0])]
+        for low, high in ends:
+            for i in range(size):
                 begin(
+                    (n, low),
+                    sources[first + i].at[pl.ds(low, high - low)],
+                    down_ref.at[pl.ds(low, high - low), pl.ds(i * LANES, LANES)],
+                )
+            if not load or low == quarter:
+                continue
+            columns = pl.ds(pl.multiple_of(column + low, QUARTER_CUTS[1]), high - low)
+            for i, source in enumerate((tokens_ref, other_ref)):
+                begin(
+                    (n, low),
                     source.at[:, columns],
-                    rows_ref.at[place, pl.ds(i * rows, rows), pl.ds(k, DEPTH_TILE)],
+                    rows_ref.at[place, pl.ds(i * rows, rows), pl.ds(low, high - low)],
                 )
-                for i, source in enumerate((tokens_ref, other_ref))
-            ]
-            tiles[back].append([place, k, pair])
+        first += size
     state = None
-    for n, back in enumerate(backs):
-        awaited(downs[n])
+    first = 0
+    for n, ((size, back), down_ref) in enumerate(zip(groups, down_refs)):
         shrink = None
-        for tile in tiles[back]:
-            place, k, pair = tile
-            awaited(pair)
-            tile[2] = []
+        for low, high in cuts:
+            awaited(waits[n, low])
             part = jnp.dot(
-                rows_ref[place, :, k : k + DEPTH_TILE],
-                down_ref[n, k : k + DEPTH_TILE, :],
+                rows_ref[places[back], :, low:high],
+                down_ref[low:high],
                 preferred_element_type=jnp.float32,
             )
             shrink = part if shrink is None else shrink + part
+        awaited(waits[n, quarter])
         height = up_ref.shape[0] // count
-        for i in range(TOGETHER):
-            lanes, which = slice(i * LANES, (i + 1) * LANES), TOGETHER * n + i
-            wanted = column_slot_ref[:, which * LANES : (which + 1) * LANES]
+        for i in range(size):
+            lanes, which = slice(i * LANES, (i + 1) * LANES), first + i
+            wanted = column_slot_ref[:, (start + which) * LANES : (start + which + 1) * LANES]
             kept = jnp.where(row_slot_ref[...] == wanted, shrink[:, lanes], 0.0)
             state = kept if state is None else state + kept
             for j in range(up_ref.shape[1] // LANES):
-                first = quarter + j * height
+                top = quarter + j * height
                 up_ref[
                     which * height : (which + 1) * height, j * LANES : (j + 1) * LANES
-                ] = down_ref[n, first : first + height, lanes]
+                ] = down_ref[top : top + height, lanes]
+        first += size
     for i, out_ref in enumerate(outs):
         own = state[i * rows : (i + 1) * rows]
         out_ref[...] = own + before[i][...] if more else own
 
 
-def absorb(info, row_slots, column_slot, tokens, other, width, fours, before=None):
+def absorb(info, row_slots, column_slots, tokens, other, width, groups, start, before):
     rows, depth = tokens.shape
-    pieces = [piece for four, _ in fours for piece in four]
-    backs = [back for _, back in fours]
+    pieces = [piece for group, _ in groups for piece in group]
+    sizes = [(len(group), back) for group, back in groups]
     quarter = depth // 4
     height = pieces[0].shape[0]
     anywhere = pl.BlockSpec(memory_space=pl.ANY)
@@ -261,39 +246,42 @@
     more = before is not None
     state = jax.ShapeDtypeStruct((rows, LANES), jnp.float32)
     up_rows = len(pieces) * (height - quarter) * LANES // width
-    quarters = len(set(backs))
-    copies = len(pieces) + 2 * quarters * (quarter // DEPTH_TILE)
+    quarters = len({back for _, back in groups})
+    cuts = len(QUARTER_CUTS) - 1
+    copies = len(pieces) * (cuts + 1) + 2 * quarters * cuts
     return pl.pallas_call(
-        functools.partial(absorb_kernel, backs, more),
+        functools.partial(absorb_kernel, sizes, start, more),
         out_shape=(state, state, jax.ShapeDtypeStruct((up_rows, width), tokens.dtype)),
         in_specs=[pl.BlockSpec(memory_space=pltpu.SMEM), vmem, vmem]
         + [anywhere] * (2 + len(pieces))
         + [vmem] * (2 * more),
         out_specs=(vmem, vmem, vmem),
-        scratch_shapes=[
-            pltpu.VMEM((quarters, 2 * rows, quarter), tokens.dtype),
-            pltpu.VMEM((len(fours), height, TOGETHER * LANES), tokens.dtype),
-            pltpu.SemaphoreType.DMA((copies,)),
-        ],
+        scratch_shapes=[pltpu.VMEM((quarters, 2 * rows, quarter), tokens.dtype)]
+        + [pltpu.VMEM((height, size * LANES), tokens.dtype) for size, _ in sizes]
+        + [pltpu.SemaphoreType.DMA((copies,))],
         cost_estimate=pl.CostEstimate(
             flops=4 * rows * len(pieces) * LANES * quarter,
             bytes_accessed=4 * rows * quarters * quarter + 2 * len(pieces) * LANES * height,
             transcendentals=0,
         ),
         compiler_params=params(),
-    )(info, row_slots, column_slot, tokens, other, *pieces, *(before or ()))
+    )(info, row_slots, column_slots, tokens, other, *pieces, *(before or ()))
 
 
 def finish_kernel(
-    count, info_ref, row_slot_ref, mine_ref, theirs_ref, total_ref, *refs
+    count, info_ref, row_slot_ref, mine_ref, theirs_ref, left_ref, right_ref, *refs
 ):
     sources, (out_ref, total, up, sems) = refs[:count], refs[count:]
     rows = out_ref.shape[0]
     height = up.shape[0] // (len(PIECES) * 2)
-    copies = [pltpu.make_async_copy(total_ref, total, sems.at[0])]
+    half = left_ref.shape[1]
+    copies = [
+        pltpu.make_async_copy(source, total.at[:, pl.ds(n * half, half)], sems.at[n])
+        for n, source in enumerate((left_ref, right_ref))
+    ]
     for source in sources:
         for n in range(0, source.shape[0], height):
-            first = pl.multiple_of(info_ref[1 + len(copies)], height)
+            first = pl.multiple_of(info_ref[len(copies)], height)
             copies.append(
                 pltpu.make_async_copy(
                     source.at[pl.ds(n, height)], up.at[pl.ds(first, height)], sems.at[len(copies)]
@@ -313,8 +301,8 @@
     out_ref[...] = (total[...] + (lora[:rows] + lora[rows:])).astype(out_ref.dtype)
 
 
-def finish(info, row_slot, mine, theirs, total, ups):
-    rows, width = total.shape
+def finish(info, row_slot, mine, theirs, left, right, ups):
+    rows, width = left.shape[0], 2 * left.shape[1]
     anywhere = pl.BlockSpec(memory_space=pl.ANY)
     vmem = pl.BlockSpec(memory_space=pltpu.VMEM)
     up_rows = sum(up.shape[0] for up in ups)
@@ -322,12 +310,12 @@
         functools.partial(finish_kernel, len(ups)),
         out_shape=jax.ShapeDtypeStruct((rows, width), jnp.bfloat16),
         in_specs=[pl.BlockSpec(memory_space=pltpu.SMEM), vmem, vmem, vmem]
-        + [anywhere] * (1 + len(ups)),
+        + [anywhere] * (2 + len(ups)),
         out_specs=vmem,
         scratch_shapes=[
             pltpu.VMEM((rows, width), jnp.float32),
             pltpu.VMEM((up_rows, width), ups[0].dtype),
-            pltpu.SemaphoreType.DMA((1 + 2 * len(PIECES),)),
+            pltpu.SemaphoreType.DMA((2 + 2 * len(PIECES),)),
         ],
         cost_estimate=pl.CostEstimate(
             flops=4 * rows * width * up_rows,
@@ -335,7 +323,7 @@
             transcendentals=0,
         ),
         compiler_params=params(),
-    )(info, row_slot, mine, theirs, total, *ups)
+    )(info, row_slot, mine, theirs, left, right, *ups)
 
 
 def passed_round(
@@ -372,7 +360,7 @@
         return (along_z(r, -piece[0]) ^ (2 * piece[1])) // 2
 
     per_chip = LANES // rank
-    kernels = (PIECES[:4], PIECES[4:12], PIECES[12:])
+    kernels = [PIECES[low:high] for low, high in zip(KERNEL_BOUNDS, KERNEL_BOUNDS[1:])]
     column_table, info_table = [], []
     for g in range(planes):
         for r in range(owners):
@@ -396,50 +384,67 @@
     def together(*values):
         return lax.optimization_barrier(values)
 
+    def after(value, *others):
+        return lax.optimization_barrier((value, *others))[0]
+
     there = core_swap(adapter_down_weight)
     row_slot = slots_of_rows(row_adapter_index, adapter_storage_slot)
     there, tokens_late, info, row_slot, column_slots = together(
         there, tokens, info, row_slot, column_slots
     )
-    piece = lambda back: assemble(back, info, adapter_down_weight, there, adapter_up_weight)
+
+    def piece(back, *others):
+        return assemble(
+            back, after(info, *others), adapter_down_weight, there, adapter_up_weight
+        )
+
     front = piece(0)
 
     z1, x0 = z_ring(front), x_swap(front)
     other = core_swap(tokens_late)
     other_slot = core_swap(row_slot[:, 0])
-    back = piece(1)
-    third = 3 * DEPTH_TILE
-    total = base_part(tokens, base_value_weight, 0, third)
+    left = base_half(after(tokens, front), base_value_weight, 0)
     row_slots = jnp.concatenate([row_slot, other_slot[:, None]], axis=0)
-    z1, x0, front, back, total, row_slots = together(z1, x0, front, back, total, row_slots)
-
-    z2, x1, yx0 = z_ring(z1), x_swap(z1), y_swap(x0)
-    total = base_part(tokens, base_value_weight, third, 2 * third, total)
-    z2, x1, yx0, front, other, total = together(z2, x1, yx0, front, other, total)
+
+    z2 = z_ring(after(z1, left))
+    x1 = x_swap(after(z1, x0, left))
+    yx0 = y_swap(after(x0, left))
+    right = base_half(after(tokens, z1, x0, left, row_slots), base_value_weight, 1)
     ups = []
 
-    def update(first, fours, before=None):
-        lanes = slice(first * LANES, (first + TOGETHER * len(fours)) * LANES)
+    def update(number, groups, before, *others):
         mine, others, up = absorb(
-            info, row_slots, column_slots[:, lanes], tokens, other, width, fours, before
+            after(info, *others),
+            row_slots,
+            column_slots,
+            tokens,
+            other,
+            width,
+            groups,
+            KERNEL_BOUNDS[number],
+            before,
         )
         ups.extend([up, core_swap(up)])
         return mine, others
 
-    z3, x2, yz2 = z_back(front), x_swap(z2), y_swap(z2)
-    state = update(0, [((front, z1, x0, z2), 0)])
-    z3, x2, yz2, x1, back, state, total = together(z3, x2, yz2, x1, back, state, total)
-
-    zb1, x3, yx1 = z_ring(back), x_swap(z3), y_swap(x1)
-    total = base_part(tokens, base_value_weight, 2 * third, depth, total)
-    zb1, x3, yx1, yz2, back, state, total = together(zb1, x3, yx1, yz2, back, state, total)
-
-    zb3, xyz2, yx3 = z_back(back), x_swap(yz2), y_swap(x3)
-    state = update(4, [((x1, z3, x2, x3), 0), ((back, yx0, yz2, zb1), 1)], state)
-    zb3, xyz2, yx3, state = together(zb3, xyz2, yx3, state)
-
-    mine, others = update(12, [((yx1, zb3, xyz2, yx3), 1)], state)
-    return finish(info, row_slot, mine, core_swap(others), total, ups)
+    z3 = z_back(after(front, z2, right))
+    x2 = x_swap(after(z2, x1, right))
+    yz2 = y_swap(after(z2, yx0, right))
+    state = update(0, [((front, z1, x0), 0)], None, z2, x1, yx0, right)
+    back = piece(1, z2, x1, yx0, right)
+
+    zb1 = z_ring(after(back, z3, state[0]))
+    x3 = x_swap(after(z3, x2, state[0]))
+    yx1 = y_swap(after(x1, yz2, state[0]))
+    state = update(1, [((z2, x1, z3, x2), 0)], state, z3, x2, yz2, back)
+
+    zb3 = z_back(after(back, zb1, state[0]))
+    xyz2 = x_swap(after(yz2, x3, state[0]))
+    yx3 = y_swap(after(x3, yx1, state[0]))
+    state = update(2, [((back, yx0, yz2, zb1), 1), ((x3,), 0)], state, zb1, x3, yx1, ups[1])
+
+    mine, others = update(3, [((yx1, zb3, xyz2, yx3), 1)], state, ups[3], ups[5])
+    return finish(info, row_slot, mine, core_swap(others), left, right, ups)
 
 
 def solution(mesh):

time: 103 us -> 109 us (1.058)
  Pallas kernels: 60.2 us -> 68.7 us
  starting transfers between devices: 20 us -> 18.5 us
  waiting for transfers between devices: 15.7 us -> 14.5 us
    pallas_call x6, Pallas kernels: 47.5 us -> 55.9 us  [the longest x4 32.6 us: absorb(): pl.pallas_call(functools.partial(absorb_kernel, sizes, start, more), out_...]
    ppermute x21 -> x22, starting transfers between devices: 20 us -> 18.5 us  [permuted(): return lax.ppermute(array, axes, pairs)]
    slice x2 -> x0, local copies, waits for them, and re-layouts: 1.18 us -> none  [update(): column_slots[:, lanes]]
    ppermute x21 -> x22, waiting for transfers between devices: 15.7 us -> 14.5 us  [permuted(): return lax.ppermute(array, axes, pairs)]
  transfers between devices with their start and end apart: 21 -> 22, of which waited for: 10 -> 8; matrix products, arithmetic and copies ran while one was open for 6% -> 5% of each run, Pallas kernels for 52% -> 50%
where the time goes in v8:
time: 109 us; the launch traced here: 108 us
  Pallas kernels  68.7 us (63%)
  starting transfers between devices  18.5 us (17%)
  waiting for transfers between devices  14.5 us (13%)
  local copies, waits for them, and re-layouts  5.56 us (5%)
    pallas_call x4, Pallas kernels, absorb(): pl.pallas_call(functools.partial(absorb_kernel, sizes, start, more), out_...  32.6 us
    pallas_call x2, Pallas kernels, base_half(): pl.pallas_call(base_kernel, out_shape=jax.ShapeDtypeStruct((rows, width),...  23.3 us
    ppermute x22, starting transfers between devices, permuted(): return lax.ppermute(array, axes, pairs)  18.5 us
    ppermute x22, waiting for transfers between devices, permuted(): return lax.ppermute(array, axes, pairs)  14.5 us
    pallas_call x1, Pallas kernels, finish(): pl.pallas_call(functools.partial(finish_kernel, len(ups)), out_shape=jax....  6.79 us
    pallas_call x2, Pallas kernels, assemble(): pl.pallas_call(functools.partial(assemble_kernel, back), out_shape=jax.Sh...  5.97 us
  transfers between devices with their start and end apart: 22, of which 8 were waited for; matrix products, arithmetic and copies ran while one was open for 5% of the time, Pallas kernels for 50%

profile of v8, /device:TPU:0, one launch (start us, length us, event | category | flops | bytes accessed | tf_op | source)
XLA Modules:
  0.0 108.3 jit_solution(2750404751372760177)
XLA Ops:
  0.0 0.5 collective-permute-start
  0.5 1.3 %dynamic-slice_bitcast_fusion.info_ref = s32[34]{0:T(128)} fusion(s32[32,34]{1,0:T(8,128)} %constant.26.clone, s32[]{:T(128)S(6)} %select_n.10), kind=kLoop, calls=%fused_computation.3 | loop fusion | bytes 276 | tf_op jit(solution)/shard_map/jit(dynamic_index_in_dim)/squeeze | solution.py:379
  1.7 0.8 select_reduce_fusion
  2.5 1.4 %constant_dynamic-slice_fusion.column_slot_ref = s32[1,2048]{1,0:T(1,128)} fusion(s32[32,2048]{1,0:T(8,128)} %constant.27.clone, s32[]{:T(128)S(6)} %select_n.10), kind=kLoop, calls=%fused_computation.4 | loop fusion | bytes 16388 | tf_op jit(solution)/shard_map/jit(dynamic_index_in_dim)/dynamic_slice | solution.py:379
  4.0 0.0 collective-permute-done.there_ref
  4.0 0.1 collective-permute-start.10
  4.0 3.0 %shard_map.82.refs_0_ = bf16[2304,128]{1,0:T(8,128)(2,1)} custom-call(s32[34]{0:T(128)} %dynamic-slice_bitcast_fusion.info_ref, bf16[4,16,8192]{2,1,0:T(8,128)(2,1)} %here_ref.3, bf16[4,16,8192]{2,1,0:T(8,128)(2,1)} %collective-permute-done.there_ref, bf16[4,16,1024]{2,1,0:T(8,128)(2,1)} %up_ref.3), custom_call_target="tpu_custom_call" | custom-call | tf_op jit(solution)/shard_map/pallas_call | solution.py:117
  7.0 3.1 %collective-permute-start.1 = (bf16[2304,128]{1,0:T(8,128)(2,1)}, bf16[2304,128]{1,0:T(8,128)(2,1)}, u32[]{:S(2)}, u32[]{:S(2)}) collective-permute-start(bf16[2304,128]{1,0:T(8,128)(2,1)} %shard_map.82.refs_0_), channel_id=1, source_target_pairs={{0,4},{1,5},{2,6},{3,7},{4,12},{5,13},{6,14},{7,15},{8,0},{9,1},{1... | collective-permute-start | bytes 1769480 | tf_op jit(solution)/shard_map/ppermute | solution.py:348
  10.1 1.5 %collective-permute-start.3 = (bf16[2304,128]{1,0:T(8,128)(2,1)}, bf16[2304,128]{1,0:T(8,128)(2,1)}, u32[]{:S(2)}, u32[]{:S(2)}) collective-permute-start(bf16[2304,128]{1,0:T(8,128)(2,1)} %shard_map.82.refs_0_), channel_id=1, source_target_pairs={{0,2},{1,3},{2,0},{3,1},{4,6},{5,7},{6,4},{7,5},{8,10},{9,11},{10,... | collective-permute-start | bytes 1769480 | tf_op jit(solution)/shard_map/ppermute | solution.py:348
  11.6 11.7 %shard_map.83.left_ref = f32[512,512]{1,0:T(8,128)} custom-call(bf16[512,8192]{1,0:T(8,128)(2,1)} %tokens_ref.9, bf16[8192,1024]{1,0:T(8,128)(2,1)} %weight_ref.3), custom_call_target="tpu_custom_call" | custom-call | flops 4294967296 | bytes 17825792 | tf_op jit(solution)/shard_map/pallas_call | solution.py:146
  23.3 1.6 %collective-permute-done.1.refs_1_ = bf16[2304,128]{1,0:T(8,128)(2,1)} collective-permute-done((bf16[2304,128]{1,0:T(8,128)(2,1)}, bf16[2304,128]{1,0:T(8,128)(2,1)}, u32[]{:S(2)}, u32[]{:S(2)}) %collective-permute-start.1) | collective-permute-done | bytes 589856 | tf_op jit(solution)/shard_map/ppermute | solution.py:348
  24.9 0.9 collective-permute-start.2
  25.9 0.0 collective-permute-done.3.refs_2_
  25.9 1.4 %collective-permute-start.6 = (bf16[2304,128]{1,0:T(8,128)(2,1)}, bf16[2304,128]{1,0:T(8,128)(2,1)}, u32[]{:S(2)}, u32[]{:S(2)}) collective-permute-start(bf16[2304,128]{1,0:T(8,128)(2,1)} %collective-permute-done.1.refs_1_), channel_id=1, source_target_pairs={{0,2},{1,3},{2,0},{3,1},{4,6},{5,7},{6,4},{7,5},{8,10},{9,11},{10,... | collective-permute-start | bytes 1769480 | tf_op jit(solution)/shard_map/ppermute | solution.py:348
  27.2 1.5 %collective-permute-start.8 = (bf16[2304,128]{1,0:T(8,128)(2,1)}, bf16[2304,128]{1,0:T(8,128)(2,1)}, u32[]{:S(2)}, u32[]{:S(2)}) collective-permute-start(bf16[2304,128]{1,0:T(8,128)(2,1)} %collective-permute-done.3.refs_2_), channel_id=1, source_target_pairs={{0,16},{1,17},{2,18},{3,19},{4,20},{5,21},{6,22},{7,23},{8,24},{9,... | collective-permute-start | bytes 1769480 | tf_op jit(solution)/shard_map/ppermute | solution.py:348
  28.8 0.0 collective-permute-start.4
  28.8 1.2 %collective-permute-done.4 = s32[512]{0:T(512)S(1)} collective-permute-done((s32[512]{0:T(512)S(1)}, s32[512]{0:T(512)S(1)}, u32[]{:S(2)}, u32[]{:S(2)}) %collective-permute-start.4) | collective-permute-done | bytes 2080 | tf_op jit(solution)/shard_map/ppermute | solution.py:348
  29.9 11.6 %shard_map.84.right_ref = f32[512,512]{1,0:T(8,128)} custom-call(bf16[512,8192]{1,0:T(8,128)(2,1)} %tokens_ref.9, bf16[8192,1024]{1,0:T(8,128)(2,1)} %weight_ref.3), custom_call_target="tpu_custom_call" | custom-call | flops 4294967296 | bytes 17825792 | tf_op jit(solution)/shard_map/pallas_call | solution.py:146
  41.5 0.0 collective-permute-done.2.refs_0_
  41.5 2.1 %collective-permute-start.5 = (bf16[2304,128]{1,0:T(8,128)(2,1)}, bf16[2304,128]{1,0:T(8,128)(2,1)}, u32[]{:S(2)}, u32[]{:S(2)}) collective-permute-start(bf16[2304,128]{1,0:T(8,128)(2,1)} %shard_map.82.refs_0_), channel_id=1, source_target_pairs={{0,8},{1,9},{2,10},{3,11},{4,0},{5,1},{6,2},{7,3},{8,12},{9,13},{1... | collective-permute-start | bytes 1769480 | tf_op jit(solution)/shard_map/ppermute | solution.py:348
  43.7 0.0 collective-permute-done.6.refs_1_
  43.7 0.5 collective-permute-start.7
  44.2 0.0 collective-permute-done.8.refs_1_
  44.2 0.9 collective-permute-start.9
  45.1 1.0 copy.18.row_slot_ref
  46.1 3.0 %shard_map.85.refs_0_ = bf16[2304,128]{1,0:T(8,128)(2,1)} custom-call(s32[34]{0:T(128)} %dynamic-slice_bitcast_fusion.info_ref, bf16[4,16,8192]{2,1,0:T(8,128)(2,1)} %here_ref.3, bf16[4,16,8192]{2,1,0:T(8,128)(2,1)} %collective-permute-done.there_ref, bf16[4,16,1024]{2,1,0:T(8,128)(2,1)} %up_ref.3), custom_call_target="tpu_custom_call" | custom-call | tf_op jit(solution)/shard_map/pallas_call | solution.py:117
  49.1 0.0 collective-permute-done.10.other_ref
  49.2 6.7 %shard_map.86 = (f32[512,128]{1,0:T(8,128)}, f32[512,128]{1,0:T(8,128)}, bf16[96,1024]{1,0:T(8,128)(2,1)}) custom-call(s32[34]{0:T(128)} %dynamic-slice_bitcast_fusion.info_ref, s32[1024,1]{1,0:T(8,128)} %copy.18.row_slot_ref, s32[1,2048]{1,0:T(1,128)} %constant_dynamic-slice_fusion.column_slot_ref, bf16[512,8192]{1,0:T(8,128)(2,1)} %tokens_ref.9, ...), custom_call_target="tpu_custom_call" | custom-call | flops 1610612736 | bytes 5963776 | tf_op jit(solution)/shard_map/pallas_call | solution.py:252
  55.9 3.0 %collective-permute-done.5.refs_2_ = bf16[2304,128]{1,0:T(8,128)(2,1)} collective-permute-done((bf16[2304,128]{1,0:T(8,128)(2,1)}, bf16[2304,128]{1,0:T(8,128)(2,1)}, u32[]{:S(2)}, u32[]{:S(2)}) %collective-permute-start.5) | collective-permute-done | bytes 589856 | tf_op jit(solution)/shard_map/ppermute | solution.py:348
  58.9 2.6 %collective-permute-start.12 = (bf16[2304,128]{1,0:T(8,128)(2,1)}, bf16[2304,128]{1,0:T(8,128)(2,1)}, u32[]{:S(2)}, u32[]{:S(2)}) collective-permute-start(bf16[2304,128]{1,0:T(8,128)(2,1)} %shard_map.85.refs_0_), channel_id=1, source_target_pairs={{0,4},{1,5},{2,6},{3,7},{4,12},{5,13},{6,14},{7,15},{8,0},{9,1},{1... | collective-permute-start | bytes 1769480 | tf_op jit(solution)/shard_map/ppermute | solution.py:348
  61.5 0.0 collective-permute-done.7.refs_3_
  61.5 0.5 collective-permute-start.13
  62.1 0.0 collective-permute-done.9.refs_2_
  62.1 0.5 collective-permute-start.14
  62.6 0.0 collective-permute-start.15
  62.6 7.3 %shard_map.87 = (f32[512,128]{1,0:T(8,128)}, f32[512,128]{1,0:T(8,128)}, bf16[128,1024]{1,0:T(8,128)(2,1)}) custom-call(s32[34]{0:T(128)} %dynamic-slice_bitcast_fusion.info_ref, s32[1024,1]{1,0:T(8,128)} %copy.18.row_slot_ref, s32[1,2048]{1,0:T(1,128)} %constant_dynamic-slice_fusion.column_slot_ref, bf16[512,8192]{1,0:T(8,128)(2,1)} %tokens_ref.9, ...), custom_call_target="tpu_custom_call" | custom-call | flops 2147483648 | bytes 6553600 | tf_op jit(solution)/shard_map/pallas_call | solution.py:252
  69.9 5.1 %collective-permute-done.12.refs_3_ = bf16[2304,128]{1,0:T(8,128)(2,1)} collective-permute-done((bf16[2304,128]{1,0:T(8,128)(2,1)}, bf16[2304,128]{1,0:T(8,128)(2,1)}, u32[]{:S(2)}, u32[]{:S(2)}) %collective-permute-start.12) | collective-permute-done | bytes 589856 | tf_op jit(solution)/shard_map/ppermute | solution.py:348
  75.0 0.2 collective-permute-start.17
  75.2 1.0 collective-permute-done.13.refs_4_
  76.2 0.5 collective-permute-start.18
  76.7 0.0 collective-permute-done.14.refs_0_
  76.7 0.5 collective-permute-start.19
  77.2 0.0 collective-permute-done.15.refs_1_
  77.2 0.0 copy-start.3
  77.2 11.2 %shard_map.88 = (f32[512,128]{1,0:T(8,128)}, f32[512,128]{1,0:T(8,128)}, bf16[160,1024]{1,0:T(8,128)(2,1)}) custom-call(s32[34]{0:T(128)} %dynamic-slice_bitcast_fusion.info_ref, s32[1024,1]{1,0:T(8,128)} %copy.18.row_slot_ref, s32[1,2048]{1,0:T(1,128)} %constant_dynamic-slice_fusion.column_slot_ref, bf16[512,8192]{1,0:T(8,128)(2,1)} %tokens_ref.9, ...), custom_call_target="tpu_custom_call" | custom-call | flops 2684354560 | bytes 11337728 | tf_op jit(solution)/shard_map/pallas_call | solution.py:252
  88.4 0.0 copy-done.3
  88.4 0.1 collective-permute-start.16
  88.5 0.5 collective-permute-start.11
  89.0 1.7 %collective-permute-done.11.refs_3_ = bf16[128,1024]{1,0:T(8,128)(2,1)S(1)} collective-permute-done((bf16[128,1024]{1,0:T(8,128)(2,1)}, bf16[128,1024]{1,0:T(8,128)(2,1)S(1)}, u32[]{:S(2)}, u32[]{:S(2)}) %collective-permute-start.11) | collective-permute-done | bytes 262176 | tf_op jit(solution)/shard_map/ppermute | solution.py:348
  90.7 0.0 copy-start.1
  90.7 0.0 collective-permute-done.16.refs_5_
  90.7 0.7 copy-done.1
  91.4 0.0 collective-permute-done.17.refs_1_
  91.4 0.0 collective-permute-done.18.refs_2_
  91.4 0.0 collective-permute-done.19.refs_3_
  91.5 7.4 %shard_map.89 = (f32[512,128]{1,0:T(8,128)}, f32[512,128]{1,0:T(8,128)}, bf16[128,1024]{1,0:T(8,128)(2,1)}) custom-call(s32[34]{0:T(128)} %dynamic-slice_bitcast_fusion.info_ref, s32[1024,1]{1,0:T(8,128)} %copy.18.row_slot_ref, s32[1,2048]{1,0:T(1,128)} %constant_dynamic-slice_fusion.column_slot_ref, bf16[512,8192]{1,0:T(8,128)(2,1)} %tokens_ref.9, ...), custom_call_target="tpu_custom_call" | custom-call | flops 2147483648 | bytes 6553600 | tf_op jit(solution)/shard_map/pallas_call | solution.py:252
  98.8 0.0 copy-done
  98.9 0.2 collective-permute-start.20
  99.1 0.4 collective-permute-start.21
  99.4 0.9 copy.21.row_slot_ref
  100.3 0.4 collective-permute-done.20.theirs_ref
  100.7 0.5 collective-permute-done.21.refs_7_
  101.2 0.2 copy-done.2
  101.4 6.8 %shard_map.90 = bf16[512,1024]{1,0:T(8,128)(2,1)} custom-call(s32[34]{0:T(128)} %dynamic-slice_bitcast_fusion.info_ref, s32[512,1]{1,0:T(8,128)} %copy.21.row_slot_ref, f32[512,128]{1,0:T(8,128)} %get-tuple-element.72.mine_ref, f32[512,128]{1,0:T(8,128)} %copy-done.2, f32[512,512]{1,0:T(8,128)} %shard_map.83.left_ref, f32[512,512]{1,0:T(8,128)} %shard_map.84.right_ref, ...), custom_call_target="tpu_custom_call" | custom-call | flops 2147483648 | bytes 5242880 | tf_op jit(solution)/shard_map/pallas_call | solution.py:309
  (3 shorter events, 0.0 us)
Async XLA Ops:
  0.0 4.0 %collective-permute-start = (bf16[4,16,8192]{2,1,0:T(8,128)(2,1)}, bf16[4,16,8192]{2,1,0:T(8,128)(2,1)}, u32[]{:S(2)}, u32[]{:S(2)}) collective-permute-start(bf16[4,16,8192]{2,1,0:T(8,128)(2,1)} %here_ref.3), channel_id=1, source_target_pairs={{0,1},{1,0},{2,3},{3,2},{4,5},{5,4},{6,7},{7,6},{8,9},{9,8},{10,11... | collective-permute-start | bytes 3145736 | tf_op jit(solution)/shard_map/ppermute | solution.py:348
  4.0 45.2 %collective-permute-start.10 = (bf16[512,8192]{1,0:T(8,128)(2,1)}, bf16[512,8192]{1,0:T(8,128)(2,1)}, u32[]{:S(2)}, u32[]{:S(2)}) collective-permute-start(bf16[512,8192]{1,0:T(8,128)(2,1)} %tokens_ref.9), channel_id=1, source_target_pairs={{0,1},{1,0},{2,3},{3,2},{4,5},{5,4},{6,7},{7,6},{8,9},{9,8},{10,11... | collective-permute-start | bytes 25165832 | tf_op jit(solution)/shard_map/ppermute | solution.py:348
  7.0 17.9 %collective-permute-start.1 = (bf16[2304,128]{1,0:T(8,128)(2,1)}, bf16[2304,128]{1,0:T(8,128)(2,1)}, u32[]{:S(2)}, u32[]{:S(2)}) collective-permute-start(bf16[2304,128]{1,0:T(8,128)(2,1)} %shard_map.82.refs_0_), channel_id=1, source_target_pairs={{0,4},{1,5},{2,6},{3,7},{4,12},{5,13},{6,14},{7,15},{8,0},{9,1},{1... | collective-permute-start | bytes 1769480 | tf_op jit(solution)/shard_map/ppermute | solution.py:348
  10.1 15.8 %collective-permute-start.3 = (bf16[2304,128]{1,0:T(8,128)(2,1)}, bf16[2304,128]{1,0:T(8,128)(2,1)}, u32[]{:S(2)}, u32[]{:S(2)}) collective-permute-start(bf16[2304,128]{1,0:T(8,128)(2,1)} %shard_map.82.refs_0_), channel_id=1, source_target_pairs={{0,2},{1,3},{2,0},{3,1},{4,6},{5,7},{6,4},{7,5},{8,10},{9,11},{10,... | collective-permute-start | bytes 1769480 | tf_op jit(solution)/shard_map/ppermute | solution.py:348
  24.9 16.6 %collective-permute-start.2 = (bf16[2304,128]{1,0:T(8,128)(2,1)}, bf16[2304,128]{1,0:T(8,128)(2,1)}, u32[]{:S(2)}, u32[]{:S(2)}) collective-permute-start(bf16[2304,128]{1,0:T(8,128)(2,1)} %collective-permute-done.1.refs_1_), channel_id=1, source_target_pairs={{0,4},{1,5},{2,6},{3,7},{4,12},{5,13},{6,14},{7,15},{8,0},{9,1},{1... | collective-permute-start | bytes 1769480 | tf_op jit(solution)/shard_map/ppermute | solution.py:348
  25.9 17.8 %collective-permute-start.6 = (bf16[2304,128]{1,0:T(8,128)(2,1)}, bf16[2304,128]{1,0:T(8,128)(2,1)}, u32[]{:S(2)}, u32[]{:S(2)}) collective-permute-start(bf16[2304,128]{1,0:T(8,128)(2,1)} %collective-permute-done.1.refs_1_), channel_id=1, source_target_pairs={{0,2},{1,3},{2,0},{3,1},{4,6},{5,7},{6,4},{7,5},{8,10},{9,11},{10,... | collective-permute-start | bytes 1769480 | tf_op jit(solution)/shard_map/ppermute | solution.py:348
  27.2 17.0 %collective-permute-start.8 = (bf16[2304,128]{1,0:T(8,128)(2,1)}, bf16[2304,128]{1,0:T(8,128)(2,1)}, u32[]{:S(2)}, u32[]{:S(2)}) collective-permute-start(bf16[2304,128]{1,0:T(8,128)(2,1)} %collective-permute-done.3.refs_2_), channel_id=1, source_target_pairs={{0,16},{1,17},{2,18},{3,19},{4,20},{5,21},{6,22},{7,23},{8,24},{9,... | collective-permute-start | bytes 1769480 | tf_op jit(solution)/shard_map/ppermute | solution.py:348
  28.8 1.2 %collective-permute-start.4 = (s32[512]{0:T(512)S(1)}, s32[512]{0:T(512)S(1)}, u32[]{:S(2)}, u32[]{:S(2)}) collective-permute-start(s32[512]{0:T(512)S(1)} %select_reduce_fusion), channel_id=1, source_target_pairs={{0,1},{1,0},{2,3},{3,2},{4,5},{5,4},{6,7},{7,6},{8,9},{9,8},{10,11... | collective-permute-start | bytes 6152 | tf_op jit(solution)/shard_map/ppermute | solution.py:348
  41.5 17.4 %collective-permute-start.5 = (bf16[2304,128]{1,0:T(8,128)(2,1)}, bf16[2304,128]{1,0:T(8,128)(2,1)}, u32[]{:S(2)}, u32[]{:S(2)}) collective-permute-start(bf16[2304,128]{1,0:T(8,128)(2,1)} %shard_map.82.refs_0_), channel_id=1, source_target_pairs={{0,8},{1,9},{2,10},{3,11},{4,0},{5,1},{6,2},{7,3},{8,12},{9,13},{1... | collective-permute-start | bytes 1769480 | tf_op jit(solution)/shard_map/ppermute | solution.py:348
  43.7 17.9 %collective-permute-start.7 = (bf16[2304,128]{1,0:T(8,128)(2,1)}, bf16[2304,128]{1,0:T(8,128)(2,1)}, u32[]{:S(2)}, u32[]{:S(2)}) collective-permute-start(bf16[2304,128]{1,0:T(8,128)(2,1)} %collective-permute-done.2.refs_0_), channel_id=1, source_target_pairs={{0,2},{1,3},{2,0},{3,1},{4,6},{5,7},{6,4},{7,5},{8,10},{9,11},{10,... | collective-permute-start | bytes 1769480 | tf_op jit(solution)/shard_map/ppermute | solution.py:348
  44.2 17.9 %collective-permute-start.9 = (bf16[2304,128]{1,0:T(8,128)(2,1)}, bf16[2304,128]{1,0:T(8,128)(2,1)}, u32[]{:S(2)}, u32[]{:S(2)}) collective-permute-start(bf16[2304,128]{1,0:T(8,128)(2,1)} %collective-permute-done.2.refs_0_), channel_id=1, source_target_pairs={{0,16},{1,17},{2,18},{3,19},{4,20},{5,21},{6,22},{7,23},{8,24},{9,... | collective-permute-start | bytes 1769480 | tf_op jit(solution)/shard_map/ppermute | solution.py:348
  58.9 16.1 %collective-permute-start.12 = (bf16[2304,128]{1,0:T(8,128)(2,1)}, bf16[2304,128]{1,0:T(8,128)(2,1)}, u32[]{:S(2)}, u32[]{:S(2)}) collective-permute-start(bf16[2304,128]{1,0:T(8,128)(2,1)} %shard_map.85.refs_0_), channel_id=1, source_target_pairs={{0,4},{1,5},{2,6},{3,7},{4,12},{5,13},{6,14},{7,15},{8,0},{9,1},{1... | collective-permute-start | bytes 1769480 | tf_op jit(solution)/shard_map/ppermute | solution.py:348
  61.5 14.6 %collective-permute-start.13 = (bf16[2304,128]{1,0:T(8,128)(2,1)}, bf16[2304,128]{1,0:T(8,128)(2,1)}, u32[]{:S(2)}, u32[]{:S(2)}) collective-permute-start(bf16[2304,128]{1,0:T(8,128)(2,1)} %collective-permute-done.5.refs_2_), channel_id=1, source_target_pairs={{0,2},{1,3},{2,0},{3,1},{4,6},{5,7},{6,4},{7,5},{8,10},{9,11},{10,... | collective-permute-start | bytes 1769480 | tf_op jit(solution)/shard_map/ppermute | solution.py:348
  62.1 14.6 %collective-permute-start.14 = (bf16[2304,128]{1,0:T(8,128)(2,1)}, bf16[2304,128]{1,0:T(8,128)(2,1)}, u32[]{:S(2)}, u32[]{:S(2)}) collective-permute-start(bf16[2304,128]{1,0:T(8,128)(2,1)} %collective-permute-done.6.refs_1_), channel_id=1, source_target_pairs={{0,16},{1,17},{2,18},{3,19},{4,20},{5,21},{6,22},{7,23},{8,24},{9,... | collective-permute-start | bytes 1769480 | tf_op jit(solution)/shard_map/ppermute | solution.py:348
  62.6 14.6 %collective-permute-start.15 = (bf16[96,1024]{1,0:T(8,128)(2,1)}, bf16[96,1024]{1,0:T(8,128)(2,1)S(1)}, u32[]{:S(2)}, u32[]{:S(2)}) collective-permute-start(bf16[96,1024]{1,0:T(8,128)(2,1)} %get-tuple-element.61.refs_0_), channel_id=1, source_target_pairs={{0,1},{1,0},{2,3},{3,2},{4,5},{5,4},{6,7},{7,6},{8,9},{9,8},{10,11... | collective-permute-start | bytes 589832 | tf_op jit(solution)/shard_map/ppermute | solution.py:348
  75.0 16.4 %collective-permute-start.17 = (bf16[2304,128]{1,0:T(8,128)(2,1)}, bf16[2304,128]{1,0:T(8,128)(2,1)}, u32[]{:S(2)}, u32[]{:S(2)}) collective-permute-start(bf16[2304,128]{1,0:T(8,128)(2,1)} %shard_map.85.refs_0_), channel_id=1, source_target_pairs={{0,8},{1,9},{2,10},{3,11},{4,0},{5,1},{6,2},{7,3},{8,12},{9,13},{1... | collective-permute-start | bytes 1769480 | tf_op jit(solution)/shard_map/ppermute | solution.py:348
  76.2 15.3 %collective-permute-start.18 = (bf16[2304,128]{1,0:T(8,128)(2,1)}, bf16[2304,128]{1,0:T(8,128)(2,1)}, u32[]{:S(2)}, u32[]{:S(2)}) collective-permute-start(bf16[2304,128]{1,0:T(8,128)(2,1)} %collective-permute-done.9.refs_2_), channel_id=1, source_target_pairs={{0,2},{1,3},{2,0},{3,1},{4,6},{5,7},{6,4},{7,5},{8,10},{9,11},{10,... | collective-permute-start | bytes 1769480 | tf_op jit(solution)/shard_map/ppermute | solution.py:348
  76.7 14.7 %collective-permute-start.19 = (bf16[2304,128]{1,0:T(8,128)(2,1)}, bf16[2304,128]{1,0:T(8,128)(2,1)}, u32[]{:S(2)}, u32[]{:S(2)}) collective-permute-start(bf16[2304,128]{1,0:T(8,128)(2,1)} %collective-permute-done.13.refs_4_), channel_id=1, source_target_pairs={{0,16},{1,17},{2,18},{3,19},{4,20},{5,21},{6,22},{7,23},{8,24},{9,... | collective-permute-start | bytes 1769480 | tf_op jit(solution)/shard_map/ppermute | solution.py:348
  77.2 11.2 %copy-start.3 = (bf16[96,1024]{1,0:T(8,128)(2,1)}, bf16[96,1024]{1,0:T(8,128)(2,1)S(1)}, u32[]{:S(2)}) copy-start(bf16[96,1024]{1,0:T(8,128)(2,1)S(1)} %collective-permute-done.15.refs_1_) | copy-start | bytes 589828
  88.4 2.3 %collective-permute-start.16 = (bf16[160,1024]{1,0:T(8,128)(2,1)}, bf16[160,1024]{1,0:T(8,128)(2,1)S(1)}, u32[]{:S(2)}, u32[]{:S(2)}) collective-permute-start(bf16[160,1024]{1,0:T(8,128)(2,1)} %get-tuple-element.65.refs_4_), channel_id=1, source_target_pairs={{0,1},{1,0},{2,3},{3,2},{4,5},{5,4},{6,7},{7,6},{8,9},{9,8},{10,11... | collective-permute-start | bytes 983048 | tf_op jit(solution)/shard_map/ppermute | solution.py:348
  88.5 2.2 %collective-permute-start.11 = (bf16[128,1024]{1,0:T(8,128)(2,1)}, bf16[128,1024]{1,0:T(8,128)(2,1)S(1)}, u32[]{:S(2)}, u32[]{:S(2)}) collective-permute-start(bf16[128,1024]{1,0:T(8,128)(2,1)} %get-tuple-element.57.refs_2_), channel_id=1, source_target_pairs={{0,1},{1,0},{2,3},{3,2},{4,5},{5,4},{6,7},{7,6},{8,9},{9,8},{10,11... | collective-permute-start | bytes 786440 | tf_op jit(solution)/shard_map/ppermute | solution.py:348
  90.7 0.7 copy-start.1
  91.4 7.4 %copy-start = (bf16[160,1024]{1,0:T(8,128)(2,1)}, bf16[160,1024]{1,0:T(8,128)(2,1)S(1)}, u32[]{:S(2)}) copy-start(bf16[160,1024]{1,0:T(8,128)(2,1)S(1)} %collective-permute-done.16.refs_5_) | copy-start | bytes 983044
  98.9 1.8 %collective-permute-start.20 = (f32[512,128]{1,0:T(8,128)}, f32[512,128]{1,0:T(8,128)S(1)}, u32[]{:S(2)}, u32[]{:S(2)}) collective-permute-start(f32[512,128]{1,0:T(8,128)} %get-tuple-element.73), channel_id=1, source_target_pairs={{0,1},{1,0},{2,3},{3,2},{4,5},{5,4},{6,7},{7,6},{8,9},{9,8},{10,11... | collective-permute-start | bytes 786440 | tf_op jit(solution)/shard_map/ppermute | solution.py:348
  99.1 2.1 %collective-permute-start.21 = (bf16[128,1024]{1,0:T(8,128)(2,1)}, bf16[128,1024]{1,0:T(8,128)(2,1)}, u32[]{:S(2)}, u32[]{:S(2)}) collective-permute-start(bf16[128,1024]{1,0:T(8,128)(2,1)} %get-tuple-element.74.refs_6_), channel_id=1, source_target_pairs={{0,1},{1,0},{2,3},{3,2},{4,5},{5,4},{6,7},{7,6},{8,9},{9,8},{10,11... | collective-permute-start | bytes 786440 | tf_op jit(solution)/shard_map/ppermute | solution.py:348
  100.7 0.7 copy-start.2

commit v9 on v8

--- a/solution.py
+++ b/solution.py
@@ -15,12 +15,12 @@
 RANK = 16
 
 PIECES = (
-    *((0, 0, 0), (1, 0, 0), (0, 1, 0)),
-    *((2, 0, 0), (1, 1, 0), (3, 0, 0), (2, 1, 0)),
-    *((0, 0, 1), (0, 1, 1), (2, 0, 1), (1, 0, 1), (3, 1, 0)),
+    *((0, 0, 0), (1, 0, 0), (0, 1, 0), (2, 0, 0)),
+    *((1, 1, 0), (3, 0, 0), (2, 1, 0), (3, 1, 0)),
+    *((0, 0, 1), (0, 1, 1), (2, 0, 1), (1, 0, 1)),
     *((1, 1, 1), (3, 0, 1), (2, 1, 1), (3, 1, 1)),
 )
-KERNEL_BOUNDS = (0, 3, 7, 12, 16)
+KERNEL_BOUNDS = (0, 4, 12, 16)
 QUARTER_CUTS = (0, 512, 1024, 2048)
 VMEM_BYTES = 64 * 1024 * 1024 - 512 * 1024
 
@@ -127,38 +127,56 @@
     )(info, here, there, up)
 
 
-def base_kernel(tokens_ref, weight_ref, out_ref):
+def base_kernel(steps, tokens_ref, weight_ref, *refs):
     step = pl.program_id(0)
+    more = len(refs) > 1
+    out_ref = refs[1] if more else refs[0]
+    copies = [pltpu.make_async_copy(refs[0], refs[2], refs[3].at[0])] if more else []
     part = jnp.dot(tokens_ref[...], weight_ref[...], preferred_element_type=jnp.float32)
 
     @pl.when(step == 0)
     def _():
+        started(copies)
         out_ref[...] = part
 
     @pl.when(step > 0)
     def _():
         out_ref[...] += part
 
-
-def base_half(tokens, weight, half):
+    if more:
+
+        @pl.when(step == steps - 1)
+        def _():
+            awaited(copies)
+            out_ref[...] += refs[2][...]
+
+
+def base_part(tokens, weight, begin, end, total=None):
     rows, depth = tokens.shape
-    width = weight.shape[1] // 2
+    width = weight.shape[1]
+    steps, first = (end - begin) // DEPTH_TILE, begin // DEPTH_TILE
+    result = jax.ShapeDtypeStruct((rows, width), jnp.float32)
+    more = total is not None
     return pl.pallas_call(
-        base_kernel,
-        out_shape=jax.ShapeDtypeStruct((rows, width), jnp.float32),
-        grid=(depth // DEPTH_TILE,),
+        functools.partial(base_kernel, steps),
+        out_shape=result,
+        grid=(steps,),
         in_specs=[
-            pl.BlockSpec((rows, DEPTH_TILE), lambda k: (0, k)),
-            pl.BlockSpec((DEPTH_TILE, width), lambda k: (k, half)),
-        ],
+            pl.BlockSpec((rows, DEPTH_TILE), lambda k: (0, first + k)),
+            pl.BlockSpec((DEPTH_TILE, width), lambda k: (first + k, 0)),
+        ]
+        + [pl.BlockSpec(memory_space=pl.ANY)] * more,
         out_specs=pl.BlockSpec((rows, width), lambda k: (0, 0)),
+        scratch_shapes=[pltpu.VMEM((rows, width), jnp.float32), pltpu.SemaphoreType.DMA((1,))]
+        if more
+        else [],
         cost_estimate=pl.CostEstimate(
-            flops=2 * rows * width * depth,
-            bytes_accessed=2 * (rows + width) * depth + 4 * rows * width,
+            flops=2 * rows * width * (end - begin),
+            bytes_accessed=2 * (rows + width) * (end - begin) + 4 * rows * width,
             transcendentals=0,
         ),
         compiler_params=params(),
-    )(tokens, weight)
+    )(tokens, weight, *([total] if more else []))
 
 
 def absorb_kernel(
@@ -269,19 +287,15 @@
 
 
 def finish_kernel(
-    count, info_ref, row_slot_ref, mine_ref, theirs_ref, left_ref, right_ref, *refs
+    count, info_ref, row_slot_ref, mine_ref, theirs_ref, total_ref, *refs
 ):
     sources, (out_ref, total, up, sems) = refs[:count], refs[count:]
     rows = out_ref.shape[0]
     height = up.shape[0] // (len(PIECES) * 2)
-    half = left_ref.shape[1]
-    copies = [
-        pltpu.make_async_copy(source, total.at[:, pl.ds(n * half, half)], sems.at[n])
-        for n, source in enumerate((left_ref, right_ref))
-    ]
+    copies = [pltpu.make_async_copy(total_ref, total, sems.at[0])]
     for source in sources:
         for n in range(0, source.shape[0], height):
-            first = pl.multiple_of(info_ref[len(copies)], height)
+            first = pl.multiple_of(info_ref[1 + len(copies)], height)
             copies.append(
                 pltpu.make_async_copy(
                     source.at[pl.ds(n, height)], up.at[pl.ds(first, height)], sems.at[len(copies)]
@@ -301,8 +315,8 @@
     out_ref[...] = (total[...] + (lora[:rows] + lora[rows:])).astype(out_ref.dtype)
 
 
-def finish(info, row_slot, mine, theirs, left, right, ups):
-    rows, width = left.shape[0], 2 * left.shape[1]
+def finish(info, row_slot, mine, theirs, total, ups):
+    rows, width = total.shape
     anywhere = pl.BlockSpec(memory_space=pl.ANY)
     vmem = pl.BlockSpec(memory_space=pltpu.VMEM)
     up_rows = sum(up.shape[0] for up in ups)
@@ -310,12 +324,12 @@
         functools.partial(finish_kernel, len(ups)),
         out_shape=jax.ShapeDtypeStruct((rows, width), jnp.bfloat16),
         in_specs=[pl.BlockSpec(memory_space=pltpu.SMEM), vmem, vmem, vmem]
-        + [anywhere] * (2 + len(ups)),
+        + [anywhere] * (1 + len(ups)),
         out_specs=vmem,
         scratch_shapes=[
             pltpu.VMEM((rows, width), jnp.float32),
             pltpu.VMEM((up_rows, width), ups[0].dtype),
-            pltpu.SemaphoreType.DMA((2 + 2 * len(PIECES),)),
+            pltpu.SemaphoreType.DMA((1 + 2 * len(PIECES),)),
         ],
         cost_estimate=pl.CostEstimate(
             flops=4 * rows * width * up_rows,
@@ -323,7 +337,7 @@
             transcendentals=0,
         ),
         compiler_params=params(),
-    )(info, row_slot, mine, theirs, left, right, *ups)
+    )(info, row_slot, mine, theirs, total, *ups)
 
 
 def passed_round(
@@ -376,10 +390,9 @@
                     for p in pieces
                 ]
             )
-    here_of = lambda table: lax.dynamic_index_in_dim(
-        jnp.array(np.array(table, np.int32)), device, 0, keepdims=False
-    )
-    info, column_slots = here_of(info_table), here_of(column_table)[None, :]
+    here_of = lambda table, which: lax.dynamic_index_in_dim(
+        jnp.array(np.array(table, np.int32)), which, 0, keepdims=False
+    )
 
     def together(*values):
         return lax.optimization_barrier(values)
@@ -388,28 +401,31 @@
         return lax.optimization_barrier((value, *others))[0]
 
     there = core_swap(adapter_down_weight)
-    row_slot = slots_of_rows(row_adapter_index, adapter_storage_slot)
-    there, tokens_late, info, row_slot, column_slots = together(
-        there, tokens, info, row_slot, column_slots
-    )
+    at = jnp.stack([lax.axis_index("groups"), lax.axis_index("req") % 2])
+    there, at, tokens_late = together(there, at, tokens)
 
     def piece(back, *others):
         return assemble(
-            back, after(info, *others), adapter_down_weight, there, adapter_up_weight
+            back, after(at, *others), adapter_down_weight, there, adapter_up_weight
         )
 
     front = piece(0)
 
     z1, x0 = z_ring(front), x_swap(front)
     other = core_swap(tokens_late)
+    row_index = after(row_adapter_index, front)
+    row_slot = slots_of_rows(row_index, adapter_storage_slot)
     other_slot = core_swap(row_slot[:, 0])
-    left = base_half(after(tokens, front), base_value_weight, 0)
+    device = after(device, front)
+    info, column_slots = here_of(info_table, device), here_of(column_table, device)[None, :]
+    total = base_part(after(tokens, front), base_value_weight, 0, depth // 2)
     row_slots = jnp.concatenate([row_slot, other_slot[:, None]], axis=0)
 
-    z2 = z_ring(after(z1, left))
-    x1 = x_swap(after(z1, x0, left))
-    yx0 = y_swap(after(x0, left))
-    right = base_half(after(tokens, z1, x0, left, row_slots), base_value_weight, 1)
+    z2 = z_ring(after(z1, total))
+    x1 = x_swap(after(z1, x0, total))
+    yx0 = y_swap(after(x0, total))
+    tokens_late = after(tokens, z1, x0, total, row_slots, info, column_slots)
+    total = base_part(tokens_late, base_value_weight, depth // 2, depth, total)
     ups = []
 
     def update(number, groups, before, *others):
@@ -427,24 +443,25 @@
         ups.extend([up, core_swap(up)])
         return mine, others
 
-    z3 = z_back(after(front, z2, right))
-    x2 = x_swap(after(z2, x1, right))
-    yz2 = y_swap(after(z2, yx0, right))
-    state = update(0, [((front, z1, x0), 0)], None, z2, x1, yx0, right)
-    back = piece(1, z2, x1, yx0, right)
+    z3 = z_back(after(front, z2, total))
+    x2 = x_swap(after(z2, x1, total))
+    yz2 = y_swap(after(z2, yx0, total))
+    state = update(0, [((front, z1, x0, z2), 0)], None, x1, yx0, total)
+    back = piece(1, z2, x1, yx0, total)
 
     zb1 = z_ring(after(back, z3, state[0]))
     x3 = x_swap(after(z3, x2, state[0]))
     yx1 = y_swap(after(x1, yz2, state[0]))
-    state = update(1, [((z2, x1, z3, x2), 0)], state, z3, x2, yz2, back)
-
-    zb3 = z_back(after(back, zb1, state[0]))
-    xyz2 = x_swap(after(yz2, x3, state[0]))
-    yx3 = y_swap(after(x3, yx1, state[0]))
-    state = update(2, [((back, yx0, yz2, zb1), 1), ((x3,), 0)], state, zb1, x3, yx1, ups[1])
-
-    mine, others = update(3, [((yx1, zb3, xyz2, yx3), 1)], state, ups[3], ups[5])
-    return finish(info, row_slot, mine, core_swap(others), left, right, ups)
+
+    zb3 = z_back(after(back, zb1))
+    xyz2 = x_swap(after(yz2, x3))
+    yx3 = y_swap(after(x3, yx1))
+    state = update(
+        1, [((x1, z3, x2, x3), 0), ((back, yx0, yz2, zb1), 1)], state, yx1, ups[1]
+    )
+
+    mine, others = update(2, [((yx1, zb3, xyz2, yx3), 1)], state, ups[3])
+    return finish(info, row_slot, mine, core_swap(others), total, ups)
 
 
 def solution(mesh):

time: 109 us -> 117 us (1.073)
  the two profiles are of different devices: /device:TPU:0 before, /device:TPU:17 now
where the time goes in v9:
time: 117 us
  Pallas kernels  57.4 us (49%)
  starting transfers between devices  36.8 us (31%)
  waiting for transfers between devices  15.9 us (14%)
  local copies, waits for them, and re-layouts  4.78 us (4%)
  other arithmetic  1.45 us (1%)
    ppermute x21, starting transfers between devices, permuted(): return lax.ppermute(array, axes, pairs)  36.8 us
    pallas_call x3, Pallas kernels, absorb(): pl.pallas_call(functools.partial(absorb_kernel, sizes, start, more), out_...  25.2 us
    pallas_call x2, Pallas kernels, base_part(): pl.pallas_call(functools.partial(base_kernel, steps), out_shape=result, g...  19.5 us
    ppermute x21, waiting for transfers between devices, permuted(): return lax.ppermute(array, axes, pairs)  15.9 us
    pallas_call x1, Pallas kernels, finish(): pl.pallas_call(functools.partial(finish_kernel, len(ups)), out_shape=jax....  6.78 us
    pallas_call x2, Pallas kernels, assemble(): pl.pallas_call(functools.partial(assemble_kernel, back), out_shape=jax.Sh...  5.94 us
  transfers between devices with their start and end apart: 21, of which 11 were waited for; matrix products, arithmetic and copies ran while one was open for 5% of the time, Pallas kernels for 37%

profile of v9, /device:TPU:17, one launch (start us, length us, event | category | flops | bytes accessed | tf_op | source)
XLA Modules:
  0.0 116.6 jit_solution(6714108593326893265)
XLA Ops:
  0.0 0.7 collective-permute-start
  0.7 0.7 pad_add_fusion.1.info_ref
  1.3 2.0 %collective-permute-done.there_ref = bf16[4,16,8192]{2,1,0:T(8,128)(2,1)} collective-permute-done((bf16[4,16,8192]{2,1,0:T(8,128)(2,1)}, bf16[4,16,8192]{2,1,0:T(8,128)(2,1)}, u32[]{:S(2)}, u32[]{:S(2)}) %collective-permute-start) | collective-permute-done | bytes 1048608 | tf_op jit(solution)/shard_map/ppermute | solution.py:362
  3.3 0.4 collective-permute-start.8
  3.7 3.0 %shard_map.82.refs_0_ = bf16[2304,128]{1,0:T(8,128)(2,1)} custom-call(s32[2]{0:T(128)} %pad_add_fusion.1.info_ref, bf16[4,16,8192]{2,1,0:T(8,128)(2,1)} %here_ref.3, bf16[4,16,8192]{2,1,0:T(8,128)(2,1)} %collective-permute-done.there_ref, bf16[4,16,1024]{2,1,0:T(8,128)(2,1)} %up_ref.3), custom_call_target="tpu_custom_call" | custom-call | tf_op jit(solution)/shard_map/pallas_call | solution.py:117
  6.7 0.1 collective-permute-start.1
  6.7 1.3 %collective-permute-start.2 = (bf16[2304,128]{1,0:T(8,128)(2,1)}, bf16[2304,128]{1,0:T(8,128)(2,1)}, u32[]{:S(2)}, u32[]{:S(2)}) collective-permute-start(bf16[2304,128]{1,0:T(8,128)(2,1)} %shard_map.82.refs_0_), channel_id=1, source_target_pairs={{0,2},{1,3},{2,0},{3,1},{4,6},{5,7},{6,4},{7,5},{8,10},{9,11},{10,... | collective-permute-start | bytes 1769480 | tf_op jit(solution)/shard_map/ppermute | solution.py:362
  8.0 0.8 select_reduce_fusion
  8.8 0.8 collective-permute-start.6
  9.5 1.4 %constant_dynamic-slice_fusion.column_slot_ref = s32[1,2048]{1,0:T(1,128)} fusion(s32[32,2048]{1,0:T(8,128)} %constant.39.clone, s32[]{:T(128)S(6)} %select_n.18), kind=kLoop, calls=%fused_computation.5 | loop fusion | bytes 16388 | tf_op jit(solution)/shard_map/jit(dynamic_index_in_dim)/dynamic_slice | solution.py:393
  11.0 9.6 %shard_map.83.refs_0_ = f32[512,1024]{1,0:T(8,128)} custom-call(bf16[512,8192]{1,0:T(8,128)(2,1)} %tokens_ref.7, bf16[8192,1024]{1,0:T(8,128)(2,1)} %weight_ref.3), custom_call_target="tpu_custom_call" | custom-call | flops 4294967296 | bytes 14680064 | tf_op jit(solution)/shard_map/pallas_call | solution.py:160
  20.6 1.2 %collective-permute-done.1.refs_1_ = bf16[2304,128]{1,0:T(8,128)(2,1)} collective-permute-done((bf16[2304,128]{1,0:T(8,128)(2,1)}, bf16[2304,128]{1,0:T(8,128)(2,1)}, u32[]{:S(2)}, u32[]{:S(2)}) %collective-permute-start.1) | collective-permute-done | bytes 589856 | tf_op jit(solution)/shard_map/ppermute | solution.py:362
  21.8 0.1 collective-permute-done.2.refs_2_
  21.9 1.1 collective-permute-start.3
  23.0 1.0 collective-permute-start.4
  24.1 1.2 %collective-permute-start.5 = (bf16[2304,128]{1,0:T(8,128)(2,1)}, bf16[2304,128]{1,0:T(8,128)(2,1)}, u32[]{:S(2)}, u32[]{:S(2)}) collective-permute-start(bf16[2304,128]{1,0:T(8,128)(2,1)} %collective-permute-done.2.refs_2_), channel_id=1, source_target_pairs={{0,16},{1,17},{2,18},{3,19},{4,20},{5,21},{6,22},{7,23},{8,24},{9,... | collective-permute-start | bytes 1769480 | tf_op jit(solution)/shard_map/ppermute | solution.py:362
  25.3 1.3 %dynamic-slice_bitcast_fusion.info_ref = s32[34]{0:T(128)} fusion(s32[32,34]{1,0:T(8,128)} %constant.38.clone, s32[]{:T(128)S(6)} %select_n.18), kind=kLoop, calls=%fused_computation.4 | loop fusion | bytes 276 | tf_op jit(solution)/shard_map/jit(dynamic_index_in_dim)/squeeze | solution.py:393
  26.6 0.0 collective-permute-done.6
  26.6 9.9 %shard_map.84.total_ref = f32[512,1024]{1,0:T(8,128)} custom-call(bf16[512,8192]{1,0:T(8,128)(2,1)} %tokens_ref.7, bf16[8192,1024]{1,0:T(8,128)(2,1)} %weight_ref.3, f32[512,1024]{1,0:T(8,128)} %shard_map.83.refs_0_), custom_call_target="tpu_custom_call" | custom-call | flops 4294967296 | bytes 14680064 | tf_op jit(solution)/shard_map/pallas_call | solution.py:160
  36.5 1.5 %collective-permute-done.4.refs_3_ = bf16[2304,128]{1,0:T(8,128)(2,1)} collective-permute-done((bf16[2304,128]{1,0:T(8,128)(2,1)}, bf16[2304,128]{1,0:T(8,128)(2,1)}, u32[]{:S(2)}, u32[]{:S(2)}) %collective-permute-start.4) | collective-permute-done | bytes 589856 | tf_op jit(solution)/shard_map/ppermute | solution.py:362
  38.0 0.0 collective-permute-done.5.refs_5_
  38.0 1.2 %collective-permute-start.7 = (bf16[2304,128]{1,0:T(8,128)(2,1)}, bf16[2304,128]{1,0:T(8,128)(2,1)}, u32[]{:S(2)}, u32[]{:S(2)}) collective-permute-start(bf16[2304,128]{1,0:T(8,128)(2,1)} %collective-permute-done.4.refs_3_), channel_id=1, source_target_pairs={{0,16},{1,17},{2,18},{3,19},{4,20},{5,21},{6,22},{7,23},{8,24},{9,... | collective-permute-start | bytes 1769480 | tf_op jit(solution)/shard_map/ppermute | solution.py:362
  39.2 2.0 %collective-permute-start.11 = (bf16[2304,128]{1,0:T(8,128)(2,1)}, bf16[2304,128]{1,0:T(8,128)(2,1)}, u32[]{:S(2)}, u32[]{:S(2)}) collective-permute-start(bf16[2304,128]{1,0:T(8,128)(2,1)} %shard_map.82.refs_0_), channel_id=1, source_target_pairs={{0,8},{1,9},{2,10},{3,11},{4,0},{5,1},{6,2},{7,3},{8,12},{9,13},{1... | collective-permute-start | bytes 1769480 | tf_op jit(solution)/shard_map/ppermute | solution.py:362
  41.3 0.0 collective-permute-done.3.refs_0_
  41.3 0.3 collective-permute-start.12
  41.5 1.0 copy.16.row_slot_ref
  42.6 3.0 %shard_map.86.refs_4_ = bf16[2304,128]{1,0:T(8,128)(2,1)} custom-call(s32[2]{0:T(128)} %pad_add_fusion.1.info_ref, bf16[4,16,8192]{2,1,0:T(8,128)(2,1)} %here_ref.3, bf16[4,16,8192]{2,1,0:T(8,128)(2,1)} %collective-permute-done.there_ref, bf16[4,16,1024]{2,1,0:T(8,128)(2,1)} %up_ref.3), custom_call_target="tpu_custom_call" | custom-call | tf_op jit(solution)/shard_map/pallas_call | solution.py:117
  45.5 0.0 collective-permute-done.8.other_ref
  45.5 7.1 %shard_map.85 = (f32[512,128]{1,0:T(8,128)}, f32[512,128]{1,0:T(8,128)}, bf16[128,1024]{1,0:T(8,128)(2,1)}) custom-call(s32[34]{0:T(128)} %dynamic-slice_bitcast_fusion.info_ref, s32[1024,1]{1,0:T(8,128)} %copy.16.row_slot_ref, s32[1,2048]{1,0:T(1,128)} %constant_dynamic-slice_fusion.column_slot_ref, bf16[512,8192]{1,0:T(8,128)(2,1)} %tokens_ref.7, ...), custom_call_target="tpu_custom_call" | custom-call | flops 2147483648 | bytes 6553600 | tf_op jit(solution)/shard_map/pallas_call | solution.py:270
  52.6 0.0 collective-permute-done.7.refs_6_
  52.6 0.3 collective-permute-start.9
  52.9 0.0 collective-permute-done.11.refs_1_
  52.9 0.4 collective-permute-start.14
  53.3 0.4 collective-permute-done.12.refs_2_
  53.7 0.8 collective-permute-start.13
  54.5 3.8 %collective-permute-start.10 = (bf16[128,1024]{1,0:T(8,128)(2,1)}, bf16[128,1024]{1,0:T(8,128)(2,1)S(1)}, u32[]{:S(2)}, u32[]{:S(2)}) collective-permute-start(bf16[128,1024]{1,0:T(8,128)(2,1)} %get-tuple-element.51.refs_0_), channel_id=1, source_target_pairs={{0,1},{1,0},{2,3},{3,2},{4,5},{5,4},{6,7},{7,6},{8,9},{9,8},{10,11... | collective-permute-start | bytes 786440 | tf_op jit(solution)/shard_map/ppermute | solution.py:362
  58.3 1.4 %collective-permute-done.10.refs_1_ = bf16[128,1024]{1,0:T(8,128)(2,1)S(1)} collective-permute-done((bf16[128,1024]{1,0:T(8,128)(2,1)}, bf16[128,1024]{1,0:T(8,128)(2,1)S(1)}, u32[]{:S(2)}, u32[]{:S(2)}) %collective-permute-start.10) | collective-permute-done | bytes 262176 | tf_op jit(solution)/shard_map/ppermute | solution.py:362
  59.7 0.0 copy-start
  59.7 5.2 %collective-permute-done.9.refs_0_ = bf16[2304,128]{1,0:T(8,128)(2,1)} collective-permute-done((bf16[2304,128]{1,0:T(8,128)(2,1)}, bf16[2304,128]{1,0:T(8,128)(2,1)}, u32[]{:S(2)}, u32[]{:S(2)}) %collective-permute-start.9) | collective-permute-done | bytes 589856 | tf_op jit(solution)/shard_map/ppermute | solution.py:362
  64.8 1.3 %collective-permute-done.14.refs_7_ = bf16[2304,128]{1,0:T(8,128)(2,1)} collective-permute-done((bf16[2304,128]{1,0:T(8,128)(2,1)}, bf16[2304,128]{1,0:T(8,128)(2,1)}, u32[]{:S(2)}, u32[]{:S(2)}) %collective-permute-start.14) | collective-permute-done | bytes 589856 | tf_op jit(solution)/shard_map/ppermute | solution.py:362
  66.2 0.7 collective-permute-start.16
  66.9 0.0 collective-permute-done.13.refs_3_
  66.9 0.9 collective-permute-start.17
  67.8 1.3 %collective-permute-start.18 = (bf16[2304,128]{1,0:T(8,128)(2,1)}, bf16[2304,128]{1,0:T(8,128)(2,1)}, u32[]{:S(2)}, u32[]{:S(2)}) collective-permute-start(bf16[2304,128]{1,0:T(8,128)(2,1)} %collective-permute-done.13.refs_3_), channel_id=1, source_target_pairs={{0,16},{1,17},{2,18},{3,19},{4,20},{5,21},{6,22},{7,23},{8,24},{9,... | collective-permute-start | bytes 1769480 | tf_op jit(solution)/shard_map/ppermute | solution.py:362
  69.1 10.8 %shard_map.87 = (f32[512,128]{1,0:T(8,128)}, f32[512,128]{1,0:T(8,128)}, bf16[256,1024]{1,0:T(8,128)(2,1)}) custom-call(s32[34]{0:T(128)} %dynamic-slice_bitcast_fusion.info_ref, s32[1024,1]{1,0:T(8,128)} %copy.16.row_slot_ref, s32[1,2048]{1,0:T(1,128)} %constant_dynamic-slice_fusion.column_slot_ref, bf16[512,8192]{1,0:T(8,128)(2,1)} %tokens_ref.7, ...), custom_call_target="tpu_custom_call" | custom-call | flops 4294967296 | bytes 13107200 | tf_op jit(solution)/shard_map/pallas_call | solution.py:270
  79.9 0.0 copy-done
  79.9 18.0 %collective-permute-start.15 = (bf16[256,1024]{1,0:T(8,128)(2,1)}, bf16[256,1024]{1,0:T(8,128)(2,1)}, u32[]{:S(2)}, u32[]{:S(2)}) collective-permute-start(bf16[256,1024]{1,0:T(8,128)(2,1)} %get-tuple-element.59.refs_2_), channel_id=1, source_target_pairs={{0,1},{1,0},{2,3},{3,2},{4,5},{5,4},{6,7},{7,6},{8,9},{9,8},{10,11... | collective-permute-start | bytes 1572872 | tf_op jit(solution)/shard_map/ppermute | solution.py:362
  97.9 1.9 %collective-permute-done.15.refs_3_ = bf16[256,1024]{1,0:T(8,128)(2,1)} collective-permute-done((bf16[256,1024]{1,0:T(8,128)(2,1)}, bf16[256,1024]{1,0:T(8,128)(2,1)}, u32[]{:S(2)}, u32[]{:S(2)}) %collective-permute-start.15) | collective-permute-done | bytes 524320 | tf_op jit(solution)/shard_map/ppermute | solution.py:362
  99.8 0.0 collective-permute-done.16.refs_1_
  99.8 0.0 collective-permute-done.17.refs_2_
  99.8 0.0 collective-permute-done.18.refs_3_
  99.8 7.3 %shard_map.88 = (f32[512,128]{1,0:T(8,128)}, f32[512,128]{1,0:T(8,128)}, bf16[128,1024]{1,0:T(8,128)(2,1)}) custom-call(s32[34]{0:T(128)} %dynamic-slice_bitcast_fusion.info_ref, s32[1024,1]{1,0:T(8,128)} %copy.16.row_slot_ref, s32[1,2048]{1,0:T(1,128)} %constant_dynamic-slice_fusion.column_slot_ref, bf16[512,8192]{1,0:T(8,128)(2,1)} %tokens_ref.7, ...), custom_call_target="tpu_custom_call" | custom-call | flops 2147483648 | bytes 6553600 | tf_op jit(solution)/shard_map/pallas_call | solution.py:270
  107.1 0.4 collective-permute-start.19
  107.5 0.1 collective-permute-start.20
  107.7 0.9 copy.19.row_slot_ref
  108.5 0.4 collective-permute-done.19.theirs_ref
  108.9 0.0 copy-start.1
  108.9 0.5 collective-permute-done.20.refs_5_
  109.4 0.2 copy-done.1
  109.6 6.8 %shard_map.89 = bf16[512,1024]{1,0:T(8,128)(2,1)} custom-call(s32[34]{0:T(128)} %dynamic-slice_bitcast_fusion.info_ref, s32[512,1]{1,0:T(8,128)} %copy.19.row_slot_ref, f32[512,128]{1,0:T(8,128)} %get-tuple-element.66.mine_ref, f32[512,128]{1,0:T(8,128)} %copy-done.1, f32[512,1024]{1,0:T(8,128)} %shard_map.84.total_ref, ...), custom_call_target="tpu_custom_call" | custom-call | flops 2147483648 | bytes 5242880 | tf_op jit(solution)/shard_map/pallas_call | solution.py:323
  (1 shorter events, 0.0 us)
Async XLA Ops:
  0.0 3.3 %collective-permute-start = (bf16[4,16,8192]{2,1,0:T(8,128)(2,1)}, bf16[4,16,8192]{2,1,0:T(8,128)(2,1)}, u32[]{:S(2)}, u32[]{:S(2)}) collective-permute-start(bf16[4,16,8192]{2,1,0:T(8,128)(2,1)} %here_ref.3), channel_id=1, source_target_pairs={{0,1},{1,0},{2,3},{3,2},{4,5},{5,4},{6,7},{7,6},{8,9},{9,8},{10,11... | collective-permute-start | bytes 3145736 | tf_op jit(solution)/shard_map/ppermute | solution.py:362
  3.3 42.2 %collective-permute-start.8 = (bf16[512,8192]{1,0:T(8,128)(2,1)}, bf16[512,8192]{1,0:T(8,128)(2,1)}, u32[]{:S(2)}, u32[]{:S(2)}) collective-permute-start(bf16[512,8192]{1,0:T(8,128)(2,1)} %tokens_ref.7), channel_id=1, source_target_pairs={{0,1},{1,0},{2,3},{3,2},{4,5},{5,4},{6,7},{7,6},{8,9},{9,8},{10,11... | collective-permute-start | bytes 25165832 | tf_op jit(solution)/shard_map/ppermute | solution.py:362
  6.7 15.2 %collective-permute-start.1 = (bf16[2304,128]{1,0:T(8,128)(2,1)}, bf16[2304,128]{1,0:T(8,128)(2,1)}, u32[]{:S(2)}, u32[]{:S(2)}) collective-permute-start(bf16[2304,128]{1,0:T(8,128)(2,1)} %shard_map.82.refs_0_), channel_id=1, source_target_pairs={{0,4},{1,5},{2,6},{3,7},{4,12},{5,13},{6,14},{7,15},{8,0},{9,1},{1... | collective-permute-start | bytes 1769480 | tf_op jit(solution)/shard_map/ppermute | solution.py:362
  6.7 15.2 %collective-permute-start.2 = (bf16[2304,128]{1,0:T(8,128)(2,1)}, bf16[2304,128]{1,0:T(8,128)(2,1)}, u32[]{:S(2)}, u32[]{:S(2)}) collective-permute-start(bf16[2304,128]{1,0:T(8,128)(2,1)} %shard_map.82.refs_0_), channel_id=1, source_target_pairs={{0,2},{1,3},{2,0},{3,1},{4,6},{5,7},{6,4},{7,5},{8,10},{9,11},{10,... | collective-permute-start | bytes 1769480 | tf_op jit(solution)/shard_map/ppermute | solution.py:362
  8.8 17.8 %collective-permute-start.6 = (s32[512]{0:T(512)S(1)}, s32[512]{0:T(512)S(1)}, u32[]{:S(2)}, u32[]{:S(2)}) collective-permute-start(s32[512]{0:T(512)S(1)} %select_reduce_fusion), channel_id=1, source_target_pairs={{0,1},{1,0},{2,3},{3,2},{4,5},{5,4},{6,7},{7,6},{8,9},{9,8},{10,11... | collective-permute-start | bytes 6152 | tf_op jit(solution)/shard_map/ppermute | solution.py:362
  21.9 19.4 %collective-permute-start.3 = (bf16[2304,128]{1,0:T(8,128)(2,1)}, bf16[2304,128]{1,0:T(8,128)(2,1)}, u32[]{:S(2)}, u32[]{:S(2)}) collective-permute-start(bf16[2304,128]{1,0:T(8,128)(2,1)} %collective-permute-done.1.refs_1_), channel_id=1, source_target_pairs={{0,2},{1,3},{2,0},{3,1},{4,6},{5,7},{6,4},{7,5},{8,10},{9,11},{10,... | collective-permute-start | bytes 1769480 | tf_op jit(solution)/shard_map/ppermute | solution.py:362
  23.0 15.0 %collective-permute-start.4 = (bf16[2304,128]{1,0:T(8,128)(2,1)}, bf16[2304,128]{1,0:T(8,128)(2,1)}, u32[]{:S(2)}, u32[]{:S(2)}) collective-permute-start(bf16[2304,128]{1,0:T(8,128)(2,1)} %collective-permute-done.1.refs_1_), channel_id=1, source_target_pairs={{0,4},{1,5},{2,6},{3,7},{4,12},{5,13},{6,14},{7,15},{8,0},{9,1},{1... | collective-permute-start | bytes 1769480 | tf_op jit(solution)/shard_map/ppermute | solution.py:362
  24.1 13.9 %collective-permute-start.5 = (bf16[2304,128]{1,0:T(8,128)(2,1)}, bf16[2304,128]{1,0:T(8,128)(2,1)}, u32[]{:S(2)}, u32[]{:S(2)}) collective-permute-start(bf16[2304,128]{1,0:T(8,128)(2,1)} %collective-permute-done.2.refs_2_), channel_id=1, source_target_pairs={{0,16},{1,17},{2,18},{3,19},{4,20},{5,21},{6,22},{7,23},{8,24},{9,... | collective-permute-start | bytes 1769480 | tf_op jit(solution)/shard_map/ppermute | solution.py:362
  38.0 14.6 %collective-permute-start.7 = (bf16[2304,128]{1,0:T(8,128)(2,1)}, bf16[2304,128]{1,0:T(8,128)(2,1)}, u32[]{:S(2)}, u32[]{:S(2)}) collective-permute-start(bf16[2304,128]{1,0:T(8,128)(2,1)} %collective-permute-done.4.refs_3_), channel_id=1, source_target_pairs={{0,16},{1,17},{2,18},{3,19},{4,20},{5,21},{6,22},{7,23},{8,24},{9,... | collective-permute-start | bytes 1769480 | tf_op jit(solution)/shard_map/ppermute | solution.py:362
  39.2 13.7 %collective-permute-start.11 = (bf16[2304,128]{1,0:T(8,128)(2,1)}, bf16[2304,128]{1,0:T(8,128)(2,1)}, u32[]{:S(2)}, u32[]{:S(2)}) collective-permute-start(bf16[2304,128]{1,0:T(8,128)(2,1)} %shard_map.82.refs_0_), channel_id=1, source_target_pairs={{0,8},{1,9},{2,10},{3,11},{4,0},{5,1},{6,2},{7,3},{8,12},{9,13},{1... | collective-permute-start | bytes 1769480 | tf_op jit(solution)/shard_map/ppermute | solution.py:362
  41.3 12.4 %collective-permute-start.12 = (bf16[2304,128]{1,0:T(8,128)(2,1)}, bf16[2304,128]{1,0:T(8,128)(2,1)}, u32[]{:S(2)}, u32[]{:S(2)}) collective-permute-start(bf16[2304,128]{1,0:T(8,128)(2,1)} %collective-permute-done.4.refs_3_), channel_id=1, source_target_pairs={{0,2},{1,3},{2,0},{3,1},{4,6},{5,7},{6,4},{7,5},{8,10},{9,11},{10,... | collective-permute-start | bytes 1769480 | tf_op jit(solution)/shard_map/ppermute | solution.py:362
  52.6 12.2 %collective-permute-start.9 = (bf16[2304,128]{1,0:T(8,128)(2,1)}, bf16[2304,128]{1,0:T(8,128)(2,1)}, u32[]{:S(2)}, u32[]{:S(2)}) collective-permute-start(bf16[2304,128]{1,0:T(8,128)(2,1)} %collective-permute-done.3.refs_0_), channel_id=1, source_target_pairs={{0,16},{1,17},{2,18},{3,19},{4,20},{5,21},{6,22},{7,23},{8,24},{9,... | collective-permute-start | bytes 1769480 | tf_op jit(solution)/shard_map/ppermute | solution.py:362
  52.9 13.2 %collective-permute-start.14 = (bf16[2304,128]{1,0:T(8,128)(2,1)}, bf16[2304,128]{1,0:T(8,128)(2,1)}, u32[]{:S(2)}, u32[]{:S(2)}) collective-permute-start(bf16[2304,128]{1,0:T(8,128)(2,1)} %shard_map.86.refs_4_), channel_id=1, source_target_pairs={{0,4},{1,5},{2,6},{3,7},{4,12},{5,13},{6,14},{7,15},{8,0},{9,1},{1... | collective-permute-start | bytes 1769480 | tf_op jit(solution)/shard_map/ppermute | solution.py:362
  53.7 13.2 %collective-permute-start.13 = (bf16[2304,128]{1,0:T(8,128)(2,1)}, bf16[2304,128]{1,0:T(8,128)(2,1)}, u32[]{:S(2)}, u32[]{:S(2)}) collective-permute-start(bf16[2304,128]{1,0:T(8,128)(2,1)} %collective-permute-done.11.refs_1_), channel_id=1, source_target_pairs={{0,2},{1,3},{2,0},{3,1},{4,6},{5,7},{6,4},{7,5},{8,10},{9,11},{10,... | collective-permute-start | bytes 1769480 | tf_op jit(solution)/shard_map/ppermute | solution.py:362
  54.5 5.2 %collective-permute-start.10 = (bf16[128,1024]{1,0:T(8,128)(2,1)}, bf16[128,1024]{1,0:T(8,128)(2,1)S(1)}, u32[]{:S(2)}, u32[]{:S(2)}) collective-permute-start(bf16[128,1024]{1,0:T(8,128)(2,1)} %get-tuple-element.51.refs_0_), channel_id=1, source_target_pairs={{0,1},{1,0},{2,3},{3,2},{4,5},{5,4},{6,7},{7,6},{8,9},{9,8},{10,11... | collective-permute-start | bytes 786440 | tf_op jit(solution)/shard_map/ppermute | solution.py:362
  59.7 20.2 %copy-start = (bf16[128,1024]{1,0:T(8,128)(2,1)}, bf16[128,1024]{1,0:T(8,128)(2,1)S(1)}, u32[]{:S(2)}) copy-start(bf16[128,1024]{1,0:T(8,128)(2,1)S(1)} %collective-permute-done.10.refs_1_) | copy-start | bytes 786436
  66.2 33.6 %collective-permute-start.16 = (bf16[2304,128]{1,0:T(8,128)(2,1)}, bf16[2304,128]{1,0:T(8,128)(2,1)}, u32[]{:S(2)}, u32[]{:S(2)}) collective-permute-start(bf16[2304,128]{1,0:T(8,128)(2,1)} %shard_map.86.refs_4_), channel_id=1, source_target_pairs={{0,8},{1,9},{2,10},{3,11},{4,0},{5,1},{6,2},{7,3},{8,12},{9,13},{1... | collective-permute-start | bytes 1769480 | tf_op jit(solution)/shard_map/ppermute | solution.py:362
  66.9 32.9 %collective-permute-start.17 = (bf16[2304,128]{1,0:T(8,128)(2,1)}, bf16[2304,128]{1,0:T(8,128)(2,1)}, u32[]{:S(2)}, u32[]{:S(2)}) collective-permute-start(bf16[2304,128]{1,0:T(8,128)(2,1)} %collective-permute-done.7.refs_6_), channel_id=1, source_target_pairs={{0,2},{1,3},{2,0},{3,1},{4,6},{5,7},{6,4},{7,5},{8,10},{9,11},{10,... | collective-permute-start | bytes 1769480 | tf_op jit(solution)/shard_map/ppermute | solution.py:362
  67.8 32.0 %collective-permute-start.18 = (bf16[2304,128]{1,0:T(8,128)(2,1)}, bf16[2304,128]{1,0:T(8,128)(2,1)}, u32[]{:S(2)}, u32[]{:S(2)}) collective-permute-start(bf16[2304,128]{1,0:T(8,128)(2,1)} %collective-permute-done.13.refs_3_), channel_id=1, source_target_pairs={{0,16},{1,17},{2,18},{3,19},{4,20},{5,21},{6,22},{7,23},{8,24},{9,... | collective-permute-start | bytes 1769480 | tf_op jit(solution)/shard_map/ppermute | solution.py:362
  79.9 19.9 %collective-permute-start.15 = (bf16[256,1024]{1,0:T(8,128)(2,1)}, bf16[256,1024]{1,0:T(8,128)(2,1)}, u32[]{:S(2)}, u32[]{:S(2)}) collective-permute-start(bf16[256,1024]{1,0:T(8,128)(2,1)} %get-tuple-element.59.refs_2_), channel_id=1, source_target_pairs={{0,1},{1,0},{2,3},{3,2},{4,5},{5,4},{6,7},{7,6},{8,9},{9,8},{10,11... | collective-permute-start | bytes 1572872 | tf_op jit(solution)/shard_map/ppermute | solution.py:362
  107.1 1.8 %collective-permute-start.19 = (f32[512,128]{1,0:T(8,128)}, f32[512,128]{1,0:T(8,128)S(1)}, u32[]{:S(2)}, u32[]{:S(2)}) collective-permute-start(f32[512,128]{1,0:T(8,128)} %get-tuple-element.67), channel_id=1, source_target_pairs={{0,1},{1,0},{2,3},{3,2},{4,5},{5,4},{6,7},{7,6},{8,9},{9,8},{10,11... | collective-permute-start | bytes 786440 | tf_op jit(solution)/shard_map/ppermute | solution.py:362
  107.5 1.9 %collective-permute-start.20 = (bf16[128,1024]{1,0:T(8,128)(2,1)}, bf16[128,1024]{1,0:T(8,128)(2,1)}, u32[]{:S(2)}, u32[]{:S(2)}) collective-permute-start(bf16[128,1024]{1,0:T(8,128)(2,1)} %get-tuple-element.68.refs_4_), channel_id=1, source_target_pairs={{0,1},{1,0},{2,3},{3,2},{4,5},{5,4},{6,7},{7,6},{8,9},{9,8},{10,11... | collective-permute-start | bytes 786440 | tf_op jit(solution)/shard_map/ppermute | solution.py:362
  108.9 0.7 copy-start.1

commit v10 on v9

--- a/solution.py
+++ b/solution.py
@@ -15,12 +15,11 @@
 RANK = 16
 
 PIECES = (
-    *((0, 0, 0), (1, 0, 0), (0, 1, 0), (2, 0, 0)),
-    *((1, 1, 0), (3, 0, 0), (2, 1, 0), (3, 1, 0)),
-    *((0, 0, 1), (0, 1, 1), (2, 0, 1), (1, 0, 1)),
-    *((1, 1, 1), (3, 0, 1), (2, 1, 1), (3, 1, 1)),
+    *((0, 0, 0), (1, 0, 0), (0, 1, 0), (2, 0, 0), (0, 0, 1), (0, 1, 1), (2, 0, 1)),
+    *((1, 1, 0), (3, 0, 0), (2, 1, 0), (3, 1, 0), (1, 0, 1), (1, 1, 1)),
+    *((3, 0, 1), (2, 1, 1), (3, 1, 1)),
 )
-KERNEL_BOUNDS = (0, 4, 12, 16)
+KERNEL_BOUNDS = (0, 7, 13, 16)
 QUARTER_CUTS = (0, 512, 1024, 2048)
 VMEM_BYTES = 64 * 1024 * 1024 - 512 * 1024
 
@@ -180,7 +179,7 @@
 
 
 def absorb_kernel(
-    groups, start, more, info_ref, row_slot_ref, column_slot_ref, tokens_ref, other_ref, *refs
+    groups, start, more, info_ref, row_slot_ref, tokens_ref, other_ref, *refs
 ):
     count = sum(size for size, _ in groups)
     sources, refs = refs[:count], refs[count:]
@@ -223,6 +222,7 @@
                     rows_ref.at[place, pl.ds(i * rows, rows), pl.ds(low, high - low)],
                 )
         first += size
+    lane_slot = lax.broadcasted_iota(jnp.int32, (1, LANES), 1) // RANK
     state = None
     first = 0
     for n, ((size, back), down_ref) in enumerate(zip(groups, down_refs)):
@@ -239,7 +239,8 @@
         height = up_ref.shape[0] // count
         for i in range(size):
             lanes, which = slice(i * LANES, (i + 1) * LANES), first + i
-            wanted = column_slot_ref[:, (start + which) * LANES : (start + which + 1) * LANES]
+            chip = info_ref[2 + 2 * len(PIECES) + start + which]
+            wanted = lane_slot + chip * (LANES // RANK)
             kept = jnp.where(row_slot_ref[...] == wanted, shrink[:, lanes], 0.0)
             state = kept if state is None else state + kept
             for j in range(up_ref.shape[1] // LANES):
@@ -253,7 +254,7 @@
         out_ref[...] = own + before[i][...] if more else own
 
 
-def absorb(info, row_slots, column_slots, tokens, other, width, groups, start, before):
+def absorb(info, row_slots, tokens, other, width, groups, start, before):
     rows, depth = tokens.shape
     pieces = [piece for group, _ in groups for piece in group]
     sizes = [(len(group), back) for group, back in groups]
@@ -270,7 +271,7 @@
     return pl.pallas_call(
         functools.partial(absorb_kernel, sizes, start, more),
         out_shape=(state, state, jax.ShapeDtypeStruct((up_rows, width), tokens.dtype)),
-        in_specs=[pl.BlockSpec(memory_space=pltpu.SMEM), vmem, vmem]
+        in_specs=[pl.BlockSpec(memory_space=pltpu.SMEM), vmem]
         + [anywhere] * (2 + len(pieces))
         + [vmem] * (2 * more),
         out_specs=(vmem, vmem, vmem),
@@ -283,7 +284,7 @@
             transcendentals=0,
         ),
         compiler_params=params(),
-    )(info, row_slots, column_slots, tokens, other, *pieces, *(before or ()))
+    )(info, row_slots, tokens, other, *pieces, *(before or ()))
 
 
 def finish_kernel(
@@ -306,7 +307,7 @@
     lane_slot = lax.broadcasted_iota(jnp.int32, (rows, LANES), 1) // RANK
     high, low = [], []
     for n in range(up.shape[0] // LANES):
-        kept = jnp.where(row_slot_ref[...] == lane_slot + n * (LANES // RANK), shrink, 0.0)
+        kept = jnp.where(row_slot_ref[:rows] == lane_slot + n * (LANES // RANK), shrink, 0.0)
         high.append(kept.astype(jnp.bfloat16))
         low.append((kept - high[-1].astype(jnp.float32)).astype(jnp.bfloat16))
     awaited(copies)
@@ -315,7 +316,7 @@
     out_ref[...] = (total[...] + (lora[:rows] + lora[rows:])).astype(out_ref.dtype)
 
 
-def finish(info, row_slot, mine, theirs, total, ups):
+def finish(info, row_slots, mine, theirs, total, ups):
     rows, width = total.shape
     anywhere = pl.BlockSpec(memory_space=pl.ANY)
     vmem = pl.BlockSpec(memory_space=pltpu.VMEM)
@@ -337,7 +338,7 @@
             transcendentals=0,
         ),
         compiler_params=params(),
-    )(info, row_slot, mine, theirs, total, *ups)
+    )(info, row_slots, mine, theirs, total, *ups)
 
 
 def passed_round(
@@ -373,25 +374,21 @@
     def chip(r, piece):
         return (along_z(r, -piece[0]) ^ (2 * piece[1])) // 2
 
-    per_chip = LANES // rank
     kernels = [PIECES[low:high] for low, high in zip(KERNEL_BOUNDS, KERNEL_BOUNDS[1:])]
-    column_table, info_table = [], []
-    for g in range(planes):
-        for r in range(owners):
-            column_table.append(
-                [chip(r, p) * per_chip + n // rank for p in PIECES for n in range(LANES)]
-            )
-            info_table.append(
-                [g, r % 2]
-                + [
-                    chip(r, p) * LANES + core * held * rank + (g ^ p[2]) * (held // 2 * rank)
-                    for pieces in kernels
-                    for core in (r % 2, 1 - r % 2)
-                    for p in pieces
-                ]
-            )
-    here_of = lambda table, which: lax.dynamic_index_in_dim(
-        jnp.array(np.array(table, np.int32)), which, 0, keepdims=False
+    info_table = [
+        [g, r % 2]
+        + [
+            chip(r, p) * LANES + core * held * rank + (g ^ p[2]) * (held // 2 * rank)
+            for pieces in kernels
+            for core in (r % 2, 1 - r % 2)
+            for p in pieces
+        ]
+        + [chip(r, p) for p in PIECES]
+        for g in range(planes)
+        for r in range(owners)
+    ]
+    info = lax.dynamic_index_in_dim(
+        jnp.array(np.array(info_table, np.int32)), device, 0, keepdims=False
     )
 
     def together(*values):
@@ -401,38 +398,43 @@
         return lax.optimization_barrier((value, *others))[0]
 
     there = core_swap(adapter_down_weight)
-    at = jnp.stack([lax.axis_index("groups"), lax.axis_index("req") % 2])
-    there, at, tokens_late = together(there, at, tokens)
+    row_slot = slots_of_rows(row_adapter_index, adapter_storage_slot)
+    there, info, row_slot, tokens_late = together(there, info, row_slot, tokens)
 
     def piece(back, *others):
         return assemble(
-            back, after(at, *others), adapter_down_weight, there, adapter_up_weight
+            back, after(info, *others), adapter_down_weight, there, adapter_up_weight
         )
 
     front = piece(0)
+    cuts = (0, 3 * DEPTH_TILE, 6 * DEPTH_TILE, depth)
+
+    def base(number, before, *others):
+        low, high = cuts[number : number + 2]
+        return base_part(after(tokens, *others), base_value_weight, low, high, before)
 
     z1, x0 = z_ring(front), x_swap(front)
     other = core_swap(tokens_late)
-    row_index = after(row_adapter_index, front)
-    row_slot = slots_of_rows(row_index, adapter_storage_slot)
     other_slot = core_swap(row_slot[:, 0])
-    device = after(device, front)
-    info, column_slots = here_of(info_table, device), here_of(column_table, device)[None, :]
-    total = base_part(after(tokens, front), base_value_weight, 0, depth // 2)
+    total = base(0, None, front)
     row_slots = jnp.concatenate([row_slot, other_slot[:, None]], axis=0)
 
     z2 = z_ring(after(z1, total))
     x1 = x_swap(after(z1, x0, total))
     yx0 = y_swap(after(x0, total))
-    tokens_late = after(tokens, z1, x0, total, row_slots, info, column_slots)
-    total = base_part(tokens_late, base_value_weight, depth // 2, depth, total)
+    total = base(1, total, z1, x0, total, row_slots)
+
+    z3 = z_back(after(front, z2, total))
+    x2 = x_swap(after(z2, x1, total))
+    yz2 = y_swap(after(z2, yx0, total))
+    back = piece(1, z2, x1, yx0, total)
+    total = base(2, total, z2, x1, yx0, back, other)
     ups = []
 
     def update(number, groups, before, *others):
         mine, others, up = absorb(
             after(info, *others),
             row_slots,
-            column_slots,
             tokens,
             other,
             width,
@@ -443,25 +445,20 @@
         ups.extend([up, core_swap(up)])
         return mine, others
 
-    z3 = z_back(after(front, z2, total))
-    x2 = x_swap(after(z2, x1, total))
-    yz2 = y_swap(after(z2, yx0, total))
-    state = update(0, [((front, z1, x0, z2), 0)], None, x1, yx0, total)
-    back = piece(1, z2, x1, yx0, total)
-
-    zb1 = z_ring(after(back, z3, state[0]))
-    x3 = x_swap(after(z3, x2, state[0]))
-    yx1 = y_swap(after(x1, yz2, state[0]))
-
-    zb3 = z_back(after(back, zb1))
-    xyz2 = x_swap(after(yz2, x3))
-    yx3 = y_swap(after(x3, yx1))
+    zb1 = z_ring(after(back, z3, total))
+    x3 = x_swap(after(z3, x2, total))
+    yx1 = y_swap(after(x1, yz2, total))
     state = update(
-        1, [((x1, z3, x2, x3), 0), ((back, yx0, yz2, zb1), 1)], state, yx1, ups[1]
-    )
-
-    mine, others = update(2, [((yx1, zb3, xyz2, yx3), 1)], state, ups[3])
-    return finish(info, row_slot, mine, core_swap(others), total, ups)
+        0, [((front, z1, x0, z2), 0), ((back, yx0, yz2), 1)], None, z3, x2, yz2, total
+    )
+
+    zb3 = z_back(after(back, zb1, state[0]))
+    xyz2 = x_swap(after(yz2, x3, state[0]))
+    yx3 = y_swap(after(x3, yx1, state[0]))
+    state = update(1, [((x1, z3, x2, x3), 0), ((zb1, yx1), 1)], state, zb1, x3, yx1)
+
+    mine, others = update(2, [((zb3, xyz2, yx3), 1)], state, ups[1], ups[3])
+    return finish(info, row_slots, mine, core_swap(others), total, ups)
 
 
 def solution(mesh):

time: 117 us -> 106 us (0.906)
  the two profiles are of different devices: /device:TPU:17 before, /device:TPU:0 now
where the time goes in v10:
time: 106 us
  Pallas kernels  64.2 us (61%)
  starting transfers between devices  21.6 us (20%)
  waiting for transfers between devices  15.9 us (15%)
  local copies, waits for them, and re-layouts  3.08 us (3%)
    pallas_call x3, Pallas kernels, absorb(): pl.pallas_call(functools.partial(absorb_kernel, sizes, start, more), out_...  28.6 us
    pallas_call x3, Pallas kernels, base_part(): pl.pallas_call(functools.partial(base_kernel, steps), out_shape=result, g...  22.8 us
    ppermute x21, starting transfers between devices, permuted(): return lax.ppermute(array, axes, pairs)  21.6 us
    ppermute x21, waiting for transfers between devices, permuted(): return lax.ppermute(array, axes, pairs)  15.9 us
    pallas_call x1, Pallas kernels, finish(): pl.pallas_call(functools.partial(finish_kernel, len(ups)), out_shape=jax....  6.86 us
    pallas_call x2, Pallas kernels, assemble(): pl.pallas_call(functools.partial(assemble_kernel, back), out_shape=jax.Sh...  5.96 us
  transfers between devices with their start and end apart: 21, of which 9 were waited for; matrix products, arithmetic and copies ran while one was open for 3% of the time, Pallas kernels for 48%

profile of v10, /device:TPU:0, one launch (start us, length us, event | category | flops | bytes accessed | tf_op | source)
XLA Modules:
  0.0 105.9 jit_solution(2544007223577234358)
XLA Ops:
  0.0 0.5 collective-permute-start
  0.5 1.3 %dynamic-slice_bitcast_fusion.info_ref = s32[50]{0:T(128)} fusion(s32[32,50]{1,0:T(8,128)} %constant.20.clone, s32[]{:T(128)S(6)} %select_n.8), kind=kLoop, calls=%fused_computation.3 | loop fusion | bytes 404 | tf_op jit(solution)/shard_map/jit(dynamic_index_in_dim)/squeeze | solution.py:390
  1.7 0.8 select_reduce_fusion
  2.5 0.6 collective-permute-done.there_ref
  3.1 0.4 collective-permute-start.10
  3.5 3.0 %shard_map.73.refs_0_ = bf16[2304,128]{1,0:T(8,128)(2,1)} custom-call(s32[50]{0:T(128)} %dynamic-slice_bitcast_fusion.info_ref, bf16[4,16,8192]{2,1,0:T(8,128)(2,1)} %here_ref.3, bf16[4,16,8192]{2,1,0:T(8,128)(2,1)} %collective-permute-done.there_ref, bf16[4,16,1024]{2,1,0:T(8,128)(2,1)} %up_ref.3), custom_call_target="tpu_custom_call" | custom-call | tf_op jit(solution)/shard_map/pallas_call | solution.py:116
  6.5 2.8 %collective-permute-start.2 = (bf16[2304,128]{1,0:T(8,128)(2,1)}, bf16[2304,128]{1,0:T(8,128)(2,1)}, u32[]{:S(2)}, u32[]{:S(2)}) collective-permute-start(bf16[2304,128]{1,0:T(8,128)(2,1)} %shard_map.73.refs_0_), channel_id=1, source_target_pairs={{0,4},{1,5},{2,6},{3,7},{4,12},{5,13},{6,14},{7,15},{8,0},{9,1},{1... | collective-permute-start | bytes 1769480 | tf_op jit(solution)/shard_map/ppermute | solution.py:363
  9.2 1.5 %collective-permute-start.4 = (bf16[2304,128]{1,0:T(8,128)(2,1)}, bf16[2304,128]{1,0:T(8,128)(2,1)}, u32[]{:S(2)}, u32[]{:S(2)}) collective-permute-start(bf16[2304,128]{1,0:T(8,128)(2,1)} %shard_map.73.refs_0_), channel_id=1, source_target_pairs={{0,2},{1,3},{2,0},{3,1},{4,6},{5,7},{6,4},{7,5},{8,10},{9,11},{10,... | collective-permute-start | bytes 1769480 | tf_op jit(solution)/shard_map/ppermute | solution.py:363
  10.7 8.1 %shard_map.74.refs_0_ = f32[512,1024]{1,0:T(8,128)} custom-call(bf16[512,8192]{1,0:T(8,128)(2,1)} %tokens_ref.8, bf16[8192,1024]{1,0:T(8,128)(2,1)} %weight_ref.5), custom_call_target="tpu_custom_call" | custom-call | flops 3221225472 | bytes 11534336 | tf_op jit(solution)/shard_map/pallas_call | solution.py:159
  18.8 5.6 %collective-permute-done.2.refs_1_ = bf16[2304,128]{1,0:T(8,128)(2,1)} collective-permute-done((bf16[2304,128]{1,0:T(8,128)(2,1)}, bf16[2304,128]{1,0:T(8,128)(2,1)}, u32[]{:S(2)}, u32[]{:S(2)}) %collective-permute-start.2) | collective-permute-done | bytes 589856 | tf_op jit(solution)/shard_map/ppermute | solution.py:363
  24.4 0.8 collective-permute-start.3
  25.2 0.0 collective-permute-done.4.refs_2_
  25.2 1.5 %collective-permute-start.6 = (bf16[2304,128]{1,0:T(8,128)(2,1)}, bf16[2304,128]{1,0:T(8,128)(2,1)}, u32[]{:S(2)}, u32[]{:S(2)}) collective-permute-start(bf16[2304,128]{1,0:T(8,128)(2,1)} %collective-permute-done.2.refs_1_), channel_id=1, source_target_pairs={{0,2},{1,3},{2,0},{3,1},{4,6},{5,7},{6,4},{7,5},{8,10},{9,11},{10,... | collective-permute-start | bytes 1769480 | tf_op jit(solution)/shard_map/ppermute | solution.py:363
  26.7 1.5 %collective-permute-start.8 = (bf16[2304,128]{1,0:T(8,128)(2,1)}, bf16[2304,128]{1,0:T(8,128)(2,1)}, u32[]{:S(2)}, u32[]{:S(2)}) collective-permute-start(bf16[2304,128]{1,0:T(8,128)(2,1)} %collective-permute-done.4.refs_2_), channel_id=1, source_target_pairs={{0,16},{1,17},{2,18},{3,19},{4,20},{5,21},{6,22},{7,23},{8,24},{9,... | collective-permute-start | bytes 1769480 | tf_op jit(solution)/shard_map/ppermute | solution.py:363
  28.3 0.0 collective-permute-start.1
  28.3 1.2 %collective-permute-done.1 = s32[512]{0:T(512)S(1)} collective-permute-done((s32[512]{0:T(512)S(1)}, s32[512]{0:T(512)S(1)}, u32[]{:S(2)}, u32[]{:S(2)}) %collective-permute-start.1) | collective-permute-done | bytes 2080 | tf_op jit(solution)/shard_map/ppermute | solution.py:363
  29.4 8.4 %shard_map.75.refs_0_ = f32[512,1024]{1,0:T(8,128)} custom-call(bf16[512,8192]{1,0:T(8,128)(2,1)} %tokens_ref.8, bf16[8192,1024]{1,0:T(8,128)(2,1)} %weight_ref.5, f32[512,1024]{1,0:T(8,128)} %shard_map.74.refs_0_), custom_call_target="tpu_custom_call" | custom-call | flops 3221225472 | bytes 11534336 | tf_op jit(solution)/shard_map/pallas_call | solution.py:159
  37.8 2.9 %collective-permute-done.3.refs_3_ = bf16[2304,128]{1,0:T(8,128)(2,1)} collective-permute-done((bf16[2304,128]{1,0:T(8,128)(2,1)}, bf16[2304,128]{1,0:T(8,128)(2,1)}, u32[]{:S(2)}, u32[]{:S(2)}) %collective-permute-start.3) | collective-permute-done | bytes 589856 | tf_op jit(solution)/shard_map/ppermute | solution.py:363
  40.7 1.3 %collective-permute-start.5 = (bf16[2304,128]{1,0:T(8,128)(2,1)}, bf16[2304,128]{1,0:T(8,128)(2,1)}, u32[]{:S(2)}, u32[]{:S(2)}) collective-permute-start(bf16[2304,128]{1,0:T(8,128)(2,1)} %shard_map.73.refs_0_), channel_id=1, source_target_pairs={{0,8},{1,9},{2,10},{3,11},{4,0},{5,1},{6,2},{7,3},{8,12},{9,13},{1... | collective-permute-start | bytes 1769480 | tf_op jit(solution)/shard_map/ppermute | solution.py:363
  42.0 0.0 collective-permute-done.6.refs_0_
  42.0 1.5 %collective-permute-start.7 = (bf16[2304,128]{1,0:T(8,128)(2,1)}, bf16[2304,128]{1,0:T(8,128)(2,1)}, u32[]{:S(2)}, u32[]{:S(2)}) collective-permute-start(bf16[2304,128]{1,0:T(8,128)(2,1)} %collective-permute-done.3.refs_3_), channel_id=1, source_target_pairs={{0,2},{1,3},{2,0},{3,1},{4,6},{5,7},{6,4},{7,5},{8,10},{9,11},{10,... | collective-permute-start | bytes 1769480 | tf_op jit(solution)/shard_map/ppermute | solution.py:363
  43.5 0.0 collective-permute-done.8.refs_5_
  43.5 1.5 %collective-permute-start.9 = (bf16[2304,128]{1,0:T(8,128)(2,1)}, bf16[2304,128]{1,0:T(8,128)(2,1)}, u32[]{:S(2)}, u32[]{:S(2)}) collective-permute-start(bf16[2304,128]{1,0:T(8,128)(2,1)} %collective-permute-done.3.refs_3_), channel_id=1, source_target_pairs={{0,16},{1,17},{2,18},{3,19},{4,20},{5,21},{6,22},{7,23},{8,24},{9,... | collective-permute-start | bytes 1769480 | tf_op jit(solution)/shard_map/ppermute | solution.py:363
  45.0 3.0 %shard_map.76.refs_4_ = bf16[2304,128]{1,0:T(8,128)(2,1)} custom-call(s32[50]{0:T(128)} %dynamic-slice_bitcast_fusion.info_ref, bf16[4,16,8192]{2,1,0:T(8,128)(2,1)} %here_ref.3, bf16[4,16,8192]{2,1,0:T(8,128)(2,1)} %collective-permute-done.there_ref, bf16[4,16,1024]{2,1,0:T(8,128)(2,1)} %up_ref.3), custom_call_target="tpu_custom_call" | custom-call | tf_op jit(solution)/shard_map/pallas_call | solution.py:116
  48.0 0.0 collective-permute-done.10.other_ref
  48.0 6.4 %shard_map.77.total_ref = f32[512,1024]{1,0:T(8,128)} custom-call(bf16[512,8192]{1,0:T(8,128)(2,1)} %tokens_ref.8, bf16[8192,1024]{1,0:T(8,128)(2,1)} %weight_ref.5, f32[512,1024]{1,0:T(8,128)} %shard_map.75.refs_0_), custom_call_target="tpu_custom_call" | custom-call | flops 2147483648 | bytes 8388608 | tf_op jit(solution)/shard_map/pallas_call | solution.py:159
  54.4 0.8 collective-permute-done.5.refs_1_
  55.2 2.7 %collective-permute-start.12 = (bf16[2304,128]{1,0:T(8,128)(2,1)}, bf16[2304,128]{1,0:T(8,128)(2,1)}, u32[]{:S(2)}, u32[]{:S(2)}) collective-permute-start(bf16[2304,128]{1,0:T(8,128)(2,1)} %shard_map.76.refs_4_), channel_id=1, source_target_pairs={{0,4},{1,5},{2,6},{3,7},{4,12},{5,13},{6,14},{7,15},{8,0},{9,1},{1... | collective-permute-start | bytes 1769480 | tf_op jit(solution)/shard_map/ppermute | solution.py:363
  57.9 0.0 collective-permute-done.7.refs_2_
  57.9 0.7 collective-permute-start.13
  58.6 0.0 collective-permute-done.9.refs_6_
  58.6 1.5 %collective-permute-start.14 = (bf16[2304,128]{1,0:T(8,128)(2,1)}, bf16[2304,128]{1,0:T(8,128)(2,1)}, u32[]{:S(2)}, u32[]{:S(2)}) collective-permute-start(bf16[2304,128]{1,0:T(8,128)(2,1)} %collective-permute-done.6.refs_0_), channel_id=1, source_target_pairs={{0,16},{1,17},{2,18},{3,19},{4,20},{5,21},{6,22},{7,23},{8,24},{9,... | collective-permute-start | bytes 1769480 | tf_op jit(solution)/shard_map/ppermute | solution.py:363
  60.1 1.0 copy.17.row_slot_ref
  61.1 10.3 %shard_map.78 = (f32[512,128]{1,0:T(8,128)}, f32[512,128]{1,0:T(8,128)}, bf16[224,1024]{1,0:T(8,128)(2,1)}) custom-call(s32[50]{0:T(128)} %dynamic-slice_bitcast_fusion.info_ref, s32[1024,1]{1,0:T(8,128)} %copy.17.row_slot_ref, bf16[512,8192]{1,0:T(8,128)(2,1)} %tokens_ref.8, bf16[512,8192]{1,0:T(8,128)(2,1)} %collective-permute-done.10.other_ref, ...), custom_call_target="tpu_custom_call" | custom-call | flops 3758096384 | bytes 12517376 | tf_op jit(solution)/shard_map/pallas_call | solution.py:271
  71.5 0.1 collective-permute-start.11
  71.6 0.0 collective-permute-done.12.refs_4_
  71.6 1.7 %collective-permute-start.16 = (bf16[2304,128]{1,0:T(8,128)(2,1)}, bf16[2304,128]{1,0:T(8,128)(2,1)}, u32[]{:S(2)}, u32[]{:S(2)}) collective-permute-start(bf16[2304,128]{1,0:T(8,128)(2,1)} %shard_map.76.refs_4_), channel_id=1, source_target_pairs={{0,8},{1,9},{2,10},{3,11},{4,0},{5,1},{6,2},{7,3},{8,12},{9,13},{1... | collective-permute-start | bytes 1769480 | tf_op jit(solution)/shard_map/ppermute | solution.py:363
  73.3 0.0 collective-permute-done.13.refs_3_
  73.3 0.5 collective-permute-start.17
  73.8 0.0 collective-permute-done.14.refs_5_
  73.8 0.5 collective-permute-start.18
  74.3 11.3 %shard_map.79 = (f32[512,128]{1,0:T(8,128)}, f32[512,128]{1,0:T(8,128)}, bf16[192,1024]{1,0:T(8,128)(2,1)}) custom-call(s32[50]{0:T(128)} %dynamic-slice_bitcast_fusion.info_ref, s32[1024,1]{1,0:T(8,128)} %copy.17.row_slot_ref, bf16[512,8192]{1,0:T(8,128)(2,1)} %tokens_ref.8, bf16[512,8192]{1,0:T(8,128)(2,1)} %collective-permute-done.10.other_ref, ...), custom_call_target="tpu_custom_call" | custom-call | flops 3221225472 | bytes 11927552 | tf_op jit(solution)/shard_map/pallas_call | solution.py:271
  85.6 0.1 collective-permute-start.15
  85.7 0.0 collective-permute-done.11.refs_1_
  85.7 0.0 copy-start
  85.7 2.0 %collective-permute-done.15.refs_3_ = bf16[192,1024]{1,0:T(8,128)(2,1)} collective-permute-done((bf16[192,1024]{1,0:T(8,128)(2,1)}, bf16[192,1024]{1,0:T(8,128)(2,1)}, u32[]{:S(2)}, u32[]{:S(2)}) %collective-permute-start.15) | collective-permute-done | bytes 393248 | tf_op jit(solution)/shard_map/ppermute | solution.py:363
  87.8 0.0 collective-permute-done.16.refs_0_
  87.8 1.0 collective-permute-done.17.refs_1_
  88.8 0.3 collective-permute-done.18.refs_2_
  89.1 6.9 %shard_map.80 = (f32[512,128]{1,0:T(8,128)}, f32[512,128]{1,0:T(8,128)}, bf16[96,1024]{1,0:T(8,128)(2,1)}) custom-call(s32[50]{0:T(128)} %dynamic-slice_bitcast_fusion.info_ref, s32[1024,1]{1,0:T(8,128)} %copy.17.row_slot_ref, bf16[512,8192]{1,0:T(8,128)(2,1)} %tokens_ref.8, bf16[512,8192]{1,0:T(8,128)(2,1)} %collective-permute-done.10.other_ref, ...), custom_call_target="tpu_custom_call" | custom-call | flops 1610612736 | bytes 5963776 | tf_op jit(solution)/shard_map/pallas_call | solution.py:271
  96.0 0.0 copy-done
  96.0 0.1 collective-permute-start.19
  96.0 0.5 collective-permute-start.20
  96.5 1.5 %collective-permute-done.20.refs_5_ = bf16[96,1024]{1,0:T(8,128)(2,1)S(1)} collective-permute-done((bf16[96,1024]{1,0:T(8,128)(2,1)}, bf16[96,1024]{1,0:T(8,128)(2,1)S(1)}, u32[]{:S(2)}, u32[]{:S(2)}) %collective-permute-start.20) | collective-permute-done | bytes 196640 | tf_op jit(solution)/shard_map/ppermute | solution.py:363
  98.1 0.0 copy-start.2
  98.1 0.0 collective-permute-done.19.theirs_ref
  98.1 0.0 copy-start.1
  98.1 0.7 copy-done.2
  98.7 0.1 copy-done.1
  98.9 6.9 %shard_map.81 = bf16[512,1024]{1,0:T(8,128)(2,1)} custom-call(s32[50]{0:T(128)} %dynamic-slice_bitcast_fusion.info_ref, s32[1024,1]{1,0:T(8,128)} %copy.17.row_slot_ref, f32[512,128]{1,0:T(8,128)} %get-tuple-element.66.mine_ref, f32[512,128]{1,0:T(8,128)} %copy-done.1, f32[512,1024]{1,0:T(8,128)} %shard_map.77.total_ref, ...), custom_call_target="tpu_custom_call" | custom-call | flops 2147483648 | bytes 5242880 | tf_op jit(solution)/shard_map/pallas_call | solution.py:324
  (1 shorter events, 0.0 us)
Async XLA Ops:
  0.0 3.1 %collective-permute-start = (bf16[4,16,8192]{2,1,0:T(8,128)(2,1)}, bf16[4,16,8192]{2,1,0:T(8,128)(2,1)}, u32[]{:S(2)}, u32[]{:S(2)}) collective-permute-start(bf16[4,16,8192]{2,1,0:T(8,128)(2,1)} %here_ref.3), channel_id=1, source_target_pairs={{0,1},{1,0},{2,3},{3,2},{4,5},{5,4},{6,7},{7,6},{8,9},{9,8},{10,11... | collective-permute-start | bytes 3145736 | tf_op jit(solution)/shard_map/ppermute | solution.py:363
  3.1 44.9 %collective-permute-start.10 = (bf16[512,8192]{1,0:T(8,128)(2,1)}, bf16[512,8192]{1,0:T(8,128)(2,1)}, u32[]{:S(2)}, u32[]{:S(2)}) collective-permute-start(bf16[512,8192]{1,0:T(8,128)(2,1)} %tokens_ref.8), channel_id=1, source_target_pairs={{0,1},{1,0},{2,3},{3,2},{4,5},{5,4},{6,7},{7,6},{8,9},{9,8},{10,11... | collective-permute-start | bytes 25165832 | tf_op jit(solution)/shard_map/ppermute | solution.py:363
  6.5 18.0 %collective-permute-start.2 = (bf16[2304,128]{1,0:T(8,128)(2,1)}, bf16[2304,128]{1,0:T(8,128)(2,1)}, u32[]{:S(2)}, u32[]{:S(2)}) collective-permute-start(bf16[2304,128]{1,0:T(8,128)(2,1)} %shard_map.73.refs_0_), channel_id=1, source_target_pairs={{0,4},{1,5},{2,6},{3,7},{4,12},{5,13},{6,14},{7,15},{8,0},{9,1},{1... | collective-permute-start | bytes 1769480 | tf_op jit(solution)/shard_map/ppermute | solution.py:363
  9.2 16.0 %collective-permute-start.4 = (bf16[2304,128]{1,0:T(8,128)(2,1)}, bf16[2304,128]{1,0:T(8,128)(2,1)}, u32[]{:S(2)}, u32[]{:S(2)}) collective-permute-start(bf16[2304,128]{1,0:T(8,128)(2,1)} %shard_map.73.refs_0_), channel_id=1, source_target_pairs={{0,2},{1,3},{2,0},{3,1},{4,6},{5,7},{6,4},{7,5},{8,10},{9,11},{10,... | collective-permute-start | bytes 1769480 | tf_op jit(solution)/shard_map/ppermute | solution.py:363
  24.4 16.2 %collective-permute-start.3 = (bf16[2304,128]{1,0:T(8,128)(2,1)}, bf16[2304,128]{1,0:T(8,128)(2,1)}, u32[]{:S(2)}, u32[]{:S(2)}) collective-permute-start(bf16[2304,128]{1,0:T(8,128)(2,1)} %collective-permute-done.2.refs_1_), channel_id=1, source_target_pairs={{0,4},{1,5},{2,6},{3,7},{4,12},{5,13},{6,14},{7,15},{8,0},{9,1},{1... | collective-permute-start | bytes 1769480 | tf_op jit(solution)/shard_map/ppermute | solution.py:363
  25.2 16.7 %collective-permute-start.6 = (bf16[2304,128]{1,0:T(8,128)(2,1)}, bf16[2304,128]{1,0:T(8,128)(2,1)}, u32[]{:S(2)}, u32[]{:S(2)}) collective-permute-start(bf16[2304,128]{1,0:T(8,128)(2,1)} %collective-permute-done.2.refs_1_), channel_id=1, source_target_pairs={{0,2},{1,3},{2,0},{3,1},{4,6},{5,7},{6,4},{7,5},{8,10},{9,11},{10,... | collective-permute-start | bytes 1769480 | tf_op jit(solution)/shard_map/ppermute | solution.py:363
  26.7 16.7 %collective-permute-start.8 = (bf16[2304,128]{1,0:T(8,128)(2,1)}, bf16[2304,128]{1,0:T(8,128)(2,1)}, u32[]{:S(2)}, u32[]{:S(2)}) collective-permute-start(bf16[2304,128]{1,0:T(8,128)(2,1)} %collective-permute-done.4.refs_2_), channel_id=1, source_target_pairs={{0,16},{1,17},{2,18},{3,19},{4,20},{5,21},{6,22},{7,23},{8,24},{9,... | collective-permute-start | bytes 1769480 | tf_op jit(solution)/shard_map/ppermute | solution.py:363
  28.3 1.2 %collective-permute-start.1 = (s32[512]{0:T(512)S(1)}, s32[512]{0:T(512)S(1)}, u32[]{:S(2)}, u32[]{:S(2)}) collective-permute-start(s32[512]{0:T(512)S(1)} %select_reduce_fusion), channel_id=1, source_target_pairs={{0,1},{1,0},{2,3},{3,2},{4,5},{5,4},{6,7},{7,6},{8,9},{9,8},{10,11... | collective-permute-start | bytes 6152 | tf_op jit(solution)/shard_map/ppermute | solution.py:363
  40.7 14.6 %collective-permute-start.5 = (bf16[2304,128]{1,0:T(8,128)(2,1)}, bf16[2304,128]{1,0:T(8,128)(2,1)}, u32[]{:S(2)}, u32[]{:S(2)}) collective-permute-start(bf16[2304,128]{1,0:T(8,128)(2,1)} %shard_map.73.refs_0_), channel_id=1, source_target_pairs={{0,8},{1,9},{2,10},{3,11},{4,0},{5,1},{6,2},{7,3},{8,12},{9,13},{1... | collective-permute-start | bytes 1769480 | tf_op jit(solution)/shard_map/ppermute | solution.py:363
  42.0 15.9 %collective-permute-start.7 = (bf16[2304,128]{1,0:T(8,128)(2,1)}, bf16[2304,128]{1,0:T(8,128)(2,1)}, u32[]{:S(2)}, u32[]{:S(2)}) collective-permute-start(bf16[2304,128]{1,0:T(8,128)(2,1)} %collective-permute-done.3.refs_3_), channel_id=1, source_target_pairs={{0,2},{1,3},{2,0},{3,1},{4,6},{5,7},{6,4},{7,5},{8,10},{9,11},{10,... | collective-permute-start | bytes 1769480 | tf_op jit(solution)/shard_map/ppermute | solution.py:363
  43.5 15.1 %collective-permute-start.9 = (bf16[2304,128]{1,0:T(8,128)(2,1)}, bf16[2304,128]{1,0:T(8,128)(2,1)}, u32[]{:S(2)}, u32[]{:S(2)}) collective-permute-start(bf16[2304,128]{1,0:T(8,128)(2,1)} %collective-permute-done.3.refs_3_), channel_id=1, source_target_pairs={{0,16},{1,17},{2,18},{3,19},{4,20},{5,21},{6,22},{7,23},{8,24},{9,... | collective-permute-start | bytes 1769480 | tf_op jit(solution)/shard_map/ppermute | solution.py:363
  55.2 16.4 %collective-permute-start.12 = (bf16[2304,128]{1,0:T(8,128)(2,1)}, bf16[2304,128]{1,0:T(8,128)(2,1)}, u32[]{:S(2)}, u32[]{:S(2)}) collective-permute-start(bf16[2304,128]{1,0:T(8,128)(2,1)} %shard_map.76.refs_4_), channel_id=1, source_target_pairs={{0,4},{1,5},{2,6},{3,7},{4,12},{5,13},{6,14},{7,15},{8,0},{9,1},{1... | collective-permute-start | bytes 1769480 | tf_op jit(solution)/shard_map/ppermute | solution.py:363
  57.9 15.4 %collective-permute-start.13 = (bf16[2304,128]{1,0:T(8,128)(2,1)}, bf16[2304,128]{1,0:T(8,128)(2,1)}, u32[]{:S(2)}, u32[]{:S(2)}) collective-permute-start(bf16[2304,128]{1,0:T(8,128)(2,1)} %collective-permute-done.5.refs_1_), channel_id=1, source_target_pairs={{0,2},{1,3},{2,0},{3,1},{4,6},{5,7},{6,4},{7,5},{8,10},{9,11},{10,... | collective-permute-start | bytes 1769480 | tf_op jit(solution)/shard_map/ppermute | solution.py:363
  58.6 15.2 %collective-permute-start.14 = (bf16[2304,128]{1,0:T(8,128)(2,1)}, bf16[2304,128]{1,0:T(8,128)(2,1)}, u32[]{:S(2)}, u32[]{:S(2)}) collective-permute-start(bf16[2304,128]{1,0:T(8,128)(2,1)} %collective-permute-done.6.refs_0_), channel_id=1, source_target_pairs={{0,16},{1,17},{2,18},{3,19},{4,20},{5,21},{6,22},{7,23},{8,24},{9,... | collective-permute-start | bytes 1769480 | tf_op jit(solution)/shard_map/ppermute | solution.py:363
  71.5 14.2 %collective-permute-start.11 = (bf16[224,1024]{1,0:T(8,128)(2,1)}, bf16[224,1024]{1,0:T(8,128)(2,1)S(1)}, u32[]{:S(2)}, u32[]{:S(2)}) collective-permute-start(bf16[224,1024]{1,0:T(8,128)(2,1)} %get-tuple-element.52.refs_0_), channel_id=1, source_target_pairs={{0,1},{1,0},{2,3},{3,2},{4,5},{5,4},{6,7},{7,6},{8,9},{9,8},{10,11... | collective-permute-start | bytes 1376264 | tf_op jit(solution)/shard_map/ppermute | solution.py:363
  71.6 16.2 %collective-permute-start.16 = (bf16[2304,128]{1,0:T(8,128)(2,1)}, bf16[2304,128]{1,0:T(8,128)(2,1)}, u32[]{:S(2)}, u32[]{:S(2)}) collective-permute-start(bf16[2304,128]{1,0:T(8,128)(2,1)} %shard_map.76.refs_4_), channel_id=1, source_target_pairs={{0,8},{1,9},{2,10},{3,11},{4,0},{5,1},{6,2},{7,3},{8,12},{9,13},{1... | collective-permute-start | bytes 1769480 | tf_op jit(solution)/shard_map/ppermute | solution.py:363
  73.3 15.5 %collective-permute-start.17 = (bf16[2304,128]{1,0:T(8,128)(2,1)}, bf16[2304,128]{1,0:T(8,128)(2,1)}, u32[]{:S(2)}, u32[]{:S(2)}) collective-permute-start(bf16[2304,128]{1,0:T(8,128)(2,1)} %collective-permute-done.9.refs_6_), channel_id=1, source_target_pairs={{0,2},{1,3},{2,0},{3,1},{4,6},{5,7},{6,4},{7,5},{8,10},{9,11},{10,... | collective-permute-start | bytes 1769480 | tf_op jit(solution)/shard_map/ppermute | solution.py:363
  73.8 15.2 %collective-permute-start.18 = (bf16[2304,128]{1,0:T(8,128)(2,1)}, bf16[2304,128]{1,0:T(8,128)(2,1)}, u32[]{:S(2)}, u32[]{:S(2)}) collective-permute-start(bf16[2304,128]{1,0:T(8,128)(2,1)} %collective-permute-done.13.refs_3_), channel_id=1, source_target_pairs={{0,16},{1,17},{2,18},{3,19},{4,20},{5,21},{6,22},{7,23},{8,24},{9,... | collective-permute-start | bytes 1769480 | tf_op jit(solution)/shard_map/ppermute | solution.py:363
  85.6 2.1 %collective-permute-start.15 = (bf16[192,1024]{1,0:T(8,128)(2,1)}, bf16[192,1024]{1,0:T(8,128)(2,1)}, u32[]{:S(2)}, u32[]{:S(2)}) collective-permute-start(bf16[192,1024]{1,0:T(8,128)(2,1)} %get-tuple-element.59.refs_2_), channel_id=1, source_target_pairs={{0,1},{1,0},{2,3},{3,2},{4,5},{5,4},{6,7},{7,6},{8,9},{9,8},{10,11... | collective-permute-start | bytes 1179656 | tf_op jit(solution)/shard_map/ppermute | solution.py:363
  85.7 10.2 %copy-start = (bf16[224,1024]{1,0:T(8,128)(2,1)}, bf16[224,1024]{1,0:T(8,128)(2,1)S(1)}, u32[]{:S(2)}) copy-start(bf16[224,1024]{1,0:T(8,128)(2,1)S(1)} %collective-permute-done.11.refs_1_) | copy-start | bytes 1376260
  96.0 2.1 %collective-permute-start.19 = (f32[512,128]{1,0:T(8,128)}, f32[512,128]{1,0:T(8,128)S(1)}, u32[]{:S(2)}, u32[]{:S(2)}) collective-permute-start(f32[512,128]{1,0:T(8,128)} %get-tuple-element.67), channel_id=1, source_target_pairs={{0,1},{1,0},{2,3},{3,2},{4,5},{5,4},{6,7},{7,6},{8,9},{9,8},{10,11... | collective-permute-start | bytes 786440 | tf_op jit(solution)/shard_map/ppermute | solution.py:363
  96.0 2.0 %collective-permute-start.20 = (bf16[96,1024]{1,0:T(8,128)(2,1)}, bf16[96,1024]{1,0:T(8,128)(2,1)S(1)}, u32[]{:S(2)}, u32[]{:S(2)}) collective-permute-start(bf16[96,1024]{1,0:T(8,128)(2,1)} %get-tuple-element.68.refs_4_), channel_id=1, source_target_pairs={{0,1},{1,0},{2,3},{3,2},{4,5},{5,4},{6,7},{7,6},{8,9},{9,8},{10,11... | collective-permute-start | bytes 589832 | tf_op jit(solution)/shard_map/ppermute | solution.py:363
  98.1 0.7 copy-start.2
  98.1 0.8 copy-start.1

commit v11 on v10

--- a/solution.py
+++ b/solution.py
@@ -15,11 +15,11 @@
 RANK = 16
 
 PIECES = (
-    *((0, 0, 0), (1, 0, 0), (0, 1, 0), (2, 0, 0), (0, 0, 1), (0, 1, 1), (2, 0, 1)),
-    *((1, 1, 0), (3, 0, 0), (2, 1, 0), (3, 1, 0), (1, 0, 1), (1, 1, 1)),
-    *((3, 0, 1), (2, 1, 1), (3, 1, 1)),
+    *((0, 0, 0), (1, 0, 0), (0, 1, 0), (2, 0, 0)),
+    *((1, 1, 0), (3, 0, 0), (2, 1, 0), (3, 1, 0), (0, 0, 1), (0, 1, 1), (2, 0, 1), (1, 0, 1)),
+    *((1, 1, 1), (3, 0, 1), (2, 1, 1), (3, 1, 1)),
 )
-KERNEL_BOUNDS = (0, 7, 13, 16)
+KERNEL_BOUNDS = (0, 4, 12, 16)
 QUARTER_CUTS = (0, 512, 1024, 2048)
 VMEM_BYTES = 64 * 1024 * 1024 - 512 * 1024
 
@@ -124,6 +124,29 @@
         ],
         compiler_params=params(),
     )(info, here, there, up)
+
+
+def copy_kernel(info_ref, in_ref, out_ref):
+    out_ref[...] = in_ref[...]
+
+
+def half_for_partner(info, tokens):
+    rows, depth = tokens.shape
+    height = rows // 4
+    return pl.pallas_call(
+        copy_kernel,
+        out_shape=jax.ShapeDtypeStruct((rows, depth // 2), tokens.dtype),
+        grid_spec=pltpu.PrefetchScalarGridSpec(
+            num_scalar_prefetch=1,
+            grid=(rows // height,),
+            in_specs=[pl.BlockSpec((height, depth // 2), lambda n, info: (n, 1 - info[1]))],
+            out_specs=pl.BlockSpec((height, depth // 2), lambda n, info: (n, 0)),
+        ),
+        cost_estimate=pl.CostEstimate(
+            flops=0, bytes_accessed=2 * rows * depth, transcendentals=0
+        ),
+        compiler_params=params(),
+    )(info, tokens)
 
 
 def base_kernel(steps, tokens_ref, weight_ref, *refs):
@@ -178,15 +201,14 @@
     )(tokens, weight, *([total] if more else []))
 
 
-def absorb_kernel(
-    groups, start, more, info_ref, row_slot_ref, tokens_ref, other_ref, *refs
-):
+def absorb_kernel(groups, start, sides, more, has_up, info_ref, row_slot_ref, *refs):
     count = sum(size for size, _ in groups)
-    sources, refs = refs[:count], refs[count:]
-    before, refs = refs[: 2 * more], refs[2 * more :]
-    outs, up_ref, rows_ref, refs = refs[:2], refs[2], refs[3], refs[4:]
-    down_refs, sems = refs[: len(groups)], refs[len(groups)]
-    rows = tokens_ref.shape[0]
+    token_refs, sources, refs = refs[: len(sides)], refs[len(sides) :][:count], refs[len(sides) + count :]
+    before, refs = refs[: len(sides) * more], refs[len(sides) * more :]
+    outs, refs = refs[: len(sides)], refs[len(sides) :]
+    up_ref, refs = (refs[0], refs[1:]) if has_up else (None, refs)
+    rows_ref, down_refs, sems = refs[0], refs[1:-1], refs[-1]
+    rows = token_refs[0].shape[0]
     quarter = rows_ref.shape[2]
     y, core = info_ref[0], info_ref[1]
     cuts = list(zip(QUARTER_CUTS, QUARTER_CUTS[1:]))
@@ -203,8 +225,7 @@
     for n, ((size, back), down_ref) in enumerate(zip(groups, down_refs)):
         load = back not in places
         place = places.setdefault(back, len(places))
-        column = (2 * core + (1 - y if back else y)) * quarter
-        ends = cuts + [(quarter, sources[0].shape[0])]
+        ends = cuts + [(quarter, sources[0].shape[0])] * has_up
         for low, high in ends:
             for i in range(size):
                 begin(
@@ -214,15 +235,20 @@
                 )
             if not load or low == quarter:
                 continue
-            columns = pl.ds(pl.multiple_of(column + low, QUARTER_CUTS[1]), high - low)
-            for i, source in enumerate((tokens_ref, other_ref)):
+            for i, (side, source) in enumerate(zip(sides, token_refs)):
+                column = (1 - y if back else y) * quarter + low
+                if side == 0:
+                    column += core * 2 * quarter
                 begin(
                     (n, low),
-                    source.at[:, columns],
+                    source.at[:, pl.ds(pl.multiple_of(column, QUARTER_CUTS[1]), high - low)],
                     rows_ref.at[place, pl.ds(i * rows, rows), pl.ds(low, high - low)],
                 )
         first += size
     lane_slot = lax.broadcasted_iota(jnp.int32, (1, LANES), 1) // RANK
+    row_slot = jnp.concatenate(
+        [row_slot_ref[side * rows : (side + 1) * rows] for side in sides], axis=0
+    )
     state = None
     first = 0
     for n, ((size, back), down_ref) in enumerate(zip(groups, down_refs)):
@@ -235,56 +261,62 @@
                 preferred_element_type=jnp.float32,
             )
             shrink = part if shrink is None else shrink + part
-        awaited(waits[n, quarter])
-        height = up_ref.shape[0] // count
         for i in range(size):
             lanes, which = slice(i * LANES, (i + 1) * LANES), first + i
             chip = info_ref[2 + 2 * len(PIECES) + start + which]
             wanted = lane_slot + chip * (LANES // RANK)
-            kept = jnp.where(row_slot_ref[...] == wanted, shrink[:, lanes], 0.0)
+            kept = jnp.where(row_slot == wanted, shrink[:, lanes], 0.0)
             state = kept if state is None else state + kept
-            for j in range(up_ref.shape[1] // LANES):
-                top = quarter + j * height
-                up_ref[
-                    which * height : (which + 1) * height, j * LANES : (j + 1) * LANES
-                ] = down_ref[top : top + height, lanes]
+        if has_up:
+            awaited(waits[n, quarter])
+            height = up_ref.shape[0] // count
+            for i in range(size):
+                lanes, which = slice(i * LANES, (i + 1) * LANES), first + i
+                for j in range(up_ref.shape[1] // LANES):
+                    top = quarter + j * height
+                    up_ref[
+                        which * height : (which + 1) * height, j * LANES : (j + 1) * LANES
+                    ] = down_ref[top : top + height, lanes]
         first += size
     for i, out_ref in enumerate(outs):
         own = state[i * rows : (i + 1) * rows]
         out_ref[...] = own + before[i][...] if more else own
 
 
-def absorb(info, row_slots, tokens, other, width, groups, start, before):
-    rows, depth = tokens.shape
+def absorb(info, row_slots, sides, tokens, width, groups, start, before, has_up):
+    rows = tokens[0].shape[0]
     pieces = [piece for group, _ in groups for piece in group]
     sizes = [(len(group), back) for group, back in groups]
-    quarter = depth // 4
+    quarter = tokens[-1].shape[1] // (4 if sides == (0,) else 2)
     height = pieces[0].shape[0]
     anywhere = pl.BlockSpec(memory_space=pl.ANY)
     vmem = pl.BlockSpec(memory_space=pltpu.VMEM)
     more = before is not None
     state = jax.ShapeDtypeStruct((rows, LANES), jnp.float32)
     up_rows = len(pieces) * (height - quarter) * LANES // width
+    up = jax.ShapeDtypeStruct((up_rows, width), tokens[0].dtype)
     quarters = len({back for _, back in groups})
     cuts = len(QUARTER_CUTS) - 1
-    copies = len(pieces) * (cuts + 1) + 2 * quarters * cuts
+    copies = len(pieces) * (cuts + has_up) + len(sides) * quarters * cuts
+    outs = (state,) * len(sides) + (up,) * has_up
     return pl.pallas_call(
-        functools.partial(absorb_kernel, sizes, start, more),
-        out_shape=(state, state, jax.ShapeDtypeStruct((up_rows, width), tokens.dtype)),
+        functools.partial(absorb_kernel, sizes, start, sides, more, has_up),
+        out_shape=outs,
         in_specs=[pl.BlockSpec(memory_space=pltpu.SMEM), vmem]
-        + [anywhere] * (2 + len(pieces))
-        + [vmem] * (2 * more),
-        out_specs=(vmem, vmem, vmem),
-        scratch_shapes=[pltpu.VMEM((quarters, 2 * rows, quarter), tokens.dtype)]
-        + [pltpu.VMEM((height, size * LANES), tokens.dtype) for size, _ in sizes]
+        + [anywhere] * (len(sides) + len(pieces))
+        + [vmem] * (len(sides) * more),
+        out_specs=(vmem,) * len(outs),
+        scratch_shapes=[pltpu.VMEM((quarters, len(sides) * rows, quarter), tokens[0].dtype)]
+        + [pltpu.VMEM((height, size * LANES), tokens[0].dtype) for size, _ in sizes]
         + [pltpu.SemaphoreType.DMA((copies,))],
         cost_estimate=pl.CostEstimate(
-            flops=4 * rows * len(pieces) * LANES * quarter,
-            bytes_accessed=4 * rows * quarters * quarter + 2 * len(pieces) * LANES * height,
+            flops=2 * len(sides) * rows * len(pieces) * LANES * quarter,
+            bytes_accessed=2 * len(sides) * rows * quarters * quarter
+            + 2 * len(pieces) * LANES * height,
             transcendentals=0,
         ),
         compiler_params=params(),
-    )(info, row_slots, tokens, other, *pieces, *(before or ()))
+    )(info, row_slots, *tokens, *pieces, *(before or ()))
 
 
 def finish_kernel(
@@ -399,7 +431,7 @@
 
     there = core_swap(adapter_down_weight)
     row_slot = slots_of_rows(row_adapter_index, adapter_storage_slot)
-    there, info, row_slot, tokens_late = together(there, info, row_slot, tokens)
+    there, info, row_slot = together(there, info, row_slot)
 
     def piece(back, *others):
         return assemble(
@@ -414,14 +446,15 @@
         return base_part(after(tokens, *others), base_value_weight, low, high, before)
 
     z1, x0 = z_ring(front), x_swap(front)
-    other = core_swap(tokens_late)
     other_slot = core_swap(row_slot[:, 0])
     total = base(0, None, front)
+    half = half_for_partner(after(info, total), tokens)
+    other = core_swap(half)
     row_slots = jnp.concatenate([row_slot, other_slot[:, None]], axis=0)
 
-    z2 = z_ring(after(z1, total))
-    x1 = x_swap(after(z1, x0, total))
-    yx0 = y_swap(after(x0, total))
+    z2 = z_ring(after(z1, half))
+    x1 = x_swap(after(z1, x0, half))
+    yx0 = y_swap(after(x0, half))
     total = base(1, total, z1, x0, total, row_slots)
 
     z3 = z_back(after(front, z2, total))
@@ -429,36 +462,47 @@
     yz2 = y_swap(after(z2, yx0, total))
     back = piece(1, z2, x1, yx0, total)
     total = base(2, total, z2, x1, yx0, back, other)
-    ups = []
-
-    def update(number, groups, before, *others):
-        mine, others, up = absorb(
+
+    def update(number, sides, groups, before, has_up, *others):
+        return absorb(
             after(info, *others),
             row_slots,
-            tokens,
-            other,
+            sides,
+            [(tokens, other)[side] for side in sides],
             width,
             groups,
             KERNEL_BOUNDS[number],
             before,
+            has_up,
         )
-        ups.extend([up, core_swap(up)])
-        return mine, others
 
     zb1 = z_ring(after(back, z3, total))
     x3 = x_swap(after(z3, x2, total))
     yx1 = y_swap(after(x1, yz2, total))
-    state = update(
-        0, [((front, z1, x0, z2), 0), ((back, yx0, yz2), 1)], None, z3, x2, yz2, total
-    )
+    *state, up_a = update(0, (0, 1), [((front, z1, x0, z2), 0)], None, True, z3, x2, yz2, total)
+    there_a = core_swap(up_a)
 
     zb3 = z_back(after(back, zb1, state[0]))
     xyz2 = x_swap(after(yz2, x3, state[0]))
     yx3 = y_swap(after(x3, yx1, state[0]))
-    state = update(1, [((x1, z3, x2, x3), 0), ((zb1, yx1), 1)], state, zb1, x3, yx1)
-
-    mine, others = update(2, [((zb3, xyz2, yx3), 1)], state, ups[1], ups[3])
-    return finish(info, row_slots, mine, core_swap(others), total, ups)
+    *state, up_b = update(
+        1,
+        (0, 1),
+        [((x1, z3, x2, x3), 0), ((back, yx0, yz2, zb1), 1)],
+        state,
+        True,
+        zb1,
+        x3,
+        yx1,
+    )
+    there_b = core_swap(up_b)
+
+    last = [((yx1, zb3, xyz2, yx3), 1)]
+    others, up_c = update(2, (1,), last, state[1:], True)
+    theirs, there_c = core_swap(others), core_swap(up_c)
+    (mine,) = update(2, (0,), last, state[:1], False, others, there_a, there_b)
+    ups = (up_a, there_a, up_b, there_b, up_c, there_c)
+    return finish(info, row_slots, mine, theirs, total, ups)
 
 
 def solution(mesh):

time: 106 us -> 117 us (1.10)
  waiting for transfers between devices: 15.9 us -> 24 us
  Pallas kernels: 64.2 us -> 67.2 us
    ppermute x21, waiting for transfers between devices: 15.9 us -> 24 us  [permuted(): return lax.ppermute(array, axes, pairs)]
    pallas_call x3 -> x5, Pallas kernels: 28.6 us -> 31.6 us  [the longest x4 26.2 us: absorb(): pl.pallas_call(functools.partial(absorb_kernel, sizes, start, sides, more...]
  transfers between devices with their start and end apart: 21 -> 21, of which waited for: 9 -> 8; matrix products, arithmetic and copies ran while one was open for 3% -> 3% of each run, Pallas kernels for 48% -> 38%
where the time goes in v11:
time: 117 us; the launch traced here: 116 us
  Pallas kernels  67.2 us (57%)
  waiting for transfers between devices  24 us (21%)
  starting transfers between devices  21.7 us (19%)
  local copies, waits for them, and re-layouts  2.23 us (2%)
    pallas_call x4, Pallas kernels, absorb(): pl.pallas_call(functools.partial(absorb_kernel, sizes, start, sides, more...  26.2 us
    ppermute x21, waiting for transfers between devices, permuted(): return lax.ppermute(array, axes, pairs)  24 us
    pallas_call x3, Pallas kernels, base_part(): pl.pallas_call(functools.partial(base_kernel, steps), out_shape=result, g...  22.8 us
    ppermute x21, starting transfers between devices, permuted(): return lax.ppermute(array, axes, pairs)  21.7 us
    pallas_call x1, Pallas kernels, finish(): pl.pallas_call(functools.partial(finish_kernel, len(ups)), out_shape=jax....  6.86 us
    pallas_call x2, Pallas kernels, assemble(): pl.pallas_call(functools.partial(assemble_kernel, back), out_shape=jax.Sh...  5.94 us
    pallas_call x1, Pallas kernels, half_for_partner(): pl.pallas_call(copy_kernel, out_shape=jax.ShapeDtypeStruct((rows, depth /...  5.45 us
  transfers between devices with their start and end apart: 21, of which 8 were waited for; matrix products, arithmetic and copies ran while one was open for 3% of the time, Pallas kernels for 38%

profile of v11, /device:TPU:0, one launch (start us, length us, event | category | flops | bytes accessed | tf_op | source)
XLA Modules:
  0.0 116.2 jit_solution(16140576134695311510)
XLA Ops:
  0.0 0.5 collective-permute-start
  0.5 1.2 %dynamic-slice_bitcast_fusion.info_ref = s32[50]{0:T(128)} fusion(s32[32,50]{1,0:T(8,128)} %constant.20.clone, s32[]{:T(128)S(6)} %select_n.8), kind=kLoop, calls=%fused_computation.3 | loop fusion | bytes 404 | tf_op jit(solution)/shard_map/jit(dynamic_index_in_dim)/squeeze | solution.py:422
  1.7 0.8 select_reduce_fusion
  2.4 0.6 collective-permute-done.there_ref
  3.1 3.0 %shard_map.73.refs_2_ = bf16[2304,128]{1,0:T(8,128)(2,1)} custom-call(s32[50]{0:T(128)} %dynamic-slice_bitcast_fusion.info_ref, bf16[4,16,8192]{2,1,0:T(8,128)(2,1)} %here_ref.3, bf16[4,16,8192]{2,1,0:T(8,128)(2,1)} %collective-permute-done.there_ref, bf16[4,16,1024]{2,1,0:T(8,128)(2,1)} %up_ref.3), custom_call_target="tpu_custom_call" | custom-call | tf_op jit(solution)/shard_map/pallas_call | solution.py:116
  6.1 8.1 %shard_map.74.refs_0_ = f32[512,1024]{1,0:T(8,128)} custom-call(bf16[512,8192]{1,0:T(8,128)(2,1)} %refs_0_.5, bf16[8192,1024]{1,0:T(8,128)(2,1)} %weight_ref.5), custom_call_target="tpu_custom_call" | custom-call | flops 3221225472 | bytes 11534336 | tf_op jit(solution)/shard_map/pallas_call | solution.py:182
  14.1 5.5 %shard_map.75 = bf16[512,4096]{1,0:T(8,128)(2,1)} custom-call(s32[50]{0:T(128)} %dynamic-slice_bitcast_fusion.info_ref, bf16[512,8192]{1,0:T(8,128)(2,1)} %refs_0_.5), custom_call_target="tpu_custom_call" | custom-call | bytes 8388608 | tf_op jit(solution)/shard_map/pallas_call | solution.py:136
  19.6 0.4 collective-permute-start.2
  20.0 2.7 %collective-permute-start.3 = (bf16[2304,128]{1,0:T(8,128)(2,1)}, bf16[2304,128]{1,0:T(8,128)(2,1)}, u32[]{:S(2)}, u32[]{:S(2)}) collective-permute-start(bf16[2304,128]{1,0:T(8,128)(2,1)} %shard_map.73.refs_2_), channel_id=1, source_target_pairs={{0,4},{1,5},{2,6},{3,7},{4,12},{5,13},{6,14},{7,15},{8,0},{9,1},{1... | collective-permute-start | bytes 1769480 | tf_op jit(solution)/shard_map/ppermute | solution.py:395
  22.7 1.5 %collective-permute-start.4 = (bf16[2304,128]{1,0:T(8,128)(2,1)}, bf16[2304,128]{1,0:T(8,128)(2,1)}, u32[]{:S(2)}, u32[]{:S(2)}) collective-permute-start(bf16[2304,128]{1,0:T(8,128)(2,1)} %shard_map.73.refs_2_), channel_id=1, source_target_pairs={{0,2},{1,3},{2,0},{3,1},{4,6},{5,7},{6,4},{7,5},{8,10},{9,11},{10,... | collective-permute-start | bytes 1769480 | tf_op jit(solution)/shard_map/ppermute | solution.py:395
  24.2 13.7 %collective-permute-done.3.refs_3_ = bf16[2304,128]{1,0:T(8,128)(2,1)} collective-permute-done((bf16[2304,128]{1,0:T(8,128)(2,1)}, bf16[2304,128]{1,0:T(8,128)(2,1)}, u32[]{:S(2)}, u32[]{:S(2)}) %collective-permute-start.3) | collective-permute-done | bytes 589856 | tf_op jit(solution)/shard_map/ppermute | solution.py:395
  37.9 0.8 collective-permute-start.6
  38.7 0.0 collective-permute-done.4.refs_4_
  38.7 1.5 %collective-permute-start.5 = (bf16[2304,128]{1,0:T(8,128)(2,1)}, bf16[2304,128]{1,0:T(8,128)(2,1)}, u32[]{:S(2)}, u32[]{:S(2)}) collective-permute-start(bf16[2304,128]{1,0:T(8,128)(2,1)} %collective-permute-done.3.refs_3_), channel_id=1, source_target_pairs={{0,2},{1,3},{2,0},{3,1},{4,6},{5,7},{6,4},{7,5},{8,10},{9,11},{10,... | collective-permute-start | bytes 1769480 | tf_op jit(solution)/shard_map/ppermute | solution.py:395
  40.2 1.5 %collective-permute-start.7 = (bf16[2304,128]{1,0:T(8,128)(2,1)}, bf16[2304,128]{1,0:T(8,128)(2,1)}, u32[]{:S(2)}, u32[]{:S(2)}) collective-permute-start(bf16[2304,128]{1,0:T(8,128)(2,1)} %collective-permute-done.4.refs_4_), channel_id=1, source_target_pairs={{0,16},{1,17},{2,18},{3,19},{4,20},{5,21},{6,22},{7,23},{8,24},{9,... | collective-permute-start | bytes 1769480 | tf_op jit(solution)/shard_map/ppermute | solution.py:395
  41.7 0.0 collective-permute-start.1
  41.7 1.2 collective-permute-done.1
  42.9 8.3 %shard_map.76.refs_0_ = f32[512,1024]{1,0:T(8,128)} custom-call(bf16[512,8192]{1,0:T(8,128)(2,1)} %refs_0_.5, bf16[8192,1024]{1,0:T(8,128)(2,1)} %weight_ref.5, f32[512,1024]{1,0:T(8,128)} %shard_map.74.refs_0_), custom_call_target="tpu_custom_call" | custom-call | flops 3221225472 | bytes 11534336 | tf_op jit(solution)/shard_map/pallas_call | solution.py:182
  51.2 2.9 %collective-permute-done.6.refs_5_ = bf16[2304,128]{1,0:T(8,128)(2,1)} collective-permute-done((bf16[2304,128]{1,0:T(8,128)(2,1)}, bf16[2304,128]{1,0:T(8,128)(2,1)}, u32[]{:S(2)}, u32[]{:S(2)}) %collective-permute-start.6) | collective-permute-done | bytes 589856 | tf_op jit(solution)/shard_map/ppermute | solution.py:395
  54.1 1.3 %collective-permute-start.10 = (bf16[2304,128]{1,0:T(8,128)(2,1)}, bf16[2304,128]{1,0:T(8,128)(2,1)}, u32[]{:S(2)}, u32[]{:S(2)}) collective-permute-start(bf16[2304,128]{1,0:T(8,128)(2,1)} %shard_map.73.refs_2_), channel_id=1, source_target_pairs={{0,8},{1,9},{2,10},{3,11},{4,0},{5,1},{6,2},{7,3},{8,12},{9,13},{1... | collective-permute-start | bytes 1769480 | tf_op jit(solution)/shard_map/ppermute | solution.py:395
  55.5 0.0 collective-permute-done.5.refs_2_
  55.5 1.5 %collective-permute-start.12 = (bf16[2304,128]{1,0:T(8,128)(2,1)}, bf16[2304,128]{1,0:T(8,128)(2,1)}, u32[]{:S(2)}, u32[]{:S(2)}) collective-permute-start(bf16[2304,128]{1,0:T(8,128)(2,1)} %collective-permute-done.6.refs_5_), channel_id=1, source_target_pairs={{0,2},{1,3},{2,0},{3,1},{4,6},{5,7},{6,4},{7,5},{8,10},{9,11},{10,... | collective-permute-start | bytes 1769480 | tf_op jit(solution)/shard_map/ppermute | solution.py:395
  57.0 0.0 collective-permute-done.7.refs_7_
  57.0 1.5 %collective-permute-start.8 = (bf16[2304,128]{1,0:T(8,128)(2,1)}, bf16[2304,128]{1,0:T(8,128)(2,1)}, u32[]{:S(2)}, u32[]{:S(2)}) collective-permute-start(bf16[2304,128]{1,0:T(8,128)(2,1)} %collective-permute-done.6.refs_5_), channel_id=1, source_target_pairs={{0,16},{1,17},{2,18},{3,19},{4,20},{5,21},{6,22},{7,23},{8,24},{9,... | collective-permute-start | bytes 1769480 | tf_op jit(solution)/shard_map/ppermute | solution.py:395
  58.5 3.0 %shard_map.77.refs_6_ = bf16[2304,128]{1,0:T(8,128)(2,1)} custom-call(s32[50]{0:T(128)} %dynamic-slice_bitcast_fusion.info_ref, bf16[4,16,8192]{2,1,0:T(8,128)(2,1)} %here_ref.3, bf16[4,16,8192]{2,1,0:T(8,128)(2,1)} %collective-permute-done.there_ref, bf16[4,16,1024]{2,1,0:T(8,128)(2,1)} %up_ref.3), custom_call_target="tpu_custom_call" | custom-call | tf_op jit(solution)/shard_map/pallas_call | solution.py:116
  61.5 0.0 collective-permute-done.2.refs_1_.refs_0_
  61.5 6.4 %shard_map.78.total_ref = f32[512,1024]{1,0:T(8,128)} custom-call(bf16[512,8192]{1,0:T(8,128)(2,1)} %refs_0_.5, bf16[8192,1024]{1,0:T(8,128)(2,1)} %weight_ref.5, f32[512,1024]{1,0:T(8,128)} %shard_map.76.refs_0_), custom_call_target="tpu_custom_call" | custom-call | flops 2147483648 | bytes 8388608 | tf_op jit(solution)/shard_map/pallas_call | solution.py:182
  67.8 0.8 collective-permute-done.10.refs_3_
  68.7 2.7 %collective-permute-start.11 = (bf16[2304,128]{1,0:T(8,128)(2,1)}, bf16[2304,128]{1,0:T(8,128)(2,1)}, u32[]{:S(2)}, u32[]{:S(2)}) collective-permute-start(bf16[2304,128]{1,0:T(8,128)(2,1)} %shard_map.77.refs_6_), channel_id=1, source_target_pairs={{0,4},{1,5},{2,6},{3,7},{4,12},{5,13},{6,14},{7,15},{8,0},{9,1},{1... | collective-permute-start | bytes 1769480 | tf_op jit(solution)/shard_map/ppermute | solution.py:395
  71.3 0.0 collective-permute-done.12.refs_4_
  71.3 0.7 collective-permute-start.14
  72.0 0.0 collective-permute-done.8.refs_8_
  72.0 1.5 %collective-permute-start.9 = (bf16[2304,128]{1,0:T(8,128)(2,1)}, bf16[2304,128]{1,0:T(8,128)(2,1)}, u32[]{:S(2)}, u32[]{:S(2)}) collective-permute-start(bf16[2304,128]{1,0:T(8,128)(2,1)} %collective-permute-done.5.refs_2_), channel_id=1, source_target_pairs={{0,16},{1,17},{2,18},{3,19},{4,20},{5,21},{6,22},{7,23},{8,24},{9,... | collective-permute-start | bytes 1769480 | tf_op jit(solution)/shard_map/ppermute | solution.py:395
  73.6 1.0 copy.19.row_slot_ref
  74.6 6.5 %shard_map.79 = (f32[512,128]{1,0:T(8,128)}, f32[512,128]{1,0:T(8,128)}, bf16[128,1024]{1,0:T(8,128)(2,1)}) custom-call(s32[50]{0:T(128)} %dynamic-slice_bitcast_fusion.info_ref, s32[1024,1]{1,0:T(8,128)} %copy.19.row_slot_ref, bf16[512,8192]{1,0:T(8,128)(2,1)} %refs_0_.5, bf16[512,4096]{1,0:T(8,128)(2,1)} %collective-permute-done.2.refs_1_.refs_0_, ...), custom_call_target="tpu_custom_call" | custom-call | flops 2147483648 | bytes 6553600 | tf_op jit(solution)/shard_map/pallas_call | solution.py:302
  81.1 3.1 %collective-permute-done.11.refs_9_ = bf16[2304,128]{1,0:T(8,128)(2,1)} collective-permute-done((bf16[2304,128]{1,0:T(8,128)(2,1)}, bf16[2304,128]{1,0:T(8,128)(2,1)}, u32[]{:S(2)}, u32[]{:S(2)}) %collective-permute-start.11) | collective-permute-done | bytes 589856 | tf_op jit(solution)/shard_map/ppermute | solution.py:395
  84.2 0.3 collective-permute-start.13
  84.5 0.9 collective-permute-done.14.refs_5_
  85.3 0.6 collective-permute-start.15
  86.0 0.0 collective-permute-done.9.refs_1_
  86.0 1.5 %collective-permute-start.16 = (bf16[2304,128]{1,0:T(8,128)(2,1)}, bf16[2304,128]{1,0:T(8,128)(2,1)}, u32[]{:S(2)}, u32[]{:S(2)}) collective-permute-start(bf16[2304,128]{1,0:T(8,128)(2,1)} %collective-permute-done.14.refs_5_), channel_id=1, source_target_pairs={{0,16},{1,17},{2,18},{3,19},{4,20},{5,21},{6,22},{7,23},{8,24},{9,... | collective-permute-start | bytes 1769480 | tf_op jit(solution)/shard_map/ppermute | solution.py:395
  87.5 0.0 copy-start
  87.5 9.6 %shard_map.80 = (f32[512,128]{1,0:T(8,128)}, f32[512,128]{1,0:T(8,128)}, bf16[256,1024]{1,0:T(8,128)(2,1)}) custom-call(s32[50]{0:T(128)} %dynamic-slice_bitcast_fusion.info_ref, s32[1024,1]{1,0:T(8,128)} %copy.19.row_slot_ref, bf16[512,8192]{1,0:T(8,128)(2,1)} %refs_0_.5, bf16[512,4096]{1,0:T(8,128)(2,1)} %collective-permute-done.2.refs_1_.refs_0_, ...), custom_call_target="tpu_custom_call" | custom-call | flops 4294967296 | bytes 13107200 | tf_op jit(solution)/shard_map/pallas_call | solution.py:302
  97.1 0.1 collective-permute-start.18
  97.1 0.0 copy-done
  97.2 0.5 collective-permute-start.17
  97.6 0.0 collective-permute-done.13.refs_2_
  97.6 0.8 collective-permute-done.15.refs_3_
  98.4 0.0 collective-permute-done.16.refs_4_
  98.4 5.1 %shard_map.81 = (f32[512,128]{1,0:T(8,128)}, bf16[128,1024]{1,0:T(8,128)(2,1)}) custom-call(s32[50]{0:T(128)} %dynamic-slice_bitcast_fusion.info_ref, s32[1024,1]{1,0:T(8,128)} %copy.19.row_slot_ref, bf16[512,4096]{1,0:T(8,128)(2,1)} %collective-permute-done.2.refs_1_.refs_0_, bf16[2304,128]{1,0:T(8,128)(2,1)} %collective-permute-done.9.refs_1_, ...), custom_call_target="tpu_custom_call" | custom-call | flops 1073741824 | bytes 4456448 | tf_op jit(solution)/shard_map/pallas_call | solution.py:302
  103.6 0.1 collective-permute-start.19
  103.7 0.5 collective-permute-start.20
  104.2 0.0 collective-permute-done.17.refs_1_
  104.2 0.0 collective-permute-done.18.refs_3_
  104.2 5.0 %shard_map.82.mine_ref = f32[512,128]{1,0:T(8,128)} custom-call(s32[50]{0:T(128)} %dynamic-slice_bitcast_fusion.info_ref, s32[1024,1]{1,0:T(8,128)} %copy.19.row_slot_ref, bf16[512,8192]{1,0:T(8,128)(2,1)} %refs_0_.5, bf16[2304,128]{1,0:T(8,128)(2,1)} %collective-permute-done.9.refs_1_, bf16[2304,128]{1,0:T(8,128)(2,1)} %collective-permute-done.13.refs_2_, ...), custom_call_target="tpu_custom_call" | custom-call | flops 1073741824 | bytes 4456448 | tf_op jit(solution)/shard_map/pallas_call | solution.py:302
  109.1 0.0 collective-permute-done.19.theirs_ref
  109.2 0.0 collective-permute-done.20.refs_5_
  109.2 6.9 %shard_map.83 = bf16[512,1024]{1,0:T(8,128)(2,1)} custom-call(s32[50]{0:T(128)} %dynamic-slice_bitcast_fusion.info_ref, s32[1024,1]{1,0:T(8,128)} %copy.19.row_slot_ref, f32[512,128]{1,0:T(8,128)} %shard_map.82.mine_ref, f32[512,128]{1,0:T(8,128)} %collective-permute-done.19.theirs_ref, f32[512,1024]{1,0:T(8,128)} %shard_map.78.total_ref, ...), custom_call_target="tpu_custom_call" | custom-call | flops 2147483648 | bytes 5242880 | tf_op jit(solution)/shard_map/pallas_call | solution.py:356
  (1 shorter events, 0.0 us)
Async XLA Ops:
  0.0 3.1 %collective-permute-start = (bf16[4,16,8192]{2,1,0:T(8,128)(2,1)}, bf16[4,16,8192]{2,1,0:T(8,128)(2,1)}, u32[]{:S(2)}, u32[]{:S(2)}) collective-permute-start(bf16[4,16,8192]{2,1,0:T(8,128)(2,1)} %here_ref.3), channel_id=1, source_target_pairs={{0,1},{1,0},{2,3},{3,2},{4,5},{5,4},{6,7},{7,6},{8,9},{9,8},{10,11... | collective-permute-start | bytes 3145736 | tf_op jit(solution)/shard_map/ppermute | solution.py:395
  19.6 41.9 %collective-permute-start.2 = (bf16[512,4096]{1,0:T(8,128)(2,1)}, bf16[512,4096]{1,0:T(8,128)(2,1)}, u32[]{:S(2)}, u32[]{:S(2)}) collective-permute-start(bf16[512,4096]{1,0:T(8,128)(2,1)} %shard_map.75), channel_id=1, source_target_pairs={{0,1},{1,0},{2,3},{3,2},{4,5},{5,4},{6,7},{7,6},{8,9},{9,8},{10,11... | collective-permute-start | bytes 12582920 | tf_op jit(solution)/shard_map/ppermute | solution.py:395
  20.0 17.9 %collective-permute-start.3 = (bf16[2304,128]{1,0:T(8,128)(2,1)}, bf16[2304,128]{1,0:T(8,128)(2,1)}, u32[]{:S(2)}, u32[]{:S(2)}) collective-permute-start(bf16[2304,128]{1,0:T(8,128)(2,1)} %shard_map.73.refs_2_), channel_id=1, source_target_pairs={{0,4},{1,5},{2,6},{3,7},{4,12},{5,13},{6,14},{7,15},{8,0},{9,1},{1... | collective-permute-start | bytes 1769480 | tf_op jit(solution)/shard_map/ppermute | solution.py:395
  22.7 16.0 %collective-permute-start.4 = (bf16[2304,128]{1,0:T(8,128)(2,1)}, bf16[2304,128]{1,0:T(8,128)(2,1)}, u32[]{:S(2)}, u32[]{:S(2)}) collective-permute-start(bf16[2304,128]{1,0:T(8,128)(2,1)} %shard_map.73.refs_2_), channel_id=1, source_target_pairs={{0,2},{1,3},{2,0},{3,1},{4,6},{5,7},{6,4},{7,5},{8,10},{9,11},{10,... | collective-permute-start | bytes 1769480 | tf_op jit(solution)/shard_map/ppermute | solution.py:395
  37.9 16.2 %collective-permute-start.6 = (bf16[2304,128]{1,0:T(8,128)(2,1)}, bf16[2304,128]{1,0:T(8,128)(2,1)}, u32[]{:S(2)}, u32[]{:S(2)}) collective-permute-start(bf16[2304,128]{1,0:T(8,128)(2,1)} %collective-permute-done.3.refs_3_), channel_id=1, source_target_pairs={{0,4},{1,5},{2,6},{3,7},{4,12},{5,13},{6,14},{7,15},{8,0},{9,1},{1... | collective-permute-start | bytes 1769480 | tf_op jit(solution)/shard_map/ppermute | solution.py:395
  38.7 16.7 %collective-permute-start.5 = (bf16[2304,128]{1,0:T(8,128)(2,1)}, bf16[2304,128]{1,0:T(8,128)(2,1)}, u32[]{:S(2)}, u32[]{:S(2)}) collective-permute-start(bf16[2304,128]{1,0:T(8,128)(2,1)} %collective-permute-done.3.refs_3_), channel_id=1, source_target_pairs={{0,2},{1,3},{2,0},{3,1},{4,6},{5,7},{6,4},{7,5},{8,10},{9,11},{10,... | collective-permute-start | bytes 1769480 | tf_op jit(solution)/shard_map/ppermute | solution.py:395
  40.2 16.7 %collective-permute-start.7 = (bf16[2304,128]{1,0:T(8,128)(2,1)}, bf16[2304,128]{1,0:T(8,128)(2,1)}, u32[]{:S(2)}, u32[]{:S(2)}) collective-permute-start(bf16[2304,128]{1,0:T(8,128)(2,1)} %collective-permute-done.4.refs_4_), channel_id=1, source_target_pairs={{0,16},{1,17},{2,18},{3,19},{4,20},{5,21},{6,22},{7,23},{8,24},{9,... | collective-permute-start | bytes 1769480 | tf_op jit(solution)/shard_map/ppermute | solution.py:395
  41.7 1.2 collective-permute-start.1
  54.1 14.5 %collective-permute-start.10 = (bf16[2304,128]{1,0:T(8,128)(2,1)}, bf16[2304,128]{1,0:T(8,128)(2,1)}, u32[]{:S(2)}, u32[]{:S(2)}) collective-permute-start(bf16[2304,128]{1,0:T(8,128)(2,1)} %shard_map.73.refs_2_), channel_id=1, source_target_pairs={{0,8},{1,9},{2,10},{3,11},{4,0},{5,1},{6,2},{7,3},{8,12},{9,13},{1... | collective-permute-start | bytes 1769480 | tf_op jit(solution)/shard_map/ppermute | solution.py:395
  55.5 15.9 %collective-permute-start.12 = (bf16[2304,128]{1,0:T(8,128)(2,1)}, bf16[2304,128]{1,0:T(8,128)(2,1)}, u32[]{:S(2)}, u32[]{:S(2)}) collective-permute-start(bf16[2304,128]{1,0:T(8,128)(2,1)} %collective-permute-done.6.refs_5_), channel_id=1, source_target_pairs={{0,2},{1,3},{2,0},{3,1},{4,6},{5,7},{6,4},{7,5},{8,10},{9,11},{10,... | collective-permute-start | bytes 1769480 | tf_op jit(solution)/shard_map/ppermute | solution.py:395
  57.0 15.1 %collective-permute-start.8 = (bf16[2304,128]{1,0:T(8,128)(2,1)}, bf16[2304,128]{1,0:T(8,128)(2,1)}, u32[]{:S(2)}, u32[]{:S(2)}) collective-permute-start(bf16[2304,128]{1,0:T(8,128)(2,1)} %collective-permute-done.6.refs_5_), channel_id=1, source_target_pairs={{0,16},{1,17},{2,18},{3,19},{4,20},{5,21},{6,22},{7,23},{8,24},{9,... | collective-permute-start | bytes 1769480 | tf_op jit(solution)/shard_map/ppermute | solution.py:395
  68.7 15.5 %collective-permute-start.11 = (bf16[2304,128]{1,0:T(8,128)(2,1)}, bf16[2304,128]{1,0:T(8,128)(2,1)}, u32[]{:S(2)}, u32[]{:S(2)}) collective-permute-start(bf16[2304,128]{1,0:T(8,128)(2,1)} %shard_map.77.refs_6_), channel_id=1, source_target_pairs={{0,4},{1,5},{2,6},{3,7},{4,12},{5,13},{6,14},{7,15},{8,0},{9,1},{1... | collective-permute-start | bytes 1769480 | tf_op jit(solution)/shard_map/ppermute | solution.py:395
  71.3 14.0 %collective-permute-start.14 = (bf16[2304,128]{1,0:T(8,128)(2,1)}, bf16[2304,128]{1,0:T(8,128)(2,1)}, u32[]{:S(2)}, u32[]{:S(2)}) collective-permute-start(bf16[2304,128]{1,0:T(8,128)(2,1)} %collective-permute-done.10.refs_3_), channel_id=1, source_target_pairs={{0,2},{1,3},{2,0},{3,1},{4,6},{5,7},{6,4},{7,5},{8,10},{9,11},{10,... | collective-permute-start | bytes 1769480 | tf_op jit(solution)/shard_map/ppermute | solution.py:395
  72.0 13.9 %collective-permute-start.9 = (bf16[2304,128]{1,0:T(8,128)(2,1)}, bf16[2304,128]{1,0:T(8,128)(2,1)}, u32[]{:S(2)}, u32[]{:S(2)}) collective-permute-start(bf16[2304,128]{1,0:T(8,128)(2,1)} %collective-permute-done.5.refs_2_), channel_id=1, source_target_pairs={{0,16},{1,17},{2,18},{3,19},{4,20},{5,21},{6,22},{7,23},{8,24},{9,... | collective-permute-start | bytes 1769480 | tf_op jit(solution)/shard_map/ppermute | solution.py:395
  84.2 13.5 %collective-permute-start.13 = (bf16[2304,128]{1,0:T(8,128)(2,1)}, bf16[2304,128]{1,0:T(8,128)(2,1)}, u32[]{:S(2)}, u32[]{:S(2)}) collective-permute-start(bf16[2304,128]{1,0:T(8,128)(2,1)} %shard_map.77.refs_6_), channel_id=1, source_target_pairs={{0,8},{1,9},{2,10},{3,11},{4,0},{5,1},{6,2},{7,3},{8,12},{9,13},{1... | collective-permute-start | bytes 1769480 | tf_op jit(solution)/shard_map/ppermute | solution.py:395
  85.3 13.1 %collective-permute-start.15 = (bf16[2304,128]{1,0:T(8,128)(2,1)}, bf16[2304,128]{1,0:T(8,128)(2,1)}, u32[]{:S(2)}, u32[]{:S(2)}) collective-permute-start(bf16[2304,128]{1,0:T(8,128)(2,1)} %collective-permute-done.8.refs_8_), channel_id=1, source_target_pairs={{0,2},{1,3},{2,0},{3,1},{4,6},{5,7},{6,4},{7,5},{8,10},{9,11},{10,... | collective-permute-start | bytes 1769480 | tf_op jit(solution)/shard_map/ppermute | solution.py:395
  86.0 12.5 %collective-permute-start.16 = (bf16[2304,128]{1,0:T(8,128)(2,1)}, bf16[2304,128]{1,0:T(8,128)(2,1)}, u32[]{:S(2)}, u32[]{:S(2)}) collective-permute-start(bf16[2304,128]{1,0:T(8,128)(2,1)} %collective-permute-done.14.refs_5_), channel_id=1, source_target_pairs={{0,16},{1,17},{2,18},{3,19},{4,20},{5,21},{6,22},{7,23},{8,24},{9,... | collective-permute-start | bytes 1769480 | tf_op jit(solution)/shard_map/ppermute | solution.py:395
  87.5 9.7 %copy-start = (bf16[128,1024]{1,0:T(8,128)(2,1)S(1)}, bf16[128,1024]{1,0:T(8,128)(2,1)}, u32[]{:S(2)}) copy-start(bf16[128,1024]{1,0:T(8,128)(2,1)} %get-tuple-element.62.refs_0_) | copy-start | bytes 786436
  97.1 7.1 %collective-permute-start.18 = (bf16[256,1024]{1,0:T(8,128)(2,1)}, bf16[256,1024]{1,0:T(8,128)(2,1)}, u32[]{:S(2)}, u32[]{:S(2)}) collective-permute-start(bf16[256,1024]{1,0:T(8,128)(2,1)} %get-tuple-element.63.refs_2_), channel_id=1, source_target_pairs={{0,1},{1,0},{2,3},{3,2},{4,5},{5,4},{6,7},{7,6},{8,9},{9,8},{10,11... | collective-permute-start | bytes 1572872 | tf_op jit(solution)/shard_map/ppermute | solution.py:395
  97.2 7.0 %collective-permute-start.17 = (bf16[128,1024]{1,0:T(8,128)(2,1)S(1)}, bf16[128,1024]{1,0:T(8,128)(2,1)}, u32[]{:S(2)}, u32[]{:S(2)}) collective-permute-start(bf16[128,1024]{1,0:T(8,128)(2,1)S(1)} %copy-done), channel_id=1, source_target_pairs={{0,1},{1,0},{2,3},{3,2},{4,5},{5,4},{6,7},{7,6},{8,9},{9,8},{10,11... | collective-permute-start | bytes 786440 | tf_op jit(solution)/shard_map/ppermute | solution.py:395
  103.6 5.6 %collective-permute-start.19 = (f32[512,128]{1,0:T(8,128)}, f32[512,128]{1,0:T(8,128)}, u32[]{:S(2)}, u32[]{:S(2)}) collective-permute-start(f32[512,128]{1,0:T(8,128)} %get-tuple-element.61), channel_id=1, source_target_pairs={{0,1},{1,0},{2,3},{3,2},{4,5},{5,4},{6,7},{7,6},{8,9},{9,8},{10,11... | collective-permute-start | bytes 786440 | tf_op jit(solution)/shard_map/ppermute | solution.py:395
  103.7 5.5 %collective-permute-start.20 = (bf16[128,1024]{1,0:T(8,128)(2,1)}, bf16[128,1024]{1,0:T(8,128)(2,1)}, u32[]{:S(2)}, u32[]{:S(2)}) collective-permute-start(bf16[128,1024]{1,0:T(8,128)(2,1)} %get-tuple-element.66.refs_4_), channel_id=1, source_target_pairs={{0,1},{1,0},{2,3},{3,2},{4,5},{5,4},{6,7},{7,6},{8,9},{9,8},{10,11... | collective-permute-start | bytes 786440 | tf_op jit(solution)/shard_map/ppermute | solution.py:395

commit v12 on v11

--- a/solution.py
+++ b/solution.py
@@ -16,10 +16,11 @@
 
 PIECES = (
     *((0, 0, 0), (1, 0, 0), (0, 1, 0), (2, 0, 0)),
-    *((1, 1, 0), (3, 0, 0), (2, 1, 0), (3, 1, 0), (0, 0, 1), (0, 1, 1), (2, 0, 1), (1, 0, 1)),
-    *((1, 1, 1), (3, 0, 1), (2, 1, 1), (3, 1, 1)),
+    *((1, 1, 0), (3, 0, 0), (2, 1, 0), (3, 1, 0)),
+    *((0, 0, 1), (0, 1, 1), (2, 0, 1), (1, 0, 1), (1, 1, 1)),
+    *((3, 0, 1), (2, 1, 1), (3, 1, 1)),
 )
-KERNEL_BOUNDS = (0, 4, 12, 16)
+KERNEL_BOUNDS = (0, 4, 13, 16)
 QUARTER_CUTS = (0, 512, 1024, 2048)
 VMEM_BYTES = 64 * 1024 * 1024 - 512 * 1024
 
@@ -124,29 +125,6 @@
         ],
         compiler_params=params(),
     )(info, here, there, up)
-
-
-def copy_kernel(info_ref, in_ref, out_ref):
-    out_ref[...] = in_ref[...]
-
-
-def half_for_partner(info, tokens):
-    rows, depth = tokens.shape
-    height = rows // 4
-    return pl.pallas_call(
-        copy_kernel,
-        out_shape=jax.ShapeDtypeStruct((rows, depth // 2), tokens.dtype),
-        grid_spec=pltpu.PrefetchScalarGridSpec(
-            num_scalar_prefetch=1,
-            grid=(rows // height,),
-            in_specs=[pl.BlockSpec((height, depth // 2), lambda n, info: (n, 1 - info[1]))],
-            out_specs=pl.BlockSpec((height, depth // 2), lambda n, info: (n, 0)),
-        ),
-        cost_estimate=pl.CostEstimate(
-            flops=0, bytes_accessed=2 * rows * depth, transcendentals=0
-        ),
-        compiler_params=params(),
-    )(info, tokens)
 
 
 def base_kernel(steps, tokens_ref, weight_ref, *refs):
@@ -235,10 +213,8 @@
                 )
             if not load or low == quarter:
                 continue
-            for i, (side, source) in enumerate(zip(sides, token_refs)):
-                column = (1 - y if back else y) * quarter + low
-                if side == 0:
-                    column += core * 2 * quarter
+            for i, source in enumerate(token_refs):
+                column = (2 * core + (1 - y if back else y)) * quarter + low
                 begin(
                     (n, low),
                     source.at[:, pl.ds(pl.multiple_of(column, QUARTER_CUTS[1]), high - low)],
@@ -287,7 +263,7 @@
     rows = tokens[0].shape[0]
     pieces = [piece for group, _ in groups for piece in group]
     sizes = [(len(group), back) for group, back in groups]
-    quarter = tokens[-1].shape[1] // (4 if sides == (0,) else 2)
+    quarter = tokens[0].shape[1] // 4
     height = pieces[0].shape[0]
     anywhere = pl.BlockSpec(memory_space=pl.ANY)
     vmem = pl.BlockSpec(memory_space=pltpu.VMEM)
@@ -319,31 +295,35 @@
     )(info, row_slots, *tokens, *pieces, *(before or ()))
 
 
-def finish_kernel(
-    count, info_ref, row_slot_ref, mine_ref, theirs_ref, total_ref, *refs
-):
-    sources, (out_ref, total, up, sems) = refs[:count], refs[count:]
+def finish_kernel(count, info_ref, row_slot_ref, mine_ref, theirs_ref, total_ref, *refs):
+    sources, refs = refs[:count], refs[count:]
+    out_ref, row_slot, mine, theirs, total, up, sems = refs
     rows = out_ref.shape[0]
     height = up.shape[0] // (len(PIECES) * 2)
-    copies = [pltpu.make_async_copy(total_ref, total, sems.at[0])]
+    copies = []
+
+    def begin(source, target):
+        copies.append(pltpu.make_async_copy(source, target, sems.at[len(copies)]))
+        copies[-1].start()
+
+    begin(row_slot_ref.at[pl.ds(0, rows)], row_slot)
+    begin(mine_ref, mine)
+    begin(theirs_ref, theirs)
+    begin(total_ref, total)
     for source in sources:
         for n in range(0, source.shape[0], height):
-            first = pl.multiple_of(info_ref[1 + len(copies)], height)
-            copies.append(
-                pltpu.make_async_copy(
-                    source.at[pl.ds(n, height)], up.at[pl.ds(first, height)], sems.at[len(copies)]
-                )
-            )
-    started(copies)
-    shrink = mine_ref[...] + theirs_ref[...]
-    lane_slot = lax.broadcasted_iota(jnp.int32, (rows, LANES), 1) // RANK
+            first = pl.multiple_of(info_ref[len(copies) - 2], height)
+            begin(source.at[pl.ds(n, height)], up.at[pl.ds(first, height)])
+    awaited(copies[:3])
+    shrink = mine[...] + theirs[...]
+    lane_slot = lax.broadcasted_iota(jnp.int32, (1, LANES), 1) // RANK
     high, low = [], []
     for n in range(up.shape[0] // LANES):
-        kept = jnp.where(row_slot_ref[:rows] == lane_slot + n * (LANES // RANK), shrink, 0.0)
+        kept = jnp.where(row_slot[...] == lane_slot + n * (LANES // RANK), shrink, 0.0)
         high.append(kept.astype(jnp.bfloat16))
         low.append((kept - high[-1].astype(jnp.float32)).astype(jnp.bfloat16))
-    awaited(copies)
     both = jnp.concatenate([jnp.concatenate(part, axis=1) for part in (low, high)], axis=0)
+    awaited(copies[3:])
     lora = jnp.dot(both, up[...], preferred_element_type=jnp.float32)
     out_ref[...] = (total[...] + (lora[:rows] + lora[rows:])).astype(out_ref.dtype)
 
@@ -351,18 +331,19 @@
 def finish(info, row_slots, mine, theirs, total, ups):
     rows, width = total.shape
     anywhere = pl.BlockSpec(memory_space=pl.ANY)
-    vmem = pl.BlockSpec(memory_space=pltpu.VMEM)
     up_rows = sum(up.shape[0] for up in ups)
     return pl.pallas_call(
         functools.partial(finish_kernel, len(ups)),
         out_shape=jax.ShapeDtypeStruct((rows, width), jnp.bfloat16),
-        in_specs=[pl.BlockSpec(memory_space=pltpu.SMEM), vmem, vmem, vmem]
-        + [anywhere] * (1 + len(ups)),
-        out_specs=vmem,
+        in_specs=[pl.BlockSpec(memory_space=pltpu.SMEM)] + [anywhere] * (4 + len(ups)),
+        out_specs=pl.BlockSpec(memory_space=pltpu.VMEM),
         scratch_shapes=[
+            pltpu.VMEM((rows, 1), jnp.int32),
+            pltpu.VMEM((rows, LANES), jnp.float32),
+            pltpu.VMEM((rows, LANES), jnp.float32),
             pltpu.VMEM((rows, width), jnp.float32),
             pltpu.VMEM((up_rows, width), ups[0].dtype),
-            pltpu.SemaphoreType.DMA((1 + 2 * len(PIECES),)),
+            pltpu.SemaphoreType.DMA((4 + 2 * len(PIECES),)),
         ],
         cost_estimate=pl.CostEstimate(
             flops=4 * rows * width * up_rows,
@@ -431,7 +412,7 @@
 
     there = core_swap(adapter_down_weight)
     row_slot = slots_of_rows(row_adapter_index, adapter_storage_slot)
-    there, info, row_slot = together(there, info, row_slot)
+    there, info, row_slot, tokens_late = together(there, info, row_slot, tokens)
 
     def piece(back, *others):
         return assemble(
@@ -446,15 +427,14 @@
         return base_part(after(tokens, *others), base_value_weight, low, high, before)
 
     z1, x0 = z_ring(front), x_swap(front)
+    other = core_swap(tokens_late)
     other_slot = core_swap(row_slot[:, 0])
     total = base(0, None, front)
-    half = half_for_partner(after(info, total), tokens)
-    other = core_swap(half)
     row_slots = jnp.concatenate([row_slot, other_slot[:, None]], axis=0)
 
-    z2 = z_ring(after(z1, half))
-    x1 = x_swap(after(z1, x0, half))
-    yx0 = y_swap(after(x0, half))
+    z2 = z_ring(after(z1, total))
+    x1 = x_swap(after(z1, x0, total))
+    yx0 = y_swap(after(x0, total))
     total = base(1, total, z1, x0, total, row_slots)
 
     z3 = z_back(after(front, z2, total))
@@ -463,46 +443,42 @@
     back = piece(1, z2, x1, yx0, total)
     total = base(2, total, z2, x1, yx0, back, other)
 
-    def update(number, sides, groups, before, has_up, *others):
+    def update(number, groups, before, *others):
         return absorb(
             after(info, *others),
             row_slots,
-            sides,
-            [(tokens, other)[side] for side in sides],
+            (0, 1),
+            [tokens, other],
             width,
             groups,
             KERNEL_BOUNDS[number],
             before,
-            has_up,
+            True,
         )
 
     zb1 = z_ring(after(back, z3, total))
     x3 = x_swap(after(z3, x2, total))
     yx1 = y_swap(after(x1, yz2, total))
-    *state, up_a = update(0, (0, 1), [((front, z1, x0, z2), 0)], None, True, z3, x2, yz2, total)
+    *state, up_a = update(0, [((front, z1, x0, z2), 0)], None, z3, x2, yz2, total)
     there_a = core_swap(up_a)
 
-    zb3 = z_back(after(back, zb1, state[0]))
+    zb3 = z_back(after(back, state[0]))
     xyz2 = x_swap(after(yz2, x3, state[0]))
     yx3 = y_swap(after(x3, yx1, state[0]))
     *state, up_b = update(
         1,
-        (0, 1),
-        [((x1, z3, x2, x3), 0), ((back, yx0, yz2, zb1), 1)],
+        [((x1, z3, x2, x3), 0), ((back, yx0, yz2, zb1, yx1), 1)],
         state,
-        True,
         zb1,
         x3,
         yx1,
+        there_a,
     )
     there_b = core_swap(up_b)
 
-    last = [((yx1, zb3, xyz2, yx3), 1)]
-    others, up_c = update(2, (1,), last, state[1:], True)
-    theirs, there_c = core_swap(others), core_swap(up_c)
-    (mine,) = update(2, (0,), last, state[:1], False, others, there_a, there_b)
-    ups = (up_a, there_a, up_b, there_b, up_c, there_c)
-    return finish(info, row_slots, mine, theirs, total, ups)
+    mine, others, up_c = update(2, [((zb3, xyz2, yx3), 1)], state)
+    ups = (up_a, there_a, up_b, there_b, up_c, core_swap(up_c))
+    return finish(info, row_slots, mine, core_swap(others), total, ups)
 
 
 def solution(mesh):

time: 117 us -> 104 us (0.89)
  waiting for transfers between devices: 24 us -> 15.2 us
  Pallas kernels: 67.2 us -> 61.5 us
    ppermute x21, waiting for transfers between devices: 24 us -> 15.2 us  [permuted(): return lax.ppermute(array, axes, pairs)]
    pallas_call x1 -> x0, Pallas kernels: 5.45 us -> none  [half_for_partner(): pl.pallas_call(copy_kernel, out_shape=jax.ShapeDtypeStruct((rows, depth /...]
    pallas_call x4 -> x3, Pallas kernels: 26.2 us -> 26.1 us  [absorb(): pl.pallas_call(functools.partial(absorb_kernel, sizes, start, sides, more...]
  transfers between devices with their start and end apart: 21 -> 21, of which waited for: 8 -> 9; matrix products, arithmetic and copies ran while one was open for 3% -> 3% of each run, Pallas kernels for 38% -> 53%
where the time goes in v12:
time: 104 us; the launch traced here: 103 us
  Pallas kernels  61.5 us (59%)
  starting transfers between devices  22.6 us (22%)
  waiting for transfers between devices  15.2 us (15%)
  local copies, waits for them, and re-layouts  3.03 us (3%)
    pallas_call x3, Pallas kernels, absorb(): pl.pallas_call(functools.partial(absorb_kernel, sizes, start, sides, more...  26.1 us
    pallas_call x3, Pallas kernels, base_part(): pl.pallas_call(functools.partial(base_kernel, steps), out_shape=result, g...  22.8 us
    ppermute x21, starting transfers between devices, permuted(): return lax.ppermute(array, axes, pairs)  22.6 us
    ppermute x21, waiting for transfers between devices, permuted(): return lax.ppermute(array, axes, pairs)  15.2 us
    pallas_call x1, Pallas kernels, finish(): pl.pallas_call(functools.partial(finish_kernel, len(ups)), out_shape=jax....  6.6 us
    pallas_call x2, Pallas kernels, assemble(): pl.pallas_call(functools.partial(assemble_kernel, back), out_shape=jax.Sh...  5.96 us
  transfers between devices with their start and end apart: 21, of which 9 were waited for; matrix products, arithmetic and copies ran while one was open for 3% of the time, Pallas kernels for 53%

profile of v12, /device:TPU:0, one launch (start us, length us, event | category | flops | bytes accessed | tf_op | source)
XLA Modules:
  0.0 103.4 jit_solution(9522396849897556801)
XLA Ops:
  0.0 0.5 collective-permute-start
  0.5 1.2 %dynamic-slice_bitcast_fusion.info_ref = s32[50]{0:T(128)} fusion(s32[32,50]{1,0:T(8,128)} %constant.20.clone, s32[]{:T(128)S(6)} %select_n.8), kind=kLoop, calls=%fused_computation.3 | loop fusion | bytes 404 | tf_op jit(solution)/shard_map/jit(dynamic_index_in_dim)/squeeze | solution.py:403
  1.7 0.8 select_reduce_fusion
  2.5 0.6 collective-permute-done.there_ref
  3.1 0.4 collective-permute-start.2
  3.5 3.0 %shard_map.73.refs_2_ = bf16[2304,128]{1,0:T(8,128)(2,1)} custom-call(s32[50]{0:T(128)} %dynamic-slice_bitcast_fusion.info_ref, bf16[4,16,8192]{2,1,0:T(8,128)(2,1)} %here_ref.3, bf16[4,16,8192]{2,1,0:T(8,128)(2,1)} %collective-permute-done.there_ref, bf16[4,16,1024]{2,1,0:T(8,128)(2,1)} %up_ref.3), custom_call_target="tpu_custom_call" | custom-call | tf_op jit(solution)/shard_map/pallas_call | solution.py:117
  6.5 2.8 %collective-permute-start.3 = (bf16[2304,128]{1,0:T(8,128)(2,1)}, bf16[2304,128]{1,0:T(8,128)(2,1)}, u32[]{:S(2)}, u32[]{:S(2)}) collective-permute-start(bf16[2304,128]{1,0:T(8,128)(2,1)} %shard_map.73.refs_2_), channel_id=1, source_target_pairs={{0,4},{1,5},{2,6},{3,7},{4,12},{5,13},{6,14},{7,15},{8,0},{9,1},{1... | collective-permute-start | bytes 1769480 | tf_op jit(solution)/shard_map/ppermute | solution.py:376
  9.2 1.5 %collective-permute-start.5 = (bf16[2304,128]{1,0:T(8,128)(2,1)}, bf16[2304,128]{1,0:T(8,128)(2,1)}, u32[]{:S(2)}, u32[]{:S(2)}) collective-permute-start(bf16[2304,128]{1,0:T(8,128)(2,1)} %shard_map.73.refs_2_), channel_id=1, source_target_pairs={{0,2},{1,3},{2,0},{3,1},{4,6},{5,7},{6,4},{7,5},{8,10},{9,11},{10,... | collective-permute-start | bytes 1769480 | tf_op jit(solution)/shard_map/ppermute | solution.py:376
  10.7 8.1 %shard_map.74.refs_0_ = f32[512,1024]{1,0:T(8,128)} custom-call(bf16[512,8192]{1,0:T(8,128)(2,1)} %refs_0_.5, bf16[8192,1024]{1,0:T(8,128)(2,1)} %weight_ref.5), custom_call_target="tpu_custom_call" | custom-call | flops 3221225472 | bytes 11534336 | tf_op jit(solution)/shard_map/pallas_call | solution.py:160
  18.8 5.6 %collective-permute-done.3.refs_3_ = bf16[2304,128]{1,0:T(8,128)(2,1)} collective-permute-done((bf16[2304,128]{1,0:T(8,128)(2,1)}, bf16[2304,128]{1,0:T(8,128)(2,1)}, u32[]{:S(2)}, u32[]{:S(2)}) %collective-permute-start.3) | collective-permute-done | bytes 589856 | tf_op jit(solution)/shard_map/ppermute | solution.py:376
  24.4 0.8 collective-permute-start.4
  25.2 0.0 collective-permute-done.5.refs_4_
  25.2 1.5 %collective-permute-start.7 = (bf16[2304,128]{1,0:T(8,128)(2,1)}, bf16[2304,128]{1,0:T(8,128)(2,1)}, u32[]{:S(2)}, u32[]{:S(2)}) collective-permute-start(bf16[2304,128]{1,0:T(8,128)(2,1)} %collective-permute-done.5.refs_4_), channel_id=1, source_target_pairs={{0,16},{1,17},{2,18},{3,19},{4,20},{5,21},{6,22},{7,23},{8,24},{9,... | collective-permute-start | bytes 1769480 | tf_op jit(solution)/shard_map/ppermute | solution.py:376
  26.8 1.5 %collective-permute-start.6 = (bf16[2304,128]{1,0:T(8,128)(2,1)}, bf16[2304,128]{1,0:T(8,128)(2,1)}, u32[]{:S(2)}, u32[]{:S(2)}) collective-permute-start(bf16[2304,128]{1,0:T(8,128)(2,1)} %collective-permute-done.3.refs_3_), channel_id=1, source_target_pairs={{0,2},{1,3},{2,0},{3,1},{4,6},{5,7},{6,4},{7,5},{8,10},{9,11},{10,... | collective-permute-start | bytes 1769480 | tf_op jit(solution)/shard_map/ppermute | solution.py:376
  28.3 0.0 collective-permute-start.1
  28.3 1.2 %collective-permute-done.1 = s32[512]{0:T(512)S(1)} collective-permute-done((s32[512]{0:T(512)S(1)}, s32[512]{0:T(512)S(1)}, u32[]{:S(2)}, u32[]{:S(2)}) %collective-permute-start.1) | collective-permute-done | bytes 2080 | tf_op jit(solution)/shard_map/ppermute | solution.py:376
  29.4 8.4 %shard_map.75.refs_0_ = f32[512,1024]{1,0:T(8,128)} custom-call(bf16[512,8192]{1,0:T(8,128)(2,1)} %refs_0_.5, bf16[8192,1024]{1,0:T(8,128)(2,1)} %weight_ref.5, f32[512,1024]{1,0:T(8,128)} %shard_map.74.refs_0_), custom_call_target="tpu_custom_call" | custom-call | flops 3221225472 | bytes 11534336 | tf_op jit(solution)/shard_map/pallas_call | solution.py:160
  37.8 2.9 %collective-permute-done.4.refs_5_ = bf16[2304,128]{1,0:T(8,128)(2,1)} collective-permute-done((bf16[2304,128]{1,0:T(8,128)(2,1)}, bf16[2304,128]{1,0:T(8,128)(2,1)}, u32[]{:S(2)}, u32[]{:S(2)}) %collective-permute-start.4) | collective-permute-done | bytes 589856 | tf_op jit(solution)/shard_map/ppermute | solution.py:376
  40.7 1.3 %collective-permute-start.8 = (bf16[2304,128]{1,0:T(8,128)(2,1)}, bf16[2304,128]{1,0:T(8,128)(2,1)}, u32[]{:S(2)}, u32[]{:S(2)}) collective-permute-start(bf16[2304,128]{1,0:T(8,128)(2,1)} %shard_map.73.refs_2_), channel_id=1, source_target_pairs={{0,8},{1,9},{2,10},{3,11},{4,0},{5,1},{6,2},{7,3},{8,12},{9,13},{1... | collective-permute-start | bytes 1769480 | tf_op jit(solution)/shard_map/ppermute | solution.py:376
  42.0 0.0 collective-permute-done.7.refs_7_
  42.0 1.5 %collective-permute-start.10 = (bf16[2304,128]{1,0:T(8,128)(2,1)}, bf16[2304,128]{1,0:T(8,128)(2,1)}, u32[]{:S(2)}, u32[]{:S(2)}) collective-permute-start(bf16[2304,128]{1,0:T(8,128)(2,1)} %collective-permute-done.4.refs_5_), channel_id=1, source_target_pairs={{0,16},{1,17},{2,18},{3,19},{4,20},{5,21},{6,22},{7,23},{8,24},{9,... | collective-permute-start | bytes 1769480 | tf_op jit(solution)/shard_map/ppermute | solution.py:376
  43.5 0.0 collective-permute-done.6.refs_2_
  43.5 1.5 %collective-permute-start.9 = (bf16[2304,128]{1,0:T(8,128)(2,1)}, bf16[2304,128]{1,0:T(8,128)(2,1)}, u32[]{:S(2)}, u32[]{:S(2)}) collective-permute-start(bf16[2304,128]{1,0:T(8,128)(2,1)} %collective-permute-done.4.refs_5_), channel_id=1, source_target_pairs={{0,2},{1,3},{2,0},{3,1},{4,6},{5,7},{6,4},{7,5},{8,10},{9,11},{10,... | collective-permute-start | bytes 1769480 | tf_op jit(solution)/shard_map/ppermute | solution.py:376
  45.0 3.0 %shard_map.76.refs_6_ = bf16[2304,128]{1,0:T(8,128)(2,1)} custom-call(s32[50]{0:T(128)} %dynamic-slice_bitcast_fusion.info_ref, bf16[4,16,8192]{2,1,0:T(8,128)(2,1)} %here_ref.3, bf16[4,16,8192]{2,1,0:T(8,128)(2,1)} %collective-permute-done.there_ref, bf16[4,16,1024]{2,1,0:T(8,128)(2,1)} %up_ref.3), custom_call_target="tpu_custom_call" | custom-call | tf_op jit(solution)/shard_map/pallas_call | solution.py:117
  48.0 0.0 collective-permute-done.2.refs_1_
  48.0 6.4 %shard_map.77.total_ref = f32[512,1024]{1,0:T(8,128)} custom-call(bf16[512,8192]{1,0:T(8,128)(2,1)} %refs_0_.5, bf16[8192,1024]{1,0:T(8,128)(2,1)} %weight_ref.5, f32[512,1024]{1,0:T(8,128)} %shard_map.75.refs_0_), custom_call_target="tpu_custom_call" | custom-call | flops 2147483648 | bytes 8388608 | tf_op jit(solution)/shard_map/pallas_call | solution.py:160
  54.4 0.8 collective-permute-done.8.refs_3_
  55.2 2.7 %collective-permute-start.16 = (bf16[2304,128]{1,0:T(8,128)(2,1)}, bf16[2304,128]{1,0:T(8,128)(2,1)}, u32[]{:S(2)}, u32[]{:S(2)}) collective-permute-start(bf16[2304,128]{1,0:T(8,128)(2,1)} %shard_map.76.refs_6_), channel_id=1, source_target_pairs={{0,4},{1,5},{2,6},{3,7},{4,12},{5,13},{6,14},{7,15},{8,0},{9,1},{1... | collective-permute-start | bytes 1769480 | tf_op jit(solution)/shard_map/ppermute | solution.py:376
  57.9 0.0 collective-permute-done.10.refs_8_
  57.9 0.7 collective-permute-start.14
  58.6 0.0 collective-permute-done.9.refs_4_
  58.6 1.5 %collective-permute-start.12 = (bf16[2304,128]{1,0:T(8,128)(2,1)}, bf16[2304,128]{1,0:T(8,128)(2,1)}, u32[]{:S(2)}, u32[]{:S(2)}) collective-permute-start(bf16[2304,128]{1,0:T(8,128)(2,1)} %collective-permute-done.8.refs_3_), channel_id=1, source_target_pairs={{0,2},{1,3},{2,0},{3,1},{4,6},{5,7},{6,4},{7,5},{8,10},{9,11},{10,... | collective-permute-start | bytes 1769480 | tf_op jit(solution)/shard_map/ppermute | solution.py:376
  60.1 1.0 %copy.17.row_slot_ref = s32[1024,1]{1,0:T(8,128)} copy(s32[1024,1]{0,1:T(1,128)S(1)} %pad_add_fusion) | data formatting | bytes 8192 | tf_op jit(solution)/shard_map/concatenate | solution.py:433
  61.1 6.5 %shard_map.78 = (f32[512,128]{1,0:T(8,128)}, f32[512,128]{1,0:T(8,128)}, bf16[128,1024]{1,0:T(8,128)(2,1)}) custom-call(s32[50]{0:T(128)} %dynamic-slice_bitcast_fusion.info_ref, s32[1024,1]{1,0:T(8,128)} %copy.17.row_slot_ref, bf16[512,8192]{1,0:T(8,128)(2,1)} %refs_0_.5, bf16[512,8192]{1,0:T(8,128)(2,1)} %collective-permute-done.2.refs_1_, ...), custom_call_target="tpu_custom_call" | custom-call | flops 2147483648 | bytes 6553600 | tf_op jit(solution)/shard_map/pallas_call | solution.py:278
  67.7 0.1 collective-permute-start.17
  67.8 1.7 %collective-permute-start.11 = (bf16[2304,128]{1,0:T(8,128)(2,1)}, bf16[2304,128]{1,0:T(8,128)(2,1)}, u32[]{:S(2)}, u32[]{:S(2)}) collective-permute-start(bf16[2304,128]{1,0:T(8,128)(2,1)} %shard_map.76.refs_6_), channel_id=1, source_target_pairs={{0,8},{1,9},{2,10},{3,11},{4,0},{5,1},{6,2},{7,3},{8,12},{9,13},{1... | collective-permute-start | bytes 1769480 | tf_op jit(solution)/shard_map/ppermute | solution.py:376
  69.5 0.0 collective-permute-done.17.refs_1_
  69.5 0.0 copy-start
  69.5 0.4 collective-permute-done.16.refs_9_
  69.9 2.0 %collective-permute-done.14.refs_10_ = bf16[2304,128]{1,0:T(8,128)(2,1)} collective-permute-done((bf16[2304,128]{1,0:T(8,128)(2,1)}, bf16[2304,128]{1,0:T(8,128)(2,1)}, u32[]{:S(2)}, u32[]{:S(2)}) %collective-permute-start.14) | collective-permute-done | bytes 589856 | tf_op jit(solution)/shard_map/ppermute | solution.py:376
  71.9 0.1 collective-permute-done.12.refs_5_
  72.0 1.7 %collective-permute-start.15 = (bf16[2304,128]{1,0:T(8,128)(2,1)}, bf16[2304,128]{1,0:T(8,128)(2,1)}, u32[]{:S(2)}, u32[]{:S(2)}) collective-permute-start(bf16[2304,128]{1,0:T(8,128)(2,1)} %collective-permute-done.12.refs_5_), channel_id=1, source_target_pairs={{0,16},{1,17},{2,18},{3,19},{4,20},{5,21},{6,22},{7,23},{8,24},{9,... | collective-permute-start | bytes 1769480 | tf_op jit(solution)/shard_map/ppermute | solution.py:376
  73.7 0.3 collective-permute-start.13
  74.0 13.1 %shard_map.79 = (f32[512,128]{1,0:T(8,128)}, f32[512,128]{1,0:T(8,128)}, bf16[288,1024]{1,0:T(8,128)(2,1)}) custom-call(s32[50]{0:T(128)} %dynamic-slice_bitcast_fusion.info_ref, s32[1024,1]{1,0:T(8,128)} %copy.17.row_slot_ref, bf16[512,8192]{1,0:T(8,128)(2,1)} %refs_0_.5, bf16[512,8192]{1,0:T(8,128)(2,1)} %collective-permute-done.2.refs_1_, ...), custom_call_target="tpu_custom_call" | custom-call | flops 4831838208 | bytes 13697024 | tf_op jit(solution)/shard_map/pallas_call | solution.py:278
  87.0 0.0 copy-done
  87.0 0.1 collective-permute-start.19
  87.1 0.0 collective-permute-done.11.refs_2_
  87.1 0.0 collective-permute-done.15.refs_4_
  87.1 0.0 collective-permute-done.13.refs_3_
  87.1 6.5 %shard_map.80 = (f32[512,128]{1,0:T(8,128)}, f32[512,128]{1,0:T(8,128)}, bf16[96,1024]{1,0:T(8,128)(2,1)}) custom-call(s32[50]{0:T(128)} %dynamic-slice_bitcast_fusion.info_ref, s32[1024,1]{1,0:T(8,128)} %copy.17.row_slot_ref, bf16[512,8192]{1,0:T(8,128)(2,1)} %refs_0_.5, bf16[512,8192]{1,0:T(8,128)(2,1)} %collective-permute-done.2.refs_1_, ...), custom_call_target="tpu_custom_call" | custom-call | flops 1610612736 | bytes 5963776 | tf_op jit(solution)/shard_map/pallas_call | solution.py:278
  93.7 0.5 collective-permute-start.18
  94.2 0.1 collective-permute-start.20
  94.3 0.0 collective-permute-done.19.refs_3_
  94.3 1.6 %collective-permute-done.20.refs_5_ = bf16[96,1024]{1,0:T(8,128)(2,1)S(1)} collective-permute-done((bf16[96,1024]{1,0:T(8,128)(2,1)}, bf16[96,1024]{1,0:T(8,128)(2,1)S(1)}, u32[]{:S(2)}, u32[]{:S(2)}) %collective-permute-start.20) | collective-permute-done | bytes 196640 | tf_op jit(solution)/shard_map/ppermute | solution.py:376
  95.9 0.0 copy-start.2
  95.9 0.0 collective-permute-done.18.theirs_ref
  95.9 0.0 copy-start.1
  95.9 0.7 copy-done.2
  96.5 0.1 copy-done.1
  96.6 6.6 %shard_map.81 = bf16[512,1024]{1,0:T(8,128)(2,1)} custom-call(s32[50]{0:T(128)} %dynamic-slice_bitcast_fusion.info_ref, s32[1024,1]{1,0:T(8,128)} %copy.17.row_slot_ref, f32[512,128]{1,0:T(8,128)} %get-tuple-element.63.mine_ref, f32[512,128]{1,0:T(8,128)} %copy-done.1, f32[512,1024]{1,0:T(8,128)} %shard_map.77.total_ref, ...), custom_call_target="tpu_custom_call" | custom-call | flops 2147483648 | bytes 5242880 | tf_op jit(solution)/shard_map/pallas_call | solution.py:335
  (1 shorter events, 0.0 us)
Async XLA Ops:
  0.0 3.1 %collective-permute-start = (bf16[4,16,8192]{2,1,0:T(8,128)(2,1)}, bf16[4,16,8192]{2,1,0:T(8,128)(2,1)}, u32[]{:S(2)}, u32[]{:S(2)}) collective-permute-start(bf16[4,16,8192]{2,1,0:T(8,128)(2,1)} %here_ref.3), channel_id=1, source_target_pairs={{0,1},{1,0},{2,3},{3,2},{4,5},{5,4},{6,7},{7,6},{8,9},{9,8},{10,11... | collective-permute-start | bytes 3145736 | tf_op jit(solution)/shard_map/ppermute | solution.py:376
  3.1 44.9 %collective-permute-start.2 = (bf16[512,8192]{1,0:T(8,128)(2,1)}, bf16[512,8192]{1,0:T(8,128)(2,1)}, u32[]{:S(2)}, u32[]{:S(2)}) collective-permute-start(bf16[512,8192]{1,0:T(8,128)(2,1)} %refs_0_.5), channel_id=1, source_target_pairs={{0,1},{1,0},{2,3},{3,2},{4,5},{5,4},{6,7},{7,6},{8,9},{9,8},{10,11... | collective-permute-start | bytes 25165832 | tf_op jit(solution)/shard_map/ppermute | solution.py:376
  6.5 18.0 %collective-permute-start.3 = (bf16[2304,128]{1,0:T(8,128)(2,1)}, bf16[2304,128]{1,0:T(8,128)(2,1)}, u32[]{:S(2)}, u32[]{:S(2)}) collective-permute-start(bf16[2304,128]{1,0:T(8,128)(2,1)} %shard_map.73.refs_2_), channel_id=1, source_target_pairs={{0,4},{1,5},{2,6},{3,7},{4,12},{5,13},{6,14},{7,15},{8,0},{9,1},{1... | collective-permute-start | bytes 1769480 | tf_op jit(solution)/shard_map/ppermute | solution.py:376
  9.2 16.0 %collective-permute-start.5 = (bf16[2304,128]{1,0:T(8,128)(2,1)}, bf16[2304,128]{1,0:T(8,128)(2,1)}, u32[]{:S(2)}, u32[]{:S(2)}) collective-permute-start(bf16[2304,128]{1,0:T(8,128)(2,1)} %shard_map.73.refs_2_), channel_id=1, source_target_pairs={{0,2},{1,3},{2,0},{3,1},{4,6},{5,7},{6,4},{7,5},{8,10},{9,11},{10,... | collective-permute-start | bytes 1769480 | tf_op jit(solution)/shard_map/ppermute | solution.py:376
  24.4 16.2 %collective-permute-start.4 = (bf16[2304,128]{1,0:T(8,128)(2,1)}, bf16[2304,128]{1,0:T(8,128)(2,1)}, u32[]{:S(2)}, u32[]{:S(2)}) collective-permute-start(bf16[2304,128]{1,0:T(8,128)(2,1)} %collective-permute-done.3.refs_3_), channel_id=1, source_target_pairs={{0,4},{1,5},{2,6},{3,7},{4,12},{5,13},{6,14},{7,15},{8,0},{9,1},{1... | collective-permute-start | bytes 1769480 | tf_op jit(solution)/shard_map/ppermute | solution.py:376
  25.2 16.7 %collective-permute-start.7 = (bf16[2304,128]{1,0:T(8,128)(2,1)}, bf16[2304,128]{1,0:T(8,128)(2,1)}, u32[]{:S(2)}, u32[]{:S(2)}) collective-permute-start(bf16[2304,128]{1,0:T(8,128)(2,1)} %collective-permute-done.5.refs_4_), channel_id=1, source_target_pairs={{0,16},{1,17},{2,18},{3,19},{4,20},{5,21},{6,22},{7,23},{8,24},{9,... | collective-permute-start | bytes 1769480 | tf_op jit(solution)/shard_map/ppermute | solution.py:376
  26.8 16.7 %collective-permute-start.6 = (bf16[2304,128]{1,0:T(8,128)(2,1)}, bf16[2304,128]{1,0:T(8,128)(2,1)}, u32[]{:S(2)}, u32[]{:S(2)}) collective-permute-start(bf16[2304,128]{1,0:T(8,128)(2,1)} %collective-permute-done.3.refs_3_), channel_id=1, source_target_pairs={{0,2},{1,3},{2,0},{3,1},{4,6},{5,7},{6,4},{7,5},{8,10},{9,11},{10,... | collective-permute-start | bytes 1769480 | tf_op jit(solution)/shard_map/ppermute | solution.py:376
  28.3 1.2 %collective-permute-start.1 = (s32[512]{0:T(512)S(1)}, s32[512]{0:T(512)S(1)}, u32[]{:S(2)}, u32[]{:S(2)}) collective-permute-start(s32[512]{0:T(512)S(1)} %select_reduce_fusion), channel_id=1, source_target_pairs={{0,1},{1,0},{2,3},{3,2},{4,5},{5,4},{6,7},{7,6},{8,9},{9,8},{10,11... | collective-permute-start | bytes 6152 | tf_op jit(solution)/shard_map/ppermute | solution.py:376
  40.7 14.6 %collective-permute-start.8 = (bf16[2304,128]{1,0:T(8,128)(2,1)}, bf16[2304,128]{1,0:T(8,128)(2,1)}, u32[]{:S(2)}, u32[]{:S(2)}) collective-permute-start(bf16[2304,128]{1,0:T(8,128)(2,1)} %shard_map.73.refs_2_), channel_id=1, source_target_pairs={{0,8},{1,9},{2,10},{3,11},{4,0},{5,1},{6,2},{7,3},{8,12},{9,13},{1... | collective-permute-start | bytes 1769480 | tf_op jit(solution)/shard_map/ppermute | solution.py:376
  42.0 15.9 %collective-permute-start.10 = (bf16[2304,128]{1,0:T(8,128)(2,1)}, bf16[2304,128]{1,0:T(8,128)(2,1)}, u32[]{:S(2)}, u32[]{:S(2)}) collective-permute-start(bf16[2304,128]{1,0:T(8,128)(2,1)} %collective-permute-done.4.refs_5_), channel_id=1, source_target_pairs={{0,16},{1,17},{2,18},{3,19},{4,20},{5,21},{6,22},{7,23},{8,24},{9,... | collective-permute-start | bytes 1769480 | tf_op jit(solution)/shard_map/ppermute | solution.py:376
  43.5 15.1 %collective-permute-start.9 = (bf16[2304,128]{1,0:T(8,128)(2,1)}, bf16[2304,128]{1,0:T(8,128)(2,1)}, u32[]{:S(2)}, u32[]{:S(2)}) collective-permute-start(bf16[2304,128]{1,0:T(8,128)(2,1)} %collective-permute-done.4.refs_5_), channel_id=1, source_target_pairs={{0,2},{1,3},{2,0},{3,1},{4,6},{5,7},{6,4},{7,5},{8,10},{9,11},{10,... | collective-permute-start | bytes 1769480 | tf_op jit(solution)/shard_map/ppermute | solution.py:376
  55.2 14.7 %collective-permute-start.16 = (bf16[2304,128]{1,0:T(8,128)(2,1)}, bf16[2304,128]{1,0:T(8,128)(2,1)}, u32[]{:S(2)}, u32[]{:S(2)}) collective-permute-start(bf16[2304,128]{1,0:T(8,128)(2,1)} %shard_map.76.refs_6_), channel_id=1, source_target_pairs={{0,4},{1,5},{2,6},{3,7},{4,12},{5,13},{6,14},{7,15},{8,0},{9,1},{1... | collective-permute-start | bytes 1769480 | tf_op jit(solution)/shard_map/ppermute | solution.py:376
  57.9 14.1 %collective-permute-start.14 = (bf16[2304,128]{1,0:T(8,128)(2,1)}, bf16[2304,128]{1,0:T(8,128)(2,1)}, u32[]{:S(2)}, u32[]{:S(2)}) collective-permute-start(bf16[2304,128]{1,0:T(8,128)(2,1)} %collective-permute-done.6.refs_2_), channel_id=1, source_target_pairs={{0,16},{1,17},{2,18},{3,19},{4,20},{5,21},{6,22},{7,23},{8,24},{9,... | collective-permute-start | bytes 1769480 | tf_op jit(solution)/shard_map/ppermute | solution.py:376
  58.6 13.4 %collective-permute-start.12 = (bf16[2304,128]{1,0:T(8,128)(2,1)}, bf16[2304,128]{1,0:T(8,128)(2,1)}, u32[]{:S(2)}, u32[]{:S(2)}) collective-permute-start(bf16[2304,128]{1,0:T(8,128)(2,1)} %collective-permute-done.8.refs_3_), channel_id=1, source_target_pairs={{0,2},{1,3},{2,0},{3,1},{4,6},{5,7},{6,4},{7,5},{8,10},{9,11},{10,... | collective-permute-start | bytes 1769480 | tf_op jit(solution)/shard_map/ppermute | solution.py:376
  67.7 1.8 %collective-permute-start.17 = (bf16[128,1024]{1,0:T(8,128)(2,1)}, bf16[128,1024]{1,0:T(8,128)(2,1)S(1)}, u32[]{:S(2)}, u32[]{:S(2)}) collective-permute-start(bf16[128,1024]{1,0:T(8,128)(2,1)} %get-tuple-element.58.refs_0_), channel_id=1, source_target_pairs={{0,1},{1,0},{2,3},{3,2},{4,5},{5,4},{6,7},{7,6},{8,9},{9,8},{10,11... | collective-permute-start | bytes 786440 | tf_op jit(solution)/shard_map/ppermute | solution.py:376
  67.8 19.3 %collective-permute-start.11 = (bf16[2304,128]{1,0:T(8,128)(2,1)}, bf16[2304,128]{1,0:T(8,128)(2,1)}, u32[]{:S(2)}, u32[]{:S(2)}) collective-permute-start(bf16[2304,128]{1,0:T(8,128)(2,1)} %shard_map.76.refs_6_), channel_id=1, source_target_pairs={{0,8},{1,9},{2,10},{3,11},{4,0},{5,1},{6,2},{7,3},{8,12},{9,13},{1... | collective-permute-start | bytes 1769480 | tf_op jit(solution)/shard_map/ppermute | solution.py:376
  69.5 17.5 %copy-start = (bf16[128,1024]{1,0:T(8,128)(2,1)}, bf16[128,1024]{1,0:T(8,128)(2,1)S(1)}, u32[]{:S(2)}) copy-start(bf16[128,1024]{1,0:T(8,128)(2,1)S(1)} %collective-permute-done.17.refs_1_) | copy-start | bytes 786436
  72.0 15.1 %collective-permute-start.15 = (bf16[2304,128]{1,0:T(8,128)(2,1)}, bf16[2304,128]{1,0:T(8,128)(2,1)}, u32[]{:S(2)}, u32[]{:S(2)}) collective-permute-start(bf16[2304,128]{1,0:T(8,128)(2,1)} %collective-permute-done.12.refs_5_), channel_id=1, source_target_pairs={{0,16},{1,17},{2,18},{3,19},{4,20},{5,21},{6,22},{7,23},{8,24},{9,... | collective-permute-start | bytes 1769480 | tf_op jit(solution)/shard_map/ppermute | solution.py:376
  73.7 13.5 %collective-permute-start.13 = (bf16[2304,128]{1,0:T(8,128)(2,1)}, bf16[2304,128]{1,0:T(8,128)(2,1)}, u32[]{:S(2)}, u32[]{:S(2)}) collective-permute-start(bf16[2304,128]{1,0:T(8,128)(2,1)} %collective-permute-done.10.refs_8_), channel_id=1, source_target_pairs={{0,2},{1,3},{2,0},{3,1},{4,6},{5,7},{6,4},{7,5},{8,10},{9,11},{10,... | collective-permute-start | bytes 1769480 | tf_op jit(solution)/shard_map/ppermute | solution.py:376
  87.0 7.2 %collective-permute-start.19 = (bf16[288,1024]{1,0:T(8,128)(2,1)}, bf16[288,1024]{1,0:T(8,128)(2,1)}, u32[]{:S(2)}, u32[]{:S(2)}) collective-permute-start(bf16[288,1024]{1,0:T(8,128)(2,1)} %get-tuple-element.65.refs_2_), channel_id=1, source_target_pairs={{0,1},{1,0},{2,3},{3,2},{4,5},{5,4},{6,7},{7,6},{8,9},{9,8},{10,11... | collective-permute-start | bytes 1769480 | tf_op jit(solution)/shard_map/ppermute | solution.py:376
  93.7 2.2 %collective-permute-start.18 = (f32[512,128]{1,0:T(8,128)}, f32[512,128]{1,0:T(8,128)S(1)}, u32[]{:S(2)}, u32[]{:S(2)}) collective-permute-start(f32[512,128]{1,0:T(8,128)} %get-tuple-element.64), channel_id=1, source_target_pairs={{0,1},{1,0},{2,3},{3,2},{4,5},{5,4},{6,7},{7,6},{8,9},{9,8},{10,11... | collective-permute-start | bytes 786440 | tf_op jit(solution)/shard_map/ppermute | solution.py:376
  94.2 1.7 %collective-permute-start.20 = (bf16[96,1024]{1,0:T(8,128)(2,1)}, bf16[96,1024]{1,0:T(8,128)(2,1)S(1)}, u32[]{:S(2)}, u32[]{:S(2)}) collective-permute-start(bf16[96,1024]{1,0:T(8,128)(2,1)} %get-tuple-element.66.refs_4_), channel_id=1, source_target_pairs={{0,1},{1,0},{2,3},{3,2},{4,5},{5,4},{6,7},{7,6},{8,9},{9,8},{10,11... | collective-permute-start | bytes 589832 | tf_op jit(solution)/shard_map/ppermute | solution.py:376
  95.9 0.7 copy-start.2
  95.9 0.8 copy-start.1

commit v13 on v12

--- a/solution.py
+++ b/solution.py
@@ -16,11 +16,11 @@
 
 PIECES = (
     *((0, 0, 0), (1, 0, 0), (0, 1, 0), (2, 0, 0)),
-    *((1, 1, 0), (3, 0, 0), (2, 1, 0), (3, 1, 0)),
-    *((0, 0, 1), (0, 1, 1), (2, 0, 1), (1, 0, 1), (1, 1, 1)),
+    *((0, 0, 1), (0, 1, 1), (2, 0, 1)),
+    *((1, 1, 0), (3, 0, 0), (2, 1, 0), (3, 1, 0), (1, 0, 1), (1, 1, 1)),
     *((3, 0, 1), (2, 1, 1), (3, 1, 1)),
 )
-KERNEL_BOUNDS = (0, 4, 13, 16)
+KERNEL_BOUNDS = (0, 4, 7, 13, 16)
 QUARTER_CUTS = (0, 512, 1024, 2048)
 VMEM_BYTES = 64 * 1024 * 1024 - 512 * 1024
 
@@ -420,7 +420,7 @@
         )
 
     front = piece(0)
-    cuts = (0, 3 * DEPTH_TILE, 6 * DEPTH_TILE, depth)
+    cuts = (0, depth // 2, depth)
 
     def base(number, before, *others):
         low, high = cuts[number : number + 2]
@@ -436,12 +436,6 @@
     x1 = x_swap(after(z1, x0, total))
     yx0 = y_swap(after(x0, total))
     total = base(1, total, z1, x0, total, row_slots)
-
-    z3 = z_back(after(front, z2, total))
-    x2 = x_swap(after(z2, x1, total))
-    yz2 = y_swap(after(z2, yx0, total))
-    back = piece(1, z2, x1, yx0, total)
-    total = base(2, total, z2, x1, yx0, back, other)
 
     def update(number, groups, before, *others):
         return absorb(
@@ -456,28 +450,32 @@
             True,
         )
 
-    zb1 = z_ring(after(back, z3, total))
-    x3 = x_swap(after(z3, x2, total))
-    yx1 = y_swap(after(x1, yz2, total))
-    *state, up_a = update(0, [((front, z1, x0, z2), 0)], None, z3, x2, yz2, total)
+    z3 = z_back(after(front, z2, total))
+    x2 = x_swap(after(z2, x1, total))
+    yz2 = y_swap(after(z2, yx0, total))
+    back = piece(1, z2, x1, yx0, total, other)
+    *state, up_a = update(0, [((front, z1, x0, z2), 0)], None, x1, yx0, total, back)
     there_a = core_swap(up_a)
 
-    zb3 = z_back(after(back, state[0]))
+    zb1 = z_ring(after(back, z3, state[0]))
+    x3 = x_swap(after(z3, x2, state[0]))
+    yx1 = y_swap(after(x1, yz2, state[0]))
+    *state, up_b = update(1, [((back, yx0, yz2), 1)], state, z3, x2, there_a)
+    there_b = core_swap(up_b)
+
+    zb3 = z_back(after(back, zb1, state[0]))
     xyz2 = x_swap(after(yz2, x3, state[0]))
     yx3 = y_swap(after(x3, yx1, state[0]))
-    *state, up_b = update(
-        1,
-        [((x1, z3, x2, x3), 0), ((back, yx0, yz2, zb1, yx1), 1)],
+    *state, up_c = update(
+        2,
+        [((x1, z3, x2, x3), 0), ((zb1, yx1), 1)],
         state,
-        zb1,
-        x3,
-        yx1,
-        there_a,
-    )
-    there_b = core_swap(up_b)
-
-    mine, others, up_c = update(2, [((zb3, xyz2, yx3), 1)], state)
-    ups = (up_a, there_a, up_b, there_b, up_c, core_swap(up_c))
+        there_b,
+    )
+    there_c = core_swap(up_c)
+
+    mine, others, up_d = update(3, [((zb3, xyz2, yx3), 1)], state)
+    ups = (up_a, there_a, up_b, there_b, up_c, there_c, up_d, core_swap(up_d))
     return finish(info, row_slots, mine, core_swap(others), total, ups)
 
 

time: 104 us -> 104 us (level)
  waiting for transfers between devices: 15.2 us -> 19.6 us
  starting transfers between devices: 22.6 us -> 18.6 us
    ppermute x21 -> x22, waiting for transfers between devices: 15.2 us -> 19.6 us  [permuted(): return lax.ppermute(array, axes, pairs)]
    ppermute x21 -> x22, starting transfers between devices: 22.6 us -> 18.6 us  [permuted(): return lax.ppermute(array, axes, pairs)]
    pallas_call x3 -> x4, Pallas kernels: 26.1 us -> 30 us  [absorb(): pl.pallas_call(functools.partial(absorb_kernel, sizes, start, sides, more...]
    pallas_call x3 -> x2, Pallas kernels: 22.8 us -> 19.5 us  [base_part(): pl.pallas_call(functools.partial(base_kernel, steps), out_shape=result, g...]
  transfers between devices with their start and end apart: 21 -> 22, of which waited for: 9 -> 12; matrix products, arithmetic and copies ran while one was open for 3% -> 3% of each run, Pallas kernels for 53% -> 54%
where the time goes in v13:
time: 104 us; the launch traced here: 103 us
  Pallas kernels  62 us (60%)
  waiting for transfers between devices  19.6 us (19%)
  starting transfers between devices  18.6 us (18%)
  local copies, waits for them, and re-layouts  2.29 us (2%)
    pallas_call x4, Pallas kernels, absorb(): pl.pallas_call(functools.partial(absorb_kernel, sizes, start, sides, more...  30 us
    ppermute x22, waiting for transfers between devices, permuted(): return lax.ppermute(array, axes, pairs)  19.6 us
    pallas_call x2, Pallas kernels, base_part(): pl.pallas_call(functools.partial(base_kernel, steps), out_shape=result, g...  19.5 us
    ppermute x22, starting transfers between devices, permuted(): return lax.ppermute(array, axes, pairs)  18.6 us
    pallas_call x1, Pallas kernels, finish(): pl.pallas_call(functools.partial(finish_kernel, len(ups)), out_shape=jax....  6.59 us
    pallas_call x2, Pallas kernels, assemble(): pl.pallas_call(functools.partial(assemble_kernel, back), out_shape=jax.Sh...  5.97 us
  transfers between devices with their start and end apart: 22, of which 12 were waited for; matrix products, arithmetic and copies ran while one was open for 3% of the time, Pallas kernels for 54%

profile of v13, /device:TPU:0, one launch (start us, length us, event | category | flops | bytes accessed | tf_op | source)
XLA Modules:
  0.0 103.5 jit_solution(9817838500450333477)
XLA Ops:
  0.0 0.5 collective-permute-start
  0.5 1.3 %dynamic-slice_bitcast_fusion.info_ref = s32[50]{0:T(128)} fusion(s32[32,50]{1,0:T(8,128)} %constant.20.clone, s32[]{:T(128)S(6)} %select_n.8), kind=kLoop, calls=%fused_computation.3 | loop fusion | bytes 404 | tf_op jit(solution)/shard_map/jit(dynamic_index_in_dim)/squeeze | solution.py:403
  1.7 0.8 select_reduce_fusion
  2.5 0.6 collective-permute-done.there_ref
  3.1 0.4 collective-permute-start.2
  3.5 3.0 %shard_map.73.refs_2_ = bf16[2304,128]{1,0:T(8,128)(2,1)} custom-call(s32[50]{0:T(128)} %dynamic-slice_bitcast_fusion.info_ref, bf16[4,16,8192]{2,1,0:T(8,128)(2,1)} %here_ref.3, bf16[4,16,8192]{2,1,0:T(8,128)(2,1)} %collective-permute-done.there_ref, bf16[4,16,1024]{2,1,0:T(8,128)(2,1)} %up_ref.3), custom_call_target="tpu_custom_call" | custom-call | tf_op jit(solution)/shard_map/pallas_call | solution.py:117
  6.5 2.8 %collective-permute-start.3 = (bf16[2304,128]{1,0:T(8,128)(2,1)}, bf16[2304,128]{1,0:T(8,128)(2,1)}, u32[]{:S(2)}, u32[]{:S(2)}) collective-permute-start(bf16[2304,128]{1,0:T(8,128)(2,1)} %shard_map.73.refs_2_), channel_id=1, source_target_pairs={{0,4},{1,5},{2,6},{3,7},{4,12},{5,13},{6,14},{7,15},{8,0},{9,1},{1... | collective-permute-start | bytes 1769480 | tf_op jit(solution)/shard_map/ppermute | solution.py:376
  9.2 1.5 %collective-permute-start.5 = (bf16[2304,128]{1,0:T(8,128)(2,1)}, bf16[2304,128]{1,0:T(8,128)(2,1)}, u32[]{:S(2)}, u32[]{:S(2)}) collective-permute-start(bf16[2304,128]{1,0:T(8,128)(2,1)} %shard_map.73.refs_2_), channel_id=1, source_target_pairs={{0,2},{1,3},{2,0},{3,1},{4,6},{5,7},{6,4},{7,5},{8,10},{9,11},{10,... | collective-permute-start | bytes 1769480 | tf_op jit(solution)/shard_map/ppermute | solution.py:376
  10.7 9.6 %shard_map.74.refs_0_ = f32[512,1024]{1,0:T(8,128)} custom-call(bf16[512,8192]{1,0:T(8,128)(2,1)} %refs_0_.7, bf16[8192,1024]{1,0:T(8,128)(2,1)} %weight_ref.3), custom_call_target="tpu_custom_call" | custom-call | flops 4294967296 | bytes 14680064 | tf_op jit(solution)/shard_map/pallas_call | solution.py:160
  20.3 4.1 %collective-permute-done.3.refs_3_ = bf16[2304,128]{1,0:T(8,128)(2,1)} collective-permute-done((bf16[2304,128]{1,0:T(8,128)(2,1)}, bf16[2304,128]{1,0:T(8,128)(2,1)}, u32[]{:S(2)}, u32[]{:S(2)}) %collective-permute-start.3) | collective-permute-done | bytes 589856 | tf_op jit(solution)/shard_map/ppermute | solution.py:376
  24.4 0.8 collective-permute-start.4
  25.3 0.0 collective-permute-done.5.refs_4_
  25.3 1.5 %collective-permute-start.6 = (bf16[2304,128]{1,0:T(8,128)(2,1)}, bf16[2304,128]{1,0:T(8,128)(2,1)}, u32[]{:S(2)}, u32[]{:S(2)}) collective-permute-start(bf16[2304,128]{1,0:T(8,128)(2,1)} %collective-permute-done.3.refs_3_), channel_id=1, source_target_pairs={{0,2},{1,3},{2,0},{3,1},{4,6},{5,7},{6,4},{7,5},{8,10},{9,11},{10,... | collective-permute-start | bytes 1769480 | tf_op jit(solution)/shard_map/ppermute | solution.py:376
  26.8 1.5 %collective-permute-start.7 = (bf16[2304,128]{1,0:T(8,128)(2,1)}, bf16[2304,128]{1,0:T(8,128)(2,1)}, u32[]{:S(2)}, u32[]{:S(2)}) collective-permute-start(bf16[2304,128]{1,0:T(8,128)(2,1)} %collective-permute-done.5.refs_4_), channel_id=1, source_target_pairs={{0,16},{1,17},{2,18},{3,19},{4,20},{5,21},{6,22},{7,23},{8,24},{9,... | collective-permute-start | bytes 1769480 | tf_op jit(solution)/shard_map/ppermute | solution.py:376
  28.3 0.0 collective-permute-start.1
  28.3 1.2 %collective-permute-done.1 = s32[512]{0:T(512)S(1)} collective-permute-done((s32[512]{0:T(512)S(1)}, s32[512]{0:T(512)S(1)}, u32[]{:S(2)}, u32[]{:S(2)}) %collective-permute-start.1) | collective-permute-done | bytes 2080 | tf_op jit(solution)/shard_map/ppermute | solution.py:376
  29.4 9.9 %shard_map.75.total_ref = f32[512,1024]{1,0:T(8,128)} custom-call(bf16[512,8192]{1,0:T(8,128)(2,1)} %refs_0_.7, bf16[8192,1024]{1,0:T(8,128)(2,1)} %weight_ref.3, f32[512,1024]{1,0:T(8,128)} %shard_map.74.refs_0_), custom_call_target="tpu_custom_call" | custom-call | flops 4294967296 | bytes 14680064 | tf_op jit(solution)/shard_map/pallas_call | solution.py:160
  39.3 1.3 %collective-permute-done.4.refs_5_ = bf16[2304,128]{1,0:T(8,128)(2,1)} collective-permute-done((bf16[2304,128]{1,0:T(8,128)(2,1)}, bf16[2304,128]{1,0:T(8,128)(2,1)}, u32[]{:S(2)}, u32[]{:S(2)}) %collective-permute-start.4) | collective-permute-done | bytes 589856 | tf_op jit(solution)/shard_map/ppermute | solution.py:376
  40.7 1.3 %collective-permute-start.8 = (bf16[2304,128]{1,0:T(8,128)(2,1)}, bf16[2304,128]{1,0:T(8,128)(2,1)}, u32[]{:S(2)}, u32[]{:S(2)}) collective-permute-start(bf16[2304,128]{1,0:T(8,128)(2,1)} %shard_map.73.refs_2_), channel_id=1, source_target_pairs={{0,8},{1,9},{2,10},{3,11},{4,0},{5,1},{6,2},{7,3},{8,12},{9,13},{1... | collective-permute-start | bytes 1769480 | tf_op jit(solution)/shard_map/ppermute | solution.py:376
  42.0 0.0 collective-permute-done.6.refs_2_
  42.0 1.5 %collective-permute-start.10 = (bf16[2304,128]{1,0:T(8,128)(2,1)}, bf16[2304,128]{1,0:T(8,128)(2,1)}, u32[]{:S(2)}, u32[]{:S(2)}) collective-permute-start(bf16[2304,128]{1,0:T(8,128)(2,1)} %collective-permute-done.4.refs_5_), channel_id=1, source_target_pairs={{0,2},{1,3},{2,0},{3,1},{4,6},{5,7},{6,4},{7,5},{8,10},{9,11},{10,... | collective-permute-start | bytes 1769480 | tf_op jit(solution)/shard_map/ppermute | solution.py:376
  43.5 0.0 collective-permute-done.7.refs_3_
  43.5 1.5 %collective-permute-start.12 = (bf16[2304,128]{1,0:T(8,128)(2,1)}, bf16[2304,128]{1,0:T(8,128)(2,1)}, u32[]{:S(2)}, u32[]{:S(2)}) collective-permute-start(bf16[2304,128]{1,0:T(8,128)(2,1)} %collective-permute-done.4.refs_5_), channel_id=1, source_target_pairs={{0,16},{1,17},{2,18},{3,19},{4,20},{5,21},{6,22},{7,23},{8,24},{9,... | collective-permute-start | bytes 1769480 | tf_op jit(solution)/shard_map/ppermute | solution.py:376
  45.0 1.0 copy.19.row_slot_ref
  46.0 0.0 collective-permute-done.2.refs_1_
  46.1 3.0 %shard_map.76.refs_2_ = bf16[2304,128]{1,0:T(8,128)(2,1)} custom-call(s32[50]{0:T(128)} %dynamic-slice_bitcast_fusion.info_ref, bf16[4,16,8192]{2,1,0:T(8,128)(2,1)} %here_ref.3, bf16[4,16,8192]{2,1,0:T(8,128)(2,1)} %collective-permute-done.there_ref, bf16[4,16,1024]{2,1,0:T(8,128)(2,1)} %up_ref.3), custom_call_target="tpu_custom_call" | custom-call | tf_op jit(solution)/shard_map/pallas_call | solution.py:117
  49.0 6.5 %shard_map.77 = (f32[512,128]{1,0:T(8,128)}, f32[512,128]{1,0:T(8,128)}, bf16[128,1024]{1,0:T(8,128)(2,1)}) custom-call(s32[50]{0:T(128)} %dynamic-slice_bitcast_fusion.info_ref, s32[1024,1]{1,0:T(8,128)} %copy.19.row_slot_ref, bf16[512,8192]{1,0:T(8,128)(2,1)} %refs_0_.7, bf16[512,8192]{1,0:T(8,128)(2,1)} %collective-permute-done.2.refs_1_, ...), custom_call_target="tpu_custom_call" | custom-call | flops 2147483648 | bytes 6553600 | tf_op jit(solution)/shard_map/pallas_call | solution.py:278
  55.6 1.2 %collective-permute-done.8.refs_3_ = bf16[2304,128]{1,0:T(8,128)(2,1)} collective-permute-done((bf16[2304,128]{1,0:T(8,128)(2,1)}, bf16[2304,128]{1,0:T(8,128)(2,1)}, u32[]{:S(2)}, u32[]{:S(2)}) %collective-permute-start.8) | collective-permute-done | bytes 589856 | tf_op jit(solution)/shard_map/ppermute | solution.py:376
  56.8 2.6 %collective-permute-start.9 = (bf16[2304,128]{1,0:T(8,128)(2,1)}, bf16[2304,128]{1,0:T(8,128)(2,1)}, u32[]{:S(2)}, u32[]{:S(2)}) collective-permute-start(bf16[2304,128]{1,0:T(8,128)(2,1)} %shard_map.76.refs_2_), channel_id=1, source_target_pairs={{0,4},{1,5},{2,6},{3,7},{4,12},{5,13},{6,14},{7,15},{8,0},{9,1},{1... | collective-permute-start | bytes 1769480 | tf_op jit(solution)/shard_map/ppermute | solution.py:376
  59.4 0.0 collective-permute-done.10.refs_4_
  59.4 0.5 collective-permute-start.14
  59.9 0.0 collective-permute-done.12.refs_4_
  59.9 0.5 collective-permute-start.16
  60.5 0.0 collective-permute-start.11
  60.5 1.9 %collective-permute-done.11.refs_1_ = bf16[128,1024]{1,0:T(8,128)(2,1)} collective-permute-done((bf16[128,1024]{1,0:T(8,128)(2,1)}, bf16[128,1024]{1,0:T(8,128)(2,1)}, u32[]{:S(2)}, u32[]{:S(2)}) %collective-permute-start.11) | collective-permute-done | bytes 262176 | tf_op jit(solution)/shard_map/ppermute | solution.py:376
  62.4 6.5 %shard_map.78 = (f32[512,128]{1,0:T(8,128)}, f32[512,128]{1,0:T(8,128)}, bf16[96,1024]{1,0:T(8,128)(2,1)}) custom-call(s32[50]{0:T(128)} %dynamic-slice_bitcast_fusion.info_ref, s32[1024,1]{1,0:T(8,128)} %copy.19.row_slot_ref, bf16[512,8192]{1,0:T(8,128)(2,1)} %refs_0_.7, bf16[512,8192]{1,0:T(8,128)(2,1)} %collective-permute-done.2.refs_1_, ...), custom_call_target="tpu_custom_call" | custom-call | flops 1610612736 | bytes 5963776 | tf_op jit(solution)/shard_map/pallas_call | solution.py:278
  68.9 4.0 %collective-permute-done.9.refs_6_ = bf16[2304,128]{1,0:T(8,128)(2,1)} collective-permute-done((bf16[2304,128]{1,0:T(8,128)(2,1)}, bf16[2304,128]{1,0:T(8,128)(2,1)}, u32[]{:S(2)}, u32[]{:S(2)}) %collective-permute-start.9) | collective-permute-done | bytes 589856 | tf_op jit(solution)/shard_map/ppermute | solution.py:376
  72.9 0.0 collective-permute-start.13
  72.9 1.1 %collective-permute-done.14.refs_5_ = bf16[2304,128]{1,0:T(8,128)(2,1)} collective-permute-done((bf16[2304,128]{1,0:T(8,128)(2,1)}, bf16[2304,128]{1,0:T(8,128)(2,1)}, u32[]{:S(2)}, u32[]{:S(2)}) %collective-permute-start.14) | collective-permute-done | bytes 589856 | tf_op jit(solution)/shard_map/ppermute | solution.py:376
  74.0 0.5 collective-permute-start.15
  74.6 0.0 collective-permute-done.16.refs_7_
  74.6 0.2 collective-permute-start.17
  74.8 0.0 collective-permute-start.18
  74.8 1.8 %collective-permute-done.18.refs_3_ = bf16[96,1024]{1,0:T(8,128)(2,1)} collective-permute-done((bf16[96,1024]{1,0:T(8,128)(2,1)}, bf16[96,1024]{1,0:T(8,128)(2,1)}, u32[]{:S(2)}, u32[]{:S(2)}) %collective-permute-start.18) | collective-permute-done | bytes 196640 | tf_op jit(solution)/shard_map/ppermute | solution.py:376
  76.6 10.5 %shard_map.79 = (f32[512,128]{1,0:T(8,128)}, f32[512,128]{1,0:T(8,128)}, bf16[192,1024]{1,0:T(8,128)(2,1)}) custom-call(s32[50]{0:T(128)} %dynamic-slice_bitcast_fusion.info_ref, s32[1024,1]{1,0:T(8,128)} %copy.19.row_slot_ref, bf16[512,8192]{1,0:T(8,128)(2,1)} %refs_0_.7, bf16[512,8192]{1,0:T(8,128)(2,1)} %collective-permute-done.2.refs_1_, ...), custom_call_target="tpu_custom_call" | custom-call | flops 3221225472 | bytes 11927552 | tf_op jit(solution)/shard_map/pallas_call | solution.py:278
  87.1 0.2 collective-permute-start.20
  87.3 0.0 collective-permute-done.13.refs_2_
  87.3 0.4 collective-permute-done.15.refs_3_
  87.7 0.3 collective-permute-done.17.refs_4_
  88.0 6.5 %shard_map.80 = (f32[512,128]{1,0:T(8,128)}, f32[512,128]{1,0:T(8,128)}, bf16[96,1024]{1,0:T(8,128)(2,1)}) custom-call(s32[50]{0:T(128)} %dynamic-slice_bitcast_fusion.info_ref, s32[1024,1]{1,0:T(8,128)} %copy.19.row_slot_ref, bf16[512,8192]{1,0:T(8,128)(2,1)} %refs_0_.7, bf16[512,8192]{1,0:T(8,128)(2,1)} %collective-permute-done.2.refs_1_, ...), custom_call_target="tpu_custom_call" | custom-call | flops 1610612736 | bytes 5963776 | tf_op jit(solution)/shard_map/pallas_call | solution.py:278
  94.5 0.1 collective-permute-start.19
  94.6 0.5 collective-permute-start.21
  95.1 0.0 collective-permute-done.20.refs_5_
  95.1 0.0 copy-start
  95.1 1.6 %collective-permute-done.21.refs_7_ = bf16[96,1024]{1,0:T(8,128)(2,1)} collective-permute-done((bf16[96,1024]{1,0:T(8,128)(2,1)}, bf16[96,1024]{1,0:T(8,128)(2,1)}, u32[]{:S(2)}, u32[]{:S(2)}) %collective-permute-start.21) | collective-permute-done | bytes 196640 | tf_op jit(solution)/shard_map/ppermute | solution.py:376
  96.7 0.0 collective-permute-done.19.theirs_ref
  96.7 0.0 copy-done
  96.7 6.6 %shard_map.81 = bf16[512,1024]{1,0:T(8,128)(2,1)} custom-call(s32[50]{0:T(128)} %dynamic-slice_bitcast_fusion.info_ref, s32[1024,1]{1,0:T(8,128)} %copy.19.row_slot_ref, f32[512,128]{1,0:T(8,128)} %get-tuple-element.69.mine_ref, f32[512,128]{1,0:T(8,128)} %collective-permute-done.19.theirs_ref, f32[512,1024]{1,0:T(8,128)} %shard_map.75.total_ref, ...), custom_call_target="tpu_custom_call" | custom-call | flops 2147483648 | bytes 5242880 | tf_op jit(solution)/shard_map/pallas_call | solution.py:335
  (1 shorter events, 0.0 us)
Async XLA Ops:
  0.0 3.1 %collective-permute-start = (bf16[4,16,8192]{2,1,0:T(8,128)(2,1)}, bf16[4,16,8192]{2,1,0:T(8,128)(2,1)}, u32[]{:S(2)}, u32[]{:S(2)}) collective-permute-start(bf16[4,16,8192]{2,1,0:T(8,128)(2,1)} %here_ref.3), channel_id=1, source_target_pairs={{0,1},{1,0},{2,3},{3,2},{4,5},{5,4},{6,7},{7,6},{8,9},{9,8},{10,11... | collective-permute-start | bytes 3145736 | tf_op jit(solution)/shard_map/ppermute | solution.py:376
  3.1 43.0 %collective-permute-start.2 = (bf16[512,8192]{1,0:T(8,128)(2,1)}, bf16[512,8192]{1,0:T(8,128)(2,1)}, u32[]{:S(2)}, u32[]{:S(2)}) collective-permute-start(bf16[512,8192]{1,0:T(8,128)(2,1)} %refs_0_.7), channel_id=1, source_target_pairs={{0,1},{1,0},{2,3},{3,2},{4,5},{5,4},{6,7},{7,6},{8,9},{9,8},{10,11... | collective-permute-start | bytes 25165832 | tf_op jit(solution)/shard_map/ppermute | solution.py:376
  6.5 18.0 %collective-permute-start.3 = (bf16[2304,128]{1,0:T(8,128)(2,1)}, bf16[2304,128]{1,0:T(8,128)(2,1)}, u32[]{:S(2)}, u32[]{:S(2)}) collective-permute-start(bf16[2304,128]{1,0:T(8,128)(2,1)} %shard_map.73.refs_2_), channel_id=1, source_target_pairs={{0,4},{1,5},{2,6},{3,7},{4,12},{5,13},{6,14},{7,15},{8,0},{9,1},{1... | collective-permute-start | bytes 1769480 | tf_op jit(solution)/shard_map/ppermute | solution.py:376
  9.2 16.0 %collective-permute-start.5 = (bf16[2304,128]{1,0:T(8,128)(2,1)}, bf16[2304,128]{1,0:T(8,128)(2,1)}, u32[]{:S(2)}, u32[]{:S(2)}) collective-permute-start(bf16[2304,128]{1,0:T(8,128)(2,1)} %shard_map.73.refs_2_), channel_id=1, source_target_pairs={{0,2},{1,3},{2,0},{3,1},{4,6},{5,7},{6,4},{7,5},{8,10},{9,11},{10,... | collective-permute-start | bytes 1769480 | tf_op jit(solution)/shard_map/ppermute | solution.py:376
  24.4 16.2 %collective-permute-start.4 = (bf16[2304,128]{1,0:T(8,128)(2,1)}, bf16[2304,128]{1,0:T(8,128)(2,1)}, u32[]{:S(2)}, u32[]{:S(2)}) collective-permute-start(bf16[2304,128]{1,0:T(8,128)(2,1)} %collective-permute-done.3.refs_3_), channel_id=1, source_target_pairs={{0,4},{1,5},{2,6},{3,7},{4,12},{5,13},{6,14},{7,15},{8,0},{9,1},{1... | collective-permute-start | bytes 1769480 | tf_op jit(solution)/shard_map/ppermute | solution.py:376
  25.3 16.7 %collective-permute-start.6 = (bf16[2304,128]{1,0:T(8,128)(2,1)}, bf16[2304,128]{1,0:T(8,128)(2,1)}, u32[]{:S(2)}, u32[]{:S(2)}) collective-permute-start(bf16[2304,128]{1,0:T(8,128)(2,1)} %collective-permute-done.3.refs_3_), channel_id=1, source_target_pairs={{0,2},{1,3},{2,0},{3,1},{4,6},{5,7},{6,4},{7,5},{8,10},{9,11},{10,... | collective-permute-start | bytes 1769480 | tf_op jit(solution)/shard_map/ppermute | solution.py:376
  26.8 16.7 %collective-permute-start.7 = (bf16[2304,128]{1,0:T(8,128)(2,1)}, bf16[2304,128]{1,0:T(8,128)(2,1)}, u32[]{:S(2)}, u32[]{:S(2)}) collective-permute-start(bf16[2304,128]{1,0:T(8,128)(2,1)} %collective-permute-done.5.refs_4_), channel_id=1, source_target_pairs={{0,16},{1,17},{2,18},{3,19},{4,20},{5,21},{6,22},{7,23},{8,24},{9,... | collective-permute-start | bytes 1769480 | tf_op jit(solution)/shard_map/ppermute | solution.py:376
  28.3 1.2 %collective-permute-start.1 = (s32[512]{0:T(512)S(1)}, s32[512]{0:T(512)S(1)}, u32[]{:S(2)}, u32[]{:S(2)}) collective-permute-start(s32[512]{0:T(512)S(1)} %select_reduce_fusion), channel_id=1, source_target_pairs={{0,1},{1,0},{2,3},{3,2},{4,5},{5,4},{6,7},{7,6},{8,9},{9,8},{10,11... | collective-permute-start | bytes 6152 | tf_op jit(solution)/shard_map/ppermute | solution.py:376
  40.7 16.1 %collective-permute-start.8 = (bf16[2304,128]{1,0:T(8,128)(2,1)}, bf16[2304,128]{1,0:T(8,128)(2,1)}, u32[]{:S(2)}, u32[]{:S(2)}) collective-permute-start(bf16[2304,128]{1,0:T(8,128)(2,1)} %shard_map.73.refs_2_), channel_id=1, source_target_pairs={{0,8},{1,9},{2,10},{3,11},{4,0},{5,1},{6,2},{7,3},{8,12},{9,13},{1... | collective-permute-start | bytes 1769480 | tf_op jit(solution)/shard_map/ppermute | solution.py:376
  42.0 17.4 %collective-permute-start.10 = (bf16[2304,128]{1,0:T(8,128)(2,1)}, bf16[2304,128]{1,0:T(8,128)(2,1)}, u32[]{:S(2)}, u32[]{:S(2)}) collective-permute-start(bf16[2304,128]{1,0:T(8,128)(2,1)} %collective-permute-done.4.refs_5_), channel_id=1, source_target_pairs={{0,2},{1,3},{2,0},{3,1},{4,6},{5,7},{6,4},{7,5},{8,10},{9,11},{10,... | collective-permute-start | bytes 1769480 | tf_op jit(solution)/shard_map/ppermute | solution.py:376
  43.5 16.4 %collective-permute-start.12 = (bf16[2304,128]{1,0:T(8,128)(2,1)}, bf16[2304,128]{1,0:T(8,128)(2,1)}, u32[]{:S(2)}, u32[]{:S(2)}) collective-permute-start(bf16[2304,128]{1,0:T(8,128)(2,1)} %collective-permute-done.4.refs_5_), channel_id=1, source_target_pairs={{0,16},{1,17},{2,18},{3,19},{4,20},{5,21},{6,22},{7,23},{8,24},{9,... | collective-permute-start | bytes 1769480 | tf_op jit(solution)/shard_map/ppermute | solution.py:376
  56.8 16.1 %collective-permute-start.9 = (bf16[2304,128]{1,0:T(8,128)(2,1)}, bf16[2304,128]{1,0:T(8,128)(2,1)}, u32[]{:S(2)}, u32[]{:S(2)}) collective-permute-start(bf16[2304,128]{1,0:T(8,128)(2,1)} %shard_map.76.refs_2_), channel_id=1, source_target_pairs={{0,4},{1,5},{2,6},{3,7},{4,12},{5,13},{6,14},{7,15},{8,0},{9,1},{1... | collective-permute-start | bytes 1769480 | tf_op jit(solution)/shard_map/ppermute | solution.py:376
  59.4 14.6 %collective-permute-start.14 = (bf16[2304,128]{1,0:T(8,128)(2,1)}, bf16[2304,128]{1,0:T(8,128)(2,1)}, u32[]{:S(2)}, u32[]{:S(2)}) collective-permute-start(bf16[2304,128]{1,0:T(8,128)(2,1)} %collective-permute-done.8.refs_3_), channel_id=1, source_target_pairs={{0,2},{1,3},{2,0},{3,1},{4,6},{5,7},{6,4},{7,5},{8,10},{9,11},{10,... | collective-permute-start | bytes 1769480 | tf_op jit(solution)/shard_map/ppermute | solution.py:376
  59.9 14.6 %collective-permute-start.16 = (bf16[2304,128]{1,0:T(8,128)(2,1)}, bf16[2304,128]{1,0:T(8,128)(2,1)}, u32[]{:S(2)}, u32[]{:S(2)}) collective-permute-start(bf16[2304,128]{1,0:T(8,128)(2,1)} %collective-permute-done.6.refs_2_), channel_id=1, source_target_pairs={{0,16},{1,17},{2,18},{3,19},{4,20},{5,21},{6,22},{7,23},{8,24},{9,... | collective-permute-start | bytes 1769480 | tf_op jit(solution)/shard_map/ppermute | solution.py:376
  60.5 1.9 %collective-permute-start.11 = (bf16[128,1024]{1,0:T(8,128)(2,1)}, bf16[128,1024]{1,0:T(8,128)(2,1)}, u32[]{:S(2)}, u32[]{:S(2)}) collective-permute-start(bf16[128,1024]{1,0:T(8,128)(2,1)} %get-tuple-element.54.refs_0_), channel_id=1, source_target_pairs={{0,1},{1,0},{2,3},{3,2},{4,5},{5,4},{6,7},{7,6},{8,9},{9,8},{10,11... | collective-permute-start | bytes 786440 | tf_op jit(solution)/shard_map/ppermute | solution.py:376
  72.9 14.4 %collective-permute-start.13 = (bf16[2304,128]{1,0:T(8,128)(2,1)}, bf16[2304,128]{1,0:T(8,128)(2,1)}, u32[]{:S(2)}, u32[]{:S(2)}) collective-permute-start(bf16[2304,128]{1,0:T(8,128)(2,1)} %shard_map.76.refs_2_), channel_id=1, source_target_pairs={{0,8},{1,9},{2,10},{3,11},{4,0},{5,1},{6,2},{7,3},{8,12},{9,13},{1... | collective-permute-start | bytes 1769480 | tf_op jit(solution)/shard_map/ppermute | solution.py:376
  74.0 13.7 %collective-permute-start.15 = (bf16[2304,128]{1,0:T(8,128)(2,1)}, bf16[2304,128]{1,0:T(8,128)(2,1)}, u32[]{:S(2)}, u32[]{:S(2)}) collective-permute-start(bf16[2304,128]{1,0:T(8,128)(2,1)} %collective-permute-done.12.refs_4_), channel_id=1, source_target_pairs={{0,2},{1,3},{2,0},{3,1},{4,6},{5,7},{6,4},{7,5},{8,10},{9,11},{10,... | collective-permute-start | bytes 1769480 | tf_op jit(solution)/shard_map/ppermute | solution.py:376
  74.6 13.4 %collective-permute-start.17 = (bf16[2304,128]{1,0:T(8,128)(2,1)}, bf16[2304,128]{1,0:T(8,128)(2,1)}, u32[]{:S(2)}, u32[]{:S(2)}) collective-permute-start(bf16[2304,128]{1,0:T(8,128)(2,1)} %collective-permute-done.14.refs_5_), channel_id=1, source_target_pairs={{0,16},{1,17},{2,18},{3,19},{4,20},{5,21},{6,22},{7,23},{8,24},{9,... | collective-permute-start | bytes 1769480 | tf_op jit(solution)/shard_map/ppermute | solution.py:376
  74.8 1.8 %collective-permute-start.18 = (bf16[96,1024]{1,0:T(8,128)(2,1)}, bf16[96,1024]{1,0:T(8,128)(2,1)}, u32[]{:S(2)}, u32[]{:S(2)}) collective-permute-start(bf16[96,1024]{1,0:T(8,128)(2,1)} %get-tuple-element.64.refs_2_), channel_id=1, source_target_pairs={{0,1},{1,0},{2,3},{3,2},{4,5},{5,4},{6,7},{7,6},{8,9},{9,8},{10,11... | collective-permute-start | bytes 589832 | tf_op jit(solution)/shard_map/ppermute | solution.py:376
  87.1 8.0 %collective-permute-start.20 = (bf16[192,1024]{1,0:T(8,128)(2,1)}, bf16[192,1024]{1,0:T(8,128)(2,1)S(1)}, u32[]{:S(2)}, u32[]{:S(2)}) collective-permute-start(bf16[192,1024]{1,0:T(8,128)(2,1)} %get-tuple-element.71.refs_4_), channel_id=1, source_target_pairs={{0,1},{1,0},{2,3},{3,2},{4,5},{5,4},{6,7},{7,6},{8,9},{9,8},{10,11... | collective-permute-start | bytes 1179656 | tf_op jit(solution)/shard_map/ppermute | solution.py:376
  94.5 2.2 %collective-permute-start.19 = (f32[512,128]{1,0:T(8,128)}, f32[512,128]{1,0:T(8,128)}, u32[]{:S(2)}, u32[]{:S(2)}) collective-permute-start(f32[512,128]{1,0:T(8,128)} %get-tuple-element.70), channel_id=1, source_target_pairs={{0,1},{1,0},{2,3},{3,2},{4,5},{5,4},{6,7},{7,6},{8,9},{9,8},{10,11... | collective-permute-start | bytes 786440 | tf_op jit(solution)/shard_map/ppermute | solution.py:376
  94.6 2.1 %collective-permute-start.21 = (bf16[96,1024]{1,0:T(8,128)(2,1)}, bf16[96,1024]{1,0:T(8,128)(2,1)}, u32[]{:S(2)}, u32[]{:S(2)}) collective-permute-start(bf16[96,1024]{1,0:T(8,128)(2,1)} %get-tuple-element.72.refs_6_), channel_id=1, source_target_pairs={{0,1},{1,0},{2,3},{3,2},{4,5},{5,4},{6,7},{7,6},{8,9},{9,8},{10,11... | collective-permute-start | bytes 589832 | tf_op jit(solution)/shard_map/ppermute | solution.py:376
  95.1 1.7 %copy-start = (bf16[192,1024]{1,0:T(8,128)(2,1)}, bf16[192,1024]{1,0:T(8,128)(2,1)S(1)}, u32[]{:S(2)}) copy-start(bf16[192,1024]{1,0:T(8,128)(2,1)S(1)} %collective-permute-done.20.refs_5_) | copy-start | bytes 1179652

commit v14 on v13

--- a/solution.py
+++ b/solution.py
@@ -16,11 +16,13 @@
 
 PIECES = (
     *((0, 0, 0), (1, 0, 0), (0, 1, 0), (2, 0, 0)),
-    *((0, 0, 1), (0, 1, 1), (2, 0, 1)),
-    *((1, 1, 0), (3, 0, 0), (2, 1, 0), (3, 1, 0), (1, 0, 1), (1, 1, 1)),
+    *((0, 0, 1), (0, 1, 1), (2, 0, 1), (1, 1, 0), (3, 0, 0), (2, 1, 0)),
+    *((3, 1, 0), (1, 0, 1), (1, 1, 1)),
     *((3, 0, 1), (2, 1, 1), (3, 1, 1)),
 )
-KERNEL_BOUNDS = (0, 4, 7, 13, 16)
+KERNEL_BOUNDS = (0, 4, 10, 13, 16)
+EARLY_CHIPS = ((0, 0), (0, 1), (2, 0))
+LATE_CHIPS = ((1, 0), (3, 0), (1, 1), (2, 1), (3, 1))
 QUARTER_CUTS = (0, 512, 1024, 2048)
 VMEM_BYTES = 64 * 1024 * 1024 - 512 * 1024
 
@@ -84,7 +86,7 @@
         copy.wait()
 
 
-def assemble_kernel(back, info_ref, here_ref, there_ref, up_ref, out_ref, down_ref, sems):
+def assemble_kernel(back, info_ref, here_ref, there_ref, up_ref, out_ref, down_ref, own_ref, sems):
     y, core = info_ref[0], info_ref[1]
     place = 1 - y if back else y
     held, rank, quarter = down_ref.shape
@@ -96,13 +98,16 @@
         )
         for n, (source, of_core) in enumerate(((here_ref, core), (there_ref, 1 - core)))
     ]
+    copies.append(
+        pltpu.make_async_copy(up_ref.at[pl.ds(place * (held // 2), held // 2)], own_ref, sems.at[2])
+    )
     started(copies)
-    up = up_ref[pl.ds(place * (held // 2), held // 2)].reshape(held // 2 * rank, -1)
+    awaited(copies)
+    up = own_ref[...].reshape(held // 2 * rank, -1)
     rows = up.shape[0]
     for n in range(up.shape[1] // LANES):
         first = quarter + n * rows
         out_ref[first : first + rows] = up[:, n * LANES : (n + 1) * LANES]
-    awaited(copies)
     for n in range(0, quarter, LANES):
         block = down_ref[:, :, n : n + LANES].reshape(2 * held * rank, LANES)
         out_ref[n : n + LANES] = block.T
@@ -113,15 +118,15 @@
     width = up.shape[2]
     rows = depth // 4 + held // 2 * rank * width // LANES
     anywhere = pl.BlockSpec(memory_space=pl.ANY)
-    vmem = pl.BlockSpec(memory_space=pltpu.VMEM)
     return pl.pallas_call(
         functools.partial(assemble_kernel, back),
         out_shape=jax.ShapeDtypeStruct((rows, LANES), here.dtype),
-        in_specs=[pl.BlockSpec(memory_space=pltpu.SMEM), anywhere, anywhere, vmem],
-        out_specs=vmem,
+        in_specs=[pl.BlockSpec(memory_space=pltpu.SMEM)] + [anywhere] * 3,
+        out_specs=pl.BlockSpec(memory_space=pltpu.VMEM),
         scratch_shapes=[
             pltpu.VMEM((2 * held, rank, depth // 4), here.dtype),
-            pltpu.SemaphoreType.DMA((2,)),
+            pltpu.VMEM((held // 2, rank, width), up.dtype),
+            pltpu.SemaphoreType.DMA((3,)),
         ],
         compiler_params=params(),
     )(info, here, there, up)
@@ -295,11 +300,13 @@
     )(info, row_slots, *tokens, *pieces, *(before or ()))
 
 
-def finish_kernel(count, info_ref, row_slot_ref, mine_ref, theirs_ref, total_ref, *refs):
+def expand_kernel(
+    count, chips, blocks, info_ref, row_slot_ref, mine_ref, theirs_ref, total_ref, *refs
+):
     sources, refs = refs[:count], refs[count:]
     out_ref, row_slot, mine, theirs, total, up, sems = refs
     rows = out_ref.shape[0]
-    height = up.shape[0] // (len(PIECES) * 2)
+    height = LANES // 4
     copies = []
 
     def begin(source, target):
@@ -310,16 +317,16 @@
     begin(mine_ref, mine)
     begin(theirs_ref, theirs)
     begin(total_ref, total)
-    for source in sources:
-        for n in range(0, source.shape[0], height):
-            first = pl.multiple_of(info_ref[len(copies) - 2], height)
-            begin(source.at[pl.ds(n, height)], up.at[pl.ds(first, height)])
+    for array, at, chip, which in blocks:
+        first = pl.multiple_of(chip * LANES + info_ref[which], height)
+        begin(sources[array].at[pl.ds(at * height, height)], up.at[pl.ds(first, height)])
     awaited(copies[:3])
     shrink = mine[...] + theirs[...]
     lane_slot = lax.broadcasted_iota(jnp.int32, (1, LANES), 1) // RANK
     high, low = [], []
-    for n in range(up.shape[0] // LANES):
-        kept = jnp.where(row_slot[...] == lane_slot + n * (LANES // RANK), shrink, 0.0)
+    for which in chips:
+        wanted = lane_slot + info_ref[which] * (LANES // RANK)
+        kept = jnp.where(row_slot[...] == wanted, shrink, 0.0)
         high.append(kept.astype(jnp.bfloat16))
         low.append((kept - high[-1].astype(jnp.float32)).astype(jnp.bfloat16))
     both = jnp.concatenate([jnp.concatenate(part, axis=1) for part in (low, high)], axis=0)
@@ -328,30 +335,41 @@
     out_ref[...] = (total[...] + (lora[:rows] + lora[rows:])).astype(out_ref.dtype)
 
 
-def finish(info, row_slots, mine, theirs, total, ups):
+def expand(info, row_slots, mine, theirs, total, ups, chips, out_dtype):
     rows, width = total.shape
     anywhere = pl.BlockSpec(memory_space=pl.ANY)
-    up_rows = sum(up.shape[0] for up in ups)
+    blocks, chip_places = [], []
+    for kernel, (low, high) in enumerate(zip(KERNEL_BOUNDS, KERNEL_BOUNDS[1:])):
+        for n in range(low, high):
+            if PIECES[n][:2] in chips:
+                for side in (0, 1):
+                    blocks.append(
+                        (2 * kernel + side, n - low, chips.index(PIECES[n][:2]), 2 + 2 * n + side)
+                    )
+    for chip in chips:
+        chip_places.append(2 + 2 * len(PIECES) + PIECES.index((*chip, 0)))
+    arrays = [array for pair in ups for array in pair]
+    up_rows = len(chips) * LANES
     return pl.pallas_call(
-        functools.partial(finish_kernel, len(ups)),
-        out_shape=jax.ShapeDtypeStruct((rows, width), jnp.bfloat16),
-        in_specs=[pl.BlockSpec(memory_space=pltpu.SMEM)] + [anywhere] * (4 + len(ups)),
+        functools.partial(expand_kernel, len(arrays), chip_places, blocks),
+        out_shape=jax.ShapeDtypeStruct((rows, width), out_dtype),
+        in_specs=[pl.BlockSpec(memory_space=pltpu.SMEM)] + [anywhere] * (4 + len(arrays)),
         out_specs=pl.BlockSpec(memory_space=pltpu.VMEM),
         scratch_shapes=[
             pltpu.VMEM((rows, 1), jnp.int32),
             pltpu.VMEM((rows, LANES), jnp.float32),
             pltpu.VMEM((rows, LANES), jnp.float32),
             pltpu.VMEM((rows, width), jnp.float32),
-            pltpu.VMEM((up_rows, width), ups[0].dtype),
-            pltpu.SemaphoreType.DMA((4 + 2 * len(PIECES),)),
+            pltpu.VMEM((up_rows, width), arrays[0].dtype),
+            pltpu.SemaphoreType.DMA((4 + len(blocks),)),
         ],
         cost_estimate=pl.CostEstimate(
             flops=4 * rows * width * up_rows,
-            bytes_accessed=6 * rows * width + 2 * up_rows * width,
+            bytes_accessed=8 * rows * width + 2 * up_rows * width,
             transcendentals=0,
         ),
         compiler_params=params(),
-    )(info, row_slots, mine, theirs, total, *ups)
+    )(info, row_slots, mine, theirs, total, *arrays)
 
 
 def passed_round(
@@ -387,14 +405,12 @@
     def chip(r, piece):
         return (along_z(r, -piece[0]) ^ (2 * piece[1])) // 2
 
-    kernels = [PIECES[low:high] for low, high in zip(KERNEL_BOUNDS, KERNEL_BOUNDS[1:])]
     info_table = [
         [g, r % 2]
         + [
-            chip(r, p) * LANES + core * held * rank + (g ^ p[2]) * (held // 2 * rank)
-            for pieces in kernels
+            core * held * rank + (g ^ p[2]) * (held // 2 * rank)
+            for p in PIECES
             for core in (r % 2, 1 - r % 2)
-            for p in pieces
         ]
         + [chip(r, p) for p in PIECES]
         for g in range(planes)
@@ -460,23 +476,27 @@
     zb1 = z_ring(after(back, z3, state[0]))
     x3 = x_swap(after(z3, x2, state[0]))
     yx1 = y_swap(after(x1, yz2, state[0]))
-    *state, up_b = update(1, [((back, yx0, yz2), 1)], state, z3, x2, there_a)
-    there_b = core_swap(up_b)
+    *state, up_b = update(
+        1, [((back, yx0, yz2), 1), ((x1, z3, x2), 0)], state, there_a
+    )
+    there_b, theirs = core_swap(up_b), core_swap(state[1])
+    early = state[0]
 
     zb3 = z_back(after(back, zb1, state[0]))
     xyz2 = x_swap(after(yz2, x3, state[0]))
     yx3 = y_swap(after(x3, yx1, state[0]))
-    *state, up_c = update(
-        2,
-        [((x1, z3, x2, x3), 0), ((zb1, yx1), 1)],
-        state,
-        there_b,
-    )
+    *state, up_c = update(2, [((x3,), 0), ((zb1, yx1), 1)], state)
     there_c = core_swap(up_c)
-
-    mine, others, up_d = update(3, [((zb3, xyz2, yx3), 1)], state)
-    ups = (up_a, there_a, up_b, there_b, up_c, there_c, up_d, core_swap(up_d))
-    return finish(info, row_slots, mine, core_swap(others), total, ups)
+    ups = [(up_a, there_a), (up_b, there_b)]
+    total = expand(
+        after(info, state[0]), row_slots, early, theirs, total, ups, EARLY_CHIPS, jnp.float32
+    )
+
+    mine, others, up_d = update(3, [((zb3, xyz2, yx3), 1)], state, total, there_c)
+    ups += [(up_c, there_c), (up_d, core_swap(up_d))]
+    return expand(
+        info, row_slots, mine, core_swap(others), total, ups, LATE_CHIPS, jnp.bfloat16
+    )
 
 
 def solution(mesh):

time: 104 us -> 106 us (1.019)
  waiting for transfers between devices: 19.6 us -> 12.6 us
  Pallas kernels: 62 us -> 67.1 us
  starting transfers between devices: 18.6 us -> 21.2 us
  local copies, waits for them, and re-layouts: 2.29 us -> 3.8 us
    ppermute x22 -> x23, waiting for transfers between devices: 19.6 us -> 12.6 us  [permuted(): return lax.ppermute(array, axes, pairs)]
    pallas_call x1 -> x2, Pallas kernels: 6.59 us -> 11.1 us  [expand(): pl.pallas_call(functools.partial(expand_kernel, len(arrays), chip_places,...]
    ppermute x22 -> x23, starting transfers between devices: 18.6 us -> 21.2 us  [permuted(): return lax.ppermute(array, axes, pairs)]
    unnamed x2 -> x6, local copies, waits for them, and re-layouts: 0.01 us -> 1.56 us
    pallas_call x4, Pallas kernels: 30 us -> 31.1 us  [absorb(): pl.pallas_call(functools.partial(absorb_kernel, sizes, start, sides, more...]
  transfers between devices with their start and end apart: 22 -> 23, of which waited for: 12 -> 7; matrix products, arithmetic and copies ran while one was open for 3% -> 3% of each run, Pallas kernels for 54% -> 52%
where the time goes in v14:
time: 106 us
  Pallas kernels  67.1 us (63%)
  starting transfers between devices  21.2 us (20%)
  waiting for transfers between devices  12.6 us (12%)
  local copies, waits for them, and re-layouts  3.8 us (4%)
    pallas_call x4, Pallas kernels, absorb(): pl.pallas_call(functools.partial(absorb_kernel, sizes, start, sides, more...  31.1 us
    ppermute x23, starting transfers between devices, permuted(): return lax.ppermute(array, axes, pairs)  21.2 us
    pallas_call x2, Pallas kernels, base_part(): pl.pallas_call(functools.partial(base_kernel, steps), out_shape=result, g...  19.5 us
    ppermute x23, waiting for transfers between devices, permuted(): return lax.ppermute(array, axes, pairs)  12.6 us
    pallas_call x2, Pallas kernels, expand(): pl.pallas_call(functools.partial(expand_kernel, len(arrays), chip_places,...  11.1 us
    pallas_call x2, Pallas kernels, assemble(): pl.pallas_call(functools.partial(assemble_kernel, back), out_shape=jax.Sh...  5.49 us
  transfers between devices with their start and end apart: 23, of which 7 were waited for; matrix products, arithmetic and copies ran while one was open for 3% of the time, Pallas kernels for 52%

profile of v14, /device:TPU:0, one launch (start us, length us, event | category | flops | bytes accessed | tf_op | source)
XLA Modules:
  0.0 105.8 jit_solution(12874219532573597099)
XLA Ops:
  0.0 0.5 collective-permute-start
  0.5 1.2 %dynamic-slice_bitcast_fusion.info_ref = s32[50]{0:T(128)} fusion(s32[32,50]{1,0:T(8,128)} %constant.20.clone, s32[]{:T(128)S(6)} %select_n.8), kind=kLoop, calls=%fused_computation.3 | loop fusion | bytes 404 | tf_op jit(solution)/shard_map/jit(dynamic_index_in_dim)/squeeze | solution.py:419
  1.7 0.8 select_reduce_fusion
  2.5 0.6 collective-permute-done.there_ref
  3.1 0.4 collective-permute-start.2
  3.5 2.8 %shard_map.73.refs_2_ = bf16[2304,128]{1,0:T(8,128)(2,1)} custom-call(s32[50]{0:T(128)} %dynamic-slice_bitcast_fusion.info_ref, bf16[4,16,8192]{2,1,0:T(8,128)(2,1)} %here_ref.3, bf16[4,16,8192]{2,1,0:T(8,128)(2,1)} %collective-permute-done.there_ref, bf16[4,16,1024]{2,1,0:T(8,128)(2,1)} %up_ref.3), custom_call_target="tpu_custom_call" | custom-call | tf_op jit(solution)/shard_map/pallas_call | solution.py:121
  6.2 2.8 %collective-permute-start.3 = (bf16[2304,128]{1,0:T(8,128)(2,1)}, bf16[2304,128]{1,0:T(8,128)(2,1)}, u32[]{:S(2)}, u32[]{:S(2)}) collective-permute-start(bf16[2304,128]{1,0:T(8,128)(2,1)} %shard_map.73.refs_2_), channel_id=1, source_target_pairs={{0,4},{1,5},{2,6},{3,7},{4,12},{5,13},{6,14},{7,15},{8,0},{9,1},{1... | collective-permute-start | bytes 1769480 | tf_op jit(solution)/shard_map/ppermute | solution.py:394
  9.0 1.5 %collective-permute-start.5 = (bf16[2304,128]{1,0:T(8,128)(2,1)}, bf16[2304,128]{1,0:T(8,128)(2,1)}, u32[]{:S(2)}, u32[]{:S(2)}) collective-permute-start(bf16[2304,128]{1,0:T(8,128)(2,1)} %shard_map.73.refs_2_), channel_id=1, source_target_pairs={{0,2},{1,3},{2,0},{3,1},{4,6},{5,7},{6,4},{7,5},{8,10},{9,11},{10,... | collective-permute-start | bytes 1769480 | tf_op jit(solution)/shard_map/ppermute | solution.py:394
  10.5 9.6 %shard_map.74.refs_0_ = f32[512,1024]{1,0:T(8,128)} custom-call(bf16[512,8192]{1,0:T(8,128)(2,1)} %refs_0_.7, bf16[8192,1024]{1,0:T(8,128)(2,1)} %weight_ref.3), custom_call_target="tpu_custom_call" | custom-call | flops 4294967296 | bytes 14680064 | tf_op jit(solution)/shard_map/pallas_call | solution.py:165
  20.1 4.1 %collective-permute-done.3.refs_3_ = bf16[2304,128]{1,0:T(8,128)(2,1)} collective-permute-done((bf16[2304,128]{1,0:T(8,128)(2,1)}, bf16[2304,128]{1,0:T(8,128)(2,1)}, u32[]{:S(2)}, u32[]{:S(2)}) %collective-permute-start.3) | collective-permute-done | bytes 589856 | tf_op jit(solution)/shard_map/ppermute | solution.py:394
  24.2 0.8 collective-permute-start.4
  25.0 0.0 collective-permute-done.5.refs_4_
  25.0 1.5 %collective-permute-start.9 = (bf16[2304,128]{1,0:T(8,128)(2,1)}, bf16[2304,128]{1,0:T(8,128)(2,1)}, u32[]{:S(2)}, u32[]{:S(2)}) collective-permute-start(bf16[2304,128]{1,0:T(8,128)(2,1)} %collective-permute-done.5.refs_4_), channel_id=1, source_target_pairs={{0,16},{1,17},{2,18},{3,19},{4,20},{5,21},{6,22},{7,23},{8,24},{9,... | collective-permute-start | bytes 1769480 | tf_op jit(solution)/shard_map/ppermute | solution.py:394
  26.5 1.5 %collective-permute-start.7 = (bf16[2304,128]{1,0:T(8,128)(2,1)}, bf16[2304,128]{1,0:T(8,128)(2,1)}, u32[]{:S(2)}, u32[]{:S(2)}) collective-permute-start(bf16[2304,128]{1,0:T(8,128)(2,1)} %collective-permute-done.3.refs_3_), channel_id=1, source_target_pairs={{0,2},{1,3},{2,0},{3,1},{4,6},{5,7},{6,4},{7,5},{8,10},{9,11},{10,... | collective-permute-start | bytes 1769480 | tf_op jit(solution)/shard_map/ppermute | solution.py:394
  28.0 0.0 collective-permute-start.1
  28.0 1.2 %collective-permute-done.1 = s32[512]{0:T(512)S(1)} collective-permute-done((s32[512]{0:T(512)S(1)}, s32[512]{0:T(512)S(1)}, u32[]{:S(2)}, u32[]{:S(2)}) %collective-permute-start.1) | collective-permute-done | bytes 2080 | tf_op jit(solution)/shard_map/ppermute | solution.py:394
  29.2 9.9 %shard_map.75.total_ref = f32[512,1024]{1,0:T(8,128)} custom-call(bf16[512,8192]{1,0:T(8,128)(2,1)} %refs_0_.7, bf16[8192,1024]{1,0:T(8,128)(2,1)} %weight_ref.3, f32[512,1024]{1,0:T(8,128)} %shard_map.74.refs_0_), custom_call_target="tpu_custom_call" | custom-call | flops 4294967296 | bytes 14680064 | tf_op jit(solution)/shard_map/pallas_call | solution.py:165
  39.1 1.3 %collective-permute-done.4.refs_5_ = bf16[2304,128]{1,0:T(8,128)(2,1)} collective-permute-done((bf16[2304,128]{1,0:T(8,128)(2,1)}, bf16[2304,128]{1,0:T(8,128)(2,1)}, u32[]{:S(2)}, u32[]{:S(2)}) %collective-permute-start.4) | collective-permute-done | bytes 589856 | tf_op jit(solution)/shard_map/ppermute | solution.py:394
  40.4 0.0 collective-permute-done.9.refs_3_
  40.4 1.3 %collective-permute-start.12 = (bf16[2304,128]{1,0:T(8,128)(2,1)}, bf16[2304,128]{1,0:T(8,128)(2,1)}, u32[]{:S(2)}, u32[]{:S(2)}) collective-permute-start(bf16[2304,128]{1,0:T(8,128)(2,1)} %collective-permute-done.4.refs_5_), channel_id=1, source_target_pairs={{0,16},{1,17},{2,18},{3,19},{4,20},{5,21},{6,22},{7,23},{8,24},{9,... | collective-permute-start | bytes 1769480 | tf_op jit(solution)/shard_map/ppermute | solution.py:394
  41.8 0.0 collective-permute-done.7.refs_5_
  41.8 1.5 %collective-permute-start.8 = (bf16[2304,128]{1,0:T(8,128)(2,1)}, bf16[2304,128]{1,0:T(8,128)(2,1)}, u32[]{:S(2)}, u32[]{:S(2)}) collective-permute-start(bf16[2304,128]{1,0:T(8,128)(2,1)} %collective-permute-done.4.refs_5_), channel_id=1, source_target_pairs={{0,2},{1,3},{2,0},{3,1},{4,6},{5,7},{6,4},{7,5},{8,10},{9,11},{10,... | collective-permute-start | bytes 1769480 | tf_op jit(solution)/shard_map/ppermute | solution.py:394
  43.3 1.7 %collective-permute-start.6 = (bf16[2304,128]{1,0:T(8,128)(2,1)}, bf16[2304,128]{1,0:T(8,128)(2,1)}, u32[]{:S(2)}, u32[]{:S(2)}) collective-permute-start(bf16[2304,128]{1,0:T(8,128)(2,1)} %shard_map.73.refs_2_), channel_id=1, source_target_pairs={{0,8},{1,9},{2,10},{3,11},{4,0},{5,1},{6,2},{7,3},{8,12},{9,13},{1... | collective-permute-start | bytes 1769480 | tf_op jit(solution)/shard_map/ppermute | solution.py:394
  45.0 1.0 copy.21.row_slot_ref
  46.0 0.0 collective-permute-done.2.refs_1_
  46.0 2.7 %shard_map.76.refs_2_ = bf16[2304,128]{1,0:T(8,128)(2,1)} custom-call(s32[50]{0:T(128)} %dynamic-slice_bitcast_fusion.info_ref, bf16[4,16,8192]{2,1,0:T(8,128)(2,1)} %here_ref.3, bf16[4,16,8192]{2,1,0:T(8,128)(2,1)} %collective-permute-done.there_ref, bf16[4,16,1024]{2,1,0:T(8,128)(2,1)} %up_ref.3), custom_call_target="tpu_custom_call" | custom-call | tf_op jit(solution)/shard_map/pallas_call | solution.py:121
  48.8 6.5 %shard_map.77 = (f32[512,128]{1,0:T(8,128)}, f32[512,128]{1,0:T(8,128)}, bf16[128,1024]{1,0:T(8,128)(2,1)}) custom-call(s32[50]{0:T(128)} %dynamic-slice_bitcast_fusion.info_ref, s32[1024,1]{1,0:T(8,128)} %copy.21.row_slot_ref, bf16[512,8192]{1,0:T(8,128)(2,1)} %refs_0_.7, bf16[512,8192]{1,0:T(8,128)(2,1)} %collective-permute-done.2.refs_1_, ...), custom_call_target="tpu_custom_call" | custom-call | flops 2147483648 | bytes 6553600 | tf_op jit(solution)/shard_map/pallas_call | solution.py:283
  55.2 0.0 collective-permute-done.12.refs_4_
  55.3 0.7 collective-permute-start.13
  56.0 0.0 collective-permute-done.8.refs_7_
  56.0 1.9 %collective-permute-done.6.refs_6_ = bf16[2304,128]{1,0:T(8,128)(2,1)} collective-permute-done((bf16[2304,128]{1,0:T(8,128)(2,1)}, bf16[2304,128]{1,0:T(8,128)(2,1)}, u32[]{:S(2)}, u32[]{:S(2)}) %collective-permute-start.6) | collective-permute-done | bytes 589856 | tf_op jit(solution)/shard_map/ppermute | solution.py:394
  57.8 0.7 collective-permute-start.10
  58.5 2.6 %collective-permute-start.11 = (bf16[2304,128]{1,0:T(8,128)(2,1)}, bf16[2304,128]{1,0:T(8,128)(2,1)}, u32[]{:S(2)}, u32[]{:S(2)}) collective-permute-start(bf16[2304,128]{1,0:T(8,128)(2,1)} %shard_map.76.refs_2_), channel_id=1, source_target_pairs={{0,4},{1,5},{2,6},{3,7},{4,12},{5,13},{6,14},{7,15},{8,0},{9,1},{1... | collective-permute-start | bytes 1769480 | tf_op jit(solution)/shard_map/ppermute | solution.py:394
  61.2 0.0 collective-permute-start.14
  61.2 1.9 %collective-permute-done.14.refs_1_ = bf16[128,1024]{1,0:T(8,128)(2,1)} collective-permute-done((bf16[128,1024]{1,0:T(8,128)(2,1)}, bf16[128,1024]{1,0:T(8,128)(2,1)}, u32[]{:S(2)}, u32[]{:S(2)}) %collective-permute-start.14) | collective-permute-done | bytes 262176 | tf_op jit(solution)/shard_map/ppermute | solution.py:394
  63.0 9.3 %shard_map.78 = (f32[512,128]{1,0:T(8,128)}, f32[512,128]{1,0:T(8,128)}, bf16[192,1024]{1,0:T(8,128)(2,1)}) custom-call(s32[50]{0:T(128)} %dynamic-slice_bitcast_fusion.info_ref, s32[1024,1]{1,0:T(8,128)} %copy.21.row_slot_ref, bf16[512,8192]{1,0:T(8,128)(2,1)} %refs_0_.7, bf16[512,8192]{1,0:T(8,128)(2,1)} %collective-permute-done.2.refs_1_, ...), custom_call_target="tpu_custom_call" | custom-call | flops 3221225472 | bytes 11927552 | tf_op jit(solution)/shard_map/pallas_call | solution.py:283
  72.4 0.0 collective-permute-done.13.refs_4_
  72.4 0.0 collective-permute-done.10.refs_2_
  72.4 2.0 %collective-permute-start.20 = (bf16[2304,128]{1,0:T(8,128)(2,1)}, bf16[2304,128]{1,0:T(8,128)(2,1)}, u32[]{:S(2)}, u32[]{:S(2)}) collective-permute-start(bf16[2304,128]{1,0:T(8,128)(2,1)} %collective-permute-done.10.refs_2_), channel_id=1, source_target_pairs={{0,16},{1,17},{2,18},{3,19},{4,20},{5,21},{6,22},{7,23},{8,24},{9,... | collective-permute-start | bytes 1769480 | tf_op jit(solution)/shard_map/ppermute | solution.py:394
  74.4 0.1 collective-permute-start.19
  74.5 0.0 collective-permute-done.11.refs_3_
  74.5 0.3 collective-permute-start.18
  74.8 0.0 collective-permute-start.16
  74.8 0.5 collective-permute-start.15
  75.3 8.8 %shard_map.79 = (f32[512,128]{1,0:T(8,128)}, f32[512,128]{1,0:T(8,128)}, bf16[96,1024]{1,0:T(8,128)(2,1)}) custom-call(s32[50]{0:T(128)} %dynamic-slice_bitcast_fusion.info_ref, s32[1024,1]{1,0:T(8,128)} %copy.21.row_slot_ref, bf16[512,8192]{1,0:T(8,128)(2,1)} %refs_0_.7, bf16[512,8192]{1,0:T(8,128)(2,1)} %collective-permute-done.2.refs_1_, ...), custom_call_target="tpu_custom_call" | custom-call | flops 1610612736 | bytes 10158080 | tf_op jit(solution)/shard_map/pallas_call | solution.py:283
  84.1 0.0 collective-permute-done.15.theirs_ref
  84.2 0.1 collective-permute-start.17
  84.2 0.0 collective-permute-done.16.refs_3_
  84.2 0.0 copy-start
  84.3 0.8 copy-done
  85.0 5.3 %shard_map.80.total_ref = f32[512,1024]{1,0:T(8,128)} custom-call(s32[50]{0:T(128)} %dynamic-slice_bitcast_fusion.info_ref, s32[1024,1]{1,0:T(8,128)} %copy.21.row_slot_ref, f32[512,128]{1,0:T(8,128)} %get-tuple-element.61.refs_5_.mine_ref, f32[512,128]{1,0:T(8,128)} %collective-permute-done.15.theirs_ref, f32[512,1024]{1,0:T(8,128)} %shard_map.75.total_ref, ...), custom_call_target="tpu_custom_call" | custom-call | flops 805306368 | bytes 4980736 | tf_op jit(solution)/shard_map/pallas_call | solution.py:353
  90.3 0.0 collective-permute-done.17.refs_5_
  90.3 0.0 collective-permute-done.20.refs_4_
  90.3 0.0 collective-permute-done.19.refs_3_
  90.4 0.0 collective-permute-done.18.refs_2_
  90.4 6.5 %shard_map.81 = (f32[512,128]{1,0:T(8,128)}, f32[512,128]{1,0:T(8,128)}, bf16[96,1024]{1,0:T(8,128)(2,1)}) custom-call(s32[50]{0:T(128)} %dynamic-slice_bitcast_fusion.info_ref, s32[1024,1]{1,0:T(8,128)} %copy.21.row_slot_ref, bf16[512,8192]{1,0:T(8,128)(2,1)} %refs_0_.7, bf16[512,8192]{1,0:T(8,128)(2,1)} %collective-permute-done.2.refs_1_, ...), custom_call_target="tpu_custom_call" | custom-call | flops 1610612736 | bytes 5963776 | tf_op jit(solution)/shard_map/pallas_call | solution.py:283
  96.9 0.6 collective-permute-start.21
  97.4 0.1 collective-permute-start.22
  97.5 1.6 %collective-permute-done.22.refs_7_ = bf16[96,1024]{1,0:T(8,128)(2,1)S(1)} collective-permute-done((bf16[96,1024]{1,0:T(8,128)(2,1)}, bf16[96,1024]{1,0:T(8,128)(2,1)S(1)}, u32[]{:S(2)}, u32[]{:S(2)}) %collective-permute-start.22) | collective-permute-done | bytes 196640 | tf_op jit(solution)/shard_map/ppermute | solution.py:394
  99.1 0.0 copy-start.2
  99.1 0.0 collective-permute-done.21.theirs_ref
  99.1 0.7 copy-done.2
  99.8 0.1 copy-done.1
  99.9 5.8 %shard_map.82 = bf16[512,1024]{1,0:T(8,128)(2,1)} custom-call(s32[50]{0:T(128)} %dynamic-slice_bitcast_fusion.info_ref, s32[1024,1]{1,0:T(8,128)} %copy.21.row_slot_ref, f32[512,128]{1,0:T(8,128)} %get-tuple-element.72.mine_ref, f32[512,128]{1,0:T(8,128)} %copy-done.1, f32[512,1024]{1,0:T(8,128)} %shard_map.80.total_ref, ...), custom_call_target="tpu_custom_call" | custom-call | flops 1342177280 | bytes 5505024 | tf_op jit(solution)/shard_map/pallas_call | solution.py:353
  (2 shorter events, 0.0 us)
Async XLA Ops:
  0.0 3.1 %collective-permute-start = (bf16[4,16,8192]{2,1,0:T(8,128)(2,1)}, bf16[4,16,8192]{2,1,0:T(8,128)(2,1)}, u32[]{:S(2)}, u32[]{:S(2)}) collective-permute-start(bf16[4,16,8192]{2,1,0:T(8,128)(2,1)} %here_ref.3), channel_id=1, source_target_pairs={{0,1},{1,0},{2,3},{3,2},{4,5},{5,4},{6,7},{7,6},{8,9},{9,8},{10,11... | collective-permute-start | bytes 3145736 | tf_op jit(solution)/shard_map/ppermute | solution.py:394
  3.1 42.9 %collective-permute-start.2 = (bf16[512,8192]{1,0:T(8,128)(2,1)}, bf16[512,8192]{1,0:T(8,128)(2,1)}, u32[]{:S(2)}, u32[]{:S(2)}) collective-permute-start(bf16[512,8192]{1,0:T(8,128)(2,1)} %refs_0_.7), channel_id=1, source_target_pairs={{0,1},{1,0},{2,3},{3,2},{4,5},{5,4},{6,7},{7,6},{8,9},{9,8},{10,11... | collective-permute-start | bytes 25165832 | tf_op jit(solution)/shard_map/ppermute | solution.py:394
  6.2 18.0 %collective-permute-start.3 = (bf16[2304,128]{1,0:T(8,128)(2,1)}, bf16[2304,128]{1,0:T(8,128)(2,1)}, u32[]{:S(2)}, u32[]{:S(2)}) collective-permute-start(bf16[2304,128]{1,0:T(8,128)(2,1)} %shard_map.73.refs_2_), channel_id=1, source_target_pairs={{0,4},{1,5},{2,6},{3,7},{4,12},{5,13},{6,14},{7,15},{8,0},{9,1},{1... | collective-permute-start | bytes 1769480 | tf_op jit(solution)/shard_map/ppermute | solution.py:394
  9.0 16.0 %collective-permute-start.5 = (bf16[2304,128]{1,0:T(8,128)(2,1)}, bf16[2304,128]{1,0:T(8,128)(2,1)}, u32[]{:S(2)}, u32[]{:S(2)}) collective-permute-start(bf16[2304,128]{1,0:T(8,128)(2,1)} %shard_map.73.refs_2_), channel_id=1, source_target_pairs={{0,2},{1,3},{2,0},{3,1},{4,6},{5,7},{6,4},{7,5},{8,10},{9,11},{10,... | collective-permute-start | bytes 1769480 | tf_op jit(solution)/shard_map/ppermute | solution.py:394
  24.2 16.2 %collective-permute-start.4 = (bf16[2304,128]{1,0:T(8,128)(2,1)}, bf16[2304,128]{1,0:T(8,128)(2,1)}, u32[]{:S(2)}, u32[]{:S(2)}) collective-permute-start(bf16[2304,128]{1,0:T(8,128)(2,1)} %collective-permute-done.3.refs_3_), channel_id=1, source_target_pairs={{0,4},{1,5},{2,6},{3,7},{4,12},{5,13},{6,14},{7,15},{8,0},{9,1},{1... | collective-permute-start | bytes 1769480 | tf_op jit(solution)/shard_map/ppermute | solution.py:394
  25.0 15.4 %collective-permute-start.9 = (bf16[2304,128]{1,0:T(8,128)(2,1)}, bf16[2304,128]{1,0:T(8,128)(2,1)}, u32[]{:S(2)}, u32[]{:S(2)}) collective-permute-start(bf16[2304,128]{1,0:T(8,128)(2,1)} %collective-permute-done.5.refs_4_), channel_id=1, source_target_pairs={{0,16},{1,17},{2,18},{3,19},{4,20},{5,21},{6,22},{7,23},{8,24},{9,... | collective-permute-start | bytes 1769480 | tf_op jit(solution)/shard_map/ppermute | solution.py:394
  26.5 15.2 %collective-permute-start.7 = (bf16[2304,128]{1,0:T(8,128)(2,1)}, bf16[2304,128]{1,0:T(8,128)(2,1)}, u32[]{:S(2)}, u32[]{:S(2)}) collective-permute-start(bf16[2304,128]{1,0:T(8,128)(2,1)} %collective-permute-done.3.refs_3_), channel_id=1, source_target_pairs={{0,2},{1,3},{2,0},{3,1},{4,6},{5,7},{6,4},{7,5},{8,10},{9,11},{10,... | collective-permute-start | bytes 1769480 | tf_op jit(solution)/shard_map/ppermute | solution.py:394
  28.0 1.2 %collective-permute-start.1 = (s32[512]{0:T(512)S(1)}, s32[512]{0:T(512)S(1)}, u32[]{:S(2)}, u32[]{:S(2)}) collective-permute-start(s32[512]{0:T(512)S(1)} %select_reduce_fusion), channel_id=1, source_target_pairs={{0,1},{1,0},{2,3},{3,2},{4,5},{5,4},{6,7},{7,6},{8,9},{9,8},{10,11... | collective-permute-start | bytes 6152 | tf_op jit(solution)/shard_map/ppermute | solution.py:394
  40.4 14.8 %collective-permute-start.12 = (bf16[2304,128]{1,0:T(8,128)(2,1)}, bf16[2304,128]{1,0:T(8,128)(2,1)}, u32[]{:S(2)}, u32[]{:S(2)}) collective-permute-start(bf16[2304,128]{1,0:T(8,128)(2,1)} %collective-permute-done.4.refs_5_), channel_id=1, source_target_pairs={{0,16},{1,17},{2,18},{3,19},{4,20},{5,21},{6,22},{7,23},{8,24},{9,... | collective-permute-start | bytes 1769480 | tf_op jit(solution)/shard_map/ppermute | solution.py:394
  41.8 14.2 %collective-permute-start.8 = (bf16[2304,128]{1,0:T(8,128)(2,1)}, bf16[2304,128]{1,0:T(8,128)(2,1)}, u32[]{:S(2)}, u32[]{:S(2)}) collective-permute-start(bf16[2304,128]{1,0:T(8,128)(2,1)} %collective-permute-done.4.refs_5_), channel_id=1, source_target_pairs={{0,2},{1,3},{2,0},{3,1},{4,6},{5,7},{6,4},{7,5},{8,10},{9,11},{10,... | collective-permute-start | bytes 1769480 | tf_op jit(solution)/shard_map/ppermute | solution.py:394
  43.3 14.6 %collective-permute-start.6 = (bf16[2304,128]{1,0:T(8,128)(2,1)}, bf16[2304,128]{1,0:T(8,128)(2,1)}, u32[]{:S(2)}, u32[]{:S(2)}) collective-permute-start(bf16[2304,128]{1,0:T(8,128)(2,1)} %shard_map.73.refs_2_), channel_id=1, source_target_pairs={{0,8},{1,9},{2,10},{3,11},{4,0},{5,1},{6,2},{7,3},{8,12},{9,13},{1... | collective-permute-start | bytes 1769480 | tf_op jit(solution)/shard_map/ppermute | solution.py:394
  55.3 17.1 %collective-permute-start.13 = (bf16[2304,128]{1,0:T(8,128)(2,1)}, bf16[2304,128]{1,0:T(8,128)(2,1)}, u32[]{:S(2)}, u32[]{:S(2)}) collective-permute-start(bf16[2304,128]{1,0:T(8,128)(2,1)} %collective-permute-done.7.refs_5_), channel_id=1, source_target_pairs={{0,16},{1,17},{2,18},{3,19},{4,20},{5,21},{6,22},{7,23},{8,24},{9,... | collective-permute-start | bytes 1769480 | tf_op jit(solution)/shard_map/ppermute | solution.py:394
  57.8 14.5 %collective-permute-start.10 = (bf16[2304,128]{1,0:T(8,128)(2,1)}, bf16[2304,128]{1,0:T(8,128)(2,1)}, u32[]{:S(2)}, u32[]{:S(2)}) collective-permute-start(bf16[2304,128]{1,0:T(8,128)(2,1)} %collective-permute-done.6.refs_6_), channel_id=1, source_target_pairs={{0,2},{1,3},{2,0},{3,1},{4,6},{5,7},{6,4},{7,5},{8,10},{9,11},{10,... | collective-permute-start | bytes 1769480 | tf_op jit(solution)/shard_map/ppermute | solution.py:394
  58.5 16.0 %collective-permute-start.11 = (bf16[2304,128]{1,0:T(8,128)(2,1)}, bf16[2304,128]{1,0:T(8,128)(2,1)}, u32[]{:S(2)}, u32[]{:S(2)}) collective-permute-start(bf16[2304,128]{1,0:T(8,128)(2,1)} %shard_map.76.refs_2_), channel_id=1, source_target_pairs={{0,4},{1,5},{2,6},{3,7},{4,12},{5,13},{6,14},{7,15},{8,0},{9,1},{1... | collective-permute-start | bytes 1769480 | tf_op jit(solution)/shard_map/ppermute | solution.py:394
  61.2 1.9 %collective-permute-start.14 = (bf16[128,1024]{1,0:T(8,128)(2,1)}, bf16[128,1024]{1,0:T(8,128)(2,1)}, u32[]{:S(2)}, u32[]{:S(2)}) collective-permute-start(bf16[128,1024]{1,0:T(8,128)(2,1)} %get-tuple-element.58.refs_0_), channel_id=1, source_target_pairs={{0,1},{1,0},{2,3},{3,2},{4,5},{5,4},{6,7},{7,6},{8,9},{9,8},{10,11... | collective-permute-start | bytes 786440 | tf_op jit(solution)/shard_map/ppermute | solution.py:394
  72.4 18.0 %collective-permute-start.20 = (bf16[2304,128]{1,0:T(8,128)(2,1)}, bf16[2304,128]{1,0:T(8,128)(2,1)}, u32[]{:S(2)}, u32[]{:S(2)}) collective-permute-start(bf16[2304,128]{1,0:T(8,128)(2,1)} %collective-permute-done.10.refs_2_), channel_id=1, source_target_pairs={{0,16},{1,17},{2,18},{3,19},{4,20},{5,21},{6,22},{7,23},{8,24},{9,... | collective-permute-start | bytes 1769480 | tf_op jit(solution)/shard_map/ppermute | solution.py:394
  74.4 16.0 %collective-permute-start.19 = (bf16[2304,128]{1,0:T(8,128)(2,1)}, bf16[2304,128]{1,0:T(8,128)(2,1)}, u32[]{:S(2)}, u32[]{:S(2)}) collective-permute-start(bf16[2304,128]{1,0:T(8,128)(2,1)} %collective-permute-done.12.refs_4_), channel_id=1, source_target_pairs={{0,2},{1,3},{2,0},{3,1},{4,6},{5,7},{6,4},{7,5},{8,10},{9,11},{10,... | collective-permute-start | bytes 1769480 | tf_op jit(solution)/shard_map/ppermute | solution.py:394
  74.5 15.9 %collective-permute-start.18 = (bf16[2304,128]{1,0:T(8,128)(2,1)}, bf16[2304,128]{1,0:T(8,128)(2,1)}, u32[]{:S(2)}, u32[]{:S(2)}) collective-permute-start(bf16[2304,128]{1,0:T(8,128)(2,1)} %shard_map.76.refs_2_), channel_id=1, source_target_pairs={{0,8},{1,9},{2,10},{3,11},{4,0},{5,1},{6,2},{7,3},{8,12},{9,13},{1... | collective-permute-start | bytes 1769480 | tf_op jit(solution)/shard_map/ppermute | solution.py:394
  74.8 9.4 %collective-permute-start.16 = (bf16[192,1024]{1,0:T(8,128)(2,1)}, bf16[192,1024]{1,0:T(8,128)(2,1)S(1)}, u32[]{:S(2)}, u32[]{:S(2)}) collective-permute-start(bf16[192,1024]{1,0:T(8,128)(2,1)} %get-tuple-element.65.refs_2_), channel_id=1, source_target_pairs={{0,1},{1,0},{2,3},{3,2},{4,5},{5,4},{6,7},{7,6},{8,9},{9,8},{10,11... | collective-permute-start | bytes 1179656 | tf_op jit(solution)/shard_map/ppermute | solution.py:394
  74.8 9.3 %collective-permute-start.15 = (f32[512,128]{1,0:T(8,128)}, f32[512,128]{1,0:T(8,128)}, u32[]{:S(2)}, u32[]{:S(2)}) collective-permute-start(f32[512,128]{1,0:T(8,128)} %get-tuple-element.62.refs_6_), channel_id=1, source_target_pairs={{0,1},{1,0},{2,3},{3,2},{4,5},{5,4},{6,7},{7,6},{8,9},{9,8},{10,11... | collective-permute-start | bytes 786440 | tf_op jit(solution)/shard_map/ppermute | solution.py:394
  84.2 6.2 %collective-permute-start.17 = (bf16[96,1024]{1,0:T(8,128)(2,1)}, bf16[96,1024]{1,0:T(8,128)(2,1)}, u32[]{:S(2)}, u32[]{:S(2)}) collective-permute-start(bf16[96,1024]{1,0:T(8,128)(2,1)} %get-tuple-element.66.refs_4_), channel_id=1, source_target_pairs={{0,1},{1,0},{2,3},{3,2},{4,5},{5,4},{6,7},{7,6},{8,9},{9,8},{10,11... | collective-permute-start | bytes 589832 | tf_op jit(solution)/shard_map/ppermute | solution.py:394
  84.2 0.8 copy-start
  96.9 2.2 %collective-permute-start.21 = (f32[512,128]{1,0:T(8,128)}, f32[512,128]{1,0:T(8,128)S(1)}, u32[]{:S(2)}, u32[]{:S(2)}) collective-permute-start(f32[512,128]{1,0:T(8,128)} %get-tuple-element.73), channel_id=1, source_target_pairs={{0,1},{1,0},{2,3},{3,2},{4,5},{5,4},{6,7},{7,6},{8,9},{9,8},{10,11... | collective-permute-start | bytes 786440 | tf_op jit(solution)/shard_map/ppermute | solution.py:394
  97.4 1.7 %collective-permute-start.22 = (bf16[96,1024]{1,0:T(8,128)(2,1)}, bf16[96,1024]{1,0:T(8,128)(2,1)S(1)}, u32[]{:S(2)}, u32[]{:S(2)}) collective-permute-start(bf16[96,1024]{1,0:T(8,128)(2,1)} %get-tuple-element.74.refs_6_), channel_id=1, source_target_pairs={{0,1},{1,0},{2,3},{3,2},{4,5},{5,4},{6,7},{7,6},{8,9},{9,8},{10,11... | collective-permute-start | bytes 589832 | tf_op jit(solution)/shard_map/ppermute | solution.py:394
  99.1 0.7 copy-start.2
  99.1 0.8 copy-start.1

commit v15 on v13

--- a/solution.py
+++ b/solution.py
@@ -84,7 +84,7 @@
         copy.wait()
 
 
-def assemble_kernel(back, info_ref, here_ref, there_ref, up_ref, out_ref, down_ref, sems):
+def assemble_kernel(back, info_ref, here_ref, there_ref, up_ref, out_ref, down_ref, own_ref, sems):
     y, core = info_ref[0], info_ref[1]
     place = 1 - y if back else y
     held, rank, quarter = down_ref.shape
@@ -96,13 +96,16 @@
         )
         for n, (source, of_core) in enumerate(((here_ref, core), (there_ref, 1 - core)))
     ]
+    copies.append(
+        pltpu.make_async_copy(up_ref.at[pl.ds(place * (held // 2), held // 2)], own_ref, sems.at[2])
+    )
     started(copies)
-    up = up_ref[pl.ds(place * (held // 2), held // 2)].reshape(held // 2 * rank, -1)
+    awaited(copies)
+    up = own_ref[...].reshape(held // 2 * rank, -1)
     rows = up.shape[0]
     for n in range(up.shape[1] // LANES):
         first = quarter + n * rows
         out_ref[first : first + rows] = up[:, n * LANES : (n + 1) * LANES]
-    awaited(copies)
     for n in range(0, quarter, LANES):
         block = down_ref[:, :, n : n + LANES].reshape(2 * held * rank, LANES)
         out_ref[n : n + LANES] = block.T
@@ -113,15 +116,15 @@
     width = up.shape[2]
     rows = depth // 4 + held // 2 * rank * width // LANES
     anywhere = pl.BlockSpec(memory_space=pl.ANY)
-    vmem = pl.BlockSpec(memory_space=pltpu.VMEM)
     return pl.pallas_call(
         functools.partial(assemble_kernel, back),
         out_shape=jax.ShapeDtypeStruct((rows, LANES), here.dtype),
-        in_specs=[pl.BlockSpec(memory_space=pltpu.SMEM), anywhere, anywhere, vmem],
-        out_specs=vmem,
+        in_specs=[pl.BlockSpec(memory_space=pltpu.SMEM)] + [anywhere] * 3,
+        out_specs=pl.BlockSpec(memory_space=pltpu.VMEM),
         scratch_shapes=[
             pltpu.VMEM((2 * held, rank, depth // 4), here.dtype),
-            pltpu.SemaphoreType.DMA((2,)),
+            pltpu.VMEM((held // 2, rank, width), up.dtype),
+            pltpu.SemaphoreType.DMA((3,)),
         ],
         compiler_params=params(),
     )(info, here, there, up)
@@ -431,15 +434,15 @@
     other_slot = core_swap(row_slot[:, 0])
     total = base(0, None, front)
     row_slots = jnp.concatenate([row_slot, other_slot[:, None]], axis=0)
-
-    z2 = z_ring(after(z1, total))
-    x1 = x_swap(after(z1, x0, total))
-    yx0 = y_swap(after(x0, total))
-    total = base(1, total, z1, x0, total, row_slots)
-
-    def update(number, groups, before, *others):
+    z1, x0, front, total, row_slots = together(z1, x0, front, total, row_slots)
+
+    z2, x1, yx0 = z_ring(z1), x_swap(z1), y_swap(x0)
+    total = base(1, total, total)
+    z2, x1, yx0, front, other, total, info = together(z2, x1, yx0, front, other, total, info)
+
+    def update(number, groups, before):
         return absorb(
-            after(info, *others),
+            info,
             row_slots,
             (0, 1),
             [tokens, other],
@@ -450,28 +453,22 @@
             True,
         )
 
-    z3 = z_back(after(front, z2, total))
-    x2 = x_swap(after(z2, x1, total))
-    yz2 = y_swap(after(z2, yx0, total))
-    back = piece(1, z2, x1, yx0, total, other)
-    *state, up_a = update(0, [((front, z1, x0, z2), 0)], None, x1, yx0, total, back)
+    z3, x2, yz2 = z_back(front), x_swap(z2), y_swap(z2)
+    back = piece(1, z2)
+    *state, up_a = update(0, [((front, z1, x0, z2), 0)], None)
+    z3, x2, yz2, x1, back, state, total = together(z3, x2, yz2, x1, back, state, total)
     there_a = core_swap(up_a)
 
-    zb1 = z_ring(after(back, z3, state[0]))
-    x3 = x_swap(after(z3, x2, state[0]))
-    yx1 = y_swap(after(x1, yz2, state[0]))
-    *state, up_b = update(1, [((back, yx0, yz2), 1)], state, z3, x2, there_a)
+    zb1, x3, yx1 = z_ring(back), x_swap(z3), y_swap(x1)
+    *state, up_b = update(1, [((back, yx0, yz2), 1)], state)
+    zb1, x3, yx1, yz2, back, state, there_a = together(
+        zb1, x3, yx1, yz2, back, state, there_a
+    )
     there_b = core_swap(up_b)
 
-    zb3 = z_back(after(back, zb1, state[0]))
-    xyz2 = x_swap(after(yz2, x3, state[0]))
-    yx3 = y_swap(after(x3, yx1, state[0]))
-    *state, up_c = update(
-        2,
-        [((x1, z3, x2, x3), 0), ((zb1, yx1), 1)],
-        state,
-        there_b,
-    )
+    zb3, xyz2, yx3 = z_back(back), x_swap(yz2), y_swap(x3)
+    *state, up_c = update(2, [((x1, z3, x2, x3), 0), ((zb1, yx1), 1)], state)
+    zb3, xyz2, yx3, state, there_b = together(zb3, xyz2, yx3, state, there_b)
     there_c = core_swap(up_c)
 
     mine, others, up_d = update(3, [((zb3, xyz2, yx3), 1)], state)

time: 104 us -> 102 us (0.981)
  waiting for transfers between devices: 19.6 us -> 16.4 us
  starting transfers between devices: 18.6 us -> 20 us
    ppermute x22, waiting for transfers between devices: 19.6 us -> 16.4 us  [permuted(): return lax.ppermute(array, axes, pairs)]
    ppermute x22, starting transfers between devices: 18.6 us -> 20 us  [permuted(): return lax.ppermute(array, axes, pairs)]
  transfers between devices with their start and end apart: 22 -> 22, of which waited for: 12 -> 13; matrix products, arithmetic and copies ran while one was open for 3% -> 3% of each run, Pallas kernels for 54% -> 54%
where the time goes in v15:
time: 102 us; the launch traced here: 101 us
  Pallas kernels  61.6 us (60%)
  starting transfers between devices  20 us (20%)
  waiting for transfers between devices  16.4 us (16%)
  local copies, waits for them, and re-layouts  2.27 us (2%)
    pallas_call x4, Pallas kernels, absorb(): pl.pallas_call(functools.partial(absorb_kernel, sizes, start, sides, more...  30 us
    ppermute x22, starting transfers between devices, permuted(): return lax.ppermute(array, axes, pairs)  20 us
    pallas_call x2, Pallas kernels, base_part(): pl.pallas_call(functools.partial(base_kernel, steps), out_shape=result, g...  19.5 us
    ppermute x22, waiting for transfers between devices, permuted(): return lax.ppermute(array, axes, pairs)  16.4 us
    pallas_call x1, Pallas kernels, finish(): pl.pallas_call(functools.partial(finish_kernel, len(ups)), out_shape=jax....  6.59 us
    pallas_call x2, Pallas kernels, assemble(): pl.pallas_call(functools.partial(assemble_kernel, back), out_shape=jax.Sh...  5.5 us
  transfers between devices with their start and end apart: 22, of which 13 were waited for; matrix products, arithmetic and copies ran while one was open for 3% of the time, Pallas kernels for 54%

profile of v15, /device:TPU:0, one launch (start us, length us, event | category | flops | bytes accessed | tf_op | source)
XLA Modules:
  0.0 101.3 jit_solution(955560061273840911)
XLA Ops:
  0.0 0.5 collective-permute-start
  0.5 1.2 %dynamic-slice_bitcast_fusion.info_ref = s32[50]{0:T(128)} fusion(s32[32,50]{1,0:T(8,128)} %constant.20.clone, s32[]{:T(128)S(6)} %select_n.8), kind=kLoop, calls=%fused_computation.3 | loop fusion | bytes 404 | tf_op jit(solution)/shard_map/jit(dynamic_index_in_dim)/squeeze | solution.py:406
  1.7 0.8 select_reduce_fusion
  2.5 0.6 collective-permute-done.there_ref
  3.1 0.4 collective-permute-start.7
  3.5 2.8 %shard_map.73.refs_2_ = bf16[2304,128]{1,0:T(8,128)(2,1)} custom-call(s32[50]{0:T(128)} %dynamic-slice_bitcast_fusion.info_ref, bf16[4,16,8192]{2,1,0:T(8,128)(2,1)} %here_ref.3, bf16[4,16,8192]{2,1,0:T(8,128)(2,1)} %collective-permute-done.there_ref, bf16[4,16,1024]{2,1,0:T(8,128)(2,1)} %up_ref.3), custom_call_target="tpu_custom_call" | custom-call | tf_op jit(solution)/shard_map/pallas_call | solution.py:119
  6.2 2.8 %collective-permute-start.1 = (bf16[2304,128]{1,0:T(8,128)(2,1)}, bf16[2304,128]{1,0:T(8,128)(2,1)}, u32[]{:S(2)}, u32[]{:S(2)}) collective-permute-start(bf16[2304,128]{1,0:T(8,128)(2,1)} %shard_map.73.refs_2_), channel_id=1, source_target_pairs={{0,4},{1,5},{2,6},{3,7},{4,12},{5,13},{6,14},{7,15},{8,0},{9,1},{1... | collective-permute-start | bytes 1769480 | tf_op jit(solution)/shard_map/ppermute | solution.py:379
  9.0 1.5 %collective-permute-start.2 = (bf16[2304,128]{1,0:T(8,128)(2,1)}, bf16[2304,128]{1,0:T(8,128)(2,1)}, u32[]{:S(2)}, u32[]{:S(2)}) collective-permute-start(bf16[2304,128]{1,0:T(8,128)(2,1)} %shard_map.73.refs_2_), channel_id=1, source_target_pairs={{0,2},{1,3},{2,0},{3,1},{4,6},{5,7},{6,4},{7,5},{8,10},{9,11},{10,... | collective-permute-start | bytes 1769480 | tf_op jit(solution)/shard_map/ppermute | solution.py:379
  10.5 0.0 collective-permute-start.3
  10.5 9.6 %shard_map.74.refs_0_ = f32[512,1024]{1,0:T(8,128)} custom-call(bf16[512,8192]{1,0:T(8,128)(2,1)} %refs_0_.7, bf16[8192,1024]{1,0:T(8,128)(2,1)} %weight_ref.3), custom_call_target="tpu_custom_call" | custom-call | flops 4294967296 | bytes 14680064 | tf_op jit(solution)/shard_map/pallas_call | solution.py:163
  20.1 0.0 collective-permute-done.3
  20.1 4.1 %collective-permute-done.1.refs_3_ = bf16[2304,128]{1,0:T(8,128)(2,1)} collective-permute-done((bf16[2304,128]{1,0:T(8,128)(2,1)}, bf16[2304,128]{1,0:T(8,128)(2,1)}, u32[]{:S(2)}, u32[]{:S(2)}) %collective-permute-start.1) | collective-permute-done | bytes 589856 | tf_op jit(solution)/shard_map/ppermute | solution.py:379
  24.2 0.4 collective-permute-done.2.refs_4_
  24.6 2.6 %collective-permute-start.4 = (bf16[2304,128]{1,0:T(8,128)(2,1)}, bf16[2304,128]{1,0:T(8,128)(2,1)}, u32[]{:S(2)}, u32[]{:S(2)}) collective-permute-start(bf16[2304,128]{1,0:T(8,128)(2,1)} %collective-permute-done.1.refs_3_), channel_id=1, source_target_pairs={{0,4},{1,5},{2,6},{3,7},{4,12},{5,13},{6,14},{7,15},{8,0},{9,1},{1... | collective-permute-start | bytes 1769480 | tf_op jit(solution)/shard_map/ppermute | solution.py:379
  27.2 1.5 %collective-permute-start.5 = (bf16[2304,128]{1,0:T(8,128)(2,1)}, bf16[2304,128]{1,0:T(8,128)(2,1)}, u32[]{:S(2)}, u32[]{:S(2)}) collective-permute-start(bf16[2304,128]{1,0:T(8,128)(2,1)} %collective-permute-done.1.refs_3_), channel_id=1, source_target_pairs={{0,2},{1,3},{2,0},{3,1},{4,6},{5,7},{6,4},{7,5},{8,10},{9,11},{10,... | collective-permute-start | bytes 1769480 | tf_op jit(solution)/shard_map/ppermute | solution.py:379
  28.7 1.5 %collective-permute-start.6 = (bf16[2304,128]{1,0:T(8,128)(2,1)}, bf16[2304,128]{1,0:T(8,128)(2,1)}, u32[]{:S(2)}, u32[]{:S(2)}) collective-permute-start(bf16[2304,128]{1,0:T(8,128)(2,1)} %collective-permute-done.2.refs_4_), channel_id=1, source_target_pairs={{0,16},{1,17},{2,18},{3,19},{4,20},{5,21},{6,22},{7,23},{8,24},{9,... | collective-permute-start | bytes 1769480 | tf_op jit(solution)/shard_map/ppermute | solution.py:379
  30.2 9.9 %shard_map.75.total_ref = f32[512,1024]{1,0:T(8,128)} custom-call(bf16[512,8192]{1,0:T(8,128)(2,1)} %refs_0_.7, bf16[8192,1024]{1,0:T(8,128)(2,1)} %weight_ref.3, f32[512,1024]{1,0:T(8,128)} %shard_map.74.refs_0_), custom_call_target="tpu_custom_call" | custom-call | flops 4294967296 | bytes 14680064 | tf_op jit(solution)/shard_map/pallas_call | solution.py:163
  40.2 0.3 collective-permute-done.4.refs_5_
  40.4 1.3 %collective-permute-done.5.refs_2_ = bf16[2304,128]{1,0:T(8,128)(2,1)} collective-permute-done((bf16[2304,128]{1,0:T(8,128)(2,1)}, bf16[2304,128]{1,0:T(8,128)(2,1)}, u32[]{:S(2)}, u32[]{:S(2)}) %collective-permute-start.5) | collective-permute-done | bytes 589856 | tf_op jit(solution)/shard_map/ppermute | solution.py:379
  41.7 1.2 %collective-permute-done.6.refs_3_ = bf16[2304,128]{1,0:T(8,128)(2,1)} collective-permute-done((bf16[2304,128]{1,0:T(8,128)(2,1)}, bf16[2304,128]{1,0:T(8,128)(2,1)}, u32[]{:S(2)}, u32[]{:S(2)}) %collective-permute-start.6) | collective-permute-done | bytes 589856 | tf_op jit(solution)/shard_map/ppermute | solution.py:379
  42.9 0.0 collective-permute-done.7.refs_1_
  42.9 1.5 %collective-permute-start.10 = (bf16[2304,128]{1,0:T(8,128)(2,1)}, bf16[2304,128]{1,0:T(8,128)(2,1)}, u32[]{:S(2)}, u32[]{:S(2)}) collective-permute-start(bf16[2304,128]{1,0:T(8,128)(2,1)} %collective-permute-done.4.refs_5_), channel_id=1, source_target_pairs={{0,16},{1,17},{2,18},{3,19},{4,20},{5,21},{6,22},{7,23},{8,24},{9,... | collective-permute-start | bytes 1769480 | tf_op jit(solution)/shard_map/ppermute | solution.py:379
  44.5 0.3 collective-permute-start.8
  44.8 0.5 collective-permute-start.9
  45.3 1.0 %copy.19.row_slot_ref = s32[1024,1]{1,0:T(8,128)} copy(s32[1024,1]{0,1:T(1,128)S(1)} %pad_add_fusion) | data formatting | bytes 8192 | tf_op jit(solution)/shard_map/optimization_barrier | solution.py:411
  46.4 2.7 %shard_map.76.refs_2_ = bf16[2304,128]{1,0:T(8,128)(2,1)} custom-call(s32[50]{0:T(128)} %dynamic-slice_bitcast_fusion.info_ref, bf16[4,16,8192]{2,1,0:T(8,128)(2,1)} %here_ref.3, bf16[4,16,8192]{2,1,0:T(8,128)(2,1)} %collective-permute-done.there_ref, bf16[4,16,1024]{2,1,0:T(8,128)(2,1)} %up_ref.3), custom_call_target="tpu_custom_call" | custom-call | tf_op jit(solution)/shard_map/pallas_call | solution.py:119
  49.1 6.5 %shard_map.77 = (f32[512,128]{1,0:T(8,128)}, f32[512,128]{1,0:T(8,128)}, bf16[128,1024]{1,0:T(8,128)(2,1)}) custom-call(s32[50]{0:T(128)} %dynamic-slice_bitcast_fusion.info_ref, s32[1024,1]{1,0:T(8,128)} %copy.19.row_slot_ref, bf16[512,8192]{1,0:T(8,128)(2,1)} %refs_0_.7, bf16[512,8192]{1,0:T(8,128)(2,1)} %collective-permute-done.7.refs_1_, ...), custom_call_target="tpu_custom_call" | custom-call | flops 2147483648 | bytes 6553600 | tf_op jit(solution)/shard_map/pallas_call | solution.py:281
  55.6 0.6 collective-permute-done.10.refs_4_
  56.3 1.3 %collective-permute-done.8.refs_3_ = bf16[2304,128]{1,0:T(8,128)(2,1)} collective-permute-done((bf16[2304,128]{1,0:T(8,128)(2,1)}, bf16[2304,128]{1,0:T(8,128)(2,1)}, u32[]{:S(2)}, u32[]{:S(2)}) %collective-permute-start.8) | collective-permute-done | bytes 589856 | tf_op jit(solution)/shard_map/ppermute | solution.py:379
  57.6 0.0 collective-permute-done.9.refs_4_
  57.6 3.1 %collective-permute-start.11 = (bf16[2304,128]{1,0:T(8,128)(2,1)}, bf16[2304,128]{1,0:T(8,128)(2,1)}, u32[]{:S(2)}, u32[]{:S(2)}) collective-permute-start(bf16[2304,128]{1,0:T(8,128)(2,1)} %shard_map.76.refs_2_), channel_id=1, source_target_pairs={{0,4},{1,5},{2,6},{3,7},{4,12},{5,13},{6,14},{7,15},{8,0},{9,1},{1... | collective-permute-start | bytes 1769480 | tf_op jit(solution)/shard_map/ppermute | solution.py:379
  60.6 0.2 collective-permute-start.12
  60.8 0.5 collective-permute-start.13
  61.4 0.0 collective-permute-start.14
  61.4 6.5 %shard_map.78 = (f32[512,128]{1,0:T(8,128)}, f32[512,128]{1,0:T(8,128)}, bf16[96,1024]{1,0:T(8,128)(2,1)}) custom-call(s32[50]{0:T(128)} %dynamic-slice_bitcast_fusion.info_ref, s32[1024,1]{1,0:T(8,128)} %copy.19.row_slot_ref, bf16[512,8192]{1,0:T(8,128)(2,1)} %refs_0_.7, bf16[512,8192]{1,0:T(8,128)(2,1)} %collective-permute-done.7.refs_1_, ...), custom_call_target="tpu_custom_call" | custom-call | flops 1610612736 | bytes 5963776 | tf_op jit(solution)/shard_map/pallas_call | solution.py:281
  67.9 0.0 collective-permute-done.14.refs_1_
  67.9 0.0 copy-start.1
  67.9 4.4 %collective-permute-done.11.refs_6_ = bf16[2304,128]{1,0:T(8,128)(2,1)} collective-permute-done((bf16[2304,128]{1,0:T(8,128)(2,1)}, bf16[2304,128]{1,0:T(8,128)(2,1)}, u32[]{:S(2)}, u32[]{:S(2)}) %collective-permute-start.11) | collective-permute-done | bytes 589856 | tf_op jit(solution)/shard_map/ppermute | solution.py:379
  72.3 0.1 collective-permute-done.12.refs_5_
  72.4 0.3 collective-permute-done.13.refs_7_
  72.7 1.1 %collective-permute-start.15 = (bf16[2304,128]{1,0:T(8,128)(2,1)}, bf16[2304,128]{1,0:T(8,128)(2,1)}, u32[]{:S(2)}, u32[]{:S(2)}) collective-permute-start(bf16[2304,128]{1,0:T(8,128)(2,1)} %shard_map.76.refs_2_), channel_id=1, source_target_pairs={{0,8},{1,9},{2,10},{3,11},{4,0},{5,1},{6,2},{7,3},{8,12},{9,13},{1... | collective-permute-start | bytes 1769480 | tf_op jit(solution)/shard_map/ppermute | solution.py:379
  73.7 0.4 collective-permute-start.16
  74.1 0.5 collective-permute-start.17
  74.7 0.0 collective-permute-start.18
  74.7 10.5 %shard_map.79 = (f32[512,128]{1,0:T(8,128)}, f32[512,128]{1,0:T(8,128)}, bf16[192,1024]{1,0:T(8,128)(2,1)}) custom-call(s32[50]{0:T(128)} %dynamic-slice_bitcast_fusion.info_ref, s32[1024,1]{1,0:T(8,128)} %copy.19.row_slot_ref, bf16[512,8192]{1,0:T(8,128)(2,1)} %refs_0_.7, bf16[512,8192]{1,0:T(8,128)(2,1)} %collective-permute-done.7.refs_1_, ...), custom_call_target="tpu_custom_call" | custom-call | flops 3221225472 | bytes 11927552 | tf_op jit(solution)/shard_map/pallas_call | solution.py:281
  85.1 0.0 copy-done.1
  85.1 0.6 collective-permute-start.20
  85.7 0.0 collective-permute-done.18.refs_3_
  85.7 0.0 collective-permute-done.15.refs_2_
  85.7 0.0 collective-permute-done.16.refs_3_
  85.7 0.1 collective-permute-done.17.refs_4_
  85.8 6.5 %shard_map.80 = (f32[512,128]{1,0:T(8,128)}, f32[512,128]{1,0:T(8,128)}, bf16[96,1024]{1,0:T(8,128)(2,1)}) custom-call(s32[50]{0:T(128)} %dynamic-slice_bitcast_fusion.info_ref, s32[1024,1]{1,0:T(8,128)} %copy.19.row_slot_ref, bf16[512,8192]{1,0:T(8,128)(2,1)} %refs_0_.7, bf16[512,8192]{1,0:T(8,128)(2,1)} %collective-permute-done.7.refs_1_, ...), custom_call_target="tpu_custom_call" | custom-call | flops 1610612736 | bytes 5963776 | tf_op jit(solution)/shard_map/pallas_call | solution.py:281
  92.3 0.1 collective-permute-start.19
  92.4 0.5 collective-permute-start.21
  92.9 0.0 collective-permute-done.20.refs_5_
  92.9 0.0 copy-start
  92.9 1.6 %collective-permute-done.21.refs_7_ = bf16[96,1024]{1,0:T(8,128)(2,1)} collective-permute-done((bf16[96,1024]{1,0:T(8,128)(2,1)}, bf16[96,1024]{1,0:T(8,128)(2,1)}, u32[]{:S(2)}, u32[]{:S(2)}) %collective-permute-start.21) | collective-permute-done | bytes 196640 | tf_op jit(solution)/shard_map/ppermute | solution.py:379
  94.6 0.0 collective-permute-done.19.theirs_ref
  94.6 0.0 copy-done
  94.6 6.6 %shard_map.81 = bf16[512,1024]{1,0:T(8,128)(2,1)} custom-call(s32[50]{0:T(128)} %dynamic-slice_bitcast_fusion.info_ref, s32[1024,1]{1,0:T(8,128)} %copy.19.row_slot_ref, f32[512,128]{1,0:T(8,128)} %get-tuple-element.104.mine_ref, f32[512,128]{1,0:T(8,128)} %collective-permute-done.19.theirs_ref, f32[512,1024]{1,0:T(8,128)} %shard_map.75.total_ref, ...), custom_call_target="tpu_custom_call" | custom-call | flops 2147483648 | bytes 5242880 | tf_op jit(solution)/shard_map/pallas_call | solution.py:338
  (1 shorter events, 0.0 us)
Async XLA Ops:
  0.0 3.1 %collective-permute-start = (bf16[4,16,8192]{2,1,0:T(8,128)(2,1)}, bf16[4,16,8192]{2,1,0:T(8,128)(2,1)}, u32[]{:S(2)}, u32[]{:S(2)}) collective-permute-start(bf16[4,16,8192]{2,1,0:T(8,128)(2,1)} %here_ref.3), channel_id=1, source_target_pairs={{0,1},{1,0},{2,3},{3,2},{4,5},{5,4},{6,7},{7,6},{8,9},{9,8},{10,11... | collective-permute-start | bytes 3145736 | tf_op jit(solution)/shard_map/ppermute | solution.py:379
  3.1 39.9 %collective-permute-start.7 = (bf16[512,8192]{1,0:T(8,128)(2,1)}, bf16[512,8192]{1,0:T(8,128)(2,1)}, u32[]{:S(2)}, u32[]{:S(2)}) collective-permute-start(bf16[512,8192]{1,0:T(8,128)(2,1)} %refs_0_.7), channel_id=1, source_target_pairs={{0,1},{1,0},{2,3},{3,2},{4,5},{5,4},{6,7},{7,6},{8,9},{9,8},{10,11... | collective-permute-start | bytes 25165832 | tf_op jit(solution)/shard_map/ppermute | solution.py:379
  6.2 18.0 %collective-permute-start.1 = (bf16[2304,128]{1,0:T(8,128)(2,1)}, bf16[2304,128]{1,0:T(8,128)(2,1)}, u32[]{:S(2)}, u32[]{:S(2)}) collective-permute-start(bf16[2304,128]{1,0:T(8,128)(2,1)} %shard_map.73.refs_2_), channel_id=1, source_target_pairs={{0,4},{1,5},{2,6},{3,7},{4,12},{5,13},{6,14},{7,15},{8,0},{9,1},{1... | collective-permute-start | bytes 1769480 | tf_op jit(solution)/shard_map/ppermute | solution.py:379
  9.0 15.6 %collective-permute-start.2 = (bf16[2304,128]{1,0:T(8,128)(2,1)}, bf16[2304,128]{1,0:T(8,128)(2,1)}, u32[]{:S(2)}, u32[]{:S(2)}) collective-permute-start(bf16[2304,128]{1,0:T(8,128)(2,1)} %shard_map.73.refs_2_), channel_id=1, source_target_pairs={{0,2},{1,3},{2,0},{3,1},{4,6},{5,7},{6,4},{7,5},{8,10},{9,11},{10,... | collective-permute-start | bytes 1769480 | tf_op jit(solution)/shard_map/ppermute | solution.py:379
  10.5 9.6 %collective-permute-start.3 = (s32[512]{0:T(512)S(1)}, s32[512]{0:T(512)S(1)}, u32[]{:S(2)}, u32[]{:S(2)}) collective-permute-start(s32[512]{0:T(512)S(1)} %select_reduce_fusion), channel_id=1, source_target_pairs={{0,1},{1,0},{2,3},{3,2},{4,5},{5,4},{6,7},{7,6},{8,9},{9,8},{10,11... | collective-permute-start | bytes 6152 | tf_op jit(solution)/shard_map/ppermute | solution.py:379
  24.6 15.8 %collective-permute-start.4 = (bf16[2304,128]{1,0:T(8,128)(2,1)}, bf16[2304,128]{1,0:T(8,128)(2,1)}, u32[]{:S(2)}, u32[]{:S(2)}) collective-permute-start(bf16[2304,128]{1,0:T(8,128)(2,1)} %collective-permute-done.1.refs_3_), channel_id=1, source_target_pairs={{0,4},{1,5},{2,6},{3,7},{4,12},{5,13},{6,14},{7,15},{8,0},{9,1},{1... | collective-permute-start | bytes 1769480 | tf_op jit(solution)/shard_map/ppermute | solution.py:379
  27.2 14.5 %collective-permute-start.5 = (bf16[2304,128]{1,0:T(8,128)(2,1)}, bf16[2304,128]{1,0:T(8,128)(2,1)}, u32[]{:S(2)}, u32[]{:S(2)}) collective-permute-start(bf16[2304,128]{1,0:T(8,128)(2,1)} %collective-permute-done.1.refs_3_), channel_id=1, source_target_pairs={{0,2},{1,3},{2,0},{3,1},{4,6},{5,7},{6,4},{7,5},{8,10},{9,11},{10,... | collective-permute-start | bytes 1769480 | tf_op jit(solution)/shard_map/ppermute | solution.py:379
  28.7 14.2 %collective-permute-start.6 = (bf16[2304,128]{1,0:T(8,128)(2,1)}, bf16[2304,128]{1,0:T(8,128)(2,1)}, u32[]{:S(2)}, u32[]{:S(2)}) collective-permute-start(bf16[2304,128]{1,0:T(8,128)(2,1)} %collective-permute-done.2.refs_4_), channel_id=1, source_target_pairs={{0,16},{1,17},{2,18},{3,19},{4,20},{5,21},{6,22},{7,23},{8,24},{9,... | collective-permute-start | bytes 1769480 | tf_op jit(solution)/shard_map/ppermute | solution.py:379
  42.9 13.3 %collective-permute-start.10 = (bf16[2304,128]{1,0:T(8,128)(2,1)}, bf16[2304,128]{1,0:T(8,128)(2,1)}, u32[]{:S(2)}, u32[]{:S(2)}) collective-permute-start(bf16[2304,128]{1,0:T(8,128)(2,1)} %collective-permute-done.4.refs_5_), channel_id=1, source_target_pairs={{0,16},{1,17},{2,18},{3,19},{4,20},{5,21},{6,22},{7,23},{8,24},{9,... | collective-permute-start | bytes 1769480 | tf_op jit(solution)/shard_map/ppermute | solution.py:379
  44.5 13.1 %collective-permute-start.8 = (bf16[2304,128]{1,0:T(8,128)(2,1)}, bf16[2304,128]{1,0:T(8,128)(2,1)}, u32[]{:S(2)}, u32[]{:S(2)}) collective-permute-start(bf16[2304,128]{1,0:T(8,128)(2,1)} %shard_map.73.refs_2_), channel_id=1, source_target_pairs={{0,8},{1,9},{2,10},{3,11},{4,0},{5,1},{6,2},{7,3},{8,12},{9,13},{1... | collective-permute-start | bytes 1769480 | tf_op jit(solution)/shard_map/ppermute | solution.py:379
  44.8 12.8 %collective-permute-start.9 = (bf16[2304,128]{1,0:T(8,128)(2,1)}, bf16[2304,128]{1,0:T(8,128)(2,1)}, u32[]{:S(2)}, u32[]{:S(2)}) collective-permute-start(bf16[2304,128]{1,0:T(8,128)(2,1)} %collective-permute-done.4.refs_5_), channel_id=1, source_target_pairs={{0,2},{1,3},{2,0},{3,1},{4,6},{5,7},{6,4},{7,5},{8,10},{9,11},{10,... | collective-permute-start | bytes 1769480 | tf_op jit(solution)/shard_map/ppermute | solution.py:379
  57.6 14.7 %collective-permute-start.11 = (bf16[2304,128]{1,0:T(8,128)(2,1)}, bf16[2304,128]{1,0:T(8,128)(2,1)}, u32[]{:S(2)}, u32[]{:S(2)}) collective-permute-start(bf16[2304,128]{1,0:T(8,128)(2,1)} %shard_map.76.refs_2_), channel_id=1, source_target_pairs={{0,4},{1,5},{2,6},{3,7},{4,12},{5,13},{6,14},{7,15},{8,0},{9,1},{1... | collective-permute-start | bytes 1769480 | tf_op jit(solution)/shard_map/ppermute | solution.py:379
  60.6 11.7 %collective-permute-start.12 = (bf16[2304,128]{1,0:T(8,128)(2,1)}, bf16[2304,128]{1,0:T(8,128)(2,1)}, u32[]{:S(2)}, u32[]{:S(2)}) collective-permute-start(bf16[2304,128]{1,0:T(8,128)(2,1)} %collective-permute-done.8.refs_3_), channel_id=1, source_target_pairs={{0,2},{1,3},{2,0},{3,1},{4,6},{5,7},{6,4},{7,5},{8,10},{9,11},{10,... | collective-permute-start | bytes 1769480 | tf_op jit(solution)/shard_map/ppermute | solution.py:379
  60.8 11.8 %collective-permute-start.13 = (bf16[2304,128]{1,0:T(8,128)(2,1)}, bf16[2304,128]{1,0:T(8,128)(2,1)}, u32[]{:S(2)}, u32[]{:S(2)}) collective-permute-start(bf16[2304,128]{1,0:T(8,128)(2,1)} %collective-permute-done.5.refs_2_), channel_id=1, source_target_pairs={{0,16},{1,17},{2,18},{3,19},{4,20},{5,21},{6,22},{7,23},{8,24},{9,... | collective-permute-start | bytes 1769480 | tf_op jit(solution)/shard_map/ppermute | solution.py:379
  61.4 6.5 %collective-permute-start.14 = (bf16[128,1024]{1,0:T(8,128)(2,1)}, bf16[128,1024]{1,0:T(8,128)(2,1)S(1)}, u32[]{:S(2)}, u32[]{:S(2)}) collective-permute-start(bf16[128,1024]{1,0:T(8,128)(2,1)} %get-tuple-element.87.refs_0_), channel_id=1, source_target_pairs={{0,1},{1,0},{2,3},{3,2},{4,5},{5,4},{6,7},{7,6},{8,9},{9,8},{10,11... | collective-permute-start | bytes 786440 | tf_op jit(solution)/shard_map/ppermute | solution.py:379
  67.9 17.2 %copy-start.1 = (bf16[128,1024]{1,0:T(8,128)(2,1)}, bf16[128,1024]{1,0:T(8,128)(2,1)S(1)}, u32[]{:S(2)}) copy-start(bf16[128,1024]{1,0:T(8,128)(2,1)S(1)} %collective-permute-done.14.refs_1_) | copy-start | bytes 786436
  72.7 13.0 %collective-permute-start.15 = (bf16[2304,128]{1,0:T(8,128)(2,1)}, bf16[2304,128]{1,0:T(8,128)(2,1)}, u32[]{:S(2)}, u32[]{:S(2)}) collective-permute-start(bf16[2304,128]{1,0:T(8,128)(2,1)} %shard_map.76.refs_2_), channel_id=1, source_target_pairs={{0,8},{1,9},{2,10},{3,11},{4,0},{5,1},{6,2},{7,3},{8,12},{9,13},{1... | collective-permute-start | bytes 1769480 | tf_op jit(solution)/shard_map/ppermute | solution.py:379
  73.7 12.0 %collective-permute-start.16 = (bf16[2304,128]{1,0:T(8,128)(2,1)}, bf16[2304,128]{1,0:T(8,128)(2,1)}, u32[]{:S(2)}, u32[]{:S(2)}) collective-permute-start(bf16[2304,128]{1,0:T(8,128)(2,1)} %collective-permute-done.10.refs_4_), channel_id=1, source_target_pairs={{0,2},{1,3},{2,0},{3,1},{4,6},{5,7},{6,4},{7,5},{8,10},{9,11},{10,... | collective-permute-start | bytes 1769480 | tf_op jit(solution)/shard_map/ppermute | solution.py:379
  74.1 11.7 %collective-permute-start.17 = (bf16[2304,128]{1,0:T(8,128)(2,1)}, bf16[2304,128]{1,0:T(8,128)(2,1)}, u32[]{:S(2)}, u32[]{:S(2)}) collective-permute-start(bf16[2304,128]{1,0:T(8,128)(2,1)} %collective-permute-done.12.refs_5_), channel_id=1, source_target_pairs={{0,16},{1,17},{2,18},{3,19},{4,20},{5,21},{6,22},{7,23},{8,24},{9,... | collective-permute-start | bytes 1769480 | tf_op jit(solution)/shard_map/ppermute | solution.py:379
  74.7 11.0 %collective-permute-start.18 = (bf16[96,1024]{1,0:T(8,128)(2,1)}, bf16[96,1024]{1,0:T(8,128)(2,1)}, u32[]{:S(2)}, u32[]{:S(2)}) collective-permute-start(bf16[96,1024]{1,0:T(8,128)(2,1)} %get-tuple-element.98.refs_2_), channel_id=1, source_target_pairs={{0,1},{1,0},{2,3},{3,2},{4,5},{5,4},{6,7},{7,6},{8,9},{9,8},{10,11... | collective-permute-start | bytes 589832 | tf_op jit(solution)/shard_map/ppermute | solution.py:379
  85.1 7.8 %collective-permute-start.20 = (bf16[192,1024]{1,0:T(8,128)(2,1)}, bf16[192,1024]{1,0:T(8,128)(2,1)S(1)}, u32[]{:S(2)}, u32[]{:S(2)}) collective-permute-start(bf16[192,1024]{1,0:T(8,128)(2,1)} %get-tuple-element.109.refs_4_), channel_id=1, source_target_pairs={{0,1},{1,0},{2,3},{3,2},{4,5},{5,4},{6,7},{7,6},{8,9},{9,8},{10,11... | collective-permute-start | bytes 1179656 | tf_op jit(solution)/shard_map/ppermute | solution.py:379
  92.3 2.2 %collective-permute-start.19 = (f32[512,128]{1,0:T(8,128)}, f32[512,128]{1,0:T(8,128)}, u32[]{:S(2)}, u32[]{:S(2)}) collective-permute-start(f32[512,128]{1,0:T(8,128)} %get-tuple-element.105), channel_id=1, source_target_pairs={{0,1},{1,0},{2,3},{3,2},{4,5},{5,4},{6,7},{7,6},{8,9},{9,8},{10,11... | collective-permute-start | bytes 786440 | tf_op jit(solution)/shard_map/ppermute | solution.py:379
  92.4 2.1 %collective-permute-start.21 = (bf16[96,1024]{1,0:T(8,128)(2,1)}, bf16[96,1024]{1,0:T(8,128)(2,1)}, u32[]{:S(2)}, u32[]{:S(2)}) collective-permute-start(bf16[96,1024]{1,0:T(8,128)(2,1)} %get-tuple-element.110.refs_6_), channel_id=1, source_target_pairs={{0,1},{1,0},{2,3},{3,2},{4,5},{5,4},{6,7},{7,6},{8,9},{9,8},{10,11... | collective-permute-start | bytes 589832 | tf_op jit(solution)/shard_map/ppermute | solution.py:379
  92.9 1.7 %copy-start = (bf16[192,1024]{1,0:T(8,128)(2,1)}, bf16[192,1024]{1,0:T(8,128)(2,1)S(1)}, u32[]{:S(2)}) copy-start(bf16[192,1024]{1,0:T(8,128)(2,1)S(1)} %collective-permute-done.20.refs_5_) | copy-start | bytes 1179652

commit v16 on v15

--- a/solution.py
+++ b/solution.py
@@ -188,7 +188,8 @@
     before, refs = refs[: len(sides) * more], refs[len(sides) * more :]
     outs, refs = refs[: len(sides)], refs[len(sides) :]
     up_ref, refs = (refs[0], refs[1:]) if has_up else (None, refs)
-    rows_ref, down_refs, sems = refs[0], refs[1:-1], refs[-1]
+    rows_ref, row_slot, held_refs, refs = refs[0], refs[1], refs[2 : 2 + len(before)], refs[2 + len(before) :]
+    down_refs, sems = refs[:-1], refs[-1]
     rows = token_refs[0].shape[0]
     quarter = rows_ref.shape[2]
     y, core = info_ref[0], info_ref[1]
@@ -224,10 +225,10 @@
                     rows_ref.at[place, pl.ds(i * rows, rows), pl.ds(low, high - low)],
                 )
         first += size
+    begin("late", row_slot_ref, row_slot)
+    for source, target in zip(before, held_refs):
+        begin("late", source, target)
     lane_slot = lax.broadcasted_iota(jnp.int32, (1, LANES), 1) // RANK
-    row_slot = jnp.concatenate(
-        [row_slot_ref[side * rows : (side + 1) * rows] for side in sides], axis=0
-    )
     state = None
     first = 0
     for n, ((size, back), down_ref) in enumerate(zip(groups, down_refs)):
@@ -240,11 +241,13 @@
                 preferred_element_type=jnp.float32,
             )
             shrink = part if shrink is None else shrink + part
+        if n == 0:
+            awaited(waits["late"])
         for i in range(size):
             lanes, which = slice(i * LANES, (i + 1) * LANES), first + i
             chip = info_ref[2 + 2 * len(PIECES) + start + which]
             wanted = lane_slot + chip * (LANES // RANK)
-            kept = jnp.where(row_slot == wanted, shrink[:, lanes], 0.0)
+            kept = jnp.where(row_slot[...] == wanted, shrink[:, lanes], 0.0)
             state = kept if state is None else state + kept
         if has_up:
             awaited(waits[n, quarter])
@@ -259,7 +262,7 @@
         first += size
     for i, out_ref in enumerate(outs):
         own = state[i * rows : (i + 1) * rows]
-        out_ref[...] = own + before[i][...] if more else own
+        out_ref[...] = own + held_refs[i][...] if more else own
 
 
 def absorb(info, row_slots, sides, tokens, width, groups, start, before, has_up):
@@ -276,16 +279,19 @@
     up = jax.ShapeDtypeStruct((up_rows, width), tokens[0].dtype)
     quarters = len({back for _, back in groups})
     cuts = len(QUARTER_CUTS) - 1
-    copies = len(pieces) * (cuts + has_up) + len(sides) * quarters * cuts
+    copies = len(pieces) * (cuts + has_up) + len(sides) * (quarters * cuts + more) + 1
     outs = (state,) * len(sides) + (up,) * has_up
     return pl.pallas_call(
         functools.partial(absorb_kernel, sizes, start, sides, more, has_up),
         out_shape=outs,
-        in_specs=[pl.BlockSpec(memory_space=pltpu.SMEM), vmem]
-        + [anywhere] * (len(sides) + len(pieces))
-        + [vmem] * (len(sides) * more),
+        in_specs=[pl.BlockSpec(memory_space=pltpu.SMEM)]
+        + [anywhere] * (1 + len(sides) + len(pieces) + len(sides) * more),
         out_specs=(vmem,) * len(outs),
-        scratch_shapes=[pltpu.VMEM((quarters, len(sides) * rows, quarter), tokens[0].dtype)]
+        scratch_shapes=[
+            pltpu.VMEM((quarters, len(sides) * rows, quarter), tokens[0].dtype),
+            pltpu.VMEM(row_slots.shape, row_slots.dtype),
+        ]
+        + [pltpu.VMEM((rows, LANES), jnp.float32)] * (len(sides) * more)
         + [pltpu.VMEM((height, size * LANES), tokens[0].dtype) for size, _ in sizes]
         + [pltpu.SemaphoreType.DMA((copies,))],
         cost_estimate=pl.CostEstimate(

time: 102 us -> 101 us (level)
  no operation moved by 1% of the time
where the time goes in v16:
time: 101 us
  Pallas kernels  60.6 us (60%)
  starting transfers between devices  20 us (20%)
  waiting for transfers between devices  16.8 us (17%)
  local copies, waits for them, and re-layouts  2.27 us (2%)
    pallas_call x4, Pallas kernels, absorb(): pl.pallas_call(functools.partial(absorb_kernel, sizes, start, sides, more...  29 us
    ppermute x22, starting transfers between devices, permuted(): return lax.ppermute(array, axes, pairs)  20 us
    pallas_call x2, Pallas kernels, base_part(): pl.pallas_call(functools.partial(base_kernel, steps), out_shape=result, g...  19.5 us
    ppermute x22, waiting for transfers between devices, permuted(): return lax.ppermute(array, axes, pairs)  16.8 us
    pallas_call x1, Pallas kernels, finish(): pl.pallas_call(functools.partial(finish_kernel, len(ups)), out_shape=jax....  6.59 us
    pallas_call x2, Pallas kernels, assemble(): pl.pallas_call(functools.partial(assemble_kernel, back), out_shape=jax.Sh...  5.5 us
  transfers between devices with their start and end apart: 22, of which 13 were waited for; matrix products, arithmetic and copies ran while one was open for 3% of the time, Pallas kernels for 54%

profile of v16, /device:TPU:0, one launch (start us, length us, event | category | flops | bytes accessed | tf_op | source)
XLA Modules:
  0.0 100.7 jit_solution(11317064554184455749)
XLA Ops:
  0.0 0.5 collective-permute-start
  0.5 1.2 %dynamic-slice_bitcast_fusion.info_ref = s32[50]{0:T(128)} fusion(s32[32,50]{1,0:T(8,128)} %constant.20.clone, s32[]{:T(128)S(6)} %select_n.8), kind=kLoop, calls=%fused_computation.3 | loop fusion | bytes 404 | tf_op jit(solution)/shard_map/jit(dynamic_index_in_dim)/squeeze | solution.py:412
  1.7 0.8 select_reduce_fusion
  2.5 0.6 collective-permute-done.there_ref
  3.1 0.4 collective-permute-start.7
  3.5 2.8 %shard_map.73.refs_2_ = bf16[2304,128]{1,0:T(8,128)(2,1)} custom-call(s32[50]{0:T(128)} %dynamic-slice_bitcast_fusion.info_ref, bf16[4,16,8192]{2,1,0:T(8,128)(2,1)} %here_ref.3, bf16[4,16,8192]{2,1,0:T(8,128)(2,1)} %collective-permute-done.there_ref, bf16[4,16,1024]{2,1,0:T(8,128)(2,1)} %up_ref.3), custom_call_target="tpu_custom_call" | custom-call | tf_op jit(solution)/shard_map/pallas_call | solution.py:119
  6.2 2.8 %collective-permute-start.1 = (bf16[2304,128]{1,0:T(8,128)(2,1)}, bf16[2304,128]{1,0:T(8,128)(2,1)}, u32[]{:S(2)}, u32[]{:S(2)}) collective-permute-start(bf16[2304,128]{1,0:T(8,128)(2,1)} %shard_map.73.refs_2_), channel_id=1, source_target_pairs={{0,4},{1,5},{2,6},{3,7},{4,12},{5,13},{6,14},{7,15},{8,0},{9,1},{1... | collective-permute-start | bytes 1769480 | tf_op jit(solution)/shard_map/ppermute | solution.py:385
  9.0 1.5 %collective-permute-start.2 = (bf16[2304,128]{1,0:T(8,128)(2,1)}, bf16[2304,128]{1,0:T(8,128)(2,1)}, u32[]{:S(2)}, u32[]{:S(2)}) collective-permute-start(bf16[2304,128]{1,0:T(8,128)(2,1)} %shard_map.73.refs_2_), channel_id=1, source_target_pairs={{0,2},{1,3},{2,0},{3,1},{4,6},{5,7},{6,4},{7,5},{8,10},{9,11},{10,... | collective-permute-start | bytes 1769480 | tf_op jit(solution)/shard_map/ppermute | solution.py:385
  10.5 0.0 collective-permute-start.3
  10.5 9.6 %shard_map.74.refs_0_ = f32[512,1024]{1,0:T(8,128)} custom-call(bf16[512,8192]{1,0:T(8,128)(2,1)} %refs_0_.7, bf16[8192,1024]{1,0:T(8,128)(2,1)} %weight_ref.3), custom_call_target="tpu_custom_call" | custom-call | flops 4294967296 | bytes 14680064 | tf_op jit(solution)/shard_map/pallas_call | solution.py:163
  20.1 0.0 collective-permute-done.3
  20.1 4.1 %collective-permute-done.1.refs_3_ = bf16[2304,128]{1,0:T(8,128)(2,1)} collective-permute-done((bf16[2304,128]{1,0:T(8,128)(2,1)}, bf16[2304,128]{1,0:T(8,128)(2,1)}, u32[]{:S(2)}, u32[]{:S(2)}) %collective-permute-start.1) | collective-permute-done | bytes 589856 | tf_op jit(solution)/shard_map/ppermute | solution.py:385
  24.2 0.4 collective-permute-done.2.refs_4_
  24.6 2.6 %collective-permute-start.4 = (bf16[2304,128]{1,0:T(8,128)(2,1)}, bf16[2304,128]{1,0:T(8,128)(2,1)}, u32[]{:S(2)}, u32[]{:S(2)}) collective-permute-start(bf16[2304,128]{1,0:T(8,128)(2,1)} %collective-permute-done.1.refs_3_), channel_id=1, source_target_pairs={{0,4},{1,5},{2,6},{3,7},{4,12},{5,13},{6,14},{7,15},{8,0},{9,1},{1... | collective-permute-start | bytes 1769480 | tf_op jit(solution)/shard_map/ppermute | solution.py:385
  27.2 1.5 %collective-permute-start.5 = (bf16[2304,128]{1,0:T(8,128)(2,1)}, bf16[2304,128]{1,0:T(8,128)(2,1)}, u32[]{:S(2)}, u32[]{:S(2)}) collective-permute-start(bf16[2304,128]{1,0:T(8,128)(2,1)} %collective-permute-done.1.refs_3_), channel_id=1, source_target_pairs={{0,2},{1,3},{2,0},{3,1},{4,6},{5,7},{6,4},{7,5},{8,10},{9,11},{10,... | collective-permute-start | bytes 1769480 | tf_op jit(solution)/shard_map/ppermute | solution.py:385
  28.7 1.5 %collective-permute-start.6 = (bf16[2304,128]{1,0:T(8,128)(2,1)}, bf16[2304,128]{1,0:T(8,128)(2,1)}, u32[]{:S(2)}, u32[]{:S(2)}) collective-permute-start(bf16[2304,128]{1,0:T(8,128)(2,1)} %collective-permute-done.2.refs_4_), channel_id=1, source_target_pairs={{0,16},{1,17},{2,18},{3,19},{4,20},{5,21},{6,22},{7,23},{8,24},{9,... | collective-permute-start | bytes 1769480 | tf_op jit(solution)/shard_map/ppermute | solution.py:385
  30.2 9.9 %shard_map.75.total_ref = f32[512,1024]{1,0:T(8,128)} custom-call(bf16[512,8192]{1,0:T(8,128)(2,1)} %refs_0_.7, bf16[8192,1024]{1,0:T(8,128)(2,1)} %weight_ref.3, f32[512,1024]{1,0:T(8,128)} %shard_map.74.refs_0_), custom_call_target="tpu_custom_call" | custom-call | flops 4294967296 | bytes 14680064 | tf_op jit(solution)/shard_map/pallas_call | solution.py:163
  40.2 0.3 collective-permute-done.4.refs_5_
  40.4 1.3 %collective-permute-done.5.refs_2_ = bf16[2304,128]{1,0:T(8,128)(2,1)} collective-permute-done((bf16[2304,128]{1,0:T(8,128)(2,1)}, bf16[2304,128]{1,0:T(8,128)(2,1)}, u32[]{:S(2)}, u32[]{:S(2)}) %collective-permute-start.5) | collective-permute-done | bytes 589856 | tf_op jit(solution)/shard_map/ppermute | solution.py:385
  41.7 1.2 %collective-permute-done.6.refs_3_ = bf16[2304,128]{1,0:T(8,128)(2,1)} collective-permute-done((bf16[2304,128]{1,0:T(8,128)(2,1)}, bf16[2304,128]{1,0:T(8,128)(2,1)}, u32[]{:S(2)}, u32[]{:S(2)}) %collective-permute-start.6) | collective-permute-done | bytes 589856 | tf_op jit(solution)/shard_map/ppermute | solution.py:385
  42.9 0.0 collective-permute-done.7.refs_1_
  42.9 1.5 %collective-permute-start.10 = (bf16[2304,128]{1,0:T(8,128)(2,1)}, bf16[2304,128]{1,0:T(8,128)(2,1)}, u32[]{:S(2)}, u32[]{:S(2)}) collective-permute-start(bf16[2304,128]{1,0:T(8,128)(2,1)} %collective-permute-done.4.refs_5_), channel_id=1, source_target_pairs={{0,16},{1,17},{2,18},{3,19},{4,20},{5,21},{6,22},{7,23},{8,24},{9,... | collective-permute-start | bytes 1769480 | tf_op jit(solution)/shard_map/ppermute | solution.py:385
  44.5 0.3 collective-permute-start.8
  44.8 0.5 collective-permute-start.9
  45.3 1.0 %copy.19.row_slot_ref = s32[1024,1]{1,0:T(8,128)} copy(s32[1024,1]{0,1:T(1,128)S(1)} %pad_add_fusion) | data formatting | bytes 8192 | tf_op jit(solution)/shard_map/optimization_barrier | solution.py:417
  46.4 2.7 %shard_map.76.refs_2_ = bf16[2304,128]{1,0:T(8,128)(2,1)} custom-call(s32[50]{0:T(128)} %dynamic-slice_bitcast_fusion.info_ref, bf16[4,16,8192]{2,1,0:T(8,128)(2,1)} %here_ref.3, bf16[4,16,8192]{2,1,0:T(8,128)(2,1)} %collective-permute-done.there_ref, bf16[4,16,1024]{2,1,0:T(8,128)(2,1)} %up_ref.3), custom_call_target="tpu_custom_call" | custom-call | tf_op jit(solution)/shard_map/pallas_call | solution.py:119
  49.1 6.4 %shard_map.77 = (f32[512,128]{1,0:T(8,128)}, f32[512,128]{1,0:T(8,128)}, bf16[128,1024]{1,0:T(8,128)(2,1)}) custom-call(s32[50]{0:T(128)} %dynamic-slice_bitcast_fusion.info_ref, s32[1024,1]{1,0:T(8,128)} %copy.19.row_slot_ref, bf16[512,8192]{1,0:T(8,128)(2,1)} %refs_0_.7, bf16[512,8192]{1,0:T(8,128)(2,1)} %collective-permute-done.7.refs_1_, ...), custom_call_target="tpu_custom_call" | custom-call | flops 2147483648 | bytes 6553600 | tf_op jit(solution)/shard_map/pallas_call | solution.py:284
  55.5 0.7 collective-permute-done.10.refs_4_
  56.3 1.3 %collective-permute-done.8.refs_3_ = bf16[2304,128]{1,0:T(8,128)(2,1)} collective-permute-done((bf16[2304,128]{1,0:T(8,128)(2,1)}, bf16[2304,128]{1,0:T(8,128)(2,1)}, u32[]{:S(2)}, u32[]{:S(2)}) %collective-permute-start.8) | collective-permute-done | bytes 589856 | tf_op jit(solution)/shard_map/ppermute | solution.py:385
  57.6 0.0 collective-permute-done.9.refs_4_
  57.6 3.1 %collective-permute-start.11 = (bf16[2304,128]{1,0:T(8,128)(2,1)}, bf16[2304,128]{1,0:T(8,128)(2,1)}, u32[]{:S(2)}, u32[]{:S(2)}) collective-permute-start(bf16[2304,128]{1,0:T(8,128)(2,1)} %shard_map.76.refs_2_), channel_id=1, source_target_pairs={{0,4},{1,5},{2,6},{3,7},{4,12},{5,13},{6,14},{7,15},{8,0},{9,1},{1... | collective-permute-start | bytes 1769480 | tf_op jit(solution)/shard_map/ppermute | solution.py:385
  60.6 0.2 collective-permute-start.12
  60.8 0.5 collective-permute-start.13
  61.4 0.0 collective-permute-start.14
  61.4 6.2 %shard_map.78 = (f32[512,128]{1,0:T(8,128)}, f32[512,128]{1,0:T(8,128)}, bf16[96,1024]{1,0:T(8,128)(2,1)}) custom-call(s32[50]{0:T(128)} %dynamic-slice_bitcast_fusion.info_ref, s32[1024,1]{1,0:T(8,128)} %copy.19.row_slot_ref, bf16[512,8192]{1,0:T(8,128)(2,1)} %refs_0_.7, bf16[512,8192]{1,0:T(8,128)(2,1)} %collective-permute-done.7.refs_1_, ...), custom_call_target="tpu_custom_call" | custom-call | flops 1610612736 | bytes 5963776 | tf_op jit(solution)/shard_map/pallas_call | solution.py:284
  67.6 0.0 collective-permute-done.14.refs_1_
  67.6 0.0 copy-start.1
  67.6 4.7 %collective-permute-done.11.refs_6_ = bf16[2304,128]{1,0:T(8,128)(2,1)} collective-permute-done((bf16[2304,128]{1,0:T(8,128)(2,1)}, bf16[2304,128]{1,0:T(8,128)(2,1)}, u32[]{:S(2)}, u32[]{:S(2)}) %collective-permute-start.11) | collective-permute-done | bytes 589856 | tf_op jit(solution)/shard_map/ppermute | solution.py:385
  72.3 0.1 collective-permute-done.12.refs_5_
  72.4 0.3 collective-permute-done.13.refs_7_
  72.7 1.1 %collective-permute-start.15 = (bf16[2304,128]{1,0:T(8,128)(2,1)}, bf16[2304,128]{1,0:T(8,128)(2,1)}, u32[]{:S(2)}, u32[]{:S(2)}) collective-permute-start(bf16[2304,128]{1,0:T(8,128)(2,1)} %shard_map.76.refs_2_), channel_id=1, source_target_pairs={{0,8},{1,9},{2,10},{3,11},{4,0},{5,1},{6,2},{7,3},{8,12},{9,13},{1... | collective-permute-start | bytes 1769480 | tf_op jit(solution)/shard_map/ppermute | solution.py:385
  73.7 0.4 collective-permute-start.16
  74.1 0.5 collective-permute-start.17
  74.7 0.0 collective-permute-start.18
  74.7 10.2 %shard_map.79 = (f32[512,128]{1,0:T(8,128)}, f32[512,128]{1,0:T(8,128)}, bf16[192,1024]{1,0:T(8,128)(2,1)}) custom-call(s32[50]{0:T(128)} %dynamic-slice_bitcast_fusion.info_ref, s32[1024,1]{1,0:T(8,128)} %copy.19.row_slot_ref, bf16[512,8192]{1,0:T(8,128)(2,1)} %refs_0_.7, bf16[512,8192]{1,0:T(8,128)(2,1)} %collective-permute-done.7.refs_1_, ...), custom_call_target="tpu_custom_call" | custom-call | flops 3221225472 | bytes 11927552 | tf_op jit(solution)/shard_map/pallas_call | solution.py:284
  84.9 0.0 copy-done.1
  84.9 0.6 collective-permute-start.20
  85.4 0.0 collective-permute-done.18.refs_3_
  85.4 0.0 collective-permute-done.15.refs_2_
  85.5 0.0 collective-permute-done.16.refs_3_
  85.5 0.1 collective-permute-done.17.refs_4_
  85.6 6.2 %shard_map.80 = (f32[512,128]{1,0:T(8,128)}, f32[512,128]{1,0:T(8,128)}, bf16[96,1024]{1,0:T(8,128)(2,1)}) custom-call(s32[50]{0:T(128)} %dynamic-slice_bitcast_fusion.info_ref, s32[1024,1]{1,0:T(8,128)} %copy.19.row_slot_ref, bf16[512,8192]{1,0:T(8,128)(2,1)} %refs_0_.7, bf16[512,8192]{1,0:T(8,128)(2,1)} %collective-permute-done.7.refs_1_, ...), custom_call_target="tpu_custom_call" | custom-call | flops 1610612736 | bytes 5963776 | tf_op jit(solution)/shard_map/pallas_call | solution.py:284
  91.7 0.1 collective-permute-start.19
  91.8 0.5 collective-permute-start.21
  92.3 0.0 collective-permute-done.20.refs_5_
  92.3 0.0 copy-start
  92.3 1.6 %collective-permute-done.21.refs_7_ = bf16[96,1024]{1,0:T(8,128)(2,1)} collective-permute-done((bf16[96,1024]{1,0:T(8,128)(2,1)}, bf16[96,1024]{1,0:T(8,128)(2,1)}, u32[]{:S(2)}, u32[]{:S(2)}) %collective-permute-start.21) | collective-permute-done | bytes 196640 | tf_op jit(solution)/shard_map/ppermute | solution.py:385
  94.0 0.0 collective-permute-done.19.theirs_ref
  94.0 0.0 copy-done
  94.0 6.6 %shard_map.81 = bf16[512,1024]{1,0:T(8,128)(2,1)} custom-call(s32[50]{0:T(128)} %dynamic-slice_bitcast_fusion.info_ref, s32[1024,1]{1,0:T(8,128)} %copy.19.row_slot_ref, f32[512,128]{1,0:T(8,128)} %get-tuple-element.104.mine_ref, f32[512,128]{1,0:T(8,128)} %collective-permute-done.19.theirs_ref, f32[512,1024]{1,0:T(8,128)} %shard_map.75.total_ref, ...), custom_call_target="tpu_custom_call" | custom-call | flops 2147483648 | bytes 5242880 | tf_op jit(solution)/shard_map/pallas_call | solution.py:344
  (1 shorter events, 0.0 us)
Async XLA Ops:
  0.0 3.1 %collective-permute-start = (bf16[4,16,8192]{2,1,0:T(8,128)(2,1)}, bf16[4,16,8192]{2,1,0:T(8,128)(2,1)}, u32[]{:S(2)}, u32[]{:S(2)}) collective-permute-start(bf16[4,16,8192]{2,1,0:T(8,128)(2,1)} %here_ref.3), channel_id=1, source_target_pairs={{0,1},{1,0},{2,3},{3,2},{4,5},{5,4},{6,7},{7,6},{8,9},{9,8},{10,11... | collective-permute-start | bytes 3145736 | tf_op jit(solution)/shard_map/ppermute | solution.py:385
  3.1 39.9 %collective-permute-start.7 = (bf16[512,8192]{1,0:T(8,128)(2,1)}, bf16[512,8192]{1,0:T(8,128)(2,1)}, u32[]{:S(2)}, u32[]{:S(2)}) collective-permute-start(bf16[512,8192]{1,0:T(8,128)(2,1)} %refs_0_.7), channel_id=1, source_target_pairs={{0,1},{1,0},{2,3},{3,2},{4,5},{5,4},{6,7},{7,6},{8,9},{9,8},{10,11... | collective-permute-start | bytes 25165832 | tf_op jit(solution)/shard_map/ppermute | solution.py:385
  6.2 18.0 %collective-permute-start.1 = (bf16[2304,128]{1,0:T(8,128)(2,1)}, bf16[2304,128]{1,0:T(8,128)(2,1)}, u32[]{:S(2)}, u32[]{:S(2)}) collective-permute-start(bf16[2304,128]{1,0:T(8,128)(2,1)} %shard_map.73.refs_2_), channel_id=1, source_target_pairs={{0,4},{1,5},{2,6},{3,7},{4,12},{5,13},{6,14},{7,15},{8,0},{9,1},{1... | collective-permute-start | bytes 1769480 | tf_op jit(solution)/shard_map/ppermute | solution.py:385
  9.0 15.6 %collective-permute-start.2 = (bf16[2304,128]{1,0:T(8,128)(2,1)}, bf16[2304,128]{1,0:T(8,128)(2,1)}, u32[]{:S(2)}, u32[]{:S(2)}) collective-permute-start(bf16[2304,128]{1,0:T(8,128)(2,1)} %shard_map.73.refs_2_), channel_id=1, source_target_pairs={{0,2},{1,3},{2,0},{3,1},{4,6},{5,7},{6,4},{7,5},{8,10},{9,11},{10,... | collective-permute-start | bytes 1769480 | tf_op jit(solution)/shard_map/ppermute | solution.py:385
  10.5 9.6 %collective-permute-start.3 = (s32[512]{0:T(512)S(1)}, s32[512]{0:T(512)S(1)}, u32[]{:S(2)}, u32[]{:S(2)}) collective-permute-start(s32[512]{0:T(512)S(1)} %select_reduce_fusion), channel_id=1, source_target_pairs={{0,1},{1,0},{2,3},{3,2},{4,5},{5,4},{6,7},{7,6},{8,9},{9,8},{10,11... | collective-permute-start | bytes 6152 | tf_op jit(solution)/shard_map/ppermute | solution.py:385
  24.6 15.8 %collective-permute-start.4 = (bf16[2304,128]{1,0:T(8,128)(2,1)}, bf16[2304,128]{1,0:T(8,128)(2,1)}, u32[]{:S(2)}, u32[]{:S(2)}) collective-permute-start(bf16[2304,128]{1,0:T(8,128)(2,1)} %collective-permute-done.1.refs_3_), channel_id=1, source_target_pairs={{0,4},{1,5},{2,6},{3,7},{4,12},{5,13},{6,14},{7,15},{8,0},{9,1},{1... | collective-permute-start | bytes 1769480 | tf_op jit(solution)/shard_map/ppermute | solution.py:385
  27.2 14.5 %collective-permute-start.5 = (bf16[2304,128]{1,0:T(8,128)(2,1)}, bf16[2304,128]{1,0:T(8,128)(2,1)}, u32[]{:S(2)}, u32[]{:S(2)}) collective-permute-start(bf16[2304,128]{1,0:T(8,128)(2,1)} %collective-permute-done.1.refs_3_), channel_id=1, source_target_pairs={{0,2},{1,3},{2,0},{3,1},{4,6},{5,7},{6,4},{7,5},{8,10},{9,11},{10,... | collective-permute-start | bytes 1769480 | tf_op jit(solution)/shard_map/ppermute | solution.py:385
  28.7 14.2 %collective-permute-start.6 = (bf16[2304,128]{1,0:T(8,128)(2,1)}, bf16[2304,128]{1,0:T(8,128)(2,1)}, u32[]{:S(2)}, u32[]{:S(2)}) collective-permute-start(bf16[2304,128]{1,0:T(8,128)(2,1)} %collective-permute-done.2.refs_4_), channel_id=1, source_target_pairs={{0,16},{1,17},{2,18},{3,19},{4,20},{5,21},{6,22},{7,23},{8,24},{9,... | collective-permute-start | bytes 1769480 | tf_op jit(solution)/shard_map/ppermute | solution.py:385
  42.9 13.3 %collective-permute-start.10 = (bf16[2304,128]{1,0:T(8,128)(2,1)}, bf16[2304,128]{1,0:T(8,128)(2,1)}, u32[]{:S(2)}, u32[]{:S(2)}) collective-permute-start(bf16[2304,128]{1,0:T(8,128)(2,1)} %collective-permute-done.4.refs_5_), channel_id=1, source_target_pairs={{0,16},{1,17},{2,18},{3,19},{4,20},{5,21},{6,22},{7,23},{8,24},{9,... | collective-permute-start | bytes 1769480 | tf_op jit(solution)/shard_map/ppermute | solution.py:385
  44.5 13.1 %collective-permute-start.8 = (bf16[2304,128]{1,0:T(8,128)(2,1)}, bf16[2304,128]{1,0:T(8,128)(2,1)}, u32[]{:S(2)}, u32[]{:S(2)}) collective-permute-start(bf16[2304,128]{1,0:T(8,128)(2,1)} %shard_map.73.refs_2_), channel_id=1, source_target_pairs={{0,8},{1,9},{2,10},{3,11},{4,0},{5,1},{6,2},{7,3},{8,12},{9,13},{1... | collective-permute-start | bytes 1769480 | tf_op jit(solution)/shard_map/ppermute | solution.py:385
  44.8 12.8 %collective-permute-start.9 = (bf16[2304,128]{1,0:T(8,128)(2,1)}, bf16[2304,128]{1,0:T(8,128)(2,1)}, u32[]{:S(2)}, u32[]{:S(2)}) collective-permute-start(bf16[2304,128]{1,0:T(8,128)(2,1)} %collective-permute-done.4.refs_5_), channel_id=1, source_target_pairs={{0,2},{1,3},{2,0},{3,1},{4,6},{5,7},{6,4},{7,5},{8,10},{9,11},{10,... | collective-permute-start | bytes 1769480 | tf_op jit(solution)/shard_map/ppermute | solution.py:385
  57.6 14.7 %collective-permute-start.11 = (bf16[2304,128]{1,0:T(8,128)(2,1)}, bf16[2304,128]{1,0:T(8,128)(2,1)}, u32[]{:S(2)}, u32[]{:S(2)}) collective-permute-start(bf16[2304,128]{1,0:T(8,128)(2,1)} %shard_map.76.refs_2_), channel_id=1, source_target_pairs={{0,4},{1,5},{2,6},{3,7},{4,12},{5,13},{6,14},{7,15},{8,0},{9,1},{1... | collective-permute-start | bytes 1769480 | tf_op jit(solution)/shard_map/ppermute | solution.py:385
  60.6 11.7 %collective-permute-start.12 = (bf16[2304,128]{1,0:T(8,128)(2,1)}, bf16[2304,128]{1,0:T(8,128)(2,1)}, u32[]{:S(2)}, u32[]{:S(2)}) collective-permute-start(bf16[2304,128]{1,0:T(8,128)(2,1)} %collective-permute-done.8.refs_3_), channel_id=1, source_target_pairs={{0,2},{1,3},{2,0},{3,1},{4,6},{5,7},{6,4},{7,5},{8,10},{9,11},{10,... | collective-permute-start | bytes 1769480 | tf_op jit(solution)/shard_map/ppermute | solution.py:385
  60.8 11.8 %collective-permute-start.13 = (bf16[2304,128]{1,0:T(8,128)(2,1)}, bf16[2304,128]{1,0:T(8,128)(2,1)}, u32[]{:S(2)}, u32[]{:S(2)}) collective-permute-start(bf16[2304,128]{1,0:T(8,128)(2,1)} %collective-permute-done.5.refs_2_), channel_id=1, source_target_pairs={{0,16},{1,17},{2,18},{3,19},{4,20},{5,21},{6,22},{7,23},{8,24},{9,... | collective-permute-start | bytes 1769480 | tf_op jit(solution)/shard_map/ppermute | solution.py:385
  61.4 6.2 %collective-permute-start.14 = (bf16[128,1024]{1,0:T(8,128)(2,1)}, bf16[128,1024]{1,0:T(8,128)(2,1)S(1)}, u32[]{:S(2)}, u32[]{:S(2)}) collective-permute-start(bf16[128,1024]{1,0:T(8,128)(2,1)} %get-tuple-element.87.refs_0_), channel_id=1, source_target_pairs={{0,1},{1,0},{2,3},{3,2},{4,5},{5,4},{6,7},{7,6},{8,9},{9,8},{10,11... | collective-permute-start | bytes 786440 | tf_op jit(solution)/shard_map/ppermute | solution.py:385
  67.6 17.3 %copy-start.1 = (bf16[128,1024]{1,0:T(8,128)(2,1)}, bf16[128,1024]{1,0:T(8,128)(2,1)S(1)}, u32[]{:S(2)}) copy-start(bf16[128,1024]{1,0:T(8,128)(2,1)S(1)} %collective-permute-done.14.refs_1_) | copy-start | bytes 786436
  72.7 12.8 %collective-permute-start.15 = (bf16[2304,128]{1,0:T(8,128)(2,1)}, bf16[2304,128]{1,0:T(8,128)(2,1)}, u32[]{:S(2)}, u32[]{:S(2)}) collective-permute-start(bf16[2304,128]{1,0:T(8,128)(2,1)} %shard_map.76.refs_2_), channel_id=1, source_target_pairs={{0,8},{1,9},{2,10},{3,11},{4,0},{5,1},{6,2},{7,3},{8,12},{9,13},{1... | collective-permute-start | bytes 1769480 | tf_op jit(solution)/shard_map/ppermute | solution.py:385
  73.7 11.7 %collective-permute-start.16 = (bf16[2304,128]{1,0:T(8,128)(2,1)}, bf16[2304,128]{1,0:T(8,128)(2,1)}, u32[]{:S(2)}, u32[]{:S(2)}) collective-permute-start(bf16[2304,128]{1,0:T(8,128)(2,1)} %collective-permute-done.10.refs_4_), channel_id=1, source_target_pairs={{0,2},{1,3},{2,0},{3,1},{4,6},{5,7},{6,4},{7,5},{8,10},{9,11},{10,... | collective-permute-start | bytes 1769480 | tf_op jit(solution)/shard_map/ppermute | solution.py:385
  74.1 11.4 %collective-permute-start.17 = (bf16[2304,128]{1,0:T(8,128)(2,1)}, bf16[2304,128]{1,0:T(8,128)(2,1)}, u32[]{:S(2)}, u32[]{:S(2)}) collective-permute-start(bf16[2304,128]{1,0:T(8,128)(2,1)} %collective-permute-done.12.refs_5_), channel_id=1, source_target_pairs={{0,16},{1,17},{2,18},{3,19},{4,20},{5,21},{6,22},{7,23},{8,24},{9,... | collective-permute-start | bytes 1769480 | tf_op jit(solution)/shard_map/ppermute | solution.py:385
  74.7 10.8 %collective-permute-start.18 = (bf16[96,1024]{1,0:T(8,128)(2,1)}, bf16[96,1024]{1,0:T(8,128)(2,1)}, u32[]{:S(2)}, u32[]{:S(2)}) collective-permute-start(bf16[96,1024]{1,0:T(8,128)(2,1)} %get-tuple-element.98.refs_2_), channel_id=1, source_target_pairs={{0,1},{1,0},{2,3},{3,2},{4,5},{5,4},{6,7},{7,6},{8,9},{9,8},{10,11... | collective-permute-start | bytes 589832 | tf_op jit(solution)/shard_map/ppermute | solution.py:385
  84.9 7.4 %collective-permute-start.20 = (bf16[192,1024]{1,0:T(8,128)(2,1)}, bf16[192,1024]{1,0:T(8,128)(2,1)S(1)}, u32[]{:S(2)}, u32[]{:S(2)}) collective-permute-start(bf16[192,1024]{1,0:T(8,128)(2,1)} %get-tuple-element.109.refs_4_), channel_id=1, source_target_pairs={{0,1},{1,0},{2,3},{3,2},{4,5},{5,4},{6,7},{7,6},{8,9},{9,8},{10,11... | collective-permute-start | bytes 1179656 | tf_op jit(solution)/shard_map/ppermute | solution.py:385
  91.7 2.2 %collective-permute-start.19 = (f32[512,128]{1,0:T(8,128)}, f32[512,128]{1,0:T(8,128)}, u32[]{:S(2)}, u32[]{:S(2)}) collective-permute-start(f32[512,128]{1,0:T(8,128)} %get-tuple-element.105), channel_id=1, source_target_pairs={{0,1},{1,0},{2,3},{3,2},{4,5},{5,4},{6,7},{7,6},{8,9},{9,8},{10,11... | collective-permute-start | bytes 786440 | tf_op jit(solution)/shard_map/ppermute | solution.py:385
  91.8 2.1 %collective-permute-start.21 = (bf16[96,1024]{1,0:T(8,128)(2,1)}, bf16[96,1024]{1,0:T(8,128)(2,1)}, u32[]{:S(2)}, u32[]{:S(2)}) collective-permute-start(bf16[96,1024]{1,0:T(8,128)(2,1)} %get-tuple-element.110.refs_6_), channel_id=1, source_target_pairs={{0,1},{1,0},{2,3},{3,2},{4,5},{5,4},{6,7},{7,6},{8,9},{9,8},{10,11... | collective-permute-start | bytes 589832 | tf_op jit(solution)/shard_map/ppermute | solution.py:385
  92.3 1.7 %copy-start = (bf16[192,1024]{1,0:T(8,128)(2,1)}, bf16[192,1024]{1,0:T(8,128)(2,1)S(1)}, u32[]{:S(2)}) copy-start(bf16[192,1024]{1,0:T(8,128)(2,1)S(1)} %collective-permute-done.20.refs_5_) | copy-start | bytes 1179652

commit v17 on v16

--- a/solution.py
+++ b/solution.py
@@ -318,11 +318,11 @@
     begin(row_slot_ref.at[pl.ds(0, rows)], row_slot)
     begin(mine_ref, mine)
     begin(theirs_ref, theirs)
-    begin(total_ref, total)
     for source in sources:
         for n in range(0, source.shape[0], height):
-            first = pl.multiple_of(info_ref[len(copies) - 2], height)
+            first = pl.multiple_of(info_ref[len(copies) - 1], height)
             begin(source.at[pl.ds(n, height)], up.at[pl.ds(first, height)])
+    begin(total_ref, total)
     awaited(copies[:3])
     shrink = mine[...] + theirs[...]
     lane_slot = lax.broadcasted_iota(jnp.int32, (1, LANES), 1) // RANK
@@ -332,8 +332,9 @@
         high.append(kept.astype(jnp.bfloat16))
         low.append((kept - high[-1].astype(jnp.float32)).astype(jnp.bfloat16))
     both = jnp.concatenate([jnp.concatenate(part, axis=1) for part in (low, high)], axis=0)
-    awaited(copies[3:])
+    awaited(copies[3:-1])
     lora = jnp.dot(both, up[...], preferred_element_type=jnp.float32)
+    awaited(copies[-1:])
     out_ref[...] = (total[...] + (lora[:rows] + lora[rows:])).astype(out_ref.dtype)
 
 

time: 101 us -> 101 us (level)
  no operation moved by 1% of the time
where the time goes in v17:
time: 101 us; the launch traced here: 100 us
  Pallas kernels  60.2 us (60%)
  starting transfers between devices  20 us (20%)
  waiting for transfers between devices  16.8 us (17%)
  local copies, waits for them, and re-layouts  2.27 us (2%)
    pallas_call x4, Pallas kernels, absorb(): pl.pallas_call(functools.partial(absorb_kernel, sizes, start, sides, more...  29 us
    ppermute x22, starting transfers between devices, permuted(): return lax.ppermute(array, axes, pairs)  20 us
    pallas_call x2, Pallas kernels, base_part(): pl.pallas_call(functools.partial(base_kernel, steps), out_shape=result, g...  19.5 us
    ppermute x22, waiting for transfers between devices, permuted(): return lax.ppermute(array, axes, pairs)  16.8 us
    pallas_call x1, Pallas kernels, finish(): pl.pallas_call(functools.partial(finish_kernel, len(ups)), out_shape=jax....  6.19 us
    pallas_call x2, Pallas kernels, assemble(): pl.pallas_call(functools.partial(assemble_kernel, back), out_shape=jax.Sh...  5.5 us
  transfers between devices with their start and end apart: 22, of which 13 were waited for; matrix products, arithmetic and copies ran while one was open for 3% of the time, Pallas kernels for 54%

profile of v17, /device:TPU:0, one launch (start us, length us, event | category | flops | bytes accessed | tf_op | source)
XLA Modules:
  0.0 100.3 jit_solution(13268457927997297797)
XLA Ops:
  0.0 0.5 collective-permute-start
  0.5 1.2 %dynamic-slice_bitcast_fusion.info_ref = s32[50]{0:T(128)} fusion(s32[32,50]{1,0:T(8,128)} %constant.20.clone, s32[]{:T(128)S(6)} %select_n.8), kind=kLoop, calls=%fused_computation.3 | loop fusion | bytes 404 | tf_op jit(solution)/shard_map/jit(dynamic_index_in_dim)/squeeze | solution.py:413
  1.7 0.8 select_reduce_fusion
  2.5 0.6 collective-permute-done.there_ref
  3.1 0.4 collective-permute-start.7
  3.5 2.8 %shard_map.73.refs_2_ = bf16[2304,128]{1,0:T(8,128)(2,1)} custom-call(s32[50]{0:T(128)} %dynamic-slice_bitcast_fusion.info_ref, bf16[4,16,8192]{2,1,0:T(8,128)(2,1)} %here_ref.3, bf16[4,16,8192]{2,1,0:T(8,128)(2,1)} %collective-permute-done.there_ref, bf16[4,16,1024]{2,1,0:T(8,128)(2,1)} %up_ref.3), custom_call_target="tpu_custom_call" | custom-call | tf_op jit(solution)/shard_map/pallas_call | solution.py:119
  6.2 2.8 %collective-permute-start.1 = (bf16[2304,128]{1,0:T(8,128)(2,1)}, bf16[2304,128]{1,0:T(8,128)(2,1)}, u32[]{:S(2)}, u32[]{:S(2)}) collective-permute-start(bf16[2304,128]{1,0:T(8,128)(2,1)} %shard_map.73.refs_2_), channel_id=1, source_target_pairs={{0,4},{1,5},{2,6},{3,7},{4,12},{5,13},{6,14},{7,15},{8,0},{9,1},{1... | collective-permute-start | bytes 1769480 | tf_op jit(solution)/shard_map/ppermute | solution.py:386
  9.0 1.5 %collective-permute-start.2 = (bf16[2304,128]{1,0:T(8,128)(2,1)}, bf16[2304,128]{1,0:T(8,128)(2,1)}, u32[]{:S(2)}, u32[]{:S(2)}) collective-permute-start(bf16[2304,128]{1,0:T(8,128)(2,1)} %shard_map.73.refs_2_), channel_id=1, source_target_pairs={{0,2},{1,3},{2,0},{3,1},{4,6},{5,7},{6,4},{7,5},{8,10},{9,11},{10,... | collective-permute-start | bytes 1769480 | tf_op jit(solution)/shard_map/ppermute | solution.py:386
  10.5 0.0 collective-permute-start.3
  10.5 9.6 %shard_map.74.refs_0_ = f32[512,1024]{1,0:T(8,128)} custom-call(bf16[512,8192]{1,0:T(8,128)(2,1)} %refs_0_.7, bf16[8192,1024]{1,0:T(8,128)(2,1)} %weight_ref.3), custom_call_target="tpu_custom_call" | custom-call | flops 4294967296 | bytes 14680064 | tf_op jit(solution)/shard_map/pallas_call | solution.py:163
  20.1 0.0 collective-permute-done.3
  20.1 4.1 %collective-permute-done.1.refs_3_ = bf16[2304,128]{1,0:T(8,128)(2,1)} collective-permute-done((bf16[2304,128]{1,0:T(8,128)(2,1)}, bf16[2304,128]{1,0:T(8,128)(2,1)}, u32[]{:S(2)}, u32[]{:S(2)}) %collective-permute-start.1) | collective-permute-done | bytes 589856 | tf_op jit(solution)/shard_map/ppermute | solution.py:386
  24.2 0.4 collective-permute-done.2.refs_4_
  24.6 2.6 %collective-permute-start.4 = (bf16[2304,128]{1,0:T(8,128)(2,1)}, bf16[2304,128]{1,0:T(8,128)(2,1)}, u32[]{:S(2)}, u32[]{:S(2)}) collective-permute-start(bf16[2304,128]{1,0:T(8,128)(2,1)} %collective-permute-done.1.refs_3_), channel_id=1, source_target_pairs={{0,4},{1,5},{2,6},{3,7},{4,12},{5,13},{6,14},{7,15},{8,0},{9,1},{1... | collective-permute-start | bytes 1769480 | tf_op jit(solution)/shard_map/ppermute | solution.py:386
  27.2 1.5 %collective-permute-start.5 = (bf16[2304,128]{1,0:T(8,128)(2,1)}, bf16[2304,128]{1,0:T(8,128)(2,1)}, u32[]{:S(2)}, u32[]{:S(2)}) collective-permute-start(bf16[2304,128]{1,0:T(8,128)(2,1)} %collective-permute-done.1.refs_3_), channel_id=1, source_target_pairs={{0,2},{1,3},{2,0},{3,1},{4,6},{5,7},{6,4},{7,5},{8,10},{9,11},{10,... | collective-permute-start | bytes 1769480 | tf_op jit(solution)/shard_map/ppermute | solution.py:386
  28.7 1.5 %collective-permute-start.6 = (bf16[2304,128]{1,0:T(8,128)(2,1)}, bf16[2304,128]{1,0:T(8,128)(2,1)}, u32[]{:S(2)}, u32[]{:S(2)}) collective-permute-start(bf16[2304,128]{1,0:T(8,128)(2,1)} %collective-permute-done.2.refs_4_), channel_id=1, source_target_pairs={{0,16},{1,17},{2,18},{3,19},{4,20},{5,21},{6,22},{7,23},{8,24},{9,... | collective-permute-start | bytes 1769480 | tf_op jit(solution)/shard_map/ppermute | solution.py:386
  30.2 9.9 %shard_map.75.total_ref = f32[512,1024]{1,0:T(8,128)} custom-call(bf16[512,8192]{1,0:T(8,128)(2,1)} %refs_0_.7, bf16[8192,1024]{1,0:T(8,128)(2,1)} %weight_ref.3, f32[512,1024]{1,0:T(8,128)} %shard_map.74.refs_0_), custom_call_target="tpu_custom_call" | custom-call | flops 4294967296 | bytes 14680064 | tf_op jit(solution)/shard_map/pallas_call | solution.py:163
  40.2 0.3 collective-permute-done.4.refs_5_
  40.4 1.3 %collective-permute-done.5.refs_2_ = bf16[2304,128]{1,0:T(8,128)(2,1)} collective-permute-done((bf16[2304,128]{1,0:T(8,128)(2,1)}, bf16[2304,128]{1,0:T(8,128)(2,1)}, u32[]{:S(2)}, u32[]{:S(2)}) %collective-permute-start.5) | collective-permute-done | bytes 589856 | tf_op jit(solution)/shard_map/ppermute | solution.py:386
  41.7 1.2 %collective-permute-done.6.refs_3_ = bf16[2304,128]{1,0:T(8,128)(2,1)} collective-permute-done((bf16[2304,128]{1,0:T(8,128)(2,1)}, bf16[2304,128]{1,0:T(8,128)(2,1)}, u32[]{:S(2)}, u32[]{:S(2)}) %collective-permute-start.6) | collective-permute-done | bytes 589856 | tf_op jit(solution)/shard_map/ppermute | solution.py:386
  42.9 0.0 collective-permute-done.7.refs_1_
  42.9 1.5 %collective-permute-start.10 = (bf16[2304,128]{1,0:T(8,128)(2,1)}, bf16[2304,128]{1,0:T(8,128)(2,1)}, u32[]{:S(2)}, u32[]{:S(2)}) collective-permute-start(bf16[2304,128]{1,0:T(8,128)(2,1)} %collective-permute-done.4.refs_5_), channel_id=1, source_target_pairs={{0,16},{1,17},{2,18},{3,19},{4,20},{5,21},{6,22},{7,23},{8,24},{9,... | collective-permute-start | bytes 1769480 | tf_op jit(solution)/shard_map/ppermute | solution.py:386
  44.5 0.3 collective-permute-start.8
  44.8 0.5 collective-permute-start.9
  45.3 1.0 %copy.19.row_slot_ref = s32[1024,1]{1,0:T(8,128)} copy(s32[1024,1]{0,1:T(1,128)S(1)} %pad_add_fusion) | data formatting | bytes 8192 | tf_op jit(solution)/shard_map/optimization_barrier | solution.py:418
  46.4 2.7 %shard_map.76.refs_2_ = bf16[2304,128]{1,0:T(8,128)(2,1)} custom-call(s32[50]{0:T(128)} %dynamic-slice_bitcast_fusion.info_ref, bf16[4,16,8192]{2,1,0:T(8,128)(2,1)} %here_ref.3, bf16[4,16,8192]{2,1,0:T(8,128)(2,1)} %collective-permute-done.there_ref, bf16[4,16,1024]{2,1,0:T(8,128)(2,1)} %up_ref.3), custom_call_target="tpu_custom_call" | custom-call | tf_op jit(solution)/shard_map/pallas_call | solution.py:119
  49.1 6.4 %shard_map.77 = (f32[512,128]{1,0:T(8,128)}, f32[512,128]{1,0:T(8,128)}, bf16[128,1024]{1,0:T(8,128)(2,1)}) custom-call(s32[50]{0:T(128)} %dynamic-slice_bitcast_fusion.info_ref, s32[1024,1]{1,0:T(8,128)} %copy.19.row_slot_ref, bf16[512,8192]{1,0:T(8,128)(2,1)} %refs_0_.7, bf16[512,8192]{1,0:T(8,128)(2,1)} %collective-permute-done.7.refs_1_, ...), custom_call_target="tpu_custom_call" | custom-call | flops 2147483648 | bytes 6553600 | tf_op jit(solution)/shard_map/pallas_call | solution.py:284
  55.5 0.7 collective-permute-done.10.refs_4_
  56.3 1.3 %collective-permute-done.8.refs_3_ = bf16[2304,128]{1,0:T(8,128)(2,1)} collective-permute-done((bf16[2304,128]{1,0:T(8,128)(2,1)}, bf16[2304,128]{1,0:T(8,128)(2,1)}, u32[]{:S(2)}, u32[]{:S(2)}) %collective-permute-start.8) | collective-permute-done | bytes 589856 | tf_op jit(solution)/shard_map/ppermute | solution.py:386
  57.6 0.0 collective-permute-done.9.refs_4_
  57.6 3.1 %collective-permute-start.11 = (bf16[2304,128]{1,0:T(8,128)(2,1)}, bf16[2304,128]{1,0:T(8,128)(2,1)}, u32[]{:S(2)}, u32[]{:S(2)}) collective-permute-start(bf16[2304,128]{1,0:T(8,128)(2,1)} %shard_map.76.refs_2_), channel_id=1, source_target_pairs={{0,4},{1,5},{2,6},{3,7},{4,12},{5,13},{6,14},{7,15},{8,0},{9,1},{1... | collective-permute-start | bytes 1769480 | tf_op jit(solution)/shard_map/ppermute | solution.py:386
  60.6 0.2 collective-permute-start.12
  60.8 0.5 collective-permute-start.13
  61.4 0.0 collective-permute-start.14
  61.4 6.2 %shard_map.78 = (f32[512,128]{1,0:T(8,128)}, f32[512,128]{1,0:T(8,128)}, bf16[96,1024]{1,0:T(8,128)(2,1)}) custom-call(s32[50]{0:T(128)} %dynamic-slice_bitcast_fusion.info_ref, s32[1024,1]{1,0:T(8,128)} %copy.19.row_slot_ref, bf16[512,8192]{1,0:T(8,128)(2,1)} %refs_0_.7, bf16[512,8192]{1,0:T(8,128)(2,1)} %collective-permute-done.7.refs_1_, ...), custom_call_target="tpu_custom_call" | custom-call | flops 1610612736 | bytes 5963776 | tf_op jit(solution)/shard_map/pallas_call | solution.py:284
  67.6 0.0 collective-permute-done.14.refs_1_
  67.6 0.0 copy-start.1
  67.6 4.7 %collective-permute-done.11.refs_6_ = bf16[2304,128]{1,0:T(8,128)(2,1)} collective-permute-done((bf16[2304,128]{1,0:T(8,128)(2,1)}, bf16[2304,128]{1,0:T(8,128)(2,1)}, u32[]{:S(2)}, u32[]{:S(2)}) %collective-permute-start.11) | collective-permute-done | bytes 589856 | tf_op jit(solution)/shard_map/ppermute | solution.py:386
  72.3 0.1 collective-permute-done.12.refs_5_
  72.4 0.3 collective-permute-done.13.refs_7_
  72.7 1.1 %collective-permute-start.15 = (bf16[2304,128]{1,0:T(8,128)(2,1)}, bf16[2304,128]{1,0:T(8,128)(2,1)}, u32[]{:S(2)}, u32[]{:S(2)}) collective-permute-start(bf16[2304,128]{1,0:T(8,128)(2,1)} %shard_map.76.refs_2_), channel_id=1, source_target_pairs={{0,8},{1,9},{2,10},{3,11},{4,0},{5,1},{6,2},{7,3},{8,12},{9,13},{1... | collective-permute-start | bytes 1769480 | tf_op jit(solution)/shard_map/ppermute | solution.py:386
  73.7 0.4 collective-permute-start.16
  74.1 0.5 collective-permute-start.17
  74.7 0.0 collective-permute-start.18
  74.7 10.2 %shard_map.79 = (f32[512,128]{1,0:T(8,128)}, f32[512,128]{1,0:T(8,128)}, bf16[192,1024]{1,0:T(8,128)(2,1)}) custom-call(s32[50]{0:T(128)} %dynamic-slice_bitcast_fusion.info_ref, s32[1024,1]{1,0:T(8,128)} %copy.19.row_slot_ref, bf16[512,8192]{1,0:T(8,128)(2,1)} %refs_0_.7, bf16[512,8192]{1,0:T(8,128)(2,1)} %collective-permute-done.7.refs_1_, ...), custom_call_target="tpu_custom_call" | custom-call | flops 3221225472 | bytes 11927552 | tf_op jit(solution)/shard_map/pallas_call | solution.py:284
  84.9 0.0 copy-done.1
  84.9 0.6 collective-permute-start.20
  85.4 0.0 collective-permute-done.18.refs_3_
  85.4 0.0 collective-permute-done.15.refs_2_
  85.5 0.0 collective-permute-done.16.refs_3_
  85.5 0.1 collective-permute-done.17.refs_4_
  85.6 6.2 %shard_map.80 = (f32[512,128]{1,0:T(8,128)}, f32[512,128]{1,0:T(8,128)}, bf16[96,1024]{1,0:T(8,128)(2,1)}) custom-call(s32[50]{0:T(128)} %dynamic-slice_bitcast_fusion.info_ref, s32[1024,1]{1,0:T(8,128)} %copy.19.row_slot_ref, bf16[512,8192]{1,0:T(8,128)(2,1)} %refs_0_.7, bf16[512,8192]{1,0:T(8,128)(2,1)} %collective-permute-done.7.refs_1_, ...), custom_call_target="tpu_custom_call" | custom-call | flops 1610612736 | bytes 5963776 | tf_op jit(solution)/shard_map/pallas_call | solution.py:284
  91.7 0.1 collective-permute-start.19
  91.8 0.5 collective-permute-start.21
  92.3 0.0 collective-permute-done.20.refs_5_
  92.3 0.0 copy-start
  92.3 1.6 %collective-permute-done.21.refs_7_ = bf16[96,1024]{1,0:T(8,128)(2,1)} collective-permute-done((bf16[96,1024]{1,0:T(8,128)(2,1)}, bf16[96,1024]{1,0:T(8,128)(2,1)}, u32[]{:S(2)}, u32[]{:S(2)}) %collective-permute-start.21) | collective-permute-done | bytes 196640 | tf_op jit(solution)/shard_map/ppermute | solution.py:386
  94.0 0.0 collective-permute-done.19.theirs_ref
  94.0 0.0 copy-done
  94.0 6.2 %shard_map.81 = bf16[512,1024]{1,0:T(8,128)(2,1)} custom-call(s32[50]{0:T(128)} %dynamic-slice_bitcast_fusion.info_ref, s32[1024,1]{1,0:T(8,128)} %copy.19.row_slot_ref, f32[512,128]{1,0:T(8,128)} %get-tuple-element.104.mine_ref, f32[512,128]{1,0:T(8,128)} %collective-permute-done.19.theirs_ref, f32[512,1024]{1,0:T(8,128)} %shard_map.75.total_ref, ...), custom_call_target="tpu_custom_call" | custom-call | flops 2147483648 | bytes 5242880 | tf_op jit(solution)/shard_map/pallas_call | solution.py:345
  (1 shorter events, 0.0 us)
Async XLA Ops:
  0.0 3.1 %collective-permute-start = (bf16[4,16,8192]{2,1,0:T(8,128)(2,1)}, bf16[4,16,8192]{2,1,0:T(8,128)(2,1)}, u32[]{:S(2)}, u32[]{:S(2)}) collective-permute-start(bf16[4,16,8192]{2,1,0:T(8,128)(2,1)} %here_ref.3), channel_id=1, source_target_pairs={{0,1},{1,0},{2,3},{3,2},{4,5},{5,4},{6,7},{7,6},{8,9},{9,8},{10,11... | collective-permute-start | bytes 3145736 | tf_op jit(solution)/shard_map/ppermute | solution.py:386
  3.1 39.9 %collective-permute-start.7 = (bf16[512,8192]{1,0:T(8,128)(2,1)}, bf16[512,8192]{1,0:T(8,128)(2,1)}, u32[]{:S(2)}, u32[]{:S(2)}) collective-permute-start(bf16[512,8192]{1,0:T(8,128)(2,1)} %refs_0_.7), channel_id=1, source_target_pairs={{0,1},{1,0},{2,3},{3,2},{4,5},{5,4},{6,7},{7,6},{8,9},{9,8},{10,11... | collective-permute-start | bytes 25165832 | tf_op jit(solution)/shard_map/ppermute | solution.py:386
  6.2 18.0 %collective-permute-start.1 = (bf16[2304,128]{1,0:T(8,128)(2,1)}, bf16[2304,128]{1,0:T(8,128)(2,1)}, u32[]{:S(2)}, u32[]{:S(2)}) collective-permute-start(bf16[2304,128]{1,0:T(8,128)(2,1)} %shard_map.73.refs_2_), channel_id=1, source_target_pairs={{0,4},{1,5},{2,6},{3,7},{4,12},{5,13},{6,14},{7,15},{8,0},{9,1},{1... | collective-permute-start | bytes 1769480 | tf_op jit(solution)/shard_map/ppermute | solution.py:386
  9.0 15.6 %collective-permute-start.2 = (bf16[2304,128]{1,0:T(8,128)(2,1)}, bf16[2304,128]{1,0:T(8,128)(2,1)}, u32[]{:S(2)}, u32[]{:S(2)}) collective-permute-start(bf16[2304,128]{1,0:T(8,128)(2,1)} %shard_map.73.refs_2_), channel_id=1, source_target_pairs={{0,2},{1,3},{2,0},{3,1},{4,6},{5,7},{6,4},{7,5},{8,10},{9,11},{10,... | collective-permute-start | bytes 1769480 | tf_op jit(solution)/shard_map/ppermute | solution.py:386
  10.5 9.6 %collective-permute-start.3 = (s32[512]{0:T(512)S(1)}, s32[512]{0:T(512)S(1)}, u32[]{:S(2)}, u32[]{:S(2)}) collective-permute-start(s32[512]{0:T(512)S(1)} %select_reduce_fusion), channel_id=1, source_target_pairs={{0,1},{1,0},{2,3},{3,2},{4,5},{5,4},{6,7},{7,6},{8,9},{9,8},{10,11... | collective-permute-start | bytes 6152 | tf_op jit(solution)/shard_map/ppermute | solution.py:386
  24.6 15.8 %collective-permute-start.4 = (bf16[2304,128]{1,0:T(8,128)(2,1)}, bf16[2304,128]{1,0:T(8,128)(2,1)}, u32[]{:S(2)}, u32[]{:S(2)}) collective-permute-start(bf16[2304,128]{1,0:T(8,128)(2,1)} %collective-permute-done.1.refs_3_), channel_id=1, source_target_pairs={{0,4},{1,5},{2,6},{3,7},{4,12},{5,13},{6,14},{7,15},{8,0},{9,1},{1... | collective-permute-start | bytes 1769480 | tf_op jit(solution)/shard_map/ppermute | solution.py:386
  27.2 14.5 %collective-permute-start.5 = (bf16[2304,128]{1,0:T(8,128)(2,1)}, bf16[2304,128]{1,0:T(8,128)(2,1)}, u32[]{:S(2)}, u32[]{:S(2)}) collective-permute-start(bf16[2304,128]{1,0:T(8,128)(2,1)} %collective-permute-done.1.refs_3_), channel_id=1, source_target_pairs={{0,2},{1,3},{2,0},{3,1},{4,6},{5,7},{6,4},{7,5},{8,10},{9,11},{10,... | collective-permute-start | bytes 1769480 | tf_op jit(solution)/shard_map/ppermute | solution.py:386
  28.7 14.2 %collective-permute-start.6 = (bf16[2304,128]{1,0:T(8,128)(2,1)}, bf16[2304,128]{1,0:T(8,128)(2,1)}, u32[]{:S(2)}, u32[]{:S(2)}) collective-permute-start(bf16[2304,128]{1,0:T(8,128)(2,1)} %collective-permute-done.2.refs_4_), channel_id=1, source_target_pairs={{0,16},{1,17},{2,18},{3,19},{4,20},{5,21},{6,22},{7,23},{8,24},{9,... | collective-permute-start | bytes 1769480 | tf_op jit(solution)/shard_map/ppermute | solution.py:386
  42.9 13.3 %collective-permute-start.10 = (bf16[2304,128]{1,0:T(8,128)(2,1)}, bf16[2304,128]{1,0:T(8,128)(2,1)}, u32[]{:S(2)}, u32[]{:S(2)}) collective-permute-start(bf16[2304,128]{1,0:T(8,128)(2,1)} %collective-permute-done.4.refs_5_), channel_id=1, source_target_pairs={{0,16},{1,17},{2,18},{3,19},{4,20},{5,21},{6,22},{7,23},{8,24},{9,... | collective-permute-start | bytes 1769480 | tf_op jit(solution)/shard_map/ppermute | solution.py:386
  44.5 13.1 %collective-permute-start.8 = (bf16[2304,128]{1,0:T(8,128)(2,1)}, bf16[2304,128]{1,0:T(8,128)(2,1)}, u32[]{:S(2)}, u32[]{:S(2)}) collective-permute-start(bf16[2304,128]{1,0:T(8,128)(2,1)} %shard_map.73.refs_2_), channel_id=1, source_target_pairs={{0,8},{1,9},{2,10},{3,11},{4,0},{5,1},{6,2},{7,3},{8,12},{9,13},{1... | collective-permute-start | bytes 1769480 | tf_op jit(solution)/shard_map/ppermute | solution.py:386
  44.8 12.8 %collective-permute-start.9 = (bf16[2304,128]{1,0:T(8,128)(2,1)}, bf16[2304,128]{1,0:T(8,128)(2,1)}, u32[]{:S(2)}, u32[]{:S(2)}) collective-permute-start(bf16[2304,128]{1,0:T(8,128)(2,1)} %collective-permute-done.4.refs_5_), channel_id=1, source_target_pairs={{0,2},{1,3},{2,0},{3,1},{4,6},{5,7},{6,4},{7,5},{8,10},{9,11},{10,... | collective-permute-start | bytes 1769480 | tf_op jit(solution)/shard_map/ppermute | solution.py:386
  57.6 14.7 %collective-permute-start.11 = (bf16[2304,128]{1,0:T(8,128)(2,1)}, bf16[2304,128]{1,0:T(8,128)(2,1)}, u32[]{:S(2)}, u32[]{:S(2)}) collective-permute-start(bf16[2304,128]{1,0:T(8,128)(2,1)} %shard_map.76.refs_2_), channel_id=1, source_target_pairs={{0,4},{1,5},{2,6},{3,7},{4,12},{5,13},{6,14},{7,15},{8,0},{9,1},{1... | collective-permute-start | bytes 1769480 | tf_op jit(solution)/shard_map/ppermute | solution.py:386
  60.6 11.7 %collective-permute-start.12 = (bf16[2304,128]{1,0:T(8,128)(2,1)}, bf16[2304,128]{1,0:T(8,128)(2,1)}, u32[]{:S(2)}, u32[]{:S(2)}) collective-permute-start(bf16[2304,128]{1,0:T(8,128)(2,1)} %collective-permute-done.8.refs_3_), channel_id=1, source_target_pairs={{0,2},{1,3},{2,0},{3,1},{4,6},{5,7},{6,4},{7,5},{8,10},{9,11},{10,... | collective-permute-start | bytes 1769480 | tf_op jit(solution)/shard_map/ppermute | solution.py:386
  60.8 11.8 %collective-permute-start.13 = (bf16[2304,128]{1,0:T(8,128)(2,1)}, bf16[2304,128]{1,0:T(8,128)(2,1)}, u32[]{:S(2)}, u32[]{:S(2)}) collective-permute-start(bf16[2304,128]{1,0:T(8,128)(2,1)} %collective-permute-done.5.refs_2_), channel_id=1, source_target_pairs={{0,16},{1,17},{2,18},{3,19},{4,20},{5,21},{6,22},{7,23},{8,24},{9,... | collective-permute-start | bytes 1769480 | tf_op jit(solution)/shard_map/ppermute | solution.py:386
  61.4 6.2 %collective-permute-start.14 = (bf16[128,1024]{1,0:T(8,128)(2,1)}, bf16[128,1024]{1,0:T(8,128)(2,1)S(1)}, u32[]{:S(2)}, u32[]{:S(2)}) collective-permute-start(bf16[128,1024]{1,0:T(8,128)(2,1)} %get-tuple-element.87.refs_0_), channel_id=1, source_target_pairs={{0,1},{1,0},{2,3},{3,2},{4,5},{5,4},{6,7},{7,6},{8,9},{9,8},{10,11... | collective-permute-start | bytes 786440 | tf_op jit(solution)/shard_map/ppermute | solution.py:386
  67.6 17.3 %copy-start.1 = (bf16[128,1024]{1,0:T(8,128)(2,1)}, bf16[128,1024]{1,0:T(8,128)(2,1)S(1)}, u32[]{:S(2)}) copy-start(bf16[128,1024]{1,0:T(8,128)(2,1)S(1)} %collective-permute-done.14.refs_1_) | copy-start | bytes 786436
  72.7 12.8 %collective-permute-start.15 = (bf16[2304,128]{1,0:T(8,128)(2,1)}, bf16[2304,128]{1,0:T(8,128)(2,1)}, u32[]{:S(2)}, u32[]{:S(2)}) collective-permute-start(bf16[2304,128]{1,0:T(8,128)(2,1)} %shard_map.76.refs_2_), channel_id=1, source_target_pairs={{0,8},{1,9},{2,10},{3,11},{4,0},{5,1},{6,2},{7,3},{8,12},{9,13},{1... | collective-permute-start | bytes 1769480 | tf_op jit(solution)/shard_map/ppermute | solution.py:386
  73.7 11.7 %collective-permute-start.16 = (bf16[2304,128]{1,0:T(8,128)(2,1)}, bf16[2304,128]{1,0:T(8,128)(2,1)}, u32[]{:S(2)}, u32[]{:S(2)}) collective-permute-start(bf16[2304,128]{1,0:T(8,128)(2,1)} %collective-permute-done.10.refs_4_), channel_id=1, source_target_pairs={{0,2},{1,3},{2,0},{3,1},{4,6},{5,7},{6,4},{7,5},{8,10},{9,11},{10,... | collective-permute-start | bytes 1769480 | tf_op jit(solution)/shard_map/ppermute | solution.py:386
  74.1 11.4 %collective-permute-start.17 = (bf16[2304,128]{1,0:T(8,128)(2,1)}, bf16[2304,128]{1,0:T(8,128)(2,1)}, u32[]{:S(2)}, u32[]{:S(2)}) collective-permute-start(bf16[2304,128]{1,0:T(8,128)(2,1)} %collective-permute-done.12.refs_5_), channel_id=1, source_target_pairs={{0,16},{1,17},{2,18},{3,19},{4,20},{5,21},{6,22},{7,23},{8,24},{9,... | collective-permute-start | bytes 1769480 | tf_op jit(solution)/shard_map/ppermute | solution.py:386
  74.7 10.8 %collective-permute-start.18 = (bf16[96,1024]{1,0:T(8,128)(2,1)}, bf16[96,1024]{1,0:T(8,128)(2,1)}, u32[]{:S(2)}, u32[]{:S(2)}) collective-permute-start(bf16[96,1024]{1,0:T(8,128)(2,1)} %get-tuple-element.98.refs_2_), channel_id=1, source_target_pairs={{0,1},{1,0},{2,3},{3,2},{4,5},{5,4},{6,7},{7,6},{8,9},{9,8},{10,11... | collective-permute-start | bytes 589832 | tf_op jit(solution)/shard_map/ppermute | solution.py:386
  84.9 7.4 %collective-permute-start.20 = (bf16[192,1024]{1,0:T(8,128)(2,1)}, bf16[192,1024]{1,0:T(8,128)(2,1)S(1)}, u32[]{:S(2)}, u32[]{:S(2)}) collective-permute-start(bf16[192,1024]{1,0:T(8,128)(2,1)} %get-tuple-element.109.refs_4_), channel_id=1, source_target_pairs={{0,1},{1,0},{2,3},{3,2},{4,5},{5,4},{6,7},{7,6},{8,9},{9,8},{10,11... | collective-permute-start | bytes 1179656 | tf_op jit(solution)/shard_map/ppermute | solution.py:386
  91.7 2.2 %collective-permute-start.19 = (f32[512,128]{1,0:T(8,128)}, f32[512,128]{1,0:T(8,128)}, u32[]{:S(2)}, u32[]{:S(2)}) collective-permute-start(f32[512,128]{1,0:T(8,128)} %get-tuple-element.105), channel_id=1, source_target_pairs={{0,1},{1,0},{2,3},{3,2},{4,5},{5,4},{6,7},{7,6},{8,9},{9,8},{10,11... | collective-permute-start | bytes 786440 | tf_op jit(solution)/shard_map/ppermute | solution.py:386
  91.8 2.1 %collective-permute-start.21 = (bf16[96,1024]{1,0:T(8,128)(2,1)}, bf16[96,1024]{1,0:T(8,128)(2,1)}, u32[]{:S(2)}, u32[]{:S(2)}) collective-permute-start(bf16[96,1024]{1,0:T(8,128)(2,1)} %get-tuple-element.110.refs_6_), channel_id=1, source_target_pairs={{0,1},{1,0},{2,3},{3,2},{4,5},{5,4},{6,7},{7,6},{8,9},{9,8},{10,11... | collective-permute-start | bytes 589832 | tf_op jit(solution)/shard_map/ppermute | solution.py:386
  92.3 1.7 %copy-start = (bf16[192,1024]{1,0:T(8,128)(2,1)}, bf16[192,1024]{1,0:T(8,128)(2,1)S(1)}, u32[]{:S(2)}) copy-start(bf16[192,1024]{1,0:T(8,128)(2,1)S(1)} %collective-permute-done.20.refs_5_) | copy-start | bytes 1179652

commit v18 on v17

--- a/solution.py
+++ b/solution.py
@@ -437,15 +437,17 @@
         return base_part(after(tokens, *others), base_value_weight, low, high, before)
 
     z1, x0 = z_ring(front), x_swap(front)
-    other = core_swap(tokens_late)
     other_slot = core_swap(row_slot[:, 0])
     total = base(0, None, front)
     row_slots = jnp.concatenate([row_slot, other_slot[:, None]], axis=0)
-    z1, x0, front, total, row_slots = together(z1, x0, front, total, row_slots)
+    z1, x0, front, total, row_slots, tokens_late = together(
+        z1, x0, front, total, row_slots, tokens_late
+    )
 
     z2, x1, yx0 = z_ring(z1), x_swap(z1), y_swap(x0)
+    other = core_swap(tokens_late)
     total = base(1, total, total)
-    z2, x1, yx0, front, other, total, info = together(z2, x1, yx0, front, other, total, info)
+    z2, x1, yx0, front, total, info = together(z2, x1, yx0, front, total, info)
 
     def update(number, groups, before):
         return absorb(

time: 101 us -> 104 us (1.030)
  waiting for transfers between devices: 16.8 us -> 20.2 us
    ppermute x22, waiting for transfers between devices: 16.8 us -> 20.2 us  [permuted(): return lax.ppermute(array, axes, pairs)]
  transfers between devices with their start and end apart: 22 -> 22, of which waited for: 13 -> 13; matrix products, arithmetic and copies ran while one was open for 3% -> 3% of each run, Pallas kernels for 54% -> 49%
where the time goes in v18:
time: 104 us
  Pallas kernels  60.2 us (58%)
  waiting for transfers between devices  20.2 us (19%)
  starting transfers between devices  20 us (19%)
  local copies, waits for them, and re-layouts  2.27 us (2%)
    pallas_call x4, Pallas kernels, absorb(): pl.pallas_call(functools.partial(absorb_kernel, sizes, start, sides, more...  29 us
    ppermute x22, waiting for transfers between devices, permuted(): return lax.ppermute(array, axes, pairs)  20.2 us
    ppermute x22, starting transfers between devices, permuted(): return lax.ppermute(array, axes, pairs)  20 us
    pallas_call x2, Pallas kernels, base_part(): pl.pallas_call(functools.partial(base_kernel, steps), out_shape=result, g...  19.5 us
    pallas_call x1, Pallas kernels, finish(): pl.pallas_call(functools.partial(finish_kernel, len(ups)), out_shape=jax....  6.19 us
    pallas_call x2, Pallas kernels, assemble(): pl.pallas_call(functools.partial(assemble_kernel, back), out_shape=jax.Sh...  5.5 us
  transfers between devices with their start and end apart: 22, of which 13 were waited for; matrix products, arithmetic and copies ran while one was open for 3% of the time, Pallas kernels for 49%

profile of v18, /device:TPU:0, one launch (start us, length us, event | category | flops | bytes accessed | tf_op | source)
XLA Modules:
  0.0 103.7 jit_solution(7175126712562836581)
XLA Ops:
  0.0 0.5 collective-permute-start
  0.5 1.2 %dynamic-slice_bitcast_fusion.info_ref = s32[50]{0:T(128)} fusion(s32[32,50]{1,0:T(8,128)} %constant.20.clone, s32[]{:T(128)S(6)} %select_n.8), kind=kLoop, calls=%fused_computation.3 | loop fusion | bytes 404 | tf_op jit(solution)/shard_map/jit(dynamic_index_in_dim)/squeeze | solution.py:413
  1.7 0.8 select_reduce_fusion
  2.5 0.6 collective-permute-done.there_ref
  3.1 2.8 %shard_map.73.refs_2_ = bf16[2304,128]{1,0:T(8,128)(2,1)} custom-call(s32[50]{0:T(128)} %dynamic-slice_bitcast_fusion.info_ref, bf16[4,16,8192]{2,1,0:T(8,128)(2,1)} %here_ref.3, bf16[4,16,8192]{2,1,0:T(8,128)(2,1)} %collective-permute-done.there_ref, bf16[4,16,1024]{2,1,0:T(8,128)(2,1)} %up_ref.3), custom_call_target="tpu_custom_call" | custom-call | tf_op jit(solution)/shard_map/pallas_call | solution.py:119
  5.9 3.0 %collective-permute-start.1 = (bf16[2304,128]{1,0:T(8,128)(2,1)}, bf16[2304,128]{1,0:T(8,128)(2,1)}, u32[]{:S(2)}, u32[]{:S(2)}) collective-permute-start(bf16[2304,128]{1,0:T(8,128)(2,1)} %shard_map.73.refs_2_), channel_id=1, source_target_pairs={{0,4},{1,5},{2,6},{3,7},{4,12},{5,13},{6,14},{7,15},{8,0},{9,1},{1... | collective-permute-start | bytes 1769480 | tf_op jit(solution)/shard_map/ppermute | solution.py:386
  8.9 1.5 %collective-permute-start.2 = (bf16[2304,128]{1,0:T(8,128)(2,1)}, bf16[2304,128]{1,0:T(8,128)(2,1)}, u32[]{:S(2)}, u32[]{:S(2)}) collective-permute-start(bf16[2304,128]{1,0:T(8,128)(2,1)} %shard_map.73.refs_2_), channel_id=1, source_target_pairs={{0,2},{1,3},{2,0},{3,1},{4,6},{5,7},{6,4},{7,5},{8,10},{9,11},{10,... | collective-permute-start | bytes 1769480 | tf_op jit(solution)/shard_map/ppermute | solution.py:386
  10.3 0.0 collective-permute-start.3
  10.4 9.6 %shard_map.74.refs_0_ = f32[512,1024]{1,0:T(8,128)} custom-call(bf16[512,8192]{1,0:T(8,128)(2,1)} %refs_0_.7, bf16[8192,1024]{1,0:T(8,128)(2,1)} %weight_ref.3), custom_call_target="tpu_custom_call" | custom-call | flops 4294967296 | bytes 14680064 | tf_op jit(solution)/shard_map/pallas_call | solution.py:163
  20.0 0.0 collective-permute-done.3
  20.0 3.9 %collective-permute-done.1.refs_3_ = bf16[2304,128]{1,0:T(8,128)(2,1)} collective-permute-done((bf16[2304,128]{1,0:T(8,128)(2,1)}, bf16[2304,128]{1,0:T(8,128)(2,1)}, u32[]{:S(2)}, u32[]{:S(2)}) %collective-permute-start.1) | collective-permute-done | bytes 589856 | tf_op jit(solution)/shard_map/ppermute | solution.py:386
  23.8 0.4 collective-permute-done.2.refs_4_
  24.3 0.0 collective-permute-start.7
  24.3 2.6 %collective-permute-start.4 = (bf16[2304,128]{1,0:T(8,128)(2,1)}, bf16[2304,128]{1,0:T(8,128)(2,1)}, u32[]{:S(2)}, u32[]{:S(2)}) collective-permute-start(bf16[2304,128]{1,0:T(8,128)(2,1)} %collective-permute-done.1.refs_3_), channel_id=1, source_target_pairs={{0,4},{1,5},{2,6},{3,7},{4,12},{5,13},{6,14},{7,15},{8,0},{9,1},{1... | collective-permute-start | bytes 1769480 | tf_op jit(solution)/shard_map/ppermute | solution.py:386
  26.9 1.5 %collective-permute-start.5 = (bf16[2304,128]{1,0:T(8,128)(2,1)}, bf16[2304,128]{1,0:T(8,128)(2,1)}, u32[]{:S(2)}, u32[]{:S(2)}) collective-permute-start(bf16[2304,128]{1,0:T(8,128)(2,1)} %collective-permute-done.1.refs_3_), channel_id=1, source_target_pairs={{0,2},{1,3},{2,0},{3,1},{4,6},{5,7},{6,4},{7,5},{8,10},{9,11},{10,... | collective-permute-start | bytes 1769480 | tf_op jit(solution)/shard_map/ppermute | solution.py:386
  28.3 1.5 %collective-permute-start.6 = (bf16[2304,128]{1,0:T(8,128)(2,1)}, bf16[2304,128]{1,0:T(8,128)(2,1)}, u32[]{:S(2)}, u32[]{:S(2)}) collective-permute-start(bf16[2304,128]{1,0:T(8,128)(2,1)} %collective-permute-done.2.refs_4_), channel_id=1, source_target_pairs={{0,16},{1,17},{2,18},{3,19},{4,20},{5,21},{6,22},{7,23},{8,24},{9,... | collective-permute-start | bytes 1769480 | tf_op jit(solution)/shard_map/ppermute | solution.py:386
  29.9 9.9 %shard_map.75.total_ref = f32[512,1024]{1,0:T(8,128)} custom-call(bf16[512,8192]{1,0:T(8,128)(2,1)} %refs_0_.7, bf16[8192,1024]{1,0:T(8,128)(2,1)} %weight_ref.3, f32[512,1024]{1,0:T(8,128)} %shard_map.74.refs_0_), custom_call_target="tpu_custom_call" | custom-call | flops 4294967296 | bytes 14680064 | tf_op jit(solution)/shard_map/pallas_call | solution.py:163
  39.8 1.4 %collective-permute-done.4.refs_5_ = bf16[2304,128]{1,0:T(8,128)(2,1)} collective-permute-done((bf16[2304,128]{1,0:T(8,128)(2,1)}, bf16[2304,128]{1,0:T(8,128)(2,1)}, u32[]{:S(2)}, u32[]{:S(2)}) %collective-permute-start.4) | collective-permute-done | bytes 589856 | tf_op jit(solution)/shard_map/ppermute | solution.py:386
  41.2 1.4 %collective-permute-done.5.refs_2_ = bf16[2304,128]{1,0:T(8,128)(2,1)} collective-permute-done((bf16[2304,128]{1,0:T(8,128)(2,1)}, bf16[2304,128]{1,0:T(8,128)(2,1)}, u32[]{:S(2)}, u32[]{:S(2)}) %collective-permute-start.5) | collective-permute-done | bytes 589856 | tf_op jit(solution)/shard_map/ppermute | solution.py:386
  42.6 1.2 %collective-permute-done.6.refs_3_ = bf16[2304,128]{1,0:T(8,128)(2,1)} collective-permute-done((bf16[2304,128]{1,0:T(8,128)(2,1)}, bf16[2304,128]{1,0:T(8,128)(2,1)}, u32[]{:S(2)}, u32[]{:S(2)}) %collective-permute-start.6) | collective-permute-done | bytes 589856 | tf_op jit(solution)/shard_map/ppermute | solution.py:386
  43.8 1.5 %collective-permute-start.10 = (bf16[2304,128]{1,0:T(8,128)(2,1)}, bf16[2304,128]{1,0:T(8,128)(2,1)}, u32[]{:S(2)}, u32[]{:S(2)}) collective-permute-start(bf16[2304,128]{1,0:T(8,128)(2,1)} %collective-permute-done.4.refs_5_), channel_id=1, source_target_pairs={{0,16},{1,17},{2,18},{3,19},{4,20},{5,21},{6,22},{7,23},{8,24},{9,... | collective-permute-start | bytes 1769480 | tf_op jit(solution)/shard_map/ppermute | solution.py:386
  45.4 0.3 collective-permute-start.8
  45.7 0.5 collective-permute-start.9
  46.2 1.0 %copy.19.row_slot_ref = s32[1024,1]{1,0:T(8,128)} copy(s32[1024,1]{0,1:T(1,128)S(1)} %pad_add_fusion) | data formatting | bytes 8192 | tf_op jit(solution)/shard_map/optimization_barrier | solution.py:418
  47.3 2.7 %shard_map.76.refs_2_ = bf16[2304,128]{1,0:T(8,128)(2,1)} custom-call(s32[50]{0:T(128)} %dynamic-slice_bitcast_fusion.info_ref, bf16[4,16,8192]{2,1,0:T(8,128)(2,1)} %here_ref.3, bf16[4,16,8192]{2,1,0:T(8,128)(2,1)} %collective-permute-done.there_ref, bf16[4,16,1024]{2,1,0:T(8,128)(2,1)} %up_ref.3), custom_call_target="tpu_custom_call" | custom-call | tf_op jit(solution)/shard_map/pallas_call | solution.py:119
  50.0 0.0 collective-permute-done.7.refs_1_
  50.0 6.4 %shard_map.77 = (f32[512,128]{1,0:T(8,128)}, f32[512,128]{1,0:T(8,128)}, bf16[128,1024]{1,0:T(8,128)(2,1)}) custom-call(s32[50]{0:T(128)} %dynamic-slice_bitcast_fusion.info_ref, s32[1024,1]{1,0:T(8,128)} %copy.19.row_slot_ref, bf16[512,8192]{1,0:T(8,128)(2,1)} %refs_0_.7, bf16[512,8192]{1,0:T(8,128)(2,1)} %collective-permute-done.7.refs_1_, ...), custom_call_target="tpu_custom_call" | custom-call | flops 2147483648 | bytes 6553600 | tf_op jit(solution)/shard_map/pallas_call | solution.py:284
  56.4 2.1 %collective-permute-done.10.refs_4_ = bf16[2304,128]{1,0:T(8,128)(2,1)} collective-permute-done((bf16[2304,128]{1,0:T(8,128)(2,1)}, bf16[2304,128]{1,0:T(8,128)(2,1)}, u32[]{:S(2)}, u32[]{:S(2)}) %collective-permute-start.10) | collective-permute-done | bytes 589856 | tf_op jit(solution)/shard_map/ppermute | solution.py:386
  58.5 1.2 %collective-permute-done.8.refs_3_ = bf16[2304,128]{1,0:T(8,128)(2,1)} collective-permute-done((bf16[2304,128]{1,0:T(8,128)(2,1)}, bf16[2304,128]{1,0:T(8,128)(2,1)}, u32[]{:S(2)}, u32[]{:S(2)}) %collective-permute-start.8) | collective-permute-done | bytes 589856 | tf_op jit(solution)/shard_map/ppermute | solution.py:386
  59.7 0.1 collective-permute-done.9.refs_4_
  59.8 2.0 %collective-permute-start.11 = (bf16[2304,128]{1,0:T(8,128)(2,1)}, bf16[2304,128]{1,0:T(8,128)(2,1)}, u32[]{:S(2)}, u32[]{:S(2)}) collective-permute-start(bf16[2304,128]{1,0:T(8,128)(2,1)} %shard_map.76.refs_2_), channel_id=1, source_target_pairs={{0,4},{1,5},{2,6},{3,7},{4,12},{5,13},{6,14},{7,15},{8,0},{9,1},{1... | collective-permute-start | bytes 1769480 | tf_op jit(solution)/shard_map/ppermute | solution.py:386
  61.8 0.6 collective-permute-start.12
  62.4 0.5 collective-permute-start.13
  62.9 0.0 collective-permute-start.14
  62.9 6.2 %shard_map.78 = (f32[512,128]{1,0:T(8,128)}, f32[512,128]{1,0:T(8,128)}, bf16[96,1024]{1,0:T(8,128)(2,1)}) custom-call(s32[50]{0:T(128)} %dynamic-slice_bitcast_fusion.info_ref, s32[1024,1]{1,0:T(8,128)} %copy.19.row_slot_ref, bf16[512,8192]{1,0:T(8,128)(2,1)} %refs_0_.7, bf16[512,8192]{1,0:T(8,128)(2,1)} %collective-permute-done.7.refs_1_, ...), custom_call_target="tpu_custom_call" | custom-call | flops 1610612736 | bytes 5963776 | tf_op jit(solution)/shard_map/pallas_call | solution.py:284
  69.2 0.0 collective-permute-done.14.refs_1_
  69.2 0.0 copy-start.1
  69.2 4.9 %collective-permute-done.11.refs_6_ = bf16[2304,128]{1,0:T(8,128)(2,1)} collective-permute-done((bf16[2304,128]{1,0:T(8,128)(2,1)}, bf16[2304,128]{1,0:T(8,128)(2,1)}, u32[]{:S(2)}, u32[]{:S(2)}) %collective-permute-start.11) | collective-permute-done | bytes 589856 | tf_op jit(solution)/shard_map/ppermute | solution.py:386
  74.1 0.9 collective-permute-done.12.refs_5_
  75.0 0.4 collective-permute-done.13.refs_7_
  75.4 0.9 collective-permute-start.15
  76.2 1.3 %collective-permute-start.16 = (bf16[2304,128]{1,0:T(8,128)(2,1)}, bf16[2304,128]{1,0:T(8,128)(2,1)}, u32[]{:S(2)}, u32[]{:S(2)}) collective-permute-start(bf16[2304,128]{1,0:T(8,128)(2,1)} %collective-permute-done.10.refs_4_), channel_id=1, source_target_pairs={{0,2},{1,3},{2,0},{3,1},{4,6},{5,7},{6,4},{7,5},{8,10},{9,11},{10,... | collective-permute-start | bytes 1769480 | tf_op jit(solution)/shard_map/ppermute | solution.py:386
  77.6 0.6 collective-permute-start.17
  78.1 0.0 collective-permute-start.18
  78.1 10.2 %shard_map.79 = (f32[512,128]{1,0:T(8,128)}, f32[512,128]{1,0:T(8,128)}, bf16[192,1024]{1,0:T(8,128)(2,1)}) custom-call(s32[50]{0:T(128)} %dynamic-slice_bitcast_fusion.info_ref, s32[1024,1]{1,0:T(8,128)} %copy.19.row_slot_ref, bf16[512,8192]{1,0:T(8,128)(2,1)} %refs_0_.7, bf16[512,8192]{1,0:T(8,128)(2,1)} %collective-permute-done.7.refs_1_, ...), custom_call_target="tpu_custom_call" | custom-call | flops 3221225472 | bytes 11927552 | tf_op jit(solution)/shard_map/pallas_call | solution.py:284
  88.3 0.0 copy-done.1
  88.3 0.6 collective-permute-start.20
  88.9 0.0 collective-permute-done.18.refs_3_
  88.9 0.0 collective-permute-done.15.refs_2_
  88.9 0.0 collective-permute-done.16.refs_3_
  88.9 0.0 collective-permute-done.17.refs_4_
  88.9 6.2 %shard_map.80 = (f32[512,128]{1,0:T(8,128)}, f32[512,128]{1,0:T(8,128)}, bf16[96,1024]{1,0:T(8,128)(2,1)}) custom-call(s32[50]{0:T(128)} %dynamic-slice_bitcast_fusion.info_ref, s32[1024,1]{1,0:T(8,128)} %copy.19.row_slot_ref, bf16[512,8192]{1,0:T(8,128)(2,1)} %refs_0_.7, bf16[512,8192]{1,0:T(8,128)(2,1)} %collective-permute-done.7.refs_1_, ...), custom_call_target="tpu_custom_call" | custom-call | flops 1610612736 | bytes 5963776 | tf_op jit(solution)/shard_map/pallas_call | solution.py:284
  95.1 0.1 collective-permute-start.19
  95.2 0.5 collective-permute-start.21
  95.7 0.0 collective-permute-done.20.refs_5_
  95.7 0.0 copy-start
  95.7 1.6 %collective-permute-done.21.refs_7_ = bf16[96,1024]{1,0:T(8,128)(2,1)} collective-permute-done((bf16[96,1024]{1,0:T(8,128)(2,1)}, bf16[96,1024]{1,0:T(8,128)(2,1)}, u32[]{:S(2)}, u32[]{:S(2)}) %collective-permute-start.21) | collective-permute-done | bytes 196640 | tf_op jit(solution)/shard_map/ppermute | solution.py:386
  97.3 0.0 collective-permute-done.19.theirs_ref
  97.4 0.0 copy-done
  97.4 6.2 %shard_map.81 = bf16[512,1024]{1,0:T(8,128)(2,1)} custom-call(s32[50]{0:T(128)} %dynamic-slice_bitcast_fusion.info_ref, s32[1024,1]{1,0:T(8,128)} %copy.19.row_slot_ref, f32[512,128]{1,0:T(8,128)} %get-tuple-element.104.mine_ref, f32[512,128]{1,0:T(8,128)} %collective-permute-done.19.theirs_ref, f32[512,1024]{1,0:T(8,128)} %shard_map.75.total_ref, ...), custom_call_target="tpu_custom_call" | custom-call | flops 2147483648 | bytes 5242880 | tf_op jit(solution)/shard_map/pallas_call | solution.py:345
  (1 shorter events, 0.0 us)
Async XLA Ops:
  0.0 3.1 %collective-permute-start = (bf16[4,16,8192]{2,1,0:T(8,128)(2,1)}, bf16[4,16,8192]{2,1,0:T(8,128)(2,1)}, u32[]{:S(2)}, u32[]{:S(2)}) collective-permute-start(bf16[4,16,8192]{2,1,0:T(8,128)(2,1)} %here_ref.3), channel_id=1, source_target_pairs={{0,1},{1,0},{2,3},{3,2},{4,5},{5,4},{6,7},{7,6},{8,9},{9,8},{10,11... | collective-permute-start | bytes 3145736 | tf_op jit(solution)/shard_map/ppermute | solution.py:386
  5.9 18.0 %collective-permute-start.1 = (bf16[2304,128]{1,0:T(8,128)(2,1)}, bf16[2304,128]{1,0:T(8,128)(2,1)}, u32[]{:S(2)}, u32[]{:S(2)}) collective-permute-start(bf16[2304,128]{1,0:T(8,128)(2,1)} %shard_map.73.refs_2_), channel_id=1, source_target_pairs={{0,4},{1,5},{2,6},{3,7},{4,12},{5,13},{6,14},{7,15},{8,0},{9,1},{1... | collective-permute-start | bytes 1769480 | tf_op jit(solution)/shard_map/ppermute | solution.py:386
  8.9 15.4 %collective-permute-start.2 = (bf16[2304,128]{1,0:T(8,128)(2,1)}, bf16[2304,128]{1,0:T(8,128)(2,1)}, u32[]{:S(2)}, u32[]{:S(2)}) collective-permute-start(bf16[2304,128]{1,0:T(8,128)(2,1)} %shard_map.73.refs_2_), channel_id=1, source_target_pairs={{0,2},{1,3},{2,0},{3,1},{4,6},{5,7},{6,4},{7,5},{8,10},{9,11},{10,... | collective-permute-start | bytes 1769480 | tf_op jit(solution)/shard_map/ppermute | solution.py:386
  10.3 9.6 %collective-permute-start.3 = (s32[512]{0:T(512)S(1)}, s32[512]{0:T(512)S(1)}, u32[]{:S(2)}, u32[]{:S(2)}) collective-permute-start(s32[512]{0:T(512)S(1)} %select_reduce_fusion), channel_id=1, source_target_pairs={{0,1},{1,0},{2,3},{3,2},{4,5},{5,4},{6,7},{7,6},{8,9},{9,8},{10,11... | collective-permute-start | bytes 6152 | tf_op jit(solution)/shard_map/ppermute | solution.py:386
  24.3 25.8 %collective-permute-start.7 = (bf16[512,8192]{1,0:T(8,128)(2,1)}, bf16[512,8192]{1,0:T(8,128)(2,1)}, u32[]{:S(2)}, u32[]{:S(2)}) collective-permute-start(bf16[512,8192]{1,0:T(8,128)(2,1)} %refs_0_.7), channel_id=1, source_target_pairs={{0,1},{1,0},{2,3},{3,2},{4,5},{5,4},{6,7},{7,6},{8,9},{9,8},{10,11... | collective-permute-start | bytes 25165832 | tf_op jit(solution)/shard_map/ppermute | solution.py:386
  24.3 17.0 %collective-permute-start.4 = (bf16[2304,128]{1,0:T(8,128)(2,1)}, bf16[2304,128]{1,0:T(8,128)(2,1)}, u32[]{:S(2)}, u32[]{:S(2)}) collective-permute-start(bf16[2304,128]{1,0:T(8,128)(2,1)} %collective-permute-done.1.refs_3_), channel_id=1, source_target_pairs={{0,4},{1,5},{2,6},{3,7},{4,12},{5,13},{6,14},{7,15},{8,0},{9,1},{1... | collective-permute-start | bytes 1769480 | tf_op jit(solution)/shard_map/ppermute | solution.py:386
  26.9 15.8 %collective-permute-start.5 = (bf16[2304,128]{1,0:T(8,128)(2,1)}, bf16[2304,128]{1,0:T(8,128)(2,1)}, u32[]{:S(2)}, u32[]{:S(2)}) collective-permute-start(bf16[2304,128]{1,0:T(8,128)(2,1)} %collective-permute-done.1.refs_3_), channel_id=1, source_target_pairs={{0,2},{1,3},{2,0},{3,1},{4,6},{5,7},{6,4},{7,5},{8,10},{9,11},{10,... | collective-permute-start | bytes 1769480 | tf_op jit(solution)/shard_map/ppermute | solution.py:386
  28.3 15.5 %collective-permute-start.6 = (bf16[2304,128]{1,0:T(8,128)(2,1)}, bf16[2304,128]{1,0:T(8,128)(2,1)}, u32[]{:S(2)}, u32[]{:S(2)}) collective-permute-start(bf16[2304,128]{1,0:T(8,128)(2,1)} %collective-permute-done.2.refs_4_), channel_id=1, source_target_pairs={{0,16},{1,17},{2,18},{3,19},{4,20},{5,21},{6,22},{7,23},{8,24},{9,... | collective-permute-start | bytes 1769480 | tf_op jit(solution)/shard_map/ppermute | solution.py:386
  43.8 14.6 %collective-permute-start.10 = (bf16[2304,128]{1,0:T(8,128)(2,1)}, bf16[2304,128]{1,0:T(8,128)(2,1)}, u32[]{:S(2)}, u32[]{:S(2)}) collective-permute-start(bf16[2304,128]{1,0:T(8,128)(2,1)} %collective-permute-done.4.refs_5_), channel_id=1, source_target_pairs={{0,16},{1,17},{2,18},{3,19},{4,20},{5,21},{6,22},{7,23},{8,24},{9,... | collective-permute-start | bytes 1769480 | tf_op jit(solution)/shard_map/ppermute | solution.py:386
  45.4 14.4 %collective-permute-start.8 = (bf16[2304,128]{1,0:T(8,128)(2,1)}, bf16[2304,128]{1,0:T(8,128)(2,1)}, u32[]{:S(2)}, u32[]{:S(2)}) collective-permute-start(bf16[2304,128]{1,0:T(8,128)(2,1)} %shard_map.73.refs_2_), channel_id=1, source_target_pairs={{0,8},{1,9},{2,10},{3,11},{4,0},{5,1},{6,2},{7,3},{8,12},{9,13},{1... | collective-permute-start | bytes 1769480 | tf_op jit(solution)/shard_map/ppermute | solution.py:386
  45.7 14.1 %collective-permute-start.9 = (bf16[2304,128]{1,0:T(8,128)(2,1)}, bf16[2304,128]{1,0:T(8,128)(2,1)}, u32[]{:S(2)}, u32[]{:S(2)}) collective-permute-start(bf16[2304,128]{1,0:T(8,128)(2,1)} %collective-permute-done.4.refs_5_), channel_id=1, source_target_pairs={{0,2},{1,3},{2,0},{3,1},{4,6},{5,7},{6,4},{7,5},{8,10},{9,11},{10,... | collective-permute-start | bytes 1769480 | tf_op jit(solution)/shard_map/ppermute | solution.py:386
  59.8 14.3 %collective-permute-start.11 = (bf16[2304,128]{1,0:T(8,128)(2,1)}, bf16[2304,128]{1,0:T(8,128)(2,1)}, u32[]{:S(2)}, u32[]{:S(2)}) collective-permute-start(bf16[2304,128]{1,0:T(8,128)(2,1)} %shard_map.76.refs_2_), channel_id=1, source_target_pairs={{0,4},{1,5},{2,6},{3,7},{4,12},{5,13},{6,14},{7,15},{8,0},{9,1},{1... | collective-permute-start | bytes 1769480 | tf_op jit(solution)/shard_map/ppermute | solution.py:386
  61.8 13.2 %collective-permute-start.12 = (bf16[2304,128]{1,0:T(8,128)(2,1)}, bf16[2304,128]{1,0:T(8,128)(2,1)}, u32[]{:S(2)}, u32[]{:S(2)}) collective-permute-start(bf16[2304,128]{1,0:T(8,128)(2,1)} %collective-permute-done.8.refs_3_), channel_id=1, source_target_pairs={{0,2},{1,3},{2,0},{3,1},{4,6},{5,7},{6,4},{7,5},{8,10},{9,11},{10,... | collective-permute-start | bytes 1769480 | tf_op jit(solution)/shard_map/ppermute | solution.py:386
  62.4 12.9 %collective-permute-start.13 = (bf16[2304,128]{1,0:T(8,128)(2,1)}, bf16[2304,128]{1,0:T(8,128)(2,1)}, u32[]{:S(2)}, u32[]{:S(2)}) collective-permute-start(bf16[2304,128]{1,0:T(8,128)(2,1)} %collective-permute-done.5.refs_2_), channel_id=1, source_target_pairs={{0,16},{1,17},{2,18},{3,19},{4,20},{5,21},{6,22},{7,23},{8,24},{9,... | collective-permute-start | bytes 1769480 | tf_op jit(solution)/shard_map/ppermute | solution.py:386
  62.9 6.2 %collective-permute-start.14 = (bf16[128,1024]{1,0:T(8,128)(2,1)}, bf16[128,1024]{1,0:T(8,128)(2,1)S(1)}, u32[]{:S(2)}, u32[]{:S(2)}) collective-permute-start(bf16[128,1024]{1,0:T(8,128)(2,1)} %get-tuple-element.87.refs_0_), channel_id=1, source_target_pairs={{0,1},{1,0},{2,3},{3,2},{4,5},{5,4},{6,7},{7,6},{8,9},{9,8},{10,11... | collective-permute-start | bytes 786440 | tf_op jit(solution)/shard_map/ppermute | solution.py:386
  69.2 19.2 %copy-start.1 = (bf16[128,1024]{1,0:T(8,128)(2,1)}, bf16[128,1024]{1,0:T(8,128)(2,1)S(1)}, u32[]{:S(2)}) copy-start(bf16[128,1024]{1,0:T(8,128)(2,1)S(1)} %collective-permute-done.14.refs_1_) | copy-start | bytes 786436
  75.4 13.6 %collective-permute-start.15 = (bf16[2304,128]{1,0:T(8,128)(2,1)}, bf16[2304,128]{1,0:T(8,128)(2,1)}, u32[]{:S(2)}, u32[]{:S(2)}) collective-permute-start(bf16[2304,128]{1,0:T(8,128)(2,1)} %shard_map.76.refs_2_), channel_id=1, source_target_pairs={{0,8},{1,9},{2,10},{3,11},{4,0},{5,1},{6,2},{7,3},{8,12},{9,13},{1... | collective-permute-start | bytes 1769480 | tf_op jit(solution)/shard_map/ppermute | solution.py:386
  76.2 12.7 %collective-permute-start.16 = (bf16[2304,128]{1,0:T(8,128)(2,1)}, bf16[2304,128]{1,0:T(8,128)(2,1)}, u32[]{:S(2)}, u32[]{:S(2)}) collective-permute-start(bf16[2304,128]{1,0:T(8,128)(2,1)} %collective-permute-done.10.refs_4_), channel_id=1, source_target_pairs={{0,2},{1,3},{2,0},{3,1},{4,6},{5,7},{6,4},{7,5},{8,10},{9,11},{10,... | collective-permute-start | bytes 1769480 | tf_op jit(solution)/shard_map/ppermute | solution.py:386
  77.6 11.4 %collective-permute-start.17 = (bf16[2304,128]{1,0:T(8,128)(2,1)}, bf16[2304,128]{1,0:T(8,128)(2,1)}, u32[]{:S(2)}, u32[]{:S(2)}) collective-permute-start(bf16[2304,128]{1,0:T(8,128)(2,1)} %collective-permute-done.12.refs_5_), channel_id=1, source_target_pairs={{0,16},{1,17},{2,18},{3,19},{4,20},{5,21},{6,22},{7,23},{8,24},{9,... | collective-permute-start | bytes 1769480 | tf_op jit(solution)/shard_map/ppermute | solution.py:386
  78.1 10.8 %collective-permute-start.18 = (bf16[96,1024]{1,0:T(8,128)(2,1)}, bf16[96,1024]{1,0:T(8,128)(2,1)}, u32[]{:S(2)}, u32[]{:S(2)}) collective-permute-start(bf16[96,1024]{1,0:T(8,128)(2,1)} %get-tuple-element.98.refs_2_), channel_id=1, source_target_pairs={{0,1},{1,0},{2,3},{3,2},{4,5},{5,4},{6,7},{7,6},{8,9},{9,8},{10,11... | collective-permute-start | bytes 589832 | tf_op jit(solution)/shard_map/ppermute | solution.py:386
  88.3 7.4 %collective-permute-start.20 = (bf16[192,1024]{1,0:T(8,128)(2,1)}, bf16[192,1024]{1,0:T(8,128)(2,1)S(1)}, u32[]{:S(2)}, u32[]{:S(2)}) collective-permute-start(bf16[192,1024]{1,0:T(8,128)(2,1)} %get-tuple-element.109.refs_4_), channel_id=1, source_target_pairs={{0,1},{1,0},{2,3},{3,2},{4,5},{5,4},{6,7},{7,6},{8,9},{9,8},{10,11... | collective-permute-start | bytes 1179656 | tf_op jit(solution)/shard_map/ppermute | solution.py:386
  95.1 2.2 %collective-permute-start.19 = (f32[512,128]{1,0:T(8,128)}, f32[512,128]{1,0:T(8,128)}, u32[]{:S(2)}, u32[]{:S(2)}) collective-permute-start(f32[512,128]{1,0:T(8,128)} %get-tuple-element.105), channel_id=1, source_target_pairs={{0,1},{1,0},{2,3},{3,2},{4,5},{5,4},{6,7},{7,6},{8,9},{9,8},{10,11... | collective-permute-start | bytes 786440 | tf_op jit(solution)/shard_map/ppermute | solution.py:386
  95.2 2.1 %collective-permute-start.21 = (bf16[96,1024]{1,0:T(8,128)(2,1)}, bf16[96,1024]{1,0:T(8,128)(2,1)}, u32[]{:S(2)}, u32[]{:S(2)}) collective-permute-start(bf16[96,1024]{1,0:T(8,128)(2,1)} %get-tuple-element.110.refs_6_), channel_id=1, source_target_pairs={{0,1},{1,0},{2,3},{3,2},{4,5},{5,4},{6,7},{7,6},{8,9},{9,8},{10,11... | collective-permute-start | bytes 589832 | tf_op jit(solution)/shard_map/ppermute | solution.py:386
  95.7 1.7 %copy-start = (bf16[192,1024]{1,0:T(8,128)(2,1)}, bf16[192,1024]{1,0:T(8,128)(2,1)S(1)}, u32[]{:S(2)}) copy-start(bf16[192,1024]{1,0:T(8,128)(2,1)S(1)} %collective-permute-done.20.refs_5_) | copy-start | bytes 1179652

commit v19 on v17

--- a/solution.py
+++ b/solution.py
@@ -182,10 +182,11 @@
     )(tokens, weight, *([total] if more else []))
 
 
-def absorb_kernel(groups, start, sides, more, has_up, info_ref, row_slot_ref, *refs):
+def absorb_kernel(groups, start, sides, more, has_up, keep_up, info_ref, row_slot_ref, *refs):
     count = sum(size for size, _ in groups)
     token_refs, sources, refs = refs[: len(sides)], refs[len(sides) :][:count], refs[len(sides) + count :]
     before, refs = refs[: len(sides) * more], refs[len(sides) * more :]
+    ups_before, refs = refs[:keep_up], refs[keep_up:]
     outs, refs = refs[: len(sides)], refs[len(sides) :]
     up_ref, refs = (refs[0], refs[1:]) if has_up else (None, refs)
     rows_ref, row_slot, held_refs, refs = refs[0], refs[1], refs[2 : 2 + len(before)], refs[2 + len(before) :]
@@ -228,6 +229,10 @@
     begin("late", row_slot_ref, row_slot)
     for source, target in zip(before, held_refs):
         begin("late", source, target)
+    kept_rows = 0
+    for source in ups_before:
+        kept_rows = source.shape[0]
+        begin("late", source, up_ref.at[pl.ds(0, kept_rows)])
     lane_slot = lax.broadcasted_iota(jnp.int32, (1, LANES), 1) // RANK
     state = None
     first = 0
@@ -251,21 +256,22 @@
             state = kept if state is None else state + kept
         if has_up:
             awaited(waits[n, quarter])
-            height = up_ref.shape[0] // count
+            height = (up_ref.shape[0] - kept_rows) // count
             for i in range(size):
                 lanes, which = slice(i * LANES, (i + 1) * LANES), first + i
                 for j in range(up_ref.shape[1] // LANES):
                     top = quarter + j * height
-                    up_ref[
-                        which * height : (which + 1) * height, j * LANES : (j + 1) * LANES
-                    ] = down_ref[top : top + height, lanes]
+                    bottom = kept_rows + which * height
+                    up_ref[bottom : bottom + height, j * LANES : (j + 1) * LANES] = down_ref[
+                        top : top + height, lanes
+                    ]
         first += size
     for i, out_ref in enumerate(outs):
         own = state[i * rows : (i + 1) * rows]
         out_ref[...] = own + held_refs[i][...] if more else own
 
 
-def absorb(info, row_slots, sides, tokens, width, groups, start, before, has_up):
+def absorb(info, row_slots, sides, tokens, width, groups, start, before, has_up, up_before):
     rows = tokens[0].shape[0]
     pieces = [piece for group, _ in groups for piece in group]
     sizes = [(len(group), back) for group, back in groups]
@@ -275,17 +281,20 @@
     vmem = pl.BlockSpec(memory_space=pltpu.VMEM)
     more = before is not None
     state = jax.ShapeDtypeStruct((rows, LANES), jnp.float32)
+    keep_up = up_before is not None
     up_rows = len(pieces) * (height - quarter) * LANES // width
+    if keep_up:
+        up_rows += up_before.shape[0]
     up = jax.ShapeDtypeStruct((up_rows, width), tokens[0].dtype)
     quarters = len({back for _, back in groups})
     cuts = len(QUARTER_CUTS) - 1
-    copies = len(pieces) * (cuts + has_up) + len(sides) * (quarters * cuts + more) + 1
+    copies = len(pieces) * (cuts + has_up) + len(sides) * (quarters * cuts + more) + 1 + keep_up
     outs = (state,) * len(sides) + (up,) * has_up
     return pl.pallas_call(
-        functools.partial(absorb_kernel, sizes, start, sides, more, has_up),
+        functools.partial(absorb_kernel, sizes, start, sides, more, has_up, keep_up),
         out_shape=outs,
         in_specs=[pl.BlockSpec(memory_space=pltpu.SMEM)]
-        + [anywhere] * (1 + len(sides) + len(pieces) + len(sides) * more),
+        + [anywhere] * (1 + len(sides) + len(pieces) + len(sides) * more + keep_up),
         out_specs=(vmem,) * len(outs),
         scratch_shapes=[
             pltpu.VMEM((quarters, len(sides) * rows, quarter), tokens[0].dtype),
@@ -301,7 +310,7 @@
             transcendentals=0,
         ),
         compiler_params=params(),
-    )(info, row_slots, *tokens, *pieces, *(before or ()))
+    )(info, row_slots, *tokens, *pieces, *(before or ()), *([up_before] if keep_up else []))
 
 
 def finish_kernel(count, info_ref, row_slot_ref, mine_ref, theirs_ref, total_ref, *refs):
@@ -397,7 +406,7 @@
     def chip(r, piece):
         return (along_z(r, -piece[0]) ^ (2 * piece[1])) // 2
 
-    kernels = [PIECES[low:high] for low, high in zip(KERNEL_BOUNDS, KERNEL_BOUNDS[1:])]
+    kernels = (PIECES[: KERNEL_BOUNDS[-2]], PIECES[KERNEL_BOUNDS[-2] :])
     info_table = [
         [g, r % 2]
         + [
@@ -447,7 +456,7 @@
     total = base(1, total, total)
     z2, x1, yx0, front, other, total, info = together(z2, x1, yx0, front, other, total, info)
 
-    def update(number, groups, before):
+    def update(number, groups, before, up_before=None):
         return absorb(
             info,
             row_slots,
@@ -458,28 +467,25 @@
             KERNEL_BOUNDS[number],
             before,
             True,
+            up_before,
         )
 
     z3, x2, yz2 = z_back(front), x_swap(z2), y_swap(z2)
     back = piece(1, z2)
-    *state, up_a = update(0, [((front, z1, x0, z2), 0)], None)
+    *state, up = update(0, [((front, z1, x0, z2), 0)], None)
     z3, x2, yz2, x1, back, state, total = together(z3, x2, yz2, x1, back, state, total)
-    there_a = core_swap(up_a)
 
     zb1, x3, yx1 = z_ring(back), x_swap(z3), y_swap(x1)
-    *state, up_b = update(1, [((back, yx0, yz2), 1)], state)
-    zb1, x3, yx1, yz2, back, state, there_a = together(
-        zb1, x3, yx1, yz2, back, state, there_a
-    )
-    there_b = core_swap(up_b)
+    *state, up = update(1, [((back, yx0, yz2), 1)], state, up)
+    zb1, x3, yx1, yz2, back, state = together(zb1, x3, yx1, yz2, back, state)
 
     zb3, xyz2, yx3 = z_back(back), x_swap(yz2), y_swap(x3)
-    *state, up_c = update(2, [((x1, z3, x2, x3), 0), ((zb1, yx1), 1)], state)
-    zb3, xyz2, yx3, state, there_b = together(zb3, xyz2, yx3, state, there_b)
-    there_c = core_swap(up_c)
-
-    mine, others, up_d = update(3, [((zb3, xyz2, yx3), 1)], state)
-    ups = (up_a, there_a, up_b, there_b, up_c, there_c, up_d, core_swap(up_d))
+    *state, up = update(2, [((x1, z3, x2, x3), 0), ((zb1, yx1), 1)], state, up)
+    zb3, xyz2, yx3, state = together(zb3, xyz2, yx3, state)
+    there_up = core_swap(up)
+
+    mine, others, last_up = update(3, [((zb3, xyz2, yx3), 1)], state)
+    ups = (up, there_up, last_up, core_swap(last_up))
     return finish(info, row_slots, mine, core_swap(others), total, ups)
 
 

time: 101 us -> 106 us (1.050)
  the two profiles are of different devices: /device:TPU:0 before, /device:TPU:23 now
where the time goes in v19:
time: 106 us
  Pallas kernels  60.4 us (57%)
  starting transfers between devices  25.4 us (24%)
  waiting for transfers between devices  15.8 us (15%)
  local copies, waits for them, and re-layouts  2.98 us (3%)
    pallas_call x4, Pallas kernels, absorb(): pl.pallas_call(functools.partial(absorb_kernel, sizes, start, sides, more...  29.3 us
    ppermute x20, starting transfers between devices, permuted(): return lax.ppermute(array, axes, pairs)  25.4 us
    pallas_call x2, Pallas kernels, base_part(): pl.pallas_call(functools.partial(base_kernel, steps), out_shape=result, g...  19.5 us
    ppermute x20, waiting for transfers between devices, permuted(): return lax.ppermute(array, axes, pairs)  15.8 us
    pallas_call x1, Pallas kernels, finish(): pl.pallas_call(functools.partial(finish_kernel, len(ups)), out_shape=jax....  6.19 us
    pallas_call x2, Pallas kernels, assemble(): pl.pallas_call(functools.partial(assemble_kernel, back), out_shape=jax.Sh...  5.46 us
  transfers between devices with their start and end apart: 20, of which 8 were waited for; matrix products, arithmetic and copies ran while one was open for 3% of the time, Pallas kernels for 51%

profile of v19, /device:TPU:23, one launch (start us, length us, event | category | flops | bytes accessed | tf_op | source)
XLA Modules:
  0.0 105.7 jit_solution(11549458350519773640)
XLA Ops:
  0.0 0.7 collective-permute-start
  0.7 1.2 %dynamic-slice_bitcast_fusion.info_ref = s32[50]{0:T(128)} fusion(s32[32,50]{1,0:T(8,128)} %constant.20.clone, s32[]{:T(128)S(6)} %select_n.8), kind=kLoop, calls=%fused_computation.3 | loop fusion | bytes 404 | tf_op jit(solution)/shard_map/jit(dynamic_index_in_dim)/squeeze | solution.py:422
  1.8 0.8 select_reduce_fusion
  2.6 0.7 collective-permute-done.there_ref
  3.3 0.4 collective-permute-start.7
  3.7 2.7 %shard_map.73.refs_2_ = bf16[2304,128]{1,0:T(8,128)(2,1)} custom-call(s32[50]{0:T(128)} %dynamic-slice_bitcast_fusion.info_ref, bf16[4,16,8192]{2,1,0:T(8,128)(2,1)} %here_ref.3, bf16[4,16,8192]{2,1,0:T(8,128)(2,1)} %collective-permute-done.there_ref, bf16[4,16,1024]{2,1,0:T(8,128)(2,1)} %up_ref.3), custom_call_target="tpu_custom_call" | custom-call | tf_op jit(solution)/shard_map/pallas_call | solution.py:119
  6.4 0.3 collective-permute-start.2
  6.7 0.1 collective-permute-start.1
  6.8 0.7 collective-permute-start.3
  7.5 9.6 %shard_map.74.refs_0_ = f32[512,1024]{1,0:T(8,128)} custom-call(bf16[512,8192]{1,0:T(8,128)(2,1)} %refs_0_.7, bf16[8192,1024]{1,0:T(8,128)(2,1)} %weight_ref.3), custom_call_target="tpu_custom_call" | custom-call | flops 4294967296 | bytes 14680064 | tf_op jit(solution)/shard_map/pallas_call | solution.py:163
  17.1 0.0 collective-permute-done.3
  17.1 4.5 %collective-permute-done.2.refs_4_ = bf16[2304,128]{1,0:T(8,128)(2,1)} collective-permute-done((bf16[2304,128]{1,0:T(8,128)(2,1)}, bf16[2304,128]{1,0:T(8,128)(2,1)}, u32[]{:S(2)}, u32[]{:S(2)}) %collective-permute-start.2) | collective-permute-done | bytes 589856 | tf_op jit(solution)/shard_map/ppermute | solution.py:395
  21.6 0.0 collective-permute-done.1.refs_3_
  21.6 0.2 collective-permute-start.6
  21.8 1.1 %collective-permute-start.5 = (bf16[2304,128]{1,0:T(8,128)(2,1)}, bf16[2304,128]{1,0:T(8,128)(2,1)}, u32[]{:S(2)}, u32[]{:S(2)}) collective-permute-start(bf16[2304,128]{1,0:T(8,128)(2,1)} %collective-permute-done.1.refs_3_), channel_id=1, source_target_pairs={{0,2},{1,3},{2,0},{3,1},{4,6},{5,7},{6,4},{7,5},{8,10},{9,11},{10,... | collective-permute-start | bytes 1769480 | tf_op jit(solution)/shard_map/ppermute | solution.py:395
  23.0 1.0 collective-permute-start.4
  24.0 9.9 %shard_map.75.total_ref = f32[512,1024]{1,0:T(8,128)} custom-call(bf16[512,8192]{1,0:T(8,128)(2,1)} %refs_0_.7, bf16[8192,1024]{1,0:T(8,128)(2,1)} %weight_ref.3, f32[512,1024]{1,0:T(8,128)} %shard_map.74.refs_0_), custom_call_target="tpu_custom_call" | custom-call | flops 4294967296 | bytes 14680064 | tf_op jit(solution)/shard_map/pallas_call | solution.py:163
  33.9 1.7 %collective-permute-done.6.refs_3_ = bf16[2304,128]{1,0:T(8,128)(2,1)} collective-permute-done((bf16[2304,128]{1,0:T(8,128)(2,1)}, bf16[2304,128]{1,0:T(8,128)(2,1)}, u32[]{:S(2)}, u32[]{:S(2)}) %collective-permute-start.6) | collective-permute-done | bytes 589856 | tf_op jit(solution)/shard_map/ppermute | solution.py:395
  35.5 0.0 collective-permute-done.5.refs_2_
  35.5 1.8 %collective-permute-done.4.refs_5_ = bf16[2304,128]{1,0:T(8,128)(2,1)} collective-permute-done((bf16[2304,128]{1,0:T(8,128)(2,1)}, bf16[2304,128]{1,0:T(8,128)(2,1)}, u32[]{:S(2)}, u32[]{:S(2)}) %collective-permute-start.4) | collective-permute-done | bytes 589856 | tf_op jit(solution)/shard_map/ppermute | solution.py:395
  37.3 0.0 collective-permute-done.7.refs_1_
  37.3 2.1 %collective-permute-start.8 = (bf16[2304,128]{1,0:T(8,128)(2,1)}, bf16[2304,128]{1,0:T(8,128)(2,1)}, u32[]{:S(2)}, u32[]{:S(2)}) collective-permute-start(bf16[2304,128]{1,0:T(8,128)(2,1)} %shard_map.73.refs_2_), channel_id=1, source_target_pairs={{0,8},{1,9},{2,10},{3,11},{4,0},{5,1},{6,2},{7,3},{8,12},{9,13},{1... | collective-permute-start | bytes 1769480 | tf_op jit(solution)/shard_map/ppermute | solution.py:395
  39.4 1.2 %collective-permute-start.10 = (bf16[2304,128]{1,0:T(8,128)(2,1)}, bf16[2304,128]{1,0:T(8,128)(2,1)}, u32[]{:S(2)}, u32[]{:S(2)}) collective-permute-start(bf16[2304,128]{1,0:T(8,128)(2,1)} %collective-permute-done.4.refs_5_), channel_id=1, source_target_pairs={{0,16},{1,17},{2,18},{3,19},{4,20},{5,21},{6,22},{7,23},{8,24},{9,... | collective-permute-start | bytes 1769480 | tf_op jit(solution)/shard_map/ppermute | solution.py:395
  40.6 0.3 collective-permute-start.9
  40.9 1.0 copy.19.row_slot_ref
  41.9 2.7 %shard_map.76.refs_2_ = bf16[2304,128]{1,0:T(8,128)(2,1)} custom-call(s32[50]{0:T(128)} %dynamic-slice_bitcast_fusion.info_ref, bf16[4,16,8192]{2,1,0:T(8,128)(2,1)} %here_ref.3, bf16[4,16,8192]{2,1,0:T(8,128)(2,1)} %collective-permute-done.there_ref, bf16[4,16,1024]{2,1,0:T(8,128)(2,1)} %up_ref.3), custom_call_target="tpu_custom_call" | custom-call | tf_op jit(solution)/shard_map/pallas_call | solution.py:119
  44.6 6.4 %shard_map.77 = (f32[512,128]{1,0:T(8,128)}, f32[512,128]{1,0:T(8,128)}, bf16[128,1024]{1,0:T(8,128)(2,1)}) custom-call(s32[50]{0:T(128)} %dynamic-slice_bitcast_fusion.info_ref, s32[1024,1]{1,0:T(8,128)} %copy.19.row_slot_ref, bf16[512,8192]{1,0:T(8,128)(2,1)} %refs_0_.7, bf16[512,8192]{1,0:T(8,128)(2,1)} %collective-permute-done.7.refs_1_, ...), custom_call_target="tpu_custom_call" | custom-call | flops 2147483648 | bytes 6553600 | tf_op jit(solution)/shard_map/pallas_call | solution.py:293
  51.0 0.0 collective-permute-done.8.refs_3_
  51.0 0.4 collective-permute-done.10.refs_4_
  51.5 1.0 collective-permute-done.9.refs_4_
  52.4 0.3 collective-permute-start.12
  52.7 0.3 collective-permute-start.13
  53.0 0.6 collective-permute-start.11
  53.6 6.3 %shard_map.78 = (f32[512,128]{1,0:T(8,128)}, f32[512,128]{1,0:T(8,128)}, bf16[224,1024]{1,0:T(8,128)(2,1)}) custom-call(s32[50]{0:T(128)} %dynamic-slice_bitcast_fusion.info_ref, s32[1024,1]{1,0:T(8,128)} %copy.19.row_slot_ref, bf16[512,8192]{1,0:T(8,128)(2,1)} %refs_0_.7, bf16[512,8192]{1,0:T(8,128)(2,1)} %collective-permute-done.7.refs_1_, ...), custom_call_target="tpu_custom_call" | custom-call | flops 1610612736 | bytes 5963776 | tf_op jit(solution)/shard_map/pallas_call | solution.py:293
  59.9 4.3 %collective-permute-done.12.refs_5_ = bf16[2304,128]{1,0:T(8,128)(2,1)} collective-permute-done((bf16[2304,128]{1,0:T(8,128)(2,1)}, bf16[2304,128]{1,0:T(8,128)(2,1)}, u32[]{:S(2)}, u32[]{:S(2)}) %collective-permute-start.12) | collective-permute-done | bytes 589856 | tf_op jit(solution)/shard_map/ppermute | solution.py:395
  64.2 0.0 collective-permute-done.13.refs_7_
  64.2 0.0 collective-permute-done.11.refs_6_
  64.2 0.3 collective-permute-start.14
  64.5 1.1 %collective-permute-start.15 = (bf16[2304,128]{1,0:T(8,128)(2,1)}, bf16[2304,128]{1,0:T(8,128)(2,1)}, u32[]{:S(2)}, u32[]{:S(2)}) collective-permute-start(bf16[2304,128]{1,0:T(8,128)(2,1)} %collective-permute-done.10.refs_4_), channel_id=1, source_target_pairs={{0,2},{1,3},{2,0},{3,1},{4,6},{5,7},{6,4},{7,5},{8,10},{9,11},{10,... | collective-permute-start | bytes 1769480 | tf_op jit(solution)/shard_map/ppermute | solution.py:395
  65.6 1.1 %collective-permute-start.16 = (bf16[2304,128]{1,0:T(8,128)(2,1)}, bf16[2304,128]{1,0:T(8,128)(2,1)}, u32[]{:S(2)}, u32[]{:S(2)}) collective-permute-start(bf16[2304,128]{1,0:T(8,128)(2,1)} %collective-permute-done.12.refs_5_), channel_id=1, source_target_pairs={{0,16},{1,17},{2,18},{3,19},{4,20},{5,21},{6,22},{7,23},{8,24},{9,... | collective-permute-start | bytes 1769480 | tf_op jit(solution)/shard_map/ppermute | solution.py:395
  66.7 10.4 %shard_map.79 = (f32[512,128]{1,0:T(8,128)}, f32[512,128]{1,0:T(8,128)}, bf16[416,1024]{1,0:T(8,128)(2,1)}) custom-call(s32[50]{0:T(128)} %dynamic-slice_bitcast_fusion.info_ref, s32[1024,1]{1,0:T(8,128)} %copy.19.row_slot_ref, bf16[512,8192]{1,0:T(8,128)(2,1)} %refs_0_.7, bf16[512,8192]{1,0:T(8,128)(2,1)} %collective-permute-done.7.refs_1_, ...), custom_call_target="tpu_custom_call" | custom-call | flops 3221225472 | bytes 11927552 | tf_op jit(solution)/shard_map/pallas_call | solution.py:293
  77.1 13.1 %collective-permute-start.18 = (bf16[416,1024]{1,0:T(8,128)(2,1)}, bf16[416,1024]{1,0:T(8,128)(2,1)}, u32[]{:S(2)}, u32[]{:S(2)}) collective-permute-start(bf16[416,1024]{1,0:T(8,128)(2,1)} %get-tuple-element.105.refs_0_), channel_id=1, source_target_pairs={{0,1},{1,0},{2,3},{3,2},{4,5},{5,4},{6,7},{7,6},{8,9},{9,8},{10,11... | collective-permute-start | bytes 2555912 | tf_op jit(solution)/shard_map/ppermute | solution.py:395
  90.2 0.0 collective-permute-done.14.refs_2_
  90.2 0.0 collective-permute-done.15.refs_3_
  90.2 0.0 collective-permute-done.16.refs_4_
  90.2 6.2 %shard_map.80 = (f32[512,128]{1,0:T(8,128)}, f32[512,128]{1,0:T(8,128)}, bf16[96,1024]{1,0:T(8,128)(2,1)}) custom-call(s32[50]{0:T(128)} %dynamic-slice_bitcast_fusion.info_ref, s32[1024,1]{1,0:T(8,128)} %copy.19.row_slot_ref, bf16[512,8192]{1,0:T(8,128)(2,1)} %refs_0_.7, bf16[512,8192]{1,0:T(8,128)(2,1)} %collective-permute-done.7.refs_1_, ...), custom_call_target="tpu_custom_call" | custom-call | flops 1610612736 | bytes 5963776 | tf_op jit(solution)/shard_map/pallas_call | solution.py:293
  96.4 0.1 collective-permute-start.17
  96.5 0.5 collective-permute-start.19
  97.0 1.5 %collective-permute-done.19.refs_3_ = bf16[96,1024]{1,0:T(8,128)(2,1)S(1)} collective-permute-done((bf16[96,1024]{1,0:T(8,128)(2,1)}, bf16[96,1024]{1,0:T(8,128)(2,1)S(1)}, u32[]{:S(2)}, u32[]{:S(2)}) %collective-permute-start.19) | collective-permute-done | bytes 196640 | tf_op jit(solution)/shard_map/ppermute | solution.py:395
  98.5 0.0 copy-start.1
  98.5 0.0 collective-permute-done.18.refs_1_
  98.5 0.0 collective-permute-done.17.theirs_ref
  98.6 0.0 copy-start
  98.6 0.7 copy-done.1
  99.2 0.1 copy-done
  99.3 6.2 %shard_map.81 = bf16[512,1024]{1,0:T(8,128)(2,1)} custom-call(s32[50]{0:T(128)} %dynamic-slice_bitcast_fusion.info_ref, s32[1024,1]{1,0:T(8,128)} %copy.19.row_slot_ref, f32[512,128]{1,0:T(8,128)} %get-tuple-element.102.mine_ref, f32[512,128]{1,0:T(8,128)} %copy-done, f32[512,1024]{1,0:T(8,128)} %shard_map.75.total_ref, ...), custom_call_target="tpu_custom_call" | custom-call | flops 2147483648 | bytes 5242880 | tf_op jit(solution)/shard_map/pallas_call | solution.py:354
  (1 shorter events, 0.0 us)
Async XLA Ops:
  0.0 3.3 %collective-permute-start = (bf16[4,16,8192]{2,1,0:T(8,128)(2,1)}, bf16[4,16,8192]{2,1,0:T(8,128)(2,1)}, u32[]{:S(2)}, u32[]{:S(2)}) collective-permute-start(bf16[4,16,8192]{2,1,0:T(8,128)(2,1)} %here_ref.3), channel_id=1, source_target_pairs={{0,1},{1,0},{2,3},{3,2},{4,5},{5,4},{6,7},{7,6},{8,9},{9,8},{10,11... | collective-permute-start | bytes 3145736 | tf_op jit(solution)/shard_map/ppermute | solution.py:395
  3.3 34.0 %collective-permute-start.7 = (bf16[512,8192]{1,0:T(8,128)(2,1)}, bf16[512,8192]{1,0:T(8,128)(2,1)}, u32[]{:S(2)}, u32[]{:S(2)}) collective-permute-start(bf16[512,8192]{1,0:T(8,128)(2,1)} %refs_0_.7), channel_id=1, source_target_pairs={{0,1},{1,0},{2,3},{3,2},{4,5},{5,4},{6,7},{7,6},{8,9},{9,8},{10,11... | collective-permute-start | bytes 25165832 | tf_op jit(solution)/shard_map/ppermute | solution.py:395
  6.4 15.2 %collective-permute-start.2 = (bf16[2304,128]{1,0:T(8,128)(2,1)}, bf16[2304,128]{1,0:T(8,128)(2,1)}, u32[]{:S(2)}, u32[]{:S(2)}) collective-permute-start(bf16[2304,128]{1,0:T(8,128)(2,1)} %shard_map.73.refs_2_), channel_id=1, source_target_pairs={{0,2},{1,3},{2,0},{3,1},{4,6},{5,7},{6,4},{7,5},{8,10},{9,11},{10,... | collective-permute-start | bytes 1769480 | tf_op jit(solution)/shard_map/ppermute | solution.py:395
  6.7 14.9 %collective-permute-start.1 = (bf16[2304,128]{1,0:T(8,128)(2,1)}, bf16[2304,128]{1,0:T(8,128)(2,1)}, u32[]{:S(2)}, u32[]{:S(2)}) collective-permute-start(bf16[2304,128]{1,0:T(8,128)(2,1)} %shard_map.73.refs_2_), channel_id=1, source_target_pairs={{0,4},{1,5},{2,6},{3,7},{4,12},{5,13},{6,14},{7,15},{8,0},{9,1},{1... | collective-permute-start | bytes 1769480 | tf_op jit(solution)/shard_map/ppermute | solution.py:395
  6.8 10.3 %collective-permute-start.3 = (s32[512]{0:T(512)S(1)}, s32[512]{0:T(512)S(1)}, u32[]{:S(2)}, u32[]{:S(2)}) collective-permute-start(s32[512]{0:T(512)S(1)} %select_reduce_fusion), channel_id=1, source_target_pairs={{0,1},{1,0},{2,3},{3,2},{4,5},{5,4},{6,7},{7,6},{8,9},{9,8},{10,11... | collective-permute-start | bytes 6152 | tf_op jit(solution)/shard_map/ppermute | solution.py:395
  21.6 13.9 %collective-permute-start.6 = (bf16[2304,128]{1,0:T(8,128)(2,1)}, bf16[2304,128]{1,0:T(8,128)(2,1)}, u32[]{:S(2)}, u32[]{:S(2)}) collective-permute-start(bf16[2304,128]{1,0:T(8,128)(2,1)} %collective-permute-done.2.refs_4_), channel_id=1, source_target_pairs={{0,16},{1,17},{2,18},{3,19},{4,20},{5,21},{6,22},{7,23},{8,24},{9,... | collective-permute-start | bytes 1769480 | tf_op jit(solution)/shard_map/ppermute | solution.py:395
  21.8 13.7 %collective-permute-start.5 = (bf16[2304,128]{1,0:T(8,128)(2,1)}, bf16[2304,128]{1,0:T(8,128)(2,1)}, u32[]{:S(2)}, u32[]{:S(2)}) collective-permute-start(bf16[2304,128]{1,0:T(8,128)(2,1)} %collective-permute-done.1.refs_3_), channel_id=1, source_target_pairs={{0,2},{1,3},{2,0},{3,1},{4,6},{5,7},{6,4},{7,5},{8,10},{9,11},{10,... | collective-permute-start | bytes 1769480 | tf_op jit(solution)/shard_map/ppermute | solution.py:395
  23.0 14.3 %collective-permute-start.4 = (bf16[2304,128]{1,0:T(8,128)(2,1)}, bf16[2304,128]{1,0:T(8,128)(2,1)}, u32[]{:S(2)}, u32[]{:S(2)}) collective-permute-start(bf16[2304,128]{1,0:T(8,128)(2,1)} %collective-permute-done.1.refs_3_), channel_id=1, source_target_pairs={{0,4},{1,5},{2,6},{3,7},{4,12},{5,13},{6,14},{7,15},{8,0},{9,1},{1... | collective-permute-start | bytes 1769480 | tf_op jit(solution)/shard_map/ppermute | solution.py:395
  37.3 13.7 %collective-permute-start.8 = (bf16[2304,128]{1,0:T(8,128)(2,1)}, bf16[2304,128]{1,0:T(8,128)(2,1)}, u32[]{:S(2)}, u32[]{:S(2)}) collective-permute-start(bf16[2304,128]{1,0:T(8,128)(2,1)} %shard_map.73.refs_2_), channel_id=1, source_target_pairs={{0,8},{1,9},{2,10},{3,11},{4,0},{5,1},{6,2},{7,3},{8,12},{9,13},{1... | collective-permute-start | bytes 1769480 | tf_op jit(solution)/shard_map/ppermute | solution.py:395
  39.4 12.1 %collective-permute-start.10 = (bf16[2304,128]{1,0:T(8,128)(2,1)}, bf16[2304,128]{1,0:T(8,128)(2,1)}, u32[]{:S(2)}, u32[]{:S(2)}) collective-permute-start(bf16[2304,128]{1,0:T(8,128)(2,1)} %collective-permute-done.4.refs_5_), channel_id=1, source_target_pairs={{0,16},{1,17},{2,18},{3,19},{4,20},{5,21},{6,22},{7,23},{8,24},{9,... | collective-permute-start | bytes 1769480 | tf_op jit(solution)/shard_map/ppermute | solution.py:395
  40.6 11.8 %collective-permute-start.9 = (bf16[2304,128]{1,0:T(8,128)(2,1)}, bf16[2304,128]{1,0:T(8,128)(2,1)}, u32[]{:S(2)}, u32[]{:S(2)}) collective-permute-start(bf16[2304,128]{1,0:T(8,128)(2,1)} %collective-permute-done.4.refs_5_), channel_id=1, source_target_pairs={{0,2},{1,3},{2,0},{3,1},{4,6},{5,7},{6,4},{7,5},{8,10},{9,11},{10,... | collective-permute-start | bytes 1769480 | tf_op jit(solution)/shard_map/ppermute | solution.py:395
  52.4 11.8 %collective-permute-start.12 = (bf16[2304,128]{1,0:T(8,128)(2,1)}, bf16[2304,128]{1,0:T(8,128)(2,1)}, u32[]{:S(2)}, u32[]{:S(2)}) collective-permute-start(bf16[2304,128]{1,0:T(8,128)(2,1)} %collective-permute-done.8.refs_3_), channel_id=1, source_target_pairs={{0,2},{1,3},{2,0},{3,1},{4,6},{5,7},{6,4},{7,5},{8,10},{9,11},{10,... | collective-permute-start | bytes 1769480 | tf_op jit(solution)/shard_map/ppermute | solution.py:395
  52.7 11.5 %collective-permute-start.13 = (bf16[2304,128]{1,0:T(8,128)(2,1)}, bf16[2304,128]{1,0:T(8,128)(2,1)}, u32[]{:S(2)}, u32[]{:S(2)}) collective-permute-start(bf16[2304,128]{1,0:T(8,128)(2,1)} %collective-permute-done.5.refs_2_), channel_id=1, source_target_pairs={{0,16},{1,17},{2,18},{3,19},{4,20},{5,21},{6,22},{7,23},{8,24},{9,... | collective-permute-start | bytes 1769480 | tf_op jit(solution)/shard_map/ppermute | solution.py:395
  53.0 11.3 %collective-permute-start.11 = (bf16[2304,128]{1,0:T(8,128)(2,1)}, bf16[2304,128]{1,0:T(8,128)(2,1)}, u32[]{:S(2)}, u32[]{:S(2)}) collective-permute-start(bf16[2304,128]{1,0:T(8,128)(2,1)} %shard_map.76.refs_2_), channel_id=1, source_target_pairs={{0,4},{1,5},{2,6},{3,7},{4,12},{5,13},{6,14},{7,15},{8,0},{9,1},{1... | collective-permute-start | bytes 1769480 | tf_op jit(solution)/shard_map/ppermute | solution.py:395
  64.2 26.0 %collective-permute-start.14 = (bf16[2304,128]{1,0:T(8,128)(2,1)}, bf16[2304,128]{1,0:T(8,128)(2,1)}, u32[]{:S(2)}, u32[]{:S(2)}) collective-permute-start(bf16[2304,128]{1,0:T(8,128)(2,1)} %shard_map.76.refs_2_), channel_id=1, source_target_pairs={{0,8},{1,9},{2,10},{3,11},{4,0},{5,1},{6,2},{7,3},{8,12},{9,13},{1... | collective-permute-start | bytes 1769480 | tf_op jit(solution)/shard_map/ppermute | solution.py:395
  64.5 25.7 %collective-permute-start.15 = (bf16[2304,128]{1,0:T(8,128)(2,1)}, bf16[2304,128]{1,0:T(8,128)(2,1)}, u32[]{:S(2)}, u32[]{:S(2)}) collective-permute-start(bf16[2304,128]{1,0:T(8,128)(2,1)} %collective-permute-done.10.refs_4_), channel_id=1, source_target_pairs={{0,2},{1,3},{2,0},{3,1},{4,6},{5,7},{6,4},{7,5},{8,10},{9,11},{10,... | collective-permute-start | bytes 1769480 | tf_op jit(solution)/shard_map/ppermute | solution.py:395
  65.6 24.6 %collective-permute-start.16 = (bf16[2304,128]{1,0:T(8,128)(2,1)}, bf16[2304,128]{1,0:T(8,128)(2,1)}, u32[]{:S(2)}, u32[]{:S(2)}) collective-permute-start(bf16[2304,128]{1,0:T(8,128)(2,1)} %collective-permute-done.12.refs_5_), channel_id=1, source_target_pairs={{0,16},{1,17},{2,18},{3,19},{4,20},{5,21},{6,22},{7,23},{8,24},{9,... | collective-permute-start | bytes 1769480 | tf_op jit(solution)/shard_map/ppermute | solution.py:395
  77.1 21.5 %collective-permute-start.18 = (bf16[416,1024]{1,0:T(8,128)(2,1)}, bf16[416,1024]{1,0:T(8,128)(2,1)}, u32[]{:S(2)}, u32[]{:S(2)}) collective-permute-start(bf16[416,1024]{1,0:T(8,128)(2,1)} %get-tuple-element.105.refs_0_), channel_id=1, source_target_pairs={{0,1},{1,0},{2,3},{3,2},{4,5},{5,4},{6,7},{7,6},{8,9},{9,8},{10,11... | collective-permute-start | bytes 2555912 | tf_op jit(solution)/shard_map/ppermute | solution.py:395
  96.4 2.1 %collective-permute-start.17 = (f32[512,128]{1,0:T(8,128)}, f32[512,128]{1,0:T(8,128)S(1)}, u32[]{:S(2)}, u32[]{:S(2)}) collective-permute-start(f32[512,128]{1,0:T(8,128)} %get-tuple-element.103), channel_id=1, source_target_pairs={{0,1},{1,0},{2,3},{3,2},{4,5},{5,4},{6,7},{7,6},{8,9},{9,8},{10,11... | collective-permute-start | bytes 786440 | tf_op jit(solution)/shard_map/ppermute | solution.py:395
  96.5 2.0 %collective-permute-start.19 = (bf16[96,1024]{1,0:T(8,128)(2,1)}, bf16[96,1024]{1,0:T(8,128)(2,1)S(1)}, u32[]{:S(2)}, u32[]{:S(2)}) collective-permute-start(bf16[96,1024]{1,0:T(8,128)(2,1)} %get-tuple-element.106.refs_2_), channel_id=1, source_target_pairs={{0,1},{1,0},{2,3},{3,2},{4,5},{5,4},{6,7},{7,6},{8,9},{9,8},{10,11... | collective-permute-start | bytes 589832 | tf_op jit(solution)/shard_map/ppermute | solution.py:395
  98.5 0.7 copy-start.1
  98.6 0.8 copy-start

commit v20 on v17

--- a/solution.py
+++ b/solution.py
@@ -438,14 +438,16 @@
 
     z1, x0 = z_ring(front), x_swap(front)
     other = core_swap(tokens_late)
-    other_slot = core_swap(row_slot[:, 0])
     total = base(0, None, front)
-    row_slots = jnp.concatenate([row_slot, other_slot[:, None]], axis=0)
-    z1, x0, front, total, row_slots = together(z1, x0, front, total, row_slots)
+    z1, x0, front, total = together(z1, x0, front, total)
 
     z2, x1, yx0 = z_ring(z1), x_swap(z1), y_swap(x0)
     total = base(1, total, total)
-    z2, x1, yx0, front, other, total, info = together(z2, x1, yx0, front, other, total, info)
+    other_slot = core_swap(after(row_slot[:, 0], total))
+    z2, x1, yx0, front, other, total, info, other_slot = together(
+        z2, x1, yx0, front, other, total, info, other_slot
+    )
+    row_slots = jnp.concatenate([row_slot, other_slot[:, None]], axis=0)
 
     def update(number, groups, before):
         return absorb(
@@ -463,19 +465,21 @@
     z3, x2, yz2 = z_back(front), x_swap(z2), y_swap(z2)
     back = piece(1, z2)
     *state, up_a = update(0, [((front, z1, x0, z2), 0)], None)
-    z3, x2, yz2, x1, back, state, total = together(z3, x2, yz2, x1, back, state, total)
     there_a = core_swap(up_a)
+    z3, x2, yz2, x1, back, state, total, there_a = together(
+        z3, x2, yz2, x1, back, state, total, there_a
+    )
 
     zb1, x3, yx1 = z_ring(back), x_swap(z3), y_swap(x1)
     *state, up_b = update(1, [((back, yx0, yz2), 1)], state)
-    zb1, x3, yx1, yz2, back, state, there_a = together(
-        zb1, x3, yx1, yz2, back, state, there_a
-    )
     there_b = core_swap(up_b)
+    zb1, x3, yx1, yz2, back, state, there_b = together(
+        zb1, x3, yx1, yz2, back, state, there_b
+    )
 
     zb3, xyz2, yx3 = z_back(back), x_swap(yz2), y_swap(x3)
     *state, up_c = update(2, [((x1, z3, x2, x3), 0), ((zb1, yx1), 1)], state)
-    zb3, xyz2, yx3, state, there_b = together(zb3, xyz2, yx3, state, there_b)
+    zb3, xyz2, yx3, state = together(zb3, xyz2, yx3, state)
     there_c = core_swap(up_c)
 
     mine, others, up_d = update(3, [((zb3, xyz2, yx3), 1)], state)

time: 101 us -> 106 us (1.050)
  waiting for transfers between devices: 16.8 us -> 21.5 us
    ppermute x22, waiting for transfers between devices: 16.8 us -> 21.5 us  [permuted(): return lax.ppermute(array, axes, pairs)]
  transfers between devices with their start and end apart: 22 -> 22, of which waited for: 13 -> 16; matrix products, arithmetic and copies ran while one was open for 3% -> 3% of each run, Pallas kernels for 54% -> 51%
where the time goes in v20:
time: 106 us
  Pallas kernels  60.2 us (57%)
  waiting for transfers between devices  21.5 us (20%)
  starting transfers between devices  21 us (20%)
  local copies, waits for them, and re-layouts  2.31 us (2%)
    pallas_call x4, Pallas kernels, absorb(): pl.pallas_call(functools.partial(absorb_kernel, sizes, start, sides, more...  29 us
    ppermute x22, waiting for transfers between devices, permuted(): return lax.ppermute(array, axes, pairs)  21.5 us
    ppermute x22, starting transfers between devices, permuted(): return lax.ppermute(array, axes, pairs)  21 us
    pallas_call x2, Pallas kernels, base_part(): pl.pallas_call(functools.partial(base_kernel, steps), out_shape=result, g...  19.5 us
    pallas_call x1, Pallas kernels, finish(): pl.pallas_call(functools.partial(finish_kernel, len(ups)), out_shape=jax....  6.19 us
    pallas_call x2, Pallas kernels, assemble(): pl.pallas_call(functools.partial(assemble_kernel, back), out_shape=jax.Sh...  5.5 us
  transfers between devices with their start and end apart: 22, of which 16 were waited for; matrix products, arithmetic and copies ran while one was open for 3% of the time, Pallas kernels for 51%

profile of v20, /device:TPU:0, one launch (start us, length us, event | category | flops | bytes accessed | tf_op | source)
XLA Modules:
  0.0 106.1 jit_solution(1776441902283569522)
XLA Ops:
  0.0 0.5 collective-permute-start
  0.5 1.3 %dynamic-slice_bitcast_fusion.info_ref = s32[50]{0:T(128)} fusion(s32[32,50]{1,0:T(8,128)} %constant.20.clone, s32[]{:T(128)S(6)} %select_n.8), kind=kLoop, calls=%fused_computation.3 | loop fusion | bytes 404 | tf_op jit(solution)/shard_map/jit(dynamic_index_in_dim)/squeeze | solution.py:413
  1.7 0.8 select_reduce_fusion
  2.5 0.6 collective-permute-done.there_ref
  3.1 0.4 collective-permute-start.6
  3.5 2.8 %shard_map.73.refs_2_ = bf16[2304,128]{1,0:T(8,128)(2,1)} custom-call(s32[50]{0:T(128)} %dynamic-slice_bitcast_fusion.info_ref, bf16[4,16,8192]{2,1,0:T(8,128)(2,1)} %here_ref.3, bf16[4,16,8192]{2,1,0:T(8,128)(2,1)} %collective-permute-done.there_ref, bf16[4,16,1024]{2,1,0:T(8,128)(2,1)} %up_ref.3), custom_call_target="tpu_custom_call" | custom-call | tf_op jit(solution)/shard_map/pallas_call | solution.py:119
  6.2 2.7 %collective-permute-start.2 = (bf16[2304,128]{1,0:T(8,128)(2,1)}, bf16[2304,128]{1,0:T(8,128)(2,1)}, u32[]{:S(2)}, u32[]{:S(2)}) collective-permute-start(bf16[2304,128]{1,0:T(8,128)(2,1)} %shard_map.73.refs_2_), channel_id=1, source_target_pairs={{0,2},{1,3},{2,0},{3,1},{4,6},{5,7},{6,4},{7,5},{8,10},{9,11},{10,... | collective-permute-start | bytes 1769480 | tf_op jit(solution)/shard_map/ppermute | solution.py:386
  8.9 1.6 %collective-permute-start.1 = (bf16[2304,128]{1,0:T(8,128)(2,1)}, bf16[2304,128]{1,0:T(8,128)(2,1)}, u32[]{:S(2)}, u32[]{:S(2)}) collective-permute-start(bf16[2304,128]{1,0:T(8,128)(2,1)} %shard_map.73.refs_2_), channel_id=1, source_target_pairs={{0,4},{1,5},{2,6},{3,7},{4,12},{5,13},{6,14},{7,15},{8,0},{9,1},{1... | collective-permute-start | bytes 1769480 | tf_op jit(solution)/shard_map/ppermute | solution.py:386
  10.5 9.6 %shard_map.74.refs_0_ = f32[512,1024]{1,0:T(8,128)} custom-call(bf16[512,8192]{1,0:T(8,128)(2,1)} %refs_0_.7, bf16[8192,1024]{1,0:T(8,128)(2,1)} %weight_ref.3), custom_call_target="tpu_custom_call" | custom-call | flops 4294967296 | bytes 14680064 | tf_op jit(solution)/shard_map/pallas_call | solution.py:163
  20.1 3.0 %collective-permute-done.2.refs_4_ = bf16[2304,128]{1,0:T(8,128)(2,1)} collective-permute-done((bf16[2304,128]{1,0:T(8,128)(2,1)}, bf16[2304,128]{1,0:T(8,128)(2,1)}, u32[]{:S(2)}, u32[]{:S(2)}) %collective-permute-start.2) | collective-permute-done | bytes 589856 | tf_op jit(solution)/shard_map/ppermute | solution.py:386
  23.1 2.4 %collective-permute-done.1.refs_3_ = bf16[2304,128]{1,0:T(8,128)(2,1)} collective-permute-done((bf16[2304,128]{1,0:T(8,128)(2,1)}, bf16[2304,128]{1,0:T(8,128)(2,1)}, u32[]{:S(2)}, u32[]{:S(2)}) %collective-permute-start.1) | collective-permute-done | bytes 589856 | tf_op jit(solution)/shard_map/ppermute | solution.py:386
  25.5 1.5 %collective-permute-start.5 = (bf16[2304,128]{1,0:T(8,128)(2,1)}, bf16[2304,128]{1,0:T(8,128)(2,1)}, u32[]{:S(2)}, u32[]{:S(2)}) collective-permute-start(bf16[2304,128]{1,0:T(8,128)(2,1)} %collective-permute-done.2.refs_4_), channel_id=1, source_target_pairs={{0,16},{1,17},{2,18},{3,19},{4,20},{5,21},{6,22},{7,23},{8,24},{9,... | collective-permute-start | bytes 1769480 | tf_op jit(solution)/shard_map/ppermute | solution.py:386
  27.0 0.5 collective-permute-start.4
  27.5 0.8 collective-permute-start.3
  28.3 9.9 %shard_map.75.total_ref = f32[512,1024]{1,0:T(8,128)} custom-call(bf16[512,8192]{1,0:T(8,128)(2,1)} %refs_0_.7, bf16[8192,1024]{1,0:T(8,128)(2,1)} %weight_ref.3, f32[512,1024]{1,0:T(8,128)} %shard_map.74.refs_0_), custom_call_target="tpu_custom_call" | custom-call | flops 4294967296 | bytes 14680064 | tf_op jit(solution)/shard_map/pallas_call | solution.py:163
  38.2 0.1 collective-permute-start.7
  38.3 1.1 %collective-permute-done.7 = s32[512]{0:T(512)S(1)} collective-permute-done((s32[512]{0:T(512)S(1)}, s32[512]{0:T(512)S(1)}, u32[]{:S(2)}, u32[]{:S(2)}) %collective-permute-start.7) | collective-permute-done | bytes 2080 | tf_op jit(solution)/shard_map/ppermute | solution.py:386
  39.4 0.8 collective-permute-done.5.refs_3_
  40.3 1.2 %collective-permute-done.4.refs_2_ = bf16[2304,128]{1,0:T(8,128)(2,1)} collective-permute-done((bf16[2304,128]{1,0:T(8,128)(2,1)}, bf16[2304,128]{1,0:T(8,128)(2,1)}, u32[]{:S(2)}, u32[]{:S(2)}) %collective-permute-start.4) | collective-permute-done | bytes 589856 | tf_op jit(solution)/shard_map/ppermute | solution.py:386
  41.5 1.2 %collective-permute-done.3.refs_5_ = bf16[2304,128]{1,0:T(8,128)(2,1)} collective-permute-done((bf16[2304,128]{1,0:T(8,128)(2,1)}, bf16[2304,128]{1,0:T(8,128)(2,1)}, u32[]{:S(2)}, u32[]{:S(2)}) %collective-permute-start.3) | collective-permute-done | bytes 589856 | tf_op jit(solution)/shard_map/ppermute | solution.py:386
  42.7 0.0 collective-permute-done.6.refs_1_
  42.7 1.5 %collective-permute-start.8 = (bf16[2304,128]{1,0:T(8,128)(2,1)}, bf16[2304,128]{1,0:T(8,128)(2,1)}, u32[]{:S(2)}, u32[]{:S(2)}) collective-permute-start(bf16[2304,128]{1,0:T(8,128)(2,1)} %shard_map.73.refs_2_), channel_id=1, source_target_pairs={{0,8},{1,9},{2,10},{3,11},{4,0},{5,1},{6,2},{7,3},{8,12},{9,13},{1... | collective-permute-start | bytes 1769480 | tf_op jit(solution)/shard_map/ppermute | solution.py:386
  44.2 0.5 collective-permute-start.10
  44.7 1.5 %collective-permute-start.9 = (bf16[2304,128]{1,0:T(8,128)(2,1)}, bf16[2304,128]{1,0:T(8,128)(2,1)}, u32[]{:S(2)}, u32[]{:S(2)}) collective-permute-start(bf16[2304,128]{1,0:T(8,128)(2,1)} %collective-permute-done.3.refs_5_), channel_id=1, source_target_pairs={{0,2},{1,3},{2,0},{3,1},{4,6},{5,7},{6,4},{7,5},{8,10},{9,11},{10,... | collective-permute-start | bytes 1769480 | tf_op jit(solution)/shard_map/ppermute | solution.py:386
  46.2 1.0 copy.19.row_slot_ref
  47.2 6.4 %shard_map.77 = (f32[512,128]{1,0:T(8,128)}, f32[512,128]{1,0:T(8,128)}, bf16[128,1024]{1,0:T(8,128)(2,1)}) custom-call(s32[50]{0:T(128)} %dynamic-slice_bitcast_fusion.info_ref, s32[1024,1]{1,0:T(8,128)} %copy.19.row_slot_ref, bf16[512,8192]{1,0:T(8,128)(2,1)} %refs_0_.7, bf16[512,8192]{1,0:T(8,128)(2,1)} %collective-permute-done.6.refs_1_, ...), custom_call_target="tpu_custom_call" | custom-call | flops 2147483648 | bytes 6553600 | tf_op jit(solution)/shard_map/pallas_call | solution.py:284
  53.6 0.1 collective-permute-start.11
  53.7 2.7 %shard_map.76.refs_2_ = bf16[2304,128]{1,0:T(8,128)(2,1)} custom-call(s32[50]{0:T(128)} %dynamic-slice_bitcast_fusion.info_ref, bf16[4,16,8192]{2,1,0:T(8,128)(2,1)} %here_ref.3, bf16[4,16,8192]{2,1,0:T(8,128)(2,1)} %collective-permute-done.there_ref, bf16[4,16,1024]{2,1,0:T(8,128)(2,1)} %up_ref.3), custom_call_target="tpu_custom_call" | custom-call | tf_op jit(solution)/shard_map/pallas_call | solution.py:119
  56.5 0.0 collective-permute-done.11.refs_1_
  56.5 0.0 copy-start.1
  56.5 0.4 collective-permute-done.8.refs_3_
  56.9 0.6 collective-permute-done.10.refs_4_
  57.5 0.2 collective-permute-done.9.refs_4_
  57.7 1.5 %collective-permute-start.13 = (bf16[2304,128]{1,0:T(8,128)(2,1)}, bf16[2304,128]{1,0:T(8,128)(2,1)}, u32[]{:S(2)}, u32[]{:S(2)}) collective-permute-start(bf16[2304,128]{1,0:T(8,128)(2,1)} %collective-permute-done.8.refs_3_), channel_id=1, source_target_pairs={{0,2},{1,3},{2,0},{3,1},{4,6},{5,7},{6,4},{7,5},{8,10},{9,11},{10,... | collective-permute-start | bytes 1769480 | tf_op jit(solution)/shard_map/ppermute | solution.py:386
  59.2 1.5 %collective-permute-start.14 = (bf16[2304,128]{1,0:T(8,128)(2,1)}, bf16[2304,128]{1,0:T(8,128)(2,1)}, u32[]{:S(2)}, u32[]{:S(2)}) collective-permute-start(bf16[2304,128]{1,0:T(8,128)(2,1)} %collective-permute-done.4.refs_2_), channel_id=1, source_target_pairs={{0,16},{1,17},{2,18},{3,19},{4,20},{5,21},{6,22},{7,23},{8,24},{9,... | collective-permute-start | bytes 1769480 | tf_op jit(solution)/shard_map/ppermute | solution.py:386
  60.7 1.2 %collective-permute-start.12 = (bf16[2304,128]{1,0:T(8,128)(2,1)}, bf16[2304,128]{1,0:T(8,128)(2,1)}, u32[]{:S(2)}, u32[]{:S(2)}) collective-permute-start(bf16[2304,128]{1,0:T(8,128)(2,1)} %shard_map.76.refs_2_), channel_id=1, source_target_pairs={{0,4},{1,5},{2,6},{3,7},{4,12},{5,13},{6,14},{7,15},{8,0},{9,1},{1... | collective-permute-start | bytes 1769480 | tf_op jit(solution)/shard_map/ppermute | solution.py:386
  61.9 6.2 %shard_map.78 = (f32[512,128]{1,0:T(8,128)}, f32[512,128]{1,0:T(8,128)}, bf16[96,1024]{1,0:T(8,128)(2,1)}) custom-call(s32[50]{0:T(128)} %dynamic-slice_bitcast_fusion.info_ref, s32[1024,1]{1,0:T(8,128)} %copy.19.row_slot_ref, bf16[512,8192]{1,0:T(8,128)(2,1)} %refs_0_.7, bf16[512,8192]{1,0:T(8,128)(2,1)} %collective-permute-done.6.refs_1_, ...), custom_call_target="tpu_custom_call" | custom-call | flops 1610612736 | bytes 5963776 | tf_op jit(solution)/shard_map/pallas_call | solution.py:284
  68.1 0.0 copy-done.1
  68.2 0.1 collective-permute-start.15
  68.2 1.8 %collective-permute-done.15.refs_3_ = bf16[96,1024]{1,0:T(8,128)(2,1)} collective-permute-done((bf16[96,1024]{1,0:T(8,128)(2,1)}, bf16[96,1024]{1,0:T(8,128)(2,1)}, u32[]{:S(2)}, u32[]{:S(2)}) %collective-permute-start.15) | collective-permute-done | bytes 196640 | tf_op jit(solution)/shard_map/ppermute | solution.py:386
  70.0 2.6 %collective-permute-done.13.refs_5_ = bf16[2304,128]{1,0:T(8,128)(2,1)} collective-permute-done((bf16[2304,128]{1,0:T(8,128)(2,1)}, bf16[2304,128]{1,0:T(8,128)(2,1)}, u32[]{:S(2)}, u32[]{:S(2)}) %collective-permute-start.13) | collective-permute-done | bytes 589856 | tf_op jit(solution)/shard_map/ppermute | solution.py:386
  72.6 0.3 collective-permute-done.14.refs_7_
  72.9 2.2 %collective-permute-done.12.refs_6_ = bf16[2304,128]{1,0:T(8,128)(2,1)} collective-permute-done((bf16[2304,128]{1,0:T(8,128)(2,1)}, bf16[2304,128]{1,0:T(8,128)(2,1)}, u32[]{:S(2)}, u32[]{:S(2)}) %collective-permute-start.12) | collective-permute-done | bytes 589856 | tf_op jit(solution)/shard_map/ppermute | solution.py:386
  75.0 1.7 %collective-permute-start.16 = (bf16[2304,128]{1,0:T(8,128)(2,1)}, bf16[2304,128]{1,0:T(8,128)(2,1)}, u32[]{:S(2)}, u32[]{:S(2)}) collective-permute-start(bf16[2304,128]{1,0:T(8,128)(2,1)} %shard_map.76.refs_2_), channel_id=1, source_target_pairs={{0,8},{1,9},{2,10},{3,11},{4,0},{5,1},{6,2},{7,3},{8,12},{9,13},{1... | collective-permute-start | bytes 1769480 | tf_op jit(solution)/shard_map/ppermute | solution.py:386
  76.7 2.3 %collective-permute-start.17 = (bf16[2304,128]{1,0:T(8,128)(2,1)}, bf16[2304,128]{1,0:T(8,128)(2,1)}, u32[]{:S(2)}, u32[]{:S(2)}) collective-permute-start(bf16[2304,128]{1,0:T(8,128)(2,1)} %collective-permute-done.10.refs_4_), channel_id=1, source_target_pairs={{0,2},{1,3},{2,0},{3,1},{4,6},{5,7},{6,4},{7,5},{8,10},{9,11},{10,... | collective-permute-start | bytes 1769480 | tf_op jit(solution)/shard_map/ppermute | solution.py:386
  79.0 0.5 collective-permute-start.18
  79.6 10.2 %shard_map.79 = (f32[512,128]{1,0:T(8,128)}, f32[512,128]{1,0:T(8,128)}, bf16[192,1024]{1,0:T(8,128)(2,1)}) custom-call(s32[50]{0:T(128)} %dynamic-slice_bitcast_fusion.info_ref, s32[1024,1]{1,0:T(8,128)} %copy.19.row_slot_ref, bf16[512,8192]{1,0:T(8,128)(2,1)} %refs_0_.7, bf16[512,8192]{1,0:T(8,128)(2,1)} %collective-permute-done.6.refs_1_, ...), custom_call_target="tpu_custom_call" | custom-call | flops 3221225472 | bytes 11927552 | tf_op jit(solution)/shard_map/pallas_call | solution.py:284
  89.8 0.1 collective-permute-start.20
  89.8 0.0 collective-permute-done.16.refs_2_
  89.8 0.0 collective-permute-done.17.refs_3_
  89.9 1.5 %collective-permute-done.18.refs_4_ = bf16[2304,128]{1,0:T(8,128)(2,1)} collective-permute-done((bf16[2304,128]{1,0:T(8,128)(2,1)}, bf16[2304,128]{1,0:T(8,128)(2,1)}, u32[]{:S(2)}, u32[]{:S(2)}) %collective-permute-start.18) | collective-permute-done | bytes 589856 | tf_op jit(solution)/shard_map/ppermute | solution.py:386
  91.3 6.2 %shard_map.80 = (f32[512,128]{1,0:T(8,128)}, f32[512,128]{1,0:T(8,128)}, bf16[96,1024]{1,0:T(8,128)(2,1)}) custom-call(s32[50]{0:T(128)} %dynamic-slice_bitcast_fusion.info_ref, s32[1024,1]{1,0:T(8,128)} %copy.19.row_slot_ref, bf16[512,8192]{1,0:T(8,128)(2,1)} %refs_0_.7, bf16[512,8192]{1,0:T(8,128)(2,1)} %collective-permute-done.6.refs_1_, ...), custom_call_target="tpu_custom_call" | custom-call | flops 1610612736 | bytes 5963776 | tf_op jit(solution)/shard_map/pallas_call | solution.py:284
  97.5 0.1 collective-permute-start.19
  97.6 0.5 collective-permute-start.21
  98.1 0.0 collective-permute-done.20.refs_5_
  98.1 0.0 copy-start
  98.1 1.6 %collective-permute-done.21.refs_7_ = bf16[96,1024]{1,0:T(8,128)(2,1)} collective-permute-done((bf16[96,1024]{1,0:T(8,128)(2,1)}, bf16[96,1024]{1,0:T(8,128)(2,1)}, u32[]{:S(2)}, u32[]{:S(2)}) %collective-permute-start.21) | collective-permute-done | bytes 196640 | tf_op jit(solution)/shard_map/ppermute | solution.py:386
  99.7 0.0 collective-permute-done.19.theirs_ref
  99.7 0.0 copy-done
  99.7 6.2 %shard_map.81 = bf16[512,1024]{1,0:T(8,128)(2,1)} custom-call(s32[50]{0:T(128)} %dynamic-slice_bitcast_fusion.info_ref, s32[1024,1]{1,0:T(8,128)} %copy.19.row_slot_ref, f32[512,128]{1,0:T(8,128)} %get-tuple-element.106.mine_ref, f32[512,128]{1,0:T(8,128)} %collective-permute-done.19.theirs_ref, f32[512,1024]{1,0:T(8,128)} %shard_map.75.total_ref, ...), custom_call_target="tpu_custom_call" | custom-call | flops 2147483648 | bytes 5242880 | tf_op jit(solution)/shard_map/pallas_call | solution.py:345
  (1 shorter events, 0.0 us)
Async XLA Ops:
  0.0 3.1 %collective-permute-start = (bf16[4,16,8192]{2,1,0:T(8,128)(2,1)}, bf16[4,16,8192]{2,1,0:T(8,128)(2,1)}, u32[]{:S(2)}, u32[]{:S(2)}) collective-permute-start(bf16[4,16,8192]{2,1,0:T(8,128)(2,1)} %here_ref.3), channel_id=1, source_target_pairs={{0,1},{1,0},{2,3},{3,2},{4,5},{5,4},{6,7},{7,6},{8,9},{9,8},{10,11... | collective-permute-start | bytes 3145736 | tf_op jit(solution)/shard_map/ppermute | solution.py:386
  3.1 39.6 %collective-permute-start.6 = (bf16[512,8192]{1,0:T(8,128)(2,1)}, bf16[512,8192]{1,0:T(8,128)(2,1)}, u32[]{:S(2)}, u32[]{:S(2)}) collective-permute-start(bf16[512,8192]{1,0:T(8,128)(2,1)} %refs_0_.7), channel_id=1, source_target_pairs={{0,1},{1,0},{2,3},{3,2},{4,5},{5,4},{6,7},{7,6},{8,9},{9,8},{10,11... | collective-permute-start | bytes 25165832 | tf_op jit(solution)/shard_map/ppermute | solution.py:386
  6.2 16.9 %collective-permute-start.2 = (bf16[2304,128]{1,0:T(8,128)(2,1)}, bf16[2304,128]{1,0:T(8,128)(2,1)}, u32[]{:S(2)}, u32[]{:S(2)}) collective-permute-start(bf16[2304,128]{1,0:T(8,128)(2,1)} %shard_map.73.refs_2_), channel_id=1, source_target_pairs={{0,2},{1,3},{2,0},{3,1},{4,6},{5,7},{6,4},{7,5},{8,10},{9,11},{10,... | collective-permute-start | bytes 1769480 | tf_op jit(solution)/shard_map/ppermute | solution.py:386
  8.9 16.5 %collective-permute-start.1 = (bf16[2304,128]{1,0:T(8,128)(2,1)}, bf16[2304,128]{1,0:T(8,128)(2,1)}, u32[]{:S(2)}, u32[]{:S(2)}) collective-permute-start(bf16[2304,128]{1,0:T(8,128)(2,1)} %shard_map.73.refs_2_), channel_id=1, source_target_pairs={{0,4},{1,5},{2,6},{3,7},{4,12},{5,13},{6,14},{7,15},{8,0},{9,1},{1... | collective-permute-start | bytes 1769480 | tf_op jit(solution)/shard_map/ppermute | solution.py:386
  25.5 14.8 %collective-permute-start.5 = (bf16[2304,128]{1,0:T(8,128)(2,1)}, bf16[2304,128]{1,0:T(8,128)(2,1)}, u32[]{:S(2)}, u32[]{:S(2)}) collective-permute-start(bf16[2304,128]{1,0:T(8,128)(2,1)} %collective-permute-done.2.refs_4_), channel_id=1, source_target_pairs={{0,16},{1,17},{2,18},{3,19},{4,20},{5,21},{6,22},{7,23},{8,24},{9,... | collective-permute-start | bytes 1769480 | tf_op jit(solution)/shard_map/ppermute | solution.py:386
  27.0 14.5 %collective-permute-start.4 = (bf16[2304,128]{1,0:T(8,128)(2,1)}, bf16[2304,128]{1,0:T(8,128)(2,1)}, u32[]{:S(2)}, u32[]{:S(2)}) collective-permute-start(bf16[2304,128]{1,0:T(8,128)(2,1)} %collective-permute-done.1.refs_3_), channel_id=1, source_target_pairs={{0,2},{1,3},{2,0},{3,1},{4,6},{5,7},{6,4},{7,5},{8,10},{9,11},{10,... | collective-permute-start | bytes 1769480 | tf_op jit(solution)/shard_map/ppermute | solution.py:386
  27.5 15.1 %collective-permute-start.3 = (bf16[2304,128]{1,0:T(8,128)(2,1)}, bf16[2304,128]{1,0:T(8,128)(2,1)}, u32[]{:S(2)}, u32[]{:S(2)}) collective-permute-start(bf16[2304,128]{1,0:T(8,128)(2,1)} %collective-permute-done.1.refs_3_), channel_id=1, source_target_pairs={{0,4},{1,5},{2,6},{3,7},{4,12},{5,13},{6,14},{7,15},{8,0},{9,1},{1... | collective-permute-start | bytes 1769480 | tf_op jit(solution)/shard_map/ppermute | solution.py:386
  38.2 1.2 %collective-permute-start.7 = (s32[512]{0:T(512)S(1)}, s32[512]{0:T(512)S(1)}, u32[]{:S(2)}, u32[]{:S(2)}) collective-permute-start(s32[512]{0:T(512)S(1)} %select_reduce_fusion), channel_id=1, source_target_pairs={{0,1},{1,0},{2,3},{3,2},{4,5},{5,4},{6,7},{7,6},{8,9},{9,8},{10,11... | collective-permute-start | bytes 6152 | tf_op jit(solution)/shard_map/ppermute | solution.py:386
  42.7 14.2 %collective-permute-start.8 = (bf16[2304,128]{1,0:T(8,128)(2,1)}, bf16[2304,128]{1,0:T(8,128)(2,1)}, u32[]{:S(2)}, u32[]{:S(2)}) collective-permute-start(bf16[2304,128]{1,0:T(8,128)(2,1)} %shard_map.73.refs_2_), channel_id=1, source_target_pairs={{0,8},{1,9},{2,10},{3,11},{4,0},{5,1},{6,2},{7,3},{8,12},{9,13},{1... | collective-permute-start | bytes 1769480 | tf_op jit(solution)/shard_map/ppermute | solution.py:386
  44.2 13.3 %collective-permute-start.10 = (bf16[2304,128]{1,0:T(8,128)(2,1)}, bf16[2304,128]{1,0:T(8,128)(2,1)}, u32[]{:S(2)}, u32[]{:S(2)}) collective-permute-start(bf16[2304,128]{1,0:T(8,128)(2,1)} %collective-permute-done.3.refs_5_), channel_id=1, source_target_pairs={{0,16},{1,17},{2,18},{3,19},{4,20},{5,21},{6,22},{7,23},{8,24},{9,... | collective-permute-start | bytes 1769480 | tf_op jit(solution)/shard_map/ppermute | solution.py:386
  44.7 13.0 %collective-permute-start.9 = (bf16[2304,128]{1,0:T(8,128)(2,1)}, bf16[2304,128]{1,0:T(8,128)(2,1)}, u32[]{:S(2)}, u32[]{:S(2)}) collective-permute-start(bf16[2304,128]{1,0:T(8,128)(2,1)} %collective-permute-done.3.refs_5_), channel_id=1, source_target_pairs={{0,2},{1,3},{2,0},{3,1},{4,6},{5,7},{6,4},{7,5},{8,10},{9,11},{10,... | collective-permute-start | bytes 1769480 | tf_op jit(solution)/shard_map/ppermute | solution.py:386
  53.6 2.8 %collective-permute-start.11 = (bf16[128,1024]{1,0:T(8,128)(2,1)}, bf16[128,1024]{1,0:T(8,128)(2,1)S(1)}, u32[]{:S(2)}, u32[]{:S(2)}) collective-permute-start(bf16[128,1024]{1,0:T(8,128)(2,1)} %get-tuple-element.80.refs_0_), channel_id=1, source_target_pairs={{0,1},{1,0},{2,3},{3,2},{4,5},{5,4},{6,7},{7,6},{8,9},{9,8},{10,11... | collective-permute-start | bytes 786440 | tf_op jit(solution)/shard_map/ppermute | solution.py:386
  56.5 11.7 %copy-start.1 = (bf16[128,1024]{1,0:T(8,128)(2,1)}, bf16[128,1024]{1,0:T(8,128)(2,1)S(1)}, u32[]{:S(2)}) copy-start(bf16[128,1024]{1,0:T(8,128)(2,1)S(1)} %collective-permute-done.11.refs_1_) | copy-start | bytes 786436
  57.7 14.9 %collective-permute-start.13 = (bf16[2304,128]{1,0:T(8,128)(2,1)}, bf16[2304,128]{1,0:T(8,128)(2,1)}, u32[]{:S(2)}, u32[]{:S(2)}) collective-permute-start(bf16[2304,128]{1,0:T(8,128)(2,1)} %collective-permute-done.8.refs_3_), channel_id=1, source_target_pairs={{0,2},{1,3},{2,0},{3,1},{4,6},{5,7},{6,4},{7,5},{8,10},{9,11},{10,... | collective-permute-start | bytes 1769480 | tf_op jit(solution)/shard_map/ppermute | solution.py:386
  59.2 13.6 %collective-permute-start.14 = (bf16[2304,128]{1,0:T(8,128)(2,1)}, bf16[2304,128]{1,0:T(8,128)(2,1)}, u32[]{:S(2)}, u32[]{:S(2)}) collective-permute-start(bf16[2304,128]{1,0:T(8,128)(2,1)} %collective-permute-done.4.refs_2_), channel_id=1, source_target_pairs={{0,16},{1,17},{2,18},{3,19},{4,20},{5,21},{6,22},{7,23},{8,24},{9,... | collective-permute-start | bytes 1769480 | tf_op jit(solution)/shard_map/ppermute | solution.py:386
  60.7 14.3 %collective-permute-start.12 = (bf16[2304,128]{1,0:T(8,128)(2,1)}, bf16[2304,128]{1,0:T(8,128)(2,1)}, u32[]{:S(2)}, u32[]{:S(2)}) collective-permute-start(bf16[2304,128]{1,0:T(8,128)(2,1)} %shard_map.76.refs_2_), channel_id=1, source_target_pairs={{0,4},{1,5},{2,6},{3,7},{4,12},{5,13},{6,14},{7,15},{8,0},{9,1},{1... | collective-permute-start | bytes 1769480 | tf_op jit(solution)/shard_map/ppermute | solution.py:386
  68.2 1.8 %collective-permute-start.15 = (bf16[96,1024]{1,0:T(8,128)(2,1)}, bf16[96,1024]{1,0:T(8,128)(2,1)}, u32[]{:S(2)}, u32[]{:S(2)}) collective-permute-start(bf16[96,1024]{1,0:T(8,128)(2,1)} %get-tuple-element.90.refs_2_), channel_id=1, source_target_pairs={{0,1},{1,0},{2,3},{3,2},{4,5},{5,4},{6,7},{7,6},{8,9},{9,8},{10,11... | collective-permute-start | bytes 589832 | tf_op jit(solution)/shard_map/ppermute | solution.py:386
  75.0 14.8 %collective-permute-start.16 = (bf16[2304,128]{1,0:T(8,128)(2,1)}, bf16[2304,128]{1,0:T(8,128)(2,1)}, u32[]{:S(2)}, u32[]{:S(2)}) collective-permute-start(bf16[2304,128]{1,0:T(8,128)(2,1)} %shard_map.76.refs_2_), channel_id=1, source_target_pairs={{0,8},{1,9},{2,10},{3,11},{4,0},{5,1},{6,2},{7,3},{8,12},{9,13},{1... | collective-permute-start | bytes 1769480 | tf_op jit(solution)/shard_map/ppermute | solution.py:386
  76.7 13.1 %collective-permute-start.17 = (bf16[2304,128]{1,0:T(8,128)(2,1)}, bf16[2304,128]{1,0:T(8,128)(2,1)}, u32[]{:S(2)}, u32[]{:S(2)}) collective-permute-start(bf16[2304,128]{1,0:T(8,128)(2,1)} %collective-permute-done.10.refs_4_), channel_id=1, source_target_pairs={{0,2},{1,3},{2,0},{3,1},{4,6},{5,7},{6,4},{7,5},{8,10},{9,11},{10,... | collective-permute-start | bytes 1769480 | tf_op jit(solution)/shard_map/ppermute | solution.py:386
  79.0 12.3 %collective-permute-start.18 = (bf16[2304,128]{1,0:T(8,128)(2,1)}, bf16[2304,128]{1,0:T(8,128)(2,1)}, u32[]{:S(2)}, u32[]{:S(2)}) collective-permute-start(bf16[2304,128]{1,0:T(8,128)(2,1)} %collective-permute-done.13.refs_5_), channel_id=1, source_target_pairs={{0,16},{1,17},{2,18},{3,19},{4,20},{5,21},{6,22},{7,23},{8,24},{9,... | collective-permute-start | bytes 1769480 | tf_op jit(solution)/shard_map/ppermute | solution.py:386
  89.8 8.3 %collective-permute-start.20 = (bf16[192,1024]{1,0:T(8,128)(2,1)}, bf16[192,1024]{1,0:T(8,128)(2,1)S(1)}, u32[]{:S(2)}, u32[]{:S(2)}) collective-permute-start(bf16[192,1024]{1,0:T(8,128)(2,1)} %get-tuple-element.111.refs_4_), channel_id=1, source_target_pairs={{0,1},{1,0},{2,3},{3,2},{4,5},{5,4},{6,7},{7,6},{8,9},{9,8},{10,11... | collective-permute-start | bytes 1179656 | tf_op jit(solution)/shard_map/ppermute | solution.py:386
  97.5 2.2 %collective-permute-start.19 = (f32[512,128]{1,0:T(8,128)}, f32[512,128]{1,0:T(8,128)}, u32[]{:S(2)}, u32[]{:S(2)}) collective-permute-start(f32[512,128]{1,0:T(8,128)} %get-tuple-element.107), channel_id=1, source_target_pairs={{0,1},{1,0},{2,3},{3,2},{4,5},{5,4},{6,7},{7,6},{8,9},{9,8},{10,11... | collective-permute-start | bytes 786440 | tf_op jit(solution)/shard_map/ppermute | solution.py:386
  97.6 2.1 %collective-permute-start.21 = (bf16[96,1024]{1,0:T(8,128)(2,1)}, bf16[96,1024]{1,0:T(8,128)(2,1)}, u32[]{:S(2)}, u32[]{:S(2)}) collective-permute-start(bf16[96,1024]{1,0:T(8,128)(2,1)} %get-tuple-element.112.refs_6_), channel_id=1, source_target_pairs={{0,1},{1,0},{2,3},{3,2},{4,5},{5,4},{6,7},{7,6},{8,9},{9,8},{10,11... | collective-permute-start | bytes 589832 | tf_op jit(solution)/shard_map/ppermute | solution.py:386
  98.1 1.7 %copy-start = (bf16[192,1024]{1,0:T(8,128)(2,1)}, bf16[192,1024]{1,0:T(8,128)(2,1)S(1)}, u32[]{:S(2)}) copy-start(bf16[192,1024]{1,0:T(8,128)(2,1)S(1)} %collective-permute-done.20.refs_5_) | copy-start | bytes 1179652

commit v21 on v17

--- a/solution.py
+++ b/solution.py
@@ -430,7 +430,7 @@
         )
 
     front = piece(0)
-    cuts = (0, depth // 2, depth)
+    cuts = (0, 5 * DEPTH_TILE, depth)
 
     def base(number, before, *others):
         low, high = cuts[number : number + 2]

time: 101 us -> 101 us (level)
  no operation moved by 1% of the time
where the time goes in v21:
time: 101 us; the launch traced here: 100 us
  Pallas kernels  60.5 us (60%)
  starting transfers between devices  20 us (20%)
  waiting for transfers between devices  16.5 us (16%)
  local copies, waits for them, and re-layouts  2.27 us (2%)
    pallas_call x4, Pallas kernels, absorb(): pl.pallas_call(functools.partial(absorb_kernel, sizes, start, sides, more...  29 us
    ppermute x22, starting transfers between devices, permuted(): return lax.ppermute(array, axes, pairs)  20 us
    pallas_call x2, Pallas kernels, base_part(): pl.pallas_call(functools.partial(base_kernel, steps), out_shape=result, g...  19.8 us
    ppermute x22, waiting for transfers between devices, permuted(): return lax.ppermute(array, axes, pairs)  16.5 us
    pallas_call x1, Pallas kernels, finish(): pl.pallas_call(functools.partial(finish_kernel, len(ups)), out_shape=jax....  6.19 us
    pallas_call x2, Pallas kernels, assemble(): pl.pallas_call(functools.partial(assemble_kernel, back), out_shape=jax.Sh...  5.5 us
  transfers between devices with their start and end apart: 22, of which 13 were waited for; matrix products, arithmetic and copies ran while one was open for 3% of the time, Pallas kernels for 54%

profile of v21, /device:TPU:0, one launch (start us, length us, event | category | flops | bytes accessed | tf_op | source)
XLA Modules:
  0.0 100.3 jit_solution(15409758501197276016)
XLA Ops:
  0.0 0.5 collective-permute-start
  0.5 1.2 %dynamic-slice_bitcast_fusion.info_ref = s32[50]{0:T(128)} fusion(s32[32,50]{1,0:T(8,128)} %constant.20.clone, s32[]{:T(128)S(6)} %select_n.8), kind=kLoop, calls=%fused_computation.3 | loop fusion | bytes 404 | tf_op jit(solution)/shard_map/jit(dynamic_index_in_dim)/squeeze | solution.py:413
  1.7 0.8 select_reduce_fusion
  2.5 0.6 collective-permute-done.there_ref
  3.1 0.4 collective-permute-start.7
  3.5 2.8 %shard_map.73.refs_2_ = bf16[2304,128]{1,0:T(8,128)(2,1)} custom-call(s32[50]{0:T(128)} %dynamic-slice_bitcast_fusion.info_ref, bf16[4,16,8192]{2,1,0:T(8,128)(2,1)} %here_ref.3, bf16[4,16,8192]{2,1,0:T(8,128)(2,1)} %collective-permute-done.there_ref, bf16[4,16,1024]{2,1,0:T(8,128)(2,1)} %up_ref.3), custom_call_target="tpu_custom_call" | custom-call | tf_op jit(solution)/shard_map/pallas_call | solution.py:119
  6.2 2.8 %collective-permute-start.1 = (bf16[2304,128]{1,0:T(8,128)(2,1)}, bf16[2304,128]{1,0:T(8,128)(2,1)}, u32[]{:S(2)}, u32[]{:S(2)}) collective-permute-start(bf16[2304,128]{1,0:T(8,128)(2,1)} %shard_map.73.refs_2_), channel_id=1, source_target_pairs={{0,4},{1,5},{2,6},{3,7},{4,12},{5,13},{6,14},{7,15},{8,0},{9,1},{1... | collective-permute-start | bytes 1769480 | tf_op jit(solution)/shard_map/ppermute | solution.py:386
  9.0 1.5 %collective-permute-start.2 = (bf16[2304,128]{1,0:T(8,128)(2,1)}, bf16[2304,128]{1,0:T(8,128)(2,1)}, u32[]{:S(2)}, u32[]{:S(2)}) collective-permute-start(bf16[2304,128]{1,0:T(8,128)(2,1)} %shard_map.73.refs_2_), channel_id=1, source_target_pairs={{0,2},{1,3},{2,0},{3,1},{4,6},{5,7},{6,4},{7,5},{8,10},{9,11},{10,... | collective-permute-start | bytes 1769480 | tf_op jit(solution)/shard_map/ppermute | solution.py:386
  10.5 0.0 collective-permute-start.3
  10.5 11.4 %shard_map.74.refs_0_ = f32[512,1024]{1,0:T(8,128)} custom-call(bf16[512,8192]{1,0:T(8,128)(2,1)} %refs_0_.7, bf16[8192,1024]{1,0:T(8,128)(2,1)} %weight_ref.3), custom_call_target="tpu_custom_call" | custom-call | flops 5368709120 | bytes 17825792 | tf_op jit(solution)/shard_map/pallas_call | solution.py:163
  21.9 0.0 collective-permute-done.3
  21.9 2.2 %collective-permute-done.1.refs_3_ = bf16[2304,128]{1,0:T(8,128)(2,1)} collective-permute-done((bf16[2304,128]{1,0:T(8,128)(2,1)}, bf16[2304,128]{1,0:T(8,128)(2,1)}, u32[]{:S(2)}, u32[]{:S(2)}) %collective-permute-start.1) | collective-permute-done | bytes 589856 | tf_op jit(solution)/shard_map/ppermute | solution.py:386
  24.2 0.4 collective-permute-done.2.refs_4_
  24.6 2.6 %collective-permute-start.4 = (bf16[2304,128]{1,0:T(8,128)(2,1)}, bf16[2304,128]{1,0:T(8,128)(2,1)}, u32[]{:S(2)}, u32[]{:S(2)}) collective-permute-start(bf16[2304,128]{1,0:T(8,128)(2,1)} %collective-permute-done.1.refs_3_), channel_id=1, source_target_pairs={{0,4},{1,5},{2,6},{3,7},{4,12},{5,13},{6,14},{7,15},{8,0},{9,1},{1... | collective-permute-start | bytes 1769480 | tf_op jit(solution)/shard_map/ppermute | solution.py:386
  27.2 1.5 %collective-permute-start.5 = (bf16[2304,128]{1,0:T(8,128)(2,1)}, bf16[2304,128]{1,0:T(8,128)(2,1)}, u32[]{:S(2)}, u32[]{:S(2)}) collective-permute-start(bf16[2304,128]{1,0:T(8,128)(2,1)} %collective-permute-done.1.refs_3_), channel_id=1, source_target_pairs={{0,2},{1,3},{2,0},{3,1},{4,6},{5,7},{6,4},{7,5},{8,10},{9,11},{10,... | collective-permute-start | bytes 1769480 | tf_op jit(solution)/shard_map/ppermute | solution.py:386
  28.7 1.5 %collective-permute-start.6 = (bf16[2304,128]{1,0:T(8,128)(2,1)}, bf16[2304,128]{1,0:T(8,128)(2,1)}, u32[]{:S(2)}, u32[]{:S(2)}) collective-permute-start(bf16[2304,128]{1,0:T(8,128)(2,1)} %collective-permute-done.2.refs_4_), channel_id=1, source_target_pairs={{0,16},{1,17},{2,18},{3,19},{4,20},{5,21},{6,22},{7,23},{8,24},{9,... | collective-permute-start | bytes 1769480 | tf_op jit(solution)/shard_map/ppermute | solution.py:386
  30.2 8.4 %shard_map.75.total_ref = f32[512,1024]{1,0:T(8,128)} custom-call(bf16[512,8192]{1,0:T(8,128)(2,1)} %refs_0_.7, bf16[8192,1024]{1,0:T(8,128)(2,1)} %weight_ref.3, f32[512,1024]{1,0:T(8,128)} %shard_map.74.refs_0_), custom_call_target="tpu_custom_call" | custom-call | flops 3221225472 | bytes 11534336 | tf_op jit(solution)/shard_map/pallas_call | solution.py:163
  38.6 1.8 %collective-permute-done.4.refs_5_ = bf16[2304,128]{1,0:T(8,128)(2,1)} collective-permute-done((bf16[2304,128]{1,0:T(8,128)(2,1)}, bf16[2304,128]{1,0:T(8,128)(2,1)}, u32[]{:S(2)}, u32[]{:S(2)}) %collective-permute-start.4) | collective-permute-done | bytes 589856 | tf_op jit(solution)/shard_map/ppermute | solution.py:386
  40.4 1.3 %collective-permute-done.5.refs_2_ = bf16[2304,128]{1,0:T(8,128)(2,1)} collective-permute-done((bf16[2304,128]{1,0:T(8,128)(2,1)}, bf16[2304,128]{1,0:T(8,128)(2,1)}, u32[]{:S(2)}, u32[]{:S(2)}) %collective-permute-start.5) | collective-permute-done | bytes 589856 | tf_op jit(solution)/shard_map/ppermute | solution.py:386
  41.7 1.2 %collective-permute-done.6.refs_3_ = bf16[2304,128]{1,0:T(8,128)(2,1)} collective-permute-done((bf16[2304,128]{1,0:T(8,128)(2,1)}, bf16[2304,128]{1,0:T(8,128)(2,1)}, u32[]{:S(2)}, u32[]{:S(2)}) %collective-permute-start.6) | collective-permute-done | bytes 589856 | tf_op jit(solution)/shard_map/ppermute | solution.py:386
  42.9 0.0 collective-permute-done.7.refs_1_
  42.9 1.5 %collective-permute-start.10 = (bf16[2304,128]{1,0:T(8,128)(2,1)}, bf16[2304,128]{1,0:T(8,128)(2,1)}, u32[]{:S(2)}, u32[]{:S(2)}) collective-permute-start(bf16[2304,128]{1,0:T(8,128)(2,1)} %collective-permute-done.4.refs_5_), channel_id=1, source_target_pairs={{0,16},{1,17},{2,18},{3,19},{4,20},{5,21},{6,22},{7,23},{8,24},{9,... | collective-permute-start | bytes 1769480 | tf_op jit(solution)/shard_map/ppermute | solution.py:386
  44.5 0.3 collective-permute-start.8
  44.8 0.5 collective-permute-start.9
  45.3 1.0 %copy.19.row_slot_ref = s32[1024,1]{1,0:T(8,128)} copy(s32[1024,1]{0,1:T(1,128)S(1)} %pad_add_fusion) | data formatting | bytes 8192 | tf_op jit(solution)/shard_map/optimization_barrier | solution.py:418
  46.4 2.7 %shard_map.76.refs_2_ = bf16[2304,128]{1,0:T(8,128)(2,1)} custom-call(s32[50]{0:T(128)} %dynamic-slice_bitcast_fusion.info_ref, bf16[4,16,8192]{2,1,0:T(8,128)(2,1)} %here_ref.3, bf16[4,16,8192]{2,1,0:T(8,128)(2,1)} %collective-permute-done.there_ref, bf16[4,16,1024]{2,1,0:T(8,128)(2,1)} %up_ref.3), custom_call_target="tpu_custom_call" | custom-call | tf_op jit(solution)/shard_map/pallas_call | solution.py:119
  49.1 6.4 %shard_map.77 = (f32[512,128]{1,0:T(8,128)}, f32[512,128]{1,0:T(8,128)}, bf16[128,1024]{1,0:T(8,128)(2,1)}) custom-call(s32[50]{0:T(128)} %dynamic-slice_bitcast_fusion.info_ref, s32[1024,1]{1,0:T(8,128)} %copy.19.row_slot_ref, bf16[512,8192]{1,0:T(8,128)(2,1)} %refs_0_.7, bf16[512,8192]{1,0:T(8,128)(2,1)} %collective-permute-done.7.refs_1_, ...), custom_call_target="tpu_custom_call" | custom-call | flops 2147483648 | bytes 6553600 | tf_op jit(solution)/shard_map/pallas_call | solution.py:284
  55.5 0.7 collective-permute-done.10.refs_4_
  56.3 1.3 %collective-permute-done.8.refs_3_ = bf16[2304,128]{1,0:T(8,128)(2,1)} collective-permute-done((bf16[2304,128]{1,0:T(8,128)(2,1)}, bf16[2304,128]{1,0:T(8,128)(2,1)}, u32[]{:S(2)}, u32[]{:S(2)}) %collective-permute-start.8) | collective-permute-done | bytes 589856 | tf_op jit(solution)/shard_map/ppermute | solution.py:386
  57.6 0.0 collective-permute-done.9.refs_4_
  57.6 3.1 %collective-permute-start.11 = (bf16[2304,128]{1,0:T(8,128)(2,1)}, bf16[2304,128]{1,0:T(8,128)(2,1)}, u32[]{:S(2)}, u32[]{:S(2)}) collective-permute-start(bf16[2304,128]{1,0:T(8,128)(2,1)} %shard_map.76.refs_2_), channel_id=1, source_target_pairs={{0,4},{1,5},{2,6},{3,7},{4,12},{5,13},{6,14},{7,15},{8,0},{9,1},{1... | collective-permute-start | bytes 1769480 | tf_op jit(solution)/shard_map/ppermute | solution.py:386
  60.6 0.2 collective-permute-start.12
  60.8 0.5 collective-permute-start.13
  61.4 0.0 collective-permute-start.14
  61.4 6.2 %shard_map.78 = (f32[512,128]{1,0:T(8,128)}, f32[512,128]{1,0:T(8,128)}, bf16[96,1024]{1,0:T(8,128)(2,1)}) custom-call(s32[50]{0:T(128)} %dynamic-slice_bitcast_fusion.info_ref, s32[1024,1]{1,0:T(8,128)} %copy.19.row_slot_ref, bf16[512,8192]{1,0:T(8,128)(2,1)} %refs_0_.7, bf16[512,8192]{1,0:T(8,128)(2,1)} %collective-permute-done.7.refs_1_, ...), custom_call_target="tpu_custom_call" | custom-call | flops 1610612736 | bytes 5963776 | tf_op jit(solution)/shard_map/pallas_call | solution.py:284
  67.6 0.0 collective-permute-done.14.refs_1_
  67.6 0.0 copy-start.1
  67.6 4.7 %collective-permute-done.11.refs_6_ = bf16[2304,128]{1,0:T(8,128)(2,1)} collective-permute-done((bf16[2304,128]{1,0:T(8,128)(2,1)}, bf16[2304,128]{1,0:T(8,128)(2,1)}, u32[]{:S(2)}, u32[]{:S(2)}) %collective-permute-start.11) | collective-permute-done | bytes 589856 | tf_op jit(solution)/shard_map/ppermute | solution.py:386
  72.3 0.1 collective-permute-done.12.refs_5_
  72.4 0.3 collective-permute-done.13.refs_7_
  72.7 1.1 %collective-permute-start.15 = (bf16[2304,128]{1,0:T(8,128)(2,1)}, bf16[2304,128]{1,0:T(8,128)(2,1)}, u32[]{:S(2)}, u32[]{:S(2)}) collective-permute-start(bf16[2304,128]{1,0:T(8,128)(2,1)} %shard_map.76.refs_2_), channel_id=1, source_target_pairs={{0,8},{1,9},{2,10},{3,11},{4,0},{5,1},{6,2},{7,3},{8,12},{9,13},{1... | collective-permute-start | bytes 1769480 | tf_op jit(solution)/shard_map/ppermute | solution.py:386
  73.7 0.4 collective-permute-start.16
  74.1 0.5 collective-permute-start.17
  74.7 0.0 collective-permute-start.18
  74.7 10.2 %shard_map.79 = (f32[512,128]{1,0:T(8,128)}, f32[512,128]{1,0:T(8,128)}, bf16[192,1024]{1,0:T(8,128)(2,1)}) custom-call(s32[50]{0:T(128)} %dynamic-slice_bitcast_fusion.info_ref, s32[1024,1]{1,0:T(8,128)} %copy.19.row_slot_ref, bf16[512,8192]{1,0:T(8,128)(2,1)} %refs_0_.7, bf16[512,8192]{1,0:T(8,128)(2,1)} %collective-permute-done.7.refs_1_, ...), custom_call_target="tpu_custom_call" | custom-call | flops 3221225472 | bytes 11927552 | tf_op jit(solution)/shard_map/pallas_call | solution.py:284
  84.9 0.0 copy-done.1
  84.9 0.6 collective-permute-start.20
  85.4 0.0 collective-permute-done.18.refs_3_
  85.4 0.0 collective-permute-done.15.refs_2_
  85.5 0.0 collective-permute-done.16.refs_3_
  85.5 0.1 collective-permute-done.17.refs_4_
  85.6 6.2 %shard_map.80 = (f32[512,128]{1,0:T(8,128)}, f32[512,128]{1,0:T(8,128)}, bf16[96,1024]{1,0:T(8,128)(2,1)}) custom-call(s32[50]{0:T(128)} %dynamic-slice_bitcast_fusion.info_ref, s32[1024,1]{1,0:T(8,128)} %copy.19.row_slot_ref, bf16[512,8192]{1,0:T(8,128)(2,1)} %refs_0_.7, bf16[512,8192]{1,0:T(8,128)(2,1)} %collective-permute-done.7.refs_1_, ...), custom_call_target="tpu_custom_call" | custom-call | flops 1610612736 | bytes 5963776 | tf_op jit(solution)/shard_map/pallas_call | solution.py:284
  91.7 0.1 collective-permute-start.19
  91.8 0.5 collective-permute-start.21
  92.3 0.0 collective-permute-done.20.refs_5_
  92.3 0.0 copy-start
  92.3 1.6 %collective-permute-done.21.refs_7_ = bf16[96,1024]{1,0:T(8,128)(2,1)} collective-permute-done((bf16[96,1024]{1,0:T(8,128)(2,1)}, bf16[96,1024]{1,0:T(8,128)(2,1)}, u32[]{:S(2)}, u32[]{:S(2)}) %collective-permute-start.21) | collective-permute-done | bytes 196640 | tf_op jit(solution)/shard_map/ppermute | solution.py:386
  94.0 0.0 collective-permute-done.19.theirs_ref
  94.0 0.0 copy-done
  94.0 6.2 %shard_map.81 = bf16[512,1024]{1,0:T(8,128)(2,1)} custom-call(s32[50]{0:T(128)} %dynamic-slice_bitcast_fusion.info_ref, s32[1024,1]{1,0:T(8,128)} %copy.19.row_slot_ref, f32[512,128]{1,0:T(8,128)} %get-tuple-element.104.mine_ref, f32[512,128]{1,0:T(8,128)} %collective-permute-done.19.theirs_ref, f32[512,1024]{1,0:T(8,128)} %shard_map.75.total_ref, ...), custom_call_target="tpu_custom_call" | custom-call | flops 2147483648 | bytes 5242880 | tf_op jit(solution)/shard_map/pallas_call | solution.py:345
  (1 shorter events, 0.0 us)
Async XLA Ops:
  0.0 3.1 %collective-permute-start = (bf16[4,16,8192]{2,1,0:T(8,128)(2,1)}, bf16[4,16,8192]{2,1,0:T(8,128)(2,1)}, u32[]{:S(2)}, u32[]{:S(2)}) collective-permute-start(bf16[4,16,8192]{2,1,0:T(8,128)(2,1)} %here_ref.3), channel_id=1, source_target_pairs={{0,1},{1,0},{2,3},{3,2},{4,5},{5,4},{6,7},{7,6},{8,9},{9,8},{10,11... | collective-permute-start | bytes 3145736 | tf_op jit(solution)/shard_map/ppermute | solution.py:386
  3.1 39.9 %collective-permute-start.7 = (bf16[512,8192]{1,0:T(8,128)(2,1)}, bf16[512,8192]{1,0:T(8,128)(2,1)}, u32[]{:S(2)}, u32[]{:S(2)}) collective-permute-start(bf16[512,8192]{1,0:T(8,128)(2,1)} %refs_0_.7), channel_id=1, source_target_pairs={{0,1},{1,0},{2,3},{3,2},{4,5},{5,4},{6,7},{7,6},{8,9},{9,8},{10,11... | collective-permute-start | bytes 25165832 | tf_op jit(solution)/shard_map/ppermute | solution.py:386
  6.2 18.0 %collective-permute-start.1 = (bf16[2304,128]{1,0:T(8,128)(2,1)}, bf16[2304,128]{1,0:T(8,128)(2,1)}, u32[]{:S(2)}, u32[]{:S(2)}) collective-permute-start(bf16[2304,128]{1,0:T(8,128)(2,1)} %shard_map.73.refs_2_), channel_id=1, source_target_pairs={{0,4},{1,5},{2,6},{3,7},{4,12},{5,13},{6,14},{7,15},{8,0},{9,1},{1... | collective-permute-start | bytes 1769480 | tf_op jit(solution)/shard_map/ppermute | solution.py:386
  9.0 15.6 %collective-permute-start.2 = (bf16[2304,128]{1,0:T(8,128)(2,1)}, bf16[2304,128]{1,0:T(8,128)(2,1)}, u32[]{:S(2)}, u32[]{:S(2)}) collective-permute-start(bf16[2304,128]{1,0:T(8,128)(2,1)} %shard_map.73.refs_2_), channel_id=1, source_target_pairs={{0,2},{1,3},{2,0},{3,1},{4,6},{5,7},{6,4},{7,5},{8,10},{9,11},{10,... | collective-permute-start | bytes 1769480 | tf_op jit(solution)/shard_map/ppermute | solution.py:386
  10.5 11.4 %collective-permute-start.3 = (s32[512]{0:T(512)S(1)}, s32[512]{0:T(512)S(1)}, u32[]{:S(2)}, u32[]{:S(2)}) collective-permute-start(s32[512]{0:T(512)S(1)} %select_reduce_fusion), channel_id=1, source_target_pairs={{0,1},{1,0},{2,3},{3,2},{4,5},{5,4},{6,7},{7,6},{8,9},{9,8},{10,11... | collective-permute-start | bytes 6152 | tf_op jit(solution)/shard_map/ppermute | solution.py:386
  24.6 15.8 %collective-permute-start.4 = (bf16[2304,128]{1,0:T(8,128)(2,1)}, bf16[2304,128]{1,0:T(8,128)(2,1)}, u32[]{:S(2)}, u32[]{:S(2)}) collective-permute-start(bf16[2304,128]{1,0:T(8,128)(2,1)} %collective-permute-done.1.refs_3_), channel_id=1, source_target_pairs={{0,4},{1,5},{2,6},{3,7},{4,12},{5,13},{6,14},{7,15},{8,0},{9,1},{1... | collective-permute-start | bytes 1769480 | tf_op jit(solution)/shard_map/ppermute | solution.py:386
  27.2 14.5 %collective-permute-start.5 = (bf16[2304,128]{1,0:T(8,128)(2,1)}, bf16[2304,128]{1,0:T(8,128)(2,1)}, u32[]{:S(2)}, u32[]{:S(2)}) collective-permute-start(bf16[2304,128]{1,0:T(8,128)(2,1)} %collective-permute-done.1.refs_3_), channel_id=1, source_target_pairs={{0,2},{1,3},{2,0},{3,1},{4,6},{5,7},{6,4},{7,5},{8,10},{9,11},{10,... | collective-permute-start | bytes 1769480 | tf_op jit(solution)/shard_map/ppermute | solution.py:386
  28.7 14.2 %collective-permute-start.6 = (bf16[2304,128]{1,0:T(8,128)(2,1)}, bf16[2304,128]{1,0:T(8,128)(2,1)}, u32[]{:S(2)}, u32[]{:S(2)}) collective-permute-start(bf16[2304,128]{1,0:T(8,128)(2,1)} %collective-permute-done.2.refs_4_), channel_id=1, source_target_pairs={{0,16},{1,17},{2,18},{3,19},{4,20},{5,21},{6,22},{7,23},{8,24},{9,... | collective-permute-start | bytes 1769480 | tf_op jit(solution)/shard_map/ppermute | solution.py:386
  42.9 13.3 %collective-permute-start.10 = (bf16[2304,128]{1,0:T(8,128)(2,1)}, bf16[2304,128]{1,0:T(8,128)(2,1)}, u32[]{:S(2)}, u32[]{:S(2)}) collective-permute-start(bf16[2304,128]{1,0:T(8,128)(2,1)} %collective-permute-done.4.refs_5_), channel_id=1, source_target_pairs={{0,16},{1,17},{2,18},{3,19},{4,20},{5,21},{6,22},{7,23},{8,24},{9,... | collective-permute-start | bytes 1769480 | tf_op jit(solution)/shard_map/ppermute | solution.py:386
  44.5 13.1 %collective-permute-start.8 = (bf16[2304,128]{1,0:T(8,128)(2,1)}, bf16[2304,128]{1,0:T(8,128)(2,1)}, u32[]{:S(2)}, u32[]{:S(2)}) collective-permute-start(bf16[2304,128]{1,0:T(8,128)(2,1)} %shard_map.73.refs_2_), channel_id=1, source_target_pairs={{0,8},{1,9},{2,10},{3,11},{4,0},{5,1},{6,2},{7,3},{8,12},{9,13},{1... | collective-permute-start | bytes 1769480 | tf_op jit(solution)/shard_map/ppermute | solution.py:386
  44.8 12.8 %collective-permute-start.9 = (bf16[2304,128]{1,0:T(8,128)(2,1)}, bf16[2304,128]{1,0:T(8,128)(2,1)}, u32[]{:S(2)}, u32[]{:S(2)}) collective-permute-start(bf16[2304,128]{1,0:T(8,128)(2,1)} %collective-permute-done.4.refs_5_), channel_id=1, source_target_pairs={{0,2},{1,3},{2,0},{3,1},{4,6},{5,7},{6,4},{7,5},{8,10},{9,11},{10,... | collective-permute-start | bytes 1769480 | tf_op jit(solution)/shard_map/ppermute | solution.py:386
  57.6 14.7 %collective-permute-start.11 = (bf16[2304,128]{1,0:T(8,128)(2,1)}, bf16[2304,128]{1,0:T(8,128)(2,1)}, u32[]{:S(2)}, u32[]{:S(2)}) collective-permute-start(bf16[2304,128]{1,0:T(8,128)(2,1)} %shard_map.76.refs_2_), channel_id=1, source_target_pairs={{0,4},{1,5},{2,6},{3,7},{4,12},{5,13},{6,14},{7,15},{8,0},{9,1},{1... | collective-permute-start | bytes 1769480 | tf_op jit(solution)/shard_map/ppermute | solution.py:386
  60.6 11.7 %collective-permute-start.12 = (bf16[2304,128]{1,0:T(8,128)(2,1)}, bf16[2304,128]{1,0:T(8,128)(2,1)}, u32[]{:S(2)}, u32[]{:S(2)}) collective-permute-start(bf16[2304,128]{1,0:T(8,128)(2,1)} %collective-permute-done.8.refs_3_), channel_id=1, source_target_pairs={{0,2},{1,3},{2,0},{3,1},{4,6},{5,7},{6,4},{7,5},{8,10},{9,11},{10,... | collective-permute-start | bytes 1769480 | tf_op jit(solution)/shard_map/ppermute | solution.py:386
  60.8 11.8 %collective-permute-start.13 = (bf16[2304,128]{1,0:T(8,128)(2,1)}, bf16[2304,128]{1,0:T(8,128)(2,1)}, u32[]{:S(2)}, u32[]{:S(2)}) collective-permute-start(bf16[2304,128]{1,0:T(8,128)(2,1)} %collective-permute-done.5.refs_2_), channel_id=1, source_target_pairs={{0,16},{1,17},{2,18},{3,19},{4,20},{5,21},{6,22},{7,23},{8,24},{9,... | collective-permute-start | bytes 1769480 | tf_op jit(solution)/shard_map/ppermute | solution.py:386
  61.4 6.2 %collective-permute-start.14 = (bf16[128,1024]{1,0:T(8,128)(2,1)}, bf16[128,1024]{1,0:T(8,128)(2,1)S(1)}, u32[]{:S(2)}, u32[]{:S(2)}) collective-permute-start(bf16[128,1024]{1,0:T(8,128)(2,1)} %get-tuple-element.87.refs_0_), channel_id=1, source_target_pairs={{0,1},{1,0},{2,3},{3,2},{4,5},{5,4},{6,7},{7,6},{8,9},{9,8},{10,11... | collective-permute-start | bytes 786440 | tf_op jit(solution)/shard_map/ppermute | solution.py:386
  67.6 17.3 %copy-start.1 = (bf16[128,1024]{1,0:T(8,128)(2,1)}, bf16[128,1024]{1,0:T(8,128)(2,1)S(1)}, u32[]{:S(2)}) copy-start(bf16[128,1024]{1,0:T(8,128)(2,1)S(1)} %collective-permute-done.14.refs_1_) | copy-start | bytes 786436
  72.7 12.8 %collective-permute-start.15 = (bf16[2304,128]{1,0:T(8,128)(2,1)}, bf16[2304,128]{1,0:T(8,128)(2,1)}, u32[]{:S(2)}, u32[]{:S(2)}) collective-permute-start(bf16[2304,128]{1,0:T(8,128)(2,1)} %shard_map.76.refs_2_), channel_id=1, source_target_pairs={{0,8},{1,9},{2,10},{3,11},{4,0},{5,1},{6,2},{7,3},{8,12},{9,13},{1... | collective-permute-start | bytes 1769480 | tf_op jit(solution)/shard_map/ppermute | solution.py:386
  73.7 11.7 %collective-permute-start.16 = (bf16[2304,128]{1,0:T(8,128)(2,1)}, bf16[2304,128]{1,0:T(8,128)(2,1)}, u32[]{:S(2)}, u32[]{:S(2)}) collective-permute-start(bf16[2304,128]{1,0:T(8,128)(2,1)} %collective-permute-done.10.refs_4_), channel_id=1, source_target_pairs={{0,2},{1,3},{2,0},{3,1},{4,6},{5,7},{6,4},{7,5},{8,10},{9,11},{10,... | collective-permute-start | bytes 1769480 | tf_op jit(solution)/shard_map/ppermute | solution.py:386
  74.1 11.4 %collective-permute-start.17 = (bf16[2304,128]{1,0:T(8,128)(2,1)}, bf16[2304,128]{1,0:T(8,128)(2,1)}, u32[]{:S(2)}, u32[]{:S(2)}) collective-permute-start(bf16[2304,128]{1,0:T(8,128)(2,1)} %collective-permute-done.12.refs_5_), channel_id=1, source_target_pairs={{0,16},{1,17},{2,18},{3,19},{4,20},{5,21},{6,22},{7,23},{8,24},{9,... | collective-permute-start | bytes 1769480 | tf_op jit(solution)/shard_map/ppermute | solution.py:386
  74.7 10.8 %collective-permute-start.18 = (bf16[96,1024]{1,0:T(8,128)(2,1)}, bf16[96,1024]{1,0:T(8,128)(2,1)}, u32[]{:S(2)}, u32[]{:S(2)}) collective-permute-start(bf16[96,1024]{1,0:T(8,128)(2,1)} %get-tuple-element.98.refs_2_), channel_id=1, source_target_pairs={{0,1},{1,0},{2,3},{3,2},{4,5},{5,4},{6,7},{7,6},{8,9},{9,8},{10,11... | collective-permute-start | bytes 589832 | tf_op jit(solution)/shard_map/ppermute | solution.py:386
  84.9 7.4 %collective-permute-start.20 = (bf16[192,1024]{1,0:T(8,128)(2,1)}, bf16[192,1024]{1,0:T(8,128)(2,1)S(1)}, u32[]{:S(2)}, u32[]{:S(2)}) collective-permute-start(bf16[192,1024]{1,0:T(8,128)(2,1)} %get-tuple-element.109.refs_4_), channel_id=1, source_target_pairs={{0,1},{1,0},{2,3},{3,2},{4,5},{5,4},{6,7},{7,6},{8,9},{9,8},{10,11... | collective-permute-start | bytes 1179656 | tf_op jit(solution)/shard_map/ppermute | solution.py:386
  91.7 2.2 %collective-permute-start.19 = (f32[512,128]{1,0:T(8,128)}, f32[512,128]{1,0:T(8,128)}, u32[]{:S(2)}, u32[]{:S(2)}) collective-permute-start(f32[512,128]{1,0:T(8,128)} %get-tuple-element.105), channel_id=1, source_target_pairs={{0,1},{1,0},{2,3},{3,2},{4,5},{5,4},{6,7},{7,6},{8,9},{9,8},{10,11... | collective-permute-start | bytes 786440 | tf_op jit(solution)/shard_map/ppermute | solution.py:386
  91.8 2.1 %collective-permute-start.21 = (bf16[96,1024]{1,0:T(8,128)(2,1)}, bf16[96,1024]{1,0:T(8,128)(2,1)}, u32[]{:S(2)}, u32[]{:S(2)}) collective-permute-start(bf16[96,1024]{1,0:T(8,128)(2,1)} %get-tuple-element.110.refs_6_), channel_id=1, source_target_pairs={{0,1},{1,0},{2,3},{3,2},{4,5},{5,4},{6,7},{7,6},{8,9},{9,8},{10,11... | collective-permute-start | bytes 589832 | tf_op jit(solution)/shard_map/ppermute | solution.py:386
  92.3 1.7 %copy-start = (bf16[192,1024]{1,0:T(8,128)(2,1)}, bf16[192,1024]{1,0:T(8,128)(2,1)S(1)}, u32[]{:S(2)}) copy-start(bf16[192,1024]{1,0:T(8,128)(2,1)S(1)} %collective-permute-done.20.refs_5_) | copy-start | bytes 1179652

commit v22 on v17

--- a/solution.py
+++ b/solution.py
@@ -21,7 +21,7 @@
     *((3, 0, 1), (2, 1, 1), (3, 1, 1)),
 )
 KERNEL_BOUNDS = (0, 4, 7, 13, 16)
-QUARTER_CUTS = (0, 512, 1024, 2048)
+QUARTER_CUTS = (0, 512, 2048)
 VMEM_BYTES = 64 * 1024 * 1024 - 512 * 1024
 
 

time: 101 us -> 102 us (level)
  Pallas kernels: 60.2 us -> 63.6 us
  waiting for transfers between devices: 16.8 us -> 15.1 us
    pallas_call x4, Pallas kernels: 29 us -> 32.4 us  [absorb(): pl.pallas_call(functools.partial(absorb_kernel, sizes, start, sides, more...]
    ppermute x22, waiting for transfers between devices: 16.8 us -> 15.1 us  [permuted(): return lax.ppermute(array, axes, pairs)]
  transfers between devices with their start and end apart: 22 -> 22, of which waited for: 13 -> 12; matrix products, arithmetic and copies ran while one was open for 3% -> 3% of each run, Pallas kernels for 54% -> 56%
where the time goes in v22:
time: 102 us
  Pallas kernels  63.6 us (62%)
  starting transfers between devices  20 us (20%)
  waiting for transfers between devices  15.1 us (15%)
  local copies, waits for them, and re-layouts  2.27 us (2%)
    pallas_call x4, Pallas kernels, absorb(): pl.pallas_call(functools.partial(absorb_kernel, sizes, start, sides, more...  32.4 us
    ppermute x22, starting transfers between devices, permuted(): return lax.ppermute(array, axes, pairs)  20 us
    pallas_call x2, Pallas kernels, base_part(): pl.pallas_call(functools.partial(base_kernel, steps), out_shape=result, g...  19.5 us
    ppermute x22, waiting for transfers between devices, permuted(): return lax.ppermute(array, axes, pairs)  15.1 us
    pallas_call x1, Pallas kernels, finish(): pl.pallas_call(functools.partial(finish_kernel, len(ups)), out_shape=jax....  6.19 us
    pallas_call x2, Pallas kernels, assemble(): pl.pallas_call(functools.partial(assemble_kernel, back), out_shape=jax.Sh...  5.5 us
  transfers between devices with their start and end apart: 22, of which 12 were waited for; matrix products, arithmetic and copies ran while one was open for 3% of the time, Pallas kernels for 56%

profile of v22, /device:TPU:0, one launch (start us, length us, event | category | flops | bytes accessed | tf_op | source)
XLA Modules:
  0.0 102.0 jit_solution(13587524358981594761)
XLA Ops:
  0.0 0.5 collective-permute-start
  0.5 1.2 %dynamic-slice_bitcast_fusion.info_ref = s32[50]{0:T(128)} fusion(s32[32,50]{1,0:T(8,128)} %constant.20.clone, s32[]{:T(128)S(6)} %select_n.8), kind=kLoop, calls=%fused_computation.3 | loop fusion | bytes 404 | tf_op jit(solution)/shard_map/jit(dynamic_index_in_dim)/squeeze | solution.py:413
  1.7 0.8 select_reduce_fusion
  2.5 0.6 collective-permute-done.there_ref
  3.1 0.4 collective-permute-start.7
  3.5 2.8 %shard_map.73.refs_2_ = bf16[2304,128]{1,0:T(8,128)(2,1)} custom-call(s32[50]{0:T(128)} %dynamic-slice_bitcast_fusion.info_ref, bf16[4,16,8192]{2,1,0:T(8,128)(2,1)} %here_ref.3, bf16[4,16,8192]{2,1,0:T(8,128)(2,1)} %collective-permute-done.there_ref, bf16[4,16,1024]{2,1,0:T(8,128)(2,1)} %up_ref.3), custom_call_target="tpu_custom_call" | custom-call | tf_op jit(solution)/shard_map/pallas_call | solution.py:119
  6.2 2.8 %collective-permute-start.1 = (bf16[2304,128]{1,0:T(8,128)(2,1)}, bf16[2304,128]{1,0:T(8,128)(2,1)}, u32[]{:S(2)}, u32[]{:S(2)}) collective-permute-start(bf16[2304,128]{1,0:T(8,128)(2,1)} %shard_map.73.refs_2_), channel_id=1, source_target_pairs={{0,4},{1,5},{2,6},{3,7},{4,12},{5,13},{6,14},{7,15},{8,0},{9,1},{1... | collective-permute-start | bytes 1769480 | tf_op jit(solution)/shard_map/ppermute | solution.py:386
  9.0 1.5 %collective-permute-start.2 = (bf16[2304,128]{1,0:T(8,128)(2,1)}, bf16[2304,128]{1,0:T(8,128)(2,1)}, u32[]{:S(2)}, u32[]{:S(2)}) collective-permute-start(bf16[2304,128]{1,0:T(8,128)(2,1)} %shard_map.73.refs_2_), channel_id=1, source_target_pairs={{0,2},{1,3},{2,0},{3,1},{4,6},{5,7},{6,4},{7,5},{8,10},{9,11},{10,... | collective-permute-start | bytes 1769480 | tf_op jit(solution)/shard_map/ppermute | solution.py:386
  10.5 0.0 collective-permute-start.3
  10.5 9.6 %shard_map.74.refs_0_ = f32[512,1024]{1,0:T(8,128)} custom-call(bf16[512,8192]{1,0:T(8,128)(2,1)} %refs_0_.7, bf16[8192,1024]{1,0:T(8,128)(2,1)} %weight_ref.3), custom_call_target="tpu_custom_call" | custom-call | flops 4294967296 | bytes 14680064 | tf_op jit(solution)/shard_map/pallas_call | solution.py:163
  20.1 0.0 collective-permute-done.3
  20.1 4.1 %collective-permute-done.1.refs_3_ = bf16[2304,128]{1,0:T(8,128)(2,1)} collective-permute-done((bf16[2304,128]{1,0:T(8,128)(2,1)}, bf16[2304,128]{1,0:T(8,128)(2,1)}, u32[]{:S(2)}, u32[]{:S(2)}) %collective-permute-start.1) | collective-permute-done | bytes 589856 | tf_op jit(solution)/shard_map/ppermute | solution.py:386
  24.2 0.4 collective-permute-done.2.refs_4_
  24.6 2.6 %collective-permute-start.4 = (bf16[2304,128]{1,0:T(8,128)(2,1)}, bf16[2304,128]{1,0:T(8,128)(2,1)}, u32[]{:S(2)}, u32[]{:S(2)}) collective-permute-start(bf16[2304,128]{1,0:T(8,128)(2,1)} %collective-permute-done.1.refs_3_), channel_id=1, source_target_pairs={{0,4},{1,5},{2,6},{3,7},{4,12},{5,13},{6,14},{7,15},{8,0},{9,1},{1... | collective-permute-start | bytes 1769480 | tf_op jit(solution)/shard_map/ppermute | solution.py:386
  27.2 1.5 %collective-permute-start.5 = (bf16[2304,128]{1,0:T(8,128)(2,1)}, bf16[2304,128]{1,0:T(8,128)(2,1)}, u32[]{:S(2)}, u32[]{:S(2)}) collective-permute-start(bf16[2304,128]{1,0:T(8,128)(2,1)} %collective-permute-done.1.refs_3_), channel_id=1, source_target_pairs={{0,2},{1,3},{2,0},{3,1},{4,6},{5,7},{6,4},{7,5},{8,10},{9,11},{10,... | collective-permute-start | bytes 1769480 | tf_op jit(solution)/shard_map/ppermute | solution.py:386
  28.7 1.5 %collective-permute-start.6 = (bf16[2304,128]{1,0:T(8,128)(2,1)}, bf16[2304,128]{1,0:T(8,128)(2,1)}, u32[]{:S(2)}, u32[]{:S(2)}) collective-permute-start(bf16[2304,128]{1,0:T(8,128)(2,1)} %collective-permute-done.2.refs_4_), channel_id=1, source_target_pairs={{0,16},{1,17},{2,18},{3,19},{4,20},{5,21},{6,22},{7,23},{8,24},{9,... | collective-permute-start | bytes 1769480 | tf_op jit(solution)/shard_map/ppermute | solution.py:386
  30.2 9.9 %shard_map.75.total_ref = f32[512,1024]{1,0:T(8,128)} custom-call(bf16[512,8192]{1,0:T(8,128)(2,1)} %refs_0_.7, bf16[8192,1024]{1,0:T(8,128)(2,1)} %weight_ref.3, f32[512,1024]{1,0:T(8,128)} %shard_map.74.refs_0_), custom_call_target="tpu_custom_call" | custom-call | flops 4294967296 | bytes 14680064 | tf_op jit(solution)/shard_map/pallas_call | solution.py:163
  40.2 0.3 collective-permute-done.4.refs_5_
  40.4 1.3 %collective-permute-done.5.refs_2_ = bf16[2304,128]{1,0:T(8,128)(2,1)} collective-permute-done((bf16[2304,128]{1,0:T(8,128)(2,1)}, bf16[2304,128]{1,0:T(8,128)(2,1)}, u32[]{:S(2)}, u32[]{:S(2)}) %collective-permute-start.5) | collective-permute-done | bytes 589856 | tf_op jit(solution)/shard_map/ppermute | solution.py:386
  41.7 1.2 %collective-permute-done.6.refs_3_ = bf16[2304,128]{1,0:T(8,128)(2,1)} collective-permute-done((bf16[2304,128]{1,0:T(8,128)(2,1)}, bf16[2304,128]{1,0:T(8,128)(2,1)}, u32[]{:S(2)}, u32[]{:S(2)}) %collective-permute-start.6) | collective-permute-done | bytes 589856 | tf_op jit(solution)/shard_map/ppermute | solution.py:386
  42.9 0.0 collective-permute-done.7.refs_1_
  42.9 1.5 %collective-permute-start.10 = (bf16[2304,128]{1,0:T(8,128)(2,1)}, bf16[2304,128]{1,0:T(8,128)(2,1)}, u32[]{:S(2)}, u32[]{:S(2)}) collective-permute-start(bf16[2304,128]{1,0:T(8,128)(2,1)} %collective-permute-done.4.refs_5_), channel_id=1, source_target_pairs={{0,16},{1,17},{2,18},{3,19},{4,20},{5,21},{6,22},{7,23},{8,24},{9,... | collective-permute-start | bytes 1769480 | tf_op jit(solution)/shard_map/ppermute | solution.py:386
  44.5 0.3 collective-permute-start.8
  44.8 0.5 collective-permute-start.9
  45.3 1.0 %copy.19.row_slot_ref = s32[1024,1]{1,0:T(8,128)} copy(s32[1024,1]{0,1:T(1,128)S(1)} %pad_add_fusion) | data formatting | bytes 8192 | tf_op jit(solution)/shard_map/optimization_barrier | solution.py:418
  46.4 2.7 %shard_map.76.refs_2_ = bf16[2304,128]{1,0:T(8,128)(2,1)} custom-call(s32[50]{0:T(128)} %dynamic-slice_bitcast_fusion.info_ref, bf16[4,16,8192]{2,1,0:T(8,128)(2,1)} %here_ref.3, bf16[4,16,8192]{2,1,0:T(8,128)(2,1)} %collective-permute-done.there_ref, bf16[4,16,1024]{2,1,0:T(8,128)(2,1)} %up_ref.3), custom_call_target="tpu_custom_call" | custom-call | tf_op jit(solution)/shard_map/pallas_call | solution.py:119
  49.1 7.3 %shard_map.77 = (f32[512,128]{1,0:T(8,128)}, f32[512,128]{1,0:T(8,128)}, bf16[128,1024]{1,0:T(8,128)(2,1)}) custom-call(s32[50]{0:T(128)} %dynamic-slice_bitcast_fusion.info_ref, s32[1024,1]{1,0:T(8,128)} %copy.19.row_slot_ref, bf16[512,8192]{1,0:T(8,128)(2,1)} %refs_0_.7, bf16[512,8192]{1,0:T(8,128)(2,1)} %collective-permute-done.7.refs_1_, ...), custom_call_target="tpu_custom_call" | custom-call | flops 2147483648 | bytes 6553600 | tf_op jit(solution)/shard_map/pallas_call | solution.py:284
  56.4 0.0 collective-permute-done.10.refs_4_
  56.4 1.1 %collective-permute-done.8.refs_3_ = bf16[2304,128]{1,0:T(8,128)(2,1)} collective-permute-done((bf16[2304,128]{1,0:T(8,128)(2,1)}, bf16[2304,128]{1,0:T(8,128)(2,1)}, u32[]{:S(2)}, u32[]{:S(2)}) %collective-permute-start.8) | collective-permute-done | bytes 589856 | tf_op jit(solution)/shard_map/ppermute | solution.py:386
  57.6 0.0 collective-permute-done.9.refs_4_
  57.6 3.1 %collective-permute-start.11 = (bf16[2304,128]{1,0:T(8,128)(2,1)}, bf16[2304,128]{1,0:T(8,128)(2,1)}, u32[]{:S(2)}, u32[]{:S(2)}) collective-permute-start(bf16[2304,128]{1,0:T(8,128)(2,1)} %shard_map.76.refs_2_), channel_id=1, source_target_pairs={{0,4},{1,5},{2,6},{3,7},{4,12},{5,13},{6,14},{7,15},{8,0},{9,1},{1... | collective-permute-start | bytes 1769480 | tf_op jit(solution)/shard_map/ppermute | solution.py:386
  60.6 0.2 collective-permute-start.12
  60.8 0.5 collective-permute-start.13
  61.4 0.0 collective-permute-start.14
  61.4 7.0 %shard_map.78 = (f32[512,128]{1,0:T(8,128)}, f32[512,128]{1,0:T(8,128)}, bf16[96,1024]{1,0:T(8,128)(2,1)}) custom-call(s32[50]{0:T(128)} %dynamic-slice_bitcast_fusion.info_ref, s32[1024,1]{1,0:T(8,128)} %copy.19.row_slot_ref, bf16[512,8192]{1,0:T(8,128)(2,1)} %refs_0_.7, bf16[512,8192]{1,0:T(8,128)(2,1)} %collective-permute-done.7.refs_1_, ...), custom_call_target="tpu_custom_call" | custom-call | flops 1610612736 | bytes 5963776 | tf_op jit(solution)/shard_map/pallas_call | solution.py:284
  68.4 0.0 collective-permute-done.14.refs_1_
  68.4 0.0 copy-start.1
  68.4 3.8 %collective-permute-done.11.refs_6_ = bf16[2304,128]{1,0:T(8,128)(2,1)} collective-permute-done((bf16[2304,128]{1,0:T(8,128)(2,1)}, bf16[2304,128]{1,0:T(8,128)(2,1)}, u32[]{:S(2)}, u32[]{:S(2)}) %collective-permute-start.11) | collective-permute-done | bytes 589856 | tf_op jit(solution)/shard_map/ppermute | solution.py:386
  72.3 0.1 collective-permute-done.12.refs_5_
  72.4 0.3 collective-permute-done.13.refs_7_
  72.7 1.1 %collective-permute-start.15 = (bf16[2304,128]{1,0:T(8,128)(2,1)}, bf16[2304,128]{1,0:T(8,128)(2,1)}, u32[]{:S(2)}, u32[]{:S(2)}) collective-permute-start(bf16[2304,128]{1,0:T(8,128)(2,1)} %shard_map.76.refs_2_), channel_id=1, source_target_pairs={{0,8},{1,9},{2,10},{3,11},{4,0},{5,1},{6,2},{7,3},{8,12},{9,13},{1... | collective-permute-start | bytes 1769480 | tf_op jit(solution)/shard_map/ppermute | solution.py:386
  73.7 0.4 collective-permute-start.16
  74.1 0.5 collective-permute-start.17
  74.7 0.0 collective-permute-start.18
  74.7 11.0 %shard_map.79 = (f32[512,128]{1,0:T(8,128)}, f32[512,128]{1,0:T(8,128)}, bf16[192,1024]{1,0:T(8,128)(2,1)}) custom-call(s32[50]{0:T(128)} %dynamic-slice_bitcast_fusion.info_ref, s32[1024,1]{1,0:T(8,128)} %copy.19.row_slot_ref, bf16[512,8192]{1,0:T(8,128)(2,1)} %refs_0_.7, bf16[512,8192]{1,0:T(8,128)(2,1)} %collective-permute-done.7.refs_1_, ...), custom_call_target="tpu_custom_call" | custom-call | flops 3221225472 | bytes 11927552 | tf_op jit(solution)/shard_map/pallas_call | solution.py:284
  85.7 0.0 copy-done.1
  85.7 0.6 collective-permute-start.20
  86.3 0.0 collective-permute-done.18.refs_3_
  86.3 0.0 collective-permute-done.15.refs_2_
  86.3 0.0 collective-permute-done.16.refs_3_
  86.3 0.1 collective-permute-done.17.refs_4_
  86.4 7.0 %shard_map.80 = (f32[512,128]{1,0:T(8,128)}, f32[512,128]{1,0:T(8,128)}, bf16[96,1024]{1,0:T(8,128)(2,1)}) custom-call(s32[50]{0:T(128)} %dynamic-slice_bitcast_fusion.info_ref, s32[1024,1]{1,0:T(8,128)} %copy.19.row_slot_ref, bf16[512,8192]{1,0:T(8,128)(2,1)} %refs_0_.7, bf16[512,8192]{1,0:T(8,128)(2,1)} %collective-permute-done.7.refs_1_, ...), custom_call_target="tpu_custom_call" | custom-call | flops 1610612736 | bytes 5963776 | tf_op jit(solution)/shard_map/pallas_call | solution.py:284
  93.4 0.1 collective-permute-start.19
  93.5 0.5 collective-permute-start.21
  94.0 0.0 collective-permute-done.20.refs_5_
  94.0 0.0 copy-start
  94.0 1.6 %collective-permute-done.21.refs_7_ = bf16[96,1024]{1,0:T(8,128)(2,1)} collective-permute-done((bf16[96,1024]{1,0:T(8,128)(2,1)}, bf16[96,1024]{1,0:T(8,128)(2,1)}, u32[]{:S(2)}, u32[]{:S(2)}) %collective-permute-start.21) | collective-permute-done | bytes 196640 | tf_op jit(solution)/shard_map/ppermute | solution.py:386
  95.6 0.0 collective-permute-done.19.theirs_ref
  95.6 0.0 copy-done
  95.6 6.2 %shard_map.81 = bf16[512,1024]{1,0:T(8,128)(2,1)} custom-call(s32[50]{0:T(128)} %dynamic-slice_bitcast_fusion.info_ref, s32[1024,1]{1,0:T(8,128)} %copy.19.row_slot_ref, f32[512,128]{1,0:T(8,128)} %get-tuple-element.104.mine_ref, f32[512,128]{1,0:T(8,128)} %collective-permute-done.19.theirs_ref, f32[512,1024]{1,0:T(8,128)} %shard_map.75.total_ref, ...), custom_call_target="tpu_custom_call" | custom-call | flops 2147483648 | bytes 5242880 | tf_op jit(solution)/shard_map/pallas_call | solution.py:345
  (1 shorter events, 0.0 us)
Async XLA Ops:
  0.0 3.1 %collective-permute-start = (bf16[4,16,8192]{2,1,0:T(8,128)(2,1)}, bf16[4,16,8192]{2,1,0:T(8,128)(2,1)}, u32[]{:S(2)}, u32[]{:S(2)}) collective-permute-start(bf16[4,16,8192]{2,1,0:T(8,128)(2,1)} %here_ref.3), channel_id=1, source_target_pairs={{0,1},{1,0},{2,3},{3,2},{4,5},{5,4},{6,7},{7,6},{8,9},{9,8},{10,11... | collective-permute-start | bytes 3145736 | tf_op jit(solution)/shard_map/ppermute | solution.py:386
  3.1 39.9 %collective-permute-start.7 = (bf16[512,8192]{1,0:T(8,128)(2,1)}, bf16[512,8192]{1,0:T(8,128)(2,1)}, u32[]{:S(2)}, u32[]{:S(2)}) collective-permute-start(bf16[512,8192]{1,0:T(8,128)(2,1)} %refs_0_.7), channel_id=1, source_target_pairs={{0,1},{1,0},{2,3},{3,2},{4,5},{5,4},{6,7},{7,6},{8,9},{9,8},{10,11... | collective-permute-start | bytes 25165832 | tf_op jit(solution)/shard_map/ppermute | solution.py:386
  6.2 18.0 %collective-permute-start.1 = (bf16[2304,128]{1,0:T(8,128)(2,1)}, bf16[2304,128]{1,0:T(8,128)(2,1)}, u32[]{:S(2)}, u32[]{:S(2)}) collective-permute-start(bf16[2304,128]{1,0:T(8,128)(2,1)} %shard_map.73.refs_2_), channel_id=1, source_target_pairs={{0,4},{1,5},{2,6},{3,7},{4,12},{5,13},{6,14},{7,15},{8,0},{9,1},{1... | collective-permute-start | bytes 1769480 | tf_op jit(solution)/shard_map/ppermute | solution.py:386
  9.0 15.6 %collective-permute-start.2 = (bf16[2304,128]{1,0:T(8,128)(2,1)}, bf16[2304,128]{1,0:T(8,128)(2,1)}, u32[]{:S(2)}, u32[]{:S(2)}) collective-permute-start(bf16[2304,128]{1,0:T(8,128)(2,1)} %shard_map.73.refs_2_), channel_id=1, source_target_pairs={{0,2},{1,3},{2,0},{3,1},{4,6},{5,7},{6,4},{7,5},{8,10},{9,11},{10,... | collective-permute-start | bytes 1769480 | tf_op jit(solution)/shard_map/ppermute | solution.py:386
  10.5 9.6 %collective-permute-start.3 = (s32[512]{0:T(512)S(1)}, s32[512]{0:T(512)S(1)}, u32[]{:S(2)}, u32[]{:S(2)}) collective-permute-start(s32[512]{0:T(512)S(1)} %select_reduce_fusion), channel_id=1, source_target_pairs={{0,1},{1,0},{2,3},{3,2},{4,5},{5,4},{6,7},{7,6},{8,9},{9,8},{10,11... | collective-permute-start | bytes 6152 | tf_op jit(solution)/shard_map/ppermute | solution.py:386
  24.6 15.8 %collective-permute-start.4 = (bf16[2304,128]{1,0:T(8,128)(2,1)}, bf16[2304,128]{1,0:T(8,128)(2,1)}, u32[]{:S(2)}, u32[]{:S(2)}) collective-permute-start(bf16[2304,128]{1,0:T(8,128)(2,1)} %collective-permute-done.1.refs_3_), channel_id=1, source_target_pairs={{0,4},{1,5},{2,6},{3,7},{4,12},{5,13},{6,14},{7,15},{8,0},{9,1},{1... | collective-permute-start | bytes 1769480 | tf_op jit(solution)/shard_map/ppermute | solution.py:386
  27.2 14.5 %collective-permute-start.5 = (bf16[2304,128]{1,0:T(8,128)(2,1)}, bf16[2304,128]{1,0:T(8,128)(2,1)}, u32[]{:S(2)}, u32[]{:S(2)}) collective-permute-start(bf16[2304,128]{1,0:T(8,128)(2,1)} %collective-permute-done.1.refs_3_), channel_id=1, source_target_pairs={{0,2},{1,3},{2,0},{3,1},{4,6},{5,7},{6,4},{7,5},{8,10},{9,11},{10,... | collective-permute-start | bytes 1769480 | tf_op jit(solution)/shard_map/ppermute | solution.py:386
  28.7 14.2 %collective-permute-start.6 = (bf16[2304,128]{1,0:T(8,128)(2,1)}, bf16[2304,128]{1,0:T(8,128)(2,1)}, u32[]{:S(2)}, u32[]{:S(2)}) collective-permute-start(bf16[2304,128]{1,0:T(8,128)(2,1)} %collective-permute-done.2.refs_4_), channel_id=1, source_target_pairs={{0,16},{1,17},{2,18},{3,19},{4,20},{5,21},{6,22},{7,23},{8,24},{9,... | collective-permute-start | bytes 1769480 | tf_op jit(solution)/shard_map/ppermute | solution.py:386
  42.9 13.5 %collective-permute-start.10 = (bf16[2304,128]{1,0:T(8,128)(2,1)}, bf16[2304,128]{1,0:T(8,128)(2,1)}, u32[]{:S(2)}, u32[]{:S(2)}) collective-permute-start(bf16[2304,128]{1,0:T(8,128)(2,1)} %collective-permute-done.4.refs_5_), channel_id=1, source_target_pairs={{0,16},{1,17},{2,18},{3,19},{4,20},{5,21},{6,22},{7,23},{8,24},{9,... | collective-permute-start | bytes 1769480 | tf_op jit(solution)/shard_map/ppermute | solution.py:386
  44.5 13.1 %collective-permute-start.8 = (bf16[2304,128]{1,0:T(8,128)(2,1)}, bf16[2304,128]{1,0:T(8,128)(2,1)}, u32[]{:S(2)}, u32[]{:S(2)}) collective-permute-start(bf16[2304,128]{1,0:T(8,128)(2,1)} %shard_map.73.refs_2_), channel_id=1, source_target_pairs={{0,8},{1,9},{2,10},{3,11},{4,0},{5,1},{6,2},{7,3},{8,12},{9,13},{1... | collective-permute-start | bytes 1769480 | tf_op jit(solution)/shard_map/ppermute | solution.py:386
  44.8 12.8 %collective-permute-start.9 = (bf16[2304,128]{1,0:T(8,128)(2,1)}, bf16[2304,128]{1,0:T(8,128)(2,1)}, u32[]{:S(2)}, u32[]{:S(2)}) collective-permute-start(bf16[2304,128]{1,0:T(8,128)(2,1)} %collective-permute-done.4.refs_5_), channel_id=1, source_target_pairs={{0,2},{1,3},{2,0},{3,1},{4,6},{5,7},{6,4},{7,5},{8,10},{9,11},{10,... | collective-permute-start | bytes 1769480 | tf_op jit(solution)/shard_map/ppermute | solution.py:386
  57.6 14.7 %collective-permute-start.11 = (bf16[2304,128]{1,0:T(8,128)(2,1)}, bf16[2304,128]{1,0:T(8,128)(2,1)}, u32[]{:S(2)}, u32[]{:S(2)}) collective-permute-start(bf16[2304,128]{1,0:T(8,128)(2,1)} %shard_map.76.refs_2_), channel_id=1, source_target_pairs={{0,4},{1,5},{2,6},{3,7},{4,12},{5,13},{6,14},{7,15},{8,0},{9,1},{1... | collective-permute-start | bytes 1769480 | tf_op jit(solution)/shard_map/ppermute | solution.py:386
  60.6 11.7 %collective-permute-start.12 = (bf16[2304,128]{1,0:T(8,128)(2,1)}, bf16[2304,128]{1,0:T(8,128)(2,1)}, u32[]{:S(2)}, u32[]{:S(2)}) collective-permute-start(bf16[2304,128]{1,0:T(8,128)(2,1)} %collective-permute-done.8.refs_3_), channel_id=1, source_target_pairs={{0,2},{1,3},{2,0},{3,1},{4,6},{5,7},{6,4},{7,5},{8,10},{9,11},{10,... | collective-permute-start | bytes 1769480 | tf_op jit(solution)/shard_map/ppermute | solution.py:386
  60.8 11.8 %collective-permute-start.13 = (bf16[2304,128]{1,0:T(8,128)(2,1)}, bf16[2304,128]{1,0:T(8,128)(2,1)}, u32[]{:S(2)}, u32[]{:S(2)}) collective-permute-start(bf16[2304,128]{1,0:T(8,128)(2,1)} %collective-permute-done.5.refs_2_), channel_id=1, source_target_pairs={{0,16},{1,17},{2,18},{3,19},{4,20},{5,21},{6,22},{7,23},{8,24},{9,... | collective-permute-start | bytes 1769480 | tf_op jit(solution)/shard_map/ppermute | solution.py:386
  61.4 7.1 %collective-permute-start.14 = (bf16[128,1024]{1,0:T(8,128)(2,1)}, bf16[128,1024]{1,0:T(8,128)(2,1)S(1)}, u32[]{:S(2)}, u32[]{:S(2)}) collective-permute-start(bf16[128,1024]{1,0:T(8,128)(2,1)} %get-tuple-element.87.refs_0_), channel_id=1, source_target_pairs={{0,1},{1,0},{2,3},{3,2},{4,5},{5,4},{6,7},{7,6},{8,9},{9,8},{10,11... | collective-permute-start | bytes 786440 | tf_op jit(solution)/shard_map/ppermute | solution.py:386
  68.4 17.3 %copy-start.1 = (bf16[128,1024]{1,0:T(8,128)(2,1)}, bf16[128,1024]{1,0:T(8,128)(2,1)S(1)}, u32[]{:S(2)}) copy-start(bf16[128,1024]{1,0:T(8,128)(2,1)S(1)} %collective-permute-done.14.refs_1_) | copy-start | bytes 786436
  72.7 13.6 %collective-permute-start.15 = (bf16[2304,128]{1,0:T(8,128)(2,1)}, bf16[2304,128]{1,0:T(8,128)(2,1)}, u32[]{:S(2)}, u32[]{:S(2)}) collective-permute-start(bf16[2304,128]{1,0:T(8,128)(2,1)} %shard_map.76.refs_2_), channel_id=1, source_target_pairs={{0,8},{1,9},{2,10},{3,11},{4,0},{5,1},{6,2},{7,3},{8,12},{9,13},{1... | collective-permute-start | bytes 1769480 | tf_op jit(solution)/shard_map/ppermute | solution.py:386
  73.7 12.6 %collective-permute-start.16 = (bf16[2304,128]{1,0:T(8,128)(2,1)}, bf16[2304,128]{1,0:T(8,128)(2,1)}, u32[]{:S(2)}, u32[]{:S(2)}) collective-permute-start(bf16[2304,128]{1,0:T(8,128)(2,1)} %collective-permute-done.10.refs_4_), channel_id=1, source_target_pairs={{0,2},{1,3},{2,0},{3,1},{4,6},{5,7},{6,4},{7,5},{8,10},{9,11},{10,... | collective-permute-start | bytes 1769480 | tf_op jit(solution)/shard_map/ppermute | solution.py:386
  74.1 12.2 %collective-permute-start.17 = (bf16[2304,128]{1,0:T(8,128)(2,1)}, bf16[2304,128]{1,0:T(8,128)(2,1)}, u32[]{:S(2)}, u32[]{:S(2)}) collective-permute-start(bf16[2304,128]{1,0:T(8,128)(2,1)} %collective-permute-done.12.refs_5_), channel_id=1, source_target_pairs={{0,16},{1,17},{2,18},{3,19},{4,20},{5,21},{6,22},{7,23},{8,24},{9,... | collective-permute-start | bytes 1769480 | tf_op jit(solution)/shard_map/ppermute | solution.py:386
  74.7 11.6 %collective-permute-start.18 = (bf16[96,1024]{1,0:T(8,128)(2,1)}, bf16[96,1024]{1,0:T(8,128)(2,1)}, u32[]{:S(2)}, u32[]{:S(2)}) collective-permute-start(bf16[96,1024]{1,0:T(8,128)(2,1)} %get-tuple-element.98.refs_2_), channel_id=1, source_target_pairs={{0,1},{1,0},{2,3},{3,2},{4,5},{5,4},{6,7},{7,6},{8,9},{9,8},{10,11... | collective-permute-start | bytes 589832 | tf_op jit(solution)/shard_map/ppermute | solution.py:386
  85.7 8.3 %collective-permute-start.20 = (bf16[192,1024]{1,0:T(8,128)(2,1)}, bf16[192,1024]{1,0:T(8,128)(2,1)S(1)}, u32[]{:S(2)}, u32[]{:S(2)}) collective-permute-start(bf16[192,1024]{1,0:T(8,128)(2,1)} %get-tuple-element.109.refs_4_), channel_id=1, source_target_pairs={{0,1},{1,0},{2,3},{3,2},{4,5},{5,4},{6,7},{7,6},{8,9},{9,8},{10,11... | collective-permute-start | bytes 1179656 | tf_op jit(solution)/shard_map/ppermute | solution.py:386
  93.4 2.2 %collective-permute-start.19 = (f32[512,128]{1,0:T(8,128)}, f32[512,128]{1,0:T(8,128)}, u32[]{:S(2)}, u32[]{:S(2)}) collective-permute-start(f32[512,128]{1,0:T(8,128)} %get-tuple-element.105), channel_id=1, source_target_pairs={{0,1},{1,0},{2,3},{3,2},{4,5},{5,4},{6,7},{7,6},{8,9},{9,8},{10,11... | collective-permute-start | bytes 786440 | tf_op jit(solution)/shard_map/ppermute | solution.py:386
  93.5 2.1 %collective-permute-start.21 = (bf16[96,1024]{1,0:T(8,128)(2,1)}, bf16[96,1024]{1,0:T(8,128)(2,1)}, u32[]{:S(2)}, u32[]{:S(2)}) collective-permute-start(bf16[96,1024]{1,0:T(8,128)(2,1)} %get-tuple-element.110.refs_6_), channel_id=1, source_target_pairs={{0,1},{1,0},{2,3},{3,2},{4,5},{5,4},{6,7},{7,6},{8,9},{9,8},{10,11... | collective-permute-start | bytes 589832 | tf_op jit(solution)/shard_map/ppermute | solution.py:386
  94.0 1.7 %copy-start = (bf16[192,1024]{1,0:T(8,128)(2,1)}, bf16[192,1024]{1,0:T(8,128)(2,1)S(1)}, u32[]{:S(2)}) copy-start(bf16[192,1024]{1,0:T(8,128)(2,1)S(1)} %collective-permute-done.20.refs_5_) | copy-start | bytes 1179652
